TPU v7x, 32 devices: a whole 2x2x4 slice. The times are simulated.
32 devices in a mesh: aperture: 8 (over y, x, core), beam: 4 (over z).
Axes of the slice: x: 2, y: 2, z: 4, core: 2. Of those that a mesh axis runs over, the one named last changes fastest.
Arguments:
- subimages: bfloat16 [8, 2, 1024, 512], P('aperture', None, 'beam'), may hold values from -6 to 6
- range_kernel: bfloat16 [8, 2, 512, 512], P('aperture'), may hold values from -0.1875 to 0.1875
- weights0: bfloat16 [8, 16, 2, 128, 320], P('aperture', 'beam'), may hold values from -0.25 to 0.25
- starts0: int32 [8, 16], P(None, 'beam'), may hold values from -6 to 28, as said below
- weights1: bfloat16 [8, 32, 2, 128, 320], P('aperture', 'beam'), may hold values from -0.25 to 0.25
- starts1: int32 [8, 32], P(None, 'beam'), may hold values from -6 to 60, as said below
- owners: int32 [8, 64, 1], P('aperture', 'beam'), may hold values from 0 to 3; in each aligned block of 16 rows (0 to 15, 16 to 31, ..., all dimensions but the last counted through in order) at most 8 rows name the same one
Outputs:
- merged: bfloat16 [8, 128, 2, 64, 128], P('aperture', 'beam')
Inputs may be any that keep to these rules, and one draw needn't show every extreme that they name: starts0[s, p] = 2p - (10 - 2) // 2 + e with -2 <= e <= 2; both ends of e occur. starts1[s, p] = 2p - (10 - 2) // 2 + e with -2 <= e <= 2; both ends of e occur. `owners`: among the 16 sectors homed on one beam device (aligned blocks of 16 rows of one subaperture row), at most 8 name the same owner, a bound that some block reaches.
All inputs are finite; a program needn't handle non-finite values.
Results may differ from a plain program's by a relative error of at most 0.0072.
Values may be sent and summed in bfloat16 or wider, within the bound.
No kernel may reach another device: no remote copies, remote signals or barrier semaphores. Data moves between devices by JAX's collectives and lax.ppermute only.
A program may use at most 64 MiB of HBM per device.

v0:
```python
import jax
import jax.numpy as jnp
from jax import lax
from jax.sharding import PartitionSpec as P

BLK = 32
NW = 10
REACH = 2
OS = 64


def extended(cells, sides, width):
    for axis, dim in sides:
        count = lax.axis_size(axis)
        ends = count - 1
        head = lax.slice_in_dim(cells, 0, width, axis=dim)
        tail = lax.slice_in_dim(cells, cells.shape[dim] - width, cells.shape[dim], axis=dim)
        cells = jnp.concatenate(
            [
                lax.ppermute(tail, axis, [(i, (i + 1) % count) for i in range(ends)]),
                cells,
                lax.ppermute(head, axis, [((i + 1) % count, i) for i in range(ends)]),
            ],
            axis=dim,
        )
    return cells


def partner(block, axis, distance):
    count = lax.axis_size(axis)
    route = []
    for low in range(count):
        high = low | 1 << distance
        if high != low and high < count:
            route += [(low, high), (high, low)]
    return lax.ppermute(block, axis, route)


def complex_dot(left_real, left_imag, right_real, right_imag):
    real_part = jnp.dot(left_real, right_real, preferred_element_type=jnp.float32) - jnp.dot(
        left_imag, right_imag, preferred_element_type=jnp.float32
    )
    imag_part = jnp.dot(left_real, right_imag, preferred_element_type=jnp.float32) + jnp.dot(
        left_imag, right_real, preferred_element_type=jnp.float32
    )
    return jnp.stack([real_part, imag_part])


def resample(subimage, kernel):
    return complex_dot(subimage[0], subimage[1], kernel[0], kernel[1]).astype(jnp.bfloat16)


def interpolate(padded, weights, starts, lowest_block):
    window_width = NW * BLK

    def cut_window(first_block):
        return lax.dynamic_slice_in_dim(padded, (first_block - lowest_block) * BLK, window_width, 1)

    windows = jax.vmap(cut_window)(starts)
    real_part = jnp.einsum(
        "npw,nwr->npr", weights[:, 0], windows[:, 0], preferred_element_type=jnp.float32
    ) - jnp.einsum("npw,nwr->npr", weights[:, 1], windows[:, 1], preferred_element_type=jnp.float32)
    imag_part = jnp.einsum(
        "npw,nwr->npr", weights[:, 0], windows[:, 1], preferred_element_type=jnp.float32
    ) + jnp.einsum("npw,nwr->npr", weights[:, 1], windows[:, 0], preferred_element_type=jnp.float32)
    stacked = jnp.stack([real_part, imag_part])
    return stacked.reshape(2, -1, padded.shape[2]).astype(jnp.bfloat16)


def table_row(table, row_number):
    return lax.dynamic_index_in_dim(table, row_number, 0, keepdims=False)


def range_part(array, part_index, part_width):
    return lax.dynamic_slice_in_dim(array, part_index * part_width, part_width, 2)


def local(subimages, range_kernel, weights0, starts0, weights1, starts1, owners):
    aper_index = lax.axis_index("aperture")
    beam_index = lax.axis_index("beam")
    halo_blocks = (NW - 2) // 2 + REACH
    margin = halo_blocks * BLK
    subimage = subimages[0]
    kernel = range_kernel[0]
    local_blocks = subimage.shape[1] // BLK
    source = resample(subimage, kernel)
    padded = extended(source, (("beam", 1),), margin)
    half_width = subimage.shape[2] // 2
    half_index = aper_index % 2
    lowest_first = beam_index * local_blocks - halo_blocks
    own_starts = table_row(starts0, aper_index)
    all_beams = interpolate(padded, weights0[0], own_starts, lowest_first)
    own_beams = range_part(all_beams, half_index, half_width)
    other_beams = partner(range_part(all_beams, 1 - half_index, half_width), "aperture", 0)
    level_one = (own_beams.astype(jnp.float32) + other_beams.astype(jnp.float32)).astype(
        jnp.bfloat16
    )
    padded_one = extended(level_one, (("beam", 1),), margin)
    quarter_width = half_width // 2
    quarter_index = aper_index // 2 % 2
    lowest_second = beam_index * (2 * local_blocks) - halo_blocks
    own_second = table_row(starts1, aper_index)
    final_beams = interpolate(padded_one, weights1[0], own_second, lowest_second)
    own_final = range_part(final_beams, quarter_index, quarter_width)
    other_final = partner(range_part(final_beams, 1 - quarter_index, quarter_width), "aperture", 1)
    quarter_piece = (own_final.astype(jnp.float32) + other_final.astype(jnp.float32)).astype(
        jnp.bfloat16
    )
    beam_count = lax.axis_size("beam")
    sector_count = owners.shape[1]
    capacity = max(2, 2 * sector_count // beam_count)
    per_sector = quarter_piece.reshape(2, sector_count, OS, quarter_width)
    target = owners[0, :, 0]
    one_hot = (target[:, None] == jnp.arange(beam_count, dtype=jnp.int32)[None, :]).astype(
        jnp.int32
    )
    earlier = jnp.cumsum(one_hot, axis=0) - one_hot
    slot_rank = jnp.sum(earlier * one_hot, axis=1)
    slot_index = target * capacity + slot_rank
    selector = (
        slot_index[None, :] == jnp.arange(beam_count * capacity, dtype=jnp.int32)[:, None]
    ).astype(jnp.bfloat16)
    outgoing = jnp.einsum(
        "so,copq->scpq", selector, per_sector, preferred_element_type=jnp.float32
    ).astype(jnp.bfloat16)
    received = lax.all_to_all(outgoing, "beam", split_axis=0, concat_axis=0, tiled=True)
    return received[None]


def solution(mesh):
    return jax.shard_map(
        local,
        mesh=mesh,
        in_specs=(
            P("aperture", None, "beam", None),
            P("aperture", None, None, None),
            P("aperture", "beam", None, None, None),
            P(None, "beam"),
            P("aperture", "beam", None, None, None),
            P(None, "beam"),
            P("aperture", "beam", None),
        ),
        out_specs=P("aperture", "beam", None, None, None),
        check_vma=False,
    )
```

profile of v0, /device:TPU:0, one launch (start us, length us, event | category | flops | bytes accessed | tf_op | source)
XLA Modules:
  0.0 111.0 jit_solution(11223997635640160122)
XLA Ops:
  0.0 1.5 %fusion.28 = f32[256,512]{1,0:T(8,128)S(1)} fusion(bf16[1,2,512,512]{3,2,1,0:T(8,128)(2,1)} %param.8, bf16[1,2,256,512]{3,2,1,0:T(8,128)(2,1)} %param.7), kind=kOutput, calls=%fused_computation.54 | convolution fusion | flops 134217728 | bytes 1310720 | tf_op jit(solution)/shard_map/dot_general | solution.py:43
  1.5 0.0 copy-start.6
  1.6 0.0 copy-start.4
  1.6 1.5 %fusion.32 = f32[256,512]{1,0:T(8,128)S(1)} fusion(bf16[1,2,512,512]{3,2,1,0:T(8,128)(2,1)} %param.8, bf16[1,2,256,512]{3,2,1,0:T(8,128)(2,1)} %param.7), kind=kOutput, calls=%fused_computation.58 | convolution fusion | flops 134217728 | bytes 1310720 | tf_op jit(solution)/shard_map/dot_general | solution.py:40
  3.1 0.0 copy-done.3
  3.1 0.0 copy-done.2
  3.1 0.3 fusion.16
  3.4 0.3 fusion.17
  3.7 0.8 fusion.39
  4.5 4.9 %collective-permute-start = (bf16[2,192,512]{2,1,0:T(8,128)(2,1)}, bf16[2,192,512]{2,1,0:T(8,128)(2,1)S(1)}, u32[]{:S(2)}, u32[]{:S(2)}) collective-permute-start(bf16[2,192,512]{2,1,0:T(8,128)(2,1)} %get-tuple-element.37), channel_id=1, source_target_pairs={{0,1},{1,2},{2,3},{4,5},{5,6},{6,7},{8,9},{9,10},{10,11},{12,13},{... | collective-permute-start | bytes 1179656 | tf_op jit(solution)/shard_map/ppermute | solution.py:20
  9.4 1.3 %collective-permute-start.1 = (bf16[2,192,512]{2,1,0:T(8,128)(2,1)S(1)}, bf16[2,192,512]{2,1,0:T(8,128)(2,1)S(1)}, u32[]{:S(2)}, u32[]{:S(2)}) collective-permute-start(bf16[2,192,512]{2,1,0:T(8,128)(2,1)S(1)} %get-tuple-element.38), channel_id=1, source_target_pairs={{1,0},{2,1},{3,2},{5,4},{6,5},{7,6},{9,8},{10,9},{11,10},{13,12},{... | collective-permute-start | bytes 1179656 | tf_op jit(solution)/shard_map/ppermute | solution.py:22
  10.8 0.0 copy-done.6
  10.8 0.2 fusion.54
  11.0 0.1 copy.29
  11.1 0.0 copy-done.4
  11.2 6.9 %collective-permute-done = bf16[2,192,512]{2,1,0:T(8,128)(2,1)S(1)} collective-permute-done((bf16[2,192,512]{2,1,0:T(8,128)(2,1)}, bf16[2,192,512]{2,1,0:T(8,128)(2,1)S(1)}, u32[]{:S(2)}, u32[]{:S(2)}) %collective-permute-start) | collective-permute-done | bytes 393248 | tf_op jit(solution)/shard_map/ppermute | solution.py:20
  18.1 3.8 %collective-permute-done.1 = bf16[2,192,512]{2,1,0:T(8,128)(2,1)S(1)} collective-permute-done((bf16[2,192,512]{2,1,0:T(8,128)(2,1)S(1)}, bf16[2,192,512]{2,1,0:T(8,128)(2,1)S(1)}, u32[]{:S(2)}, u32[]{:S(2)}) %collective-permute-start.1) | collective-permute-done | bytes 393248 | tf_op jit(solution)/shard_map/ppermute | solution.py:22
  21.9 0.1 pad_maximum_fusion
  22.0 9.0 %while.1 = (s32[]{:T(128)}, bf16[2,640,512]{2,1,0:T(8,128)(2,1)S(1)}, s32[4,3]{1,0:T(4,128)S(1)}, bf16[4,2,320,512]{3,2,0,1:T(8,128)(2,1)}, s32[]{:T(128)}) while((s32[]{:T(128)}, bf16[2,640,512]{2,1,0:T(8,128)(2,1)S(1)}, s32[4,3]{1,0:T(4,128)S(1)}, bf16[4,2,320,512]{3,2,0,1:T(8,128)(2,1)}, s32[]{:T(128)}) %tuple.22), condition=%wide.while_cond, body=%wide.while_body.sunk | while | flops 2 | bytes 1311841 | solution.py:57
  22.0 0.6 slice.175
  22.6 1.7 %bitcast_dynamic-update-slice_fusion.2 = bf16[4,2,320,512]{3,2,0,1:T(8,128)(2,1)} fusion(bf16[4,2,320,512]{3,2,0,1:T(8,128)(2,1)} %get-tuple-element.72, s32[]{:T(128)} %get-tuple-element.69, bf16[2,640,512]{2,1,0:T(8,128)(2,1)S(1)} %get-tuple-element.75, s32[]{:T(128)} %bitcast.103), kind=kLoop, calls=%fused_computation.1.clone.1 | loop fusion | bytes 1311744 | tf_op jit(solution)/shard_map/vmap()/gather
  24.3 0.6 slice.175
  24.9 1.7 %bitcast_dynamic-update-slice_fusion.2 = bf16[4,2,320,512]{3,2,0,1:T(8,128)(2,1)} fusion(bf16[4,2,320,512]{3,2,0,1:T(8,128)(2,1)} %get-tuple-element.72, s32[]{:T(128)} %get-tuple-element.69, bf16[2,640,512]{2,1,0:T(8,128)(2,1)S(1)} %get-tuple-element.75, s32[]{:T(128)} %bitcast.103), kind=kLoop, calls=%fused_computation.1.clone.1 | loop fusion | bytes 1311744 | tf_op jit(solution)/shard_map/vmap()/gather
  26.5 0.6 slice.175
  27.1 1.7 %bitcast_dynamic-update-slice_fusion.2 = bf16[4,2,320,512]{3,2,0,1:T(8,128)(2,1)} fusion(bf16[4,2,320,512]{3,2,0,1:T(8,128)(2,1)} %get-tuple-element.72, s32[]{:T(128)} %get-tuple-element.69, bf16[2,640,512]{2,1,0:T(8,128)(2,1)S(1)} %get-tuple-element.75, s32[]{:T(128)} %bitcast.103), kind=kLoop, calls=%fused_computation.1.clone.1 | loop fusion | bytes 1311744 | tf_op jit(solution)/shard_map/vmap()/gather
  28.8 0.6 slice.175
  29.4 1.7 %bitcast_dynamic-update-slice_fusion.2 = bf16[4,2,320,512]{3,2,0,1:T(8,128)(2,1)} fusion(bf16[4,2,320,512]{3,2,0,1:T(8,128)(2,1)} %get-tuple-element.72, s32[]{:T(128)} %get-tuple-element.69, bf16[2,640,512]{2,1,0:T(8,128)(2,1)S(1)} %get-tuple-element.75, s32[]{:T(128)} %bitcast.103), kind=kLoop, calls=%fused_computation.1.clone.1 | loop fusion | bytes 1311744 | tf_op jit(solution)/shard_map/vmap()/gather
  31.0 1.9 %fusion = f32[4,512,128]{1,2,0:T(8,128)S(1)} fusion(bf16[4,2,320,512]{3,2,0,1:T(8,128)(2,1)} %get-tuple-element.12, bf16[4,2,128,320]{2,3,0,1:T(8,128)(2,1)S(1)} %bitcast.108), kind=kOutput, calls=%fused_computation.11 | convolution fusion | flops 167772160 | bytes 2686976 | tf_op jit(solution)/shard_map/npw,nwr->npr/dot_general | solution.py:63
  33.0 0.2 copy-done.1
  33.2 0.5 fusion.4
  33.7 0.5 fusion.9
  34.2 0.8 copy.34
  35.0 0.5 fusion.6
  35.5 0.8 copy.33
  36.3 1.6 %fusion.24 = bf16[2,512,256]{2,0,1:T(2,128)(2,1)S(1)} fusion(s32[]{:T(128)S(6)} %select_n.57, bf16[1,512,512]{2,0,1:T(2,128)(2,1)S(1)} %copy.33, bf16[1,512,512]{2,0,1:T(2,128)(2,1)S(1)} %copy.34), kind=kLoop, calls=%fused_computation.48 | loop fusion | flops 1048576 | bytes 1572868 | tf_op jit(solution)/shard_map/stack | solution.py:66
  37.9 0.1 collective-permute-start.2
  38.0 1.9 %collective-permute-done.2 = bf16[2,512,256]{2,0,1:T(2,128)(2,1)S(1)} collective-permute-done((bf16[2,512,256]{2,0,1:T(2,128)(2,1)S(1)}, bf16[2,512,256]{2,0,1:T(2,128)(2,1)S(1)}, u32[]{:S(2)}, u32[]{:S(2)}) %collective-permute-start.2) | collective-permute-done | bytes 524320 | tf_op jit(solution)/shard_map/ppermute | solution.py:36
  39.9 1.6 %add_convert_fusion.1 = bf16[2,512,256]{2,0,1:T(2,128)(2,1)S(1)} fusion(bf16[2,512,256]{2,0,1:T(2,128)(2,1)S(1)} %collective-permute-done.2, s32[]{:T(128)S(6)} %select_n.56, bf16[1,512,512]{2,0,1:T(2,128)(2,1)S(1)} %copy.34, bf16[1,512,512]{2,0,1:T(2,128)(2,1)S(1)} %copy.33), kind=kLoop, calls=%fused_computation.37 | loop fusion | flops 1835008 | bytes 2097156 | tf_op jit(solution)/shard_map/convert_element_type | solution.py:95
  41.5 0.3 fusion.61
  41.8 3.5 %collective-permute-start.3 = (bf16[2,192,256]{2,0,1:T(2,128)(2,1)S(1)}, bf16[2,192,256]{2,0,1:T(2,128)(2,1)S(1)}, u32[]{:S(2)}, u32[]{:S(2)}) collective-permute-start(bf16[2,192,256]{2,0,1:T(2,128)(2,1)S(1)} %get-tuple-element.35), channel_id=1, source_target_pairs={{0,1},{1,2},{2,3},{4,5},{5,6},{6,7},{8,9},{9,10},{10,11},{12,13},{... | collective-permute-start | bytes 589832 | tf_op jit(solution)/shard_map/ppermute | solution.py:20
  45.3 1.5 %collective-permute-start.4 = (bf16[2,192,256]{2,0,1:T(2,128)(2,1)S(1)}, bf16[2,192,256]{2,0,1:T(2,128)(2,1)S(1)}, u32[]{:S(2)}, u32[]{:S(2)}) collective-permute-start(bf16[2,192,256]{2,0,1:T(2,128)(2,1)S(1)} %get-tuple-element.36), channel_id=1, source_target_pairs={{1,0},{2,1},{3,2},{5,4},{6,5},{7,6},{9,8},{10,9},{11,10},{13,12},{... | collective-permute-start | bytes 589832 | tf_op jit(solution)/shard_map/ppermute | solution.py:22
  46.8 2.5 %copy.55 = bf16[1,8,2,128,320]{3,4,1,2,0:T(8,128)(2,1)} copy(bf16[1,8,2,128,320]{3,4,2,1,0:T(8,128)(2,1)} %param.11) | data formatting | bytes 2621440 | tf_op args[4]
  49.3 0.7 fusion.59
  50.0 0.0 collective-permute-done.3
  50.0 3.9 %collective-permute-done.4 = bf16[2,192,256]{2,0,1:T(2,128)(2,1)S(1)} collective-permute-done((bf16[2,192,256]{2,0,1:T(2,128)(2,1)S(1)}, bf16[2,192,256]{2,0,1:T(2,128)(2,1)S(1)}, u32[]{:S(2)}, u32[]{:S(2)}) %collective-permute-start.4) | collective-permute-done | bytes 196640 | tf_op jit(solution)/shard_map/ppermute | solution.py:22
  53.8 1.3 %pad_maximum_fusion.1 = bf16[2,896,256]{2,0,1:T(2,128)(2,1)S(1)} fusion(bf16[2,192,256]{2,0,1:T(2,128)(2,1)S(1)} %collective-permute-done.4, bf16[2,512,256]{2,0,1:T(2,128)(2,1)S(1)} %add_convert_fusion.1, bf16[2,192,256]{2,0,1:T(2,128)(2,1)S(1)} %collective-permute-done.3), kind=kLoop, calls=%fused_computation.38 | loop fusion | flops 917504 | bytes 1835008 | tf_op jit(solution)/shard_map/concatenate | solution.py:18
  55.1 7.0 %gather_fusion = bf16[8,2,320,256]{3,1,2,0:T(2,128)(2,1)S(1)} fusion(bf16[2,896,256]{2,0,1:T(2,128)(2,1)S(1)} %pad_maximum_fusion.1, s32[8]{0:T(128)S(1)} %fusion.59), kind=kCustom, calls=%fused_computation | custom fusion | bytes 5242976 | tf_op jit(solution)/shard_map/vmap()/gather | solution.py:57
  62.2 0.0 copy-start
  62.2 4.8 %fusion.60 = (bf16[8,1,320,256]{3,1,2,0:T(2,128)(2,1)S(1)}, bf16[8,1,320,256]{3,1,2,0:T(2,128)(2,1)S(1)}) fusion(bf16[8,2,320,256]{3,1,2,0:T(2,128)(2,1)S(1)} %gather_fusion), kind=kLoop, calls=%fused_computation.97 | loop fusion | bytes 5242880 | tf_op jit(solution)/shard_map/slice | solution.py:62
  67.0 0.5 fusion.22
  67.5 0.5 fusion.23
  68.0 0.5 fusion.13
  68.5 0.0 copy-start.5
  68.5 0.5 fusion.12
  69.0 1.6 %collective-permute-start.5 = (bf16[2,1024,128]{2,1,0:T(8,128)(2,1)S(1)}, bf16[2,1024,128]{2,1,0:T(8,128)(2,1)S(1)}, u32[]{:S(2)}, u32[]{:S(2)}) collective-permute-start(bf16[2,1024,128]{2,1,0:T(8,128)(2,1)S(1)} %fusion.26), channel_id=1, source_target_pairs={{0,8},{8,0},{4,12},{12,4},{16,24},{24,16},{20,28},{28,20},{1,9},{9... | collective-permute-start | bytes 1572872 | tf_op jit(solution)/shard_map/ppermute | solution.py:36
  70.6 0.0 copy-done.5
  70.6 0.1 fusion.48
  70.7 0.2 select_reduce_fusion
  70.9 11.0 %collective-permute-done.5 = bf16[2,1024,128]{2,1,0:T(8,128)(2,1)S(1)} collective-permute-done((bf16[2,1024,128]{2,1,0:T(8,128)(2,1)S(1)}, bf16[2,1024,128]{2,1,0:T(8,128)(2,1)S(1)}, u32[]{:S(2)}, u32[]{:S(2)}) %collective-permute-start.5) | collective-permute-done | bytes 524320 | tf_op jit(solution)/shard_map/ppermute | solution.py:36
  81.9 0.1 add_convert_fusion
  82.1 0.6 convolution_convert_fusion
  82.7 0.4 copy.39
  83.1 27.0 %all_to_all.5 = bf16[32,2,64,128]{3,2,1,0:T(8,128)(2,1)S(1)} all-to-all(bf16[32,2,64,128]{3,2,1,0:T(8,128)(2,1)S(1)} %copy.39), channel_id=1, replica_groups=mesh['aperture'=8,'beam'=4] {'beam'}, dimensions={0} | all-to-all | bytes 2097152 | tf_op jit(solution)/shard_map/all_to_all | solution.py:126
  110.0 1.0 copy.65
  (16 shorter events, 0.2 us)
Async XLA Ops:
  0.0 3.1 %copy-start.3 = (bf16[1,2,256,512]{3,2,1,0:T(8,128)(2,1)S(1)}, bf16[1,2,256,512]{3,2,1,0:T(8,128)(2,1)}, u32[]{:S(2)}) copy-start(bf16[1,2,256,512]{3,2,1,0:T(8,128)(2,1)} %param.7) | copy-start | bytes 1572868
  0.0 3.1 %copy-start.2 = (bf16[1,2,512,512]{3,2,1,0:T(8,128)(2,1)S(1)}, bf16[1,2,512,512]{3,2,1,0:T(8,128)(2,1)}, u32[]{:S(2)}) copy-start(bf16[1,2,512,512]{3,2,1,0:T(8,128)(2,1)} %param.8) | copy-start | bytes 3145732
  1.5 9.2 %copy-start.6 = (s32[8,4]{0,1:T(4,128)S(1)}, s32[8,4]{0,1:T(4,128)}, u32[]{:S(2)}) copy-start(s32[8,4]{0,1:T(4,128)} %param.10) | copy-start | bytes 388
  1.6 9.6 %copy-start.4 = (bf16[1,4,2,128,320]{3,4,2,1,0:T(8,128)(2,1)S(1)}, bf16[1,4,2,128,320]{3,4,2,1,0:T(8,128)(2,1)}, u32[]{:S(2)}) copy-start(bf16[1,4,2,128,320]{3,4,2,1,0:T(8,128)(2,1)} %param.9) | copy-start | bytes 1966084
  4.5 13.6 %collective-permute-start = (bf16[2,192,512]{2,1,0:T(8,128)(2,1)}, bf16[2,192,512]{2,1,0:T(8,128)(2,1)S(1)}, u32[]{:S(2)}, u32[]{:S(2)}) collective-permute-start(bf16[2,192,512]{2,1,0:T(8,128)(2,1)} %get-tuple-element.37), channel_id=1, source_target_pairs={{0,1},{1,2},{2,3},{4,5},{5,6},{6,7},{8,9},{9,10},{10,11},{12,13},{... | collective-permute-start | bytes 1179656 | tf_op jit(solution)/shard_map/ppermute | solution.py:20
  9.4 12.5 %collective-permute-start.1 = (bf16[2,192,512]{2,1,0:T(8,128)(2,1)S(1)}, bf16[2,192,512]{2,1,0:T(8,128)(2,1)S(1)}, u32[]{:S(2)}, u32[]{:S(2)}) collective-permute-start(bf16[2,192,512]{2,1,0:T(8,128)(2,1)S(1)} %get-tuple-element.38), channel_id=1, source_target_pairs={{1,0},{2,1},{3,2},{5,4},{6,5},{7,6},{9,8},{10,9},{11,10},{13,12},{... | collective-permute-start | bytes 1179656 | tf_op jit(solution)/shard_map/ppermute | solution.py:22
  31.0 2.1 %copy-start.1 = (bf16[4,2,320,512]{3,2,0,1:T(8,128)(2,1)S(1)}, bf16[4,2,320,512]{3,2,0,1:T(8,128)(2,1)}, u32[]{:S(2)}) copy-start(bf16[4,2,320,512]{3,2,0,1:T(8,128)(2,1)} %get-tuple-element.12) | copy-start | bytes 7864324
  37.9 2.0 %collective-permute-start.2 = (bf16[2,512,256]{2,0,1:T(2,128)(2,1)S(1)}, bf16[2,512,256]{2,0,1:T(2,128)(2,1)S(1)}, u32[]{:S(2)}, u32[]{:S(2)}) collective-permute-start(bf16[2,512,256]{2,0,1:T(2,128)(2,1)S(1)} %fusion.24), channel_id=1, source_target_pairs={{0,4},{4,0},{8,12},{12,8},{16,20},{20,16},{24,28},{28,24},{1,5},{5... | collective-permute-start | bytes 1572872 | tf_op jit(solution)/shard_map/ppermute | solution.py:36
  41.8 8.2 %collective-permute-start.3 = (bf16[2,192,256]{2,0,1:T(2,128)(2,1)S(1)}, bf16[2,192,256]{2,0,1:T(2,128)(2,1)S(1)}, u32[]{:S(2)}, u32[]{:S(2)}) collective-permute-start(bf16[2,192,256]{2,0,1:T(2,128)(2,1)S(1)} %get-tuple-element.35), channel_id=1, source_target_pairs={{0,1},{1,2},{2,3},{4,5},{5,6},{6,7},{8,9},{9,10},{10,11},{12,13},{... | collective-permute-start | bytes 589832 | tf_op jit(solution)/shard_map/ppermute | solution.py:20
  45.3 8.6 %collective-permute-start.4 = (bf16[2,192,256]{2,0,1:T(2,128)(2,1)S(1)}, bf16[2,192,256]{2,0,1:T(2,128)(2,1)S(1)}, u32[]{:S(2)}, u32[]{:S(2)}) collective-permute-start(bf16[2,192,256]{2,0,1:T(2,128)(2,1)S(1)} %get-tuple-element.36), channel_id=1, source_target_pairs={{1,0},{2,1},{3,2},{5,4},{6,5},{7,6},{9,8},{10,9},{11,10},{13,12},{... | collective-permute-start | bytes 589832 | tf_op jit(solution)/shard_map/ppermute | solution.py:22
  62.2 4.8 %copy-start = (bf16[1,8,2,128,320]{3,4,1,2,0:T(8,128)(2,1)S(1)}, bf16[1,8,2,128,320]{3,4,1,2,0:T(8,128)(2,1)}, u32[]{:S(2)}) copy-start(bf16[1,8,2,128,320]{3,4,1,2,0:T(8,128)(2,1)} %copy.55) | copy-start | bytes 3932164
  68.5 2.1 %copy-start.5 = (s32[1,16,1]{1,2,0:T(1,128)S(1)}, s32[1,16,1]{1,2,0:T(1,128)}, u32[]{:S(2)}) copy-start(s32[1,16,1]{1,2,0:T(1,128)} %param.13) | copy-start | bytes 196
  69.0 12.9 %collective-permute-start.5 = (bf16[2,1024,128]{2,1,0:T(8,128)(2,1)S(1)}, bf16[2,1024,128]{2,1,0:T(8,128)(2,1)S(1)}, u32[]{:S(2)}, u32[]{:S(2)}) collective-permute-start(bf16[2,1024,128]{2,1,0:T(8,128)(2,1)S(1)} %fusion.26), channel_id=1, source_target_pairs={{0,8},{8,0},{4,12},{12,4},{16,24},{24,16},{20,28},{28,20},{1,9},{9... | collective-permute-start | bytes 1572872 | tf_op jit(solution)/shard_map/ppermute | solution.py:36
where the time goes:
time: 111 us
  waiting for transfers between devices  27.5 us (25%)
  blocking collectives  27 us (24%)
  local copies, waits for them, and re-layouts  26.9 us (24%)
  starting transfers between devices  12.8 us (12%)
  matrix products  9.61 us (9%)
  other arithmetic  6.82 us (6%)
    all_to_all x1, blocking collectives, local(): lax.all_to_all(outgoing, 'beam', split_axis=0, concat_axis=0, tiled=True)  27 us
    ppermute x2, waiting for transfers between devices, partner(): return lax.ppermute(block, axis, route)  12.9 us
    gather x12, local copies, waits for them, and re-layouts  9.01 us
    ppermute x2, starting transfers between devices, extended(): lax.ppermute(tail, axis, [(i, (i + 1) % count) for i in range(ends)])  8.41 us
    ppermute x2, waiting for transfers between devices, extended(): lax.ppermute(head, axis, [((i + 1) % count, i) for i in range(ends)])  7.67 us
    gather x1, local copies, waits for them, and re-layouts, cut_window(): lax.dynamic_slice_in_dim(padded, (first_block - lowest_block) * BLK, wind...  7.02 us
    ppermute x2, waiting for transfers between devices, extended(): lax.ppermute(tail, axis, [(i, (i + 1) % count) for i in range(ends)])  6.93 us
    slice x1, local copies, waits for them, and re-layouts, interpolate(): windows[:, 1]  4.78 us
  transfers between devices with their start and end apart: 6, of which 5 were waited for; matrix products, arithmetic and copies ran while one was open for 3% of the time, Pallas kernels for 0%

commit v1 on v0

v1 whole, which is shorter than its diff:
```python
import functools

import jax
import jax.numpy as jnp
from jax import lax
from jax.experimental import pallas as pl
from jax.experimental.pallas import tpu as pltpu
from jax.sharding import PartitionSpec as P

BLK = 32
NW = 10
REACH = 2
OS = 64
MARGIN_BLOCKS = (NW - 2) // 2 + REACH
VMEM_LIMIT = 24 * 1024 * 1024
ANY = pl.BlockSpec(memory_space=pl.ANY)
VMEM = pl.BlockSpec(memory_space=pltpu.VMEM)
SMEM = pl.BlockSpec(memory_space=pltpu.SMEM)


def params():
    return pltpu.CompilerParams(vmem_limit_bytes=VMEM_LIMIT)


def cost(macs, moved):
    return pl.CostEstimate(flops=2 * macs, bytes_accessed=moved, transcendentals=0)


def swap_route(count, first):
    route = []
    for low in range(first, count - 1, 2):
        route += [(low, low + 1), (low + 1, low)]
    return route


def exchange_edges(cells, axis, width):
    count = lax.axis_size(axis)
    even = lax.axis_index(axis) % 2 == 0
    rows = cells.shape[1]
    tail_start = jnp.where(even, rows - width, 0)
    head_start = jnp.where(even, 0, rows - width)
    first = lax.dynamic_slice_in_dim(cells, tail_start, width, 1)
    second = lax.dynamic_slice_in_dim(cells, head_start, width, 1)
    return (
        lax.ppermute(first, axis, swap_route(count, 0)),
        lax.ppermute(second, axis, swap_route(count, 1)),
    )


def partner(block, axis, distance):
    count = lax.axis_size(axis)
    route = []
    for low in range(count):
        high = low | 1 << distance
        if high != low and high < count:
            route += [(low, high), (high, low)]
    return lax.ppermute(block, axis, route)


def dot(left, right):
    return jnp.dot(left, right, preferred_element_type=jnp.float32)


def resample_into(out_ref, out_start, rows, child_ref, kernel_ref):
    real, imag = child_ref[0], child_ref[1]
    k_real, k_imag = kernel_ref[0], kernel_ref[1]
    place = pl.ds(out_start, rows)
    out_ref[0, place, :] = (dot(real, k_real) - dot(imag, k_imag)).astype(jnp.bfloat16)
    out_ref[1, place, :] = (dot(real, k_imag) + dot(imag, k_real)).astype(jnp.bfloat16)


def resample_kernel(child_ref, kernel_ref, out_ref):
    resample_into(out_ref, 0, child_ref.shape[1], child_ref, kernel_ref)


def resample(child, kernel):
    return pl.pallas_call(
        resample_kernel,
        out_shape=jax.ShapeDtypeStruct((2, child.shape[1], kernel.shape[2]), jnp.bfloat16),
        in_specs=[VMEM, VMEM],
        out_specs=VMEM,
        compiler_params=params(),
        cost_estimate=cost(4 * child.shape[1] * kernel.shape[1] * kernel.shape[2], 2**21),
        name="resample_own",
    )(child, kernel)


def complex_window(weights_ref, sector, real, imag):
    beams = weights_ref.shape[1] // 2
    with_real = dot(weights_ref[sector], real)
    with_imag = dot(weights_ref[sector], imag)
    return (
        (with_real[:beams] - with_imag[beams:]).astype(jnp.bfloat16),
        (with_imag[:beams] + with_real[beams:]).astype(jnp.bfloat16),
    )


def first_level_kernel(
    starts_ref, side_ref, own_ref, first_ref, second_ref, kernel_ref, weights_ref,
    keep_ref, send_ref, padded,
):
    margin = first_ref.shape[1]
    rows = own_ref.shape[1]
    sectors, stacked, window = weights_ref.shape
    beams = stacked // 2
    even, half = side_ref[0], side_ref[1]
    width = keep_ref.shape[2]
    padded[:, margin : margin + rows, :] = own_ref[...]
    far = margin + rows
    first_at = pl.multiple_of(even * far, BLK)
    second_at = pl.multiple_of((1 - even) * far, BLK)
    resample_into(padded, first_at, margin, first_ref, kernel_ref)
    resample_into(padded, second_at, margin, second_ref, kernel_ref)
    for sector in range(sectors):
        place = pl.ds(pl.multiple_of(starts_ref[sector] * BLK, BLK), window)
        out = pl.ds(sector * beams, beams)
        for ref, side in ((send_ref, 1 - half), (keep_ref, half)):
            columns = pl.ds(pl.multiple_of(side * width, 128), width)
            real, imag = complex_window(
                weights_ref, sector, padded[0, place, columns], padded[1, place, columns]
            )
            ref[0, out, :] = real
            ref[1, out, :] = imag


def first_level(starts, side, own, first, second, kernel, weights):
    sectors, stacked, window = weights.shape
    rng = own.shape[2]
    margin, rows = first.shape[1], own.shape[1]
    shape = jax.ShapeDtypeStruct((2, sectors * stacked // 2, rng // 2), jnp.bfloat16)
    return pl.pallas_call(
        first_level_kernel,
        out_shape=(shape, shape),
        in_specs=[SMEM, SMEM] + [VMEM] * 5,
        out_specs=(VMEM, VMEM),
        scratch_shapes=[pltpu.VMEM((2, rows + 2 * margin, rng), jnp.bfloat16)],
        compiler_params=params(),
        cost_estimate=cost(sectors * 2 * stacked * window * rng + 8 * margin * rng * rng, 2**22),
        name="first_level",
    )(starts, side, own, first, second, kernel, weights)


def second_level_kernel(
    starts_ref, side_ref, own_ref, first_ref, second_ref, weights_ref,
    keep_ref, send_ref, padded,
):
    margin = first_ref.shape[1]
    rows = own_ref.shape[1]
    sectors, stacked, window = weights_ref.shape
    beams = stacked // 2
    even, quarter = side_ref[0], side_ref[1]
    width = keep_ref.shape[3]
    padded[:, margin : margin + rows, :] = own_ref[...]
    far = margin + rows
    padded[:, pl.ds(pl.multiple_of(even * far, BLK), margin), :] = first_ref[...]
    padded[:, pl.ds(pl.multiple_of((1 - even) * far, BLK), margin), :] = second_ref[...]
    per = beams // OS
    for sector in range(sectors):
        place = pl.ds(pl.multiple_of(starts_ref[sector] * BLK, BLK), window)
        parts = complex_window(weights_ref, sector, padded[0, place, :], padded[1, place, :])

        def store(swapped):
            for ref, column in ((keep_ref, swapped), (send_ref, 1 - swapped)):
                for part in range(2):
                    for piece in range(per):
                        ref[sector * per + piece, part] = parts[part][
                            piece * OS : (piece + 1) * OS, column * width : (column + 1) * width
                        ]

        pl.when(quarter == 0)(functools.partial(store, 0))
        pl.when(quarter == 1)(functools.partial(store, 1))


def second_level(starts, side, own, first, second, weights):
    sectors, stacked, window = weights.shape
    rng = own.shape[2]
    margin, rows = first.shape[1], own.shape[1]
    shape = jax.ShapeDtypeStruct(
        (sectors * stacked // 2 // OS, 2, OS, rng // 2), jnp.bfloat16
    )
    return pl.pallas_call(
        second_level_kernel,
        out_shape=(shape, shape),
        in_specs=[SMEM, SMEM] + [VMEM] * 4,
        out_specs=(VMEM, VMEM),
        scratch_shapes=[pltpu.VMEM((2, rows + 2 * margin, rng), jnp.bfloat16)],
        compiler_params=params(),
        cost_estimate=cost(sectors * 2 * stacked * window * rng, 2**22),
        name="second_level",
    )(starts, side, own, first, second, weights)


def slots_kernel(slot_ref, keep_ref, other_ref, out_ref):
    out_ref[...] = jnp.zeros_like(out_ref)
    for sector in range(keep_ref.shape[0]):
        total = keep_ref[sector].astype(jnp.float32) + other_ref[sector].astype(jnp.float32)
        out_ref[slot_ref[sector]] = total.astype(jnp.bfloat16)


def fill_slots(slot, keep, other, slots):
    return pl.pallas_call(
        slots_kernel,
        out_shape=jax.ShapeDtypeStruct((slots,) + keep.shape[1:], jnp.bfloat16),
        in_specs=[SMEM, VMEM, VMEM],
        out_specs=VMEM,
        compiler_params=params(),
        cost_estimate=cost(0, 2**21),
        name="fill_slots",
    )(slot, keep, other)


def stacked_weights(weights):
    return weights[0].reshape(weights.shape[1], -1, weights.shape[4])


def table_row(table, row_number):
    return lax.dynamic_index_in_dim(table, row_number, 0, keepdims=False)


def local(subimages, range_kernel, weights0, starts0, weights1, starts1, owners):
    aper_index = lax.axis_index("aperture")
    beam_index = lax.axis_index("beam")
    beam_count = lax.axis_size("beam")
    margin = MARGIN_BLOCKS * BLK
    subimage = subimages[0]
    kernel = range_kernel[0]
    local_blocks = subimage.shape[1] // BLK
    even = (beam_index % 2 == 0).astype(jnp.int32)

    first, second = exchange_edges(subimage, "beam", margin)
    own = resample(subimage, kernel)
    begin0 = table_row(starts0, aper_index) - (beam_index * local_blocks - MARGIN_BLOCKS)
    side0 = jnp.stack([even, aper_index % 2])
    keep, send = first_level(
        begin0, side0, own, first, second, kernel, stacked_weights(weights0)
    )
    other = partner(send, "aperture", 0)
    level_one = (keep.astype(jnp.float32) + other.astype(jnp.float32)).astype(jnp.bfloat16)

    first, second = exchange_edges(level_one, "beam", margin)
    begin1 = table_row(starts1, aper_index) - (beam_index * 2 * local_blocks - MARGIN_BLOCKS)
    side1 = jnp.stack([even, aper_index // 2 % 2])
    keep, send = second_level(
        begin1, side1, level_one, first, second, stacked_weights(weights1)
    )
    other = partner(send, "aperture", 1)

    sector_count = owners.shape[1]
    capacity = max(2, 2 * sector_count // beam_count)
    target = owners[0, :, 0]
    one_hot = (target[:, None] == jnp.arange(beam_count, dtype=jnp.int32)[None, :]).astype(
        jnp.int32
    )
    earlier = jnp.cumsum(one_hot, axis=0) - one_hot
    slot_rank = jnp.sum(earlier * one_hot, axis=1)
    slot_index = target * capacity + slot_rank
    outgoing = fill_slots(slot_index, keep, other, beam_count * capacity)
    received = lax.all_to_all(outgoing, "beam", split_axis=0, concat_axis=0, tiled=True)
    return received[None]


def solution(mesh):
    return jax.shard_map(
        local,
        mesh=mesh,
        in_specs=(
            P("aperture", None, "beam", None),
            P("aperture", None, None, None),
            P("aperture", "beam", None, None, None),
            P(None, "beam"),
            P("aperture", "beam", None, None, None),
            P(None, "beam"),
            P("aperture", "beam", None),
        ),
        out_specs=P("aperture", "beam", None, None, None),
        check_vma=False,
    )
```

time: 111 us -> 82.5 us (0.74)
  local copies, waits for them, and re-layouts: 26.9 us -> 9.81 us
  matrix products: 9.61 us -> 0 us
  Pallas kernels: 0 us -> 8.33 us
  other arithmetic: 6.82 us -> 1.46 us
  waiting for transfers between devices: 27.5 us -> 22.2 us
  blocking collectives: 27 us -> 30.3 us
  starting transfers between devices: 12.8 us -> 9.89 us
    gather x13 -> x0, local copies, waits for them, and re-layouts: 16 us -> none
    dot_general x13 -> x0, matrix products: 9.61 us -> none  [the longest x2 2.44 us: interpolate(): jnp.einsum('npw,nwr->npr', weights[:, 0], windows[:, 1], preferred_elemen...]
    pallas_call x0 -> x4, Pallas kernels: none -> 8.33 us  [the longest x1 4.03 us: second_level(): pl.pallas_call(second_level_kernel, out_shape=(shape, shape), in_specs=[S...]
    slice x2 -> x0, local copies, waits for them, and re-layouts: 5.05 us -> none  [the longest x1 4.78 us: interpolate(): windows[:, 1]]
    ppermute x4, waiting for transfers between devices: 14.6 us -> 10.2 us  [the longest x2 10.2 us: exchange_edges(): lax.ppermute(first, axis, swap_route(count, 0))]
    unnamed x18 -> x19, local copies, waits for them, and re-layouts: 3.79 us -> 7.73 us
    all_to_all x1, blocking collectives: 27 us -> 30.3 us  [local(): lax.all_to_all(outgoing, 'beam', split_axis=0, concat_axis=0, tiled=True)]
    ppermute x4, starting transfers between devices: 11.2 us -> 8.25 us  [the longest x2 6.91 us: exchange_edges(): lax.ppermute(first, axis, swap_route(count, 0))]
  transfers between devices with their start and end apart: 6 -> 6, of which waited for: 5 -> 3; matrix products, arithmetic and copies ran while one was open for 3% -> 6% of each run, Pallas kernels for 0% -> 1%
where the time goes in v1:
time: 82.5 us; the launch traced here: 82.2 us
  blocking collectives  30.3 us (37%)
  waiting for transfers between devices  22.2 us (27%)
  starting transfers between devices  9.89 us (12%)
  local copies, waits for them, and re-layouts  9.81 us (12%)
  Pallas kernels  8.33 us (10%)
  other arithmetic  1.46 us (2%)
    all_to_all x1, blocking collectives, local(): lax.all_to_all(outgoing, 'beam', split_axis=0, concat_axis=0, tiled=True)  30.3 us
    ppermute x2, waiting for transfers between devices, partner(): return lax.ppermute(block, axis, route)  11.9 us
    ppermute x2, waiting for transfers between devices, exchange_edges(): lax.ppermute(first, axis, swap_route(count, 0))  10.2 us
    unnamed x19, local copies, waits for them, and re-layouts  7.73 us
    ppermute x2, starting transfers between devices, exchange_edges(): lax.ppermute(first, axis, swap_route(count, 0))  6.91 us
    pallas_call x1, Pallas kernels, second_level(): pl.pallas_call(second_level_kernel, out_shape=(shape, shape), in_specs=[S...  4.03 us
    pallas_call x1, Pallas kernels, first_level(): pl.pallas_call(first_level_kernel, out_shape=(shape, shape), in_specs=[SM...  2.81 us
    dynamic_slice x2, local copies, waits for them, and re-layouts, exchange_edges(): second = lax.dynamic_slice_in_dim(cells, head_start, width, 1)  2.09 us
  transfers between devices with their start and end apart: 6, of which 3 were waited for; matrix products, arithmetic and copies ran while one was open for 6% of the time, Pallas kernels for 1%

profile of v1, /device:TPU:0, one launch (start us, length us, event | category | flops | bytes accessed | tf_op | source)
XLA Modules:
  0.0 82.2 jit_solution(10158457243018773811)
XLA Ops:
  0.0 0.0 copy-start
  0.0 0.0 copy-start.7
  0.0 0.0 copy-start.1
  0.0 2.0 %dynamic-slice_bitcast_fusion = (bf16[2,192,512]{2,1,0:T(8,128)(2,1)S(1)}, bf16[2,192,512]{2,1,0:T(8,128)(2,1)}) fusion(bf16[1,2,256,512]{3,2,1,0:T(8,128)(2,1)} %param.7, s32[]{:T(128)S(6)} %select_n.52, s32[]{:T(128)S(6)} %select_n.51), kind=kLoop, calls=%fused_computation.1 | loop fusion | bytes 1572872 | tf_op jit(solution)/shard_map/dynamic_slice | solution.py:43
  2.1 3.0 %collective-permute-start = (bf16[2,192,512]{2,1,0:T(8,128)(2,1)}, bf16[2,192,512]{2,1,0:T(8,128)(2,1)S(1)}, u32[]{:S(2)}, u32[]{:S(2)}) collective-permute-start(bf16[2,192,512]{2,1,0:T(8,128)(2,1)} %get-tuple-element.16), channel_id=1, source_target_pairs={{0,1},{1,0},{2,3},{3,2},{4,5},{5,4},{6,7},{7,6},{8,9},{9,8},{10,11... | collective-permute-start | bytes 1179656 | tf_op jit(solution)/shard_map/ppermute | solution.py:45
  5.1 0.7 collective-permute-start.1
  5.8 1.4 %copy.8 = bf16[1,4,2,128,320]{4,3,2,1,0:T(8,128)(2,1)S(1)} copy(bf16[1,4,2,128,320]{3,4,2,1,0:T(8,128)(2,1)} %param.9) | data formatting | bytes 1310720 | tf_op args[2]
  7.3 0.0 copy-done.7
  7.3 0.2 subtract_reduce_fusion.starts_ref
  7.5 0.0 copy-done
  7.5 0.0 copy-done.1
  7.5 0.7 resample_own.1.own_ref
  8.2 0.1 pad_add_fusion.1.side_ref
  8.3 6.2 %collective-permute-done.first_ref = bf16[2,192,512]{2,1,0:T(8,128)(2,1)S(1)} collective-permute-done((bf16[2,192,512]{2,1,0:T(8,128)(2,1)}, bf16[2,192,512]{2,1,0:T(8,128)(2,1)S(1)}, u32[]{:S(2)}, u32[]{:S(2)}) %collective-permute-start) | collective-permute-done | bytes 393248 | tf_op jit(solution)/shard_map/ppermute | solution.py:45
  14.4 0.0 copy-start.2
  14.4 0.7 copy-done.2
  15.2 0.0 collective-permute-done.1.second_ref
  15.2 0.0 copy-start.4
  15.2 0.7 copy-done.4
  15.9 0.0 copy-start.3
  15.9 1.0 %copy-done.3 = bf16[2,192,512]{2,1,0:T(8,128)(2,1)S(1)} copy-done((bf16[2,192,512]{2,1,0:T(8,128)(2,1)S(1)}, bf16[2,192,512]{2,1,0:T(8,128)(2,1)}, u32[]{:S(2)}) %copy-start.3) | copy-done | bytes 393240
  16.9 0.0 copy-start.5
  16.9 1.0 %copy-done.5 = bf16[2,192,512]{2,1,0:T(8,128)(2,1)S(1)} copy-done((bf16[2,192,512]{2,1,0:T(8,128)(2,1)S(1)}, bf16[2,192,512]{2,1,0:T(8,128)(2,1)}, u32[]{:S(2)}) %copy-start.5) | copy-done | bytes 393240
  17.9 2.8 %first_level.1 = (bf16[2,512,256]{2,1,0:T(8,128)(2,1)S(1)}, bf16[2,512,256]{2,1,0:T(8,128)(2,1)S(1)}) custom-call(s32[4]{0:T(128)S(1)} %subtract_reduce_fusion.starts_ref, s32[2]{0:T(128)S(1)} %pad_add_fusion.1.side_ref, bf16[2,256,512]{2,1,0:T(8,128)(2,1)S(1)} %resample_own.1.own_ref, bf16[2,192,512]{2,1,0:T(8,128)(2,1)S(1)} %copy-done.3, ...), custom_call_target="tpu_custom_call" | custom-call | flops 1476395008 | bytes 4194304 | tf_op jit(solution)/shard_map/first_level/pallas_call | solution.py:131
  20.7 0.1 collective-permute-start.2
  20.8 1.8 %copy.9 = bf16[1,8,2,128,320]{4,3,2,1,0:T(8,128)(2,1)S(1)} copy(bf16[1,8,2,128,320]{3,4,2,1,0:T(8,128)(2,1)} %param.11) | data formatting | bytes 2621440 | tf_op args[4]
  22.7 0.0 collective-permute-done.2
  22.7 0.1 add_convert_fusion.own_ref
  22.8 0.0 copy-start.6
  22.9 3.9 %collective-permute-start.3 = (bf16[2,192,256]{2,1,0:T(8,128)(2,1)S(1)}, bf16[2,192,256]{2,1,0:T(8,128)(2,1)S(1)}, u32[]{:S(2)}, u32[]{:S(2)}) collective-permute-start(bf16[2,192,256]{2,1,0:T(8,128)(2,1)S(1)} %get-tuple-element.14), channel_id=1, source_target_pairs={{0,1},{1,0},{2,3},{3,2},{4,5},{5,4},{6,7},{7,6},{8,9},{9,8},{10,11... | collective-permute-start | bytes 589832 | tf_op jit(solution)/shard_map/ppermute | solution.py:45
  26.8 0.7 collective-permute-start.4
  27.4 0.1 pad_add_fusion.side_ref
  27.5 0.7 fusion.2.starts_ref
  28.2 4.1 %collective-permute-done.3.first_ref = bf16[2,192,256]{2,1,0:T(8,128)(2,1)S(1)} collective-permute-done((bf16[2,192,256]{2,1,0:T(8,128)(2,1)S(1)}, bf16[2,192,256]{2,1,0:T(8,128)(2,1)S(1)}, u32[]{:S(2)}, u32[]{:S(2)}) %collective-permute-start.3) | collective-permute-done | bytes 196640 | tf_op jit(solution)/shard_map/ppermute | solution.py:45
  32.3 0.0 collective-permute-done.4.second_ref
  32.3 4.0 %second_level.1 = (bf16[16,2,64,128]{3,2,1,0:T(8,128)(2,1)S(1)}, bf16[16,2,64,128]{3,2,1,0:T(8,128)(2,1)S(1)}) custom-call(s32[8]{0:T(128)S(1)} %fusion.2.starts_ref, s32[2]{0:T(128)S(1)} %pad_add_fusion.side_ref, bf16[2,512,256]{2,1,0:T(8,128)(2,1)S(1)} %add_convert_fusion.own_ref, bf16[2,192,256]{2,1,0:T(8,128)(2,1)S(1)} %collective-permute-done.3.first_ref, ...), custom_call_target="tpu_custom_call" | custom-call | flops 671088640 | bytes 4194304 | tf_op jit(solution)/shard_map/second_level/pallas_call | solution.py:181
  36.3 1.6 %collective-permute-start.5 = (bf16[16,2,64,128]{3,2,1,0:T(8,128)(2,1)S(1)}, bf16[16,2,64,128]{3,2,1,0:T(8,128)(2,1)S(1)}, u32[]{:S(2)}, u32[]{:S(2)}) collective-permute-start(bf16[16,2,64,128]{3,2,1,0:T(8,128)(2,1)S(1)} %get-tuple-element.12), channel_id=1, source_target_pairs={{0,8},{8,0},{4,12},{12,4},{16,24},{24,16},{20,28},{28,20},{1,9},{9... | collective-permute-start | bytes 1572872 | tf_op jit(solution)/shard_map/ppermute | solution.py:57
  37.9 0.0 copy-done.6
  37.9 0.1 fusion
  38.0 0.2 select_reduce_fusion
  38.2 11.9 %collective-permute-done.5.other_ref = bf16[16,2,64,128]{3,2,1,0:T(8,128)(2,1)S(1)} collective-permute-done((bf16[16,2,64,128]{3,2,1,0:T(8,128)(2,1)S(1)}, bf16[16,2,64,128]{3,2,1,0:T(8,128)(2,1)S(1)}, u32[]{:S(2)}, u32[]{:S(2)}) %collective-permute-start.5) | collective-permute-done | bytes 524320 | tf_op jit(solution)/shard_map/ppermute | solution.py:57
  50.1 0.8 fill_slots.1
  50.9 30.3 %all_to_all.5 = bf16[32,2,64,128]{3,2,1,0:T(8,128)(2,1)S(1)} all-to-all(bf16[32,2,64,128]{3,2,1,0:T(8,128)(2,1)S(1)} %fill_slots.1), channel_id=1, replica_groups=mesh['aperture'=8,'beam'=4] {'beam'}, dimensions={0} | all-to-all | bytes 2097152 | tf_op jit(solution)/shard_map/all_to_all | solution.py:258
  81.2 1.0 %copy.11 = bf16[1,32,2,64,128]{4,3,2,1,0:T(8,128)(2,1)} copy(bf16[1,32,2,64,128]{4,3,2,1,0:T(8,128)(2,1)S(1)} %bitcast.21) | data formatting | bytes 2097152
  (3 shorter events, 0.1 us)
Async XLA Ops:
  0.0 7.5 %copy-start = (bf16[1,2,256,512]{3,2,1,0:T(8,128)(2,1)S(1)}, bf16[1,2,256,512]{3,2,1,0:T(8,128)(2,1)}, u32[]{:S(2)}) copy-start(bf16[1,2,256,512]{3,2,1,0:T(8,128)(2,1)} %param.7) | copy-start | bytes 1572868
  0.0 7.3 %copy-start.7 = (s32[8,4]{0,1:T(4,128)S(1)}, s32[8,4]{0,1:T(4,128)}, u32[]{:S(2)}) copy-start(s32[8,4]{0,1:T(4,128)} %param.10) | copy-start | bytes 388
  0.0 7.5 %copy-start.1 = (bf16[1,2,512,512]{3,2,1,0:T(8,128)(2,1)S(1)}, bf16[1,2,512,512]{3,2,1,0:T(8,128)(2,1)}, u32[]{:S(2)}) copy-start(bf16[1,2,512,512]{3,2,1,0:T(8,128)(2,1)} %param.8) | copy-start | bytes 3145732
  2.1 12.4 %collective-permute-start = (bf16[2,192,512]{2,1,0:T(8,128)(2,1)}, bf16[2,192,512]{2,1,0:T(8,128)(2,1)S(1)}, u32[]{:S(2)}, u32[]{:S(2)}) collective-permute-start(bf16[2,192,512]{2,1,0:T(8,128)(2,1)} %get-tuple-element.16), channel_id=1, source_target_pairs={{0,1},{1,0},{2,3},{3,2},{4,5},{5,4},{6,7},{7,6},{8,9},{9,8},{10,11... | collective-permute-start | bytes 1179656 | tf_op jit(solution)/shard_map/ppermute | solution.py:45
  5.1 10.1 %collective-permute-start.1 = (bf16[2,192,512]{2,1,0:T(8,128)(2,1)S(1)}, bf16[2,192,512]{2,1,0:T(8,128)(2,1)S(1)}, u32[]{:S(2)}, u32[]{:S(2)}) collective-permute-start(bf16[2,192,512]{2,1,0:T(8,128)(2,1)S(1)} %get-tuple-element.15), channel_id=1, source_target_pairs={{1,2},{2,1},{5,6},{6,5},{9,10},{10,9},{13,14},{14,13},{17,18},{18,... | collective-permute-start | bytes 1179656 | tf_op jit(solution)/shard_map/ppermute | solution.py:46
  14.4 0.7 copy-start.2
  15.2 0.7 copy-start.4
  15.9 1.0 %copy-start.3 = (bf16[2,192,512]{2,1,0:T(8,128)(2,1)S(1)}, bf16[2,192,512]{2,1,0:T(8,128)(2,1)}, u32[]{:S(2)}) copy-start(bf16[2,192,512]{2,1,0:T(8,128)(2,1)} %copy-done.2) | copy-start | bytes 1179652
  16.9 1.0 %copy-start.5 = (bf16[2,192,512]{2,1,0:T(8,128)(2,1)S(1)}, bf16[2,192,512]{2,1,0:T(8,128)(2,1)}, u32[]{:S(2)}) copy-start(bf16[2,192,512]{2,1,0:T(8,128)(2,1)} %copy-done.4) | copy-start | bytes 1179652
  20.7 2.0 %collective-permute-start.2 = (bf16[2,512,256]{2,1,0:T(8,128)(2,1)S(1)}, bf16[2,512,256]{2,1,0:T(8,128)(2,1)S(1)}, u32[]{:S(2)}, u32[]{:S(2)}) collective-permute-start(bf16[2,512,256]{2,1,0:T(8,128)(2,1)S(1)} %get-tuple-element.10), channel_id=1, source_target_pairs={{0,4},{4,0},{8,12},{12,8},{16,20},{20,16},{24,28},{28,24},{1,5},{5... | collective-permute-start | bytes 1572872 | tf_op jit(solution)/shard_map/ppermute | solution.py:57
  22.8 15.1 %copy-start.6 = (s32[1,16,1]{1,2,0:T(1,128)S(1)}, s32[1,16,1]{1,2,0:T(1,128)}, u32[]{:S(2)}) copy-start(s32[1,16,1]{1,2,0:T(1,128)} %param.13) | copy-start | bytes 196
  22.9 9.4 %collective-permute-start.3 = (bf16[2,192,256]{2,1,0:T(8,128)(2,1)S(1)}, bf16[2,192,256]{2,1,0:T(8,128)(2,1)S(1)}, u32[]{:S(2)}, u32[]{:S(2)}) collective-permute-start(bf16[2,192,256]{2,1,0:T(8,128)(2,1)S(1)} %get-tuple-element.14), channel_id=1, source_target_pairs={{0,1},{1,0},{2,3},{3,2},{4,5},{5,4},{6,7},{7,6},{8,9},{9,8},{10,11... | collective-permute-start | bytes 589832 | tf_op jit(solution)/shard_map/ppermute | solution.py:45
  26.8 5.5 %collective-permute-start.4 = (bf16[2,192,256]{2,1,0:T(8,128)(2,1)S(1)}, bf16[2,192,256]{2,1,0:T(8,128)(2,1)S(1)}, u32[]{:S(2)}, u32[]{:S(2)}) collective-permute-start(bf16[2,192,256]{2,1,0:T(8,128)(2,1)S(1)} %get-tuple-element.13), channel_id=1, source_target_pairs={{1,2},{2,1},{5,6},{6,5},{9,10},{10,9},{13,14},{14,13},{17,18},{18,... | collective-permute-start | bytes 589832 | tf_op jit(solution)/shard_map/ppermute | solution.py:46
  36.3 13.8 %collective-permute-start.5 = (bf16[16,2,64,128]{3,2,1,0:T(8,128)(2,1)S(1)}, bf16[16,2,64,128]{3,2,1,0:T(8,128)(2,1)S(1)}, u32[]{:S(2)}, u32[]{:S(2)}) collective-permute-start(bf16[16,2,64,128]{3,2,1,0:T(8,128)(2,1)S(1)} %get-tuple-element.12), channel_id=1, source_target_pairs={{0,8},{8,0},{4,12},{12,4},{16,24},{24,16},{20,28},{28,20},{1,9},{9... | collective-permute-start | bytes 1572872 | tf_op jit(solution)/shard_map/ppermute | solution.py:57

commit v2 on v1

v2 whole, which is shorter than its diff:
```python
import functools

import jax
import jax.numpy as jnp
from jax import lax
from jax.experimental import pallas as pl
from jax.experimental.pallas import tpu as pltpu
from jax.sharding import PartitionSpec as P

BLK = 32
NW = 10
REACH = 2
OS = 64
MARGIN_BLOCKS = (NW - 2) // 2 + REACH
VMEM_LIMIT = 8 * 1024 * 1024
ANY = pl.BlockSpec(memory_space=pl.ANY)
VMEM = pl.BlockSpec(memory_space=pltpu.VMEM)
SMEM = pl.BlockSpec(memory_space=pltpu.SMEM)


def params():
    return pltpu.CompilerParams(vmem_limit_bytes=VMEM_LIMIT)


def cost(macs, moved):
    return pl.CostEstimate(flops=2 * macs, bytes_accessed=moved, transcendentals=0)


def swap_route(count, first):
    route = []
    for low in range(first, count - 1, 2):
        route += [(low, low + 1), (low + 1, low)]
    return route


def trade_edges(first, second, axis):
    count = lax.axis_size(axis)
    return (
        lax.ppermute(first, axis, swap_route(count, 0)),
        lax.ppermute(second, axis, swap_route(count, 1)),
    )


def partner(block, axis, distance):
    count = lax.axis_size(axis)
    route = []
    for low in range(count):
        high = low | 1 << distance
        if high != low and high < count:
            route += [(low, high), (high, low)]
    return lax.ppermute(block, axis, route)


def dot(left, right):
    return jnp.dot(left, right, preferred_element_type=jnp.float32)


def resample_kernel(side_ref, child_hbm, kernel_hbm, own_ref, first_ref, second_ref, child, kernel, sems):
    even, half, quarter = side_ref[0], side_ref[1], side_ref[2]
    rng = child.shape[2]
    piece = rng // 4
    copies = [pltpu.make_async_copy(child_hbm, child, sems.at[4])]
    for place in range(4):
        source = (half ^ (place // 2)) * 2 + (quarter ^ (place % 2))
        copies.append(
            pltpu.make_async_copy(
                kernel_hbm.at[:, :, pl.ds(pl.multiple_of(source * piece, 128), piece)],
                kernel.at[:, :, place * piece : (place + 1) * piece],
                sems.at[place],
            )
        )
    for copy in copies:
        copy.start()
    for copy in copies:
        copy.wait()
    real, imag = child[0], child[1]
    k_real, k_imag = kernel[0], kernel[1]
    own_ref[0] = (dot(real, k_real) - dot(imag, k_imag)).astype(jnp.bfloat16)
    own_ref[1] = (dot(real, k_imag) + dot(imag, k_real)).astype(jnp.bfloat16)
    rows, margin = own_ref.shape[1], first_ref.shape[1]
    tail = pl.multiple_of(even * (rows - margin), BLK)
    head = pl.multiple_of((1 - even) * (rows - margin), BLK)
    first_ref[...] = own_ref[:, pl.ds(tail, margin), :]
    second_ref[...] = own_ref[:, pl.ds(head, margin), :]


def resample(side, child, kernel, margin):
    rows, rng = child.shape[1:]
    shapes = [
        jax.ShapeDtypeStruct((2, count, rng), jnp.bfloat16) for count in (rows, margin, margin)
    ]
    return pl.pallas_call(
        resample_kernel,
        out_shape=shapes,
        in_specs=[SMEM, ANY, ANY],
        out_specs=[VMEM] * 3,
        scratch_shapes=[
            pltpu.VMEM(child.shape, jnp.bfloat16),
            pltpu.VMEM(kernel.shape, jnp.bfloat16),
            pltpu.SemaphoreType.DMA((5,)),
        ],
        compiler_params=params(),
        cost_estimate=cost(4 * rows * rng * rng, 2**21),
        name="resample",
    )(side, child, kernel)


def complex_window(weights_ref, sector, real, imag):
    beams = weights_ref.shape[1] // 2
    with_real = dot(weights_ref[sector], real)
    with_imag = dot(weights_ref[sector], imag)
    return (
        (with_real[:beams] - with_imag[beams:]).astype(jnp.bfloat16),
        (with_imag[:beams] + with_real[beams:]).astype(jnp.bfloat16),
    )


def pad_with(padded, even, own_ref, first_ref, second_ref):
    margin, rows = first_ref.shape[1], own_ref.shape[1]
    far = margin + rows
    padded[:, margin:far, :] = own_ref[...]
    padded[:, pl.ds(pl.multiple_of(even * far, BLK), margin), :] = first_ref[...]
    padded[:, pl.ds(pl.multiple_of((1 - even) * far, BLK), margin), :] = second_ref[...]


def first_level_kernel(
    starts_ref, side_ref, own_ref, first_ref, second_ref, weights_ref, keep_ref, send_ref, padded
):
    sectors, stacked, window = weights_ref.shape
    beams = stacked // 2
    width = keep_ref.shape[2]
    pad_with(padded, side_ref[0], own_ref, first_ref, second_ref)
    for sector in range(sectors):
        place = pl.ds(pl.multiple_of(starts_ref[sector] * BLK, BLK), window)
        parts = complex_window(weights_ref, sector, padded[0, place, :], padded[1, place, :])
        out = pl.ds(sector * beams, beams)
        for part in range(2):
            keep_ref[part, out, :] = parts[part][:, :width]
            send_ref[part, out, :] = parts[part][:, width:]


def first_level(starts, side, own, first, second, weights):
    sectors, stacked, window = weights.shape
    rng = own.shape[2]
    margin, rows = first.shape[1], own.shape[1]
    shape = jax.ShapeDtypeStruct((2, sectors * stacked // 2, rng // 2), jnp.bfloat16)
    return pl.pallas_call(
        first_level_kernel,
        out_shape=(shape, shape),
        in_specs=[SMEM, SMEM] + [VMEM] * 4,
        out_specs=(VMEM, VMEM),
        scratch_shapes=[pltpu.VMEM((2, rows + 2 * margin, rng), jnp.bfloat16)],
        compiler_params=params(),
        cost_estimate=cost(sectors * 2 * stacked * window * rng, 2**22),
        name="first_level",
    )(starts, side, own, first, second, weights)


def second_level_kernel(
    starts_ref, side_ref, own_at_ref, other_at_ref, own_ref, first_ref, second_ref, weights_ref,
    keep_ref, *refs,
):
    send_refs, (padded, send) = refs[:-2], refs[-2:]
    sectors, stacked, window = weights_ref.shape
    beams = stacked // 2
    width = keep_ref.shape[3]
    pad_with(padded, side_ref[0], own_ref, first_ref, second_ref)
    per = beams // OS
    for sector in range(sectors):
        place = pl.ds(pl.multiple_of(starts_ref[sector] * BLK, BLK), window)
        parts = complex_window(weights_ref, sector, padded[0, place, :], padded[1, place, :])
        for piece in range(per):
            own_at = own_at_ref[sector * per + piece]
            other_at = other_at_ref[sector * per + piece]
            rows = slice(piece * OS, (piece + 1) * OS)
            for part in range(2):
                keep_ref[own_at, part] = parts[part][rows, :width]
                send[other_at, part] = parts[part][rows, width:]
    done = 0
    for ref in send_refs:
        ref[...] = send[done : done + ref.shape[0]]
        done += ref.shape[0]


def second_level(starts, side, own_at, other_at, own, first, second, weights, chunks):
    sectors, stacked, window = weights.shape
    rng = own.shape[2]
    margin, rows = first.shape[1], own.shape[1]
    count = sectors * stacked // 2 // OS
    block = (2, OS, rng // 2)
    shapes = [jax.ShapeDtypeStruct((n,) + block, jnp.bfloat16) for n in (count,) + chunks]
    return pl.pallas_call(
        second_level_kernel,
        out_shape=shapes,
        in_specs=[SMEM] * 4 + [VMEM] * 4,
        out_specs=[VMEM] * len(shapes),
        scratch_shapes=[
            pltpu.VMEM((2, rows + 2 * margin, rng), jnp.bfloat16),
            pltpu.VMEM((count,) + block, jnp.bfloat16),
        ],
        compiler_params=params(),
        cost_estimate=cost(sectors * 2 * stacked * window * rng, 2**22),
        name="second_level",
    )(starts, side, own_at, other_at, own, first, second, weights)


def plan_kernel(own_ref, other_ref, own_at_ref, other_at_ref, target_ref, rank_ref, taken, filled):
    count = own_ref.shape[0]
    for owners_ref, at_ref in ((other_ref, other_at_ref), (own_ref, own_at_ref)):
        for target in range(taken.shape[0]):
            taken[target] = 0
        for rank in range(filled.shape[0]):
            filled[rank] = 0
        for sector in range(count):
            target = owners_ref[sector]
            rank = taken[target]
            taken[target] = rank + 1
            filled[rank + 1] = filled[rank + 1] + 1
            at_ref[sector] = rank
        for rank in range(1, filled.shape[0]):
            filled[rank] = filled[rank] + filled[rank - 1]
        for sector in range(count):
            rank = at_ref[sector]
            place = filled[rank]
            filled[rank] = place + 1
            at_ref[sector] = place
            if at_ref is own_at_ref:
                target_ref[place] = owners_ref[sector]
                rank_ref[place] = rank


def plan(own, other, beam_count):
    count = own.shape[0]
    shape = jax.ShapeDtypeStruct((count,), jnp.int32)
    return pl.pallas_call(
        plan_kernel,
        out_shape=[shape] * 4,
        in_specs=[SMEM, SMEM],
        out_specs=[SMEM] * 4,
        scratch_shapes=[pltpu.SMEM((beam_count,), jnp.int32), pltpu.SMEM((count + 1,), jnp.int32)],
        compiler_params=params(),
        name="plan",
    )(own, other)


def wires_kernel(low, high, me_ref, target_ref, rank_ref, keep_ref, *refs):
    wires = refs[-1]
    spare = wires.shape[0] - 1
    beam_count = spare // (high - low)
    other_refs, out_refs = refs[: -1 - beam_count], refs[-1 - beam_count : -1]
    wires[...] = jnp.zeros_like(wires)
    me = me_ref[0]
    place = 0
    for other_ref in other_refs:
        for row in range(other_ref.shape[0]):
            rank = rank_ref[place]
            wanted = jnp.logical_and(rank >= low, rank < high)
            at = jnp.where(wanted, (target_ref[place] ^ me) * (high - low) + rank - low, spare)
            total = keep_ref[place].astype(jnp.float32) + other_ref[row].astype(jnp.float32)
            wires[at] = total.astype(jnp.bfloat16)
            place += 1
    for distance, ref in enumerate(out_refs):
        ref[...] = wires[distance * (high - low) : (distance + 1) * (high - low)]


def wires(low, high, beam_count, me, target, rank, keep, *others):
    block = keep.shape[1:]
    shape = jax.ShapeDtypeStruct((high - low,) + block, jnp.bfloat16)
    return pl.pallas_call(
        functools.partial(wires_kernel, low, high),
        out_shape=[shape] * beam_count,
        in_specs=[SMEM] * 3 + [VMEM] * (1 + len(others)),
        out_specs=[VMEM] * beam_count,
        scratch_shapes=[pltpu.VMEM(((high - low) * beam_count + 1,) + block, jnp.bfloat16)],
        compiler_params=params(),
        cost_estimate=cost(0, 2**21),
        name=f"wires_{low}",
    )(me, target, rank, keep, *others)


def collect_kernel(bounds, me_ref, *refs):
    sems = refs[-1]
    out_ref = refs[-2]
    groups = len(bounds)
    beam_count = (len(refs) - 2) // groups
    capacity = bounds[-1][1]
    copies = []
    for group, (low, high) in enumerate(bounds):
        for distance in range(beam_count):
            place = group * beam_count + distance
            start = (me_ref[0] ^ distance) * capacity + low
            copies.append(
                pltpu.make_async_copy(
                    refs[place], out_ref.at[pl.ds(start, high - low)], sems.at[place]
                )
            )
    for copy in copies:
        copy.start()
    for copy in copies:
        copy.wait()


def collect(bounds, me, received):
    beam_count = len(received[0])
    flat = [array for group in received for array in group]
    shape = (beam_count * bounds[-1][1],) + flat[0].shape[1:]
    return pl.pallas_call(
        functools.partial(collect_kernel, bounds),
        out_shape=jax.ShapeDtypeStruct(shape, jnp.bfloat16),
        in_specs=[SMEM] + [ANY] * len(flat),
        out_specs=ANY,
        scratch_shapes=[pltpu.SemaphoreType.DMA((len(flat),))],
        compiler_params=params(),
        cost_estimate=cost(0, 2**21),
        name="collect",
    )(me, *flat)


def spread(group, axis):
    count = lax.axis_size(axis)
    received = {0: group[0]}
    for distance in reversed(range(1, count)):
        route = [(place, place ^ distance) for place in range(count)]
        received[distance] = lax.ppermute(group[distance], axis, route)
    return [received[distance] for distance in range(count)]


def stacked_weights(weights):
    return weights[0].reshape(weights.shape[1], -1, weights.shape[4])


def table_row(table, row_number):
    return lax.dynamic_index_in_dim(table, row_number, 0, keepdims=False)


def local(subimages, range_kernel, weights0, starts0, weights1, starts1, owners):
    aper_index = lax.axis_index("aperture")
    beam_index = lax.axis_index("beam")
    beam_count = lax.axis_size("beam")
    margin = MARGIN_BLOCKS * BLK
    local_blocks = subimages.shape[2] // BLK
    even = (beam_index % 2 == 0).astype(jnp.int32)
    side = jnp.stack([even, aper_index % 2, aper_index // 2 % 2])
    me = beam_index.reshape(1)

    sector_count = owners.shape[1]
    capacity = max(2, 2 * sector_count // beam_count)
    early = sector_count // 2 // beam_count
    paired = beam_count & (beam_count - 1) == 0
    if early and paired:
        chunks = (sector_count // 2, sector_count - sector_count // 2)
        bounds = ((0, early), (early, capacity))
    else:
        chunks = (sector_count,)
        bounds = ((0, capacity),)

    own, first, second = resample(side, subimages[0], range_kernel[0], margin)
    first, second = trade_edges(first, second, "beam")
    own_owners = owners[0, :, 0]
    other_owners = partner(owners, "aperture", 1)[0, :, 0]
    own_at, other_at, target, rank = plan(own_owners, other_owners, beam_count)
    begin0 = table_row(starts0, aper_index) - (beam_index * local_blocks - MARGIN_BLOCKS)
    keep, send = first_level(begin0, side, own, first, second, stacked_weights(weights0))
    other = partner(send, "aperture", 0)
    level_one = (keep.astype(jnp.float32) + other.astype(jnp.float32)).astype(jnp.bfloat16)

    rows = level_one.shape[1]
    first = lax.dynamic_slice_in_dim(level_one, even * (rows - margin), margin, 1)
    second = lax.dynamic_slice_in_dim(level_one, (1 - even) * (rows - margin), margin, 1)
    first, second = trade_edges(first, second, "beam")
    begin1 = table_row(starts1, aper_index) - (beam_index * 2 * local_blocks - MARGIN_BLOCKS)
    keep, *sends = second_level(
        begin1, side, own_at, other_at, level_one, first, second, stacked_weights(weights1), chunks
    )
    others = [partner(send, "aperture", 1) for send in sends]

    if len(bounds) == 1 or not paired:
        outgoing = wires(0, capacity, beam_count, me, target, rank, keep, *others)
        outgoing = jnp.stack([outgoing[0]] + list(outgoing[1:]))
        order = jnp.arange(beam_count) ^ beam_index
        outgoing = jnp.take(outgoing, order, axis=0)
        received = lax.all_to_all(outgoing, "beam", split_axis=0, concat_axis=0, tiled=True)
        return received.reshape((1, beam_count * capacity) + keep.shape[1:])
    received = []
    for number, (low, high) in enumerate(bounds):
        group = wires(low, high, beam_count, me, target, rank, keep, *others[: number + 1])
        received.append(spread(group, "beam"))
    return collect(bounds, me, received)[None]


def solution(mesh):
    return jax.shard_map(
        local,
        mesh=mesh,
        in_specs=(
            P("aperture", None, "beam", None),
            P("aperture", None, None, None),
            P("aperture", "beam", None, None, None),
            P(None, "beam"),
            P("aperture", "beam", None, None, None),
            P(None, "beam"),
            P("aperture", "beam", None),
        ),
        out_specs=P("aperture", "beam", None, None, None),
        check_vma=False,
    )
```

time: 82.5 us -> 75.5 us (0.915)
  blocking collectives: 30.3 us -> 0 us
  starting transfers between devices: 9.89 us -> 23.8 us
  waiting for transfers between devices: 22.2 us -> 35.1 us
  local copies, waits for them, and re-layouts: 9.81 us -> 5.6 us
  Pallas kernels: 8.33 us -> 9.41 us
    all_to_all x1 -> x0, blocking collectives: 30.3 us -> none  [local(): lax.all_to_all(outgoing, 'beam', split_axis=0, concat_axis=0, tiled=True)]
    ppermute x4 -> x10, waiting for transfers between devices: 10.2 us -> 22.2 us  [the longest x6 15.4 us: spread(): received[distance] = lax.ppermute(group[distance], axis, route)]
    ppermute x4 -> x10, starting transfers between devices: 8.25 us -> 20.1 us  [the longest x2 10.9 us: trade_edges(): lax.ppermute(first, axis, swap_route(count, 0))]
    unnamed x19 -> x10, local copies, waits for them, and re-layouts: 7.73 us -> 5.57 us
    dynamic_slice x2 -> x1, local copies, waits for them, and re-layouts: 2.09 us -> 0.04 us  [local(): lax.dynamic_slice_in_dim(level_one, (1 - even) * (rows - margin), margin, 1)]
    ppermute x2 -> x4, starting transfers between devices: 1.64 us -> 3.66 us  [partner(): return lax.ppermute(block, axis, route)]
    pallas_call x3 -> x6, Pallas kernels: 5.52 us -> 7.53 us  [the longest x1 1.98 us: second_level(): pl.pallas_call(second_level_kernel, out_shape=shapes, in_specs=[SMEM] * 4...]
    ppermute x2 -> x4, waiting for transfers between devices: 11.9 us -> 13 us  [partner(): return lax.ppermute(block, axis, route)]
  transfers between devices with their start and end apart: 6 -> 14, of which waited for: 3 -> 6; matrix products, arithmetic and copies ran while one was open for 6% -> 6% of each run, Pallas kernels for 1% -> 3%
where the time goes in v2:
time: 75.5 us; the launch traced here: 75.2 us
  waiting for transfers between devices  35.1 us (46%)
  starting transfers between devices  23.8 us (32%)
  Pallas kernels  9.41 us (12%)
  local copies, waits for them, and re-layouts  5.6 us (7%)
  other arithmetic  1.09 us (1%)
    ppermute x6, waiting for transfers between devices, spread(): received[distance] = lax.ppermute(group[distance], axis, route)  15.4 us
    ppermute x4, waiting for transfers between devices, partner(): return lax.ppermute(block, axis, route)  13 us
    ppermute x2, starting transfers between devices, trade_edges(): lax.ppermute(first, axis, swap_route(count, 0))  10.9 us
    ppermute x6, starting transfers between devices, spread(): received[distance] = lax.ppermute(group[distance], axis, route)  7.9 us
    ppermute x2, waiting for transfers between devices, trade_edges(): lax.ppermute(first, axis, swap_route(count, 0))  6.79 us
    unnamed x10, local copies, waits for them, and re-layouts  5.57 us
    ppermute x4, starting transfers between devices, partner(): return lax.ppermute(block, axis, route)  3.66 us
    pallas_call x1, Pallas kernels, second_level(): pl.pallas_call(second_level_kernel, out_shape=shapes, in_specs=[SMEM] * 4...  1.98 us
  transfers between devices with their start and end apart: 14, of which 6 were waited for; matrix products, arithmetic and copies ran while one was open for 6% of the time, Pallas kernels for 3%

profile of v2, /device:TPU:0, one launch (start us, length us, event | category | flops | bytes accessed | tf_op | source)
XLA Modules:
  0.0 75.2 jit_solution(10464085155338854300)
XLA Ops:
  0.0 0.1 pad_add_fusion.side_ref
  0.1 0.0 copy-start
  0.1 1.2 %copy-done = bf16[1,2,512,512]{3,2,1,0:T(8,128)(2,1)S(1)} copy-done((bf16[1,2,512,512]{3,2,1,0:T(8,128)(2,1)S(1)}, bf16[1,2,512,512]{3,2,1,0:T(8,128)(2,1)}, u32[]{:S(2)}) %copy-start) | copy-done | bytes 1048600
  1.3 0.0 copy-start.1
  1.3 1.0 %copy-done.1 = bf16[1,2,256,512]{3,2,1,0:T(8,128)(2,1)S(1)} copy-done((bf16[1,2,256,512]{3,2,1,0:T(8,128)(2,1)S(1)}, bf16[1,2,256,512]{3,2,1,0:T(8,128)(2,1)}, u32[]{:S(2)}) %copy-start.1) | copy-done | bytes 524312
  2.3 0.0 copy-start.3
  2.3 1.6 %resample.1 = (bf16[2,256,512]{2,1,0:T(8,128)(2,1)S(1)}, bf16[2,192,512]{2,1,0:T(8,128)(2,1)S(1)}, bf16[2,192,512]{2,1,0:T(8,128)(2,1)S(1)}) custom-call(s32[3]{0:T(128)S(1)} %pad_add_fusion.side_ref, bf16[2,256,512]{2,1,0:T(8,128)(2,1)S(1)} %bitcast.16, bf16[2,512,512]{2,1,0:T(8,128)(2,1)S(1)} %bitcast.15), custom_call_target="tpu_custom_call" | custom-call | flops 536870912 | bytes 2097152 | tf_op jit(solution)/shard_map/resample/pallas_call | solution.py:92
  3.9 3.1 %collective-permute-start.1 = (bf16[2,192,512]{2,1,0:T(8,128)(2,1)S(1)}, bf16[2,192,512]{2,1,0:T(8,128)(2,1)S(1)}, u32[]{:S(2)}, u32[]{:S(2)}) collective-permute-start(bf16[2,192,512]{2,1,0:T(8,128)(2,1)S(1)} %get-tuple-element.30), channel_id=1, source_target_pairs={{0,1},{1,0},{2,3},{3,2},{4,5},{5,4},{6,7},{7,6},{8,9},{9,8},{10,11... | collective-permute-start | bytes 1179656 | tf_op jit(solution)/shard_map/ppermute | solution.py:39
  7.0 0.7 collective-permute-start.2
  7.7 1.4 %copy.8 = bf16[1,4,2,128,320]{4,3,2,1,0:T(8,128)(2,1)S(1)} copy(bf16[1,4,2,128,320]{3,4,2,1,0:T(8,128)(2,1)} %param.9) | data formatting | bytes 1310720 | tf_op args[2]
  9.2 0.0 copy-done.3
  9.2 0.2 subtract_reduce_fusion.starts_ref
  9.4 6.8 %collective-permute-done.1.first_ref = bf16[2,192,512]{2,1,0:T(8,128)(2,1)S(1)} collective-permute-done((bf16[2,192,512]{2,1,0:T(8,128)(2,1)S(1)}, bf16[2,192,512]{2,1,0:T(8,128)(2,1)S(1)}, u32[]{:S(2)}, u32[]{:S(2)}) %collective-permute-start.1) | collective-permute-done | bytes 393248 | tf_op jit(solution)/shard_map/ppermute | solution.py:39
  16.1 0.0 collective-permute-done.2.second_ref
  16.1 1.9 %first_level.1 = (bf16[2,512,256]{2,1,0:T(8,128)(2,1)S(1)}, bf16[2,512,256]{2,1,0:T(8,128)(2,1)S(1)}) custom-call(s32[4]{0:T(128)S(1)} %subtract_reduce_fusion.starts_ref, s32[3]{0:T(128)S(1)} %pad_add_fusion.side_ref, bf16[2,256,512]{2,1,0:T(8,128)(2,1)S(1)} %get-tuple-element.29.own_ref, bf16[2,192,512]{2,1,0:T(8,128)(2,1)S(1)} %collective-permute-done.1.first_ref, ...), custom_call_target="tpu_custom_call" | custom-call | flops 671088640 | bytes 4194304 | tf_op jit(solution)/shard_map/first_level/pallas_call | solution.py:147
  18.0 0.0 copy-start.2
  18.0 0.1 collective-permute-start.3
  18.1 1.9 %collective-permute-done.3 = bf16[2,512,256]{2,1,0:T(8,128)(2,1)S(1)} collective-permute-done((bf16[2,512,256]{2,1,0:T(8,128)(2,1)S(1)}, bf16[2,512,256]{2,1,0:T(8,128)(2,1)S(1)}, u32[]{:S(2)}, u32[]{:S(2)}) %collective-permute-start.3) | collective-permute-done | bytes 524320 | tf_op jit(solution)/shard_map/ppermute | solution.py:51
  20.0 0.1 add_convert_fusion.own_ref
  20.2 0.7 collective-permute-start.5
  20.9 7.8 %collective-permute-start.4 = (bf16[2,192,256]{2,1,0:T(8,128)(2,1)S(1)}, bf16[2,192,256]{2,1,0:T(8,128)(2,1)S(1)}, u32[]{:S(2)}, u32[]{:S(2)}) collective-permute-start(bf16[2,192,256]{2,1,0:T(8,128)(2,1)S(1)} %get-tuple-element.46), channel_id=1, source_target_pairs={{0,1},{1,0},{2,3},{3,2},{4,5},{5,4},{6,7},{7,6},{8,9},{9,8},{10,11... | collective-permute-start | bytes 589832 | tf_op jit(solution)/shard_map/ppermute | solution.py:39
  28.7 0.0 copy-done.2
  28.7 1.5 %collective-permute-start = (s32[1,16,1]{1,2,0:T(1,128)S(1)}, s32[1,16,1]{1,2,0:T(1,128)S(1)}, u32[]{:S(2)}, u32[]{:S(2)}) collective-permute-start(s32[1,16,1]{1,2,0:T(1,128)S(1)} %copy-done.2), channel_id=1, source_target_pairs={{0,8},{8,0},{4,12},{12,4},{16,24},{24,16},{20,28},{28,20},{1,9},{9... | collective-permute-start | bytes 200 | tf_op jit(solution)/shard_map/ppermute | solution.py:51
  30.2 0.7 fusion.1.starts_ref
  30.9 1.8 %copy.9 = bf16[1,8,2,128,320]{4,3,2,1,0:T(8,128)(2,1)S(1)} copy(bf16[1,8,2,128,320]{3,4,2,1,0:T(8,128)(2,1)} %param.11) | data formatting | bytes 2621440 | tf_op args[4]
  32.7 0.0 collective-permute-done
  32.7 1.5 %plan.1 = (s32[16]{0:T(128)S(1)}, s32[16]{0:T(128)S(1)}, s32[16]{0:T(128)S(1)}, s32[16]{0:T(128)S(1)}) custom-call(s32[16]{0:T(128)S(1)} %bitcast.17, s32[16]{0:T(128)S(1)} %bitcast.18), custom_call_target="tpu_custom_call" | custom-call | tf_op jit(solution)/shard_map/plan/pallas_call | solution.py:235
  34.2 0.0 collective-permute-done.5.second_ref
  34.3 0.0 collective-permute-done.4.first_ref
  34.3 2.0 %second_level.1 = (bf16[16,2,64,128]{3,2,1,0:T(8,128)(2,1)S(1)}, bf16[8,2,64,128]{3,2,1,0:T(8,128)(2,1)S(1)}, bf16[8,2,64,128]{3,2,1,0:T(8,128)(2,1)S(1)}) custom-call(s32[8]{0:T(128)S(1)} %fusion.1.starts_ref, s32[3]{0:T(128)S(1)} %pad_add_fusion.side_ref, s32[16]{0:T(128)S(1)} %get-tuple-element.27.own_at_ref, s32[16]{0:T(128)S(1)} %get-tuple-element.28.other_at_ref, ...), custom_call_target="tpu_custom_call" | custom-call | flops 671088640 | bytes 4194304 | tf_op jit(solution)/shard_map/second_level/pallas_call | solution.py:192
  36.3 1.0 %collective-permute-start.6 = (bf16[8,2,64,128]{3,2,1,0:T(8,128)(2,1)S(1)}, bf16[8,2,64,128]{3,2,1,0:T(8,128)(2,1)S(1)}, u32[]{:S(2)}, u32[]{:S(2)}) collective-permute-start(bf16[8,2,64,128]{3,2,1,0:T(8,128)(2,1)S(1)} %get-tuple-element.35), channel_id=1, source_target_pairs={{0,8},{8,0},{4,12},{12,4},{16,24},{24,16},{20,28},{28,20},{1,9},{9... | collective-permute-start | bytes 786440 | tf_op jit(solution)/shard_map/ppermute | solution.py:51
  37.3 1.1 %collective-permute-start.10 = (bf16[8,2,64,128]{3,2,1,0:T(8,128)(2,1)S(1)}, bf16[8,2,64,128]{3,2,1,0:T(8,128)(2,1)S(1)}, u32[]{:S(2)}, u32[]{:S(2)}) collective-permute-start(bf16[8,2,64,128]{3,2,1,0:T(8,128)(2,1)S(1)} %get-tuple-element.40), channel_id=1, source_target_pairs={{0,8},{8,0},{4,12},{12,4},{16,24},{24,16},{20,28},{28,20},{1,9},{9... | collective-permute-start | bytes 786440 | tf_op jit(solution)/shard_map/ppermute | solution.py:51
  38.3 7.2 %collective-permute-done.6.refs_0_ = bf16[8,2,64,128]{3,2,1,0:T(8,128)(2,1)S(1)} collective-permute-done((bf16[8,2,64,128]{3,2,1,0:T(8,128)(2,1)S(1)}, bf16[8,2,64,128]{3,2,1,0:T(8,128)(2,1)S(1)}, u32[]{:S(2)}, u32[]{:S(2)}) %collective-permute-start.6) | collective-permute-done | bytes 262176 | tf_op jit(solution)/shard_map/ppermute | solution.py:51
  45.6 3.9 %collective-permute-done.10.refs_1_ = bf16[8,2,64,128]{3,2,1,0:T(8,128)(2,1)S(1)} collective-permute-done((bf16[8,2,64,128]{3,2,1,0:T(8,128)(2,1)S(1)}, bf16[8,2,64,128]{3,2,1,0:T(8,128)(2,1)S(1)}, u32[]{:S(2)}, u32[]{:S(2)}) %collective-permute-start.10) | collective-permute-done | bytes 262176 | tf_op jit(solution)/shard_map/ppermute | solution.py:51
  49.4 0.8 %wires_2.1 = (bf16[6,2,64,128]{3,2,1,0:T(8,128)(2,1)S(1)}, bf16[6,2,64,128]{3,2,1,0:T(8,128)(2,1)S(1)}, bf16[6,2,64,128]{3,2,1,0:T(8,128)(2,1)S(1)}, bf16[6,2,64,128]{3,2,1,0:T(8,128)(2,1)S(1)}) custom-call(s32[1]{0:T(128)} %bitcast.me_ref, s32[16]{0:T(128)S(1)} %get-tuple-element.25.target_ref, s32[16]{0:T(128)S(1)} %get-tuple-element.26.rank_ref, ...), custom_call_target="tpu_custom_call" | custom-call | bytes 2097152 | tf_op jit(solution)/shard_map/wires_2/pallas_call | solution.py:269
  50.3 0.8 %collective-permute-start.11 = (bf16[6,2,64,128]{3,2,1,0:T(8,128)(2,1)S(1)}, bf16[6,2,64,128]{3,2,1,0:T(8,128)(2,1)S(1)}, u32[]{:S(2)}, u32[]{:S(2)}) collective-permute-start(bf16[6,2,64,128]{3,2,1,0:T(8,128)(2,1)S(1)} %get-tuple-element.42), channel_id=1, source_target_pairs={{0,1},{1,0},{2,3},{3,2},{4,5},{5,4},{6,7},{7,6},{8,9},{9,8},{10,11... | collective-permute-start | bytes 589832 | tf_op jit(solution)/shard_map/ppermute | solution.py:324
  51.1 1.0 %collective-permute-start.12 = (bf16[6,2,64,128]{3,2,1,0:T(8,128)(2,1)S(1)}, bf16[6,2,64,128]{3,2,1,0:T(8,128)(2,1)S(1)}, u32[]{:S(2)}, u32[]{:S(2)}) collective-permute-start(bf16[6,2,64,128]{3,2,1,0:T(8,128)(2,1)S(1)} %get-tuple-element.43), channel_id=1, source_target_pairs={{0,2},{1,3},{2,0},{3,1},{4,6},{5,7},{6,4},{7,5},{8,10},{9,11},{10,... | collective-permute-start | bytes 589832 | tf_op jit(solution)/shard_map/ppermute | solution.py:324
  52.1 2.6 %collective-permute-start.13 = (bf16[6,2,64,128]{3,2,1,0:T(8,128)(2,1)S(1)}, bf16[6,2,64,128]{3,2,1,0:T(8,128)(2,1)S(1)}, u32[]{:S(2)}, u32[]{:S(2)}) collective-permute-start(bf16[6,2,64,128]{3,2,1,0:T(8,128)(2,1)S(1)} %get-tuple-element.44), channel_id=1, source_target_pairs={{0,3},{1,2},{2,1},{3,0},{4,7},{5,6},{6,5},{7,4},{8,11},{9,10},{10,... | collective-permute-start | bytes 589832 | tf_op jit(solution)/shard_map/ppermute | solution.py:324
  54.7 0.6 wires_0.1
  55.4 0.1 collective-permute-start.7
  55.4 1.7 %collective-permute-start.8 = (bf16[2,2,64,128]{3,2,1,0:T(8,128)(2,1)S(1)}, bf16[2,2,64,128]{3,2,1,0:T(8,128)(2,1)S(1)}, u32[]{:S(2)}, u32[]{:S(2)}) collective-permute-start(bf16[2,2,64,128]{3,2,1,0:T(8,128)(2,1)S(1)} %get-tuple-element.38), channel_id=1, source_target_pairs={{0,2},{1,3},{2,0},{3,1},{4,6},{5,7},{6,4},{7,5},{8,10},{9,11},{10,... | collective-permute-start | bytes 196616 | tf_op jit(solution)/shard_map/ppermute | solution.py:324
  57.2 7.5 %collective-permute-done.7.refs_1_ = bf16[2,2,64,128]{3,2,1,0:T(8,128)(2,1)S(1)} collective-permute-done((bf16[2,2,64,128]{3,2,1,0:T(8,128)(2,1)S(1)}, bf16[2,2,64,128]{3,2,1,0:T(8,128)(2,1)S(1)}, u32[]{:S(2)}, u32[]{:S(2)}) %collective-permute-start.7) | collective-permute-done | bytes 65568 | tf_op jit(solution)/shard_map/ppermute | solution.py:324
  64.7 1.6 %collective-permute-start.9 = (bf16[2,2,64,128]{3,2,1,0:T(8,128)(2,1)S(1)}, bf16[2,2,64,128]{3,2,1,0:T(8,128)(2,1)S(1)}, u32[]{:S(2)}, u32[]{:S(2)}) collective-permute-start(bf16[2,2,64,128]{3,2,1,0:T(8,128)(2,1)S(1)} %get-tuple-element.39), channel_id=1, source_target_pairs={{0,3},{1,2},{2,1},{3,0},{4,7},{5,6},{6,5},{7,4},{8,11},{9,10},{10,... | collective-permute-start | bytes 196616 | tf_op jit(solution)/shard_map/ppermute | solution.py:324
  66.3 7.8 %collective-permute-done.8.refs_2_ = bf16[2,2,64,128]{3,2,1,0:T(8,128)(2,1)S(1)} collective-permute-done((bf16[2,2,64,128]{3,2,1,0:T(8,128)(2,1)S(1)}, bf16[2,2,64,128]{3,2,1,0:T(8,128)(2,1)S(1)}, u32[]{:S(2)}, u32[]{:S(2)}) %collective-permute-start.8) | collective-permute-done | bytes 65568 | tf_op jit(solution)/shard_map/ppermute | solution.py:324
  74.2 0.0 collective-permute-done.9.refs_3_
  74.2 0.0 collective-permute-done.11.refs_5_
  74.2 0.0 collective-permute-done.12.refs_6_
  74.2 0.0 collective-permute-done.13.refs_7_
  74.2 1.0 %collect.1 = bf16[32,2,64,128]{3,2,1,0:T(8,128)(2,1)} custom-call(s32[1]{0:T(128)} %bitcast.me_ref, bf16[2,2,64,128]{3,2,1,0:T(8,128)(2,1)S(1)} %get-tuple-element.36.refs_0_, bf16[2,2,64,128]{3,2,1,0:T(8,128)(2,1)S(1)} %collective-permute-done.7.refs_1_, bf16[2,2,64,128]{3,2,1,0:T(8,128)(2,1)S(1)} %collective-permute-done.8.refs_2_, ...), custom_call_target="tpu_custom_call" | custom-call | bytes 2097152 | tf_op jit(solution)/shard_map/collect/pallas_call | solution.py:307
  (1 shorter events, 0.0 us)
Async XLA Ops:
  0.1 1.2 %copy-start = (bf16[1,2,512,512]{3,2,1,0:T(8,128)(2,1)S(1)}, bf16[1,2,512,512]{3,2,1,0:T(8,128)(2,1)}, u32[]{:S(2)}) copy-start(bf16[1,2,512,512]{3,2,1,0:T(8,128)(2,1)} %param.8) | copy-start | bytes 3145732
  1.3 1.0 %copy-start.1 = (bf16[1,2,256,512]{3,2,1,0:T(8,128)(2,1)S(1)}, bf16[1,2,256,512]{3,2,1,0:T(8,128)(2,1)}, u32[]{:S(2)}) copy-start(bf16[1,2,256,512]{3,2,1,0:T(8,128)(2,1)} %param.7) | copy-start | bytes 1572868
  2.3 6.8 %copy-start.3 = (s32[8,4]{0,1:T(4,128)S(1)}, s32[8,4]{0,1:T(4,128)}, u32[]{:S(2)}) copy-start(s32[8,4]{0,1:T(4,128)} %param.10) | copy-start | bytes 388
  3.9 12.2 %collective-permute-start.1 = (bf16[2,192,512]{2,1,0:T(8,128)(2,1)S(1)}, bf16[2,192,512]{2,1,0:T(8,128)(2,1)S(1)}, u32[]{:S(2)}, u32[]{:S(2)}) collective-permute-start(bf16[2,192,512]{2,1,0:T(8,128)(2,1)S(1)} %get-tuple-element.30), channel_id=1, source_target_pairs={{0,1},{1,0},{2,3},{3,2},{4,5},{5,4},{6,7},{7,6},{8,9},{9,8},{10,11... | collective-permute-start | bytes 1179656 | tf_op jit(solution)/shard_map/ppermute | solution.py:39
  7.0 9.1 %collective-permute-start.2 = (bf16[2,192,512]{2,1,0:T(8,128)(2,1)S(1)}, bf16[2,192,512]{2,1,0:T(8,128)(2,1)S(1)}, u32[]{:S(2)}, u32[]{:S(2)}) collective-permute-start(bf16[2,192,512]{2,1,0:T(8,128)(2,1)S(1)} %get-tuple-element.31), channel_id=1, source_target_pairs={{1,2},{2,1},{5,6},{6,5},{9,10},{10,9},{13,14},{14,13},{17,18},{18,... | collective-permute-start | bytes 1179656 | tf_op jit(solution)/shard_map/ppermute | solution.py:40
  18.0 10.6 %copy-start.2 = (s32[1,16,1]{1,2,0:T(1,128)S(1)}, s32[1,16,1]{1,2,0:T(1,128)}, u32[]{:S(2)}) copy-start(s32[1,16,1]{1,2,0:T(1,128)} %param.13) | copy-start | bytes 196
  18.0 2.0 %collective-permute-start.3 = (bf16[2,512,256]{2,1,0:T(8,128)(2,1)S(1)}, bf16[2,512,256]{2,1,0:T(8,128)(2,1)S(1)}, u32[]{:S(2)}, u32[]{:S(2)}) collective-permute-start(bf16[2,512,256]{2,1,0:T(8,128)(2,1)S(1)} %get-tuple-element.33), channel_id=1, source_target_pairs={{0,4},{4,0},{8,12},{12,8},{16,20},{20,16},{24,28},{28,24},{1,5},{5... | collective-permute-start | bytes 1572872 | tf_op jit(solution)/shard_map/ppermute | solution.py:51
  20.2 14.0 %collective-permute-start.5 = (bf16[2,192,256]{2,1,0:T(8,128)(2,1)S(1)}, bf16[2,192,256]{2,1,0:T(8,128)(2,1)S(1)}, u32[]{:S(2)}, u32[]{:S(2)}) collective-permute-start(bf16[2,192,256]{2,1,0:T(8,128)(2,1)S(1)} %get-tuple-element.45), channel_id=1, source_target_pairs={{1,2},{2,1},{5,6},{6,5},{9,10},{10,9},{13,14},{14,13},{17,18},{18,... | collective-permute-start | bytes 589832 | tf_op jit(solution)/shard_map/ppermute | solution.py:40
  20.9 13.4 %collective-permute-start.4 = (bf16[2,192,256]{2,1,0:T(8,128)(2,1)S(1)}, bf16[2,192,256]{2,1,0:T(8,128)(2,1)S(1)}, u32[]{:S(2)}, u32[]{:S(2)}) collective-permute-start(bf16[2,192,256]{2,1,0:T(8,128)(2,1)S(1)} %get-tuple-element.46), channel_id=1, source_target_pairs={{0,1},{1,0},{2,3},{3,2},{4,5},{5,4},{6,7},{7,6},{8,9},{9,8},{10,11... | collective-permute-start | bytes 589832 | tf_op jit(solution)/shard_map/ppermute | solution.py:39
  28.7 4.1 %collective-permute-start = (s32[1,16,1]{1,2,0:T(1,128)S(1)}, s32[1,16,1]{1,2,0:T(1,128)S(1)}, u32[]{:S(2)}, u32[]{:S(2)}) collective-permute-start(s32[1,16,1]{1,2,0:T(1,128)S(1)} %copy-done.2), channel_id=1, source_target_pairs={{0,8},{8,0},{4,12},{12,4},{16,24},{24,16},{20,28},{28,20},{1,9},{9... | collective-permute-start | bytes 200 | tf_op jit(solution)/shard_map/ppermute | solution.py:51
  36.3 9.3 %collective-permute-start.6 = (bf16[8,2,64,128]{3,2,1,0:T(8,128)(2,1)S(1)}, bf16[8,2,64,128]{3,2,1,0:T(8,128)(2,1)S(1)}, u32[]{:S(2)}, u32[]{:S(2)}) collective-permute-start(bf16[8,2,64,128]{3,2,1,0:T(8,128)(2,1)S(1)} %get-tuple-element.35), channel_id=1, source_target_pairs={{0,8},{8,0},{4,12},{12,4},{16,24},{24,16},{20,28},{28,20},{1,9},{9... | collective-permute-start | bytes 786440 | tf_op jit(solution)/shard_map/ppermute | solution.py:51
  37.3 12.2 %collective-permute-start.10 = (bf16[8,2,64,128]{3,2,1,0:T(8,128)(2,1)S(1)}, bf16[8,2,64,128]{3,2,1,0:T(8,128)(2,1)S(1)}, u32[]{:S(2)}, u32[]{:S(2)}) collective-permute-start(bf16[8,2,64,128]{3,2,1,0:T(8,128)(2,1)S(1)} %get-tuple-element.40), channel_id=1, source_target_pairs={{0,8},{8,0},{4,12},{12,4},{16,24},{24,16},{20,28},{28,20},{1,9},{9... | collective-permute-start | bytes 786440 | tf_op jit(solution)/shard_map/ppermute | solution.py:51
  50.3 23.9 %collective-permute-start.11 = (bf16[6,2,64,128]{3,2,1,0:T(8,128)(2,1)S(1)}, bf16[6,2,64,128]{3,2,1,0:T(8,128)(2,1)S(1)}, u32[]{:S(2)}, u32[]{:S(2)}) collective-permute-start(bf16[6,2,64,128]{3,2,1,0:T(8,128)(2,1)S(1)} %get-tuple-element.42), channel_id=1, source_target_pairs={{0,1},{1,0},{2,3},{3,2},{4,5},{5,4},{6,7},{7,6},{8,9},{9,8},{10,11... | collective-permute-start | bytes 589832 | tf_op jit(solution)/shard_map/ppermute | solution.py:324
  51.1 23.1 %collective-permute-start.12 = (bf16[6,2,64,128]{3,2,1,0:T(8,128)(2,1)S(1)}, bf16[6,2,64,128]{3,2,1,0:T(8,128)(2,1)S(1)}, u32[]{:S(2)}, u32[]{:S(2)}) collective-permute-start(bf16[6,2,64,128]{3,2,1,0:T(8,128)(2,1)S(1)} %get-tuple-element.43), channel_id=1, source_target_pairs={{0,2},{1,3},{2,0},{3,1},{4,6},{5,7},{6,4},{7,5},{8,10},{9,11},{10,... | collective-permute-start | bytes 589832 | tf_op jit(solution)/shard_map/ppermute | solution.py:324
  52.1 22.1 %collective-permute-start.13 = (bf16[6,2,64,128]{3,2,1,0:T(8,128)(2,1)S(1)}, bf16[6,2,64,128]{3,2,1,0:T(8,128)(2,1)S(1)}, u32[]{:S(2)}, u32[]{:S(2)}) collective-permute-start(bf16[6,2,64,128]{3,2,1,0:T(8,128)(2,1)S(1)} %get-tuple-element.44), channel_id=1, source_target_pairs={{0,3},{1,2},{2,1},{3,0},{4,7},{5,6},{6,5},{7,4},{8,11},{9,10},{10,... | collective-permute-start | bytes 589832 | tf_op jit(solution)/shard_map/ppermute | solution.py:324
  55.4 9.3 %collective-permute-start.7 = (bf16[2,2,64,128]{3,2,1,0:T(8,128)(2,1)S(1)}, bf16[2,2,64,128]{3,2,1,0:T(8,128)(2,1)S(1)}, u32[]{:S(2)}, u32[]{:S(2)}) collective-permute-start(bf16[2,2,64,128]{3,2,1,0:T(8,128)(2,1)S(1)} %get-tuple-element.37), channel_id=1, source_target_pairs={{0,1},{1,0},{2,3},{3,2},{4,5},{5,4},{6,7},{7,6},{8,9},{9,8},{10,11... | collective-permute-start | bytes 196616 | tf_op jit(solution)/shard_map/ppermute | solution.py:324
  55.4 18.7 %collective-permute-start.8 = (bf16[2,2,64,128]{3,2,1,0:T(8,128)(2,1)S(1)}, bf16[2,2,64,128]{3,2,1,0:T(8,128)(2,1)S(1)}, u32[]{:S(2)}, u32[]{:S(2)}) collective-permute-start(bf16[2,2,64,128]{3,2,1,0:T(8,128)(2,1)S(1)} %get-tuple-element.38), channel_id=1, source_target_pairs={{0,2},{1,3},{2,0},{3,1},{4,6},{5,7},{6,4},{7,5},{8,10},{9,11},{10,... | collective-permute-start | bytes 196616 | tf_op jit(solution)/shard_map/ppermute | solution.py:324
  64.7 9.5 %collective-permute-start.9 = (bf16[2,2,64,128]{3,2,1,0:T(8,128)(2,1)S(1)}, bf16[2,2,64,128]{3,2,1,0:T(8,128)(2,1)S(1)}, u32[]{:S(2)}, u32[]{:S(2)}) collective-permute-start(bf16[2,2,64,128]{3,2,1,0:T(8,128)(2,1)S(1)} %get-tuple-element.39), channel_id=1, source_target_pairs={{0,3},{1,2},{2,1},{3,0},{4,7},{5,6},{6,5},{7,4},{8,11},{9,10},{10,... | collective-permute-start | bytes 196616 | tf_op jit(solution)/shard_map/ppermute | solution.py:324

commit v3 on v2

--- a/solution.py
+++ b/solution.py
@@ -13,32 +13,31 @@
 OS = 64
 MARGIN_BLOCKS = (NW - 2) // 2 + REACH
 VMEM_LIMIT = 8 * 1024 * 1024
+WHOLE_VMEM = 60 * 1024 * 1024
 ANY = pl.BlockSpec(memory_space=pl.ANY)
 VMEM = pl.BlockSpec(memory_space=pltpu.VMEM)
 SMEM = pl.BlockSpec(memory_space=pltpu.SMEM)
 
 
-def params():
-    return pltpu.CompilerParams(vmem_limit_bytes=VMEM_LIMIT)
+def params(limit=VMEM_LIMIT):
+    return pltpu.CompilerParams(vmem_limit_bytes=limit)
 
 
 def cost(macs, moved):
     return pl.CostEstimate(flops=2 * macs, bytes_accessed=moved, transcendentals=0)
 
 
-def swap_route(count, first):
-    route = []
-    for low in range(first, count - 1, 2):
-        route += [(low, low + 1), (low + 1, low)]
-    return route
-
-
-def trade_edges(first, second, axis):
-    count = lax.axis_size(axis)
-    return (
-        lax.ppermute(first, axis, swap_route(count, 0)),
-        lax.ppermute(second, axis, swap_route(count, 1)),
-    )
+def trade_edges(first, second):
+    count = lax.axis_size("beam")
+    received = []
+    for order, block in enumerate((first, second)):
+        route = []
+        for aper in range(lax.axis_size("aperture")):
+            for low in range((aper + order) % 2, count - 1, 2):
+                place = aper * count + low
+                route += [(place, place + 1), (place + 1, place)]
+        received.append(lax.ppermute(block, ("aperture", "beam"), route))
+    return received
 
 
 def partner(block, axis, distance):
@@ -99,7 +98,7 @@
             pltpu.VMEM(kernel.shape, jnp.bfloat16),
             pltpu.SemaphoreType.DMA((5,)),
         ],
-        compiler_params=params(),
+        compiler_params=params(WHOLE_VMEM),
         cost_estimate=cost(4 * rows * rng * rng, 2**21),
         name="resample",
     )(side, child, kernel)
@@ -204,125 +203,150 @@
     )(starts, side, own_at, other_at, own, first, second, weights)
 
 
-def plan_kernel(own_ref, other_ref, own_at_ref, other_at_ref, target_ref, rank_ref, taken, filled):
+def plan_kernel(
+    me_ref, own_ref, other_ref, own_at_ref, other_at_ref, target_ref, rank_ref, taken, filled
+):
     count = own_ref.shape[0]
+    far_bit = taken.shape[0] // 2
     for owners_ref, at_ref in ((other_ref, other_at_ref), (own_ref, own_at_ref)):
         for target in range(taken.shape[0]):
             taken[target] = 0
-        for rank in range(filled.shape[0]):
-            filled[rank] = 0
+        for bucket in range(filled.shape[0]):
+            filled[bucket] = 0
         for sector in range(count):
             target = owners_ref[sector]
             rank = taken[target]
             taken[target] = rank + 1
-            filled[rank + 1] = filled[rank + 1] + 1
-            at_ref[sector] = rank
-        for rank in range(1, filled.shape[0]):
-            filled[rank] = filled[rank] + filled[rank - 1]
+            near = jnp.where(((target ^ me_ref[0]) & far_bit) == 0, count, 0)
+            at_ref[sector] = rank + near
+            filled[rank + near + 1] = filled[rank + near + 1] + 1
+        for bucket in range(1, filled.shape[0]):
+            filled[bucket] = filled[bucket] + filled[bucket - 1]
         for sector in range(count):
-            rank = at_ref[sector]
-            place = filled[rank]
-            filled[rank] = place + 1
+            bucket = at_ref[sector]
+            place = filled[bucket]
+            filled[bucket] = place + 1
             at_ref[sector] = place
             if at_ref is own_at_ref:
                 target_ref[place] = owners_ref[sector]
-                rank_ref[place] = rank
-
-
-def plan(own, other, beam_count):
+                rank_ref[place] = jnp.where(bucket >= count, bucket - count, bucket)
+
+
+def plan(me, own, other, beam_count):
     count = own.shape[0]
     shape = jax.ShapeDtypeStruct((count,), jnp.int32)
     return pl.pallas_call(
         plan_kernel,
         out_shape=[shape] * 4,
-        in_specs=[SMEM, SMEM],
+        in_specs=[SMEM] * 3,
         out_specs=[SMEM] * 4,
-        scratch_shapes=[pltpu.SMEM((beam_count,), jnp.int32), pltpu.SMEM((count + 1,), jnp.int32)],
+        scratch_shapes=[
+            pltpu.SMEM((beam_count,), jnp.int32),
+            pltpu.SMEM((2 * count + 1,), jnp.int32),
+        ],
         compiler_params=params(),
         name="plan",
-    )(own, other)
-
-
-def wires_kernel(low, high, me_ref, target_ref, rank_ref, keep_ref, *refs):
+    )(me, own, other)
+
+
+def wires_kernel(spans, me_ref, target_ref, rank_ref, keep_ref, *refs):
     wires = refs[-1]
     spare = wires.shape[0] - 1
-    beam_count = spare // (high - low)
-    other_refs, out_refs = refs[: -1 - beam_count], refs[-1 - beam_count : -1]
+    out_refs = refs[-1 - len(spans) : -1]
+    other_ref, *summed_refs = refs[: -1 - len(spans)]
     wires[...] = jnp.zeros_like(wires)
     me = me_ref[0]
-    place = 0
-    for other_ref in other_refs:
-        for row in range(other_ref.shape[0]):
-            rank = rank_ref[place]
-            wanted = jnp.logical_and(rank >= low, rank < high)
-            at = jnp.where(wanted, (target_ref[place] ^ me) * (high - low) + rank - low, spare)
-            total = keep_ref[place].astype(jnp.float32) + other_ref[row].astype(jnp.float32)
-            wires[at] = total.astype(jnp.bfloat16)
-            place += 1
-    for distance, ref in enumerate(out_refs):
-        ref[...] = wires[distance * (high - low) : (distance + 1) * (high - low)]
-
-
-def wires(low, high, beam_count, me, target, rank, keep, *others):
+    early = all(low == 0 for _, low, _ in spans)
+
+    def lay(place, total):
+        rank = rank_ref[place]
+        distance = target_ref[place] ^ me
+        at = spare
+        start = 0
+        for number, low, high in spans:
+            wanted = (distance == number) & (rank >= low) & (rank < high)
+            at = jnp.where(wanted, start + rank - low, at)
+            start += high - low
+        wires[at] = total
+
+    before = 0
+    if not early:
+        before = summed_refs[0].shape[0]
+        for row in range(before):
+            lay(row, summed_refs[0][row])
+    for row in range(other_ref.shape[0]):
+        place = before + row
+        total = keep_ref[place].astype(jnp.float32) + other_ref[row].astype(jnp.float32)
+        total = total.astype(jnp.bfloat16)
+        lay(place, total)
+        if early:
+            summed_refs[0][row] = total
+    start = 0
+    for (_, low, high), ref in zip(spans, out_refs):
+        ref[...] = wires[start : start + high - low]
+        start += high - low
+
+
+def wires(spans, me, target, rank, keep, other, summed=None):
     block = keep.shape[1:]
-    shape = jax.ShapeDtypeStruct((high - low,) + block, jnp.bfloat16)
-    return pl.pallas_call(
-        functools.partial(wires_kernel, low, high),
-        out_shape=[shape] * beam_count,
-        in_specs=[SMEM] * 3 + [VMEM] * (1 + len(others)),
-        out_specs=[VMEM] * beam_count,
-        scratch_shapes=[pltpu.VMEM(((high - low) * beam_count + 1,) + block, jnp.bfloat16)],
+    sizes = [high - low for _, low, high in spans]
+    inputs = [me, target, rank, keep, other]
+    if summed is None:
+        sizes = [other.shape[0]] + sizes
+    else:
+        inputs.append(summed)
+    shapes = [jax.ShapeDtypeStruct((size,) + block, jnp.bfloat16) for size in sizes]
+    total = sum(high - low for _, low, high in spans)
+    return pl.pallas_call(
+        functools.partial(wires_kernel, spans),
+        out_shape=shapes,
+        in_specs=[SMEM] * 3 + [VMEM] * (len(inputs) - 3),
+        out_specs=[VMEM] * len(shapes),
+        scratch_shapes=[pltpu.VMEM((total + 1,) + block, jnp.bfloat16)],
         compiler_params=params(),
         cost_estimate=cost(0, 2**21),
-        name=f"wires_{low}",
-    )(me, target, rank, keep, *others)
-
-
-def collect_kernel(bounds, me_ref, *refs):
+        name="early_wires" if summed is None else "late_wires",
+    )(*inputs)
+
+
+def collect_kernel(spans, capacity, me_ref, *refs):
     sems = refs[-1]
     out_ref = refs[-2]
-    groups = len(bounds)
-    beam_count = (len(refs) - 2) // groups
-    capacity = bounds[-1][1]
     copies = []
-    for group, (low, high) in enumerate(bounds):
-        for distance in range(beam_count):
-            place = group * beam_count + distance
-            start = (me_ref[0] ^ distance) * capacity + low
-            copies.append(
-                pltpu.make_async_copy(
-                    refs[place], out_ref.at[pl.ds(start, high - low)], sems.at[place]
-                )
+    for number, (distance, low, high) in enumerate(spans):
+        start = (me_ref[0] ^ distance) * capacity + low
+        copies.append(
+            pltpu.make_async_copy(
+                refs[number], out_ref.at[pl.ds(start, high - low)], sems.at[number]
             )
+        )
     for copy in copies:
         copy.start()
     for copy in copies:
         copy.wait()
 
 
-def collect(bounds, me, received):
-    beam_count = len(received[0])
-    flat = [array for group in received for array in group]
-    shape = (beam_count * bounds[-1][1],) + flat[0].shape[1:]
-    return pl.pallas_call(
-        functools.partial(collect_kernel, bounds),
+def collect(spans, capacity, beam_count, me, received):
+    shape = (beam_count * capacity,) + received[0].shape[1:]
+    return pl.pallas_call(
+        functools.partial(collect_kernel, spans, capacity),
         out_shape=jax.ShapeDtypeStruct(shape, jnp.bfloat16),
-        in_specs=[SMEM] + [ANY] * len(flat),
+        in_specs=[SMEM] + [ANY] * len(received),
         out_specs=ANY,
-        scratch_shapes=[pltpu.SemaphoreType.DMA((len(flat),))],
+        scratch_shapes=[pltpu.SemaphoreType.DMA((len(received),))],
         compiler_params=params(),
         cost_estimate=cost(0, 2**21),
         name="collect",
-    )(me, *flat)
-
-
-def spread(group, axis):
-    count = lax.axis_size(axis)
-    received = {0: group[0]}
-    for distance in reversed(range(1, count)):
+    )(me, *received)
+
+
+def spread(spans, group):
+    count = lax.axis_size("beam")
+    received = []
+    for (distance, _, _), wire in zip(spans, group):
         route = [(place, place ^ distance) for place in range(count)]
-        received[distance] = lax.ppermute(group[distance], axis, route)
-    return [received[distance] for distance in range(count)]
+        received.append(lax.ppermute(wire, "beam", route) if distance else wire)
+    return received
 
 
 def stacked_weights(weights):
@@ -339,27 +363,30 @@
     beam_count = lax.axis_size("beam")
     margin = MARGIN_BLOCKS * BLK
     local_blocks = subimages.shape[2] // BLK
-    even = (beam_index % 2 == 0).astype(jnp.int32)
+    even = ((beam_index + aper_index) % 2 == 0).astype(jnp.int32)
     side = jnp.stack([even, aper_index % 2, aper_index // 2 % 2])
     me = beam_index.reshape(1)
 
     sector_count = owners.shape[1]
     capacity = max(2, 2 * sector_count // beam_count)
-    early = sector_count // 2 // beam_count
-    paired = beam_count & (beam_count - 1) == 0
-    if early and paired:
-        chunks = (sector_count // 2, sector_count - sector_count // 2)
-        bounds = ((0, early), (early, capacity))
-    else:
-        chunks = (sector_count,)
-        bounds = ((0, capacity),)
+    early = max(1, 3 * capacity // 8)
+    far = beam_count // 2
+    chunks = (early * far, sector_count - early * far)
+    distances = list(reversed(range(beam_count)))
+    early_spans = tuple((distance, 0, early) for distance in distances if distance >= far)
+    late_spans = tuple(
+        (distance, early if distance >= far else 0, capacity) for distance in distances
+    )
 
     own, first, second = resample(side, subimages[0], range_kernel[0], margin)
-    first, second = trade_edges(first, second, "beam")
+    first, second = trade_edges(first, second)
     own_owners = owners[0, :, 0]
     other_owners = partner(owners, "aperture", 1)[0, :, 0]
-    own_at, other_at, target, rank = plan(own_owners, other_owners, beam_count)
+    own_at, other_at, target, rank = plan(me, own_owners, other_owners, beam_count)
     begin0 = table_row(starts0, aper_index) - (beam_index * local_blocks - MARGIN_BLOCKS)
+    first, own_at, other_at, target, rank = lax.optimization_barrier(
+        (first, own_at, other_at, target, rank)
+    )
     keep, send = first_level(begin0, side, own, first, second, stacked_weights(weights0))
     other = partner(send, "aperture", 0)
     level_one = (keep.astype(jnp.float32) + other.astype(jnp.float32)).astype(jnp.bfloat16)
@@ -367,25 +394,21 @@
     rows = level_one.shape[1]
     first = lax.dynamic_slice_in_dim(level_one, even * (rows - margin), margin, 1)
     second = lax.dynamic_slice_in_dim(level_one, (1 - even) * (rows - margin), margin, 1)
-    first, second = trade_edges(first, second, "beam")
+    first, second = trade_edges(first, second)
     begin1 = table_row(starts1, aper_index) - (beam_index * 2 * local_blocks - MARGIN_BLOCKS)
     keep, *sends = second_level(
         begin1, side, own_at, other_at, level_one, first, second, stacked_weights(weights1), chunks
     )
-    others = [partner(send, "aperture", 1) for send in sends]
-
-    if len(bounds) == 1 or not paired:
-        outgoing = wires(0, capacity, beam_count, me, target, rank, keep, *others)
-        outgoing = jnp.stack([outgoing[0]] + list(outgoing[1:]))
-        order = jnp.arange(beam_count) ^ beam_index
-        outgoing = jnp.take(outgoing, order, axis=0)
-        received = lax.all_to_all(outgoing, "beam", split_axis=0, concat_axis=0, tiled=True)
-        return received.reshape((1, beam_count * capacity) + keep.shape[1:])
-    received = []
-    for number, (low, high) in enumerate(bounds):
-        group = wires(low, high, beam_count, me, target, rank, keep, *others[: number + 1])
-        received.append(spread(group, "beam"))
-    return collect(bounds, me, received)[None]
+    other = partner(sends[0], "aperture", 1)
+
+    other, late = lax.optimization_barrier((other, sends[1]))
+    late = partner(late, "aperture", 1)
+    summed, *group = wires(early_spans, me, target, rank, keep, other)
+    received = spread(early_spans, group)
+    late, *received = lax.optimization_barrier((late, *received))
+    group = wires(late_spans, me, target, rank, keep, late, summed)
+    received += spread(late_spans, group)
+    return collect(early_spans + late_spans, capacity, beam_count, me, received)[None]
 
 
 def solution(mesh):

time: 75.5 us -> 74.8 us (level)
  waiting for transfers between devices: 35.1 us -> 32.4 us
  Pallas kernels: 9.41 us -> 11.8 us
  local copies, waits for them, and re-layouts: 5.6 us -> 3.29 us
  starting transfers between devices: 23.8 us -> 25.2 us
    ppermute x4, waiting for transfers between devices: 13 us -> 9.3 us  [partner(): return lax.ppermute(block, axis, route)]
    ppermute x4, starting transfers between devices: 3.66 us -> 6.91 us  [partner(): return lax.ppermute(block, axis, route)]
    pallas_call x1, Pallas kernels: 1.58 us -> 3.97 us  [resample(): pl.pallas_call(resample_kernel, out_shape=shapes, in_specs=[SMEM, ANY, AN...]
    unnamed x10 -> x12, local copies, waits for them, and re-layouts: 5.57 us -> 3.25 us
    ppermute x10 -> x9, starting transfers between devices: 20.1 us -> 18.3 us  [the longest x4 13.1 us: trade_edges(): received.append(lax.ppermute(block, ('aperture', 'beam'), route))]
    ppermute x10 -> x9, waiting for transfers between devices: 22.2 us -> 23.1 us  [the longest x5 20.1 us: spread(): received.append(lax.ppermute(wire, 'beam', route) if distance else wire)]
  transfers between devices with their start and end apart: 14 -> 13, of which waited for: 6 -> 9; matrix products, arithmetic and copies ran while one was open for 6% -> 4% of each run, Pallas kernels for 3% -> 3%
where the time goes in v3:
time: 74.8 us; the launch traced here: 74.4 us
  waiting for transfers between devices  32.4 us (43%)
  starting transfers between devices  25.2 us (34%)
  Pallas kernels  11.8 us (16%)
  local copies, waits for them, and re-layouts  3.29 us (4%)
  other arithmetic  1.63 us (2%)
    ppermute x5, waiting for transfers between devices, spread(): received.append(lax.ppermute(wire, 'beam', route) if distance else wire)  20.1 us
    ppermute x4, starting transfers between devices, trade_edges(): received.append(lax.ppermute(block, ('aperture', 'beam'), route))  13.1 us
    ppermute x4, waiting for transfers between devices, partner(): return lax.ppermute(block, axis, route)  9.3 us
    ppermute x4, starting transfers between devices, partner(): return lax.ppermute(block, axis, route)  6.91 us
    ppermute x5, starting transfers between devices, spread(): received.append(lax.ppermute(wire, 'beam', route) if distance else wire)  5.18 us
    pallas_call x1, Pallas kernels, resample(): pl.pallas_call(resample_kernel, out_shape=shapes, in_specs=[SMEM, ANY, AN...  3.97 us
    unnamed x12, local copies, waits for them, and re-layouts  3.25 us
    ppermute x4, waiting for transfers between devices, trade_edges(): received.append(lax.ppermute(block, ('aperture', 'beam'), route))  2.99 us
  transfers between devices with their start and end apart: 13, of which 9 were waited for; matrix products, arithmetic and copies ran while one was open for 4% of the time, Pallas kernels for 3%

profile of v3, /device:TPU:0, one launch (start us, length us, event | category | flops | bytes accessed | tf_op | source)
XLA Modules:
  0.0 74.4 jit_solution(16158839439935985234)
XLA Ops:
  0.0 0.0 copy-start.1
  0.0 0.0 copy-start.4
  0.0 0.0 copy-start.3
  0.0 0.6 pad_add_fusion.side_ref
  0.6 0.0 copy-start
  0.6 4.0 %resample.1 = (bf16[2,256,512]{2,1,0:T(8,128)(2,1)}, bf16[2,192,512]{2,1,0:T(8,128)(2,1)}, bf16[2,192,512]{2,1,0:T(8,128)(2,1)}) custom-call(s32[3]{0:T(128)} %pad_add_fusion.side_ref, bf16[2,256,512]{2,1,0:T(8,128)(2,1)} %bitcast.18, bf16[2,512,512]{2,1,0:T(8,128)(2,1)} %bitcast.17), custom_call_target="tpu_custom_call" | custom-call | flops 536870912 | bytes 2097152 | tf_op jit(solution)/shard_map/resample/pallas_call | solution.py:91
  4.6 5.0 %collective-permute-start = (bf16[2,192,512]{2,1,0:T(8,128)(2,1)}, bf16[2,192,512]{2,1,0:T(8,128)(2,1)S(1)}, u32[]{:S(2)}, u32[]{:S(2)}) collective-permute-start(bf16[2,192,512]{2,1,0:T(8,128)(2,1)} %get-tuple-element.34), channel_id=1, source_target_pairs={{0,1},{1,0},{2,3},{3,2},{5,6},{6,5},{8,9},{9,8},{10,11},{11,10},{1... | collective-permute-start | bytes 1179656 | tf_op jit(solution)/shard_map/ppermute | solution.py:39
  9.6 0.7 collective-permute-start.2
  10.3 0.0 copy-done.1
  10.3 1.6 %collective-permute-start.1 = (s32[1,16,1]{1,2,0:T(1,128)S(1)}, s32[1,16,1]{1,2,0:T(1,128)S(1)}, u32[]{:S(2)}, u32[]{:S(2)}) collective-permute-start(s32[1,16,1]{1,2,0:T(1,128)S(1)} %copy-done.1), channel_id=1, source_target_pairs={{0,8},{8,0},{4,12},{12,4},{16,24},{24,16},{20,28},{28,20},{1,9},{9... | collective-permute-start | bytes 200 | tf_op jit(solution)/shard_map/ppermute | solution.py:50
  11.8 0.0 copy-done.4
  11.8 0.2 subtract_reduce_fusion.starts_ref
  12.0 0.0 copy-done.3
  12.0 0.4 copy.8
  12.4 1.5 %collective-permute-done.1 = s32[1,16,1]{1,2,0:T(1,128)S(1)} collective-permute-done((s32[1,16,1]{1,2,0:T(1,128)S(1)}, s32[1,16,1]{1,2,0:T(1,128)S(1)}, u32[]{:S(2)}, u32[]{:S(2)}) %collective-permute-start.1) | collective-permute-done | bytes 96 | tf_op jit(solution)/shard_map/ppermute | solution.py:50
  13.9 1.5 %plan.1 = (s32[16]{0:T(128)S(1)}, s32[16]{0:T(128)S(1)}, s32[16]{0:T(128)S(1)}, s32[16]{0:T(128)S(1)}) custom-call(s32[1]{0:T(128)} %bitcast.me_ref, s32[16]{0:T(128)S(1)} %bitcast.15, s32[16]{0:T(128)S(1)} %bitcast.16), custom_call_target="tpu_custom_call" | custom-call | tf_op jit(solution)/shard_map/plan/pallas_call | solution.py:238
  15.4 1.9 %collective-permute-done.first_ref = bf16[2,192,512]{2,1,0:T(8,128)(2,1)S(1)} collective-permute-done((bf16[2,192,512]{2,1,0:T(8,128)(2,1)}, bf16[2,192,512]{2,1,0:T(8,128)(2,1)S(1)}, u32[]{:S(2)}, u32[]{:S(2)}) %collective-permute-start) | collective-permute-done | bytes 393248 | tf_op jit(solution)/shard_map/ppermute | solution.py:39
  17.3 0.0 collective-permute-done.2.second_ref
  17.3 0.0 copy-done
  17.3 0.0 copy-start.2
  17.3 1.0 %copy-done.2 = bf16[2,256,512]{2,1,0:T(8,128)(2,1)S(1)} copy-done((bf16[2,256,512]{2,1,0:T(8,128)(2,1)S(1)}, bf16[2,256,512]{2,1,0:T(8,128)(2,1)}, u32[]{:S(2)}) %copy-start.2) | copy-done | bytes 524312
  18.4 1.9 %first_level.1 = (bf16[2,512,256]{2,1,0:T(8,128)(2,1)S(1)}, bf16[2,512,256]{2,1,0:T(8,128)(2,1)S(1)}) custom-call(s32[4]{0:T(128)S(1)} %subtract_reduce_fusion.starts_ref, s32[3]{0:T(128)S(1)} %copy-done, bf16[2,256,512]{2,1,0:T(8,128)(2,1)S(1)} %copy-done.2, bf16[2,192,512]{2,1,0:T(8,128)(2,1)S(1)} %collective-permute-done.first_ref, ...), custom_call_target="tpu_custom_call" | custom-call | flops 671088640 | bytes 4194304 | tf_op jit(solution)/shard_map/first_level/pallas_call | solution.py:146
  20.3 2.3 %collective-permute-start.3 = (bf16[2,512,256]{2,1,0:T(8,128)(2,1)S(1)}, bf16[2,512,256]{2,1,0:T(8,128)(2,1)S(1)}, u32[]{:S(2)}, u32[]{:S(2)}) collective-permute-start(bf16[2,512,256]{2,1,0:T(8,128)(2,1)S(1)} %get-tuple-element.45), channel_id=1, source_target_pairs={{0,4},{4,0},{8,12},{12,8},{16,20},{20,16},{24,28},{28,24},{1,5},{5... | collective-permute-start | bytes 1572872 | tf_op jit(solution)/shard_map/ppermute | solution.py:50
  22.6 1.5 %collective-permute-done.3 = bf16[2,512,256]{2,1,0:T(8,128)(2,1)S(1)} collective-permute-done((bf16[2,512,256]{2,1,0:T(8,128)(2,1)S(1)}, bf16[2,512,256]{2,1,0:T(8,128)(2,1)S(1)}, u32[]{:S(2)}, u32[]{:S(2)}) %collective-permute-start.3) | collective-permute-done | bytes 524320 | tf_op jit(solution)/shard_map/ppermute | solution.py:50
  24.1 0.1 add_convert_fusion.own_ref
  24.3 0.7 collective-permute-start.5
  25.0 6.7 %collective-permute-start.4 = (bf16[2,192,256]{2,1,0:T(8,128)(2,1)S(1)}, bf16[2,192,256]{2,1,0:T(8,128)(2,1)S(1)}, u32[]{:S(2)}, u32[]{:S(2)}) collective-permute-start(bf16[2,192,256]{2,1,0:T(8,128)(2,1)S(1)} %get-tuple-element.64), channel_id=1, source_target_pairs={{0,1},{1,0},{2,3},{3,2},{5,6},{6,5},{8,9},{9,8},{10,11},{11,10},{1... | collective-permute-start | bytes 589832 | tf_op jit(solution)/shard_map/ppermute | solution.py:39
  31.7 1.8 %copy.9 = bf16[1,8,2,128,320]{4,3,2,1,0:T(8,128)(2,1)S(1)} copy(bf16[1,8,2,128,320]{3,4,2,1,0:T(8,128)(2,1)} %param.11) | data formatting | bytes 2621440 | tf_op args[4]
  33.5 0.7 fusion.1.starts_ref
  34.2 0.0 collective-permute-done.5.second_ref
  34.3 1.1 %collective-permute-done.4.first_ref = bf16[2,192,256]{2,1,0:T(8,128)(2,1)S(1)} collective-permute-done((bf16[2,192,256]{2,1,0:T(8,128)(2,1)S(1)}, bf16[2,192,256]{2,1,0:T(8,128)(2,1)S(1)}, u32[]{:S(2)}, u32[]{:S(2)}) %collective-permute-start.4) | collective-permute-done | bytes 196640 | tf_op jit(solution)/shard_map/ppermute | solution.py:39
  35.3 2.0 %second_level.1 = (bf16[16,2,64,128]{3,2,1,0:T(8,128)(2,1)S(1)}, bf16[6,2,64,128]{3,2,1,0:T(8,128)(2,1)S(1)}, bf16[10,2,64,128]{3,2,1,0:T(8,128)(2,1)S(1)}) custom-call(s32[8]{0:T(128)S(1)} %fusion.1.starts_ref, s32[3]{0:T(128)S(1)} %copy-done, s32[16]{0:T(128)S(1)} %get-tuple-element.39.own_at_ref, s32[16]{0:T(128)S(1)} %get-tuple-element.40.other_at_ref, ...), custom_call_target="tpu_custom_call" | custom-call | flops 671088640 | bytes 4194304 | tf_op jit(solution)/shard_map/second_level/pallas_call | solution.py:191
  37.3 1.6 %collective-permute-start.6 = (bf16[6,2,64,128]{3,2,1,0:T(8,128)(2,1)S(1)}, bf16[6,2,64,128]{3,2,1,0:T(8,128)(2,1)S(1)}, u32[]{:S(2)}, u32[]{:S(2)}) collective-permute-start(bf16[6,2,64,128]{3,2,1,0:T(8,128)(2,1)S(1)} %get-tuple-element.46), channel_id=1, source_target_pairs={{0,8},{8,0},{4,12},{12,4},{16,24},{24,16},{20,28},{28,20},{1,9},{9... | collective-permute-start | bytes 589832 | tf_op jit(solution)/shard_map/ppermute | solution.py:50
  38.9 6.3 %collective-permute-done.6.refs_0_ = bf16[6,2,64,128]{3,2,1,0:T(8,128)(2,1)S(1)} collective-permute-done((bf16[6,2,64,128]{3,2,1,0:T(8,128)(2,1)S(1)}, bf16[6,2,64,128]{3,2,1,0:T(8,128)(2,1)S(1)}, u32[]{:S(2)}, u32[]{:S(2)}) %collective-permute-start.6) | collective-permute-done | bytes 196640 | tf_op jit(solution)/shard_map/ppermute | solution.py:50
  45.2 1.5 %collective-permute-start.7 = (bf16[10,2,64,128]{3,2,1,0:T(8,128)(2,1)S(1)}, bf16[10,2,64,128]{3,2,1,0:T(8,128)(2,1)S(1)}, u32[]{:S(2)}, u32[]{:S(2)}) collective-permute-start(bf16[10,2,64,128]{3,2,1,0:T(8,128)(2,1)S(1)} %get-tuple-element.48), channel_id=1, source_target_pairs={{0,8},{8,0},{4,12},{12,4},{16,24},{24,16},{20,28},{28,20},{1,9},{9... | collective-permute-start | bytes 983048 | tf_op jit(solution)/shard_map/ppermute | solution.py:50
  46.7 0.6 early_wires.1
  47.3 0.1 collective-permute-start.8
  47.4 1.6 %collective-permute-start.9 = (bf16[3,2,64,128]{3,2,1,0:T(8,128)(2,1)S(1)}, bf16[3,2,64,128]{3,2,1,0:T(8,128)(2,1)S(1)}, u32[]{:S(2)}, u32[]{:S(2)}) collective-permute-start(bf16[3,2,64,128]{3,2,1,0:T(8,128)(2,1)S(1)} %get-tuple-element.54), channel_id=1, source_target_pairs={{0,2},{1,3},{2,0},{3,1},{4,6},{5,7},{6,4},{7,5},{8,10},{9,11},{10,... | collective-permute-start | bytes 294920 | tf_op jit(solution)/shard_map/ppermute | solution.py:348
  48.9 4.9 %collective-permute-done.8.refs_0_ = bf16[3,2,64,128]{3,2,1,0:T(8,128)(2,1)S(1)} collective-permute-done((bf16[3,2,64,128]{3,2,1,0:T(8,128)(2,1)S(1)}, bf16[3,2,64,128]{3,2,1,0:T(8,128)(2,1)S(1)}, u32[]{:S(2)}, u32[]{:S(2)}) %collective-permute-start.8) | collective-permute-done | bytes 98336 | tf_op jit(solution)/shard_map/ppermute | solution.py:348
  53.9 1.9 %collective-permute-done.9.refs_1_ = bf16[3,2,64,128]{3,2,1,0:T(8,128)(2,1)S(1)} collective-permute-done((bf16[3,2,64,128]{3,2,1,0:T(8,128)(2,1)S(1)}, bf16[3,2,64,128]{3,2,1,0:T(8,128)(2,1)S(1)}, u32[]{:S(2)}, u32[]{:S(2)}) %collective-permute-start.9) | collective-permute-done | bytes 98336 | tf_op jit(solution)/shard_map/ppermute | solution.py:348
  55.7 0.0 collective-permute-done.7.refs_0_
  55.8 0.8 %late_wires.1 = (bf16[5,2,64,128]{3,2,1,0:T(8,128)(2,1)S(1)}, bf16[5,2,64,128]{3,2,1,0:T(8,128)(2,1)S(1)}, bf16[8,2,64,128]{3,2,1,0:T(8,128)(2,1)S(1)}, bf16[8,2,64,128]{3,2,1,0:T(8,128)(2,1)S(1)}) custom-call(s32[1]{0:T(128)} %bitcast.me_ref, s32[16]{0:T(128)S(1)} %get-tuple-element.49.target_ref, s32[16]{0:T(128)S(1)} %get-tuple-element.50.rank_ref, ...), custom_call_target="tpu_custom_call" | custom-call | bytes 2097152 | tf_op jit(solution)/shard_map/late_wires/pallas_call | solution.py:300
  56.6 0.1 collective-permute-start.12
  56.6 2.6 %collective-permute-start.10 = (bf16[5,2,64,128]{3,2,1,0:T(8,128)(2,1)S(1)}, bf16[5,2,64,128]{3,2,1,0:T(8,128)(2,1)S(1)}, u32[]{:S(2)}, u32[]{:S(2)}) collective-permute-start(bf16[5,2,64,128]{3,2,1,0:T(8,128)(2,1)S(1)} %get-tuple-element.59), channel_id=1, source_target_pairs={{0,3},{1,2},{2,1},{3,0},{4,7},{5,6},{6,5},{7,4},{8,11},{9,10},{10,... | collective-permute-start | bytes 491528 | tf_op jit(solution)/shard_map/ppermute | solution.py:348
  59.2 0.9 %collective-permute-start.11 = (bf16[5,2,64,128]{3,2,1,0:T(8,128)(2,1)S(1)}, bf16[5,2,64,128]{3,2,1,0:T(8,128)(2,1)S(1)}, u32[]{:S(2)}, u32[]{:S(2)}) collective-permute-start(bf16[5,2,64,128]{3,2,1,0:T(8,128)(2,1)S(1)} %get-tuple-element.60), channel_id=1, source_target_pairs={{0,2},{1,3},{2,0},{3,1},{4,6},{5,7},{6,4},{7,5},{8,10},{9,11},{10,... | collective-permute-start | bytes 491528 | tf_op jit(solution)/shard_map/ppermute | solution.py:348
  60.1 9.6 %collective-permute-done.10.refs_2_ = bf16[5,2,64,128]{3,2,1,0:T(8,128)(2,1)S(1)} collective-permute-done((bf16[5,2,64,128]{3,2,1,0:T(8,128)(2,1)S(1)}, bf16[5,2,64,128]{3,2,1,0:T(8,128)(2,1)S(1)}, u32[]{:S(2)}, u32[]{:S(2)}) %collective-permute-start.10) | collective-permute-done | bytes 163872 | tf_op jit(solution)/shard_map/ppermute | solution.py:348
  69.7 3.7 %collective-permute-done.11.refs_3_ = bf16[5,2,64,128]{3,2,1,0:T(8,128)(2,1)S(1)} collective-permute-done((bf16[5,2,64,128]{3,2,1,0:T(8,128)(2,1)S(1)}, bf16[5,2,64,128]{3,2,1,0:T(8,128)(2,1)S(1)}, u32[]{:S(2)}, u32[]{:S(2)}) %collective-permute-start.11) | collective-permute-done | bytes 163872 | tf_op jit(solution)/shard_map/ppermute | solution.py:348
  73.4 0.0 collective-permute-done.12.refs_4_
  73.4 1.0 %collect.1 = bf16[32,2,64,128]{3,2,1,0:T(8,128)(2,1)} custom-call(s32[1]{0:T(128)} %bitcast.me_ref, bf16[3,2,64,128]{3,2,1,0:T(8,128)(2,1)S(1)} %collective-permute-done.8.refs_0_, bf16[3,2,64,128]{3,2,1,0:T(8,128)(2,1)S(1)} %collective-permute-done.9.refs_1_, bf16[5,2,64,128]{3,2,1,0:T(8,128)(2,1)S(1)} %collective-permute-done.10.refs_2_, ...), custom_call_target="tpu_custom_call" | custom-call | bytes 2097152 | tf_op jit(solution)/shard_map/collect/pallas_call | solution.py:331
  (1 shorter events, 0.0 us)
Async XLA Ops:
  0.0 10.3 %copy-start.1 = (s32[1,16,1]{1,2,0:T(1,128)S(1)}, s32[1,16,1]{1,2,0:T(1,128)}, u32[]{:S(2)}) copy-start(s32[1,16,1]{1,2,0:T(1,128)} %param.13) | copy-start | bytes 196
  0.0 11.8 %copy-start.4 = (s32[8,4]{0,1:T(4,128)S(1)}, s32[8,4]{0,1:T(4,128)}, u32[]{:S(2)}) copy-start(s32[8,4]{0,1:T(4,128)} %param.10) | copy-start | bytes 388
  0.0 12.0 %copy-start.3 = (bf16[1,4,2,128,320]{3,4,2,1,0:T(8,128)(2,1)S(1)}, bf16[1,4,2,128,320]{3,4,2,1,0:T(8,128)(2,1)}, u32[]{:S(2)}) copy-start(bf16[1,4,2,128,320]{3,4,2,1,0:T(8,128)(2,1)} %param.9) | copy-start | bytes 1966084
  0.6 16.7 %copy-start = (s32[3]{0:T(128)S(1)}, s32[3]{0:T(128)}, u32[]{:S(2)}) copy-start(s32[3]{0:T(128)} %pad_add_fusion.side_ref) | copy-start | bytes 40
  4.6 12.7 %collective-permute-start = (bf16[2,192,512]{2,1,0:T(8,128)(2,1)}, bf16[2,192,512]{2,1,0:T(8,128)(2,1)S(1)}, u32[]{:S(2)}, u32[]{:S(2)}) collective-permute-start(bf16[2,192,512]{2,1,0:T(8,128)(2,1)} %get-tuple-element.34), channel_id=1, source_target_pairs={{0,1},{1,0},{2,3},{3,2},{5,6},{6,5},{8,9},{9,8},{10,11},{11,10},{1... | collective-permute-start | bytes 1179656 | tf_op jit(solution)/shard_map/ppermute | solution.py:39
  9.6 7.7 %collective-permute-start.2 = (bf16[2,192,512]{2,1,0:T(8,128)(2,1)}, bf16[2,192,512]{2,1,0:T(8,128)(2,1)S(1)}, u32[]{:S(2)}, u32[]{:S(2)}) collective-permute-start(bf16[2,192,512]{2,1,0:T(8,128)(2,1)} %get-tuple-element.43), channel_id=1, source_target_pairs={{1,2},{2,1},{4,5},{5,4},{6,7},{7,6},{9,10},{10,9},{12,13},{13,12},... | collective-permute-start | bytes 1179656 | tf_op jit(solution)/shard_map/ppermute | solution.py:39
  10.3 3.6 %collective-permute-start.1 = (s32[1,16,1]{1,2,0:T(1,128)S(1)}, s32[1,16,1]{1,2,0:T(1,128)S(1)}, u32[]{:S(2)}, u32[]{:S(2)}) collective-permute-start(s32[1,16,1]{1,2,0:T(1,128)S(1)} %copy-done.1), channel_id=1, source_target_pairs={{0,8},{8,0},{4,12},{12,4},{16,24},{24,16},{20,28},{28,20},{1,9},{9... | collective-permute-start | bytes 200 | tf_op jit(solution)/shard_map/ppermute | solution.py:50
  17.3 1.0 %copy-start.2 = (bf16[2,256,512]{2,1,0:T(8,128)(2,1)S(1)}, bf16[2,256,512]{2,1,0:T(8,128)(2,1)}, u32[]{:S(2)}) copy-start(bf16[2,256,512]{2,1,0:T(8,128)(2,1)} %get-tuple-element.41.own_ref) | copy-start | bytes 1572868
  20.3 3.8 %collective-permute-start.3 = (bf16[2,512,256]{2,1,0:T(8,128)(2,1)S(1)}, bf16[2,512,256]{2,1,0:T(8,128)(2,1)S(1)}, u32[]{:S(2)}, u32[]{:S(2)}) collective-permute-start(bf16[2,512,256]{2,1,0:T(8,128)(2,1)S(1)} %get-tuple-element.45), channel_id=1, source_target_pairs={{0,4},{4,0},{8,12},{12,8},{16,20},{20,16},{24,28},{28,24},{1,5},{5... | collective-permute-start | bytes 1572872 | tf_op jit(solution)/shard_map/ppermute | solution.py:50
  24.3 10.0 %collective-permute-start.5 = (bf16[2,192,256]{2,1,0:T(8,128)(2,1)S(1)}, bf16[2,192,256]{2,1,0:T(8,128)(2,1)S(1)}, u32[]{:S(2)}, u32[]{:S(2)}) collective-permute-start(bf16[2,192,256]{2,1,0:T(8,128)(2,1)S(1)} %get-tuple-element.63), channel_id=1, source_target_pairs={{1,2},{2,1},{4,5},{5,4},{6,7},{7,6},{9,10},{10,9},{12,13},{13,12},... | collective-permute-start | bytes 589832 | tf_op jit(solution)/shard_map/ppermute | solution.py:39
  25.0 10.4 %collective-permute-start.4 = (bf16[2,192,256]{2,1,0:T(8,128)(2,1)S(1)}, bf16[2,192,256]{2,1,0:T(8,128)(2,1)S(1)}, u32[]{:S(2)}, u32[]{:S(2)}) collective-permute-start(bf16[2,192,256]{2,1,0:T(8,128)(2,1)S(1)} %get-tuple-element.64), channel_id=1, source_target_pairs={{0,1},{1,0},{2,3},{3,2},{5,6},{6,5},{8,9},{9,8},{10,11},{11,10},{1... | collective-permute-start | bytes 589832 | tf_op jit(solution)/shard_map/ppermute | solution.py:39
  37.3 7.8 %collective-permute-start.6 = (bf16[6,2,64,128]{3,2,1,0:T(8,128)(2,1)S(1)}, bf16[6,2,64,128]{3,2,1,0:T(8,128)(2,1)S(1)}, u32[]{:S(2)}, u32[]{:S(2)}) collective-permute-start(bf16[6,2,64,128]{3,2,1,0:T(8,128)(2,1)S(1)} %get-tuple-element.46), channel_id=1, source_target_pairs={{0,8},{8,0},{4,12},{12,4},{16,24},{24,16},{20,28},{28,20},{1,9},{9... | collective-permute-start | bytes 589832 | tf_op jit(solution)/shard_map/ppermute | solution.py:50
  45.2 10.6 %collective-permute-start.7 = (bf16[10,2,64,128]{3,2,1,0:T(8,128)(2,1)S(1)}, bf16[10,2,64,128]{3,2,1,0:T(8,128)(2,1)S(1)}, u32[]{:S(2)}, u32[]{:S(2)}) collective-permute-start(bf16[10,2,64,128]{3,2,1,0:T(8,128)(2,1)S(1)} %get-tuple-element.48), channel_id=1, source_target_pairs={{0,8},{8,0},{4,12},{12,4},{16,24},{24,16},{20,28},{28,20},{1,9},{9... | collective-permute-start | bytes 983048 | tf_op jit(solution)/shard_map/ppermute | solution.py:50
  47.3 6.6 %collective-permute-start.8 = (bf16[3,2,64,128]{3,2,1,0:T(8,128)(2,1)S(1)}, bf16[3,2,64,128]{3,2,1,0:T(8,128)(2,1)S(1)}, u32[]{:S(2)}, u32[]{:S(2)}) collective-permute-start(bf16[3,2,64,128]{3,2,1,0:T(8,128)(2,1)S(1)} %get-tuple-element.53), channel_id=1, source_target_pairs={{0,3},{1,2},{2,1},{3,0},{4,7},{5,6},{6,5},{7,4},{8,11},{9,10},{10,... | collective-permute-start | bytes 294920 | tf_op jit(solution)/shard_map/ppermute | solution.py:348
  47.4 8.4 %collective-permute-start.9 = (bf16[3,2,64,128]{3,2,1,0:T(8,128)(2,1)S(1)}, bf16[3,2,64,128]{3,2,1,0:T(8,128)(2,1)S(1)}, u32[]{:S(2)}, u32[]{:S(2)}) collective-permute-start(bf16[3,2,64,128]{3,2,1,0:T(8,128)(2,1)S(1)} %get-tuple-element.54), channel_id=1, source_target_pairs={{0,2},{1,3},{2,0},{3,1},{4,6},{5,7},{6,4},{7,5},{8,10},{9,11},{10,... | collective-permute-start | bytes 294920 | tf_op jit(solution)/shard_map/ppermute | solution.py:348
  56.6 16.9 %collective-permute-start.12 = (bf16[8,2,64,128]{3,2,1,0:T(8,128)(2,1)S(1)}, bf16[8,2,64,128]{3,2,1,0:T(8,128)(2,1)S(1)}, u32[]{:S(2)}, u32[]{:S(2)}) collective-permute-start(bf16[8,2,64,128]{3,2,1,0:T(8,128)(2,1)S(1)} %get-tuple-element.61), channel_id=1, source_target_pairs={{0,1},{1,0},{2,3},{3,2},{4,5},{5,4},{6,7},{7,6},{8,9},{9,8},{10,11... | collective-permute-start | bytes 786440 | tf_op jit(solution)/shard_map/ppermute | solution.py:348
  56.6 13.0 %collective-permute-start.10 = (bf16[5,2,64,128]{3,2,1,0:T(8,128)(2,1)S(1)}, bf16[5,2,64,128]{3,2,1,0:T(8,128)(2,1)S(1)}, u32[]{:S(2)}, u32[]{:S(2)}) collective-permute-start(bf16[5,2,64,128]{3,2,1,0:T(8,128)(2,1)S(1)} %get-tuple-element.59), channel_id=1, source_target_pairs={{0,3},{1,2},{2,1},{3,0},{4,7},{5,6},{6,5},{7,4},{8,11},{9,10},{10,... | collective-permute-start | bytes 491528 | tf_op jit(solution)/shard_map/ppermute | solution.py:348
  59.2 14.2 %collective-permute-start.11 = (bf16[5,2,64,128]{3,2,1,0:T(8,128)(2,1)S(1)}, bf16[5,2,64,128]{3,2,1,0:T(8,128)(2,1)S(1)}, u32[]{:S(2)}, u32[]{:S(2)}) collective-permute-start(bf16[5,2,64,128]{3,2,1,0:T(8,128)(2,1)S(1)} %get-tuple-element.60), channel_id=1, source_target_pairs={{0,2},{1,3},{2,0},{3,1},{4,6},{5,7},{6,4},{7,5},{8,10},{9,11},{10,... | collective-permute-start | bytes 491528 | tf_op jit(solution)/shard_map/ppermute | solution.py:348

commit v4 on v3

--- a/solution.py
+++ b/solution.py
@@ -13,7 +13,7 @@
 OS = 64
 MARGIN_BLOCKS = (NW - 2) // 2 + REACH
 VMEM_LIMIT = 8 * 1024 * 1024
-WHOLE_VMEM = 60 * 1024 * 1024
+MOST_VMEM = 53 * 1024 * 1024
 ANY = pl.BlockSpec(memory_space=pl.ANY)
 VMEM = pl.BlockSpec(memory_space=pltpu.VMEM)
 SMEM = pl.BlockSpec(memory_space=pltpu.SMEM)
@@ -54,11 +54,14 @@
     return jnp.dot(left, right, preferred_element_type=jnp.float32)
 
 
-def resample_kernel(side_ref, child_hbm, kernel_hbm, own_ref, first_ref, second_ref, child, kernel, sems):
-    even, half, quarter = side_ref[0], side_ref[1], side_ref[2]
-    rng = child.shape[2]
+def resample_kernel(child_hbm, kernel_hbm, first_ref, second_ref, child, kernel, own, sems):
+    aper, beam = lax.axis_index("aperture"), lax.axis_index("beam")
+    half, quarter = aper & 1, (aper >> 1) & 1
+    even = 1 - ((aper + beam) & 1)
+    rows, rng = child.shape[1:]
     piece = rng // 4
-    copies = [pltpu.make_async_copy(child_hbm, child, sems.at[4])]
+    child_copy = pltpu.make_async_copy(child_hbm, child, sems.at[4])
+    copies = []
     for place in range(4):
         source = (half ^ (place // 2)) * 2 + (quarter ^ (place % 2))
         copies.append(
@@ -68,131 +71,171 @@
                 sems.at[place],
             )
         )
+    child_copy.start()
     for copy in copies:
         copy.start()
-    for copy in copies:
-        copy.wait()
+    child_copy.wait()
     real, imag = child[0], child[1]
-    k_real, k_imag = kernel[0], kernel[1]
-    own_ref[0] = (dot(real, k_real) - dot(imag, k_imag)).astype(jnp.bfloat16)
-    own_ref[1] = (dot(real, k_imag) + dot(imag, k_real)).astype(jnp.bfloat16)
-    rows, margin = own_ref.shape[1], first_ref.shape[1]
-    tail = pl.multiple_of(even * (rows - margin), BLK)
-    head = pl.multiple_of((1 - even) * (rows - margin), BLK)
-    first_ref[...] = own_ref[:, pl.ds(tail, margin), :]
-    second_ref[...] = own_ref[:, pl.ds(head, margin), :]
-
-
-def resample(side, child, kernel, margin):
+    margin = first_ref.shape[1]
+    tail = pl.ds(pl.multiple_of(even * (rows - margin), BLK), margin)
+    head = pl.ds(pl.multiple_of((1 - even) * (rows - margin), BLK), margin)
+    for side in range(2):
+        columns = slice(side * 2 * piece, (side + 1) * 2 * piece)
+        copies[2 * side].wait()
+        copies[2 * side + 1].wait()
+        k_real, k_imag = kernel[0, :, columns], kernel[1, :, columns]
+        own[0, :, columns] = (dot(real, k_real) - dot(imag, k_imag)).astype(jnp.bfloat16)
+        own[1, :, columns] = (dot(real, k_imag) + dot(imag, k_real)).astype(jnp.bfloat16)
+        for part in range(2):
+            first_ref[part, :, columns] = own[part, tail, columns]
+            second_ref[part, :, columns] = own[part, head, columns]
+
+
+def resample(child, kernel, margin):
     rows, rng = child.shape[1:]
-    shapes = [
-        jax.ShapeDtypeStruct((2, count, rng), jnp.bfloat16) for count in (rows, margin, margin)
-    ]
+    shape = jax.ShapeDtypeStruct((2, margin, rng), jnp.bfloat16)
     return pl.pallas_call(
         resample_kernel,
-        out_shape=shapes,
-        in_specs=[SMEM, ANY, ANY],
-        out_specs=[VMEM] * 3,
+        out_shape=(shape, shape),
+        in_specs=[ANY, ANY],
+        out_specs=(VMEM, VMEM),
         scratch_shapes=[
             pltpu.VMEM(child.shape, jnp.bfloat16),
             pltpu.VMEM(kernel.shape, jnp.bfloat16),
+            pltpu.VMEM(child.shape, jnp.bfloat16),
             pltpu.SemaphoreType.DMA((5,)),
         ],
-        compiler_params=params(WHOLE_VMEM),
+        compiler_params=params(MOST_VMEM),
         cost_estimate=cost(4 * rows * rng * rng, 2**21),
         name="resample",
-    )(side, child, kernel)
-
-
-def complex_window(weights_ref, sector, real, imag):
-    beams = weights_ref.shape[1] // 2
-    with_real = dot(weights_ref[sector], real)
-    with_imag = dot(weights_ref[sector], imag)
+    )(child, kernel)
+
+
+def complex_window(weights, real, imag):
+    beams = weights.shape[0] // 2
+    with_real = dot(weights, real)
+    with_imag = dot(weights, imag)
     return (
         (with_real[:beams] - with_imag[beams:]).astype(jnp.bfloat16),
         (with_imag[:beams] + with_real[beams:]).astype(jnp.bfloat16),
     )
 
 
-def pad_with(padded, even, own_ref, first_ref, second_ref):
-    margin, rows = first_ref.shape[1], own_ref.shape[1]
+def place_halos(padded, even, rows, first, second):
+    margin = first.shape[1]
     far = margin + rows
-    padded[:, margin:far, :] = own_ref[...]
-    padded[:, pl.ds(pl.multiple_of(even * far, BLK), margin), :] = first_ref[...]
-    padded[:, pl.ds(pl.multiple_of((1 - even) * far, BLK), margin), :] = second_ref[...]
+    padded[:, pl.ds(pl.multiple_of(even * far, BLK), margin), :] = first
+    padded[:, pl.ds(pl.multiple_of((1 - even) * far, BLK), margin), :] = second
 
 
 def first_level_kernel(
-    starts_ref, side_ref, own_ref, first_ref, second_ref, weights_ref, keep_ref, send_ref, padded
+    column, rows, starts_ref, side_ref, sent_first_ref, sent_second_ref, first_ref, second_ref,
+    weights_ref, out_ref, padded,
 ):
     sectors, stacked, window = weights_ref.shape
     beams = stacked // 2
-    width = keep_ref.shape[2]
-    pad_with(padded, side_ref[0], own_ref, first_ref, second_ref)
+    margin = first_ref.shape[1]
+    columns = slice(column, column + out_ref.shape[2])
+    even = side_ref[0]
+    tail = pl.multiple_of(margin + even * (rows - margin), BLK)
+    head = pl.multiple_of(margin + (1 - even) * (rows - margin), BLK)
+    padded[:, pl.ds(tail, margin), :] = sent_first_ref[:, :, columns]
+    padded[:, pl.ds(head, margin), :] = sent_second_ref[:, :, columns]
+    place_halos(padded, even, rows, first_ref[:, :, columns], second_ref[:, :, columns])
     for sector in range(sectors):
         place = pl.ds(pl.multiple_of(starts_ref[sector] * BLK, BLK), window)
-        parts = complex_window(weights_ref, sector, padded[0, place, :], padded[1, place, :])
-        out = pl.ds(sector * beams, beams)
+        parts = complex_window(weights_ref[sector], padded[0, place, :], padded[1, place, :])
         for part in range(2):
-            keep_ref[part, out, :] = parts[part][:, :width]
-            send_ref[part, out, :] = parts[part][:, width:]
-
-
-def first_level(starts, side, own, first, second, weights):
+            out_ref[part, sector * beams : (sector + 1) * beams, :] = parts[part]
+
+
+def first_level(column, rows, starts, side, sent, halos, weights):
     sectors, stacked, window = weights.shape
-    rng = own.shape[2]
-    margin, rows = first.shape[1], own.shape[1]
-    shape = jax.ShapeDtypeStruct((2, sectors * stacked // 2, rng // 2), jnp.bfloat16)
+    margin, rng = sent[0].shape[1:]
+    assert 2 * margin >= rows
+    width = rng // 2
     return pl.pallas_call(
-        first_level_kernel,
-        out_shape=(shape, shape),
-        in_specs=[SMEM, SMEM] + [VMEM] * 4,
-        out_specs=(VMEM, VMEM),
-        scratch_shapes=[pltpu.VMEM((2, rows + 2 * margin, rng), jnp.bfloat16)],
-        compiler_params=params(),
-        cost_estimate=cost(sectors * 2 * stacked * window * rng, 2**22),
+        functools.partial(first_level_kernel, column, rows),
+        out_shape=jax.ShapeDtypeStruct((2, sectors * stacked // 2, width), jnp.bfloat16),
+        in_specs=[SMEM, SMEM] + [VMEM] * 5,
+        out_specs=VMEM,
+        scratch_shapes=[pltpu.VMEM((2, rows + 2 * margin, width), jnp.bfloat16)],
+        compiler_params=params(),
+        cost_estimate=cost(sectors * 2 * stacked * window * width, 2**21),
         name="first_level",
-    )(starts, side, own, first, second, weights)
+    )(starts, side, *sent, *halos, weights)
+
+
+def second_level_early_kernel(
+    starts_ref, side_ref, sector_ref, own_ref, first_ref, second_ref, weights_ref, send_ref, padded
+):
+    _, stacked, window = weights_ref.shape
+    per = stacked // 2 // OS
+    margin, rows = first_ref.shape[1], own_ref.shape[1]
+    columns = slice(send_ref.shape[3], 2 * send_ref.shape[3])
+    padded[:, margin : margin + rows, :] = own_ref[:, :, columns]
+    place_halos(padded, side_ref[0], rows, first_ref[:, :, columns], second_ref[:, :, columns])
+    for place in range(send_ref.shape[0]):
+        sector = sector_ref[place] // per
+        piece = pl.multiple_of(sector_ref[place] % per * OS, OS)
+        window_rows = pl.ds(pl.multiple_of(starts_ref[sector] * BLK, BLK), window)
+        weights = jnp.concatenate(
+            [
+                weights_ref[sector, pl.ds(piece, OS), :],
+                weights_ref[sector, pl.ds(pl.multiple_of(piece + stacked // 2, OS), OS), :],
+            ]
+        )
+        parts = complex_window(weights, padded[0, window_rows, :], padded[1, window_rows, :])
+        for part in range(2):
+            send_ref[place, part] = parts[part]
 
 
 def second_level_kernel(
     starts_ref, side_ref, own_at_ref, other_at_ref, own_ref, first_ref, second_ref, weights_ref,
-    keep_ref, *refs,
+    keep_ref, send_ref, padded, send,
 ):
-    send_refs, (padded, send) = refs[:-2], refs[-2:]
     sectors, stacked, window = weights_ref.shape
     beams = stacked // 2
     width = keep_ref.shape[3]
-    pad_with(padded, side_ref[0], own_ref, first_ref, second_ref)
+    margin, rows = first_ref.shape[1], own_ref.shape[1]
+    padded[:, margin : margin + rows, :] = own_ref[...]
+    place_halos(padded, side_ref[0], rows, first_ref[...], second_ref[...])
     per = beams // OS
     for sector in range(sectors):
         place = pl.ds(pl.multiple_of(starts_ref[sector] * BLK, BLK), window)
-        parts = complex_window(weights_ref, sector, padded[0, place, :], padded[1, place, :])
+        parts = complex_window(weights_ref[sector], padded[0, place, :], padded[1, place, :])
         for piece in range(per):
             own_at = own_at_ref[sector * per + piece]
             other_at = other_at_ref[sector * per + piece]
-            rows = slice(piece * OS, (piece + 1) * OS)
+            taken = slice(piece * OS, (piece + 1) * OS)
             for part in range(2):
-                keep_ref[own_at, part] = parts[part][rows, :width]
-                send[other_at, part] = parts[part][rows, width:]
-    done = 0
-    for ref in send_refs:
-        ref[...] = send[done : done + ref.shape[0]]
-        done += ref.shape[0]
-
-
-def second_level(starts, side, own_at, other_at, own, first, second, weights, chunks):
+                keep_ref[own_at, part] = parts[part][taken, :width]
+                send[other_at, part] = parts[part][taken, width:]
+    send_ref[...] = send[send.shape[0] - send_ref.shape[0] :]
+
+
+def second_level(starts, side, planned, own, halos, weights, early):
     sectors, stacked, window = weights.shape
-    rng = own.shape[2]
-    margin, rows = first.shape[1], own.shape[1]
+    margin, rows, rng = halos[0].shape[1], own.shape[1], own.shape[2]
     count = sectors * stacked // 2 // OS
     block = (2, OS, rng // 2)
-    shapes = [jax.ShapeDtypeStruct((n,) + block, jnp.bfloat16) for n in (count,) + chunks]
-    return pl.pallas_call(
+    own_at, other_at, other_sector = planned
+    early_send = pl.pallas_call(
+        second_level_early_kernel,
+        out_shape=jax.ShapeDtypeStruct((early,) + block, jnp.bfloat16),
+        in_specs=[SMEM] * 3 + [VMEM] * 4,
+        out_specs=VMEM,
+        scratch_shapes=[pltpu.VMEM((2, rows + 2 * margin, rng // 2), jnp.bfloat16)],
+        compiler_params=params(),
+        cost_estimate=cost(early * 2 * 2 * OS * window * rng // 2, 2**20),
+        name="second_level_early",
+    )(starts, side, other_sector, own, *halos, weights)
+    shapes = [jax.ShapeDtypeStruct((n,) + block, jnp.bfloat16) for n in (count, count - early)]
+    keep, late_send = pl.pallas_call(
         second_level_kernel,
         out_shape=shapes,
         in_specs=[SMEM] * 4 + [VMEM] * 4,
-        out_specs=[VMEM] * len(shapes),
+        out_specs=[VMEM] * 2,
         scratch_shapes=[
             pltpu.VMEM((2, rows + 2 * margin, rng), jnp.bfloat16),
             pltpu.VMEM((count,) + block, jnp.bfloat16),
@@ -200,11 +243,13 @@
         compiler_params=params(),
         cost_estimate=cost(sectors * 2 * stacked * window * rng, 2**22),
         name="second_level",
-    )(starts, side, own_at, other_at, own, first, second, weights)
+    )(starts, side, own_at, other_at, own, *halos, weights)
+    return keep, early_send, late_send
 
 
 def plan_kernel(
-    me_ref, own_ref, other_ref, own_at_ref, other_at_ref, target_ref, rank_ref, taken, filled
+    me_ref, own_ref, other_ref, own_at_ref, other_at_ref, other_sector_ref, target_ref, rank_ref,
+    taken, filled,
 ):
     count = own_ref.shape[0]
     far_bit = taken.shape[0] // 2
@@ -230,6 +275,8 @@
             if at_ref is own_at_ref:
                 target_ref[place] = owners_ref[sector]
                 rank_ref[place] = jnp.where(bucket >= count, bucket - count, bucket)
+            else:
+                other_sector_ref[place] = sector
 
 
 def plan(me, own, other, beam_count):
@@ -237,9 +284,9 @@
     shape = jax.ShapeDtypeStruct((count,), jnp.int32)
     return pl.pallas_call(
         plan_kernel,
-        out_shape=[shape] * 4,
+        out_shape=[shape] * 5,
         in_specs=[SMEM] * 3,
-        out_specs=[SMEM] * 4,
+        out_specs=[SMEM] * 5,
         scratch_shapes=[
             pltpu.SMEM((beam_count,), jnp.int32),
             pltpu.SMEM((2 * count + 1,), jnp.int32),
@@ -362,46 +409,47 @@
     beam_index = lax.axis_index("beam")
     beam_count = lax.axis_size("beam")
     margin = MARGIN_BLOCKS * BLK
-    local_blocks = subimages.shape[2] // BLK
+    rows = subimages.shape[2]
+    local_blocks = rows // BLK
     even = ((beam_index + aper_index) % 2 == 0).astype(jnp.int32)
-    side = jnp.stack([even, aper_index % 2, aper_index // 2 % 2])
+    side = even.reshape(1)
     me = beam_index.reshape(1)
 
     sector_count = owners.shape[1]
     capacity = max(2, 2 * sector_count // beam_count)
     early = max(1, 3 * capacity // 8)
     far = beam_count // 2
-    chunks = (early * far, sector_count - early * far)
     distances = list(reversed(range(beam_count)))
     early_spans = tuple((distance, 0, early) for distance in distances if distance >= far)
     late_spans = tuple(
         (distance, early if distance >= far else 0, capacity) for distance in distances
     )
 
-    own, first, second = resample(side, subimages[0], range_kernel[0], margin)
-    first, second = trade_edges(first, second)
+    sent = resample(subimages[0], range_kernel[0], margin)
+    halos = trade_edges(*sent)
     own_owners = owners[0, :, 0]
     other_owners = partner(owners, "aperture", 1)[0, :, 0]
-    own_at, other_at, target, rank = plan(me, own_owners, other_owners, beam_count)
+    planned = plan(me, own_owners, other_owners, beam_count)
     begin0 = table_row(starts0, aper_index) - (beam_index * local_blocks - MARGIN_BLOCKS)
-    first, own_at, other_at, target, rank = lax.optimization_barrier(
-        (first, own_at, other_at, target, rank)
+    halos, planned = lax.optimization_barrier((halos, planned))
+    *planned, target, rank = planned
+    width = range_kernel.shape[3] // 2
+    weights = stacked_weights(weights0)
+    send = first_level(width, rows, begin0, side, sent, halos, weights)
+    other = partner(send, "aperture", 0)
+    keep = first_level(0, rows, begin0, side, sent, halos, weights)
+    level_one = (keep.astype(jnp.float32) + other.astype(jnp.float32)).astype(jnp.bfloat16)
+
+    beams = level_one.shape[1]
+    first = lax.dynamic_slice_in_dim(level_one, even * (beams - margin), margin, 1)
+    second = lax.dynamic_slice_in_dim(level_one, (1 - even) * (beams - margin), margin, 1)
+    halos = trade_edges(first, second)
+    begin1 = table_row(starts1, aper_index) - (beam_index * 2 * local_blocks - MARGIN_BLOCKS)
+    keep, send, late = second_level(
+        begin1, side, planned, level_one, halos, stacked_weights(weights1), early * far
     )
-    keep, send = first_level(begin0, side, own, first, second, stacked_weights(weights0))
-    other = partner(send, "aperture", 0)
-    level_one = (keep.astype(jnp.float32) + other.astype(jnp.float32)).astype(jnp.bfloat16)
-
-    rows = level_one.shape[1]
-    first = lax.dynamic_slice_in_dim(level_one, even * (rows - margin), margin, 1)
-    second = lax.dynamic_slice_in_dim(level_one, (1 - even) * (rows - margin), margin, 1)
-    first, second = trade_edges(first, second)
-    begin1 = table_row(starts1, aper_index) - (beam_index * 2 * local_blocks - MARGIN_BLOCKS)
-    keep, *sends = second_level(
-        begin1, side, own_at, other_at, level_one, first, second, stacked_weights(weights1), chunks
-    )
-    other = partner(sends[0], "aperture", 1)
-
-    other, late = lax.optimization_barrier((other, sends[1]))
+    other = partner(send, "aperture", 1)
+    other, late = lax.optimization_barrier((other, late))
     late = partner(late, "aperture", 1)
     summed, *group = wires(early_spans, me, target, rank, keep, other)
     received = spread(early_spans, group)

time: 74.8 us -> 70.6 us (0.944)
  waiting for transfers between devices: 32.4 us -> 26.5 us
  starting transfers between devices: 25.2 us -> 28.5 us
  local copies, waits for them, and re-layouts: 3.29 us -> 2.24 us
    ppermute x4, waiting for transfers between devices: 9.3 us -> 3.78 us  [partner(): return lax.ppermute(block, axis, route)]
    ppermute x5, starting transfers between devices: 5.18 us -> 9.98 us  [spread(): received.append(lax.ppermute(wire, 'beam', route) if distance else wire)]
    ppermute x4, starting transfers between devices: 13.1 us -> 10.2 us  [trade_edges(): received.append(lax.ppermute(block, ('aperture', 'beam'), route))]
    ppermute x4, starting transfers between devices: 6.91 us -> 8.27 us  [partner(): return lax.ppermute(block, axis, route)]
    unnamed x12 -> x8, local copies, waits for them, and re-layouts: 3.25 us -> 2.2 us
    ppermute x4, waiting for transfers between devices: 2.99 us -> 2.09 us  [trade_edges(): received.append(lax.ppermute(block, ('aperture', 'beam'), route))]
    pallas_call x3 -> x5, Pallas kernels: 7.38 us -> 7.54 us  [the longest x2 2.59 us: first_level(): pl.pallas_call(functools.partial(first_level_kernel, column, rows), out_s...]
  transfers between devices with their start and end apart: 13 -> 13, of which waited for: 9 -> 9; matrix products, arithmetic and copies ran while one was open for 4% -> 4% of each run, Pallas kernels for 3% -> 8%
where the time goes in v4:
time: 70.6 us; the launch traced here: 70.3 us
  starting transfers between devices  28.5 us (40%)
  waiting for transfers between devices  26.5 us (38%)
  Pallas kernels  12 us (17%)
  local copies, waits for them, and re-layouts  2.24 us (3%)
  other arithmetic  1.01 us (1%)
    ppermute x5, waiting for transfers between devices, spread(): received.append(lax.ppermute(wire, 'beam', route) if distance else wire)  20.7 us
    ppermute x4, starting transfers between devices, trade_edges(): received.append(lax.ppermute(block, ('aperture', 'beam'), route))  10.2 us
    ppermute x5, starting transfers between devices, spread(): received.append(lax.ppermute(wire, 'beam', route) if distance else wire)  9.98 us
    ppermute x4, starting transfers between devices, partner(): return lax.ppermute(block, axis, route)  8.27 us
    ppermute x4, waiting for transfers between devices, partner(): return lax.ppermute(block, axis, route)  3.78 us
    pallas_call x2, Pallas kernels, first_level(): pl.pallas_call(functools.partial(first_level_kernel, column, rows), out_s...  2.59 us
    pallas_call x1, Pallas kernels, resample(): pl.pallas_call(resample_kernel, out_shape=(shape, shape), in_specs=[ANY,...  2.31 us
    unnamed x8, local copies, waits for them, and re-layouts  2.2 us
  transfers between devices with their start and end apart: 13, of which 9 were waited for; matrix products, arithmetic and copies ran while one was open for 4% of the time, Pallas kernels for 8%

profile of v4, /device:TPU:0, one launch (start us, length us, event | category | flops | bytes accessed | tf_op | source)
XLA Modules:
  0.0 70.3 jit_solution(14978039777768333797)
XLA Ops:
  0.0 0.0 copy-start
  0.0 0.0 copy-start.2
  0.0 0.0 copy-start.1
  0.0 2.3 %resample.1 = (bf16[2,192,512]{2,1,0:T(8,128)(2,1)S(1)}, bf16[2,192,512]{2,1,0:T(8,128)(2,1)S(1)}) custom-call(bf16[2,256,512]{2,1,0:T(8,128)(2,1)} %bitcast.18, bf16[2,512,512]{2,1,0:T(8,128)(2,1)} %bitcast.17), custom_call_target="tpu_custom_call" | custom-call | flops 536870912 | bytes 2097152 | tf_op jit(solution)/shard_map/resample/pallas_call | solution.py:97
  2.3 4.9 %collective-permute-start = (bf16[2,192,512]{2,1,0:T(8,128)(2,1)S(1)}, bf16[2,192,512]{2,1,0:T(8,128)(2,1)S(1)}, u32[]{:S(2)}, u32[]{:S(2)}) collective-permute-start(bf16[2,192,512]{2,1,0:T(8,128)(2,1)S(1)} %get-tuple-element.33.sent_first_ref), channel_id=1, source_target_pairs={{0,1},{1,0},{2,3},{3,2},{5,6},{6,5},{8,9},{9,8},{10,11},{11,10},{1... | collective-permute-start | bytes 1179656 | tf_op jit(solution)/shard_map/ppermute | solution.py:39
  7.3 0.7 collective-permute-start.1
  8.0 0.0 copy-done
  8.0 1.6 %collective-permute-start.2 = (s32[1,16,1]{1,2,0:T(1,128)S(1)}, s32[1,16,1]{1,2,0:T(1,128)S(1)}, u32[]{:S(2)}, u32[]{:S(2)}) collective-permute-start(s32[1,16,1]{1,2,0:T(1,128)S(1)} %copy-done), channel_id=1, source_target_pairs={{0,8},{8,0},{4,12},{12,4},{16,24},{24,16},{20,28},{28,20},{1,9},{9... | collective-permute-start | bytes 200 | tf_op jit(solution)/shard_map/ppermute | solution.py:50
  9.5 0.0 copy-done.2
  9.5 0.2 subtract_reduce_fusion.starts_ref
  9.7 0.0 copy-done.1
  9.7 0.4 copy.8
  10.1 1.5 %collective-permute-done.2 = s32[1,16,1]{1,2,0:T(1,128)S(1)} collective-permute-done((s32[1,16,1]{1,2,0:T(1,128)S(1)}, s32[1,16,1]{1,2,0:T(1,128)S(1)}, u32[]{:S(2)}, u32[]{:S(2)}) %collective-permute-start.2) | collective-permute-done | bytes 96 | tf_op jit(solution)/shard_map/ppermute | solution.py:50
  11.6 1.5 %plan.1 = (s32[16]{0:T(128)S(1)}, s32[16]{0:T(128)S(1)}, s32[16]{0:T(128)S(1)}, s32[16]{0:T(128)S(1)}, s32[16]{0:T(128)S(1)}) custom-call(s32[1]{0:T(128)} %bitcast.me_ref, s32[16]{0:T(128)S(1)} %bitcast.15, s32[16]{0:T(128)S(1)} %bitcast.16), custom_call_target="tpu_custom_call" | custom-call | tf_op jit(solution)/shard_map/plan/pallas_call | solution.py:285
  13.1 1.7 %collective-permute-done.first_ref = bf16[2,192,512]{2,1,0:T(8,128)(2,1)S(1)} collective-permute-done((bf16[2,192,512]{2,1,0:T(8,128)(2,1)S(1)}, bf16[2,192,512]{2,1,0:T(8,128)(2,1)S(1)}, u32[]{:S(2)}, u32[]{:S(2)}) %collective-permute-start) | collective-permute-done | bytes 393248 | tf_op jit(solution)/shard_map/ppermute | solution.py:39
  14.8 0.0 collective-permute-done.1.second_ref
  14.8 1.3 %first_level.3 = bf16[2,512,256]{2,1,0:T(8,128)(2,1)S(1)} custom-call(s32[4]{0:T(128)S(1)} %subtract_reduce_fusion.starts_ref, s32[1]{0:T(128)} %bitcast.2.side_ref, bf16[2,192,512]{2,1,0:T(8,128)(2,1)S(1)} %get-tuple-element.33.sent_first_ref, bf16[2,192,512]{2,1,0:T(8,128)(2,1)S(1)} %get-tuple-element.34.sent_second_ref, ...), custom_call_target="tpu_custom_call" | custom-call | flops 335544320 | bytes 2097152 | tf_op jit(solution)/shard_map/first_level/pallas_call | solution.py:157
  16.1 2.3 %collective-permute-start.3 = (bf16[2,512,256]{2,1,0:T(8,128)(2,1)S(1)}, bf16[2,512,256]{2,1,0:T(8,128)(2,1)S(1)}, u32[]{:S(2)}, u32[]{:S(2)}) collective-permute-start(bf16[2,512,256]{2,1,0:T(8,128)(2,1)S(1)} %first_level.3), channel_id=1, source_target_pairs={{0,4},{4,0},{8,12},{12,8},{16,20},{20,16},{24,28},{28,24},{1,5},{5... | collective-permute-start | bytes 1572872 | tf_op jit(solution)/shard_map/ppermute | solution.py:50
  18.4 1.3 %first_level.2 = bf16[2,512,256]{2,1,0:T(8,128)(2,1)S(1)} custom-call(s32[4]{0:T(128)S(1)} %subtract_reduce_fusion.starts_ref, s32[1]{0:T(128)} %bitcast.2.side_ref, bf16[2,192,512]{2,1,0:T(8,128)(2,1)S(1)} %get-tuple-element.33.sent_first_ref, bf16[2,192,512]{2,1,0:T(8,128)(2,1)S(1)} %get-tuple-element.34.sent_second_ref, ...), custom_call_target="tpu_custom_call" | custom-call | flops 335544320 | bytes 2097152 | tf_op jit(solution)/shard_map/first_level/pallas_call | solution.py:157
  19.7 0.2 collective-permute-done.3
  19.9 0.1 add_convert_fusion.own_ref
  20.1 3.9 %collective-permute-start.4 = (bf16[2,192,256]{2,1,0:T(8,128)(2,1)S(1)}, bf16[2,192,256]{2,1,0:T(8,128)(2,1)S(1)}, u32[]{:S(2)}, u32[]{:S(2)}) collective-permute-start(bf16[2,192,256]{2,1,0:T(8,128)(2,1)S(1)} %get-tuple-element.62), channel_id=1, source_target_pairs={{0,1},{1,0},{2,3},{3,2},{5,6},{6,5},{8,9},{9,8},{10,11},{11,10},{1... | collective-permute-start | bytes 589832 | tf_op jit(solution)/shard_map/ppermute | solution.py:39
  24.0 0.7 collective-permute-start.5
  24.7 1.8 %copy.9 = bf16[1,8,2,128,320]{4,3,2,1,0:T(8,128)(2,1)S(1)} copy(bf16[1,8,2,128,320]{3,4,2,1,0:T(8,128)(2,1)} %param.11) | data formatting | bytes 2621440 | tf_op args[4]
  26.6 0.7 fusion.1.starts_ref
  27.3 0.4 collective-permute-done.4.first_ref
  27.7 0.0 collective-permute-done.5.second_ref
  27.7 1.1 %second_level_early.1 = bf16[6,2,64,128]{3,2,1,0:T(8,128)(2,1)S(1)} custom-call(s32[8]{0:T(128)S(1)} %fusion.1.starts_ref, s32[1]{0:T(128)} %bitcast.2.side_ref, s32[16]{0:T(128)S(1)} %get-tuple-element.40.sector_ref, bf16[2,512,256]{2,1,0:T(8,128)(2,1)S(1)} %add_convert_fusion.own_ref, bf16[2,192,256]{2,1,0:T(8,128)(2,1)S(1)} %collective-permute-done.4.first_ref, ...), custom_call_target="tpu_custom_call" | custom-call | flops 125829120 | bytes 1048576 | tf_op jit(solution)/shard_map/second_level_early/pallas_call | solution.py:223
  28.8 2.0 %collective-permute-start.6 = (bf16[6,2,64,128]{3,2,1,0:T(8,128)(2,1)S(1)}, bf16[6,2,64,128]{3,2,1,0:T(8,128)(2,1)S(1)}, u32[]{:S(2)}, u32[]{:S(2)}) collective-permute-start(bf16[6,2,64,128]{3,2,1,0:T(8,128)(2,1)S(1)} %second_level_early.1), channel_id=1, source_target_pairs={{0,8},{8,0},{4,12},{12,4},{16,24},{24,16},{20,28},{28,20},{1,9},{9... | collective-permute-start | bytes 589832 | tf_op jit(solution)/shard_map/ppermute | solution.py:50
  30.8 2.0 %second_level.1 = (bf16[16,2,64,128]{3,2,1,0:T(8,128)(2,1)S(1)}, bf16[10,2,64,128]{3,2,1,0:T(8,128)(2,1)S(1)}) custom-call(s32[8]{0:T(128)S(1)} %fusion.1.starts_ref, s32[1]{0:T(128)} %bitcast.2.side_ref, s32[16]{0:T(128)S(1)} %get-tuple-element.43.own_at_ref, s32[16]{0:T(128)S(1)} %get-tuple-element.44.other_at_ref, ...), custom_call_target="tpu_custom_call" | custom-call | flops 671088640 | bytes 4194304 | tf_op jit(solution)/shard_map/second_level/pallas_call | solution.py:234
  32.8 2.1 %collective-permute-done.6.refs_0_ = bf16[6,2,64,128]{3,2,1,0:T(8,128)(2,1)S(1)} collective-permute-done((bf16[6,2,64,128]{3,2,1,0:T(8,128)(2,1)S(1)}, bf16[6,2,64,128]{3,2,1,0:T(8,128)(2,1)S(1)}, u32[]{:S(2)}, u32[]{:S(2)}) %collective-permute-start.6) | collective-permute-done | bytes 196640 | tf_op jit(solution)/shard_map/ppermute | solution.py:50
  34.8 2.4 %collective-permute-start.7 = (bf16[10,2,64,128]{3,2,1,0:T(8,128)(2,1)S(1)}, bf16[10,2,64,128]{3,2,1,0:T(8,128)(2,1)S(1)}, u32[]{:S(2)}, u32[]{:S(2)}) collective-permute-start(bf16[10,2,64,128]{3,2,1,0:T(8,128)(2,1)S(1)} %get-tuple-element.46), channel_id=1, source_target_pairs={{0,8},{8,0},{4,12},{12,4},{16,24},{24,16},{20,28},{28,20},{1,9},{9... | collective-permute-start | bytes 983048 | tf_op jit(solution)/shard_map/ppermute | solution.py:50
  37.2 0.6 early_wires.1
  37.8 6.4 %collective-permute-start.8 = (bf16[3,2,64,128]{3,2,1,0:T(8,128)(2,1)S(1)}, bf16[3,2,64,128]{3,2,1,0:T(8,128)(2,1)S(1)}, u32[]{:S(2)}, u32[]{:S(2)}) collective-permute-start(bf16[3,2,64,128]{3,2,1,0:T(8,128)(2,1)S(1)} %get-tuple-element.51), channel_id=1, source_target_pairs={{0,3},{1,2},{2,1},{3,0},{4,7},{5,6},{6,5},{7,4},{8,11},{9,10},{10,... | collective-permute-start | bytes 294920 | tf_op jit(solution)/shard_map/ppermute | solution.py:395
  44.3 0.0 collective-permute-start.9
  44.3 3.1 %collective-permute-done.8.refs_0_ = bf16[3,2,64,128]{3,2,1,0:T(8,128)(2,1)S(1)} collective-permute-done((bf16[3,2,64,128]{3,2,1,0:T(8,128)(2,1)S(1)}, bf16[3,2,64,128]{3,2,1,0:T(8,128)(2,1)S(1)}, u32[]{:S(2)}, u32[]{:S(2)}) %collective-permute-start.8) | collective-permute-done | bytes 98336 | tf_op jit(solution)/shard_map/ppermute | solution.py:395
  47.4 4.1 %collective-permute-done.9.refs_1_ = bf16[3,2,64,128]{3,2,1,0:T(8,128)(2,1)S(1)} collective-permute-done((bf16[3,2,64,128]{3,2,1,0:T(8,128)(2,1)S(1)}, bf16[3,2,64,128]{3,2,1,0:T(8,128)(2,1)S(1)}, u32[]{:S(2)}, u32[]{:S(2)}) %collective-permute-start.9) | collective-permute-done | bytes 98336 | tf_op jit(solution)/shard_map/ppermute | solution.py:395
  51.5 0.0 collective-permute-done.7.refs_0_
  51.5 0.8 %late_wires.1 = (bf16[5,2,64,128]{3,2,1,0:T(8,128)(2,1)S(1)}, bf16[5,2,64,128]{3,2,1,0:T(8,128)(2,1)S(1)}, bf16[8,2,64,128]{3,2,1,0:T(8,128)(2,1)S(1)}, bf16[8,2,64,128]{3,2,1,0:T(8,128)(2,1)S(1)}) custom-call(s32[1]{0:T(128)} %bitcast.me_ref, s32[16]{0:T(128)S(1)} %get-tuple-element.47.target_ref, s32[16]{0:T(128)S(1)} %get-tuple-element.48.rank_ref, ...), custom_call_target="tpu_custom_call" | custom-call | bytes 2097152 | tf_op jit(solution)/shard_map/late_wires/pallas_call | solution.py:347
  52.3 0.1 collective-permute-start.12
  52.4 2.8 %collective-permute-start.10 = (bf16[5,2,64,128]{3,2,1,0:T(8,128)(2,1)S(1)}, bf16[5,2,64,128]{3,2,1,0:T(8,128)(2,1)S(1)}, u32[]{:S(2)}, u32[]{:S(2)}) collective-permute-start(bf16[5,2,64,128]{3,2,1,0:T(8,128)(2,1)S(1)} %get-tuple-element.57), channel_id=1, source_target_pairs={{0,3},{1,2},{2,1},{3,0},{4,7},{5,6},{6,5},{7,4},{8,11},{9,10},{10,... | collective-permute-start | bytes 491528 | tf_op jit(solution)/shard_map/ppermute | solution.py:395
  55.2 0.7 collective-permute-start.11
  55.9 8.8 %collective-permute-done.10.refs_2_ = bf16[5,2,64,128]{3,2,1,0:T(8,128)(2,1)S(1)} collective-permute-done((bf16[5,2,64,128]{3,2,1,0:T(8,128)(2,1)S(1)}, bf16[5,2,64,128]{3,2,1,0:T(8,128)(2,1)S(1)}, u32[]{:S(2)}, u32[]{:S(2)}) %collective-permute-start.10) | collective-permute-done | bytes 163872 | tf_op jit(solution)/shard_map/ppermute | solution.py:395
  64.7 4.7 %collective-permute-done.11.refs_3_ = bf16[5,2,64,128]{3,2,1,0:T(8,128)(2,1)S(1)} collective-permute-done((bf16[5,2,64,128]{3,2,1,0:T(8,128)(2,1)S(1)}, bf16[5,2,64,128]{3,2,1,0:T(8,128)(2,1)S(1)}, u32[]{:S(2)}, u32[]{:S(2)}) %collective-permute-start.11) | collective-permute-done | bytes 163872 | tf_op jit(solution)/shard_map/ppermute | solution.py:395
  69.3 0.0 collective-permute-done.12.refs_4_
  69.3 1.0 %collect.1 = bf16[32,2,64,128]{3,2,1,0:T(8,128)(2,1)} custom-call(s32[1]{0:T(128)} %bitcast.me_ref, bf16[3,2,64,128]{3,2,1,0:T(8,128)(2,1)S(1)} %collective-permute-done.8.refs_0_, bf16[3,2,64,128]{3,2,1,0:T(8,128)(2,1)S(1)} %collective-permute-done.9.refs_1_, bf16[5,2,64,128]{3,2,1,0:T(8,128)(2,1)S(1)} %collective-permute-done.10.refs_2_, ...), custom_call_target="tpu_custom_call" | custom-call | bytes 2097152 | tf_op jit(solution)/shard_map/collect/pallas_call | solution.py:378
  (1 shorter events, 0.0 us)
Async XLA Ops:
  0.0 8.0 %copy-start = (s32[1,16,1]{1,2,0:T(1,128)S(1)}, s32[1,16,1]{1,2,0:T(1,128)}, u32[]{:S(2)}) copy-start(s32[1,16,1]{1,2,0:T(1,128)} %param.13) | copy-start | bytes 196
  0.0 9.5 %copy-start.2 = (s32[8,4]{0,1:T(4,128)S(1)}, s32[8,4]{0,1:T(4,128)}, u32[]{:S(2)}) copy-start(s32[8,4]{0,1:T(4,128)} %param.10) | copy-start | bytes 388
  0.0 9.7 %copy-start.1 = (bf16[1,4,2,128,320]{3,4,2,1,0:T(8,128)(2,1)S(1)}, bf16[1,4,2,128,320]{3,4,2,1,0:T(8,128)(2,1)}, u32[]{:S(2)}) copy-start(bf16[1,4,2,128,320]{3,4,2,1,0:T(8,128)(2,1)} %param.9) | copy-start | bytes 1966084
  2.3 12.5 %collective-permute-start = (bf16[2,192,512]{2,1,0:T(8,128)(2,1)S(1)}, bf16[2,192,512]{2,1,0:T(8,128)(2,1)S(1)}, u32[]{:S(2)}, u32[]{:S(2)}) collective-permute-start(bf16[2,192,512]{2,1,0:T(8,128)(2,1)S(1)} %get-tuple-element.33.sent_first_ref), channel_id=1, source_target_pairs={{0,1},{1,0},{2,3},{3,2},{5,6},{6,5},{8,9},{9,8},{10,11},{11,10},{1... | collective-permute-start | bytes 1179656 | tf_op jit(solution)/shard_map/ppermute | solution.py:39
  7.3 7.5 %collective-permute-start.1 = (bf16[2,192,512]{2,1,0:T(8,128)(2,1)S(1)}, bf16[2,192,512]{2,1,0:T(8,128)(2,1)S(1)}, u32[]{:S(2)}, u32[]{:S(2)}) collective-permute-start(bf16[2,192,512]{2,1,0:T(8,128)(2,1)S(1)} %get-tuple-element.34.sent_second_ref), channel_id=1, source_target_pairs={{1,2},{2,1},{4,5},{5,4},{6,7},{7,6},{9,10},{10,9},{12,13},{13,12},... | collective-permute-start | bytes 1179656 | tf_op jit(solution)/shard_map/ppermute | solution.py:39
  8.0 3.6 %collective-permute-start.2 = (s32[1,16,1]{1,2,0:T(1,128)S(1)}, s32[1,16,1]{1,2,0:T(1,128)S(1)}, u32[]{:S(2)}, u32[]{:S(2)}) collective-permute-start(s32[1,16,1]{1,2,0:T(1,128)S(1)} %copy-done), channel_id=1, source_target_pairs={{0,8},{8,0},{4,12},{12,4},{16,24},{24,16},{20,28},{28,20},{1,9},{9... | collective-permute-start | bytes 200 | tf_op jit(solution)/shard_map/ppermute | solution.py:50
  16.1 3.8 %collective-permute-start.3 = (bf16[2,512,256]{2,1,0:T(8,128)(2,1)S(1)}, bf16[2,512,256]{2,1,0:T(8,128)(2,1)S(1)}, u32[]{:S(2)}, u32[]{:S(2)}) collective-permute-start(bf16[2,512,256]{2,1,0:T(8,128)(2,1)S(1)} %first_level.3), channel_id=1, source_target_pairs={{0,4},{4,0},{8,12},{12,8},{16,20},{20,16},{24,28},{28,24},{1,5},{5... | collective-permute-start | bytes 1572872 | tf_op jit(solution)/shard_map/ppermute | solution.py:50
  20.1 7.6 %collective-permute-start.4 = (bf16[2,192,256]{2,1,0:T(8,128)(2,1)S(1)}, bf16[2,192,256]{2,1,0:T(8,128)(2,1)S(1)}, u32[]{:S(2)}, u32[]{:S(2)}) collective-permute-start(bf16[2,192,256]{2,1,0:T(8,128)(2,1)S(1)} %get-tuple-element.62), channel_id=1, source_target_pairs={{0,1},{1,0},{2,3},{3,2},{5,6},{6,5},{8,9},{9,8},{10,11},{11,10},{1... | collective-permute-start | bytes 589832 | tf_op jit(solution)/shard_map/ppermute | solution.py:39
  24.0 3.6 %collective-permute-start.5 = (bf16[2,192,256]{2,1,0:T(8,128)(2,1)S(1)}, bf16[2,192,256]{2,1,0:T(8,128)(2,1)S(1)}, u32[]{:S(2)}, u32[]{:S(2)}) collective-permute-start(bf16[2,192,256]{2,1,0:T(8,128)(2,1)S(1)} %get-tuple-element.61), channel_id=1, source_target_pairs={{1,2},{2,1},{4,5},{5,4},{6,7},{7,6},{9,10},{10,9},{12,13},{13,12},... | collective-permute-start | bytes 589832 | tf_op jit(solution)/shard_map/ppermute | solution.py:39
  28.8 6.0 %collective-permute-start.6 = (bf16[6,2,64,128]{3,2,1,0:T(8,128)(2,1)S(1)}, bf16[6,2,64,128]{3,2,1,0:T(8,128)(2,1)S(1)}, u32[]{:S(2)}, u32[]{:S(2)}) collective-permute-start(bf16[6,2,64,128]{3,2,1,0:T(8,128)(2,1)S(1)} %second_level_early.1), channel_id=1, source_target_pairs={{0,8},{8,0},{4,12},{12,4},{16,24},{24,16},{20,28},{28,20},{1,9},{9... | collective-permute-start | bytes 589832 | tf_op jit(solution)/shard_map/ppermute | solution.py:50
  34.8 16.7 %collective-permute-start.7 = (bf16[10,2,64,128]{3,2,1,0:T(8,128)(2,1)S(1)}, bf16[10,2,64,128]{3,2,1,0:T(8,128)(2,1)S(1)}, u32[]{:S(2)}, u32[]{:S(2)}) collective-permute-start(bf16[10,2,64,128]{3,2,1,0:T(8,128)(2,1)S(1)} %get-tuple-element.46), channel_id=1, source_target_pairs={{0,8},{8,0},{4,12},{12,4},{16,24},{24,16},{20,28},{28,20},{1,9},{9... | collective-permute-start | bytes 983048 | tf_op jit(solution)/shard_map/ppermute | solution.py:50
  37.8 9.5 %collective-permute-start.8 = (bf16[3,2,64,128]{3,2,1,0:T(8,128)(2,1)S(1)}, bf16[3,2,64,128]{3,2,1,0:T(8,128)(2,1)S(1)}, u32[]{:S(2)}, u32[]{:S(2)}) collective-permute-start(bf16[3,2,64,128]{3,2,1,0:T(8,128)(2,1)S(1)} %get-tuple-element.51), channel_id=1, source_target_pairs={{0,3},{1,2},{2,1},{3,0},{4,7},{5,6},{6,5},{7,4},{8,11},{9,10},{10,... | collective-permute-start | bytes 294920 | tf_op jit(solution)/shard_map/ppermute | solution.py:395
  44.3 7.2 %collective-permute-start.9 = (bf16[3,2,64,128]{3,2,1,0:T(8,128)(2,1)S(1)}, bf16[3,2,64,128]{3,2,1,0:T(8,128)(2,1)S(1)}, u32[]{:S(2)}, u32[]{:S(2)}) collective-permute-start(bf16[3,2,64,128]{3,2,1,0:T(8,128)(2,1)S(1)} %get-tuple-element.52), channel_id=1, source_target_pairs={{0,2},{1,3},{2,0},{3,1},{4,6},{5,7},{6,4},{7,5},{8,10},{9,11},{10,... | collective-permute-start | bytes 294920 | tf_op jit(solution)/shard_map/ppermute | solution.py:395
  52.3 17.0 %collective-permute-start.12 = (bf16[8,2,64,128]{3,2,1,0:T(8,128)(2,1)S(1)}, bf16[8,2,64,128]{3,2,1,0:T(8,128)(2,1)S(1)}, u32[]{:S(2)}, u32[]{:S(2)}) collective-permute-start(bf16[8,2,64,128]{3,2,1,0:T(8,128)(2,1)S(1)} %get-tuple-element.59), channel_id=1, source_target_pairs={{0,1},{1,0},{2,3},{3,2},{4,5},{5,4},{6,7},{7,6},{8,9},{9,8},{10,11... | collective-permute-start | bytes 786440 | tf_op jit(solution)/shard_map/ppermute | solution.py:395
  52.4 12.3 %collective-permute-start.10 = (bf16[5,2,64,128]{3,2,1,0:T(8,128)(2,1)S(1)}, bf16[5,2,64,128]{3,2,1,0:T(8,128)(2,1)S(1)}, u32[]{:S(2)}, u32[]{:S(2)}) collective-permute-start(bf16[5,2,64,128]{3,2,1,0:T(8,128)(2,1)S(1)} %get-tuple-element.57), channel_id=1, source_target_pairs={{0,3},{1,2},{2,1},{3,0},{4,7},{5,6},{6,5},{7,4},{8,11},{9,10},{10,... | collective-permute-start | bytes 491528 | tf_op jit(solution)/shard_map/ppermute | solution.py:395
  55.2 14.2 %collective-permute-start.11 = (bf16[5,2,64,128]{3,2,1,0:T(8,128)(2,1)S(1)}, bf16[5,2,64,128]{3,2,1,0:T(8,128)(2,1)S(1)}, u32[]{:S(2)}, u32[]{:S(2)}) collective-permute-start(bf16[5,2,64,128]{3,2,1,0:T(8,128)(2,1)S(1)} %get-tuple-element.58), channel_id=1, source_target_pairs={{0,2},{1,3},{2,0},{3,1},{4,6},{5,7},{6,4},{7,5},{8,10},{9,11},{10,... | collective-permute-start | bytes 491528 | tf_op jit(solution)/shard_map/ppermute | solution.py:395

commit v5 on v4

--- a/solution.py
+++ b/solution.py
@@ -31,12 +31,10 @@
     count = lax.axis_size("beam")
     received = []
     for order, block in enumerate((first, second)):
-        route = []
-        for aper in range(lax.axis_size("aperture")):
-            for low in range((aper + order) % 2, count - 1, 2):
-                place = aper * count + low
-                route += [(place, place + 1), (place + 1, place)]
-        received.append(lax.ppermute(block, ("aperture", "beam"), route))
+        route = [(place, place) for place in range(count)]
+        for low in range(order, count - 1, 2):
+            route[low], route[low + 1] = (low, low + 1), (low + 1, low)
+        received.append(lax.ppermute(block, "beam", route))
     return received
 
 
@@ -57,7 +55,7 @@
 def resample_kernel(child_hbm, kernel_hbm, first_ref, second_ref, child, kernel, own, sems):
     aper, beam = lax.axis_index("aperture"), lax.axis_index("beam")
     half, quarter = aper & 1, (aper >> 1) & 1
-    even = 1 - ((aper + beam) & 1)
+    even = 1 - (beam & 1)
     rows, rng = child.shape[1:]
     piece = rng // 4
     child_copy = pltpu.make_async_copy(child_hbm, child, sems.at[4])
@@ -121,11 +119,21 @@
     )
 
 
-def place_halos(padded, even, rows, first, second):
+def place_halos(padded, side_ref, rows, first, second):
+    even, lowest, highest = side_ref[0], side_ref[1], side_ref[2]
     margin = first.shape[1]
     far = margin + rows
     padded[:, pl.ds(pl.multiple_of(even * far, BLK), margin), :] = first
     padded[:, pl.ds(pl.multiple_of((1 - even) * far, BLK), margin), :] = second
+    zeros = jnp.zeros_like(first)
+
+    @pl.when(lowest == 1)
+    def _():
+        padded[:, :margin, :] = zeros
+
+    @pl.when(highest == 1)
+    def _():
+        padded[:, far:, :] = zeros
 
 
 def first_level_kernel(
@@ -141,7 +149,7 @@
     head = pl.multiple_of(margin + (1 - even) * (rows - margin), BLK)
     padded[:, pl.ds(tail, margin), :] = sent_first_ref[:, :, columns]
     padded[:, pl.ds(head, margin), :] = sent_second_ref[:, :, columns]
-    place_halos(padded, even, rows, first_ref[:, :, columns], second_ref[:, :, columns])
+    place_halos(padded, side_ref, rows, first_ref[:, :, columns], second_ref[:, :, columns])
     for sector in range(sectors):
         place = pl.ds(pl.multiple_of(starts_ref[sector] * BLK, BLK), window)
         parts = complex_window(weights_ref[sector], padded[0, place, :], padded[1, place, :])
@@ -174,7 +182,7 @@
     margin, rows = first_ref.shape[1], own_ref.shape[1]
     columns = slice(send_ref.shape[3], 2 * send_ref.shape[3])
     padded[:, margin : margin + rows, :] = own_ref[:, :, columns]
-    place_halos(padded, side_ref[0], rows, first_ref[:, :, columns], second_ref[:, :, columns])
+    place_halos(padded, side_ref, rows, first_ref[:, :, columns], second_ref[:, :, columns])
     for place in range(send_ref.shape[0]):
         sector = sector_ref[place] // per
         piece = pl.multiple_of(sector_ref[place] % per * OS, OS)
@@ -199,7 +207,7 @@
     width = keep_ref.shape[3]
     margin, rows = first_ref.shape[1], own_ref.shape[1]
     padded[:, margin : margin + rows, :] = own_ref[...]
-    place_halos(padded, side_ref[0], rows, first_ref[...], second_ref[...])
+    place_halos(padded, side_ref, rows, first_ref[...], second_ref[...])
     per = beams // OS
     for sector in range(sectors):
         place = pl.ds(pl.multiple_of(starts_ref[sector] * BLK, BLK), window)
@@ -248,11 +256,16 @@
 
 
 def plan_kernel(
-    me_ref, own_ref, other_ref, own_at_ref, other_at_ref, other_sector_ref, target_ref, rank_ref,
+    shift, me_ref, own_ref, other_ref, own_at_ref, other_at_ref, other_sector_ref, target_ref, rank_ref,
     taken, filled,
 ):
     count = own_ref.shape[0]
     far_bit = taken.shape[0] // 2
+
+    def delay(target):
+        distance = target ^ me_ref[0]
+        return jnp.where((distance & far_bit) == 0, 2 * count, (distance & 1) * shift)
+
     for owners_ref, at_ref in ((other_ref, other_at_ref), (own_ref, own_at_ref)):
         for target in range(taken.shape[0]):
             taken[target] = 0
@@ -262,9 +275,9 @@
             target = owners_ref[sector]
             rank = taken[target]
             taken[target] = rank + 1
-            near = jnp.where(((target ^ me_ref[0]) & far_bit) == 0, count, 0)
-            at_ref[sector] = rank + near
-            filled[rank + near + 1] = filled[rank + near + 1] + 1
+            bucket = rank + delay(target)
+            at_ref[sector] = bucket
+            filled[bucket + 1] = filled[bucket + 1] + 1
         for bucket in range(1, filled.shape[0]):
             filled[bucket] = filled[bucket] + filled[bucket - 1]
         for sector in range(count):
@@ -274,36 +287,35 @@
             at_ref[sector] = place
             if at_ref is own_at_ref:
                 target_ref[place] = owners_ref[sector]
-                rank_ref[place] = jnp.where(bucket >= count, bucket - count, bucket)
+                rank_ref[place] = bucket - delay(owners_ref[sector])
             else:
                 other_sector_ref[place] = sector
 
 
-def plan(me, own, other, beam_count):
+def plan(shift, me, own, other, beam_count):
     count = own.shape[0]
     shape = jax.ShapeDtypeStruct((count,), jnp.int32)
     return pl.pallas_call(
-        plan_kernel,
+        functools.partial(plan_kernel, shift),
         out_shape=[shape] * 5,
         in_specs=[SMEM] * 3,
         out_specs=[SMEM] * 5,
         scratch_shapes=[
             pltpu.SMEM((beam_count,), jnp.int32),
-            pltpu.SMEM((2 * count + 1,), jnp.int32),
+            pltpu.SMEM((3 * count + 1,), jnp.int32),
         ],
         compiler_params=params(),
         name="plan",
     )(me, own, other)
 
 
-def wires_kernel(spans, me_ref, target_ref, rank_ref, keep_ref, *refs):
+def wires_kernel(spans, early, me_ref, target_ref, rank_ref, keep_ref, *refs):
     wires = refs[-1]
     spare = wires.shape[0] - 1
     out_refs = refs[-1 - len(spans) : -1]
     other_ref, *summed_refs = refs[: -1 - len(spans)]
     wires[...] = jnp.zeros_like(wires)
     me = me_ref[0]
-    early = all(low == 0 for _, low, _ in spans)
 
     def lay(place, total):
         rank = rank_ref[place]
@@ -345,7 +357,7 @@
     shapes = [jax.ShapeDtypeStruct((size,) + block, jnp.bfloat16) for size in sizes]
     total = sum(high - low for _, low, high in spans)
     return pl.pallas_call(
-        functools.partial(wires_kernel, spans),
+        functools.partial(wires_kernel, spans, summed is None),
         out_shape=shapes,
         in_specs=[SMEM] * 3 + [VMEM] * (len(inputs) - 3),
         out_specs=[VMEM] * len(shapes),
@@ -411,25 +423,31 @@
     margin = MARGIN_BLOCKS * BLK
     rows = subimages.shape[2]
     local_blocks = rows // BLK
-    even = ((beam_index + aper_index) % 2 == 0).astype(jnp.int32)
-    side = even.reshape(1)
+    even = (beam_index + 1) % 2
+    ends = (beam_index == 0, beam_index == beam_count - 1)
+    side = jnp.stack([even] + [end.astype(jnp.int32) for end in ends])
     me = beam_index.reshape(1)
 
     sector_count = owners.shape[1]
     capacity = max(2, 2 * sector_count // beam_count)
-    early = max(1, 3 * capacity // 8)
-    far = beam_count // 2
-    distances = list(reversed(range(beam_count)))
-    early_spans = tuple((distance, 0, early) for distance in distances if distance >= far)
-    late_spans = tuple(
-        (distance, early if distance >= far else 0, capacity) for distance in distances
-    )
+    shorter, longer = max(1, capacity // 4), max(1, capacity // 2)
+    far = range(beam_count // 2, beam_count)
+    odd = [distance for distance in far if distance % 2]
+    others = [distance for distance in far if distance % 2 == 0]
+    early = len(odd) * shorter + len(others) * longer
+    early_spans = [(distance, 0, shorter) for distance in odd]
+    early_spans += [(distance, 0, longer) for distance in others]
+    late_spans = [(distance, shorter, capacity) for distance in odd]
+    for distance in range(1, beam_count // 2):
+        late_spans += [(distance, 0, capacity // 2), (distance, capacity // 2, capacity)]
+    late_spans.append((0, 0, capacity))
+    last_spans = [(distance, longer, capacity) for distance in others]
 
     sent = resample(subimages[0], range_kernel[0], margin)
     halos = trade_edges(*sent)
     own_owners = owners[0, :, 0]
     other_owners = partner(owners, "aperture", 1)[0, :, 0]
-    planned = plan(me, own_owners, other_owners, beam_count)
+    planned = plan(longer - shorter, me, own_owners, other_owners, beam_count)
     begin0 = table_row(starts0, aper_index) - (beam_index * local_blocks - MARGIN_BLOCKS)
     halos, planned = lax.optimization_barrier((halos, planned))
     *planned, target, rank = planned
@@ -446,17 +464,22 @@
     halos = trade_edges(first, second)
     begin1 = table_row(starts1, aper_index) - (beam_index * 2 * local_blocks - MARGIN_BLOCKS)
     keep, send, late = second_level(
-        begin1, side, planned, level_one, halos, stacked_weights(weights1), early * far
+        begin1, side, planned, level_one, halos, stacked_weights(weights1), early
     )
     other = partner(send, "aperture", 1)
     other, late = lax.optimization_barrier((other, late))
     late = partner(late, "aperture", 1)
     summed, *group = wires(early_spans, me, target, rank, keep, other)
     received = spread(early_spans, group)
-    late, *received = lax.optimization_barrier((late, *received))
-    group = wires(late_spans, me, target, rank, keep, late, summed)
-    received += spread(late_spans, group)
-    return collect(early_spans + late_spans, capacity, beam_count, me, received)[None]
+    from_odd, from_others = received[: len(odd)], received[len(odd) :]
+    ready, from_odd = lax.optimization_barrier((late, from_odd))
+    group = wires(late_spans, me, target, rank, keep, ready, summed)
+    received = from_odd + spread(late_spans, group)
+    ready, from_others = lax.optimization_barrier((late, from_others))
+    group = wires(last_spans, me, target, rank, keep, ready, summed)
+    received += from_others + spread(last_spans, group)
+    spans = early_spans[: len(odd)] + late_spans + early_spans[len(odd) :] + last_spans
+    return collect(spans, capacity, beam_count, me, received)[None]
 
 
 def solution(mesh):

time: 70.6 us -> 66 us (0.935)
  starting transfers between devices: 28.5 us -> 25.1 us
  waiting for transfers between devices: 26.5 us -> 24.5 us
    ppermute x5 -> x6, waiting for transfers between devices: 20.7 us -> 14.4 us  [spread(): received.append(lax.ppermute(wire, 'beam', route) if distance else wire)]
    ppermute x4, starting transfers between devices: 8.27 us -> 4.66 us  [partner(): return lax.ppermute(block, axis, route)]
    ppermute x4, waiting for transfers between devices: 2.09 us -> 5.21 us  [trade_edges(): received.append(lax.ppermute(block, 'beam', route))]
    ppermute x4, waiting for transfers between devices: 3.78 us -> 4.96 us  [partner(): return lax.ppermute(block, axis, route)]
    ppermute x5 -> x6, starting transfers between devices: 9.98 us -> 11.2 us  [spread(): received.append(lax.ppermute(wire, 'beam', route) if distance else wire)]
    ppermute x4, starting transfers between devices: 10.2 us -> 9.24 us  [trade_edges(): received.append(lax.ppermute(block, 'beam', route))]
    pallas_call x3 -> x4, Pallas kernels: 2.97 us -> 3.64 us  [the longest x3 2.04 us: wires(): pl.pallas_call(functools.partial(wires_kernel, spans, summed is None), ou...]
  transfers between devices with their start and end apart: 13 -> 14, of which waited for: 9 -> 7; matrix products, arithmetic and copies ran while one was open for 4% -> 5% of each run, Pallas kernels for 8% -> 10%
where the time goes in v5:
time: 66 us; the launch traced here: 65.8 us
  starting transfers between devices  25.1 us (38%)
  waiting for transfers between devices  24.5 us (37%)
  Pallas kernels  12.7 us (19%)
  local copies, waits for them, and re-layouts  2.25 us (3%)
  other arithmetic  1.1 us (2%)
    ppermute x6, waiting for transfers between devices, spread(): received.append(lax.ppermute(wire, 'beam', route) if distance else wire)  14.4 us
    ppermute x6, starting transfers between devices, spread(): received.append(lax.ppermute(wire, 'beam', route) if distance else wire)  11.2 us
    ppermute x4, starting transfers between devices, trade_edges(): received.append(lax.ppermute(block, 'beam', route))  9.24 us
    ppermute x4, waiting for transfers between devices, trade_edges(): received.append(lax.ppermute(block, 'beam', route))  5.21 us
    ppermute x4, waiting for transfers between devices, partner(): return lax.ppermute(block, axis, route)  4.96 us
    ppermute x4, starting transfers between devices, partner(): return lax.ppermute(block, axis, route)  4.66 us
    pallas_call x2, Pallas kernels, first_level(): pl.pallas_call(functools.partial(first_level_kernel, column, rows), out_s...  2.67 us
    pallas_call x1, Pallas kernels, resample(): pl.pallas_call(resample_kernel, out_shape=(shape, shape), in_specs=[ANY,...  2.31 us
  transfers between devices with their start and end apart: 14, of which 7 were waited for; matrix products, arithmetic and copies ran while one was open for 5% of the time, Pallas kernels for 10%

profile of v5, /device:TPU:0, one launch (start us, length us, event | category | flops | bytes accessed | tf_op | source)
XLA Modules:
  0.0 65.8 jit_solution(4458171635776860672)
XLA Ops:
  0.0 0.0 copy-start
  0.0 0.0 copy-start.2
  0.0 0.0 copy-start.1
  0.0 2.3 %resample.1 = (bf16[2,192,512]{2,1,0:T(8,128)(2,1)S(1)}, bf16[2,192,512]{2,1,0:T(8,128)(2,1)S(1)}) custom-call(bf16[2,256,512]{2,1,0:T(8,128)(2,1)} %bitcast.20, bf16[2,512,512]{2,1,0:T(8,128)(2,1)} %bitcast.19), custom_call_target="tpu_custom_call" | custom-call | flops 536870912 | bytes 2097152 | tf_op jit(solution)/shard_map/resample/pallas_call | solution.py:95
  2.3 3.1 %collective-permute-start = (bf16[2,192,512]{2,1,0:T(8,128)(2,1)S(1)}, bf16[2,192,512]{2,1,0:T(8,128)(2,1)S(1)}, u32[]{:S(2)}, u32[]{:S(2)}) collective-permute-start(bf16[2,192,512]{2,1,0:T(8,128)(2,1)S(1)} %get-tuple-element.34.sent_first_ref), channel_id=1, source_target_pairs={{0,1},{1,0},{2,3},{3,2},{4,5},{5,4},{6,7},{7,6},{8,9},{9,8},{10,11... | collective-permute-start | bytes 1179656 | tf_op jit(solution)/shard_map/ppermute | solution.py:37
  5.4 0.7 %collective-permute-start.1 = (bf16[2,192,512]{2,1,0:T(8,128)(2,1)S(1)}, bf16[2,192,512]{2,1,0:T(8,128)(2,1)S(1)}, u32[]{:S(2)}, u32[]{:S(2)}) collective-permute-start(bf16[2,192,512]{2,1,0:T(8,128)(2,1)S(1)} %get-tuple-element.35.sent_second_ref), channel_id=1, source_target_pairs={{0,0},{1,2},{2,1},{3,3},{4,4},{5,6},{6,5},{7,7},{8,8},{9,10},{10,9... | collective-permute-start | bytes 1179656 | tf_op jit(solution)/shard_map/ppermute | solution.py:37
  6.1 0.0 copy-done
  6.1 1.6 %collective-permute-start.2 = (s32[1,16,1]{1,2,0:T(1,128)S(1)}, s32[1,16,1]{1,2,0:T(1,128)S(1)}, u32[]{:S(2)}, u32[]{:S(2)}) collective-permute-start(s32[1,16,1]{1,2,0:T(1,128)S(1)} %copy-done), channel_id=1, source_target_pairs={{0,8},{8,0},{4,12},{12,4},{16,24},{24,16},{20,28},{28,20},{1,9},{9... | collective-permute-start | bytes 200 | tf_op jit(solution)/shard_map/ppermute | solution.py:48
  7.7 0.0 copy-done.2
  7.7 0.2 subtract_reduce_fusion.starts_ref
  7.8 0.1 pad_add_fusion.side_ref
  7.9 0.0 copy-done.1
  7.9 0.4 copy.8
  8.3 1.4 %collective-permute-done.2 = s32[1,16,1]{1,2,0:T(1,128)S(1)} collective-permute-done((s32[1,16,1]{1,2,0:T(1,128)S(1)}, s32[1,16,1]{1,2,0:T(1,128)S(1)}, u32[]{:S(2)}, u32[]{:S(2)}) %collective-permute-start.2) | collective-permute-done | bytes 96 | tf_op jit(solution)/shard_map/ppermute | solution.py:48
  9.7 1.6 %plan.1 = (s32[16]{0:T(128)S(1)}, s32[16]{0:T(128)S(1)}, s32[16]{0:T(128)S(1)}, s32[16]{0:T(128)S(1)}, s32[16]{0:T(128)S(1)}) custom-call(s32[1]{0:T(128)} %bitcast.me_ref, s32[16]{0:T(128)S(1)} %bitcast.17, s32[16]{0:T(128)S(1)} %bitcast.18), custom_call_target="tpu_custom_call" | custom-call | tf_op jit(solution)/shard_map/plan/pallas_call | solution.py:298
  11.3 3.2 %collective-permute-done.first_ref = bf16[2,192,512]{2,1,0:T(8,128)(2,1)S(1)} collective-permute-done((bf16[2,192,512]{2,1,0:T(8,128)(2,1)S(1)}, bf16[2,192,512]{2,1,0:T(8,128)(2,1)S(1)}, u32[]{:S(2)}, u32[]{:S(2)}) %collective-permute-start) | collective-permute-done | bytes 393248 | tf_op jit(solution)/shard_map/ppermute | solution.py:37
  14.5 0.0 collective-permute-done.1.second_ref
  14.5 1.3 %first_level.3 = bf16[2,512,256]{2,1,0:T(8,128)(2,1)S(1)} custom-call(s32[4]{0:T(128)S(1)} %subtract_reduce_fusion.starts_ref, s32[3]{0:T(128)S(1)} %pad_add_fusion.side_ref, bf16[2,192,512]{2,1,0:T(8,128)(2,1)S(1)} %get-tuple-element.34.sent_first_ref, bf16[2,192,512]{2,1,0:T(8,128)(2,1)S(1)} %get-tuple-element.35.sent_second_ref, ...), custom_call_target="tpu_custom_call" | custom-call | flops 335544320 | bytes 2097152 | tf_op jit(solution)/shard_map/first_level/pallas_call | solution.py:165
  15.9 0.1 collective-permute-start.3
  16.0 1.3 %first_level.2 = bf16[2,512,256]{2,1,0:T(8,128)(2,1)S(1)} custom-call(s32[4]{0:T(128)S(1)} %subtract_reduce_fusion.starts_ref, s32[3]{0:T(128)S(1)} %pad_add_fusion.side_ref, bf16[2,192,512]{2,1,0:T(8,128)(2,1)S(1)} %get-tuple-element.34.sent_first_ref, bf16[2,192,512]{2,1,0:T(8,128)(2,1)S(1)} %get-tuple-element.35.sent_second_ref, ...), custom_call_target="tpu_custom_call" | custom-call | flops 335544320 | bytes 2097152 | tf_op jit(solution)/shard_map/first_level/pallas_call | solution.py:165
  17.3 0.5 collective-permute-done.3
  17.8 0.1 add_convert_fusion.own_ref
  18.0 4.8 %collective-permute-start.4 = (bf16[2,192,256]{2,1,0:T(8,128)(2,1)S(1)}, bf16[2,192,256]{2,1,0:T(8,128)(2,1)S(1)}, u32[]{:S(2)}, u32[]{:S(2)}) collective-permute-start(bf16[2,192,256]{2,1,0:T(8,128)(2,1)S(1)} %get-tuple-element.64), channel_id=1, source_target_pairs={{0,1},{1,0},{2,3},{3,2},{4,5},{5,4},{6,7},{7,6},{8,9},{9,8},{10,11... | collective-permute-start | bytes 589832 | tf_op jit(solution)/shard_map/ppermute | solution.py:37
  22.8 0.7 %collective-permute-start.5 = (bf16[2,192,256]{2,1,0:T(8,128)(2,1)S(1)}, bf16[2,192,256]{2,1,0:T(8,128)(2,1)S(1)}, u32[]{:S(2)}, u32[]{:S(2)}) collective-permute-start(bf16[2,192,256]{2,1,0:T(8,128)(2,1)S(1)} %get-tuple-element.63), channel_id=1, source_target_pairs={{0,0},{1,2},{2,1},{3,3},{4,4},{5,6},{6,5},{7,7},{8,8},{9,10},{10,9... | collective-permute-start | bytes 589832 | tf_op jit(solution)/shard_map/ppermute | solution.py:37
  23.5 1.8 %copy.9 = bf16[1,8,2,128,320]{4,3,2,1,0:T(8,128)(2,1)S(1)} copy(bf16[1,8,2,128,320]{3,4,2,1,0:T(8,128)(2,1)} %param.11) | data formatting | bytes 2621440 | tf_op args[4]
  25.4 0.7 %fusion.1.starts_ref = s32[8]{0:T(128)S(1)} fusion(s32[8,8]{1,0:T(8,128)} %param.12, s32[]{:T(128)S(6)} %select_n.19, s32[]{:T(128)S(6)} %sub.25), kind=kLoop, calls=%fused_computation.6 | loop fusion | flops 8 | bytes 72 | tf_op jit(solution)/shard_map/sub | solution.py:465
  26.1 2.0 %collective-permute-done.4.first_ref = bf16[2,192,256]{2,1,0:T(8,128)(2,1)S(1)} collective-permute-done((bf16[2,192,256]{2,1,0:T(8,128)(2,1)S(1)}, bf16[2,192,256]{2,1,0:T(8,128)(2,1)S(1)}, u32[]{:S(2)}, u32[]{:S(2)}) %collective-permute-start.4) | collective-permute-done | bytes 196640 | tf_op jit(solution)/shard_map/ppermute | solution.py:37
  28.0 0.0 collective-permute-done.5.second_ref
  28.1 1.1 %second_level_early.1 = bf16[6,2,64,128]{3,2,1,0:T(8,128)(2,1)S(1)} custom-call(s32[8]{0:T(128)S(1)} %fusion.1.starts_ref, s32[3]{0:T(128)S(1)} %pad_add_fusion.side_ref, s32[16]{0:T(128)S(1)} %get-tuple-element.41.sector_ref, bf16[2,512,256]{2,1,0:T(8,128)(2,1)S(1)} %add_convert_fusion.own_ref, bf16[2,192,256]{2,1,0:T(8,128)(2,1)S(1)} %collective-permute-done.4.first_ref, ...), custom_call_target="tpu_custom_call" | custom-call | flops 125829120 | bytes 1048576 | tf_op jit(solution)/shard_map/second_level_early/pallas_call | solution.py:231
  29.2 1.6 %collective-permute-start.6 = (bf16[6,2,64,128]{3,2,1,0:T(8,128)(2,1)S(1)}, bf16[6,2,64,128]{3,2,1,0:T(8,128)(2,1)S(1)}, u32[]{:S(2)}, u32[]{:S(2)}) collective-permute-start(bf16[6,2,64,128]{3,2,1,0:T(8,128)(2,1)S(1)} %second_level_early.1), channel_id=1, source_target_pairs={{0,8},{8,0},{4,12},{12,4},{16,24},{24,16},{20,28},{28,20},{1,9},{9... | collective-permute-start | bytes 589832 | tf_op jit(solution)/shard_map/ppermute | solution.py:48
  30.7 1.9 %second_level.1 = (bf16[16,2,64,128]{3,2,1,0:T(8,128)(2,1)S(1)}, bf16[10,2,64,128]{3,2,1,0:T(8,128)(2,1)S(1)}) custom-call(s32[8]{0:T(128)S(1)} %fusion.1.starts_ref, s32[3]{0:T(128)S(1)} %pad_add_fusion.side_ref, s32[16]{0:T(128)S(1)} %get-tuple-element.44.own_at_ref, s32[16]{0:T(128)S(1)} %get-tuple-element.45.other_at_ref, ...), custom_call_target="tpu_custom_call" | custom-call | flops 671088640 | bytes 4194304 | tf_op jit(solution)/shard_map/second_level/pallas_call | solution.py:242
  32.7 3.0 %collective-permute-done.6.refs_0_ = bf16[6,2,64,128]{3,2,1,0:T(8,128)(2,1)S(1)} collective-permute-done((bf16[6,2,64,128]{3,2,1,0:T(8,128)(2,1)S(1)}, bf16[6,2,64,128]{3,2,1,0:T(8,128)(2,1)S(1)}, u32[]{:S(2)}, u32[]{:S(2)}) %collective-permute-start.6) | collective-permute-done | bytes 196640 | tf_op jit(solution)/shard_map/ppermute | solution.py:48
  35.7 1.5 %collective-permute-start.7 = (bf16[10,2,64,128]{3,2,1,0:T(8,128)(2,1)S(1)}, bf16[10,2,64,128]{3,2,1,0:T(8,128)(2,1)S(1)}, u32[]{:S(2)}, u32[]{:S(2)}) collective-permute-start(bf16[10,2,64,128]{3,2,1,0:T(8,128)(2,1)S(1)} %get-tuple-element.47), channel_id=1, source_target_pairs={{0,8},{8,0},{4,12},{12,4},{16,24},{24,16},{20,28},{28,20},{1,9},{9... | collective-permute-start | bytes 983048 | tf_op jit(solution)/shard_map/ppermute | solution.py:48
  37.2 0.6 early_wires.1
  37.8 4.6 %collective-permute-start.12 = (bf16[4,2,64,128]{3,2,1,0:T(8,128)(2,1)S(1)}, bf16[4,2,64,128]{3,2,1,0:T(8,128)(2,1)S(1)}, u32[]{:S(2)}, u32[]{:S(2)}) collective-permute-start(bf16[4,2,64,128]{3,2,1,0:T(8,128)(2,1)S(1)} %get-tuple-element.60), channel_id=1, source_target_pairs={{0,2},{1,3},{2,0},{3,1},{4,6},{5,7},{6,4},{7,5},{8,10},{9,11},{10,... | collective-permute-start | bytes 393224 | tf_op jit(solution)/shard_map/ppermute | solution.py:407
  42.3 1.2 %collective-permute-start.8 = (bf16[2,2,64,128]{3,2,1,0:T(8,128)(2,1)S(1)}, bf16[2,2,64,128]{3,2,1,0:T(8,128)(2,1)S(1)}, u32[]{:S(2)}, u32[]{:S(2)}) collective-permute-start(bf16[2,2,64,128]{3,2,1,0:T(8,128)(2,1)S(1)} %get-tuple-element.52), channel_id=1, source_target_pairs={{0,3},{1,2},{2,1},{3,0},{4,7},{5,6},{6,5},{7,4},{8,11},{9,10},{10,... | collective-permute-start | bytes 196616 | tf_op jit(solution)/shard_map/ppermute | solution.py:407
  43.5 5.0 %collective-permute-done.8.refs_0_ = bf16[2,2,64,128]{3,2,1,0:T(8,128)(2,1)S(1)} collective-permute-done((bf16[2,2,64,128]{3,2,1,0:T(8,128)(2,1)S(1)}, bf16[2,2,64,128]{3,2,1,0:T(8,128)(2,1)S(1)}, u32[]{:S(2)}, u32[]{:S(2)}) %collective-permute-start.8) | collective-permute-done | bytes 65568 | tf_op jit(solution)/shard_map/ppermute | solution.py:407
  48.5 0.0 collective-permute-done.7.refs_0_
  48.5 0.8 %late_wires.2 = (bf16[6,2,64,128]{3,2,1,0:T(8,128)(2,1)S(1)}, bf16[4,2,64,128]{3,2,1,0:T(8,128)(2,1)S(1)}, bf16[4,2,64,128]{3,2,1,0:T(8,128)(2,1)S(1)}, bf16[8,2,64,128]{3,2,1,0:T(8,128)(2,1)S(1)}) custom-call(s32[1]{0:T(128)} %bitcast.me_ref, s32[16]{0:T(128)S(1)} %get-tuple-element.48.target_ref, s32[16]{0:T(128)S(1)} %get-tuple-element.49.rank_ref, ...), custom_call_target="tpu_custom_call" | custom-call | bytes 2097152 | tf_op jit(solution)/shard_map/late_wires/pallas_call | solution.py:359
  49.3 1.5 %collective-permute-start.9 = (bf16[6,2,64,128]{3,2,1,0:T(8,128)(2,1)S(1)}, bf16[6,2,64,128]{3,2,1,0:T(8,128)(2,1)S(1)}, u32[]{:S(2)}, u32[]{:S(2)}) collective-permute-start(bf16[6,2,64,128]{3,2,1,0:T(8,128)(2,1)S(1)} %get-tuple-element.56), channel_id=1, source_target_pairs={{0,3},{1,2},{2,1},{3,0},{4,7},{5,6},{6,5},{7,4},{8,11},{9,10},{10,... | collective-permute-start | bytes 589832 | tf_op jit(solution)/shard_map/ppermute | solution.py:407
  50.8 0.0 collective-permute-done.12.refs_5_
  50.8 0.6 late_wires.3
  51.4 1.9 %collective-permute-start.13 = (bf16[4,2,64,128]{3,2,1,0:T(8,128)(2,1)S(1)}, bf16[4,2,64,128]{3,2,1,0:T(8,128)(2,1)S(1)}, u32[]{:S(2)}, u32[]{:S(2)}) collective-permute-start(bf16[4,2,64,128]{3,2,1,0:T(8,128)(2,1)S(1)} %late_wires.3), channel_id=1, source_target_pairs={{0,2},{1,3},{2,0},{3,1},{4,6},{5,7},{6,4},{7,5},{8,10},{9,11},{10,... | collective-permute-start | bytes 393224 | tf_op jit(solution)/shard_map/ppermute | solution.py:407
  53.3 1.1 %collective-permute-start.10 = (bf16[4,2,64,128]{3,2,1,0:T(8,128)(2,1)S(1)}, bf16[4,2,64,128]{3,2,1,0:T(8,128)(2,1)S(1)}, u32[]{:S(2)}, u32[]{:S(2)}) collective-permute-start(bf16[4,2,64,128]{3,2,1,0:T(8,128)(2,1)S(1)} %get-tuple-element.57), channel_id=1, source_target_pairs={{0,1},{1,0},{2,3},{3,2},{4,5},{5,4},{6,7},{7,6},{8,9},{9,8},{10,11... | collective-permute-start | bytes 393224 | tf_op jit(solution)/shard_map/ppermute | solution.py:407
  54.5 0.9 %collective-permute-start.11 = (bf16[4,2,64,128]{3,2,1,0:T(8,128)(2,1)S(1)}, bf16[4,2,64,128]{3,2,1,0:T(8,128)(2,1)S(1)}, u32[]{:S(2)}, u32[]{:S(2)}) collective-permute-start(bf16[4,2,64,128]{3,2,1,0:T(8,128)(2,1)S(1)} %get-tuple-element.58), channel_id=1, source_target_pairs={{0,1},{1,0},{2,3},{3,2},{4,5},{5,4},{6,7},{7,6},{8,9},{9,8},{10,11... | collective-permute-start | bytes 393224 | tf_op jit(solution)/shard_map/ppermute | solution.py:407
  55.4 9.4 %collective-permute-done.13.refs_6_ = bf16[4,2,64,128]{3,2,1,0:T(8,128)(2,1)S(1)} collective-permute-done((bf16[4,2,64,128]{3,2,1,0:T(8,128)(2,1)S(1)}, bf16[4,2,64,128]{3,2,1,0:T(8,128)(2,1)S(1)}, u32[]{:S(2)}, u32[]{:S(2)}) %collective-permute-start.13) | collective-permute-done | bytes 131104 | tf_op jit(solution)/shard_map/ppermute | solution.py:407
  64.7 0.0 collective-permute-done.10.refs_2_
  64.7 0.0 collective-permute-done.11.refs_3_
  64.7 0.0 collective-permute-done.9.refs_1_
  64.8 1.0 %collect.1 = bf16[32,2,64,128]{3,2,1,0:T(8,128)(2,1)} custom-call(s32[1]{0:T(128)} %bitcast.me_ref, bf16[2,2,64,128]{3,2,1,0:T(8,128)(2,1)S(1)} %collective-permute-done.8.refs_0_, bf16[6,2,64,128]{3,2,1,0:T(8,128)(2,1)S(1)} %collective-permute-done.9.refs_1_, bf16[4,2,64,128]{3,2,1,0:T(8,128)(2,1)S(1)} %collective-permute-done.10.refs_2_, ...), custom_call_target="tpu_custom_call" | custom-call | bytes 2097152 | tf_op jit(solution)/shard_map/collect/pallas_call | solution.py:390
  (1 shorter events, 0.0 us)
Async XLA Ops:
  0.0 6.1 %copy-start = (s32[1,16,1]{1,2,0:T(1,128)S(1)}, s32[1,16,1]{1,2,0:T(1,128)}, u32[]{:S(2)}) copy-start(s32[1,16,1]{1,2,0:T(1,128)} %param.13) | copy-start | bytes 196
  0.0 7.7 %copy-start.2 = (s32[8,4]{0,1:T(4,128)S(1)}, s32[8,4]{0,1:T(4,128)}, u32[]{:S(2)}) copy-start(s32[8,4]{0,1:T(4,128)} %param.10) | copy-start | bytes 388
  0.0 7.9 %copy-start.1 = (bf16[1,4,2,128,320]{3,4,2,1,0:T(8,128)(2,1)S(1)}, bf16[1,4,2,128,320]{3,4,2,1,0:T(8,128)(2,1)}, u32[]{:S(2)}) copy-start(bf16[1,4,2,128,320]{3,4,2,1,0:T(8,128)(2,1)} %param.9) | copy-start | bytes 1966084
  2.3 12.2 %collective-permute-start = (bf16[2,192,512]{2,1,0:T(8,128)(2,1)S(1)}, bf16[2,192,512]{2,1,0:T(8,128)(2,1)S(1)}, u32[]{:S(2)}, u32[]{:S(2)}) collective-permute-start(bf16[2,192,512]{2,1,0:T(8,128)(2,1)S(1)} %get-tuple-element.34.sent_first_ref), channel_id=1, source_target_pairs={{0,1},{1,0},{2,3},{3,2},{4,5},{5,4},{6,7},{7,6},{8,9},{9,8},{10,11... | collective-permute-start | bytes 1179656 | tf_op jit(solution)/shard_map/ppermute | solution.py:37
  5.4 9.1 %collective-permute-start.1 = (bf16[2,192,512]{2,1,0:T(8,128)(2,1)S(1)}, bf16[2,192,512]{2,1,0:T(8,128)(2,1)S(1)}, u32[]{:S(2)}, u32[]{:S(2)}) collective-permute-start(bf16[2,192,512]{2,1,0:T(8,128)(2,1)S(1)} %get-tuple-element.35.sent_second_ref), channel_id=1, source_target_pairs={{0,0},{1,2},{2,1},{3,3},{4,4},{5,6},{6,5},{7,7},{8,8},{9,10},{10,9... | collective-permute-start | bytes 1179656 | tf_op jit(solution)/shard_map/ppermute | solution.py:37
  6.1 3.6 %collective-permute-start.2 = (s32[1,16,1]{1,2,0:T(1,128)S(1)}, s32[1,16,1]{1,2,0:T(1,128)S(1)}, u32[]{:S(2)}, u32[]{:S(2)}) collective-permute-start(s32[1,16,1]{1,2,0:T(1,128)S(1)} %copy-done), channel_id=1, source_target_pairs={{0,8},{8,0},{4,12},{12,4},{16,24},{24,16},{20,28},{28,20},{1,9},{9... | collective-permute-start | bytes 200 | tf_op jit(solution)/shard_map/ppermute | solution.py:48
  15.9 2.0 %collective-permute-start.3 = (bf16[2,512,256]{2,1,0:T(8,128)(2,1)S(1)}, bf16[2,512,256]{2,1,0:T(8,128)(2,1)S(1)}, u32[]{:S(2)}, u32[]{:S(2)}) collective-permute-start(bf16[2,512,256]{2,1,0:T(8,128)(2,1)S(1)} %first_level.3), channel_id=1, source_target_pairs={{0,4},{4,0},{8,12},{12,8},{16,20},{20,16},{24,28},{28,24},{1,5},{5... | collective-permute-start | bytes 1572872 | tf_op jit(solution)/shard_map/ppermute | solution.py:48
  18.0 10.0 %collective-permute-start.4 = (bf16[2,192,256]{2,1,0:T(8,128)(2,1)S(1)}, bf16[2,192,256]{2,1,0:T(8,128)(2,1)S(1)}, u32[]{:S(2)}, u32[]{:S(2)}) collective-permute-start(bf16[2,192,256]{2,1,0:T(8,128)(2,1)S(1)} %get-tuple-element.64), channel_id=1, source_target_pairs={{0,1},{1,0},{2,3},{3,2},{4,5},{5,4},{6,7},{7,6},{8,9},{9,8},{10,11... | collective-permute-start | bytes 589832 | tf_op jit(solution)/shard_map/ppermute | solution.py:37
  22.8 5.2 %collective-permute-start.5 = (bf16[2,192,256]{2,1,0:T(8,128)(2,1)S(1)}, bf16[2,192,256]{2,1,0:T(8,128)(2,1)S(1)}, u32[]{:S(2)}, u32[]{:S(2)}) collective-permute-start(bf16[2,192,256]{2,1,0:T(8,128)(2,1)S(1)} %get-tuple-element.63), channel_id=1, source_target_pairs={{0,0},{1,2},{2,1},{3,3},{4,4},{5,6},{6,5},{7,7},{8,8},{9,10},{10,9... | collective-permute-start | bytes 589832 | tf_op jit(solution)/shard_map/ppermute | solution.py:37
  29.2 6.5 %collective-permute-start.6 = (bf16[6,2,64,128]{3,2,1,0:T(8,128)(2,1)S(1)}, bf16[6,2,64,128]{3,2,1,0:T(8,128)(2,1)S(1)}, u32[]{:S(2)}, u32[]{:S(2)}) collective-permute-start(bf16[6,2,64,128]{3,2,1,0:T(8,128)(2,1)S(1)} %second_level_early.1), channel_id=1, source_target_pairs={{0,8},{8,0},{4,12},{12,4},{16,24},{24,16},{20,28},{28,20},{1,9},{9... | collective-permute-start | bytes 589832 | tf_op jit(solution)/shard_map/ppermute | solution.py:48
  35.7 12.8 %collective-permute-start.7 = (bf16[10,2,64,128]{3,2,1,0:T(8,128)(2,1)S(1)}, bf16[10,2,64,128]{3,2,1,0:T(8,128)(2,1)S(1)}, u32[]{:S(2)}, u32[]{:S(2)}) collective-permute-start(bf16[10,2,64,128]{3,2,1,0:T(8,128)(2,1)S(1)} %get-tuple-element.47), channel_id=1, source_target_pairs={{0,8},{8,0},{4,12},{12,4},{16,24},{24,16},{20,28},{28,20},{1,9},{9... | collective-permute-start | bytes 983048 | tf_op jit(solution)/shard_map/ppermute | solution.py:48
  37.8 13.0 %collective-permute-start.12 = (bf16[4,2,64,128]{3,2,1,0:T(8,128)(2,1)S(1)}, bf16[4,2,64,128]{3,2,1,0:T(8,128)(2,1)S(1)}, u32[]{:S(2)}, u32[]{:S(2)}) collective-permute-start(bf16[4,2,64,128]{3,2,1,0:T(8,128)(2,1)S(1)} %get-tuple-element.60), channel_id=1, source_target_pairs={{0,2},{1,3},{2,0},{3,1},{4,6},{5,7},{6,4},{7,5},{8,10},{9,11},{10,... | collective-permute-start | bytes 393224 | tf_op jit(solution)/shard_map/ppermute | solution.py:407
  42.3 6.2 %collective-permute-start.8 = (bf16[2,2,64,128]{3,2,1,0:T(8,128)(2,1)S(1)}, bf16[2,2,64,128]{3,2,1,0:T(8,128)(2,1)S(1)}, u32[]{:S(2)}, u32[]{:S(2)}) collective-permute-start(bf16[2,2,64,128]{3,2,1,0:T(8,128)(2,1)S(1)} %get-tuple-element.52), channel_id=1, source_target_pairs={{0,3},{1,2},{2,1},{3,0},{4,7},{5,6},{6,5},{7,4},{8,11},{9,10},{10,... | collective-permute-start | bytes 196616 | tf_op jit(solution)/shard_map/ppermute | solution.py:407
  49.3 15.5 %collective-permute-start.9 = (bf16[6,2,64,128]{3,2,1,0:T(8,128)(2,1)S(1)}, bf16[6,2,64,128]{3,2,1,0:T(8,128)(2,1)S(1)}, u32[]{:S(2)}, u32[]{:S(2)}) collective-permute-start(bf16[6,2,64,128]{3,2,1,0:T(8,128)(2,1)S(1)} %get-tuple-element.56), channel_id=1, source_target_pairs={{0,3},{1,2},{2,1},{3,0},{4,7},{5,6},{6,5},{7,4},{8,11},{9,10},{10,... | collective-permute-start | bytes 589832 | tf_op jit(solution)/shard_map/ppermute | solution.py:407
  51.4 13.3 %collective-permute-start.13 = (bf16[4,2,64,128]{3,2,1,0:T(8,128)(2,1)S(1)}, bf16[4,2,64,128]{3,2,1,0:T(8,128)(2,1)S(1)}, u32[]{:S(2)}, u32[]{:S(2)}) collective-permute-start(bf16[4,2,64,128]{3,2,1,0:T(8,128)(2,1)S(1)} %late_wires.3), channel_id=1, source_target_pairs={{0,2},{1,3},{2,0},{3,1},{4,6},{5,7},{6,4},{7,5},{8,10},{9,11},{10,... | collective-permute-start | bytes 393224 | tf_op jit(solution)/shard_map/ppermute | solution.py:407
  53.3 11.4 %collective-permute-start.10 = (bf16[4,2,64,128]{3,2,1,0:T(8,128)(2,1)S(1)}, bf16[4,2,64,128]{3,2,1,0:T(8,128)(2,1)S(1)}, u32[]{:S(2)}, u32[]{:S(2)}) collective-permute-start(bf16[4,2,64,128]{3,2,1,0:T(8,128)(2,1)S(1)} %get-tuple-element.57), channel_id=1, source_target_pairs={{0,1},{1,0},{2,3},{3,2},{4,5},{5,4},{6,7},{7,6},{8,9},{9,8},{10,11... | collective-permute-start | bytes 393224 | tf_op jit(solution)/shard_map/ppermute | solution.py:407
  54.5 10.3 %collective-permute-start.11 = (bf16[4,2,64,128]{3,2,1,0:T(8,128)(2,1)S(1)}, bf16[4,2,64,128]{3,2,1,0:T(8,128)(2,1)S(1)}, u32[]{:S(2)}, u32[]{:S(2)}) collective-permute-start(bf16[4,2,64,128]{3,2,1,0:T(8,128)(2,1)S(1)} %get-tuple-element.58), channel_id=1, source_target_pairs={{0,1},{1,0},{2,3},{3,2},{4,5},{5,4},{6,7},{7,6},{8,9},{9,8},{10,11... | collective-permute-start | bytes 393224 | tf_op jit(solution)/shard_map/ppermute | solution.py:407

commit v6 on v5

--- a/solution.py
+++ b/solution.py
@@ -28,13 +28,19 @@
 
 
 def trade_edges(first, second):
-    count = lax.axis_size("beam")
+    count, apertures = lax.axis_size("beam"), lax.axis_size("aperture")
     received = []
     for order, block in enumerate((first, second)):
-        route = [(place, place) for place in range(count)]
-        for low in range(order, count - 1, 2):
-            route[low], route[low + 1] = (low, low + 1), (low + 1, low)
-        received.append(lax.ppermute(block, "beam", route))
+        route = []
+        for aper in range(apertures):
+            for place in range(count):
+                other = place + 1 if (place - order) % 2 == 0 else place - 1
+                if 0 <= other < count:
+                    to = aper * count + other
+                else:
+                    to = min(aper ^ 1, apertures - 1) * count + place
+                route.append((aper * count + place, to))
+        received.append(lax.ppermute(block, ("aperture", "beam"), route))
     return received
 
 

time: 66 us -> 62.3 us (0.944)
  starting transfers between devices: 25.1 us -> 20.3 us
  waiting for transfers between devices: 24.5 us -> 25.7 us
    ppermute x4, starting transfers between devices: 9.24 us -> 6.01 us  [trade_edges(): received.append(lax.ppermute(block, ('aperture', 'beam'), route))]
    ppermute x6, starting transfers between devices: 11.2 us -> 9.7 us  [spread(): received.append(lax.ppermute(wire, 'beam', route) if distance else wire)]
    ppermute x4, waiting for transfers between devices: 5.21 us -> 6.63 us  [trade_edges(): received.append(lax.ppermute(block, ('aperture', 'beam'), route))]
  transfers between devices with their start and end apart: 14 -> 14, of which waited for: 7 -> 8; matrix products, arithmetic and copies ran while one was open for 5% -> 5% of each run, Pallas kernels for 10% -> 11%
where the time goes in v6:
time: 62.3 us; the launch traced here: 62.2 us
  waiting for transfers between devices  25.7 us (41%)
  starting transfers between devices  20.3 us (33%)
  Pallas kernels  12.7 us (20%)
  local copies, waits for them, and re-layouts  2.24 us (4%)
  other arithmetic  1.1 us (2%)
    ppermute x6, waiting for transfers between devices, spread(): received.append(lax.ppermute(wire, 'beam', route) if distance else wire)  14.1 us
    ppermute x6, starting transfers between devices, spread(): received.append(lax.ppermute(wire, 'beam', route) if distance else wire)  9.7 us
    ppermute x4, waiting for transfers between devices, trade_edges(): received.append(lax.ppermute(block, ('aperture', 'beam'), route))  6.63 us
    ppermute x4, starting transfers between devices, trade_edges(): received.append(lax.ppermute(block, ('aperture', 'beam'), route))  6.01 us
    ppermute x4, waiting for transfers between devices, partner(): return lax.ppermute(block, axis, route)  4.95 us
    ppermute x4, starting transfers between devices, partner(): return lax.ppermute(block, axis, route)  4.61 us
    pallas_call x2, Pallas kernels, first_level(): pl.pallas_call(functools.partial(first_level_kernel, column, rows), out_s...  2.67 us
    pallas_call x1, Pallas kernels, resample(): pl.pallas_call(resample_kernel, out_shape=(shape, shape), in_specs=[ANY,...  2.31 us
  transfers between devices with their start and end apart: 14, of which 8 were waited for; matrix products, arithmetic and copies ran while one was open for 5% of the time, Pallas kernels for 11%

profile of v6, /device:TPU:0, one launch (start us, length us, event | category | flops | bytes accessed | tf_op | source)
XLA Modules:
  0.0 62.2 jit_solution(3089841845190896565)
XLA Ops:
  0.0 0.0 copy-start
  0.0 0.0 copy-start.2
  0.0 0.0 copy-start.1
  0.0 2.3 %resample.1 = (bf16[2,192,512]{2,1,0:T(8,128)(2,1)S(1)}, bf16[2,192,512]{2,1,0:T(8,128)(2,1)S(1)}) custom-call(bf16[2,256,512]{2,1,0:T(8,128)(2,1)} %bitcast.20, bf16[2,512,512]{2,1,0:T(8,128)(2,1)} %bitcast.19), custom_call_target="tpu_custom_call" | custom-call | flops 536870912 | bytes 2097152 | tf_op jit(solution)/shard_map/resample/pallas_call | solution.py:101
  2.3 3.1 %collective-permute-start = (bf16[2,192,512]{2,1,0:T(8,128)(2,1)S(1)}, bf16[2,192,512]{2,1,0:T(8,128)(2,1)S(1)}, u32[]{:S(2)}, u32[]{:S(2)}) collective-permute-start(bf16[2,192,512]{2,1,0:T(8,128)(2,1)S(1)} %get-tuple-element.34.sent_first_ref), channel_id=1, source_target_pairs={{0,1},{1,0},{2,3},{3,2},{4,5},{5,4},{6,7},{7,6},{8,9},{9,8},{10,11... | collective-permute-start | bytes 1179656 | tf_op jit(solution)/shard_map/ppermute | solution.py:43
  5.4 0.0 collective-permute-start.1
  5.4 0.0 copy-done
  5.4 1.5 %collective-permute-start.2 = (s32[1,16,1]{1,2,0:T(1,128)S(1)}, s32[1,16,1]{1,2,0:T(1,128)S(1)}, u32[]{:S(2)}, u32[]{:S(2)}) collective-permute-start(s32[1,16,1]{1,2,0:T(1,128)S(1)} %copy-done), channel_id=1, source_target_pairs={{0,8},{8,0},{4,12},{12,4},{16,24},{24,16},{20,28},{28,20},{1,9},{9... | collective-permute-start | bytes 200 | tf_op jit(solution)/shard_map/ppermute | solution.py:54
  6.9 0.0 copy-done.2
  6.9 0.2 subtract_reduce_fusion.starts_ref
  7.1 0.1 pad_add_fusion.side_ref
  7.2 0.0 copy-done.1
  7.2 0.4 copy.8
  7.6 1.4 %collective-permute-done.2 = s32[1,16,1]{1,2,0:T(1,128)S(1)} collective-permute-done((s32[1,16,1]{1,2,0:T(1,128)S(1)}, s32[1,16,1]{1,2,0:T(1,128)S(1)}, u32[]{:S(2)}, u32[]{:S(2)}) %collective-permute-start.2) | collective-permute-done | bytes 96 | tf_op jit(solution)/shard_map/ppermute | solution.py:54
  9.0 1.6 %plan.1 = (s32[16]{0:T(128)S(1)}, s32[16]{0:T(128)S(1)}, s32[16]{0:T(128)S(1)}, s32[16]{0:T(128)S(1)}, s32[16]{0:T(128)S(1)}) custom-call(s32[1]{0:T(128)} %bitcast.me_ref, s32[16]{0:T(128)S(1)} %bitcast.17, s32[16]{0:T(128)S(1)} %bitcast.18), custom_call_target="tpu_custom_call" | custom-call | tf_op jit(solution)/shard_map/plan/pallas_call | solution.py:304
  10.6 4.0 %collective-permute-done.first_ref = bf16[2,192,512]{2,1,0:T(8,128)(2,1)S(1)} collective-permute-done((bf16[2,192,512]{2,1,0:T(8,128)(2,1)S(1)}, bf16[2,192,512]{2,1,0:T(8,128)(2,1)S(1)}, u32[]{:S(2)}, u32[]{:S(2)}) %collective-permute-start) | collective-permute-done | bytes 393248 | tf_op jit(solution)/shard_map/ppermute | solution.py:43
  14.5 0.0 collective-permute-done.1.second_ref
  14.5 1.3 %first_level.3 = bf16[2,512,256]{2,1,0:T(8,128)(2,1)S(1)} custom-call(s32[4]{0:T(128)S(1)} %subtract_reduce_fusion.starts_ref, s32[3]{0:T(128)S(1)} %pad_add_fusion.side_ref, bf16[2,192,512]{2,1,0:T(8,128)(2,1)S(1)} %get-tuple-element.34.sent_first_ref, bf16[2,192,512]{2,1,0:T(8,128)(2,1)S(1)} %get-tuple-element.35.sent_second_ref, ...), custom_call_target="tpu_custom_call" | custom-call | flops 335544320 | bytes 2097152 | tf_op jit(solution)/shard_map/first_level/pallas_call | solution.py:171
  15.9 0.1 collective-permute-start.3
  16.0 1.3 %first_level.2 = bf16[2,512,256]{2,1,0:T(8,128)(2,1)S(1)} custom-call(s32[4]{0:T(128)S(1)} %subtract_reduce_fusion.starts_ref, s32[3]{0:T(128)S(1)} %pad_add_fusion.side_ref, bf16[2,192,512]{2,1,0:T(8,128)(2,1)S(1)} %get-tuple-element.34.sent_first_ref, bf16[2,192,512]{2,1,0:T(8,128)(2,1)S(1)} %get-tuple-element.35.sent_second_ref, ...), custom_call_target="tpu_custom_call" | custom-call | flops 335544320 | bytes 2097152 | tf_op jit(solution)/shard_map/first_level/pallas_call | solution.py:171
  17.3 0.5 collective-permute-done.3
  17.8 0.1 add_convert_fusion.own_ref
  18.0 2.9 %collective-permute-start.4 = (bf16[2,192,256]{2,1,0:T(8,128)(2,1)S(1)}, bf16[2,192,256]{2,1,0:T(8,128)(2,1)S(1)}, u32[]{:S(2)}, u32[]{:S(2)}) collective-permute-start(bf16[2,192,256]{2,1,0:T(8,128)(2,1)S(1)} %get-tuple-element.64), channel_id=1, source_target_pairs={{0,1},{1,0},{2,3},{3,2},{4,5},{5,4},{6,7},{7,6},{8,9},{9,8},{10,11... | collective-permute-start | bytes 589832 | tf_op jit(solution)/shard_map/ppermute | solution.py:43
  21.0 0.0 collective-permute-start.5
  21.0 1.8 %copy.9 = bf16[1,8,2,128,320]{4,3,2,1,0:T(8,128)(2,1)S(1)} copy(bf16[1,8,2,128,320]{3,4,2,1,0:T(8,128)(2,1)} %param.11) | data formatting | bytes 2621440 | tf_op args[4]
  22.8 0.7 %fusion.1.starts_ref = s32[8]{0:T(128)S(1)} fusion(s32[8,8]{1,0:T(8,128)} %param.12, s32[]{:T(128)S(6)} %select_n.19, s32[]{:T(128)S(6)} %sub.25), kind=kLoop, calls=%fused_computation.6 | loop fusion | flops 8 | bytes 72 | tf_op jit(solution)/shard_map/sub | solution.py:471
  23.5 2.7 %collective-permute-done.4.first_ref = bf16[2,192,256]{2,1,0:T(8,128)(2,1)S(1)} collective-permute-done((bf16[2,192,256]{2,1,0:T(8,128)(2,1)S(1)}, bf16[2,192,256]{2,1,0:T(8,128)(2,1)S(1)}, u32[]{:S(2)}, u32[]{:S(2)}) %collective-permute-start.4) | collective-permute-done | bytes 196640 | tf_op jit(solution)/shard_map/ppermute | solution.py:43
  26.2 0.0 collective-permute-done.5.second_ref
  26.2 1.1 %second_level_early.1 = bf16[6,2,64,128]{3,2,1,0:T(8,128)(2,1)S(1)} custom-call(s32[8]{0:T(128)S(1)} %fusion.1.starts_ref, s32[3]{0:T(128)S(1)} %pad_add_fusion.side_ref, s32[16]{0:T(128)S(1)} %get-tuple-element.41.sector_ref, bf16[2,512,256]{2,1,0:T(8,128)(2,1)S(1)} %add_convert_fusion.own_ref, bf16[2,192,256]{2,1,0:T(8,128)(2,1)S(1)} %collective-permute-done.4.first_ref, ...), custom_call_target="tpu_custom_call" | custom-call | flops 125829120 | bytes 1048576 | tf_op jit(solution)/shard_map/second_level_early/pallas_call | solution.py:237
  27.3 1.6 %collective-permute-start.6 = (bf16[6,2,64,128]{3,2,1,0:T(8,128)(2,1)S(1)}, bf16[6,2,64,128]{3,2,1,0:T(8,128)(2,1)S(1)}, u32[]{:S(2)}, u32[]{:S(2)}) collective-permute-start(bf16[6,2,64,128]{3,2,1,0:T(8,128)(2,1)S(1)} %second_level_early.1), channel_id=1, source_target_pairs={{0,8},{8,0},{4,12},{12,4},{16,24},{24,16},{20,28},{28,20},{1,9},{9... | collective-permute-start | bytes 589832 | tf_op jit(solution)/shard_map/ppermute | solution.py:54
  28.8 1.9 %second_level.1 = (bf16[16,2,64,128]{3,2,1,0:T(8,128)(2,1)S(1)}, bf16[10,2,64,128]{3,2,1,0:T(8,128)(2,1)S(1)}) custom-call(s32[8]{0:T(128)S(1)} %fusion.1.starts_ref, s32[3]{0:T(128)S(1)} %pad_add_fusion.side_ref, s32[16]{0:T(128)S(1)} %get-tuple-element.44.own_at_ref, s32[16]{0:T(128)S(1)} %get-tuple-element.45.other_at_ref, ...), custom_call_target="tpu_custom_call" | custom-call | flops 671088640 | bytes 4194304 | tf_op jit(solution)/shard_map/second_level/pallas_call | solution.py:248
  30.8 3.0 %collective-permute-done.6.refs_0_ = bf16[6,2,64,128]{3,2,1,0:T(8,128)(2,1)S(1)} collective-permute-done((bf16[6,2,64,128]{3,2,1,0:T(8,128)(2,1)S(1)}, bf16[6,2,64,128]{3,2,1,0:T(8,128)(2,1)S(1)}, u32[]{:S(2)}, u32[]{:S(2)}) %collective-permute-start.6) | collective-permute-done | bytes 196640 | tf_op jit(solution)/shard_map/ppermute | solution.py:54
  33.8 1.5 %collective-permute-start.7 = (bf16[10,2,64,128]{3,2,1,0:T(8,128)(2,1)S(1)}, bf16[10,2,64,128]{3,2,1,0:T(8,128)(2,1)S(1)}, u32[]{:S(2)}, u32[]{:S(2)}) collective-permute-start(bf16[10,2,64,128]{3,2,1,0:T(8,128)(2,1)S(1)} %get-tuple-element.47), channel_id=1, source_target_pairs={{0,8},{8,0},{4,12},{12,4},{16,24},{24,16},{20,28},{28,20},{1,9},{9... | collective-permute-start | bytes 983048 | tf_op jit(solution)/shard_map/ppermute | solution.py:54
  35.3 0.6 early_wires.1
  35.9 2.7 %collective-permute-start.12 = (bf16[4,2,64,128]{3,2,1,0:T(8,128)(2,1)S(1)}, bf16[4,2,64,128]{3,2,1,0:T(8,128)(2,1)S(1)}, u32[]{:S(2)}, u32[]{:S(2)}) collective-permute-start(bf16[4,2,64,128]{3,2,1,0:T(8,128)(2,1)S(1)} %get-tuple-element.60), channel_id=1, source_target_pairs={{0,2},{1,3},{2,0},{3,1},{4,6},{5,7},{6,4},{7,5},{8,10},{9,11},{10,... | collective-permute-start | bytes 393224 | tf_op jit(solution)/shard_map/ppermute | solution.py:413
  38.6 1.3 %collective-permute-start.8 = (bf16[2,2,64,128]{3,2,1,0:T(8,128)(2,1)S(1)}, bf16[2,2,64,128]{3,2,1,0:T(8,128)(2,1)S(1)}, u32[]{:S(2)}, u32[]{:S(2)}) collective-permute-start(bf16[2,2,64,128]{3,2,1,0:T(8,128)(2,1)S(1)} %get-tuple-element.52), channel_id=1, source_target_pairs={{0,3},{1,2},{2,1},{3,0},{4,7},{5,6},{6,5},{7,4},{8,11},{9,10},{10,... | collective-permute-start | bytes 196616 | tf_op jit(solution)/shard_map/ppermute | solution.py:413
  39.8 4.9 %collective-permute-done.8.refs_0_ = bf16[2,2,64,128]{3,2,1,0:T(8,128)(2,1)S(1)} collective-permute-done((bf16[2,2,64,128]{3,2,1,0:T(8,128)(2,1)S(1)}, bf16[2,2,64,128]{3,2,1,0:T(8,128)(2,1)S(1)}, u32[]{:S(2)}, u32[]{:S(2)}) %collective-permute-start.8) | collective-permute-done | bytes 65568 | tf_op jit(solution)/shard_map/ppermute | solution.py:413
  44.7 0.0 collective-permute-done.7.refs_0_
  44.7 0.8 %late_wires.2 = (bf16[6,2,64,128]{3,2,1,0:T(8,128)(2,1)S(1)}, bf16[4,2,64,128]{3,2,1,0:T(8,128)(2,1)S(1)}, bf16[4,2,64,128]{3,2,1,0:T(8,128)(2,1)S(1)}, bf16[8,2,64,128]{3,2,1,0:T(8,128)(2,1)S(1)}) custom-call(s32[1]{0:T(128)} %bitcast.me_ref, s32[16]{0:T(128)S(1)} %get-tuple-element.48.target_ref, s32[16]{0:T(128)S(1)} %get-tuple-element.49.rank_ref, ...), custom_call_target="tpu_custom_call" | custom-call | bytes 2097152 | tf_op jit(solution)/shard_map/late_wires/pallas_call | solution.py:365
  45.5 1.5 %collective-permute-start.9 = (bf16[6,2,64,128]{3,2,1,0:T(8,128)(2,1)S(1)}, bf16[6,2,64,128]{3,2,1,0:T(8,128)(2,1)S(1)}, u32[]{:S(2)}, u32[]{:S(2)}) collective-permute-start(bf16[6,2,64,128]{3,2,1,0:T(8,128)(2,1)S(1)} %get-tuple-element.56), channel_id=1, source_target_pairs={{0,3},{1,2},{2,1},{3,0},{4,7},{5,6},{6,5},{7,4},{8,11},{9,10},{10,... | collective-permute-start | bytes 589832 | tf_op jit(solution)/shard_map/ppermute | solution.py:413
  47.0 0.0 collective-permute-done.12.refs_5_
  47.0 0.6 %late_wires.3 = bf16[4,2,64,128]{3,2,1,0:T(8,128)(2,1)S(1)} custom-call(s32[1]{0:T(128)} %bitcast.me_ref, s32[16]{0:T(128)S(1)} %get-tuple-element.48.target_ref, s32[16]{0:T(128)S(1)} %get-tuple-element.49.rank_ref, bf16[16,2,64,128]{3,2,1,0:T(8,128)(2,1)S(1)} %get-tuple-element.50.keep_ref, bf16[10,2,64,128]{3,2,1,0:T(8,128)(2,1)S(1)} %collective-permute-done.7.refs_0_, ...), custom_call_target="tpu_custom_call" | custom-call | bytes 2097152 | tf_op jit(solution)/shard_map/late_wires/pallas_call | solution.py:365
  47.6 2.3 %collective-permute-start.13 = (bf16[4,2,64,128]{3,2,1,0:T(8,128)(2,1)S(1)}, bf16[4,2,64,128]{3,2,1,0:T(8,128)(2,1)S(1)}, u32[]{:S(2)}, u32[]{:S(2)}) collective-permute-start(bf16[4,2,64,128]{3,2,1,0:T(8,128)(2,1)S(1)} %late_wires.3), channel_id=1, source_target_pairs={{0,2},{1,3},{2,0},{3,1},{4,6},{5,7},{6,4},{7,5},{8,10},{9,11},{10,... | collective-permute-start | bytes 393224 | tf_op jit(solution)/shard_map/ppermute | solution.py:413
  49.9 0.8 %collective-permute-start.10 = (bf16[4,2,64,128]{3,2,1,0:T(8,128)(2,1)S(1)}, bf16[4,2,64,128]{3,2,1,0:T(8,128)(2,1)S(1)}, u32[]{:S(2)}, u32[]{:S(2)}) collective-permute-start(bf16[4,2,64,128]{3,2,1,0:T(8,128)(2,1)S(1)} %get-tuple-element.57), channel_id=1, source_target_pairs={{0,1},{1,0},{2,3},{3,2},{4,5},{5,4},{6,7},{7,6},{8,9},{9,8},{10,11... | collective-permute-start | bytes 393224 | tf_op jit(solution)/shard_map/ppermute | solution.py:413
  50.7 1.3 %collective-permute-start.11 = (bf16[4,2,64,128]{3,2,1,0:T(8,128)(2,1)S(1)}, bf16[4,2,64,128]{3,2,1,0:T(8,128)(2,1)S(1)}, u32[]{:S(2)}, u32[]{:S(2)}) collective-permute-start(bf16[4,2,64,128]{3,2,1,0:T(8,128)(2,1)S(1)} %get-tuple-element.58), channel_id=1, source_target_pairs={{0,1},{1,0},{2,3},{3,2},{4,5},{5,4},{6,7},{7,6},{8,9},{9,8},{10,11... | collective-permute-start | bytes 393224 | tf_op jit(solution)/shard_map/ppermute | solution.py:413
  52.0 8.9 %collective-permute-done.13.refs_6_ = bf16[4,2,64,128]{3,2,1,0:T(8,128)(2,1)S(1)} collective-permute-done((bf16[4,2,64,128]{3,2,1,0:T(8,128)(2,1)S(1)}, bf16[4,2,64,128]{3,2,1,0:T(8,128)(2,1)S(1)}, u32[]{:S(2)}, u32[]{:S(2)}) %collective-permute-start.13) | collective-permute-done | bytes 131104 | tf_op jit(solution)/shard_map/ppermute | solution.py:413
  60.8 0.0 collective-permute-done.10.refs_2_
  60.8 0.3 collective-permute-done.11.refs_3_
  61.1 0.0 collective-permute-done.9.refs_1_
  61.1 1.0 %collect.1 = bf16[32,2,64,128]{3,2,1,0:T(8,128)(2,1)} custom-call(s32[1]{0:T(128)} %bitcast.me_ref, bf16[2,2,64,128]{3,2,1,0:T(8,128)(2,1)S(1)} %collective-permute-done.8.refs_0_, bf16[6,2,64,128]{3,2,1,0:T(8,128)(2,1)S(1)} %collective-permute-done.9.refs_1_, bf16[4,2,64,128]{3,2,1,0:T(8,128)(2,1)S(1)} %collective-permute-done.10.refs_2_, ...), custom_call_target="tpu_custom_call" | custom-call | bytes 2097152 | tf_op jit(solution)/shard_map/collect/pallas_call | solution.py:396
  (1 shorter events, 0.0 us)
Async XLA Ops:
  0.0 5.4 %copy-start = (s32[1,16,1]{1,2,0:T(1,128)S(1)}, s32[1,16,1]{1,2,0:T(1,128)}, u32[]{:S(2)}) copy-start(s32[1,16,1]{1,2,0:T(1,128)} %param.13) | copy-start | bytes 196
  0.0 6.9 %copy-start.2 = (s32[8,4]{0,1:T(4,128)S(1)}, s32[8,4]{0,1:T(4,128)}, u32[]{:S(2)}) copy-start(s32[8,4]{0,1:T(4,128)} %param.10) | copy-start | bytes 388
  0.0 7.2 %copy-start.1 = (bf16[1,4,2,128,320]{3,4,2,1,0:T(8,128)(2,1)S(1)}, bf16[1,4,2,128,320]{3,4,2,1,0:T(8,128)(2,1)}, u32[]{:S(2)}) copy-start(bf16[1,4,2,128,320]{3,4,2,1,0:T(8,128)(2,1)} %param.9) | copy-start | bytes 1966084
  2.3 12.2 %collective-permute-start = (bf16[2,192,512]{2,1,0:T(8,128)(2,1)S(1)}, bf16[2,192,512]{2,1,0:T(8,128)(2,1)S(1)}, u32[]{:S(2)}, u32[]{:S(2)}) collective-permute-start(bf16[2,192,512]{2,1,0:T(8,128)(2,1)S(1)} %get-tuple-element.34.sent_first_ref), channel_id=1, source_target_pairs={{0,1},{1,0},{2,3},{3,2},{4,5},{5,4},{6,7},{7,6},{8,9},{9,8},{10,11... | collective-permute-start | bytes 1179656 | tf_op jit(solution)/shard_map/ppermute | solution.py:43
  5.4 9.1 %collective-permute-start.1 = (bf16[2,192,512]{2,1,0:T(8,128)(2,1)S(1)}, bf16[2,192,512]{2,1,0:T(8,128)(2,1)S(1)}, u32[]{:S(2)}, u32[]{:S(2)}) collective-permute-start(bf16[2,192,512]{2,1,0:T(8,128)(2,1)S(1)} %get-tuple-element.35.sent_second_ref), channel_id=1, source_target_pairs={{0,4},{1,2},{2,1},{3,7},{4,0},{5,6},{6,5},{7,3},{8,12},{9,10},{10,... | collective-permute-start | bytes 1179656 | tf_op jit(solution)/shard_map/ppermute | solution.py:43
  5.4 3.5 %collective-permute-start.2 = (s32[1,16,1]{1,2,0:T(1,128)S(1)}, s32[1,16,1]{1,2,0:T(1,128)S(1)}, u32[]{:S(2)}, u32[]{:S(2)}) collective-permute-start(s32[1,16,1]{1,2,0:T(1,128)S(1)} %copy-done), channel_id=1, source_target_pairs={{0,8},{8,0},{4,12},{12,4},{16,24},{24,16},{20,28},{28,20},{1,9},{9... | collective-permute-start | bytes 200 | tf_op jit(solution)/shard_map/ppermute | solution.py:54
  15.9 2.0 %collective-permute-start.3 = (bf16[2,512,256]{2,1,0:T(8,128)(2,1)S(1)}, bf16[2,512,256]{2,1,0:T(8,128)(2,1)S(1)}, u32[]{:S(2)}, u32[]{:S(2)}) collective-permute-start(bf16[2,512,256]{2,1,0:T(8,128)(2,1)S(1)} %first_level.3), channel_id=1, source_target_pairs={{0,4},{4,0},{8,12},{12,8},{16,20},{20,16},{24,28},{28,24},{1,5},{5... | collective-permute-start | bytes 1572872 | tf_op jit(solution)/shard_map/ppermute | solution.py:54
  18.0 8.1 %collective-permute-start.4 = (bf16[2,192,256]{2,1,0:T(8,128)(2,1)S(1)}, bf16[2,192,256]{2,1,0:T(8,128)(2,1)S(1)}, u32[]{:S(2)}, u32[]{:S(2)}) collective-permute-start(bf16[2,192,256]{2,1,0:T(8,128)(2,1)S(1)} %get-tuple-element.64), channel_id=1, source_target_pairs={{0,1},{1,0},{2,3},{3,2},{4,5},{5,4},{6,7},{7,6},{8,9},{9,8},{10,11... | collective-permute-start | bytes 589832 | tf_op jit(solution)/shard_map/ppermute | solution.py:43
  21.0 5.2 %collective-permute-start.5 = (bf16[2,192,256]{2,1,0:T(8,128)(2,1)S(1)}, bf16[2,192,256]{2,1,0:T(8,128)(2,1)S(1)}, u32[]{:S(2)}, u32[]{:S(2)}) collective-permute-start(bf16[2,192,256]{2,1,0:T(8,128)(2,1)S(1)} %get-tuple-element.63), channel_id=1, source_target_pairs={{0,4},{1,2},{2,1},{3,7},{4,0},{5,6},{6,5},{7,3},{8,12},{9,10},{10,... | collective-permute-start | bytes 589832 | tf_op jit(solution)/shard_map/ppermute | solution.py:43
  27.3 6.5 %collective-permute-start.6 = (bf16[6,2,64,128]{3,2,1,0:T(8,128)(2,1)S(1)}, bf16[6,2,64,128]{3,2,1,0:T(8,128)(2,1)S(1)}, u32[]{:S(2)}, u32[]{:S(2)}) collective-permute-start(bf16[6,2,64,128]{3,2,1,0:T(8,128)(2,1)S(1)} %second_level_early.1), channel_id=1, source_target_pairs={{0,8},{8,0},{4,12},{12,4},{16,24},{24,16},{20,28},{28,20},{1,9},{9... | collective-permute-start | bytes 589832 | tf_op jit(solution)/shard_map/ppermute | solution.py:54
  33.8 10.9 %collective-permute-start.7 = (bf16[10,2,64,128]{3,2,1,0:T(8,128)(2,1)S(1)}, bf16[10,2,64,128]{3,2,1,0:T(8,128)(2,1)S(1)}, u32[]{:S(2)}, u32[]{:S(2)}) collective-permute-start(bf16[10,2,64,128]{3,2,1,0:T(8,128)(2,1)S(1)} %get-tuple-element.47), channel_id=1, source_target_pairs={{0,8},{8,0},{4,12},{12,4},{16,24},{24,16},{20,28},{28,20},{1,9},{9... | collective-permute-start | bytes 983048 | tf_op jit(solution)/shard_map/ppermute | solution.py:54
  35.9 11.1 %collective-permute-start.12 = (bf16[4,2,64,128]{3,2,1,0:T(8,128)(2,1)S(1)}, bf16[4,2,64,128]{3,2,1,0:T(8,128)(2,1)S(1)}, u32[]{:S(2)}, u32[]{:S(2)}) collective-permute-start(bf16[4,2,64,128]{3,2,1,0:T(8,128)(2,1)S(1)} %get-tuple-element.60), channel_id=1, source_target_pairs={{0,2},{1,3},{2,0},{3,1},{4,6},{5,7},{6,4},{7,5},{8,10},{9,11},{10,... | collective-permute-start | bytes 393224 | tf_op jit(solution)/shard_map/ppermute | solution.py:413
  38.6 6.2 %collective-permute-start.8 = (bf16[2,2,64,128]{3,2,1,0:T(8,128)(2,1)S(1)}, bf16[2,2,64,128]{3,2,1,0:T(8,128)(2,1)S(1)}, u32[]{:S(2)}, u32[]{:S(2)}) collective-permute-start(bf16[2,2,64,128]{3,2,1,0:T(8,128)(2,1)S(1)} %get-tuple-element.52), channel_id=1, source_target_pairs={{0,3},{1,2},{2,1},{3,0},{4,7},{5,6},{6,5},{7,4},{8,11},{9,10},{10,... | collective-permute-start | bytes 196616 | tf_op jit(solution)/shard_map/ppermute | solution.py:413
  45.5 15.6 %collective-permute-start.9 = (bf16[6,2,64,128]{3,2,1,0:T(8,128)(2,1)S(1)}, bf16[6,2,64,128]{3,2,1,0:T(8,128)(2,1)S(1)}, u32[]{:S(2)}, u32[]{:S(2)}) collective-permute-start(bf16[6,2,64,128]{3,2,1,0:T(8,128)(2,1)S(1)} %get-tuple-element.56), channel_id=1, source_target_pairs={{0,3},{1,2},{2,1},{3,0},{4,7},{5,6},{6,5},{7,4},{8,11},{9,10},{10,... | collective-permute-start | bytes 589832 | tf_op jit(solution)/shard_map/ppermute | solution.py:413
  47.6 13.2 %collective-permute-start.13 = (bf16[4,2,64,128]{3,2,1,0:T(8,128)(2,1)S(1)}, bf16[4,2,64,128]{3,2,1,0:T(8,128)(2,1)S(1)}, u32[]{:S(2)}, u32[]{:S(2)}) collective-permute-start(bf16[4,2,64,128]{3,2,1,0:T(8,128)(2,1)S(1)} %late_wires.3), channel_id=1, source_target_pairs={{0,2},{1,3},{2,0},{3,1},{4,6},{5,7},{6,4},{7,5},{8,10},{9,11},{10,... | collective-permute-start | bytes 393224 | tf_op jit(solution)/shard_map/ppermute | solution.py:413
  49.9 10.9 %collective-permute-start.10 = (bf16[4,2,64,128]{3,2,1,0:T(8,128)(2,1)S(1)}, bf16[4,2,64,128]{3,2,1,0:T(8,128)(2,1)S(1)}, u32[]{:S(2)}, u32[]{:S(2)}) collective-permute-start(bf16[4,2,64,128]{3,2,1,0:T(8,128)(2,1)S(1)} %get-tuple-element.57), channel_id=1, source_target_pairs={{0,1},{1,0},{2,3},{3,2},{4,5},{5,4},{6,7},{7,6},{8,9},{9,8},{10,11... | collective-permute-start | bytes 393224 | tf_op jit(solution)/shard_map/ppermute | solution.py:413
  50.7 10.4 %collective-permute-start.11 = (bf16[4,2,64,128]{3,2,1,0:T(8,128)(2,1)S(1)}, bf16[4,2,64,128]{3,2,1,0:T(8,128)(2,1)S(1)}, u32[]{:S(2)}, u32[]{:S(2)}) collective-permute-start(bf16[4,2,64,128]{3,2,1,0:T(8,128)(2,1)S(1)} %get-tuple-element.58), channel_id=1, source_target_pairs={{0,1},{1,0},{2,3},{3,2},{4,5},{5,4},{6,7},{7,6},{8,9},{9,8},{10,11... | collective-permute-start | bytes 393224 | tf_op jit(solution)/shard_map/ppermute | solution.py:413

commit v7 on v6

--- a/solution.py
+++ b/solution.py
@@ -58,58 +58,76 @@
     return jnp.dot(left, right, preferred_element_type=jnp.float32)
 
 
-def resample_kernel(child_hbm, kernel_hbm, first_ref, second_ref, child, kernel, own, sems):
-    aper, beam = lax.axis_index("aperture"), lax.axis_index("beam")
+def edges_kernel(child_hbm, first_ref, second_ref, sems):
+    even = 1 - (lax.axis_index("beam") & 1)
+    margin = first_ref.shape[1]
+    spare = child_hbm.shape[1] - margin
+    copies = []
+    for number, (start, ref) in enumerate(((even * spare, first_ref), ((1 - even) * spare, second_ref))):
+        rows = pl.ds(pl.multiple_of(start, BLK), margin)
+        copies.append(pltpu.make_async_copy(child_hbm.at[:, rows, :], ref, sems.at[number]))
+    for copy in copies:
+        copy.start()
+    for copy in copies:
+        copy.wait()
+
+
+def edges(child, margin):
+    shape = jax.ShapeDtypeStruct((2, margin, child.shape[2]), child.dtype)
+    return pl.pallas_call(
+        edges_kernel,
+        out_shape=(shape, shape),
+        in_specs=[ANY],
+        out_specs=(VMEM, VMEM),
+        scratch_shapes=[pltpu.SemaphoreType.DMA((2,))],
+        compiler_params=params(MOST_VMEM),
+        cost_estimate=cost(0, 2**20),
+        name="edges",
+    )(child)
+
+
+def complex_product(real, imag, k_real, k_imag):
+    return (
+        (dot(real, k_real) - dot(imag, k_imag)).astype(jnp.bfloat16),
+        (dot(real, k_imag) + dot(imag, k_real)).astype(jnp.bfloat16),
+    )
+
+
+def resample_kernel(child_ref, kernel_hbm, own_ref, kernel_ref, sems):
+    aper = lax.axis_index("aperture")
     half, quarter = aper & 1, (aper >> 1) & 1
-    even = 1 - (beam & 1)
-    rows, rng = child.shape[1:]
-    piece = rng // 4
-    child_copy = pltpu.make_async_copy(child_hbm, child, sems.at[4])
+    piece = kernel_ref.shape[2] // 4
     copies = []
     for place in range(4):
         source = (half ^ (place // 2)) * 2 + (quarter ^ (place % 2))
         copies.append(
             pltpu.make_async_copy(
                 kernel_hbm.at[:, :, pl.ds(pl.multiple_of(source * piece, 128), piece)],
-                kernel.at[:, :, place * piece : (place + 1) * piece],
+                kernel_ref.at[:, :, place * piece : (place + 1) * piece],
                 sems.at[place],
             )
         )
-    child_copy.start()
     for copy in copies:
         copy.start()
-    child_copy.wait()
-    real, imag = child[0], child[1]
-    margin = first_ref.shape[1]
-    tail = pl.ds(pl.multiple_of(even * (rows - margin), BLK), margin)
-    head = pl.ds(pl.multiple_of((1 - even) * (rows - margin), BLK), margin)
-    for side in range(2):
-        columns = slice(side * 2 * piece, (side + 1) * 2 * piece)
-        copies[2 * side].wait()
-        copies[2 * side + 1].wait()
-        k_real, k_imag = kernel[0, :, columns], kernel[1, :, columns]
-        own[0, :, columns] = (dot(real, k_real) - dot(imag, k_imag)).astype(jnp.bfloat16)
-        own[1, :, columns] = (dot(real, k_imag) + dot(imag, k_real)).astype(jnp.bfloat16)
-        for part in range(2):
-            first_ref[part, :, columns] = own[part, tail, columns]
-            second_ref[part, :, columns] = own[part, head, columns]
-
-
-def resample(child, kernel, margin):
+    for copy in copies:
+        copy.wait()
+    own_ref[0], own_ref[1] = complex_product(
+        child_ref[0], child_ref[1], kernel_ref[0], kernel_ref[1]
+    )
+
+
+def resample(child, kernel):
     rows, rng = child.shape[1:]
-    shape = jax.ShapeDtypeStruct((2, margin, rng), jnp.bfloat16)
     return pl.pallas_call(
         resample_kernel,
-        out_shape=(shape, shape),
-        in_specs=[ANY, ANY],
+        out_shape=(
+            jax.ShapeDtypeStruct(child.shape, jnp.bfloat16),
+            jax.ShapeDtypeStruct(kernel.shape, kernel.dtype),
+        ),
+        in_specs=[VMEM, ANY],
         out_specs=(VMEM, VMEM),
-        scratch_shapes=[
-            pltpu.VMEM(child.shape, jnp.bfloat16),
-            pltpu.VMEM(kernel.shape, jnp.bfloat16),
-            pltpu.VMEM(child.shape, jnp.bfloat16),
-            pltpu.SemaphoreType.DMA((5,)),
-        ],
-        compiler_params=params(MOST_VMEM),
+        scratch_shapes=[pltpu.SemaphoreType.DMA((4,))],
+        compiler_params=params(),
         cost_estimate=cost(4 * rows * rng * rng, 2**21),
         name="resample",
     )(child, kernel)
@@ -143,19 +161,18 @@
 
 
 def first_level_kernel(
-    column, rows, starts_ref, side_ref, sent_first_ref, sent_second_ref, first_ref, second_ref,
-    weights_ref, out_ref, padded,
+    column, starts_ref, side_ref, own_ref, first_ref, second_ref, kernel_ref, weights_ref,
+    out_ref, padded,
 ):
     sectors, stacked, window = weights_ref.shape
     beams = stacked // 2
-    margin = first_ref.shape[1]
+    margin, rows = first_ref.shape[1], own_ref.shape[1]
     columns = slice(column, column + out_ref.shape[2])
-    even = side_ref[0]
-    tail = pl.multiple_of(margin + even * (rows - margin), BLK)
-    head = pl.multiple_of(margin + (1 - even) * (rows - margin), BLK)
-    padded[:, pl.ds(tail, margin), :] = sent_first_ref[:, :, columns]
-    padded[:, pl.ds(head, margin), :] = sent_second_ref[:, :, columns]
-    place_halos(padded, side_ref, rows, first_ref[:, :, columns], second_ref[:, :, columns])
+    k_real, k_imag = kernel_ref[0, :, columns], kernel_ref[1, :, columns]
+    padded[:, margin : margin + rows, :] = own_ref[:, :, columns]
+    first = complex_product(first_ref[0], first_ref[1], k_real, k_imag)
+    second = complex_product(second_ref[0], second_ref[1], k_real, k_imag)
+    place_halos(padded, side_ref, rows, jnp.stack(first), jnp.stack(second))
     for sector in range(sectors):
         place = pl.ds(pl.multiple_of(starts_ref[sector] * BLK, BLK), window)
         parts = complex_window(weights_ref[sector], padded[0, place, :], padded[1, place, :])
@@ -163,21 +180,21 @@
             out_ref[part, sector * beams : (sector + 1) * beams, :] = parts[part]
 
 
-def first_level(column, rows, starts, side, sent, halos, weights):
+def first_level(column, starts, side, own, halos, kernel, weights):
     sectors, stacked, window = weights.shape
-    margin, rng = sent[0].shape[1:]
-    assert 2 * margin >= rows
+    margin, rows, rng = halos[0].shape[1], own.shape[1], own.shape[2]
     width = rng // 2
+    macs = sectors * 2 * stacked * window * width + 8 * margin * rng * width
     return pl.pallas_call(
-        functools.partial(first_level_kernel, column, rows),
+        functools.partial(first_level_kernel, column),
         out_shape=jax.ShapeDtypeStruct((2, sectors * stacked // 2, width), jnp.bfloat16),
         in_specs=[SMEM, SMEM] + [VMEM] * 5,
         out_specs=VMEM,
         scratch_shapes=[pltpu.VMEM((2, rows + 2 * margin, width), jnp.bfloat16)],
         compiler_params=params(),
-        cost_estimate=cost(sectors * 2 * stacked * window * width, 2**21),
+        cost_estimate=cost(macs, 2**21),
         name="first_level",
-    )(starts, side, *sent, *halos, weights)
+    )(starts, side, own, *halos, kernel, weights)
 
 
 def second_level_early_kernel(
@@ -427,8 +444,7 @@
     beam_index = lax.axis_index("beam")
     beam_count = lax.axis_size("beam")
     margin = MARGIN_BLOCKS * BLK
-    rows = subimages.shape[2]
-    local_blocks = rows // BLK
+    local_blocks = subimages.shape[2] // BLK
     even = (beam_index + 1) % 2
     ends = (beam_index == 0, beam_index == beam_count - 1)
     side = jnp.stack([even] + [end.astype(jnp.int32) for end in ends])
@@ -445,23 +461,24 @@
     early_spans += [(distance, 0, longer) for distance in others]
     late_spans = [(distance, shorter, capacity) for distance in odd]
     for distance in range(1, beam_count // 2):
-        late_spans += [(distance, 0, capacity // 2), (distance, capacity // 2, capacity)]
+        cut = (5 * capacity + 4) // 8
+        late_spans += [(distance, 0, cut), (distance, cut, capacity)]
     late_spans.append((0, 0, capacity))
     last_spans = [(distance, longer, capacity) for distance in others]
 
-    sent = resample(subimages[0], range_kernel[0], margin)
-    halos = trade_edges(*sent)
+    halos = trade_edges(*edges(subimages[0], margin))
+    own, kernel = resample(subimages[0], range_kernel[0])
     own_owners = owners[0, :, 0]
     other_owners = partner(owners, "aperture", 1)[0, :, 0]
     planned = plan(longer - shorter, me, own_owners, other_owners, beam_count)
     begin0 = table_row(starts0, aper_index) - (beam_index * local_blocks - MARGIN_BLOCKS)
-    halos, planned = lax.optimization_barrier((halos, planned))
+    halos, own, planned = lax.optimization_barrier((halos, own, planned))
     *planned, target, rank = planned
     width = range_kernel.shape[3] // 2
     weights = stacked_weights(weights0)
-    send = first_level(width, rows, begin0, side, sent, halos, weights)
+    send = first_level(width, begin0, side, own, halos, kernel, weights)
     other = partner(send, "aperture", 0)
-    keep = first_level(0, rows, begin0, side, sent, halos, weights)
+    keep = first_level(0, begin0, side, own, halos, kernel, weights)
     level_one = (keep.astype(jnp.float32) + other.astype(jnp.float32)).astype(jnp.bfloat16)
 
     beams = level_one.shape[1]

time: 62.3 us -> 65.1 us (1.045)
  waiting for transfers between devices: 25.7 us -> 20.7 us
  local copies, waits for them, and re-layouts: 2.24 us -> 5.59 us
  Pallas kernels: 12.7 us -> 15.5 us
  other arithmetic: 1.1 us -> 2.82 us
    unnamed x8, local copies, waits for them, and re-layouts: 2.2 us -> 5.56 us
    ppermute x4, waiting for transfers between devices: 6.63 us -> 3.33 us  [trade_edges(): received.append(lax.ppermute(block, ('aperture', 'beam'), route))]
    pallas_call x3 -> x4, Pallas kernels: 4.98 us -> 7.7 us  [the longest x2 4.75 us: first_level(): pl.pallas_call(functools.partial(first_level_kernel, column), out_shape=j...]
    ppermute x4, waiting for transfers between devices: 4.95 us -> 3.45 us  [partner(): return lax.ppermute(block, axis, route)]
    convert_element_type x1, other arithmetic: 0.14 us -> 1.17 us  [local(): (keep.astype(jnp.float32) + other.astype(jnp.float32)).astype(jnp.bfloat16)]
    sub x1, other arithmetic: 0.18 us -> 0.86 us  [local(): table_row(starts0, aper_index) - (beam_index * local_blocks - MARGIN_BLOCKS)]
  transfers between devices with their start and end apart: 14 -> 14, of which waited for: 8 -> 9; matrix products, arithmetic and copies ran while one was open for 5% -> 8% of each run, Pallas kernels for 11% -> 13%
where the time goes in v7:
time: 65.1 us; the launch traced here: 64.8 us
  waiting for transfers between devices  20.7 us (32%)
  starting transfers between devices  20 us (31%)
  Pallas kernels  15.5 us (24%)
  local copies, waits for them, and re-layouts  5.59 us (9%)
  other arithmetic  2.82 us (4%)
    ppermute x6, waiting for transfers between devices, spread(): received.append(lax.ppermute(wire, 'beam', route) if distance else wire)  13.9 us
    ppermute x6, starting transfers between devices, spread(): received.append(lax.ppermute(wire, 'beam', route) if distance else wire)  9.47 us
    ppermute x4, starting transfers between devices, trade_edges(): received.append(lax.ppermute(block, ('aperture', 'beam'), route))  6.01 us
    unnamed x8, local copies, waits for them, and re-layouts  5.56 us
    pallas_call x2, Pallas kernels, first_level(): pl.pallas_call(functools.partial(first_level_kernel, column), out_shape=j...  4.75 us
    ppermute x4, starting transfers between devices, partner(): return lax.ppermute(block, axis, route)  4.54 us
    ppermute x4, waiting for transfers between devices, partner(): return lax.ppermute(block, axis, route)  3.45 us
    ppermute x4, waiting for transfers between devices, trade_edges(): received.append(lax.ppermute(block, ('aperture', 'beam'), route))  3.33 us
  transfers between devices with their start and end apart: 14, of which 9 were waited for; matrix products, arithmetic and copies ran while one was open for 8% of the time, Pallas kernels for 13%

profile of v7, /device:TPU:0, one launch (start us, length us, event | category | flops | bytes accessed | tf_op | source)
XLA Modules:
  0.0 64.8 jit_solution(17402549710042669155)
XLA Ops:
  0.0 2.0 %edges.1 = (bf16[2,192,512]{2,1,0:T(8,128)(2,1)}, bf16[2,192,512]{2,1,0:T(8,128)(2,1)}) custom-call(bf16[2,256,512]{2,1,0:T(8,128)(2,1)} %bitcast.17), custom_call_target="tpu_custom_call" | custom-call | bytes 1048576 | tf_op jit(solution)/shard_map/edges/pallas_call | solution.py:77
  2.0 3.1 %collective-permute-start = (bf16[2,192,512]{2,1,0:T(8,128)(2,1)}, bf16[2,192,512]{2,1,0:T(8,128)(2,1)S(1)}, u32[]{:S(2)}, u32[]{:S(2)}) collective-permute-start(bf16[2,192,512]{2,1,0:T(8,128)(2,1)} %get-tuple-element.37), channel_id=1, source_target_pairs={{0,1},{1,0},{2,3},{3,2},{4,5},{5,4},{6,7},{7,6},{8,9},{9,8},{10,11... | collective-permute-start | bytes 1179656 | tf_op jit(solution)/shard_map/ppermute | solution.py:43
  5.1 0.0 collective-permute-start.1
  5.1 1.5 %collective-permute-start.2 = (s32[1,16,1]{1,2,0:T(1,128)}, s32[1,16,1]{1,2,0:T(1,128)S(1)}, u32[]{:S(2)}, u32[]{:S(2)}) collective-permute-start(s32[1,16,1]{1,2,0:T(1,128)} %param.13), channel_id=1, source_target_pairs={{0,8},{8,0},{4,12},{12,4},{16,24},{24,16},{20,28},{28,20},{1,9},{9... | collective-permute-start | bytes 200 | tf_op jit(solution)/shard_map/ppermute | solution.py:54
  6.6 0.9 %subtract_reduce_fusion.starts_ref = s32[4]{0:T(128)S(1)} fusion(s32[8,4]{0,1:T(4,128)} %param.10, s32[]{:T(128)S(6)} %select_n.19, s32[]{:T(128)S(6)} %sub.29), kind=kLoop, calls=%fused_computation.1 | loop fusion | flops 4 | bytes 40 | tf_op jit(solution)/shard_map/sub | solution.py:474
  7.5 0.0 copy-start
  7.5 1.0 %copy-done = bf16[1,2,256,512]{3,2,1,0:T(8,128)(2,1)S(1)} copy-done((bf16[1,2,256,512]{3,2,1,0:T(8,128)(2,1)S(1)}, bf16[1,2,256,512]{3,2,1,0:T(8,128)(2,1)}, u32[]{:S(2)}) %copy-start) | copy-done | bytes 524312
  8.5 0.0 copy-start.1
  8.5 1.2 %copy-done.1 = bf16[1,2,512,512]{3,2,1,0:T(8,128)(2,1)S(1)} copy-done((bf16[1,2,512,512]{3,2,1,0:T(8,128)(2,1)S(1)}, bf16[1,2,512,512]{3,2,1,0:T(8,128)(2,1)}, u32[]{:S(2)}) %copy-start.1) | copy-done | bytes 1048600
  9.7 0.0 copy-start.2
  9.7 0.9 %resample.1 = (bf16[2,256,512]{2,1,0:T(8,128)(2,1)S(1)}, bf16[2,512,512]{2,1,0:T(8,128)(2,1)S(1)}) custom-call(bf16[2,256,512]{2,1,0:T(8,128)(2,1)S(1)} %bitcast.18, bf16[2,512,512]{2,1,0:T(8,128)(2,1)S(1)} %bitcast.19), custom_call_target="tpu_custom_call" | custom-call | flops 536870912 | bytes 2097152 | tf_op jit(solution)/shard_map/resample/pallas_call | solution.py:121
  10.7 0.1 pad_add_fusion.side_ref
  10.8 1.4 %copy.8 = bf16[1,4,2,128,320]{4,3,2,1,0:T(8,128)(2,1)S(1)} copy(bf16[1,4,2,128,320]{3,4,2,1,0:T(8,128)(2,1)} %param.9) | data formatting | bytes 1310720 | tf_op args[2]
  12.2 0.0 collective-permute-done.2
  12.2 0.0 copy-done.2
  12.2 1.6 %plan.1 = (s32[16]{0:T(128)S(1)}, s32[16]{0:T(128)S(1)}, s32[16]{0:T(128)S(1)}, s32[16]{0:T(128)S(1)}, s32[16]{0:T(128)S(1)}) custom-call(s32[1]{0:T(128)} %bitcast.me_ref, s32[16]{0:T(128)S(1)} %bitcast.20, s32[16]{0:T(128)S(1)} %bitcast.21), custom_call_target="tpu_custom_call" | custom-call | tf_op jit(solution)/shard_map/plan/pallas_call | solution.py:321
  13.8 0.6 collective-permute-done.first_ref
  14.4 0.0 collective-permute-done.1.second_ref
  14.4 2.8 %first_level.3 = bf16[2,512,256]{2,1,0:T(8,128)(2,1)} custom-call(s32[4]{0:T(128)S(1)} %subtract_reduce_fusion.starts_ref, s32[3]{0:T(128)S(1)} %pad_add_fusion.side_ref, bf16[2,256,512]{2,1,0:T(8,128)(2,1)S(1)} %get-tuple-element.46.own_ref, bf16[2,192,512]{2,1,0:T(8,128)(2,1)S(1)} %collective-permute-done.first_ref, ...), custom_call_target="tpu_custom_call" | custom-call | flops 738197504 | bytes 2097152 | tf_op jit(solution)/shard_map/first_level/pallas_call | solution.py:188
  17.2 0.0 collective-permute-start.3
  17.2 2.0 %first_level.2 = bf16[2,512,256]{2,1,0:T(8,128)(2,1)S(1)} custom-call(s32[4]{0:T(128)S(1)} %subtract_reduce_fusion.starts_ref, s32[3]{0:T(128)S(1)} %pad_add_fusion.side_ref, bf16[2,256,512]{2,1,0:T(8,128)(2,1)S(1)} %get-tuple-element.46.own_ref, bf16[2,192,512]{2,1,0:T(8,128)(2,1)S(1)} %collective-permute-done.first_ref, ...), custom_call_target="tpu_custom_call" | custom-call | flops 738197504 | bytes 2097152 | tf_op jit(solution)/shard_map/first_level/pallas_call | solution.py:188
  19.2 0.3 collective-permute-done.3
  19.5 1.2 %add_convert_fusion.own_ref = bf16[2,512,256]{2,1,0:T(8,128)(2,1)S(1)} fusion(bf16[2,512,256]{2,1,0:T(8,128)(2,1)} %collective-permute-done.3, bf16[2,512,256]{2,1,0:T(8,128)(2,1)S(1)} %first_level.2), kind=kLoop, calls=%fused_computation | loop fusion | flops 1048576 | bytes 1572864 | tf_op jit(solution)/shard_map/convert_element_type | solution.py:482
  20.7 2.9 %collective-permute-start.4 = (bf16[2,192,256]{2,1,0:T(8,128)(2,1)S(1)}, bf16[2,192,256]{2,1,0:T(8,128)(2,1)S(1)}, u32[]{:S(2)}, u32[]{:S(2)}) collective-permute-start(bf16[2,192,256]{2,1,0:T(8,128)(2,1)S(1)} %get-tuple-element.70), channel_id=1, source_target_pairs={{0,1},{1,0},{2,3},{3,2},{4,5},{5,4},{6,7},{7,6},{8,9},{9,8},{10,11... | collective-permute-start | bytes 589832 | tf_op jit(solution)/shard_map/ppermute | solution.py:43
  23.6 0.0 collective-permute-start.5
  23.6 1.9 %copy.9 = bf16[1,8,2,128,320]{4,3,2,1,0:T(8,128)(2,1)S(1)} copy(bf16[1,8,2,128,320]{3,4,2,1,0:T(8,128)(2,1)} %param.11) | data formatting | bytes 2621440 | tf_op args[4]
  25.5 0.7 %fusion.1.starts_ref = s32[8]{0:T(128)S(1)} fusion(s32[8,8]{1,0:T(8,128)} %param.12, s32[]{:T(128)S(6)} %select_n.19, s32[]{:T(128)S(6)} %sub.25), kind=kLoop, calls=%fused_computation.6 | loop fusion | flops 8 | bytes 72 | tf_op jit(solution)/shard_map/sub | solution.py:488
  26.2 2.7 %collective-permute-done.4.first_ref = bf16[2,192,256]{2,1,0:T(8,128)(2,1)S(1)} collective-permute-done((bf16[2,192,256]{2,1,0:T(8,128)(2,1)S(1)}, bf16[2,192,256]{2,1,0:T(8,128)(2,1)S(1)}, u32[]{:S(2)}, u32[]{:S(2)}) %collective-permute-start.4) | collective-permute-done | bytes 196640 | tf_op jit(solution)/shard_map/ppermute | solution.py:43
  28.9 0.0 collective-permute-done.5.second_ref
  28.9 1.1 %second_level_early.1 = bf16[6,2,64,128]{3,2,1,0:T(8,128)(2,1)S(1)} custom-call(s32[8]{0:T(128)S(1)} %fusion.1.starts_ref, s32[3]{0:T(128)S(1)} %pad_add_fusion.side_ref, s32[16]{0:T(128)S(1)} %get-tuple-element.45.sector_ref, bf16[2,512,256]{2,1,0:T(8,128)(2,1)S(1)} %add_convert_fusion.own_ref, bf16[2,192,256]{2,1,0:T(8,128)(2,1)S(1)} %collective-permute-done.4.first_ref, ...), custom_call_target="tpu_custom_call" | custom-call | flops 125829120 | bytes 1048576 | tf_op jit(solution)/shard_map/second_level_early/pallas_call | solution.py:254
  30.0 1.6 %collective-permute-start.6 = (bf16[6,2,64,128]{3,2,1,0:T(8,128)(2,1)S(1)}, bf16[6,2,64,128]{3,2,1,0:T(8,128)(2,1)S(1)}, u32[]{:S(2)}, u32[]{:S(2)}) collective-permute-start(bf16[6,2,64,128]{3,2,1,0:T(8,128)(2,1)S(1)} %second_level_early.1), channel_id=1, source_target_pairs={{0,8},{8,0},{4,12},{12,4},{16,24},{24,16},{20,28},{28,20},{1,9},{9... | collective-permute-start | bytes 589832 | tf_op jit(solution)/shard_map/ppermute | solution.py:54
  31.6 2.0 %second_level.1 = (bf16[16,2,64,128]{3,2,1,0:T(8,128)(2,1)S(1)}, bf16[10,2,64,128]{3,2,1,0:T(8,128)(2,1)S(1)}) custom-call(s32[8]{0:T(128)S(1)} %fusion.1.starts_ref, s32[3]{0:T(128)S(1)} %pad_add_fusion.side_ref, s32[16]{0:T(128)S(1)} %get-tuple-element.50.own_at_ref, s32[16]{0:T(128)S(1)} %get-tuple-element.51.other_at_ref, ...), custom_call_target="tpu_custom_call" | custom-call | flops 671088640 | bytes 4194304 | tf_op jit(solution)/shard_map/second_level/pallas_call | solution.py:265
  33.6 3.1 %collective-permute-done.6.refs_0_ = bf16[6,2,64,128]{3,2,1,0:T(8,128)(2,1)S(1)} collective-permute-done((bf16[6,2,64,128]{3,2,1,0:T(8,128)(2,1)S(1)}, bf16[6,2,64,128]{3,2,1,0:T(8,128)(2,1)S(1)}, u32[]{:S(2)}, u32[]{:S(2)}) %collective-permute-start.6) | collective-permute-done | bytes 196640 | tf_op jit(solution)/shard_map/ppermute | solution.py:54
  36.6 1.5 %collective-permute-start.7 = (bf16[10,2,64,128]{3,2,1,0:T(8,128)(2,1)S(1)}, bf16[10,2,64,128]{3,2,1,0:T(8,128)(2,1)S(1)}, u32[]{:S(2)}, u32[]{:S(2)}) collective-permute-start(bf16[10,2,64,128]{3,2,1,0:T(8,128)(2,1)S(1)} %get-tuple-element.53), channel_id=1, source_target_pairs={{0,8},{8,0},{4,12},{12,4},{16,24},{24,16},{20,28},{28,20},{1,9},{9... | collective-permute-start | bytes 983048 | tf_op jit(solution)/shard_map/ppermute | solution.py:54
  38.1 0.6 early_wires.1
  38.8 2.4 %collective-permute-start.8 = (bf16[2,2,64,128]{3,2,1,0:T(8,128)(2,1)S(1)}, bf16[2,2,64,128]{3,2,1,0:T(8,128)(2,1)S(1)}, u32[]{:S(2)}, u32[]{:S(2)}) collective-permute-start(bf16[2,2,64,128]{3,2,1,0:T(8,128)(2,1)S(1)} %get-tuple-element.58), channel_id=1, source_target_pairs={{0,3},{1,2},{2,1},{3,0},{4,7},{5,6},{6,5},{7,4},{8,11},{9,10},{10,... | collective-permute-start | bytes 196616 | tf_op jit(solution)/shard_map/ppermute | solution.py:430
  41.2 0.6 collective-permute-start.12
  41.8 3.2 %collective-permute-done.8.refs_0_ = bf16[2,2,64,128]{3,2,1,0:T(8,128)(2,1)S(1)} collective-permute-done((bf16[2,2,64,128]{3,2,1,0:T(8,128)(2,1)S(1)}, bf16[2,2,64,128]{3,2,1,0:T(8,128)(2,1)S(1)}, u32[]{:S(2)}, u32[]{:S(2)}) %collective-permute-start.8) | collective-permute-done | bytes 65568 | tf_op jit(solution)/shard_map/ppermute | solution.py:430
  45.0 0.1 collective-permute-done.7.refs_0_
  45.1 0.8 %late_wires.2 = (bf16[6,2,64,128]{3,2,1,0:T(8,128)(2,1)S(1)}, bf16[5,2,64,128]{3,2,1,0:T(8,128)(2,1)S(1)}, bf16[3,2,64,128]{3,2,1,0:T(8,128)(2,1)S(1)}, bf16[8,2,64,128]{3,2,1,0:T(8,128)(2,1)S(1)}) custom-call(s32[1]{0:T(128)} %bitcast.me_ref, s32[16]{0:T(128)S(1)} %get-tuple-element.54.target_ref, s32[16]{0:T(128)S(1)} %get-tuple-element.55.rank_ref, ...), custom_call_target="tpu_custom_call" | custom-call | bytes 2097152 | tf_op jit(solution)/shard_map/late_wires/pallas_call | solution.py:382
  45.9 2.3 %collective-permute-start.9 = (bf16[6,2,64,128]{3,2,1,0:T(8,128)(2,1)S(1)}, bf16[6,2,64,128]{3,2,1,0:T(8,128)(2,1)S(1)}, u32[]{:S(2)}, u32[]{:S(2)}) collective-permute-start(bf16[6,2,64,128]{3,2,1,0:T(8,128)(2,1)S(1)} %get-tuple-element.62), channel_id=1, source_target_pairs={{0,3},{1,2},{2,1},{3,0},{4,7},{5,6},{6,5},{7,4},{8,11},{9,10},{10,... | collective-permute-start | bytes 589832 | tf_op jit(solution)/shard_map/ppermute | solution.py:430
  48.2 1.8 %collective-permute-start.10 = (bf16[5,2,64,128]{3,2,1,0:T(8,128)(2,1)S(1)}, bf16[5,2,64,128]{3,2,1,0:T(8,128)(2,1)S(1)}, u32[]{:S(2)}, u32[]{:S(2)}) collective-permute-start(bf16[5,2,64,128]{3,2,1,0:T(8,128)(2,1)S(1)} %get-tuple-element.63), channel_id=1, source_target_pairs={{0,1},{1,0},{2,3},{3,2},{4,5},{5,4},{6,7},{7,6},{8,9},{9,8},{10,11... | collective-permute-start | bytes 491528 | tf_op jit(solution)/shard_map/ppermute | solution.py:430
  50.0 5.0 %collective-permute-done.12.refs_5_ = bf16[4,2,64,128]{3,2,1,0:T(8,128)(2,1)S(1)} collective-permute-done((bf16[4,2,64,128]{3,2,1,0:T(8,128)(2,1)S(1)}, bf16[4,2,64,128]{3,2,1,0:T(8,128)(2,1)S(1)}, u32[]{:S(2)}, u32[]{:S(2)}) %collective-permute-start.12) | collective-permute-done | bytes 131104 | tf_op jit(solution)/shard_map/ppermute | solution.py:430
  55.1 0.6 late_wires.3
  55.7 0.1 collective-permute-start.13
  55.8 2.2 %collective-permute-start.11 = (bf16[3,2,64,128]{3,2,1,0:T(8,128)(2,1)S(1)}, bf16[3,2,64,128]{3,2,1,0:T(8,128)(2,1)S(1)}, u32[]{:S(2)}, u32[]{:S(2)}) collective-permute-start(bf16[3,2,64,128]{3,2,1,0:T(8,128)(2,1)S(1)} %get-tuple-element.64), channel_id=1, source_target_pairs={{0,1},{1,0},{2,3},{3,2},{4,5},{5,4},{6,7},{7,6},{8,9},{9,8},{10,11... | collective-permute-start | bytes 294920 | tf_op jit(solution)/shard_map/ppermute | solution.py:430
  58.0 2.7 %collective-permute-done.11.refs_3_ = bf16[3,2,64,128]{3,2,1,0:T(8,128)(2,1)S(1)} collective-permute-done((bf16[3,2,64,128]{3,2,1,0:T(8,128)(2,1)S(1)}, bf16[3,2,64,128]{3,2,1,0:T(8,128)(2,1)S(1)}, u32[]{:S(2)}, u32[]{:S(2)}) %collective-permute-start.11) | collective-permute-done | bytes 98336 | tf_op jit(solution)/shard_map/ppermute | solution.py:430
  60.7 3.0 %collective-permute-done.13.refs_6_ = bf16[4,2,64,128]{3,2,1,0:T(8,128)(2,1)S(1)} collective-permute-done((bf16[4,2,64,128]{3,2,1,0:T(8,128)(2,1)S(1)}, bf16[4,2,64,128]{3,2,1,0:T(8,128)(2,1)S(1)}, u32[]{:S(2)}, u32[]{:S(2)}) %collective-permute-start.13) | collective-permute-done | bytes 131104 | tf_op jit(solution)/shard_map/ppermute | solution.py:430
  63.7 0.0 collective-permute-done.10.refs_2_
  63.7 0.0 collective-permute-done.9.refs_1_
  63.7 1.0 %collect.1 = bf16[32,2,64,128]{3,2,1,0:T(8,128)(2,1)} custom-call(s32[1]{0:T(128)} %bitcast.me_ref, bf16[2,2,64,128]{3,2,1,0:T(8,128)(2,1)S(1)} %collective-permute-done.8.refs_0_, bf16[6,2,64,128]{3,2,1,0:T(8,128)(2,1)S(1)} %collective-permute-done.9.refs_1_, bf16[5,2,64,128]{3,2,1,0:T(8,128)(2,1)S(1)} %collective-permute-done.10.refs_2_, ...), custom_call_target="tpu_custom_call" | custom-call | bytes 2097152 | tf_op jit(solution)/shard_map/collect/pallas_call | solution.py:413
  (1 shorter events, 0.0 us)
Async XLA Ops:
  2.0 12.4 %collective-permute-start = (bf16[2,192,512]{2,1,0:T(8,128)(2,1)}, bf16[2,192,512]{2,1,0:T(8,128)(2,1)S(1)}, u32[]{:S(2)}, u32[]{:S(2)}) collective-permute-start(bf16[2,192,512]{2,1,0:T(8,128)(2,1)} %get-tuple-element.37), channel_id=1, source_target_pairs={{0,1},{1,0},{2,3},{3,2},{4,5},{5,4},{6,7},{7,6},{8,9},{9,8},{10,11... | collective-permute-start | bytes 1179656 | tf_op jit(solution)/shard_map/ppermute | solution.py:43
  5.1 9.3 %collective-permute-start.1 = (bf16[2,192,512]{2,1,0:T(8,128)(2,1)}, bf16[2,192,512]{2,1,0:T(8,128)(2,1)S(1)}, u32[]{:S(2)}, u32[]{:S(2)}) collective-permute-start(bf16[2,192,512]{2,1,0:T(8,128)(2,1)} %get-tuple-element.38), channel_id=1, source_target_pairs={{0,4},{1,2},{2,1},{3,7},{4,0},{5,6},{6,5},{7,3},{8,12},{9,10},{10,... | collective-permute-start | bytes 1179656 | tf_op jit(solution)/shard_map/ppermute | solution.py:43
  5.1 7.1 %collective-permute-start.2 = (s32[1,16,1]{1,2,0:T(1,128)}, s32[1,16,1]{1,2,0:T(1,128)S(1)}, u32[]{:S(2)}, u32[]{:S(2)}) collective-permute-start(s32[1,16,1]{1,2,0:T(1,128)} %param.13), channel_id=1, source_target_pairs={{0,8},{8,0},{4,12},{12,4},{16,24},{24,16},{20,28},{28,20},{1,9},{9... | collective-permute-start | bytes 200 | tf_op jit(solution)/shard_map/ppermute | solution.py:54
  7.5 1.0 %copy-start = (bf16[1,2,256,512]{3,2,1,0:T(8,128)(2,1)S(1)}, bf16[1,2,256,512]{3,2,1,0:T(8,128)(2,1)}, u32[]{:S(2)}) copy-start(bf16[1,2,256,512]{3,2,1,0:T(8,128)(2,1)} %param.7) | copy-start | bytes 1572868
  8.5 1.2 %copy-start.1 = (bf16[1,2,512,512]{3,2,1,0:T(8,128)(2,1)S(1)}, bf16[1,2,512,512]{3,2,1,0:T(8,128)(2,1)}, u32[]{:S(2)}) copy-start(bf16[1,2,512,512]{3,2,1,0:T(8,128)(2,1)} %param.8) | copy-start | bytes 3145732
  9.7 2.5 %copy-start.2 = (s32[1,16,1]{1,2,0:T(1,128)S(1)}, s32[1,16,1]{1,2,0:T(1,128)}, u32[]{:S(2)}) copy-start(s32[1,16,1]{1,2,0:T(1,128)} %param.13) | copy-start | bytes 196
  17.2 2.3 %collective-permute-start.3 = (bf16[2,512,256]{2,1,0:T(8,128)(2,1)}, bf16[2,512,256]{2,1,0:T(8,128)(2,1)}, u32[]{:S(2)}, u32[]{:S(2)}) collective-permute-start(bf16[2,512,256]{2,1,0:T(8,128)(2,1)} %first_level.3), channel_id=1, source_target_pairs={{0,4},{4,0},{8,12},{12,8},{16,20},{20,16},{24,28},{28,24},{1,5},{5... | collective-permute-start | bytes 1572872 | tf_op jit(solution)/shard_map/ppermute | solution.py:54
  20.7 8.2 %collective-permute-start.4 = (bf16[2,192,256]{2,1,0:T(8,128)(2,1)S(1)}, bf16[2,192,256]{2,1,0:T(8,128)(2,1)S(1)}, u32[]{:S(2)}, u32[]{:S(2)}) collective-permute-start(bf16[2,192,256]{2,1,0:T(8,128)(2,1)S(1)} %get-tuple-element.70), channel_id=1, source_target_pairs={{0,1},{1,0},{2,3},{3,2},{4,5},{5,4},{6,7},{7,6},{8,9},{9,8},{10,11... | collective-permute-start | bytes 589832 | tf_op jit(solution)/shard_map/ppermute | solution.py:43
  23.6 5.3 %collective-permute-start.5 = (bf16[2,192,256]{2,1,0:T(8,128)(2,1)S(1)}, bf16[2,192,256]{2,1,0:T(8,128)(2,1)S(1)}, u32[]{:S(2)}, u32[]{:S(2)}) collective-permute-start(bf16[2,192,256]{2,1,0:T(8,128)(2,1)S(1)} %get-tuple-element.69), channel_id=1, source_target_pairs={{0,4},{1,2},{2,1},{3,7},{4,0},{5,6},{6,5},{7,3},{8,12},{9,10},{10,... | collective-permute-start | bytes 589832 | tf_op jit(solution)/shard_map/ppermute | solution.py:43
  30.0 6.6 %collective-permute-start.6 = (bf16[6,2,64,128]{3,2,1,0:T(8,128)(2,1)S(1)}, bf16[6,2,64,128]{3,2,1,0:T(8,128)(2,1)S(1)}, u32[]{:S(2)}, u32[]{:S(2)}) collective-permute-start(bf16[6,2,64,128]{3,2,1,0:T(8,128)(2,1)S(1)} %second_level_early.1), channel_id=1, source_target_pairs={{0,8},{8,0},{4,12},{12,4},{16,24},{24,16},{20,28},{28,20},{1,9},{9... | collective-permute-start | bytes 589832 | tf_op jit(solution)/shard_map/ppermute | solution.py:54
  36.6 8.5 %collective-permute-start.7 = (bf16[10,2,64,128]{3,2,1,0:T(8,128)(2,1)S(1)}, bf16[10,2,64,128]{3,2,1,0:T(8,128)(2,1)S(1)}, u32[]{:S(2)}, u32[]{:S(2)}) collective-permute-start(bf16[10,2,64,128]{3,2,1,0:T(8,128)(2,1)S(1)} %get-tuple-element.53), channel_id=1, source_target_pairs={{0,8},{8,0},{4,12},{12,4},{16,24},{24,16},{20,28},{28,20},{1,9},{9... | collective-permute-start | bytes 983048 | tf_op jit(solution)/shard_map/ppermute | solution.py:54
  38.8 6.2 %collective-permute-start.8 = (bf16[2,2,64,128]{3,2,1,0:T(8,128)(2,1)S(1)}, bf16[2,2,64,128]{3,2,1,0:T(8,128)(2,1)S(1)}, u32[]{:S(2)}, u32[]{:S(2)}) collective-permute-start(bf16[2,2,64,128]{3,2,1,0:T(8,128)(2,1)S(1)} %get-tuple-element.58), channel_id=1, source_target_pairs={{0,3},{1,2},{2,1},{3,0},{4,7},{5,6},{6,5},{7,4},{8,11},{9,10},{10,... | collective-permute-start | bytes 196616 | tf_op jit(solution)/shard_map/ppermute | solution.py:430
  41.2 13.9 %collective-permute-start.12 = (bf16[4,2,64,128]{3,2,1,0:T(8,128)(2,1)S(1)}, bf16[4,2,64,128]{3,2,1,0:T(8,128)(2,1)S(1)}, u32[]{:S(2)}, u32[]{:S(2)}) collective-permute-start(bf16[4,2,64,128]{3,2,1,0:T(8,128)(2,1)S(1)} %get-tuple-element.66), channel_id=1, source_target_pairs={{0,2},{1,3},{2,0},{3,1},{4,6},{5,7},{6,4},{7,5},{8,10},{9,11},{10,... | collective-permute-start | bytes 393224 | tf_op jit(solution)/shard_map/ppermute | solution.py:430
  45.9 17.9 %collective-permute-start.9 = (bf16[6,2,64,128]{3,2,1,0:T(8,128)(2,1)S(1)}, bf16[6,2,64,128]{3,2,1,0:T(8,128)(2,1)S(1)}, u32[]{:S(2)}, u32[]{:S(2)}) collective-permute-start(bf16[6,2,64,128]{3,2,1,0:T(8,128)(2,1)S(1)} %get-tuple-element.62), channel_id=1, source_target_pairs={{0,3},{1,2},{2,1},{3,0},{4,7},{5,6},{6,5},{7,4},{8,11},{9,10},{10,... | collective-permute-start | bytes 589832 | tf_op jit(solution)/shard_map/ppermute | solution.py:430
  48.2 15.5 %collective-permute-start.10 = (bf16[5,2,64,128]{3,2,1,0:T(8,128)(2,1)S(1)}, bf16[5,2,64,128]{3,2,1,0:T(8,128)(2,1)S(1)}, u32[]{:S(2)}, u32[]{:S(2)}) collective-permute-start(bf16[5,2,64,128]{3,2,1,0:T(8,128)(2,1)S(1)} %get-tuple-element.63), channel_id=1, source_target_pairs={{0,1},{1,0},{2,3},{3,2},{4,5},{5,4},{6,7},{7,6},{8,9},{9,8},{10,11... | collective-permute-start | bytes 491528 | tf_op jit(solution)/shard_map/ppermute | solution.py:430
  55.7 8.0 %collective-permute-start.13 = (bf16[4,2,64,128]{3,2,1,0:T(8,128)(2,1)S(1)}, bf16[4,2,64,128]{3,2,1,0:T(8,128)(2,1)S(1)}, u32[]{:S(2)}, u32[]{:S(2)}) collective-permute-start(bf16[4,2,64,128]{3,2,1,0:T(8,128)(2,1)S(1)} %late_wires.3), channel_id=1, source_target_pairs={{0,2},{1,3},{2,0},{3,1},{4,6},{5,7},{6,4},{7,5},{8,10},{9,11},{10,... | collective-permute-start | bytes 393224 | tf_op jit(solution)/shard_map/ppermute | solution.py:430
  55.8 4.9 %collective-permute-start.11 = (bf16[3,2,64,128]{3,2,1,0:T(8,128)(2,1)S(1)}, bf16[3,2,64,128]{3,2,1,0:T(8,128)(2,1)S(1)}, u32[]{:S(2)}, u32[]{:S(2)}) collective-permute-start(bf16[3,2,64,128]{3,2,1,0:T(8,128)(2,1)S(1)} %get-tuple-element.64), channel_id=1, source_target_pairs={{0,1},{1,0},{2,3},{3,2},{4,5},{5,4},{6,7},{7,6},{8,9},{9,8},{10,11... | collective-permute-start | bytes 294920 | tf_op jit(solution)/shard_map/ppermute | solution.py:430

commit v8 on v6

--- a/solution.py
+++ b/solution.py
@@ -11,6 +11,7 @@
 NW = 10
 REACH = 2
 OS = 64
+COPIES = 4
 MARGIN_BLOCKS = (NW - 2) // 2 + REACH
 VMEM_LIMIT = 8 * 1024 * 1024
 MOST_VMEM = 53 * 1024 * 1024
@@ -58,35 +59,52 @@
     return jnp.dot(left, right, preferred_element_type=jnp.float32)
 
 
-def resample_kernel(child_hbm, kernel_hbm, first_ref, second_ref, child, kernel, own, sems):
+def resample_kernel(
+    child_hbm, kernel_hbm, first_ref, second_ref, child, kernel, own, child_sems, kernel_sems
+):
     aper, beam = lax.axis_index("aperture"), lax.axis_index("beam")
     half, quarter = aper & 1, (aper >> 1) & 1
     even = 1 - (beam & 1)
     rows, rng = child.shape[1:]
     piece = rng // 4
-    child_copy = pltpu.make_async_copy(child_hbm, child, sems.at[4])
+    child_copies = []
+    for part in range(2):
+        for block in range(COPIES):
+            taken = pl.ds(block * (rows // COPIES), rows // COPIES)
+            child_copies.append(
+                pltpu.make_async_copy(
+                    child_hbm.at[part, taken, :],
+                    child.at[part, taken, :],
+                    child_sems.at[part, block],
+                )
+            )
     copies = []
     for place in range(4):
         source = (half ^ (place // 2)) * 2 + (quarter ^ (place % 2))
-        copies.append(
-            pltpu.make_async_copy(
-                kernel_hbm.at[:, :, pl.ds(pl.multiple_of(source * piece, 128), piece)],
-                kernel.at[:, :, place * piece : (place + 1) * piece],
-                sems.at[place],
-            )
-        )
-    child_copy.start()
-    for copy in copies:
+        columns = pl.ds(pl.multiple_of(source * piece, 128), piece)
+        copies.append([])
+        for part in range(2):
+            for block in range(2):
+                taken = pl.ds(block * (rng // 2), rng // 2)
+                copies[place].append(
+                    pltpu.make_async_copy(
+                        kernel_hbm.at[part, taken, columns],
+                        kernel.at[part, taken, place * piece : (place + 1) * piece],
+                        kernel_sems.at[place, part, block],
+                    )
+                )
+    for copy in child_copies + copies[0] + copies[1] + copies[2] + copies[3]:
         copy.start()
-    child_copy.wait()
+    for copy in child_copies:
+        copy.wait()
     real, imag = child[0], child[1]
     margin = first_ref.shape[1]
     tail = pl.ds(pl.multiple_of(even * (rows - margin), BLK), margin)
     head = pl.ds(pl.multiple_of((1 - even) * (rows - margin), BLK), margin)
     for side in range(2):
         columns = slice(side * 2 * piece, (side + 1) * 2 * piece)
-        copies[2 * side].wait()
-        copies[2 * side + 1].wait()
+        for copy in copies[2 * side] + copies[2 * side + 1]:
+            copy.wait()
         k_real, k_imag = kernel[0, :, columns], kernel[1, :, columns]
         own[0, :, columns] = (dot(real, k_real) - dot(imag, k_imag)).astype(jnp.bfloat16)
         own[1, :, columns] = (dot(real, k_imag) + dot(imag, k_real)).astype(jnp.bfloat16)
@@ -107,7 +125,8 @@
             pltpu.VMEM(child.shape, jnp.bfloat16),
             pltpu.VMEM(kernel.shape, jnp.bfloat16),
             pltpu.VMEM(child.shape, jnp.bfloat16),
-            pltpu.SemaphoreType.DMA((5,)),
+            pltpu.SemaphoreType.DMA((2, COPIES)),
+            pltpu.SemaphoreType.DMA((4, 2, 2)),
         ],
         compiler_params=params(MOST_VMEM),
         cost_estimate=cost(4 * rows * rng * rng, 2**21),
@@ -379,12 +398,13 @@
     out_ref = refs[-2]
     copies = []
     for number, (distance, low, high) in enumerate(spans):
-        start = (me_ref[0] ^ distance) * capacity + low
-        copies.append(
-            pltpu.make_async_copy(
-                refs[number], out_ref.at[pl.ds(start, high - low)], sems.at[number]
+        start = (me_ref[0] ^ distance) * capacity
+        for slot in range(low, high):
+            copies.append(
+                pltpu.make_async_copy(
+                    refs[number].at[slot - low], out_ref.at[start + slot], sems.at[len(copies)]
+                )
             )
-        )
     for copy in copies:
         copy.start()
     for copy in copies:
@@ -398,7 +418,7 @@
         out_shape=jax.ShapeDtypeStruct(shape, jnp.bfloat16),
         in_specs=[SMEM] + [ANY] * len(received),
         out_specs=ANY,
-        scratch_shapes=[pltpu.SemaphoreType.DMA((len(received),))],
+        scratch_shapes=[pltpu.SemaphoreType.DMA((shape[0],))],
         compiler_params=params(),
         cost_estimate=cost(0, 2**21),
         name="collect",
@@ -445,7 +465,8 @@
     early_spans += [(distance, 0, longer) for distance in others]
     late_spans = [(distance, shorter, capacity) for distance in odd]
     for distance in range(1, beam_count // 2):
-        late_spans += [(distance, 0, capacity // 2), (distance, capacity // 2, capacity)]
+        cut = (5 * capacity + 4) // 8
+        late_spans += [(distance, 0, cut), (distance, cut, capacity)]
     late_spans.append((0, 0, capacity))
     last_spans = [(distance, longer, capacity) for distance in others]
 

time: 62.3 us -> 62.6 us (level)
  transfers between devices with their start and end apart: 14 -> 14, of which waited for: 8 -> 10; matrix products, arithmetic and copies ran while one was open for 5% -> 5% of each run, Pallas kernels for 11% -> 11%
where the time goes in v8:
time: 62.6 us; the launch traced here: 62.4 us
  waiting for transfers between devices  25.5 us (41%)
  starting transfers between devices  20.1 us (32%)
  Pallas kernels  13.3 us (21%)
  local copies, waits for them, and re-layouts  2.24 us (4%)
  other arithmetic  1.1 us (2%)
    ppermute x6, waiting for transfers between devices, spread(): received.append(lax.ppermute(wire, 'beam', route) if distance else wire)  13.8 us
    ppermute x6, starting transfers between devices, spread(): received.append(lax.ppermute(wire, 'beam', route) if distance else wire)  9.43 us
    ppermute x4, waiting for transfers between devices, trade_edges(): received.append(lax.ppermute(block, ('aperture', 'beam'), route))  6.63 us
    ppermute x4, starting transfers between devices, trade_edges(): received.append(lax.ppermute(block, ('aperture', 'beam'), route))  6.03 us
    ppermute x4, waiting for transfers between devices, partner(): return lax.ppermute(block, axis, route)  5.04 us
    ppermute x4, starting transfers between devices, partner(): return lax.ppermute(block, axis, route)  4.62 us
    pallas_call x1, Pallas kernels, resample(): pl.pallas_call(resample_kernel, out_shape=(shape, shape), in_specs=[ANY,...  2.73 us
    pallas_call x2, Pallas kernels, first_level(): pl.pallas_call(functools.partial(first_level_kernel, column, rows), out_s...  2.66 us
  transfers between devices with their start and end apart: 14, of which 10 were waited for; matrix products, arithmetic and copies ran while one was open for 5% of the time, Pallas kernels for 11%

profile of v8, /device:TPU:0, one launch (start us, length us, event | category | flops | bytes accessed | tf_op | source)
XLA Modules:
  0.0 62.4 jit_solution(5315897190405583949)
XLA Ops:
  0.0 0.0 copy-start
  0.0 0.0 copy-start.2
  0.0 0.0 copy-start.1
  0.0 2.7 %resample.1 = (bf16[2,192,512]{2,1,0:T(8,128)(2,1)S(1)}, bf16[2,192,512]{2,1,0:T(8,128)(2,1)S(1)}) custom-call(bf16[2,256,512]{2,1,0:T(8,128)(2,1)} %bitcast.20, bf16[2,512,512]{2,1,0:T(8,128)(2,1)} %bitcast.19), custom_call_target="tpu_custom_call" | custom-call | flops 536870912 | bytes 2097152 | tf_op jit(solution)/shard_map/resample/pallas_call | solution.py:119
  2.7 3.1 %collective-permute-start = (bf16[2,192,512]{2,1,0:T(8,128)(2,1)S(1)}, bf16[2,192,512]{2,1,0:T(8,128)(2,1)S(1)}, u32[]{:S(2)}, u32[]{:S(2)}) collective-permute-start(bf16[2,192,512]{2,1,0:T(8,128)(2,1)S(1)} %get-tuple-element.34.sent_first_ref), channel_id=1, source_target_pairs={{0,1},{1,0},{2,3},{3,2},{4,5},{5,4},{6,7},{7,6},{8,9},{9,8},{10,11... | collective-permute-start | bytes 1179656 | tf_op jit(solution)/shard_map/ppermute | solution.py:44
  5.8 0.0 collective-permute-start.1
  5.8 0.0 copy-done
  5.8 1.5 %collective-permute-start.2 = (s32[1,16,1]{1,2,0:T(1,128)S(1)}, s32[1,16,1]{1,2,0:T(1,128)S(1)}, u32[]{:S(2)}, u32[]{:S(2)}) collective-permute-start(s32[1,16,1]{1,2,0:T(1,128)S(1)} %copy-done), channel_id=1, source_target_pairs={{0,8},{8,0},{4,12},{12,4},{16,24},{24,16},{20,28},{28,20},{1,9},{9... | collective-permute-start | bytes 200 | tf_op jit(solution)/shard_map/ppermute | solution.py:55
  7.3 0.0 copy-done.2
  7.3 0.2 subtract_reduce_fusion.starts_ref
  7.5 0.1 pad_add_fusion.side_ref
  7.6 0.0 copy-done.1
  7.6 0.4 copy.8
  8.0 1.4 %collective-permute-done.2 = s32[1,16,1]{1,2,0:T(1,128)S(1)} collective-permute-done((s32[1,16,1]{1,2,0:T(1,128)S(1)}, s32[1,16,1]{1,2,0:T(1,128)S(1)}, u32[]{:S(2)}, u32[]{:S(2)}) %collective-permute-start.2) | collective-permute-done | bytes 96 | tf_op jit(solution)/shard_map/ppermute | solution.py:55
  9.4 1.6 %plan.1 = (s32[16]{0:T(128)S(1)}, s32[16]{0:T(128)S(1)}, s32[16]{0:T(128)S(1)}, s32[16]{0:T(128)S(1)}, s32[16]{0:T(128)S(1)}) custom-call(s32[1]{0:T(128)} %bitcast.me_ref, s32[16]{0:T(128)S(1)} %bitcast.17, s32[16]{0:T(128)S(1)} %bitcast.18), custom_call_target="tpu_custom_call" | custom-call | tf_op jit(solution)/shard_map/plan/pallas_call | solution.py:323
  11.0 4.0 %collective-permute-done.first_ref = bf16[2,192,512]{2,1,0:T(8,128)(2,1)S(1)} collective-permute-done((bf16[2,192,512]{2,1,0:T(8,128)(2,1)S(1)}, bf16[2,192,512]{2,1,0:T(8,128)(2,1)S(1)}, u32[]{:S(2)}, u32[]{:S(2)}) %collective-permute-start) | collective-permute-done | bytes 393248 | tf_op jit(solution)/shard_map/ppermute | solution.py:44
  15.0 0.0 collective-permute-done.1.second_ref
  15.0 1.3 %first_level.3 = bf16[2,512,256]{2,1,0:T(8,128)(2,1)S(1)} custom-call(s32[4]{0:T(128)S(1)} %subtract_reduce_fusion.starts_ref, s32[3]{0:T(128)S(1)} %pad_add_fusion.side_ref, bf16[2,192,512]{2,1,0:T(8,128)(2,1)S(1)} %get-tuple-element.34.sent_first_ref, bf16[2,192,512]{2,1,0:T(8,128)(2,1)S(1)} %get-tuple-element.35.sent_second_ref, ...), custom_call_target="tpu_custom_call" | custom-call | flops 335544320 | bytes 2097152 | tf_op jit(solution)/shard_map/first_level/pallas_call | solution.py:190
  16.3 0.1 collective-permute-start.3
  16.4 1.3 %first_level.2 = bf16[2,512,256]{2,1,0:T(8,128)(2,1)S(1)} custom-call(s32[4]{0:T(128)S(1)} %subtract_reduce_fusion.starts_ref, s32[3]{0:T(128)S(1)} %pad_add_fusion.side_ref, bf16[2,192,512]{2,1,0:T(8,128)(2,1)S(1)} %get-tuple-element.34.sent_first_ref, bf16[2,192,512]{2,1,0:T(8,128)(2,1)S(1)} %get-tuple-element.35.sent_second_ref, ...), custom_call_target="tpu_custom_call" | custom-call | flops 335544320 | bytes 2097152 | tf_op jit(solution)/shard_map/first_level/pallas_call | solution.py:190
  17.7 0.5 collective-permute-done.3
  18.3 0.1 add_convert_fusion.own_ref
  18.5 2.9 %collective-permute-start.4 = (bf16[2,192,256]{2,1,0:T(8,128)(2,1)S(1)}, bf16[2,192,256]{2,1,0:T(8,128)(2,1)S(1)}, u32[]{:S(2)}, u32[]{:S(2)}) collective-permute-start(bf16[2,192,256]{2,1,0:T(8,128)(2,1)S(1)} %get-tuple-element.64), channel_id=1, source_target_pairs={{0,1},{1,0},{2,3},{3,2},{4,5},{5,4},{6,7},{7,6},{8,9},{9,8},{10,11... | collective-permute-start | bytes 589832 | tf_op jit(solution)/shard_map/ppermute | solution.py:44
  21.4 0.0 collective-permute-start.5
  21.4 1.8 %copy.9 = bf16[1,8,2,128,320]{4,3,2,1,0:T(8,128)(2,1)S(1)} copy(bf16[1,8,2,128,320]{3,4,2,1,0:T(8,128)(2,1)} %param.11) | data formatting | bytes 2621440 | tf_op args[4]
  23.2 0.7 %fusion.1.starts_ref = s32[8]{0:T(128)S(1)} fusion(s32[8,8]{1,0:T(8,128)} %param.12, s32[]{:T(128)S(6)} %select_n.19, s32[]{:T(128)S(6)} %sub.25), kind=kLoop, calls=%fused_computation.6 | loop fusion | flops 8 | bytes 72 | tf_op jit(solution)/shard_map/sub | solution.py:492
  23.9 2.7 %collective-permute-done.4.first_ref = bf16[2,192,256]{2,1,0:T(8,128)(2,1)S(1)} collective-permute-done((bf16[2,192,256]{2,1,0:T(8,128)(2,1)S(1)}, bf16[2,192,256]{2,1,0:T(8,128)(2,1)S(1)}, u32[]{:S(2)}, u32[]{:S(2)}) %collective-permute-start.4) | collective-permute-done | bytes 196640 | tf_op jit(solution)/shard_map/ppermute | solution.py:44
  26.6 0.0 collective-permute-done.5.second_ref
  26.6 1.1 %second_level_early.1 = bf16[6,2,64,128]{3,2,1,0:T(8,128)(2,1)S(1)} custom-call(s32[8]{0:T(128)S(1)} %fusion.1.starts_ref, s32[3]{0:T(128)S(1)} %pad_add_fusion.side_ref, s32[16]{0:T(128)S(1)} %get-tuple-element.41.sector_ref, bf16[2,512,256]{2,1,0:T(8,128)(2,1)S(1)} %add_convert_fusion.own_ref, bf16[2,192,256]{2,1,0:T(8,128)(2,1)S(1)} %collective-permute-done.4.first_ref, ...), custom_call_target="tpu_custom_call" | custom-call | flops 125829120 | bytes 1048576 | tf_op jit(solution)/shard_map/second_level_early/pallas_call | solution.py:256
  27.7 1.6 %collective-permute-start.6 = (bf16[6,2,64,128]{3,2,1,0:T(8,128)(2,1)S(1)}, bf16[6,2,64,128]{3,2,1,0:T(8,128)(2,1)S(1)}, u32[]{:S(2)}, u32[]{:S(2)}) collective-permute-start(bf16[6,2,64,128]{3,2,1,0:T(8,128)(2,1)S(1)} %second_level_early.1), channel_id=1, source_target_pairs={{0,8},{8,0},{4,12},{12,4},{16,24},{24,16},{20,28},{28,20},{1,9},{9... | collective-permute-start | bytes 589832 | tf_op jit(solution)/shard_map/ppermute | solution.py:55
  29.3 1.9 %second_level.1 = (bf16[16,2,64,128]{3,2,1,0:T(8,128)(2,1)S(1)}, bf16[10,2,64,128]{3,2,1,0:T(8,128)(2,1)S(1)}) custom-call(s32[8]{0:T(128)S(1)} %fusion.1.starts_ref, s32[3]{0:T(128)S(1)} %pad_add_fusion.side_ref, s32[16]{0:T(128)S(1)} %get-tuple-element.44.own_at_ref, s32[16]{0:T(128)S(1)} %get-tuple-element.45.other_at_ref, ...), custom_call_target="tpu_custom_call" | custom-call | flops 671088640 | bytes 4194304 | tf_op jit(solution)/shard_map/second_level/pallas_call | solution.py:267
  31.2 3.0 %collective-permute-done.6.refs_0_ = bf16[6,2,64,128]{3,2,1,0:T(8,128)(2,1)S(1)} collective-permute-done((bf16[6,2,64,128]{3,2,1,0:T(8,128)(2,1)S(1)}, bf16[6,2,64,128]{3,2,1,0:T(8,128)(2,1)S(1)}, u32[]{:S(2)}, u32[]{:S(2)}) %collective-permute-start.6) | collective-permute-done | bytes 196640 | tf_op jit(solution)/shard_map/ppermute | solution.py:55
  34.2 1.5 %collective-permute-start.7 = (bf16[10,2,64,128]{3,2,1,0:T(8,128)(2,1)S(1)}, bf16[10,2,64,128]{3,2,1,0:T(8,128)(2,1)S(1)}, u32[]{:S(2)}, u32[]{:S(2)}) collective-permute-start(bf16[10,2,64,128]{3,2,1,0:T(8,128)(2,1)S(1)} %get-tuple-element.47), channel_id=1, source_target_pairs={{0,8},{8,0},{4,12},{12,4},{16,24},{24,16},{20,28},{28,20},{1,9},{9... | collective-permute-start | bytes 983048 | tf_op jit(solution)/shard_map/ppermute | solution.py:55
  35.7 0.6 early_wires.1
  36.3 2.4 %collective-permute-start.8 = (bf16[2,2,64,128]{3,2,1,0:T(8,128)(2,1)S(1)}, bf16[2,2,64,128]{3,2,1,0:T(8,128)(2,1)S(1)}, u32[]{:S(2)}, u32[]{:S(2)}) collective-permute-start(bf16[2,2,64,128]{3,2,1,0:T(8,128)(2,1)S(1)} %get-tuple-element.52), channel_id=1, source_target_pairs={{0,3},{1,2},{2,1},{3,0},{4,7},{5,6},{6,5},{7,4},{8,11},{9,10},{10,... | collective-permute-start | bytes 196616 | tf_op jit(solution)/shard_map/ppermute | solution.py:433
  38.7 0.6 collective-permute-start.12
  39.3 3.1 %collective-permute-done.8.refs_0_ = bf16[2,2,64,128]{3,2,1,0:T(8,128)(2,1)S(1)} collective-permute-done((bf16[2,2,64,128]{3,2,1,0:T(8,128)(2,1)S(1)}, bf16[2,2,64,128]{3,2,1,0:T(8,128)(2,1)S(1)}, u32[]{:S(2)}, u32[]{:S(2)}) %collective-permute-start.8) | collective-permute-done | bytes 65568 | tf_op jit(solution)/shard_map/ppermute | solution.py:433
  42.5 0.1 collective-permute-done.7.refs_0_
  42.6 0.8 %late_wires.2 = (bf16[6,2,64,128]{3,2,1,0:T(8,128)(2,1)S(1)}, bf16[5,2,64,128]{3,2,1,0:T(8,128)(2,1)S(1)}, bf16[3,2,64,128]{3,2,1,0:T(8,128)(2,1)S(1)}, bf16[8,2,64,128]{3,2,1,0:T(8,128)(2,1)S(1)}) custom-call(s32[1]{0:T(128)} %bitcast.me_ref, s32[16]{0:T(128)S(1)} %get-tuple-element.48.target_ref, s32[16]{0:T(128)S(1)} %get-tuple-element.49.rank_ref, ...), custom_call_target="tpu_custom_call" | custom-call | bytes 2097152 | tf_op jit(solution)/shard_map/late_wires/pallas_call | solution.py:384
  43.3 2.4 %collective-permute-start.9 = (bf16[6,2,64,128]{3,2,1,0:T(8,128)(2,1)S(1)}, bf16[6,2,64,128]{3,2,1,0:T(8,128)(2,1)S(1)}, u32[]{:S(2)}, u32[]{:S(2)}) collective-permute-start(bf16[6,2,64,128]{3,2,1,0:T(8,128)(2,1)S(1)} %get-tuple-element.56), channel_id=1, source_target_pairs={{0,3},{1,2},{2,1},{3,0},{4,7},{5,6},{6,5},{7,4},{8,11},{9,10},{10,... | collective-permute-start | bytes 589832 | tf_op jit(solution)/shard_map/ppermute | solution.py:433
  45.7 1.7 %collective-permute-start.10 = (bf16[5,2,64,128]{3,2,1,0:T(8,128)(2,1)S(1)}, bf16[5,2,64,128]{3,2,1,0:T(8,128)(2,1)S(1)}, u32[]{:S(2)}, u32[]{:S(2)}) collective-permute-start(bf16[5,2,64,128]{3,2,1,0:T(8,128)(2,1)S(1)} %get-tuple-element.57), channel_id=1, source_target_pairs={{0,1},{1,0},{2,3},{3,2},{4,5},{5,4},{6,7},{7,6},{8,9},{9,8},{10,11... | collective-permute-start | bytes 491528 | tf_op jit(solution)/shard_map/ppermute | solution.py:433
  47.5 5.1 %collective-permute-done.12.refs_5_ = bf16[4,2,64,128]{3,2,1,0:T(8,128)(2,1)S(1)} collective-permute-done((bf16[4,2,64,128]{3,2,1,0:T(8,128)(2,1)S(1)}, bf16[4,2,64,128]{3,2,1,0:T(8,128)(2,1)S(1)}, u32[]{:S(2)}, u32[]{:S(2)}) %collective-permute-start.12) | collective-permute-done | bytes 131104 | tf_op jit(solution)/shard_map/ppermute | solution.py:433
  52.6 0.6 %late_wires.3 = bf16[4,2,64,128]{3,2,1,0:T(8,128)(2,1)S(1)} custom-call(s32[1]{0:T(128)} %bitcast.me_ref, s32[16]{0:T(128)S(1)} %get-tuple-element.48.target_ref, s32[16]{0:T(128)S(1)} %get-tuple-element.49.rank_ref, bf16[16,2,64,128]{3,2,1,0:T(8,128)(2,1)S(1)} %get-tuple-element.50.keep_ref, bf16[10,2,64,128]{3,2,1,0:T(8,128)(2,1)S(1)} %collective-permute-done.7.refs_0_, ...), custom_call_target="tpu_custom_call" | custom-call | bytes 2097152 | tf_op jit(solution)/shard_map/late_wires/pallas_call | solution.py:384
  53.3 0.1 collective-permute-start.13
  53.3 2.2 %collective-permute-start.11 = (bf16[3,2,64,128]{3,2,1,0:T(8,128)(2,1)S(1)}, bf16[3,2,64,128]{3,2,1,0:T(8,128)(2,1)S(1)}, u32[]{:S(2)}, u32[]{:S(2)}) collective-permute-start(bf16[3,2,64,128]{3,2,1,0:T(8,128)(2,1)S(1)} %get-tuple-element.58), channel_id=1, source_target_pairs={{0,1},{1,0},{2,3},{3,2},{4,5},{5,4},{6,7},{7,6},{8,9},{9,8},{10,11... | collective-permute-start | bytes 294920 | tf_op jit(solution)/shard_map/ppermute | solution.py:433
  55.6 2.7 %collective-permute-done.11.refs_3_ = bf16[3,2,64,128]{3,2,1,0:T(8,128)(2,1)S(1)} collective-permute-done((bf16[3,2,64,128]{3,2,1,0:T(8,128)(2,1)S(1)}, bf16[3,2,64,128]{3,2,1,0:T(8,128)(2,1)S(1)}, u32[]{:S(2)}, u32[]{:S(2)}) %collective-permute-start.11) | collective-permute-done | bytes 98336 | tf_op jit(solution)/shard_map/ppermute | solution.py:433
  58.2 2.9 %collective-permute-done.13.refs_6_ = bf16[4,2,64,128]{3,2,1,0:T(8,128)(2,1)S(1)} collective-permute-done((bf16[4,2,64,128]{3,2,1,0:T(8,128)(2,1)S(1)}, bf16[4,2,64,128]{3,2,1,0:T(8,128)(2,1)S(1)}, u32[]{:S(2)}, u32[]{:S(2)}) %collective-permute-start.13) | collective-permute-done | bytes 131104 | tf_op jit(solution)/shard_map/ppermute | solution.py:433
  61.1 0.0 collective-permute-done.10.refs_2_
  61.1 0.0 collective-permute-done.9.refs_1_
  61.1 1.2 %collect.1 = bf16[32,2,64,128]{3,2,1,0:T(8,128)(2,1)} custom-call(s32[1]{0:T(128)} %bitcast.me_ref, bf16[2,2,64,128]{3,2,1,0:T(8,128)(2,1)S(1)} %collective-permute-done.8.refs_0_, bf16[6,2,64,128]{3,2,1,0:T(8,128)(2,1)S(1)} %collective-permute-done.9.refs_1_, bf16[5,2,64,128]{3,2,1,0:T(8,128)(2,1)S(1)} %collective-permute-done.10.refs_2_, ...), custom_call_target="tpu_custom_call" | custom-call | bytes 2097152 | tf_op jit(solution)/shard_map/collect/pallas_call | solution.py:416
  (1 shorter events, 0.0 us)
Async XLA Ops:
  0.0 5.8 %copy-start = (s32[1,16,1]{1,2,0:T(1,128)S(1)}, s32[1,16,1]{1,2,0:T(1,128)}, u32[]{:S(2)}) copy-start(s32[1,16,1]{1,2,0:T(1,128)} %param.13) | copy-start | bytes 196
  0.0 7.3 %copy-start.2 = (s32[8,4]{0,1:T(4,128)S(1)}, s32[8,4]{0,1:T(4,128)}, u32[]{:S(2)}) copy-start(s32[8,4]{0,1:T(4,128)} %param.10) | copy-start | bytes 388
  0.0 7.6 %copy-start.1 = (bf16[1,4,2,128,320]{3,4,2,1,0:T(8,128)(2,1)S(1)}, bf16[1,4,2,128,320]{3,4,2,1,0:T(8,128)(2,1)}, u32[]{:S(2)}) copy-start(bf16[1,4,2,128,320]{3,4,2,1,0:T(8,128)(2,1)} %param.9) | copy-start | bytes 1966084
  2.7 12.2 %collective-permute-start = (bf16[2,192,512]{2,1,0:T(8,128)(2,1)S(1)}, bf16[2,192,512]{2,1,0:T(8,128)(2,1)S(1)}, u32[]{:S(2)}, u32[]{:S(2)}) collective-permute-start(bf16[2,192,512]{2,1,0:T(8,128)(2,1)S(1)} %get-tuple-element.34.sent_first_ref), channel_id=1, source_target_pairs={{0,1},{1,0},{2,3},{3,2},{4,5},{5,4},{6,7},{7,6},{8,9},{9,8},{10,11... | collective-permute-start | bytes 1179656 | tf_op jit(solution)/shard_map/ppermute | solution.py:44
  5.8 9.1 %collective-permute-start.1 = (bf16[2,192,512]{2,1,0:T(8,128)(2,1)S(1)}, bf16[2,192,512]{2,1,0:T(8,128)(2,1)S(1)}, u32[]{:S(2)}, u32[]{:S(2)}) collective-permute-start(bf16[2,192,512]{2,1,0:T(8,128)(2,1)S(1)} %get-tuple-element.35.sent_second_ref), channel_id=1, source_target_pairs={{0,4},{1,2},{2,1},{3,7},{4,0},{5,6},{6,5},{7,3},{8,12},{9,10},{10,... | collective-permute-start | bytes 1179656 | tf_op jit(solution)/shard_map/ppermute | solution.py:44
  5.8 3.5 %collective-permute-start.2 = (s32[1,16,1]{1,2,0:T(1,128)S(1)}, s32[1,16,1]{1,2,0:T(1,128)S(1)}, u32[]{:S(2)}, u32[]{:S(2)}) collective-permute-start(s32[1,16,1]{1,2,0:T(1,128)S(1)} %copy-done), channel_id=1, source_target_pairs={{0,8},{8,0},{4,12},{12,4},{16,24},{24,16},{20,28},{28,20},{1,9},{9... | collective-permute-start | bytes 200 | tf_op jit(solution)/shard_map/ppermute | solution.py:55
  16.3 2.0 %collective-permute-start.3 = (bf16[2,512,256]{2,1,0:T(8,128)(2,1)S(1)}, bf16[2,512,256]{2,1,0:T(8,128)(2,1)S(1)}, u32[]{:S(2)}, u32[]{:S(2)}) collective-permute-start(bf16[2,512,256]{2,1,0:T(8,128)(2,1)S(1)} %first_level.3), channel_id=1, source_target_pairs={{0,4},{4,0},{8,12},{12,8},{16,20},{20,16},{24,28},{28,24},{1,5},{5... | collective-permute-start | bytes 1572872 | tf_op jit(solution)/shard_map/ppermute | solution.py:55
  18.5 8.1 %collective-permute-start.4 = (bf16[2,192,256]{2,1,0:T(8,128)(2,1)S(1)}, bf16[2,192,256]{2,1,0:T(8,128)(2,1)S(1)}, u32[]{:S(2)}, u32[]{:S(2)}) collective-permute-start(bf16[2,192,256]{2,1,0:T(8,128)(2,1)S(1)} %get-tuple-element.64), channel_id=1, source_target_pairs={{0,1},{1,0},{2,3},{3,2},{4,5},{5,4},{6,7},{7,6},{8,9},{9,8},{10,11... | collective-permute-start | bytes 589832 | tf_op jit(solution)/shard_map/ppermute | solution.py:44
  21.4 5.2 %collective-permute-start.5 = (bf16[2,192,256]{2,1,0:T(8,128)(2,1)S(1)}, bf16[2,192,256]{2,1,0:T(8,128)(2,1)S(1)}, u32[]{:S(2)}, u32[]{:S(2)}) collective-permute-start(bf16[2,192,256]{2,1,0:T(8,128)(2,1)S(1)} %get-tuple-element.63), channel_id=1, source_target_pairs={{0,4},{1,2},{2,1},{3,7},{4,0},{5,6},{6,5},{7,3},{8,12},{9,10},{10,... | collective-permute-start | bytes 589832 | tf_op jit(solution)/shard_map/ppermute | solution.py:44
  27.7 6.5 %collective-permute-start.6 = (bf16[6,2,64,128]{3,2,1,0:T(8,128)(2,1)S(1)}, bf16[6,2,64,128]{3,2,1,0:T(8,128)(2,1)S(1)}, u32[]{:S(2)}, u32[]{:S(2)}) collective-permute-start(bf16[6,2,64,128]{3,2,1,0:T(8,128)(2,1)S(1)} %second_level_early.1), channel_id=1, source_target_pairs={{0,8},{8,0},{4,12},{12,4},{16,24},{24,16},{20,28},{28,20},{1,9},{9... | collective-permute-start | bytes 589832 | tf_op jit(solution)/shard_map/ppermute | solution.py:55
  34.2 8.3 %collective-permute-start.7 = (bf16[10,2,64,128]{3,2,1,0:T(8,128)(2,1)S(1)}, bf16[10,2,64,128]{3,2,1,0:T(8,128)(2,1)S(1)}, u32[]{:S(2)}, u32[]{:S(2)}) collective-permute-start(bf16[10,2,64,128]{3,2,1,0:T(8,128)(2,1)S(1)} %get-tuple-element.47), channel_id=1, source_target_pairs={{0,8},{8,0},{4,12},{12,4},{16,24},{24,16},{20,28},{28,20},{1,9},{9... | collective-permute-start | bytes 983048 | tf_op jit(solution)/shard_map/ppermute | solution.py:55
  36.3 6.1 %collective-permute-start.8 = (bf16[2,2,64,128]{3,2,1,0:T(8,128)(2,1)S(1)}, bf16[2,2,64,128]{3,2,1,0:T(8,128)(2,1)S(1)}, u32[]{:S(2)}, u32[]{:S(2)}) collective-permute-start(bf16[2,2,64,128]{3,2,1,0:T(8,128)(2,1)S(1)} %get-tuple-element.52), channel_id=1, source_target_pairs={{0,3},{1,2},{2,1},{3,0},{4,7},{5,6},{6,5},{7,4},{8,11},{9,10},{10,... | collective-permute-start | bytes 196616 | tf_op jit(solution)/shard_map/ppermute | solution.py:433
  38.7 13.9 %collective-permute-start.12 = (bf16[4,2,64,128]{3,2,1,0:T(8,128)(2,1)S(1)}, bf16[4,2,64,128]{3,2,1,0:T(8,128)(2,1)S(1)}, u32[]{:S(2)}, u32[]{:S(2)}) collective-permute-start(bf16[4,2,64,128]{3,2,1,0:T(8,128)(2,1)S(1)} %get-tuple-element.60), channel_id=1, source_target_pairs={{0,2},{1,3},{2,0},{3,1},{4,6},{5,7},{6,4},{7,5},{8,10},{9,11},{10,... | collective-permute-start | bytes 393224 | tf_op jit(solution)/shard_map/ppermute | solution.py:433
  43.3 17.8 %collective-permute-start.9 = (bf16[6,2,64,128]{3,2,1,0:T(8,128)(2,1)S(1)}, bf16[6,2,64,128]{3,2,1,0:T(8,128)(2,1)S(1)}, u32[]{:S(2)}, u32[]{:S(2)}) collective-permute-start(bf16[6,2,64,128]{3,2,1,0:T(8,128)(2,1)S(1)} %get-tuple-element.56), channel_id=1, source_target_pairs={{0,3},{1,2},{2,1},{3,0},{4,7},{5,6},{6,5},{7,4},{8,11},{9,10},{10,... | collective-permute-start | bytes 589832 | tf_op jit(solution)/shard_map/ppermute | solution.py:433
  45.7 15.4 %collective-permute-start.10 = (bf16[5,2,64,128]{3,2,1,0:T(8,128)(2,1)S(1)}, bf16[5,2,64,128]{3,2,1,0:T(8,128)(2,1)S(1)}, u32[]{:S(2)}, u32[]{:S(2)}) collective-permute-start(bf16[5,2,64,128]{3,2,1,0:T(8,128)(2,1)S(1)} %get-tuple-element.57), channel_id=1, source_target_pairs={{0,1},{1,0},{2,3},{3,2},{4,5},{5,4},{6,7},{7,6},{8,9},{9,8},{10,11... | collective-permute-start | bytes 491528 | tf_op jit(solution)/shard_map/ppermute | solution.py:433
  53.3 7.9 %collective-permute-start.13 = (bf16[4,2,64,128]{3,2,1,0:T(8,128)(2,1)S(1)}, bf16[4,2,64,128]{3,2,1,0:T(8,128)(2,1)S(1)}, u32[]{:S(2)}, u32[]{:S(2)}) collective-permute-start(bf16[4,2,64,128]{3,2,1,0:T(8,128)(2,1)S(1)} %late_wires.3), channel_id=1, source_target_pairs={{0,2},{1,3},{2,0},{3,1},{4,6},{5,7},{6,4},{7,5},{8,10},{9,11},{10,... | collective-permute-start | bytes 393224 | tf_op jit(solution)/shard_map/ppermute | solution.py:433
  53.3 4.9 %collective-permute-start.11 = (bf16[3,2,64,128]{3,2,1,0:T(8,128)(2,1)S(1)}, bf16[3,2,64,128]{3,2,1,0:T(8,128)(2,1)S(1)}, u32[]{:S(2)}, u32[]{:S(2)}) collective-permute-start(bf16[3,2,64,128]{3,2,1,0:T(8,128)(2,1)S(1)} %get-tuple-element.58), channel_id=1, source_target_pairs={{0,1},{1,0},{2,3},{3,2},{4,5},{5,4},{6,7},{7,6},{8,9},{9,8},{10,11... | collective-permute-start | bytes 294920 | tf_op jit(solution)/shard_map/ppermute | solution.py:433

commit v9 on v6

--- a/solution.py
+++ b/solution.py
@@ -444,9 +444,7 @@
     early_spans = [(distance, 0, shorter) for distance in odd]
     early_spans += [(distance, 0, longer) for distance in others]
     late_spans = [(distance, shorter, capacity) for distance in odd]
-    for distance in range(1, beam_count // 2):
-        late_spans += [(distance, 0, capacity // 2), (distance, capacity // 2, capacity)]
-    late_spans.append((0, 0, capacity))
+    near_spans = [(distance, 0, capacity) for distance in reversed(range(beam_count // 2))]
     last_spans = [(distance, longer, capacity) for distance in others]
 
     sent = resample(subimages[0], range_kernel[0], margin)
@@ -478,13 +476,15 @@
     summed, *group = wires(early_spans, me, target, rank, keep, other)
     received = spread(early_spans, group)
     from_odd, from_others = received[: len(odd)], received[len(odd) :]
+    near = wires(near_spans, me, target, rank, keep, late, summed)
     ready, from_odd = lax.optimization_barrier((late, from_odd))
+    from_near = spread(near_spans, near)
     group = wires(late_spans, me, target, rank, keep, ready, summed)
-    received = from_odd + spread(late_spans, group)
+    from_late = spread(late_spans, group)
     ready, from_others = lax.optimization_barrier((late, from_others))
     group = wires(last_spans, me, target, rank, keep, ready, summed)
-    received += from_others + spread(last_spans, group)
-    spans = early_spans[: len(odd)] + late_spans + early_spans[len(odd) :] + last_spans
+    received = from_odd + from_others + from_near + from_late + spread(last_spans, group)
+    spans = early_spans + near_spans + late_spans + last_spans
     return collect(spans, capacity, beam_count, me, received)[None]
 
 

time: 62.3 us -> 62.7 us (level)
  starting transfers between devices: 20.3 us -> 19.4 us
  waiting for transfers between devices: 25.7 us -> 26.4 us
    ppermute x4, waiting for transfers between devices: 4.95 us -> 7.28 us  [partner(): return lax.ppermute(block, axis, route)]
    ppermute x6 -> x5, waiting for transfers between devices: 14.1 us -> 12.4 us  [spread(): received.append(lax.ppermute(wire, 'beam', route) if distance else wire)]
    ppermute x6 -> x5, starting transfers between devices: 9.7 us -> 8.81 us  [spread(): received.append(lax.ppermute(wire, 'beam', route) if distance else wire)]
    pallas_call x3 -> x4, Pallas kernels: 2.04 us -> 2.64 us  [wires(): pl.pallas_call(functools.partial(wires_kernel, spans, summed is None), ou...]
  transfers between devices with their start and end apart: 14 -> 13, of which waited for: 8 -> 8; matrix products, arithmetic and copies ran while one was open for 5% -> 5% of each run, Pallas kernels for 11% -> 12%
where the time goes in v9:
time: 62.7 us; the launch traced here: 62.5 us
  waiting for transfers between devices  26.4 us (42%)
  starting transfers between devices  19.4 us (31%)
  Pallas kernels  13.3 us (21%)
  local copies, waits for them, and re-layouts  2.24 us (4%)
  other arithmetic  1.1 us (2%)
    ppermute x5, waiting for transfers between devices, spread(): received.append(lax.ppermute(wire, 'beam', route) if distance else wire)  12.4 us
    ppermute x5, starting transfers between devices, spread(): received.append(lax.ppermute(wire, 'beam', route) if distance else wire)  8.81 us
    ppermute x4, waiting for transfers between devices, partner(): return lax.ppermute(block, axis, route)  7.28 us
    ppermute x4, waiting for transfers between devices, trade_edges(): received.append(lax.ppermute(block, ('aperture', 'beam'), route))  6.63 us
    ppermute x4, starting transfers between devices, trade_edges(): received.append(lax.ppermute(block, ('aperture', 'beam'), route))  6.02 us
    ppermute x4, starting transfers between devices, partner(): return lax.ppermute(block, axis, route)  4.6 us
    pallas_call x2, Pallas kernels, first_level(): pl.pallas_call(functools.partial(first_level_kernel, column, rows), out_s...  2.67 us
    pallas_call x4, Pallas kernels, wires(): pl.pallas_call(functools.partial(wires_kernel, spans, summed is None), ou...  2.64 us
  transfers between devices with their start and end apart: 13, of which 8 were waited for; matrix products, arithmetic and copies ran while one was open for 5% of the time, Pallas kernels for 12%

profile of v9, /device:TPU:0, one launch (start us, length us, event | category | flops | bytes accessed | tf_op | source)
XLA Modules:
  0.0 62.5 jit_solution(1771060795074076884)
XLA Ops:
  0.0 0.0 copy-start
  0.0 0.0 copy-start.2
  0.0 0.0 copy-start.1
  0.0 2.3 %resample.1 = (bf16[2,192,512]{2,1,0:T(8,128)(2,1)S(1)}, bf16[2,192,512]{2,1,0:T(8,128)(2,1)S(1)}) custom-call(bf16[2,256,512]{2,1,0:T(8,128)(2,1)} %bitcast.20, bf16[2,512,512]{2,1,0:T(8,128)(2,1)} %bitcast.19), custom_call_target="tpu_custom_call" | custom-call | flops 536870912 | bytes 2097152 | tf_op jit(solution)/shard_map/resample/pallas_call | solution.py:101
  2.3 3.1 %collective-permute-start = (bf16[2,192,512]{2,1,0:T(8,128)(2,1)S(1)}, bf16[2,192,512]{2,1,0:T(8,128)(2,1)S(1)}, u32[]{:S(2)}, u32[]{:S(2)}) collective-permute-start(bf16[2,192,512]{2,1,0:T(8,128)(2,1)S(1)} %get-tuple-element.32.sent_first_ref), channel_id=1, source_target_pairs={{0,1},{1,0},{2,3},{3,2},{4,5},{5,4},{6,7},{7,6},{8,9},{9,8},{10,11... | collective-permute-start | bytes 1179656 | tf_op jit(solution)/shard_map/ppermute | solution.py:43
  5.4 0.0 collective-permute-start.1
  5.4 0.0 copy-done
  5.4 1.5 %collective-permute-start.2 = (s32[1,16,1]{1,2,0:T(1,128)S(1)}, s32[1,16,1]{1,2,0:T(1,128)S(1)}, u32[]{:S(2)}, u32[]{:S(2)}) collective-permute-start(s32[1,16,1]{1,2,0:T(1,128)S(1)} %copy-done), channel_id=1, source_target_pairs={{0,8},{8,0},{4,12},{12,4},{16,24},{24,16},{20,28},{28,20},{1,9},{9... | collective-permute-start | bytes 200 | tf_op jit(solution)/shard_map/ppermute | solution.py:54
  6.9 0.0 copy-done.2
  6.9 0.2 subtract_reduce_fusion.starts_ref
  7.1 0.1 pad_add_fusion.side_ref
  7.2 0.0 copy-done.1
  7.2 0.4 copy.8
  7.6 1.4 %collective-permute-done.2 = s32[1,16,1]{1,2,0:T(1,128)S(1)} collective-permute-done((s32[1,16,1]{1,2,0:T(1,128)S(1)}, s32[1,16,1]{1,2,0:T(1,128)S(1)}, u32[]{:S(2)}, u32[]{:S(2)}) %collective-permute-start.2) | collective-permute-done | bytes 96 | tf_op jit(solution)/shard_map/ppermute | solution.py:54
  9.0 1.6 %plan.1 = (s32[16]{0:T(128)S(1)}, s32[16]{0:T(128)S(1)}, s32[16]{0:T(128)S(1)}, s32[16]{0:T(128)S(1)}, s32[16]{0:T(128)S(1)}) custom-call(s32[1]{0:T(128)} %bitcast.me_ref, s32[16]{0:T(128)S(1)} %bitcast.17, s32[16]{0:T(128)S(1)} %bitcast.18), custom_call_target="tpu_custom_call" | custom-call | tf_op jit(solution)/shard_map/plan/pallas_call | solution.py:304
  10.6 4.0 %collective-permute-done.first_ref = bf16[2,192,512]{2,1,0:T(8,128)(2,1)S(1)} collective-permute-done((bf16[2,192,512]{2,1,0:T(8,128)(2,1)S(1)}, bf16[2,192,512]{2,1,0:T(8,128)(2,1)S(1)}, u32[]{:S(2)}, u32[]{:S(2)}) %collective-permute-start) | collective-permute-done | bytes 393248 | tf_op jit(solution)/shard_map/ppermute | solution.py:43
  14.5 0.0 collective-permute-done.1.second_ref
  14.5 1.3 %first_level.3 = bf16[2,512,256]{2,1,0:T(8,128)(2,1)S(1)} custom-call(s32[4]{0:T(128)S(1)} %subtract_reduce_fusion.starts_ref, s32[3]{0:T(128)S(1)} %pad_add_fusion.side_ref, bf16[2,192,512]{2,1,0:T(8,128)(2,1)S(1)} %get-tuple-element.32.sent_first_ref, bf16[2,192,512]{2,1,0:T(8,128)(2,1)S(1)} %get-tuple-element.33.sent_second_ref, ...), custom_call_target="tpu_custom_call" | custom-call | flops 335544320 | bytes 2097152 | tf_op jit(solution)/shard_map/first_level/pallas_call | solution.py:171
  15.9 0.1 collective-permute-start.3
  16.0 1.3 %first_level.2 = bf16[2,512,256]{2,1,0:T(8,128)(2,1)S(1)} custom-call(s32[4]{0:T(128)S(1)} %subtract_reduce_fusion.starts_ref, s32[3]{0:T(128)S(1)} %pad_add_fusion.side_ref, bf16[2,192,512]{2,1,0:T(8,128)(2,1)S(1)} %get-tuple-element.32.sent_first_ref, bf16[2,192,512]{2,1,0:T(8,128)(2,1)S(1)} %get-tuple-element.33.sent_second_ref, ...), custom_call_target="tpu_custom_call" | custom-call | flops 335544320 | bytes 2097152 | tf_op jit(solution)/shard_map/first_level/pallas_call | solution.py:171
  17.3 0.5 collective-permute-done.3
  17.8 0.1 add_convert_fusion.own_ref
  18.0 2.9 %collective-permute-start.4 = (bf16[2,192,256]{2,1,0:T(8,128)(2,1)S(1)}, bf16[2,192,256]{2,1,0:T(8,128)(2,1)S(1)}, u32[]{:S(2)}, u32[]{:S(2)}) collective-permute-start(bf16[2,192,256]{2,1,0:T(8,128)(2,1)S(1)} %get-tuple-element.60), channel_id=1, source_target_pairs={{0,1},{1,0},{2,3},{3,2},{4,5},{5,4},{6,7},{7,6},{8,9},{9,8},{10,11... | collective-permute-start | bytes 589832 | tf_op jit(solution)/shard_map/ppermute | solution.py:43
  21.0 0.0 collective-permute-start.5
  21.0 1.8 %copy.9 = bf16[1,8,2,128,320]{4,3,2,1,0:T(8,128)(2,1)S(1)} copy(bf16[1,8,2,128,320]{3,4,2,1,0:T(8,128)(2,1)} %param.11) | data formatting | bytes 2621440 | tf_op args[4]
  22.8 0.7 %fusion.1.starts_ref = s32[8]{0:T(128)S(1)} fusion(s32[8,8]{1,0:T(8,128)} %param.12, s32[]{:T(128)S(6)} %select_n.19, s32[]{:T(128)S(6)} %sub.25), kind=kLoop, calls=%fused_computation.6 | loop fusion | flops 8 | bytes 72 | tf_op jit(solution)/shard_map/sub | solution.py:469
  23.5 2.7 %collective-permute-done.4.first_ref = bf16[2,192,256]{2,1,0:T(8,128)(2,1)S(1)} collective-permute-done((bf16[2,192,256]{2,1,0:T(8,128)(2,1)S(1)}, bf16[2,192,256]{2,1,0:T(8,128)(2,1)S(1)}, u32[]{:S(2)}, u32[]{:S(2)}) %collective-permute-start.4) | collective-permute-done | bytes 196640 | tf_op jit(solution)/shard_map/ppermute | solution.py:43
  26.2 0.0 collective-permute-done.5.second_ref
  26.2 1.1 %second_level_early.1 = bf16[6,2,64,128]{3,2,1,0:T(8,128)(2,1)S(1)} custom-call(s32[8]{0:T(128)S(1)} %fusion.1.starts_ref, s32[3]{0:T(128)S(1)} %pad_add_fusion.side_ref, s32[16]{0:T(128)S(1)} %get-tuple-element.39.sector_ref, bf16[2,512,256]{2,1,0:T(8,128)(2,1)S(1)} %add_convert_fusion.own_ref, bf16[2,192,256]{2,1,0:T(8,128)(2,1)S(1)} %collective-permute-done.4.first_ref, ...), custom_call_target="tpu_custom_call" | custom-call | flops 125829120 | bytes 1048576 | tf_op jit(solution)/shard_map/second_level_early/pallas_call | solution.py:237
  27.3 1.5 %collective-permute-start.6 = (bf16[6,2,64,128]{3,2,1,0:T(8,128)(2,1)S(1)}, bf16[6,2,64,128]{3,2,1,0:T(8,128)(2,1)S(1)}, u32[]{:S(2)}, u32[]{:S(2)}) collective-permute-start(bf16[6,2,64,128]{3,2,1,0:T(8,128)(2,1)S(1)} %second_level_early.1), channel_id=1, source_target_pairs={{0,8},{8,0},{4,12},{12,4},{16,24},{24,16},{20,28},{28,20},{1,9},{9... | collective-permute-start | bytes 589832 | tf_op jit(solution)/shard_map/ppermute | solution.py:54
  28.8 1.9 %second_level.1 = (bf16[16,2,64,128]{3,2,1,0:T(8,128)(2,1)S(1)}, bf16[10,2,64,128]{3,2,1,0:T(8,128)(2,1)S(1)}) custom-call(s32[8]{0:T(128)S(1)} %fusion.1.starts_ref, s32[3]{0:T(128)S(1)} %pad_add_fusion.side_ref, s32[16]{0:T(128)S(1)} %get-tuple-element.42.own_at_ref, s32[16]{0:T(128)S(1)} %get-tuple-element.43.other_at_ref, ...), custom_call_target="tpu_custom_call" | custom-call | flops 671088640 | bytes 4194304 | tf_op jit(solution)/shard_map/second_level/pallas_call | solution.py:248
  30.8 3.0 %collective-permute-done.6.refs_0_ = bf16[6,2,64,128]{3,2,1,0:T(8,128)(2,1)S(1)} collective-permute-done((bf16[6,2,64,128]{3,2,1,0:T(8,128)(2,1)S(1)}, bf16[6,2,64,128]{3,2,1,0:T(8,128)(2,1)S(1)}, u32[]{:S(2)}, u32[]{:S(2)}) %collective-permute-start.6) | collective-permute-done | bytes 196640 | tf_op jit(solution)/shard_map/ppermute | solution.py:54
  33.8 1.5 %collective-permute-start.7 = (bf16[10,2,64,128]{3,2,1,0:T(8,128)(2,1)S(1)}, bf16[10,2,64,128]{3,2,1,0:T(8,128)(2,1)S(1)}, u32[]{:S(2)}, u32[]{:S(2)}) collective-permute-start(bf16[10,2,64,128]{3,2,1,0:T(8,128)(2,1)S(1)} %get-tuple-element.45), channel_id=1, source_target_pairs={{0,8},{8,0},{4,12},{12,4},{16,24},{24,16},{20,28},{28,20},{1,9},{9... | collective-permute-start | bytes 983048 | tf_op jit(solution)/shard_map/ppermute | solution.py:54
  35.3 0.6 early_wires.1
  35.9 2.6 %collective-permute-start.9 = (bf16[4,2,64,128]{3,2,1,0:T(8,128)(2,1)S(1)}, bf16[4,2,64,128]{3,2,1,0:T(8,128)(2,1)S(1)}, u32[]{:S(2)}, u32[]{:S(2)}) collective-permute-start(bf16[4,2,64,128]{3,2,1,0:T(8,128)(2,1)S(1)} %get-tuple-element.52), channel_id=1, source_target_pairs={{0,2},{1,3},{2,0},{3,1},{4,6},{5,7},{6,4},{7,5},{8,10},{9,11},{10,... | collective-permute-start | bytes 393224 | tf_op jit(solution)/shard_map/ppermute | solution.py:413
  38.5 1.3 %collective-permute-start.8 = (bf16[2,2,64,128]{3,2,1,0:T(8,128)(2,1)S(1)}, bf16[2,2,64,128]{3,2,1,0:T(8,128)(2,1)S(1)}, u32[]{:S(2)}, u32[]{:S(2)}) collective-permute-start(bf16[2,2,64,128]{3,2,1,0:T(8,128)(2,1)S(1)} %get-tuple-element.50), channel_id=1, source_target_pairs={{0,3},{1,2},{2,1},{3,0},{4,7},{5,6},{6,5},{7,4},{8,11},{9,10},{10,... | collective-permute-start | bytes 196616 | tf_op jit(solution)/shard_map/ppermute | solution.py:413
  39.8 2.3 %collective-permute-done.7.refs_0_ = bf16[10,2,64,128]{3,2,1,0:T(8,128)(2,1)S(1)} collective-permute-done((bf16[10,2,64,128]{3,2,1,0:T(8,128)(2,1)S(1)}, bf16[10,2,64,128]{3,2,1,0:T(8,128)(2,1)S(1)}, u32[]{:S(2)}, u32[]{:S(2)}) %collective-permute-start.7) | collective-permute-done | bytes 327712 | tf_op jit(solution)/shard_map/ppermute | solution.py:54
  42.1 0.7 %late_wires.3 = (bf16[8,2,64,128]{3,2,1,0:T(8,128)(2,1)S(1)}, bf16[8,2,64,128]{3,2,1,0:T(8,128)(2,1)S(1)}) custom-call(s32[1]{0:T(128)} %bitcast.me_ref, s32[16]{0:T(128)S(1)} %get-tuple-element.46.target_ref, s32[16]{0:T(128)S(1)} %get-tuple-element.47.rank_ref, bf16[16,2,64,128]{3,2,1,0:T(8,128)(2,1)S(1)} %get-tuple-element.48.keep_ref, ...), custom_call_target="tpu_custom_call" | custom-call | bytes 2097152 | tf_op jit(solution)/shard_map/late_wires/pallas_call | solution.py:365
  42.9 1.2 %collective-permute-start.10 = (bf16[8,2,64,128]{3,2,1,0:T(8,128)(2,1)S(1)}, bf16[8,2,64,128]{3,2,1,0:T(8,128)(2,1)S(1)}, u32[]{:S(2)}, u32[]{:S(2)}) collective-permute-start(bf16[8,2,64,128]{3,2,1,0:T(8,128)(2,1)S(1)} %get-tuple-element.55), channel_id=1, source_target_pairs={{0,1},{1,0},{2,3},{3,2},{4,5},{5,4},{6,7},{7,6},{8,9},{9,8},{10,11... | collective-permute-start | bytes 786440 | tf_op jit(solution)/shard_map/ppermute | solution.py:413
  44.1 0.7 %collective-permute-done.8.refs_0_ = bf16[2,2,64,128]{3,2,1,0:T(8,128)(2,1)S(1)} collective-permute-done((bf16[2,2,64,128]{3,2,1,0:T(8,128)(2,1)S(1)}, bf16[2,2,64,128]{3,2,1,0:T(8,128)(2,1)S(1)}, u32[]{:S(2)}, u32[]{:S(2)}) %collective-permute-start.8) | collective-permute-done | bytes 65568 | tf_op jit(solution)/shard_map/ppermute | solution.py:413
  44.8 0.7 %late_wires.4 = bf16[6,2,64,128]{3,2,1,0:T(8,128)(2,1)S(1)} custom-call(s32[1]{0:T(128)} %bitcast.me_ref, s32[16]{0:T(128)S(1)} %get-tuple-element.46.target_ref, s32[16]{0:T(128)S(1)} %get-tuple-element.47.rank_ref, bf16[16,2,64,128]{3,2,1,0:T(8,128)(2,1)S(1)} %get-tuple-element.48.keep_ref, bf16[10,2,64,128]{3,2,1,0:T(8,128)(2,1)S(1)} %collective-permute-done.7.refs_0_, ...), custom_call_target="tpu_custom_call" | custom-call | bytes 2097152 | tf_op jit(solution)/shard_map/late_wires/pallas_call | solution.py:365
  45.5 1.8 %collective-permute-start.11 = (bf16[6,2,64,128]{3,2,1,0:T(8,128)(2,1)S(1)}, bf16[6,2,64,128]{3,2,1,0:T(8,128)(2,1)S(1)}, u32[]{:S(2)}, u32[]{:S(2)}) collective-permute-start(bf16[6,2,64,128]{3,2,1,0:T(8,128)(2,1)S(1)} %late_wires.4), channel_id=1, source_target_pairs={{0,3},{1,2},{2,1},{3,0},{4,7},{5,6},{6,5},{7,4},{8,11},{9,10},{10,... | collective-permute-start | bytes 589832 | tf_op jit(solution)/shard_map/ppermute | solution.py:413
  47.3 0.0 collective-permute-done.9.refs_1_
  47.3 0.6 %late_wires.5 = bf16[4,2,64,128]{3,2,1,0:T(8,128)(2,1)S(1)} custom-call(s32[1]{0:T(128)} %bitcast.me_ref, s32[16]{0:T(128)S(1)} %get-tuple-element.46.target_ref, s32[16]{0:T(128)S(1)} %get-tuple-element.47.rank_ref, bf16[16,2,64,128]{3,2,1,0:T(8,128)(2,1)S(1)} %get-tuple-element.48.keep_ref, bf16[10,2,64,128]{3,2,1,0:T(8,128)(2,1)S(1)} %collective-permute-done.7.refs_0_, ...), custom_call_target="tpu_custom_call" | custom-call | bytes 2097152 | tf_op jit(solution)/shard_map/late_wires/pallas_call | solution.py:365
  48.0 1.9 %collective-permute-start.12 = (bf16[4,2,64,128]{3,2,1,0:T(8,128)(2,1)S(1)}, bf16[4,2,64,128]{3,2,1,0:T(8,128)(2,1)S(1)}, u32[]{:S(2)}, u32[]{:S(2)}) collective-permute-start(bf16[4,2,64,128]{3,2,1,0:T(8,128)(2,1)S(1)} %late_wires.5), channel_id=1, source_target_pairs={{0,2},{1,3},{2,0},{3,1},{4,6},{5,7},{6,4},{7,5},{8,10},{9,11},{10,... | collective-permute-start | bytes 393224 | tf_op jit(solution)/shard_map/ppermute | solution.py:413
  49.8 11.7 %collective-permute-done.12.refs_5_ = bf16[4,2,64,128]{3,2,1,0:T(8,128)(2,1)S(1)} collective-permute-done((bf16[4,2,64,128]{3,2,1,0:T(8,128)(2,1)S(1)}, bf16[4,2,64,128]{3,2,1,0:T(8,128)(2,1)S(1)}, u32[]{:S(2)}, u32[]{:S(2)}) %collective-permute-start.12) | collective-permute-done | bytes 131104 | tf_op jit(solution)/shard_map/ppermute | solution.py:413
  61.5 0.0 collective-permute-done.11.refs_4_
  61.5 0.0 collective-permute-done.10.refs_2_
  61.5 1.0 %collect.1 = bf16[32,2,64,128]{3,2,1,0:T(8,128)(2,1)} custom-call(s32[1]{0:T(128)} %bitcast.me_ref, bf16[2,2,64,128]{3,2,1,0:T(8,128)(2,1)S(1)} %collective-permute-done.8.refs_0_, bf16[4,2,64,128]{3,2,1,0:T(8,128)(2,1)S(1)} %collective-permute-done.9.refs_1_, bf16[8,2,64,128]{3,2,1,0:T(8,128)(2,1)S(1)} %collective-permute-done.10.refs_2_, ...), custom_call_target="tpu_custom_call" | custom-call | bytes 2097152 | tf_op jit(solution)/shard_map/collect/pallas_call | solution.py:396
  (1 shorter events, 0.0 us)
Async XLA Ops:
  0.0 5.4 %copy-start = (s32[1,16,1]{1,2,0:T(1,128)S(1)}, s32[1,16,1]{1,2,0:T(1,128)}, u32[]{:S(2)}) copy-start(s32[1,16,1]{1,2,0:T(1,128)} %param.13) | copy-start | bytes 196
  0.0 6.9 %copy-start.2 = (s32[8,4]{0,1:T(4,128)S(1)}, s32[8,4]{0,1:T(4,128)}, u32[]{:S(2)}) copy-start(s32[8,4]{0,1:T(4,128)} %param.10) | copy-start | bytes 388
  0.0 7.2 %copy-start.1 = (bf16[1,4,2,128,320]{3,4,2,1,0:T(8,128)(2,1)S(1)}, bf16[1,4,2,128,320]{3,4,2,1,0:T(8,128)(2,1)}, u32[]{:S(2)}) copy-start(bf16[1,4,2,128,320]{3,4,2,1,0:T(8,128)(2,1)} %param.9) | copy-start | bytes 1966084
  2.3 12.2 %collective-permute-start = (bf16[2,192,512]{2,1,0:T(8,128)(2,1)S(1)}, bf16[2,192,512]{2,1,0:T(8,128)(2,1)S(1)}, u32[]{:S(2)}, u32[]{:S(2)}) collective-permute-start(bf16[2,192,512]{2,1,0:T(8,128)(2,1)S(1)} %get-tuple-element.32.sent_first_ref), channel_id=1, source_target_pairs={{0,1},{1,0},{2,3},{3,2},{4,5},{5,4},{6,7},{7,6},{8,9},{9,8},{10,11... | collective-permute-start | bytes 1179656 | tf_op jit(solution)/shard_map/ppermute | solution.py:43
  5.4 9.1 %collective-permute-start.1 = (bf16[2,192,512]{2,1,0:T(8,128)(2,1)S(1)}, bf16[2,192,512]{2,1,0:T(8,128)(2,1)S(1)}, u32[]{:S(2)}, u32[]{:S(2)}) collective-permute-start(bf16[2,192,512]{2,1,0:T(8,128)(2,1)S(1)} %get-tuple-element.33.sent_second_ref), channel_id=1, source_target_pairs={{0,4},{1,2},{2,1},{3,7},{4,0},{5,6},{6,5},{7,3},{8,12},{9,10},{10,... | collective-permute-start | bytes 1179656 | tf_op jit(solution)/shard_map/ppermute | solution.py:43
  5.4 3.5 %collective-permute-start.2 = (s32[1,16,1]{1,2,0:T(1,128)S(1)}, s32[1,16,1]{1,2,0:T(1,128)S(1)}, u32[]{:S(2)}, u32[]{:S(2)}) collective-permute-start(s32[1,16,1]{1,2,0:T(1,128)S(1)} %copy-done), channel_id=1, source_target_pairs={{0,8},{8,0},{4,12},{12,4},{16,24},{24,16},{20,28},{28,20},{1,9},{9... | collective-permute-start | bytes 200 | tf_op jit(solution)/shard_map/ppermute | solution.py:54
  15.9 2.0 %collective-permute-start.3 = (bf16[2,512,256]{2,1,0:T(8,128)(2,1)S(1)}, bf16[2,512,256]{2,1,0:T(8,128)(2,1)S(1)}, u32[]{:S(2)}, u32[]{:S(2)}) collective-permute-start(bf16[2,512,256]{2,1,0:T(8,128)(2,1)S(1)} %first_level.3), channel_id=1, source_target_pairs={{0,4},{4,0},{8,12},{12,8},{16,20},{20,16},{24,28},{28,24},{1,5},{5... | collective-permute-start | bytes 1572872 | tf_op jit(solution)/shard_map/ppermute | solution.py:54
  18.0 8.1 %collective-permute-start.4 = (bf16[2,192,256]{2,1,0:T(8,128)(2,1)S(1)}, bf16[2,192,256]{2,1,0:T(8,128)(2,1)S(1)}, u32[]{:S(2)}, u32[]{:S(2)}) collective-permute-start(bf16[2,192,256]{2,1,0:T(8,128)(2,1)S(1)} %get-tuple-element.60), channel_id=1, source_target_pairs={{0,1},{1,0},{2,3},{3,2},{4,5},{5,4},{6,7},{7,6},{8,9},{9,8},{10,11... | collective-permute-start | bytes 589832 | tf_op jit(solution)/shard_map/ppermute | solution.py:43
  21.0 5.2 %collective-permute-start.5 = (bf16[2,192,256]{2,1,0:T(8,128)(2,1)S(1)}, bf16[2,192,256]{2,1,0:T(8,128)(2,1)S(1)}, u32[]{:S(2)}, u32[]{:S(2)}) collective-permute-start(bf16[2,192,256]{2,1,0:T(8,128)(2,1)S(1)} %get-tuple-element.59), channel_id=1, source_target_pairs={{0,4},{1,2},{2,1},{3,7},{4,0},{5,6},{6,5},{7,3},{8,12},{9,10},{10,... | collective-permute-start | bytes 589832 | tf_op jit(solution)/shard_map/ppermute | solution.py:43
  27.3 6.5 %collective-permute-start.6 = (bf16[6,2,64,128]{3,2,1,0:T(8,128)(2,1)S(1)}, bf16[6,2,64,128]{3,2,1,0:T(8,128)(2,1)S(1)}, u32[]{:S(2)}, u32[]{:S(2)}) collective-permute-start(bf16[6,2,64,128]{3,2,1,0:T(8,128)(2,1)S(1)} %second_level_early.1), channel_id=1, source_target_pairs={{0,8},{8,0},{4,12},{12,4},{16,24},{24,16},{20,28},{28,20},{1,9},{9... | collective-permute-start | bytes 589832 | tf_op jit(solution)/shard_map/ppermute | solution.py:54
  33.8 8.3 %collective-permute-start.7 = (bf16[10,2,64,128]{3,2,1,0:T(8,128)(2,1)S(1)}, bf16[10,2,64,128]{3,2,1,0:T(8,128)(2,1)S(1)}, u32[]{:S(2)}, u32[]{:S(2)}) collective-permute-start(bf16[10,2,64,128]{3,2,1,0:T(8,128)(2,1)S(1)} %get-tuple-element.45), channel_id=1, source_target_pairs={{0,8},{8,0},{4,12},{12,4},{16,24},{24,16},{20,28},{28,20},{1,9},{9... | collective-permute-start | bytes 983048 | tf_op jit(solution)/shard_map/ppermute | solution.py:54
  35.9 11.4 %collective-permute-start.9 = (bf16[4,2,64,128]{3,2,1,0:T(8,128)(2,1)S(1)}, bf16[4,2,64,128]{3,2,1,0:T(8,128)(2,1)S(1)}, u32[]{:S(2)}, u32[]{:S(2)}) collective-permute-start(bf16[4,2,64,128]{3,2,1,0:T(8,128)(2,1)S(1)} %get-tuple-element.52), channel_id=1, source_target_pairs={{0,2},{1,3},{2,0},{3,1},{4,6},{5,7},{6,4},{7,5},{8,10},{9,11},{10,... | collective-permute-start | bytes 393224 | tf_op jit(solution)/shard_map/ppermute | solution.py:413
  38.5 6.2 %collective-permute-start.8 = (bf16[2,2,64,128]{3,2,1,0:T(8,128)(2,1)S(1)}, bf16[2,2,64,128]{3,2,1,0:T(8,128)(2,1)S(1)}, u32[]{:S(2)}, u32[]{:S(2)}) collective-permute-start(bf16[2,2,64,128]{3,2,1,0:T(8,128)(2,1)S(1)} %get-tuple-element.50), channel_id=1, source_target_pairs={{0,3},{1,2},{2,1},{3,0},{4,7},{5,6},{6,5},{7,4},{8,11},{9,10},{10,... | collective-permute-start | bytes 196616 | tf_op jit(solution)/shard_map/ppermute | solution.py:413
  42.9 18.7 %collective-permute-start.10 = (bf16[8,2,64,128]{3,2,1,0:T(8,128)(2,1)S(1)}, bf16[8,2,64,128]{3,2,1,0:T(8,128)(2,1)S(1)}, u32[]{:S(2)}, u32[]{:S(2)}) collective-permute-start(bf16[8,2,64,128]{3,2,1,0:T(8,128)(2,1)S(1)} %get-tuple-element.55), channel_id=1, source_target_pairs={{0,1},{1,0},{2,3},{3,2},{4,5},{5,4},{6,7},{7,6},{8,9},{9,8},{10,11... | collective-permute-start | bytes 786440 | tf_op jit(solution)/shard_map/ppermute | solution.py:413
  45.5 16.1 %collective-permute-start.11 = (bf16[6,2,64,128]{3,2,1,0:T(8,128)(2,1)S(1)}, bf16[6,2,64,128]{3,2,1,0:T(8,128)(2,1)S(1)}, u32[]{:S(2)}, u32[]{:S(2)}) collective-permute-start(bf16[6,2,64,128]{3,2,1,0:T(8,128)(2,1)S(1)} %late_wires.4), channel_id=1, source_target_pairs={{0,3},{1,2},{2,1},{3,0},{4,7},{5,6},{6,5},{7,4},{8,11},{9,10},{10,... | collective-permute-start | bytes 589832 | tf_op jit(solution)/shard_map/ppermute | solution.py:413
  48.0 13.6 %collective-permute-start.12 = (bf16[4,2,64,128]{3,2,1,0:T(8,128)(2,1)S(1)}, bf16[4,2,64,128]{3,2,1,0:T(8,128)(2,1)S(1)}, u32[]{:S(2)}, u32[]{:S(2)}) collective-permute-start(bf16[4,2,64,128]{3,2,1,0:T(8,128)(2,1)S(1)} %late_wires.5), channel_id=1, source_target_pairs={{0,2},{1,3},{2,0},{3,1},{4,6},{5,7},{6,4},{7,5},{8,10},{9,11},{10,... | collective-permute-start | bytes 393224 | tf_op jit(solution)/shard_map/ppermute | solution.py:413

commit v10 on v6

--- a/solution.py
+++ b/solution.py
@@ -34,11 +34,11 @@
         route = []
         for aper in range(apertures):
             for place in range(count):
-                other = place + 1 if (place - order) % 2 == 0 else place - 1
+                other = place + 1 if (place - order - aper) % 2 == 0 else place - 1
                 if 0 <= other < count:
                     to = aper * count + other
                 else:
-                    to = min(aper ^ 1, apertures - 1) * count + place
+                    to = (aper ^ 2 if aper ^ 2 < apertures else aper) * count + place
                 route.append((aper * count + place, to))
         received.append(lax.ppermute(block, ("aperture", "beam"), route))
     return received
@@ -61,7 +61,7 @@
 def resample_kernel(child_hbm, kernel_hbm, first_ref, second_ref, child, kernel, own, sems):
     aper, beam = lax.axis_index("aperture"), lax.axis_index("beam")
     half, quarter = aper & 1, (aper >> 1) & 1
-    even = 1 - (beam & 1)
+    even = 1 - ((aper + beam) & 1)
     rows, rng = child.shape[1:]
     piece = rng // 4
     child_copy = pltpu.make_async_copy(child_hbm, child, sems.at[4])
@@ -429,7 +429,7 @@
     margin = MARGIN_BLOCKS * BLK
     rows = subimages.shape[2]
     local_blocks = rows // BLK
-    even = (beam_index + 1) % 2
+    even = (aper_index + beam_index + 1) % 2
     ends = (beam_index == 0, beam_index == beam_count - 1)
     side = jnp.stack([even] + [end.astype(jnp.int32) for end in ends])
     me = beam_index.reshape(1)

time: 62.3 us -> 64.3 us (1.032)
  waiting for transfers between devices: 25.7 us -> 27.5 us
    ppermute x4, waiting for transfers between devices: 4.95 us -> 10.7 us  [partner(): return lax.ppermute(block, axis, route)]
    ppermute x4, waiting for transfers between devices: 6.63 us -> 2.09 us  [trade_edges(): received.append(lax.ppermute(block, ('aperture', 'beam'), route))]
    ppermute x4, starting transfers between devices: 4.61 us -> 2.79 us  [partner(): return lax.ppermute(block, axis, route)]
    ppermute x4, starting transfers between devices: 6.01 us -> 7.23 us  [trade_edges(): received.append(lax.ppermute(block, ('aperture', 'beam'), route))]
    ppermute x6, starting transfers between devices: 9.7 us -> 10.4 us  [spread(): received.append(lax.ppermute(wire, 'beam', route) if distance else wire)]
    ppermute x6, waiting for transfers between devices: 14.1 us -> 14.7 us  [spread(): received.append(lax.ppermute(wire, 'beam', route) if distance else wire)]
  transfers between devices with their start and end apart: 14 -> 14, of which waited for: 8 -> 6; matrix products, arithmetic and copies ran while one was open for 5% -> 5% of each run, Pallas kernels for 11% -> 11%
where the time goes in v10:
time: 64.3 us; the launch traced here: 64.1 us
  waiting for transfers between devices  27.5 us (43%)
  starting transfers between devices  20.4 us (32%)
  Pallas kernels  12.7 us (20%)
  local copies, waits for them, and re-layouts  2.24 us (3%)
  other arithmetic  1.1 us (2%)
    ppermute x6, waiting for transfers between devices, spread(): received.append(lax.ppermute(wire, 'beam', route) if distance else wire)  14.7 us
    ppermute x4, waiting for transfers between devices, partner(): return lax.ppermute(block, axis, route)  10.7 us
    ppermute x6, starting transfers between devices, spread(): received.append(lax.ppermute(wire, 'beam', route) if distance else wire)  10.4 us
    ppermute x4, starting transfers between devices, trade_edges(): received.append(lax.ppermute(block, ('aperture', 'beam'), route))  7.23 us
    ppermute x4, starting transfers between devices, partner(): return lax.ppermute(block, axis, route)  2.79 us
    pallas_call x2, Pallas kernels, first_level(): pl.pallas_call(functools.partial(first_level_kernel, column, rows), out_s...  2.67 us
    pallas_call x1, Pallas kernels, resample(): pl.pallas_call(resample_kernel, out_shape=(shape, shape), in_specs=[ANY,...  2.31 us
    unnamed x8, local copies, waits for them, and re-layouts  2.2 us
  transfers between devices with their start and end apart: 14, of which 6 were waited for; matrix products, arithmetic and copies ran while one was open for 5% of the time, Pallas kernels for 11%

profile of v10, /device:TPU:0, one launch (start us, length us, event | category | flops | bytes accessed | tf_op | source)
XLA Modules:
  0.0 64.1 jit_solution(5815799229399019443)
XLA Ops:
  0.0 0.0 copy-start
  0.0 0.0 copy-start.2
  0.0 0.0 copy-start.1
  0.0 2.3 %resample.1 = (bf16[2,192,512]{2,1,0:T(8,128)(2,1)S(1)}, bf16[2,192,512]{2,1,0:T(8,128)(2,1)S(1)}) custom-call(bf16[2,256,512]{2,1,0:T(8,128)(2,1)} %bitcast.20, bf16[2,512,512]{2,1,0:T(8,128)(2,1)} %bitcast.19), custom_call_target="tpu_custom_call" | custom-call | flops 536870912 | bytes 2097152 | tf_op jit(solution)/shard_map/resample/pallas_call | solution.py:101
  2.3 3.1 %collective-permute-start = (bf16[2,192,512]{2,1,0:T(8,128)(2,1)S(1)}, bf16[2,192,512]{2,1,0:T(8,128)(2,1)S(1)}, u32[]{:S(2)}, u32[]{:S(2)}) collective-permute-start(bf16[2,192,512]{2,1,0:T(8,128)(2,1)S(1)} %get-tuple-element.34.sent_first_ref), channel_id=1, source_target_pairs={{0,1},{1,0},{2,3},{3,2},{4,12},{5,6},{6,5},{7,15},{8,9},{9,8},{10,... | collective-permute-start | bytes 1179656 | tf_op jit(solution)/shard_map/ppermute | solution.py:43
  5.4 1.5 %collective-permute-start.1 = (bf16[2,192,512]{2,1,0:T(8,128)(2,1)S(1)}, bf16[2,192,512]{2,1,0:T(8,128)(2,1)S(1)}, u32[]{:S(2)}, u32[]{:S(2)}) collective-permute-start(bf16[2,192,512]{2,1,0:T(8,128)(2,1)S(1)} %get-tuple-element.35.sent_second_ref), channel_id=1, source_target_pairs={{0,8},{1,2},{2,1},{3,11},{4,5},{5,4},{6,7},{7,6},{8,0},{9,10},{10,... | collective-permute-start | bytes 1179656 | tf_op jit(solution)/shard_map/ppermute | solution.py:43
  6.9 0.0 copy-done
  6.9 0.5 collective-permute-start.2
  7.4 0.0 copy-done.2
  7.4 0.2 subtract_reduce_fusion.starts_ref
  7.6 0.1 pad_add_fusion.side_ref
  7.7 0.0 copy-done.1
  7.7 0.4 copy.8
  8.1 6.4 %collective-permute-done.2 = s32[1,16,1]{1,2,0:T(1,128)S(1)} collective-permute-done((s32[1,16,1]{1,2,0:T(1,128)S(1)}, s32[1,16,1]{1,2,0:T(1,128)S(1)}, u32[]{:S(2)}, u32[]{:S(2)}) %collective-permute-start.2) | collective-permute-done | bytes 96 | tf_op jit(solution)/shard_map/ppermute | solution.py:54
  14.5 1.6 %plan.1 = (s32[16]{0:T(128)S(1)}, s32[16]{0:T(128)S(1)}, s32[16]{0:T(128)S(1)}, s32[16]{0:T(128)S(1)}, s32[16]{0:T(128)S(1)}) custom-call(s32[1]{0:T(128)} %bitcast.me_ref, s32[16]{0:T(128)S(1)} %bitcast.17, s32[16]{0:T(128)S(1)} %bitcast.18), custom_call_target="tpu_custom_call" | custom-call | tf_op jit(solution)/shard_map/plan/pallas_call | solution.py:304
  16.1 0.0 collective-permute-done.first_ref
  16.1 0.0 collective-permute-done.1.second_ref
  16.1 1.3 %first_level.3 = bf16[2,512,256]{2,1,0:T(8,128)(2,1)S(1)} custom-call(s32[4]{0:T(128)S(1)} %subtract_reduce_fusion.starts_ref, s32[3]{0:T(128)S(1)} %pad_add_fusion.side_ref, bf16[2,192,512]{2,1,0:T(8,128)(2,1)S(1)} %get-tuple-element.34.sent_first_ref, bf16[2,192,512]{2,1,0:T(8,128)(2,1)S(1)} %get-tuple-element.35.sent_second_ref, ...), custom_call_target="tpu_custom_call" | custom-call | flops 335544320 | bytes 2097152 | tf_op jit(solution)/shard_map/first_level/pallas_call | solution.py:171
  17.5 0.1 collective-permute-start.3
  17.6 1.3 %first_level.2 = bf16[2,512,256]{2,1,0:T(8,128)(2,1)S(1)} custom-call(s32[4]{0:T(128)S(1)} %subtract_reduce_fusion.starts_ref, s32[3]{0:T(128)S(1)} %pad_add_fusion.side_ref, bf16[2,192,512]{2,1,0:T(8,128)(2,1)S(1)} %get-tuple-element.34.sent_first_ref, bf16[2,192,512]{2,1,0:T(8,128)(2,1)S(1)} %get-tuple-element.35.sent_second_ref, ...), custom_call_target="tpu_custom_call" | custom-call | flops 335544320 | bytes 2097152 | tf_op jit(solution)/shard_map/first_level/pallas_call | solution.py:171
  18.9 0.5 collective-permute-done.3
  19.5 0.1 add_convert_fusion.own_ref
  19.6 1.2 %collective-permute-start.4 = (bf16[2,192,256]{2,1,0:T(8,128)(2,1)S(1)}, bf16[2,192,256]{2,1,0:T(8,128)(2,1)S(1)}, u32[]{:S(2)}, u32[]{:S(2)}) collective-permute-start(bf16[2,192,256]{2,1,0:T(8,128)(2,1)S(1)} %get-tuple-element.64), channel_id=1, source_target_pairs={{0,1},{1,0},{2,3},{3,2},{4,12},{5,6},{6,5},{7,15},{8,9},{9,8},{10,... | collective-permute-start | bytes 589832 | tf_op jit(solution)/shard_map/ppermute | solution.py:43
  20.8 1.5 %collective-permute-start.5 = (bf16[2,192,256]{2,1,0:T(8,128)(2,1)S(1)}, bf16[2,192,256]{2,1,0:T(8,128)(2,1)S(1)}, u32[]{:S(2)}, u32[]{:S(2)}) collective-permute-start(bf16[2,192,256]{2,1,0:T(8,128)(2,1)S(1)} %get-tuple-element.63), channel_id=1, source_target_pairs={{0,8},{1,2},{2,1},{3,11},{4,5},{5,4},{6,7},{7,6},{8,0},{9,10},{10,... | collective-permute-start | bytes 589832 | tf_op jit(solution)/shard_map/ppermute | solution.py:43
  22.3 1.8 %copy.9 = bf16[1,8,2,128,320]{4,3,2,1,0:T(8,128)(2,1)S(1)} copy(bf16[1,8,2,128,320]{3,4,2,1,0:T(8,128)(2,1)} %param.11) | data formatting | bytes 2621440 | tf_op args[4]
  24.1 0.7 %fusion.1.starts_ref = s32[8]{0:T(128)S(1)} fusion(s32[8,8]{1,0:T(8,128)} %param.12, s32[]{:T(128)S(6)} %select_n.19, s32[]{:T(128)S(6)} %sub.25), kind=kLoop, calls=%fused_computation.6 | loop fusion | flops 8 | bytes 72 | tf_op jit(solution)/shard_map/sub | solution.py:471
  24.8 2.1 %collective-permute-done.4.first_ref = bf16[2,192,256]{2,1,0:T(8,128)(2,1)S(1)} collective-permute-done((bf16[2,192,256]{2,1,0:T(8,128)(2,1)S(1)}, bf16[2,192,256]{2,1,0:T(8,128)(2,1)S(1)}, u32[]{:S(2)}, u32[]{:S(2)}) %collective-permute-start.4) | collective-permute-done | bytes 196640 | tf_op jit(solution)/shard_map/ppermute | solution.py:43
  26.9 0.0 collective-permute-done.5.second_ref
  26.9 1.1 %second_level_early.1 = bf16[6,2,64,128]{3,2,1,0:T(8,128)(2,1)S(1)} custom-call(s32[8]{0:T(128)S(1)} %fusion.1.starts_ref, s32[3]{0:T(128)S(1)} %pad_add_fusion.side_ref, s32[16]{0:T(128)S(1)} %get-tuple-element.41.sector_ref, bf16[2,512,256]{2,1,0:T(8,128)(2,1)S(1)} %add_convert_fusion.own_ref, bf16[2,192,256]{2,1,0:T(8,128)(2,1)S(1)} %collective-permute-done.4.first_ref, ...), custom_call_target="tpu_custom_call" | custom-call | flops 125829120 | bytes 1048576 | tf_op jit(solution)/shard_map/second_level_early/pallas_call | solution.py:237
  28.0 1.6 %collective-permute-start.6 = (bf16[6,2,64,128]{3,2,1,0:T(8,128)(2,1)S(1)}, bf16[6,2,64,128]{3,2,1,0:T(8,128)(2,1)S(1)}, u32[]{:S(2)}, u32[]{:S(2)}) collective-permute-start(bf16[6,2,64,128]{3,2,1,0:T(8,128)(2,1)S(1)} %second_level_early.1), channel_id=1, source_target_pairs={{0,8},{8,0},{4,12},{12,4},{16,24},{24,16},{20,28},{28,20},{1,9},{9... | collective-permute-start | bytes 589832 | tf_op jit(solution)/shard_map/ppermute | solution.py:54
  29.7 1.9 %second_level.1 = (bf16[16,2,64,128]{3,2,1,0:T(8,128)(2,1)S(1)}, bf16[10,2,64,128]{3,2,1,0:T(8,128)(2,1)S(1)}) custom-call(s32[8]{0:T(128)S(1)} %fusion.1.starts_ref, s32[3]{0:T(128)S(1)} %pad_add_fusion.side_ref, s32[16]{0:T(128)S(1)} %get-tuple-element.44.own_at_ref, s32[16]{0:T(128)S(1)} %get-tuple-element.45.other_at_ref, ...), custom_call_target="tpu_custom_call" | custom-call | flops 671088640 | bytes 4194304 | tf_op jit(solution)/shard_map/second_level/pallas_call | solution.py:248
  31.6 3.7 %collective-permute-done.6.refs_0_ = bf16[6,2,64,128]{3,2,1,0:T(8,128)(2,1)S(1)} collective-permute-done((bf16[6,2,64,128]{3,2,1,0:T(8,128)(2,1)S(1)}, bf16[6,2,64,128]{3,2,1,0:T(8,128)(2,1)S(1)}, u32[]{:S(2)}, u32[]{:S(2)}) %collective-permute-start.6) | collective-permute-done | bytes 196640 | tf_op jit(solution)/shard_map/ppermute | solution.py:54
  35.3 0.6 collective-permute-start.7
  35.9 0.6 early_wires.1
  36.5 3.1 %collective-permute-start.12 = (bf16[4,2,64,128]{3,2,1,0:T(8,128)(2,1)S(1)}, bf16[4,2,64,128]{3,2,1,0:T(8,128)(2,1)S(1)}, u32[]{:S(2)}, u32[]{:S(2)}) collective-permute-start(bf16[4,2,64,128]{3,2,1,0:T(8,128)(2,1)S(1)} %get-tuple-element.60), channel_id=1, source_target_pairs={{0,2},{1,3},{2,0},{3,1},{4,6},{5,7},{6,4},{7,5},{8,10},{9,11},{10,... | collective-permute-start | bytes 393224 | tf_op jit(solution)/shard_map/ppermute | solution.py:413
  39.6 1.0 %collective-permute-start.8 = (bf16[2,2,64,128]{3,2,1,0:T(8,128)(2,1)S(1)}, bf16[2,2,64,128]{3,2,1,0:T(8,128)(2,1)S(1)}, u32[]{:S(2)}, u32[]{:S(2)}) collective-permute-start(bf16[2,2,64,128]{3,2,1,0:T(8,128)(2,1)S(1)} %get-tuple-element.52), channel_id=1, source_target_pairs={{0,3},{1,2},{2,1},{3,0},{4,7},{5,6},{6,5},{7,4},{8,11},{9,10},{10,... | collective-permute-start | bytes 196616 | tf_op jit(solution)/shard_map/ppermute | solution.py:413
  40.6 5.2 %collective-permute-done.8.refs_0_ = bf16[2,2,64,128]{3,2,1,0:T(8,128)(2,1)S(1)} collective-permute-done((bf16[2,2,64,128]{3,2,1,0:T(8,128)(2,1)S(1)}, bf16[2,2,64,128]{3,2,1,0:T(8,128)(2,1)S(1)}, u32[]{:S(2)}, u32[]{:S(2)}) %collective-permute-start.8) | collective-permute-done | bytes 65568 | tf_op jit(solution)/shard_map/ppermute | solution.py:413
  45.7 0.0 collective-permute-done.7.refs_0_
  45.7 0.8 %late_wires.2 = (bf16[6,2,64,128]{3,2,1,0:T(8,128)(2,1)S(1)}, bf16[4,2,64,128]{3,2,1,0:T(8,128)(2,1)S(1)}, bf16[4,2,64,128]{3,2,1,0:T(8,128)(2,1)S(1)}, bf16[8,2,64,128]{3,2,1,0:T(8,128)(2,1)S(1)}) custom-call(s32[1]{0:T(128)} %bitcast.me_ref, s32[16]{0:T(128)S(1)} %get-tuple-element.48.target_ref, s32[16]{0:T(128)S(1)} %get-tuple-element.49.rank_ref, ...), custom_call_target="tpu_custom_call" | custom-call | bytes 2097152 | tf_op jit(solution)/shard_map/late_wires/pallas_call | solution.py:365
  46.5 2.4 %collective-permute-start.9 = (bf16[6,2,64,128]{3,2,1,0:T(8,128)(2,1)S(1)}, bf16[6,2,64,128]{3,2,1,0:T(8,128)(2,1)S(1)}, u32[]{:S(2)}, u32[]{:S(2)}) collective-permute-start(bf16[6,2,64,128]{3,2,1,0:T(8,128)(2,1)S(1)} %get-tuple-element.56), channel_id=1, source_target_pairs={{0,3},{1,2},{2,1},{3,0},{4,7},{5,6},{6,5},{7,4},{8,11},{9,10},{10,... | collective-permute-start | bytes 589832 | tf_op jit(solution)/shard_map/ppermute | solution.py:413
  48.9 0.0 collective-permute-done.12.refs_5_
  48.9 0.6 %late_wires.3 = bf16[4,2,64,128]{3,2,1,0:T(8,128)(2,1)S(1)} custom-call(s32[1]{0:T(128)} %bitcast.me_ref, s32[16]{0:T(128)S(1)} %get-tuple-element.48.target_ref, s32[16]{0:T(128)S(1)} %get-tuple-element.49.rank_ref, bf16[16,2,64,128]{3,2,1,0:T(8,128)(2,1)S(1)} %get-tuple-element.50.keep_ref, bf16[10,2,64,128]{3,2,1,0:T(8,128)(2,1)S(1)} %collective-permute-done.7.refs_0_, ...), custom_call_target="tpu_custom_call" | custom-call | bytes 2097152 | tf_op jit(solution)/shard_map/late_wires/pallas_call | solution.py:365
  49.6 1.9 %collective-permute-start.13 = (bf16[4,2,64,128]{3,2,1,0:T(8,128)(2,1)S(1)}, bf16[4,2,64,128]{3,2,1,0:T(8,128)(2,1)S(1)}, u32[]{:S(2)}, u32[]{:S(2)}) collective-permute-start(bf16[4,2,64,128]{3,2,1,0:T(8,128)(2,1)S(1)} %late_wires.3), channel_id=1, source_target_pairs={{0,2},{1,3},{2,0},{3,1},{4,6},{5,7},{6,4},{7,5},{8,10},{9,11},{10,... | collective-permute-start | bytes 393224 | tf_op jit(solution)/shard_map/ppermute | solution.py:413
  51.5 0.6 collective-permute-start.10
  52.1 1.4 %collective-permute-start.11 = (bf16[4,2,64,128]{3,2,1,0:T(8,128)(2,1)S(1)}, bf16[4,2,64,128]{3,2,1,0:T(8,128)(2,1)S(1)}, u32[]{:S(2)}, u32[]{:S(2)}) collective-permute-start(bf16[4,2,64,128]{3,2,1,0:T(8,128)(2,1)S(1)} %get-tuple-element.58), channel_id=1, source_target_pairs={{0,1},{1,0},{2,3},{3,2},{4,5},{5,4},{6,7},{7,6},{8,9},{9,8},{10,11... | collective-permute-start | bytes 393224 | tf_op jit(solution)/shard_map/ppermute | solution.py:413
  53.5 9.6 %collective-permute-done.13.refs_6_ = bf16[4,2,64,128]{3,2,1,0:T(8,128)(2,1)S(1)} collective-permute-done((bf16[4,2,64,128]{3,2,1,0:T(8,128)(2,1)S(1)}, bf16[4,2,64,128]{3,2,1,0:T(8,128)(2,1)S(1)}, u32[]{:S(2)}, u32[]{:S(2)}) %collective-permute-start.13) | collective-permute-done | bytes 131104 | tf_op jit(solution)/shard_map/ppermute | solution.py:413
  63.1 0.0 collective-permute-done.10.refs_2_
  63.1 0.0 collective-permute-done.11.refs_3_
  63.1 0.0 collective-permute-done.9.refs_1_
  63.1 1.0 %collect.1 = bf16[32,2,64,128]{3,2,1,0:T(8,128)(2,1)} custom-call(s32[1]{0:T(128)} %bitcast.me_ref, bf16[2,2,64,128]{3,2,1,0:T(8,128)(2,1)S(1)} %collective-permute-done.8.refs_0_, bf16[6,2,64,128]{3,2,1,0:T(8,128)(2,1)S(1)} %collective-permute-done.9.refs_1_, bf16[4,2,64,128]{3,2,1,0:T(8,128)(2,1)S(1)} %collective-permute-done.10.refs_2_, ...), custom_call_target="tpu_custom_call" | custom-call | bytes 2097152 | tf_op jit(solution)/shard_map/collect/pallas_call | solution.py:396
  (1 shorter events, 0.0 us)
Async XLA Ops:
  0.0 6.9 %copy-start = (s32[1,16,1]{1,2,0:T(1,128)S(1)}, s32[1,16,1]{1,2,0:T(1,128)}, u32[]{:S(2)}) copy-start(s32[1,16,1]{1,2,0:T(1,128)} %param.13) | copy-start | bytes 196
  0.0 7.4 %copy-start.2 = (s32[8,4]{0,1:T(4,128)S(1)}, s32[8,4]{0,1:T(4,128)}, u32[]{:S(2)}) copy-start(s32[8,4]{0,1:T(4,128)} %param.10) | copy-start | bytes 388
  0.0 7.7 %copy-start.1 = (bf16[1,4,2,128,320]{3,4,2,1,0:T(8,128)(2,1)S(1)}, bf16[1,4,2,128,320]{3,4,2,1,0:T(8,128)(2,1)}, u32[]{:S(2)}) copy-start(bf16[1,4,2,128,320]{3,4,2,1,0:T(8,128)(2,1)} %param.9) | copy-start | bytes 1966084
  2.3 13.8 %collective-permute-start = (bf16[2,192,512]{2,1,0:T(8,128)(2,1)S(1)}, bf16[2,192,512]{2,1,0:T(8,128)(2,1)S(1)}, u32[]{:S(2)}, u32[]{:S(2)}) collective-permute-start(bf16[2,192,512]{2,1,0:T(8,128)(2,1)S(1)} %get-tuple-element.34.sent_first_ref), channel_id=1, source_target_pairs={{0,1},{1,0},{2,3},{3,2},{4,12},{5,6},{6,5},{7,15},{8,9},{9,8},{10,... | collective-permute-start | bytes 1179656 | tf_op jit(solution)/shard_map/ppermute | solution.py:43
  5.4 10.7 %collective-permute-start.1 = (bf16[2,192,512]{2,1,0:T(8,128)(2,1)S(1)}, bf16[2,192,512]{2,1,0:T(8,128)(2,1)S(1)}, u32[]{:S(2)}, u32[]{:S(2)}) collective-permute-start(bf16[2,192,512]{2,1,0:T(8,128)(2,1)S(1)} %get-tuple-element.35.sent_second_ref), channel_id=1, source_target_pairs={{0,8},{1,2},{2,1},{3,11},{4,5},{5,4},{6,7},{7,6},{8,0},{9,10},{10,... | collective-permute-start | bytes 1179656 | tf_op jit(solution)/shard_map/ppermute | solution.py:43
  6.9 7.6 %collective-permute-start.2 = (s32[1,16,1]{1,2,0:T(1,128)S(1)}, s32[1,16,1]{1,2,0:T(1,128)S(1)}, u32[]{:S(2)}, u32[]{:S(2)}) collective-permute-start(s32[1,16,1]{1,2,0:T(1,128)S(1)} %copy-done), channel_id=1, source_target_pairs={{0,8},{8,0},{4,12},{12,4},{16,24},{24,16},{20,28},{28,20},{1,9},{9... | collective-permute-start | bytes 200 | tf_op jit(solution)/shard_map/ppermute | solution.py:54
  17.5 2.0 %collective-permute-start.3 = (bf16[2,512,256]{2,1,0:T(8,128)(2,1)S(1)}, bf16[2,512,256]{2,1,0:T(8,128)(2,1)S(1)}, u32[]{:S(2)}, u32[]{:S(2)}) collective-permute-start(bf16[2,512,256]{2,1,0:T(8,128)(2,1)S(1)} %first_level.3), channel_id=1, source_target_pairs={{0,4},{4,0},{8,12},{12,8},{16,20},{20,16},{24,28},{28,24},{1,5},{5... | collective-permute-start | bytes 1572872 | tf_op jit(solution)/shard_map/ppermute | solution.py:54
  19.6 7.3 %collective-permute-start.4 = (bf16[2,192,256]{2,1,0:T(8,128)(2,1)S(1)}, bf16[2,192,256]{2,1,0:T(8,128)(2,1)S(1)}, u32[]{:S(2)}, u32[]{:S(2)}) collective-permute-start(bf16[2,192,256]{2,1,0:T(8,128)(2,1)S(1)} %get-tuple-element.64), channel_id=1, source_target_pairs={{0,1},{1,0},{2,3},{3,2},{4,12},{5,6},{6,5},{7,15},{8,9},{9,8},{10,... | collective-permute-start | bytes 589832 | tf_op jit(solution)/shard_map/ppermute | solution.py:43
  20.8 6.1 %collective-permute-start.5 = (bf16[2,192,256]{2,1,0:T(8,128)(2,1)S(1)}, bf16[2,192,256]{2,1,0:T(8,128)(2,1)S(1)}, u32[]{:S(2)}, u32[]{:S(2)}) collective-permute-start(bf16[2,192,256]{2,1,0:T(8,128)(2,1)S(1)} %get-tuple-element.63), channel_id=1, source_target_pairs={{0,8},{1,2},{2,1},{3,11},{4,5},{5,4},{6,7},{7,6},{8,0},{9,10},{10,... | collective-permute-start | bytes 589832 | tf_op jit(solution)/shard_map/ppermute | solution.py:43
  28.0 7.3 %collective-permute-start.6 = (bf16[6,2,64,128]{3,2,1,0:T(8,128)(2,1)S(1)}, bf16[6,2,64,128]{3,2,1,0:T(8,128)(2,1)S(1)}, u32[]{:S(2)}, u32[]{:S(2)}) collective-permute-start(bf16[6,2,64,128]{3,2,1,0:T(8,128)(2,1)S(1)} %second_level_early.1), channel_id=1, source_target_pairs={{0,8},{8,0},{4,12},{12,4},{16,24},{24,16},{20,28},{28,20},{1,9},{9... | collective-permute-start | bytes 589832 | tf_op jit(solution)/shard_map/ppermute | solution.py:54
  35.3 10.4 %collective-permute-start.7 = (bf16[10,2,64,128]{3,2,1,0:T(8,128)(2,1)S(1)}, bf16[10,2,64,128]{3,2,1,0:T(8,128)(2,1)S(1)}, u32[]{:S(2)}, u32[]{:S(2)}) collective-permute-start(bf16[10,2,64,128]{3,2,1,0:T(8,128)(2,1)S(1)} %get-tuple-element.47), channel_id=1, source_target_pairs={{0,8},{8,0},{4,12},{12,4},{16,24},{24,16},{20,28},{28,20},{1,9},{9... | collective-permute-start | bytes 983048 | tf_op jit(solution)/shard_map/ppermute | solution.py:54
  36.5 12.4 %collective-permute-start.12 = (bf16[4,2,64,128]{3,2,1,0:T(8,128)(2,1)S(1)}, bf16[4,2,64,128]{3,2,1,0:T(8,128)(2,1)S(1)}, u32[]{:S(2)}, u32[]{:S(2)}) collective-permute-start(bf16[4,2,64,128]{3,2,1,0:T(8,128)(2,1)S(1)} %get-tuple-element.60), channel_id=1, source_target_pairs={{0,2},{1,3},{2,0},{3,1},{4,6},{5,7},{6,4},{7,5},{8,10},{9,11},{10,... | collective-permute-start | bytes 393224 | tf_op jit(solution)/shard_map/ppermute | solution.py:413
  39.6 6.2 %collective-permute-start.8 = (bf16[2,2,64,128]{3,2,1,0:T(8,128)(2,1)S(1)}, bf16[2,2,64,128]{3,2,1,0:T(8,128)(2,1)S(1)}, u32[]{:S(2)}, u32[]{:S(2)}) collective-permute-start(bf16[2,2,64,128]{3,2,1,0:T(8,128)(2,1)S(1)} %get-tuple-element.52), channel_id=1, source_target_pairs={{0,3},{1,2},{2,1},{3,0},{4,7},{5,6},{6,5},{7,4},{8,11},{9,10},{10,... | collective-permute-start | bytes 196616 | tf_op jit(solution)/shard_map/ppermute | solution.py:413
  46.5 16.5 %collective-permute-start.9 = (bf16[6,2,64,128]{3,2,1,0:T(8,128)(2,1)S(1)}, bf16[6,2,64,128]{3,2,1,0:T(8,128)(2,1)S(1)}, u32[]{:S(2)}, u32[]{:S(2)}) collective-permute-start(bf16[6,2,64,128]{3,2,1,0:T(8,128)(2,1)S(1)} %get-tuple-element.56), channel_id=1, source_target_pairs={{0,3},{1,2},{2,1},{3,0},{4,7},{5,6},{6,5},{7,4},{8,11},{9,10},{10,... | collective-permute-start | bytes 589832 | tf_op jit(solution)/shard_map/ppermute | solution.py:413
  49.6 13.5 %collective-permute-start.13 = (bf16[4,2,64,128]{3,2,1,0:T(8,128)(2,1)S(1)}, bf16[4,2,64,128]{3,2,1,0:T(8,128)(2,1)S(1)}, u32[]{:S(2)}, u32[]{:S(2)}) collective-permute-start(bf16[4,2,64,128]{3,2,1,0:T(8,128)(2,1)S(1)} %late_wires.3), channel_id=1, source_target_pairs={{0,2},{1,3},{2,0},{3,1},{4,6},{5,7},{6,4},{7,5},{8,10},{9,11},{10,... | collective-permute-start | bytes 393224 | tf_op jit(solution)/shard_map/ppermute | solution.py:413
  51.5 11.6 %collective-permute-start.10 = (bf16[4,2,64,128]{3,2,1,0:T(8,128)(2,1)S(1)}, bf16[4,2,64,128]{3,2,1,0:T(8,128)(2,1)S(1)}, u32[]{:S(2)}, u32[]{:S(2)}) collective-permute-start(bf16[4,2,64,128]{3,2,1,0:T(8,128)(2,1)S(1)} %get-tuple-element.57), channel_id=1, source_target_pairs={{0,1},{1,0},{2,3},{3,2},{4,5},{5,4},{6,7},{7,6},{8,9},{9,8},{10,11... | collective-permute-start | bytes 393224 | tf_op jit(solution)/shard_map/ppermute | solution.py:413
  52.1 11.0 %collective-permute-start.11 = (bf16[4,2,64,128]{3,2,1,0:T(8,128)(2,1)S(1)}, bf16[4,2,64,128]{3,2,1,0:T(8,128)(2,1)S(1)}, u32[]{:S(2)}, u32[]{:S(2)}) collective-permute-start(bf16[4,2,64,128]{3,2,1,0:T(8,128)(2,1)S(1)} %get-tuple-element.58), channel_id=1, source_target_pairs={{0,1},{1,0},{2,3},{3,2},{4,5},{5,4},{6,7},{7,6},{8,9},{9,8},{10,11... | collective-permute-start | bytes 393224 | tf_op jit(solution)/shard_map/ppermute | solution.py:413

commit v11 on v6

--- a/solution.py
+++ b/solution.py
@@ -445,7 +445,8 @@
     early_spans += [(distance, 0, longer) for distance in others]
     late_spans = [(distance, shorter, capacity) for distance in odd]
     for distance in range(1, beam_count // 2):
-        late_spans += [(distance, 0, capacity // 2), (distance, capacity // 2, capacity)]
+        cut = (5 * capacity + 4) // 8
+        late_spans += [(distance, 0, cut), (distance, cut, capacity)]
     late_spans.append((0, 0, capacity))
     last_spans = [(distance, longer, capacity) for distance in others]
 

time: 62.3 us -> 61.9 us (level)
  transfers between devices with their start and end apart: 14 -> 14, of which waited for: 8 -> 10; matrix products, arithmetic and copies ran while one was open for 5% -> 5% of each run, Pallas kernels for 11% -> 11%
where the time goes in v11:
time: 61.9 us; the launch traced here: 61.7 us
  waiting for transfers between devices  25.5 us (41%)
  starting transfers between devices  20.1 us (32%)
  Pallas kernels  12.7 us (21%)
  local copies, waits for them, and re-layouts  2.24 us (4%)
  other arithmetic  1.1 us (2%)
    ppermute x6, waiting for transfers between devices, spread(): received.append(lax.ppermute(wire, 'beam', route) if distance else wire)  13.9 us
    ppermute x6, starting transfers between devices, spread(): received.append(lax.ppermute(wire, 'beam', route) if distance else wire)  9.42 us
    ppermute x4, waiting for transfers between devices, trade_edges(): received.append(lax.ppermute(block, ('aperture', 'beam'), route))  6.63 us
    ppermute x4, starting transfers between devices, trade_edges(): received.append(lax.ppermute(block, ('aperture', 'beam'), route))  6.01 us
    ppermute x4, waiting for transfers between devices, partner(): return lax.ppermute(block, axis, route)  5.03 us
    ppermute x4, starting transfers between devices, partner(): return lax.ppermute(block, axis, route)  4.62 us
    pallas_call x2, Pallas kernels, first_level(): pl.pallas_call(functools.partial(first_level_kernel, column, rows), out_s...  2.67 us
    pallas_call x1, Pallas kernels, resample(): pl.pallas_call(resample_kernel, out_shape=(shape, shape), in_specs=[ANY,...  2.31 us
  transfers between devices with their start and end apart: 14, of which 10 were waited for; matrix products, arithmetic and copies ran while one was open for 5% of the time, Pallas kernels for 11%

profile of v11, /device:TPU:0, one launch (start us, length us, event | category | flops | bytes accessed | tf_op | source)
XLA Modules:
  0.0 61.7 jit_solution(7037181662449181732)
XLA Ops:
  0.0 0.0 copy-start
  0.0 0.0 copy-start.2
  0.0 0.0 copy-start.1
  0.0 2.3 %resample.1 = (bf16[2,192,512]{2,1,0:T(8,128)(2,1)S(1)}, bf16[2,192,512]{2,1,0:T(8,128)(2,1)S(1)}) custom-call(bf16[2,256,512]{2,1,0:T(8,128)(2,1)} %bitcast.20, bf16[2,512,512]{2,1,0:T(8,128)(2,1)} %bitcast.19), custom_call_target="tpu_custom_call" | custom-call | flops 536870912 | bytes 2097152 | tf_op jit(solution)/shard_map/resample/pallas_call | solution.py:101
  2.3 3.1 %collective-permute-start = (bf16[2,192,512]{2,1,0:T(8,128)(2,1)S(1)}, bf16[2,192,512]{2,1,0:T(8,128)(2,1)S(1)}, u32[]{:S(2)}, u32[]{:S(2)}) collective-permute-start(bf16[2,192,512]{2,1,0:T(8,128)(2,1)S(1)} %get-tuple-element.34.sent_first_ref), channel_id=1, source_target_pairs={{0,1},{1,0},{2,3},{3,2},{4,5},{5,4},{6,7},{7,6},{8,9},{9,8},{10,11... | collective-permute-start | bytes 1179656 | tf_op jit(solution)/shard_map/ppermute | solution.py:43
  5.4 0.0 collective-permute-start.1
  5.4 0.0 copy-done
  5.4 1.5 %collective-permute-start.2 = (s32[1,16,1]{1,2,0:T(1,128)S(1)}, s32[1,16,1]{1,2,0:T(1,128)S(1)}, u32[]{:S(2)}, u32[]{:S(2)}) collective-permute-start(s32[1,16,1]{1,2,0:T(1,128)S(1)} %copy-done), channel_id=1, source_target_pairs={{0,8},{8,0},{4,12},{12,4},{16,24},{24,16},{20,28},{28,20},{1,9},{9... | collective-permute-start | bytes 200 | tf_op jit(solution)/shard_map/ppermute | solution.py:54
  6.9 0.0 copy-done.2
  6.9 0.2 subtract_reduce_fusion.starts_ref
  7.1 0.1 pad_add_fusion.side_ref
  7.2 0.0 copy-done.1
  7.2 0.4 copy.8
  7.6 1.4 %collective-permute-done.2 = s32[1,16,1]{1,2,0:T(1,128)S(1)} collective-permute-done((s32[1,16,1]{1,2,0:T(1,128)S(1)}, s32[1,16,1]{1,2,0:T(1,128)S(1)}, u32[]{:S(2)}, u32[]{:S(2)}) %collective-permute-start.2) | collective-permute-done | bytes 96 | tf_op jit(solution)/shard_map/ppermute | solution.py:54
  9.0 1.6 %plan.1 = (s32[16]{0:T(128)S(1)}, s32[16]{0:T(128)S(1)}, s32[16]{0:T(128)S(1)}, s32[16]{0:T(128)S(1)}, s32[16]{0:T(128)S(1)}) custom-call(s32[1]{0:T(128)} %bitcast.me_ref, s32[16]{0:T(128)S(1)} %bitcast.17, s32[16]{0:T(128)S(1)} %bitcast.18), custom_call_target="tpu_custom_call" | custom-call | tf_op jit(solution)/shard_map/plan/pallas_call | solution.py:304
  10.6 4.0 %collective-permute-done.first_ref = bf16[2,192,512]{2,1,0:T(8,128)(2,1)S(1)} collective-permute-done((bf16[2,192,512]{2,1,0:T(8,128)(2,1)S(1)}, bf16[2,192,512]{2,1,0:T(8,128)(2,1)S(1)}, u32[]{:S(2)}, u32[]{:S(2)}) %collective-permute-start) | collective-permute-done | bytes 393248 | tf_op jit(solution)/shard_map/ppermute | solution.py:43
  14.5 0.0 collective-permute-done.1.second_ref
  14.5 1.3 %first_level.3 = bf16[2,512,256]{2,1,0:T(8,128)(2,1)S(1)} custom-call(s32[4]{0:T(128)S(1)} %subtract_reduce_fusion.starts_ref, s32[3]{0:T(128)S(1)} %pad_add_fusion.side_ref, bf16[2,192,512]{2,1,0:T(8,128)(2,1)S(1)} %get-tuple-element.34.sent_first_ref, bf16[2,192,512]{2,1,0:T(8,128)(2,1)S(1)} %get-tuple-element.35.sent_second_ref, ...), custom_call_target="tpu_custom_call" | custom-call | flops 335544320 | bytes 2097152 | tf_op jit(solution)/shard_map/first_level/pallas_call | solution.py:171
  15.9 0.1 collective-permute-start.3
  16.0 1.3 %first_level.2 = bf16[2,512,256]{2,1,0:T(8,128)(2,1)S(1)} custom-call(s32[4]{0:T(128)S(1)} %subtract_reduce_fusion.starts_ref, s32[3]{0:T(128)S(1)} %pad_add_fusion.side_ref, bf16[2,192,512]{2,1,0:T(8,128)(2,1)S(1)} %get-tuple-element.34.sent_first_ref, bf16[2,192,512]{2,1,0:T(8,128)(2,1)S(1)} %get-tuple-element.35.sent_second_ref, ...), custom_call_target="tpu_custom_call" | custom-call | flops 335544320 | bytes 2097152 | tf_op jit(solution)/shard_map/first_level/pallas_call | solution.py:171
  17.3 0.5 collective-permute-done.3
  17.8 0.1 add_convert_fusion.own_ref
  18.0 2.9 %collective-permute-start.4 = (bf16[2,192,256]{2,1,0:T(8,128)(2,1)S(1)}, bf16[2,192,256]{2,1,0:T(8,128)(2,1)S(1)}, u32[]{:S(2)}, u32[]{:S(2)}) collective-permute-start(bf16[2,192,256]{2,1,0:T(8,128)(2,1)S(1)} %get-tuple-element.64), channel_id=1, source_target_pairs={{0,1},{1,0},{2,3},{3,2},{4,5},{5,4},{6,7},{7,6},{8,9},{9,8},{10,11... | collective-permute-start | bytes 589832 | tf_op jit(solution)/shard_map/ppermute | solution.py:43
  21.0 0.0 collective-permute-start.5
  21.0 1.8 %copy.9 = bf16[1,8,2,128,320]{4,3,2,1,0:T(8,128)(2,1)S(1)} copy(bf16[1,8,2,128,320]{3,4,2,1,0:T(8,128)(2,1)} %param.11) | data formatting | bytes 2621440 | tf_op args[4]
  22.8 0.7 %fusion.1.starts_ref = s32[8]{0:T(128)S(1)} fusion(s32[8,8]{1,0:T(8,128)} %param.12, s32[]{:T(128)S(6)} %select_n.19, s32[]{:T(128)S(6)} %sub.25), kind=kLoop, calls=%fused_computation.6 | loop fusion | flops 8 | bytes 72 | tf_op jit(solution)/shard_map/sub | solution.py:472
  23.5 2.7 %collective-permute-done.4.first_ref = bf16[2,192,256]{2,1,0:T(8,128)(2,1)S(1)} collective-permute-done((bf16[2,192,256]{2,1,0:T(8,128)(2,1)S(1)}, bf16[2,192,256]{2,1,0:T(8,128)(2,1)S(1)}, u32[]{:S(2)}, u32[]{:S(2)}) %collective-permute-start.4) | collective-permute-done | bytes 196640 | tf_op jit(solution)/shard_map/ppermute | solution.py:43
  26.2 0.0 collective-permute-done.5.second_ref
  26.2 1.1 %second_level_early.1 = bf16[6,2,64,128]{3,2,1,0:T(8,128)(2,1)S(1)} custom-call(s32[8]{0:T(128)S(1)} %fusion.1.starts_ref, s32[3]{0:T(128)S(1)} %pad_add_fusion.side_ref, s32[16]{0:T(128)S(1)} %get-tuple-element.41.sector_ref, bf16[2,512,256]{2,1,0:T(8,128)(2,1)S(1)} %add_convert_fusion.own_ref, bf16[2,192,256]{2,1,0:T(8,128)(2,1)S(1)} %collective-permute-done.4.first_ref, ...), custom_call_target="tpu_custom_call" | custom-call | flops 125829120 | bytes 1048576 | tf_op jit(solution)/shard_map/second_level_early/pallas_call | solution.py:237
  27.3 1.6 %collective-permute-start.6 = (bf16[6,2,64,128]{3,2,1,0:T(8,128)(2,1)S(1)}, bf16[6,2,64,128]{3,2,1,0:T(8,128)(2,1)S(1)}, u32[]{:S(2)}, u32[]{:S(2)}) collective-permute-start(bf16[6,2,64,128]{3,2,1,0:T(8,128)(2,1)S(1)} %second_level_early.1), channel_id=1, source_target_pairs={{0,8},{8,0},{4,12},{12,4},{16,24},{24,16},{20,28},{28,20},{1,9},{9... | collective-permute-start | bytes 589832 | tf_op jit(solution)/shard_map/ppermute | solution.py:54
  28.8 1.9 %second_level.1 = (bf16[16,2,64,128]{3,2,1,0:T(8,128)(2,1)S(1)}, bf16[10,2,64,128]{3,2,1,0:T(8,128)(2,1)S(1)}) custom-call(s32[8]{0:T(128)S(1)} %fusion.1.starts_ref, s32[3]{0:T(128)S(1)} %pad_add_fusion.side_ref, s32[16]{0:T(128)S(1)} %get-tuple-element.44.own_at_ref, s32[16]{0:T(128)S(1)} %get-tuple-element.45.other_at_ref, ...), custom_call_target="tpu_custom_call" | custom-call | flops 671088640 | bytes 4194304 | tf_op jit(solution)/shard_map/second_level/pallas_call | solution.py:248
  30.8 3.0 %collective-permute-done.6.refs_0_ = bf16[6,2,64,128]{3,2,1,0:T(8,128)(2,1)S(1)} collective-permute-done((bf16[6,2,64,128]{3,2,1,0:T(8,128)(2,1)S(1)}, bf16[6,2,64,128]{3,2,1,0:T(8,128)(2,1)S(1)}, u32[]{:S(2)}, u32[]{:S(2)}) %collective-permute-start.6) | collective-permute-done | bytes 196640 | tf_op jit(solution)/shard_map/ppermute | solution.py:54
  33.8 1.5 %collective-permute-start.7 = (bf16[10,2,64,128]{3,2,1,0:T(8,128)(2,1)S(1)}, bf16[10,2,64,128]{3,2,1,0:T(8,128)(2,1)S(1)}, u32[]{:S(2)}, u32[]{:S(2)}) collective-permute-start(bf16[10,2,64,128]{3,2,1,0:T(8,128)(2,1)S(1)} %get-tuple-element.47), channel_id=1, source_target_pairs={{0,8},{8,0},{4,12},{12,4},{16,24},{24,16},{20,28},{28,20},{1,9},{9... | collective-permute-start | bytes 983048 | tf_op jit(solution)/shard_map/ppermute | solution.py:54
  35.3 0.6 early_wires.1
  35.9 2.4 %collective-permute-start.8 = (bf16[2,2,64,128]{3,2,1,0:T(8,128)(2,1)S(1)}, bf16[2,2,64,128]{3,2,1,0:T(8,128)(2,1)S(1)}, u32[]{:S(2)}, u32[]{:S(2)}) collective-permute-start(bf16[2,2,64,128]{3,2,1,0:T(8,128)(2,1)S(1)} %get-tuple-element.52), channel_id=1, source_target_pairs={{0,3},{1,2},{2,1},{3,0},{4,7},{5,6},{6,5},{7,4},{8,11},{9,10},{10,... | collective-permute-start | bytes 196616 | tf_op jit(solution)/shard_map/ppermute | solution.py:413
  38.3 0.6 %collective-permute-start.12 = (bf16[4,2,64,128]{3,2,1,0:T(8,128)(2,1)S(1)}, bf16[4,2,64,128]{3,2,1,0:T(8,128)(2,1)S(1)}, u32[]{:S(2)}, u32[]{:S(2)}) collective-permute-start(bf16[4,2,64,128]{3,2,1,0:T(8,128)(2,1)S(1)} %get-tuple-element.60), channel_id=1, source_target_pairs={{0,2},{1,3},{2,0},{3,1},{4,6},{5,7},{6,4},{7,5},{8,10},{9,11},{10,... | collective-permute-start | bytes 393224 | tf_op jit(solution)/shard_map/ppermute | solution.py:413
  38.9 3.1 %collective-permute-done.8.refs_0_ = bf16[2,2,64,128]{3,2,1,0:T(8,128)(2,1)S(1)} collective-permute-done((bf16[2,2,64,128]{3,2,1,0:T(8,128)(2,1)S(1)}, bf16[2,2,64,128]{3,2,1,0:T(8,128)(2,1)S(1)}, u32[]{:S(2)}, u32[]{:S(2)}) %collective-permute-start.8) | collective-permute-done | bytes 65568 | tf_op jit(solution)/shard_map/ppermute | solution.py:413
  42.0 0.1 collective-permute-done.7.refs_0_
  42.1 0.8 %late_wires.2 = (bf16[6,2,64,128]{3,2,1,0:T(8,128)(2,1)S(1)}, bf16[5,2,64,128]{3,2,1,0:T(8,128)(2,1)S(1)}, bf16[3,2,64,128]{3,2,1,0:T(8,128)(2,1)S(1)}, bf16[8,2,64,128]{3,2,1,0:T(8,128)(2,1)S(1)}) custom-call(s32[1]{0:T(128)} %bitcast.me_ref, s32[16]{0:T(128)S(1)} %get-tuple-element.48.target_ref, s32[16]{0:T(128)S(1)} %get-tuple-element.49.rank_ref, ...), custom_call_target="tpu_custom_call" | custom-call | bytes 2097152 | tf_op jit(solution)/shard_map/late_wires/pallas_call | solution.py:365
  42.9 2.4 %collective-permute-start.9 = (bf16[6,2,64,128]{3,2,1,0:T(8,128)(2,1)S(1)}, bf16[6,2,64,128]{3,2,1,0:T(8,128)(2,1)S(1)}, u32[]{:S(2)}, u32[]{:S(2)}) collective-permute-start(bf16[6,2,64,128]{3,2,1,0:T(8,128)(2,1)S(1)} %get-tuple-element.56), channel_id=1, source_target_pairs={{0,3},{1,2},{2,1},{3,0},{4,7},{5,6},{6,5},{7,4},{8,11},{9,10},{10,... | collective-permute-start | bytes 589832 | tf_op jit(solution)/shard_map/ppermute | solution.py:413
  45.3 1.7 %collective-permute-start.10 = (bf16[5,2,64,128]{3,2,1,0:T(8,128)(2,1)S(1)}, bf16[5,2,64,128]{3,2,1,0:T(8,128)(2,1)S(1)}, u32[]{:S(2)}, u32[]{:S(2)}) collective-permute-start(bf16[5,2,64,128]{3,2,1,0:T(8,128)(2,1)S(1)} %get-tuple-element.57), channel_id=1, source_target_pairs={{0,1},{1,0},{2,3},{3,2},{4,5},{5,4},{6,7},{7,6},{8,9},{9,8},{10,11... | collective-permute-start | bytes 491528 | tf_op jit(solution)/shard_map/ppermute | solution.py:413
  47.0 5.1 %collective-permute-done.12.refs_5_ = bf16[4,2,64,128]{3,2,1,0:T(8,128)(2,1)S(1)} collective-permute-done((bf16[4,2,64,128]{3,2,1,0:T(8,128)(2,1)S(1)}, bf16[4,2,64,128]{3,2,1,0:T(8,128)(2,1)S(1)}, u32[]{:S(2)}, u32[]{:S(2)}) %collective-permute-start.12) | collective-permute-done | bytes 131104 | tf_op jit(solution)/shard_map/ppermute | solution.py:413
  52.2 0.6 %late_wires.3 = bf16[4,2,64,128]{3,2,1,0:T(8,128)(2,1)S(1)} custom-call(s32[1]{0:T(128)} %bitcast.me_ref, s32[16]{0:T(128)S(1)} %get-tuple-element.48.target_ref, s32[16]{0:T(128)S(1)} %get-tuple-element.49.rank_ref, bf16[16,2,64,128]{3,2,1,0:T(8,128)(2,1)S(1)} %get-tuple-element.50.keep_ref, bf16[10,2,64,128]{3,2,1,0:T(8,128)(2,1)S(1)} %collective-permute-done.7.refs_0_, ...), custom_call_target="tpu_custom_call" | custom-call | bytes 2097152 | tf_op jit(solution)/shard_map/late_wires/pallas_call | solution.py:365
  52.8 0.1 collective-permute-start.13
  52.9 2.2 %collective-permute-start.11 = (bf16[3,2,64,128]{3,2,1,0:T(8,128)(2,1)S(1)}, bf16[3,2,64,128]{3,2,1,0:T(8,128)(2,1)S(1)}, u32[]{:S(2)}, u32[]{:S(2)}) collective-permute-start(bf16[3,2,64,128]{3,2,1,0:T(8,128)(2,1)S(1)} %get-tuple-element.58), channel_id=1, source_target_pairs={{0,1},{1,0},{2,3},{3,2},{4,5},{5,4},{6,7},{7,6},{8,9},{9,8},{10,11... | collective-permute-start | bytes 294920 | tf_op jit(solution)/shard_map/ppermute | solution.py:413
  55.1 2.7 %collective-permute-done.11.refs_3_ = bf16[3,2,64,128]{3,2,1,0:T(8,128)(2,1)S(1)} collective-permute-done((bf16[3,2,64,128]{3,2,1,0:T(8,128)(2,1)S(1)}, bf16[3,2,64,128]{3,2,1,0:T(8,128)(2,1)S(1)}, u32[]{:S(2)}, u32[]{:S(2)}) %collective-permute-start.11) | collective-permute-done | bytes 98336 | tf_op jit(solution)/shard_map/ppermute | solution.py:413
  57.8 2.9 %collective-permute-done.13.refs_6_ = bf16[4,2,64,128]{3,2,1,0:T(8,128)(2,1)S(1)} collective-permute-done((bf16[4,2,64,128]{3,2,1,0:T(8,128)(2,1)S(1)}, bf16[4,2,64,128]{3,2,1,0:T(8,128)(2,1)S(1)}, u32[]{:S(2)}, u32[]{:S(2)}) %collective-permute-start.13) | collective-permute-done | bytes 131104 | tf_op jit(solution)/shard_map/ppermute | solution.py:413
  60.7 0.0 collective-permute-done.10.refs_2_
  60.7 0.0 collective-permute-done.9.refs_1_
  60.7 1.0 %collect.1 = bf16[32,2,64,128]{3,2,1,0:T(8,128)(2,1)} custom-call(s32[1]{0:T(128)} %bitcast.me_ref, bf16[2,2,64,128]{3,2,1,0:T(8,128)(2,1)S(1)} %collective-permute-done.8.refs_0_, bf16[6,2,64,128]{3,2,1,0:T(8,128)(2,1)S(1)} %collective-permute-done.9.refs_1_, bf16[5,2,64,128]{3,2,1,0:T(8,128)(2,1)S(1)} %collective-permute-done.10.refs_2_, ...), custom_call_target="tpu_custom_call" | custom-call | bytes 2097152 | tf_op jit(solution)/shard_map/collect/pallas_call | solution.py:396
  (1 shorter events, 0.0 us)
Async XLA Ops:
  0.0 5.4 %copy-start = (s32[1,16,1]{1,2,0:T(1,128)S(1)}, s32[1,16,1]{1,2,0:T(1,128)}, u32[]{:S(2)}) copy-start(s32[1,16,1]{1,2,0:T(1,128)} %param.13) | copy-start | bytes 196
  0.0 6.9 %copy-start.2 = (s32[8,4]{0,1:T(4,128)S(1)}, s32[8,4]{0,1:T(4,128)}, u32[]{:S(2)}) copy-start(s32[8,4]{0,1:T(4,128)} %param.10) | copy-start | bytes 388
  0.0 7.2 %copy-start.1 = (bf16[1,4,2,128,320]{3,4,2,1,0:T(8,128)(2,1)S(1)}, bf16[1,4,2,128,320]{3,4,2,1,0:T(8,128)(2,1)}, u32[]{:S(2)}) copy-start(bf16[1,4,2,128,320]{3,4,2,1,0:T(8,128)(2,1)} %param.9) | copy-start | bytes 1966084
  2.3 12.2 %collective-permute-start = (bf16[2,192,512]{2,1,0:T(8,128)(2,1)S(1)}, bf16[2,192,512]{2,1,0:T(8,128)(2,1)S(1)}, u32[]{:S(2)}, u32[]{:S(2)}) collective-permute-start(bf16[2,192,512]{2,1,0:T(8,128)(2,1)S(1)} %get-tuple-element.34.sent_first_ref), channel_id=1, source_target_pairs={{0,1},{1,0},{2,3},{3,2},{4,5},{5,4},{6,7},{7,6},{8,9},{9,8},{10,11... | collective-permute-start | bytes 1179656 | tf_op jit(solution)/shard_map/ppermute | solution.py:43
  5.4 9.1 %collective-permute-start.1 = (bf16[2,192,512]{2,1,0:T(8,128)(2,1)S(1)}, bf16[2,192,512]{2,1,0:T(8,128)(2,1)S(1)}, u32[]{:S(2)}, u32[]{:S(2)}) collective-permute-start(bf16[2,192,512]{2,1,0:T(8,128)(2,1)S(1)} %get-tuple-element.35.sent_second_ref), channel_id=1, source_target_pairs={{0,4},{1,2},{2,1},{3,7},{4,0},{5,6},{6,5},{7,3},{8,12},{9,10},{10,... | collective-permute-start | bytes 1179656 | tf_op jit(solution)/shard_map/ppermute | solution.py:43
  5.4 3.5 %collective-permute-start.2 = (s32[1,16,1]{1,2,0:T(1,128)S(1)}, s32[1,16,1]{1,2,0:T(1,128)S(1)}, u32[]{:S(2)}, u32[]{:S(2)}) collective-permute-start(s32[1,16,1]{1,2,0:T(1,128)S(1)} %copy-done), channel_id=1, source_target_pairs={{0,8},{8,0},{4,12},{12,4},{16,24},{24,16},{20,28},{28,20},{1,9},{9... | collective-permute-start | bytes 200 | tf_op jit(solution)/shard_map/ppermute | solution.py:54
  15.9 2.0 %collective-permute-start.3 = (bf16[2,512,256]{2,1,0:T(8,128)(2,1)S(1)}, bf16[2,512,256]{2,1,0:T(8,128)(2,1)S(1)}, u32[]{:S(2)}, u32[]{:S(2)}) collective-permute-start(bf16[2,512,256]{2,1,0:T(8,128)(2,1)S(1)} %first_level.3), channel_id=1, source_target_pairs={{0,4},{4,0},{8,12},{12,8},{16,20},{20,16},{24,28},{28,24},{1,5},{5... | collective-permute-start | bytes 1572872 | tf_op jit(solution)/shard_map/ppermute | solution.py:54
  18.0 8.1 %collective-permute-start.4 = (bf16[2,192,256]{2,1,0:T(8,128)(2,1)S(1)}, bf16[2,192,256]{2,1,0:T(8,128)(2,1)S(1)}, u32[]{:S(2)}, u32[]{:S(2)}) collective-permute-start(bf16[2,192,256]{2,1,0:T(8,128)(2,1)S(1)} %get-tuple-element.64), channel_id=1, source_target_pairs={{0,1},{1,0},{2,3},{3,2},{4,5},{5,4},{6,7},{7,6},{8,9},{9,8},{10,11... | collective-permute-start | bytes 589832 | tf_op jit(solution)/shard_map/ppermute | solution.py:43
  21.0 5.2 %collective-permute-start.5 = (bf16[2,192,256]{2,1,0:T(8,128)(2,1)S(1)}, bf16[2,192,256]{2,1,0:T(8,128)(2,1)S(1)}, u32[]{:S(2)}, u32[]{:S(2)}) collective-permute-start(bf16[2,192,256]{2,1,0:T(8,128)(2,1)S(1)} %get-tuple-element.63), channel_id=1, source_target_pairs={{0,4},{1,2},{2,1},{3,7},{4,0},{5,6},{6,5},{7,3},{8,12},{9,10},{10,... | collective-permute-start | bytes 589832 | tf_op jit(solution)/shard_map/ppermute | solution.py:43
  27.3 6.5 %collective-permute-start.6 = (bf16[6,2,64,128]{3,2,1,0:T(8,128)(2,1)S(1)}, bf16[6,2,64,128]{3,2,1,0:T(8,128)(2,1)S(1)}, u32[]{:S(2)}, u32[]{:S(2)}) collective-permute-start(bf16[6,2,64,128]{3,2,1,0:T(8,128)(2,1)S(1)} %second_level_early.1), channel_id=1, source_target_pairs={{0,8},{8,0},{4,12},{12,4},{16,24},{24,16},{20,28},{28,20},{1,9},{9... | collective-permute-start | bytes 589832 | tf_op jit(solution)/shard_map/ppermute | solution.py:54
  33.8 8.3 %collective-permute-start.7 = (bf16[10,2,64,128]{3,2,1,0:T(8,128)(2,1)S(1)}, bf16[10,2,64,128]{3,2,1,0:T(8,128)(2,1)S(1)}, u32[]{:S(2)}, u32[]{:S(2)}) collective-permute-start(bf16[10,2,64,128]{3,2,1,0:T(8,128)(2,1)S(1)} %get-tuple-element.47), channel_id=1, source_target_pairs={{0,8},{8,0},{4,12},{12,4},{16,24},{24,16},{20,28},{28,20},{1,9},{9... | collective-permute-start | bytes 983048 | tf_op jit(solution)/shard_map/ppermute | solution.py:54
  35.9 6.1 %collective-permute-start.8 = (bf16[2,2,64,128]{3,2,1,0:T(8,128)(2,1)S(1)}, bf16[2,2,64,128]{3,2,1,0:T(8,128)(2,1)S(1)}, u32[]{:S(2)}, u32[]{:S(2)}) collective-permute-start(bf16[2,2,64,128]{3,2,1,0:T(8,128)(2,1)S(1)} %get-tuple-element.52), channel_id=1, source_target_pairs={{0,3},{1,2},{2,1},{3,0},{4,7},{5,6},{6,5},{7,4},{8,11},{9,10},{10,... | collective-permute-start | bytes 196616 | tf_op jit(solution)/shard_map/ppermute | solution.py:413
  38.3 13.9 %collective-permute-start.12 = (bf16[4,2,64,128]{3,2,1,0:T(8,128)(2,1)S(1)}, bf16[4,2,64,128]{3,2,1,0:T(8,128)(2,1)S(1)}, u32[]{:S(2)}, u32[]{:S(2)}) collective-permute-start(bf16[4,2,64,128]{3,2,1,0:T(8,128)(2,1)S(1)} %get-tuple-element.60), channel_id=1, source_target_pairs={{0,2},{1,3},{2,0},{3,1},{4,6},{5,7},{6,4},{7,5},{8,10},{9,11},{10,... | collective-permute-start | bytes 393224 | tf_op jit(solution)/shard_map/ppermute | solution.py:413
  42.9 17.8 %collective-permute-start.9 = (bf16[6,2,64,128]{3,2,1,0:T(8,128)(2,1)S(1)}, bf16[6,2,64,128]{3,2,1,0:T(8,128)(2,1)S(1)}, u32[]{:S(2)}, u32[]{:S(2)}) collective-permute-start(bf16[6,2,64,128]{3,2,1,0:T(8,128)(2,1)S(1)} %get-tuple-element.56), channel_id=1, source_target_pairs={{0,3},{1,2},{2,1},{3,0},{4,7},{5,6},{6,5},{7,4},{8,11},{9,10},{10,... | collective-permute-start | bytes 589832 | tf_op jit(solution)/shard_map/ppermute | solution.py:413
  45.3 15.4 %collective-permute-start.10 = (bf16[5,2,64,128]{3,2,1,0:T(8,128)(2,1)S(1)}, bf16[5,2,64,128]{3,2,1,0:T(8,128)(2,1)S(1)}, u32[]{:S(2)}, u32[]{:S(2)}) collective-permute-start(bf16[5,2,64,128]{3,2,1,0:T(8,128)(2,1)S(1)} %get-tuple-element.57), channel_id=1, source_target_pairs={{0,1},{1,0},{2,3},{3,2},{4,5},{5,4},{6,7},{7,6},{8,9},{9,8},{10,11... | collective-permute-start | bytes 491528 | tf_op jit(solution)/shard_map/ppermute | solution.py:413
  52.8 7.9 %collective-permute-start.13 = (bf16[4,2,64,128]{3,2,1,0:T(8,128)(2,1)S(1)}, bf16[4,2,64,128]{3,2,1,0:T(8,128)(2,1)S(1)}, u32[]{:S(2)}, u32[]{:S(2)}) collective-permute-start(bf16[4,2,64,128]{3,2,1,0:T(8,128)(2,1)S(1)} %late_wires.3), channel_id=1, source_target_pairs={{0,2},{1,3},{2,0},{3,1},{4,6},{5,7},{6,4},{7,5},{8,10},{9,11},{10,... | collective-permute-start | bytes 393224 | tf_op jit(solution)/shard_map/ppermute | solution.py:413
  52.9 4.9 %collective-permute-start.11 = (bf16[3,2,64,128]{3,2,1,0:T(8,128)(2,1)S(1)}, bf16[3,2,64,128]{3,2,1,0:T(8,128)(2,1)S(1)}, u32[]{:S(2)}, u32[]{:S(2)}) collective-permute-start(bf16[3,2,64,128]{3,2,1,0:T(8,128)(2,1)S(1)} %get-tuple-element.58), channel_id=1, source_target_pairs={{0,1},{1,0},{2,3},{3,2},{4,5},{5,4},{6,7},{7,6},{8,9},{9,8},{10,11... | collective-permute-start | bytes 294920 | tf_op jit(solution)/shard_map/ppermute | solution.py:413

commit v12 on v11

--- a/solution.py
+++ b/solution.py
@@ -52,6 +52,14 @@
         if high != low and high < count:
             route += [(low, high), (high, low)]
     return lax.ppermute(block, axis, route)
+
+
+def gathered_partner(block, axis, distance):
+    bit = 1 << distance
+    count = lax.axis_size(axis)
+    pairs = [[low, low | bit] for low in range(count) if not low & bit]
+    both = lax.all_gather(block, axis, axis_index_groups=pairs)
+    return table_row(both, 1 - (lax.axis_index(axis) >> distance) % 2)
 
 
 def dot(left, right):
@@ -475,7 +483,7 @@
     )
     other = partner(send, "aperture", 1)
     other, late = lax.optimization_barrier((other, late))
-    late = partner(late, "aperture", 1)
+    late = gathered_partner(late, "aperture", 1)
     summed, *group = wires(early_spans, me, target, rank, keep, other)
     received = spread(early_spans, group)
     from_odd, from_others = received[: len(odd)], received[len(odd) :]

time: 61.9 us -> 65.9 us (1.065)
  blocking collectives: 0 us -> 8.31 us
  starting transfers between devices: 20.1 us -> 17.7 us
  waiting for transfers between devices: 25.5 us -> 23.5 us
    all_gather x0 -> x1, blocking collectives: none -> 8.31 us  [gathered_partner(): both = lax.all_gather(block, axis, axis_index_groups=pairs)]
    ppermute x6, waiting for transfers between devices: 13.9 us -> 12 us  [spread(): received.append(lax.ppermute(wire, 'beam', route) if distance else wire)]
    ppermute x4 -> x3, starting transfers between devices: 4.62 us -> 3.13 us  [partner(): return lax.ppermute(block, axis, route)]
    ppermute x6, starting transfers between devices: 9.42 us -> 8.51 us  [spread(): received.append(lax.ppermute(wire, 'beam', route) if distance else wire)]
    ppermute x4 -> x3, waiting for transfers between devices: 5.03 us -> 4.87 us  [partner(): return lax.ppermute(block, axis, route)]
  transfers between devices with their start and end apart: 14 -> 13, of which waited for: 10 -> 8; matrix products, arithmetic and copies ran while one was open for 5% -> 5% of each run, Pallas kernels for 11% -> 10%
where the time goes in v12:
time: 65.9 us; the launch traced here: 65.7 us
  waiting for transfers between devices  23.5 us (36%)
  starting transfers between devices  17.7 us (27%)
  Pallas kernels  12.8 us (19%)
  blocking collectives  8.31 us (13%)
  local copies, waits for them, and re-layouts  2.27 us (3%)
  other arithmetic  1.11 us (2%)
    ppermute x6, waiting for transfers between devices, spread(): received.append(lax.ppermute(wire, 'beam', route) if distance else wire)  12 us
    ppermute x6, starting transfers between devices, spread(): received.append(lax.ppermute(wire, 'beam', route) if distance else wire)  8.51 us
    all_gather x1, blocking collectives, gathered_partner(): both = lax.all_gather(block, axis, axis_index_groups=pairs)  8.31 us
    ppermute x4, waiting for transfers between devices, trade_edges(): received.append(lax.ppermute(block, ('aperture', 'beam'), route))  6.64 us
    ppermute x4, starting transfers between devices, trade_edges(): received.append(lax.ppermute(block, ('aperture', 'beam'), route))  6.01 us
    ppermute x3, waiting for transfers between devices, partner(): return lax.ppermute(block, axis, route)  4.87 us
    ppermute x3, starting transfers between devices, partner(): return lax.ppermute(block, axis, route)  3.13 us
    pallas_call x2, Pallas kernels, first_level(): pl.pallas_call(functools.partial(first_level_kernel, column, rows), out_s...  2.66 us
  transfers between devices with their start and end apart: 13, of which 8 were waited for; matrix products, arithmetic and copies ran while one was open for 5% of the time, Pallas kernels for 10%

profile of v12, /device:TPU:0, one launch (start us, length us, event | category | flops | bytes accessed | tf_op | source)
XLA Modules:
  0.0 65.7 jit_solution(15014027011320994447)
XLA Ops:
  0.0 0.0 copy-start
  0.0 0.0 copy-start.2
  0.0 0.0 copy-start.1
  0.0 2.3 %resample.1 = (bf16[2,192,512]{2,1,0:T(8,128)(2,1)S(1)}, bf16[2,192,512]{2,1,0:T(8,128)(2,1)S(1)}) custom-call(bf16[2,256,512]{2,1,0:T(8,128)(2,1)} %bitcast.24, bf16[2,512,512]{2,1,0:T(8,128)(2,1)} %bitcast.23), custom_call_target="tpu_custom_call" | custom-call | flops 536870912 | bytes 2097152 | tf_op jit(solution)/shard_map/resample/pallas_call | solution.py:109
  2.3 3.1 %collective-permute-start = (bf16[2,192,512]{2,1,0:T(8,128)(2,1)S(1)}, bf16[2,192,512]{2,1,0:T(8,128)(2,1)S(1)}, u32[]{:S(2)}, u32[]{:S(2)}) collective-permute-start(bf16[2,192,512]{2,1,0:T(8,128)(2,1)S(1)} %get-tuple-element.34.sent_first_ref), channel_id=1, source_target_pairs={{0,1},{1,0},{2,3},{3,2},{4,5},{5,4},{6,7},{7,6},{8,9},{9,8},{10,11... | collective-permute-start | bytes 1179656 | tf_op jit(solution)/shard_map/ppermute | solution.py:43
  5.4 0.0 collective-permute-start.1
  5.4 0.0 copy-done
  5.4 1.5 %collective-permute-start.2 = (s32[1,16,1]{1,2,0:T(1,128)S(1)}, s32[1,16,1]{1,2,0:T(1,128)S(1)}, u32[]{:S(2)}, u32[]{:S(2)}) collective-permute-start(s32[1,16,1]{1,2,0:T(1,128)S(1)} %copy-done), channel_id=1, source_target_pairs={{0,8},{8,0},{4,12},{12,4},{16,24},{24,16},{20,28},{28,20},{1,9},{9... | collective-permute-start | bytes 200 | tf_op jit(solution)/shard_map/ppermute | solution.py:54
  6.9 0.0 copy-done.2
  6.9 0.2 subtract_reduce_fusion.starts_ref
  7.1 0.1 pad_add_fusion.side_ref
  7.2 0.0 copy-done.1
  7.2 0.4 copy.10
  7.6 1.4 %collective-permute-done.2 = s32[1,16,1]{1,2,0:T(1,128)S(1)} collective-permute-done((s32[1,16,1]{1,2,0:T(1,128)S(1)}, s32[1,16,1]{1,2,0:T(1,128)S(1)}, u32[]{:S(2)}, u32[]{:S(2)}) %collective-permute-start.2) | collective-permute-done | bytes 96 | tf_op jit(solution)/shard_map/ppermute | solution.py:54
  9.0 1.6 %plan.1 = (s32[16]{0:T(128)S(1)}, s32[16]{0:T(128)S(1)}, s32[16]{0:T(128)S(1)}, s32[16]{0:T(128)S(1)}, s32[16]{0:T(128)S(1)}) custom-call(s32[1]{0:T(128)} %bitcast.me_ref, s32[16]{0:T(128)S(1)} %bitcast.20, s32[16]{0:T(128)S(1)} %bitcast.21), custom_call_target="tpu_custom_call" | custom-call | tf_op jit(solution)/shard_map/plan/pallas_call | solution.py:312
  10.6 4.0 %collective-permute-done.first_ref = bf16[2,192,512]{2,1,0:T(8,128)(2,1)S(1)} collective-permute-done((bf16[2,192,512]{2,1,0:T(8,128)(2,1)S(1)}, bf16[2,192,512]{2,1,0:T(8,128)(2,1)S(1)}, u32[]{:S(2)}, u32[]{:S(2)}) %collective-permute-start) | collective-permute-done | bytes 393248 | tf_op jit(solution)/shard_map/ppermute | solution.py:43
  14.5 0.0 collective-permute-done.1.second_ref
  14.5 1.3 %first_level.3 = bf16[2,512,256]{2,1,0:T(8,128)(2,1)S(1)} custom-call(s32[4]{0:T(128)S(1)} %subtract_reduce_fusion.starts_ref, s32[3]{0:T(128)S(1)} %pad_add_fusion.side_ref, bf16[2,192,512]{2,1,0:T(8,128)(2,1)S(1)} %get-tuple-element.34.sent_first_ref, bf16[2,192,512]{2,1,0:T(8,128)(2,1)S(1)} %get-tuple-element.35.sent_second_ref, ...), custom_call_target="tpu_custom_call" | custom-call | flops 335544320 | bytes 2097152 | tf_op jit(solution)/shard_map/first_level/pallas_call | solution.py:179
  15.9 0.1 collective-permute-start.3
  16.0 1.3 %first_level.2 = bf16[2,512,256]{2,1,0:T(8,128)(2,1)S(1)} custom-call(s32[4]{0:T(128)S(1)} %subtract_reduce_fusion.starts_ref, s32[3]{0:T(128)S(1)} %pad_add_fusion.side_ref, bf16[2,192,512]{2,1,0:T(8,128)(2,1)S(1)} %get-tuple-element.34.sent_first_ref, bf16[2,192,512]{2,1,0:T(8,128)(2,1)S(1)} %get-tuple-element.35.sent_second_ref, ...), custom_call_target="tpu_custom_call" | custom-call | flops 335544320 | bytes 2097152 | tf_op jit(solution)/shard_map/first_level/pallas_call | solution.py:179
  17.3 0.5 collective-permute-done.3
  17.8 0.1 add_convert_fusion.own_ref
  18.0 2.9 %collective-permute-start.4 = (bf16[2,192,256]{2,1,0:T(8,128)(2,1)S(1)}, bf16[2,192,256]{2,1,0:T(8,128)(2,1)S(1)}, u32[]{:S(2)}, u32[]{:S(2)}) collective-permute-start(bf16[2,192,256]{2,1,0:T(8,128)(2,1)S(1)} %get-tuple-element.64), channel_id=1, source_target_pairs={{0,1},{1,0},{2,3},{3,2},{4,5},{5,4},{6,7},{7,6},{8,9},{9,8},{10,11... | collective-permute-start | bytes 589832 | tf_op jit(solution)/shard_map/ppermute | solution.py:43
  21.0 0.0 collective-permute-start.5
  21.0 1.8 %copy.11 = bf16[1,8,2,128,320]{4,3,2,1,0:T(8,128)(2,1)S(1)} copy(bf16[1,8,2,128,320]{3,4,2,1,0:T(8,128)(2,1)} %param.11) | data formatting | bytes 2621440 | tf_op args[4]
  22.8 0.7 %fusion.1.starts_ref = s32[8]{0:T(128)S(1)} fusion(s32[8,8]{1,0:T(8,128)} %param.12, s32[]{:T(128)S(6)} %select_n.27, s32[]{:T(128)S(6)} %sub.28), kind=kLoop, calls=%fused_computation.7 | loop fusion | flops 8 | bytes 72 | tf_op jit(solution)/shard_map/sub | solution.py:480
  23.5 2.7 %collective-permute-done.4.first_ref = bf16[2,192,256]{2,1,0:T(8,128)(2,1)S(1)} collective-permute-done((bf16[2,192,256]{2,1,0:T(8,128)(2,1)S(1)}, bf16[2,192,256]{2,1,0:T(8,128)(2,1)S(1)}, u32[]{:S(2)}, u32[]{:S(2)}) %collective-permute-start.4) | collective-permute-done | bytes 196640 | tf_op jit(solution)/shard_map/ppermute | solution.py:43
  26.2 0.0 collective-permute-done.5.second_ref
  26.2 1.1 %second_level_early.1 = bf16[6,2,64,128]{3,2,1,0:T(8,128)(2,1)S(1)} custom-call(s32[8]{0:T(128)S(1)} %fusion.1.starts_ref, s32[3]{0:T(128)S(1)} %pad_add_fusion.side_ref, s32[16]{0:T(128)S(1)} %get-tuple-element.41.sector_ref, bf16[2,512,256]{2,1,0:T(8,128)(2,1)S(1)} %add_convert_fusion.own_ref, bf16[2,192,256]{2,1,0:T(8,128)(2,1)S(1)} %collective-permute-done.4.first_ref, ...), custom_call_target="tpu_custom_call" | custom-call | flops 125829120 | bytes 1048576 | tf_op jit(solution)/shard_map/second_level_early/pallas_call | solution.py:245
  27.3 1.6 %collective-permute-start.6 = (bf16[6,2,64,128]{3,2,1,0:T(8,128)(2,1)S(1)}, bf16[6,2,64,128]{3,2,1,0:T(8,128)(2,1)S(1)}, u32[]{:S(2)}, u32[]{:S(2)}) collective-permute-start(bf16[6,2,64,128]{3,2,1,0:T(8,128)(2,1)S(1)} %second_level_early.1), channel_id=1, source_target_pairs={{0,8},{8,0},{4,12},{12,4},{16,24},{24,16},{20,28},{28,20},{1,9},{9... | collective-permute-start | bytes 589832 | tf_op jit(solution)/shard_map/ppermute | solution.py:54
  28.9 2.0 %second_level.1 = (bf16[16,2,64,128]{3,2,1,0:T(8,128)(2,1)S(1)}, bf16[10,2,64,128]{3,2,1,0:T(8,128)(2,1)S(1)}) custom-call(s32[8]{0:T(128)S(1)} %fusion.1.starts_ref, s32[3]{0:T(128)S(1)} %pad_add_fusion.side_ref, s32[16]{0:T(128)S(1)} %get-tuple-element.44.own_at_ref, s32[16]{0:T(128)S(1)} %get-tuple-element.45.other_at_ref, ...), custom_call_target="tpu_custom_call" | custom-call | flops 671088640 | bytes 4194304 | tf_op jit(solution)/shard_map/second_level/pallas_call | solution.py:256
  30.9 2.9 %collective-permute-done.6.refs_0_ = bf16[6,2,64,128]{3,2,1,0:T(8,128)(2,1)S(1)} collective-permute-done((bf16[6,2,64,128]{3,2,1,0:T(8,128)(2,1)S(1)}, bf16[6,2,64,128]{3,2,1,0:T(8,128)(2,1)S(1)}, u32[]{:S(2)}, u32[]{:S(2)}) %collective-permute-start.6) | collective-permute-done | bytes 196640 | tf_op jit(solution)/shard_map/ppermute | solution.py:54
  33.8 0.6 early_wires.1
  34.4 2.7 %collective-permute-start.11 = (bf16[4,2,64,128]{3,2,1,0:T(8,128)(2,1)S(1)}, bf16[4,2,64,128]{3,2,1,0:T(8,128)(2,1)S(1)}, u32[]{:S(2)}, u32[]{:S(2)}) collective-permute-start(bf16[4,2,64,128]{3,2,1,0:T(8,128)(2,1)S(1)} %get-tuple-element.60), channel_id=1, source_target_pairs={{0,2},{1,3},{2,0},{3,1},{4,6},{5,7},{6,4},{7,5},{8,10},{9,11},{10,... | collective-permute-start | bytes 393224 | tf_op jit(solution)/shard_map/ppermute | solution.py:421
  37.1 8.3 %all-gather = bf16[20,2,64,128]{3,2,1,0:T(8,128)(2,1)S(1)} all-gather(bf16[10,2,64,128]{3,2,1,0:T(8,128)(2,1)S(1)} %get-tuple-element.47), channel_id=2, replica_groups={{0,8},{4,12},{16,24},{20,28},{1,9},{5,13},{17,25},{21,29},{2,10},{6,14}..., dimensions={0}, use_global_device_ids=true | all-gather | bytes 983040 | tf_op jit(solution)/shard_map/all_gather | solution.py:61
  45.4 1.3 %collective-permute-start.7 = (bf16[2,2,64,128]{3,2,1,0:T(8,128)(2,1)S(1)}, bf16[2,2,64,128]{3,2,1,0:T(8,128)(2,1)S(1)}, u32[]{:S(2)}, u32[]{:S(2)}) collective-permute-start(bf16[2,2,64,128]{3,2,1,0:T(8,128)(2,1)S(1)} %get-tuple-element.52), channel_id=1, source_target_pairs={{0,3},{1,2},{2,1},{3,0},{4,7},{5,6},{6,5},{7,4},{8,11},{9,10},{10,... | collective-permute-start | bytes 196616 | tf_op jit(solution)/shard_map/ppermute | solution.py:421
  46.7 4.8 %collective-permute-done.7.refs_0_ = bf16[2,2,64,128]{3,2,1,0:T(8,128)(2,1)S(1)} collective-permute-done((bf16[2,2,64,128]{3,2,1,0:T(8,128)(2,1)S(1)}, bf16[2,2,64,128]{3,2,1,0:T(8,128)(2,1)S(1)}, u32[]{:S(2)}, u32[]{:S(2)}) %collective-permute-start.7) | collective-permute-done | bytes 65568 | tf_op jit(solution)/shard_map/ppermute | solution.py:421
  51.6 0.8 %late_wires.2 = (bf16[6,2,64,128]{3,2,1,0:T(8,128)(2,1)S(1)}, bf16[5,2,64,128]{3,2,1,0:T(8,128)(2,1)S(1)}, bf16[3,2,64,128]{3,2,1,0:T(8,128)(2,1)S(1)}, bf16[8,2,64,128]{3,2,1,0:T(8,128)(2,1)S(1)}) custom-call(s32[1]{0:T(128)} %bitcast.me_ref, s32[16]{0:T(128)S(1)} %get-tuple-element.48.target_ref, s32[16]{0:T(128)S(1)} %get-tuple-element.49.rank_ref, ...), custom_call_target="tpu_custom_call" | custom-call | bytes 2097152 | tf_op jit(solution)/shard_map/late_wires/pallas_call | solution.py:373
  52.3 1.4 %collective-permute-start.8 = (bf16[6,2,64,128]{3,2,1,0:T(8,128)(2,1)S(1)}, bf16[6,2,64,128]{3,2,1,0:T(8,128)(2,1)S(1)}, u32[]{:S(2)}, u32[]{:S(2)}) collective-permute-start(bf16[6,2,64,128]{3,2,1,0:T(8,128)(2,1)S(1)} %get-tuple-element.56), channel_id=1, source_target_pairs={{0,3},{1,2},{2,1},{3,0},{4,7},{5,6},{6,5},{7,4},{8,11},{9,10},{10,... | collective-permute-start | bytes 589832 | tf_op jit(solution)/shard_map/ppermute | solution.py:421
  53.7 0.0 collective-permute-start.9
  53.8 0.0 collective-permute-done.11.refs_5_
  53.8 0.6 late_wires.3
  54.4 3.1 %collective-permute-start.12 = (bf16[4,2,64,128]{3,2,1,0:T(8,128)(2,1)S(1)}, bf16[4,2,64,128]{3,2,1,0:T(8,128)(2,1)S(1)}, u32[]{:S(2)}, u32[]{:S(2)}) collective-permute-start(bf16[4,2,64,128]{3,2,1,0:T(8,128)(2,1)S(1)} %late_wires.3), channel_id=1, source_target_pairs={{0,2},{1,3},{2,0},{3,1},{4,6},{5,7},{6,4},{7,5},{8,10},{9,11},{10,... | collective-permute-start | bytes 393224 | tf_op jit(solution)/shard_map/ppermute | solution.py:421
  57.5 0.0 collective-permute-start.10
  57.5 6.8 %collective-permute-done.10.refs_3_ = bf16[3,2,64,128]{3,2,1,0:T(8,128)(2,1)S(1)} collective-permute-done((bf16[3,2,64,128]{3,2,1,0:T(8,128)(2,1)S(1)}, bf16[3,2,64,128]{3,2,1,0:T(8,128)(2,1)S(1)}, u32[]{:S(2)}, u32[]{:S(2)}) %collective-permute-start.10) | collective-permute-done | bytes 98336 | tf_op jit(solution)/shard_map/ppermute | solution.py:421
  64.3 0.0 collective-permute-done.9.refs_2_
  64.3 0.3 collective-permute-done.12.refs_6_
  64.7 0.0 collective-permute-done.8.refs_1_
  64.7 1.0 %collect.1 = bf16[32,2,64,128]{3,2,1,0:T(8,128)(2,1)} custom-call(s32[1]{0:T(128)} %bitcast.me_ref, bf16[2,2,64,128]{3,2,1,0:T(8,128)(2,1)S(1)} %collective-permute-done.7.refs_0_, bf16[6,2,64,128]{3,2,1,0:T(8,128)(2,1)S(1)} %collective-permute-done.8.refs_1_, bf16[5,2,64,128]{3,2,1,0:T(8,128)(2,1)S(1)} %collective-permute-done.9.refs_2_, ...), custom_call_target="tpu_custom_call" | custom-call | bytes 2097152 | tf_op jit(solution)/shard_map/collect/pallas_call | solution.py:404
  (2 shorter events, 0.1 us)
Async XLA Ops:
  0.0 5.4 %copy-start = (s32[1,16,1]{1,2,0:T(1,128)S(1)}, s32[1,16,1]{1,2,0:T(1,128)}, u32[]{:S(2)}) copy-start(s32[1,16,1]{1,2,0:T(1,128)} %param.13) | copy-start | bytes 196
  0.0 6.9 %copy-start.2 = (s32[8,4]{0,1:T(4,128)S(1)}, s32[8,4]{0,1:T(4,128)}, u32[]{:S(2)}) copy-start(s32[8,4]{0,1:T(4,128)} %param.10) | copy-start | bytes 388
  0.0 7.2 %copy-start.1 = (bf16[1,4,2,128,320]{3,4,2,1,0:T(8,128)(2,1)S(1)}, bf16[1,4,2,128,320]{3,4,2,1,0:T(8,128)(2,1)}, u32[]{:S(2)}) copy-start(bf16[1,4,2,128,320]{3,4,2,1,0:T(8,128)(2,1)} %param.9) | copy-start | bytes 1966084
  2.3 12.2 %collective-permute-start = (bf16[2,192,512]{2,1,0:T(8,128)(2,1)S(1)}, bf16[2,192,512]{2,1,0:T(8,128)(2,1)S(1)}, u32[]{:S(2)}, u32[]{:S(2)}) collective-permute-start(bf16[2,192,512]{2,1,0:T(8,128)(2,1)S(1)} %get-tuple-element.34.sent_first_ref), channel_id=1, source_target_pairs={{0,1},{1,0},{2,3},{3,2},{4,5},{5,4},{6,7},{7,6},{8,9},{9,8},{10,11... | collective-permute-start | bytes 1179656 | tf_op jit(solution)/shard_map/ppermute | solution.py:43
  5.4 9.1 %collective-permute-start.1 = (bf16[2,192,512]{2,1,0:T(8,128)(2,1)S(1)}, bf16[2,192,512]{2,1,0:T(8,128)(2,1)S(1)}, u32[]{:S(2)}, u32[]{:S(2)}) collective-permute-start(bf16[2,192,512]{2,1,0:T(8,128)(2,1)S(1)} %get-tuple-element.35.sent_second_ref), channel_id=1, source_target_pairs={{0,4},{1,2},{2,1},{3,7},{4,0},{5,6},{6,5},{7,3},{8,12},{9,10},{10,... | collective-permute-start | bytes 1179656 | tf_op jit(solution)/shard_map/ppermute | solution.py:43
  5.4 3.5 %collective-permute-start.2 = (s32[1,16,1]{1,2,0:T(1,128)S(1)}, s32[1,16,1]{1,2,0:T(1,128)S(1)}, u32[]{:S(2)}, u32[]{:S(2)}) collective-permute-start(s32[1,16,1]{1,2,0:T(1,128)S(1)} %copy-done), channel_id=1, source_target_pairs={{0,8},{8,0},{4,12},{12,4},{16,24},{24,16},{20,28},{28,20},{1,9},{9... | collective-permute-start | bytes 200 | tf_op jit(solution)/shard_map/ppermute | solution.py:54
  15.9 2.0 %collective-permute-start.3 = (bf16[2,512,256]{2,1,0:T(8,128)(2,1)S(1)}, bf16[2,512,256]{2,1,0:T(8,128)(2,1)S(1)}, u32[]{:S(2)}, u32[]{:S(2)}) collective-permute-start(bf16[2,512,256]{2,1,0:T(8,128)(2,1)S(1)} %first_level.3), channel_id=1, source_target_pairs={{0,4},{4,0},{8,12},{12,8},{16,20},{20,16},{24,28},{28,24},{1,5},{5... | collective-permute-start | bytes 1572872 | tf_op jit(solution)/shard_map/ppermute | solution.py:54
  18.0 8.1 %collective-permute-start.4 = (bf16[2,192,256]{2,1,0:T(8,128)(2,1)S(1)}, bf16[2,192,256]{2,1,0:T(8,128)(2,1)S(1)}, u32[]{:S(2)}, u32[]{:S(2)}) collective-permute-start(bf16[2,192,256]{2,1,0:T(8,128)(2,1)S(1)} %get-tuple-element.64), channel_id=1, source_target_pairs={{0,1},{1,0},{2,3},{3,2},{4,5},{5,4},{6,7},{7,6},{8,9},{9,8},{10,11... | collective-permute-start | bytes 589832 | tf_op jit(solution)/shard_map/ppermute | solution.py:43
  21.0 5.2 %collective-permute-start.5 = (bf16[2,192,256]{2,1,0:T(8,128)(2,1)S(1)}, bf16[2,192,256]{2,1,0:T(8,128)(2,1)S(1)}, u32[]{:S(2)}, u32[]{:S(2)}) collective-permute-start(bf16[2,192,256]{2,1,0:T(8,128)(2,1)S(1)} %get-tuple-element.63), channel_id=1, source_target_pairs={{0,4},{1,2},{2,1},{3,7},{4,0},{5,6},{6,5},{7,3},{8,12},{9,10},{10,... | collective-permute-start | bytes 589832 | tf_op jit(solution)/shard_map/ppermute | solution.py:43
  27.3 6.5 %collective-permute-start.6 = (bf16[6,2,64,128]{3,2,1,0:T(8,128)(2,1)S(1)}, bf16[6,2,64,128]{3,2,1,0:T(8,128)(2,1)S(1)}, u32[]{:S(2)}, u32[]{:S(2)}) collective-permute-start(bf16[6,2,64,128]{3,2,1,0:T(8,128)(2,1)S(1)} %second_level_early.1), channel_id=1, source_target_pairs={{0,8},{8,0},{4,12},{12,4},{16,24},{24,16},{20,28},{28,20},{1,9},{9... | collective-permute-start | bytes 589832 | tf_op jit(solution)/shard_map/ppermute | solution.py:54
  34.4 19.3 %collective-permute-start.11 = (bf16[4,2,64,128]{3,2,1,0:T(8,128)(2,1)S(1)}, bf16[4,2,64,128]{3,2,1,0:T(8,128)(2,1)S(1)}, u32[]{:S(2)}, u32[]{:S(2)}) collective-permute-start(bf16[4,2,64,128]{3,2,1,0:T(8,128)(2,1)S(1)} %get-tuple-element.60), channel_id=1, source_target_pairs={{0,2},{1,3},{2,0},{3,1},{4,6},{5,7},{6,4},{7,5},{8,10},{9,11},{10,... | collective-permute-start | bytes 393224 | tf_op jit(solution)/shard_map/ppermute | solution.py:421
  45.4 6.2 %collective-permute-start.7 = (bf16[2,2,64,128]{3,2,1,0:T(8,128)(2,1)S(1)}, bf16[2,2,64,128]{3,2,1,0:T(8,128)(2,1)S(1)}, u32[]{:S(2)}, u32[]{:S(2)}) collective-permute-start(bf16[2,2,64,128]{3,2,1,0:T(8,128)(2,1)S(1)} %get-tuple-element.52), channel_id=1, source_target_pairs={{0,3},{1,2},{2,1},{3,0},{4,7},{5,6},{6,5},{7,4},{8,11},{9,10},{10,... | collective-permute-start | bytes 196616 | tf_op jit(solution)/shard_map/ppermute | solution.py:421
  52.3 12.3 %collective-permute-start.8 = (bf16[6,2,64,128]{3,2,1,0:T(8,128)(2,1)S(1)}, bf16[6,2,64,128]{3,2,1,0:T(8,128)(2,1)S(1)}, u32[]{:S(2)}, u32[]{:S(2)}) collective-permute-start(bf16[6,2,64,128]{3,2,1,0:T(8,128)(2,1)S(1)} %get-tuple-element.56), channel_id=1, source_target_pairs={{0,3},{1,2},{2,1},{3,0},{4,7},{5,6},{6,5},{7,4},{8,11},{9,10},{10,... | collective-permute-start | bytes 589832 | tf_op jit(solution)/shard_map/ppermute | solution.py:421
  53.7 10.6 %collective-permute-start.9 = (bf16[5,2,64,128]{3,2,1,0:T(8,128)(2,1)S(1)}, bf16[5,2,64,128]{3,2,1,0:T(8,128)(2,1)S(1)}, u32[]{:S(2)}, u32[]{:S(2)}) collective-permute-start(bf16[5,2,64,128]{3,2,1,0:T(8,128)(2,1)S(1)} %get-tuple-element.57), channel_id=1, source_target_pairs={{0,1},{1,0},{2,3},{3,2},{4,5},{5,4},{6,7},{7,6},{8,9},{9,8},{10,11... | collective-permute-start | bytes 491528 | tf_op jit(solution)/shard_map/ppermute | solution.py:421
  54.4 10.3 %collective-permute-start.12 = (bf16[4,2,64,128]{3,2,1,0:T(8,128)(2,1)S(1)}, bf16[4,2,64,128]{3,2,1,0:T(8,128)(2,1)S(1)}, u32[]{:S(2)}, u32[]{:S(2)}) collective-permute-start(bf16[4,2,64,128]{3,2,1,0:T(8,128)(2,1)S(1)} %late_wires.3), channel_id=1, source_target_pairs={{0,2},{1,3},{2,0},{3,1},{4,6},{5,7},{6,4},{7,5},{8,10},{9,11},{10,... | collective-permute-start | bytes 393224 | tf_op jit(solution)/shard_map/ppermute | solution.py:421
  57.5 6.8 %collective-permute-start.10 = (bf16[3,2,64,128]{3,2,1,0:T(8,128)(2,1)S(1)}, bf16[3,2,64,128]{3,2,1,0:T(8,128)(2,1)S(1)}, u32[]{:S(2)}, u32[]{:S(2)}) collective-permute-start(bf16[3,2,64,128]{3,2,1,0:T(8,128)(2,1)S(1)} %get-tuple-element.58), channel_id=1, source_target_pairs={{0,1},{1,0},{2,3},{3,2},{4,5},{5,4},{6,7},{7,6},{8,9},{9,8},{10,11... | collective-permute-start | bytes 294920 | tf_op jit(solution)/shard_map/ppermute | solution.py:421

commit v13 on v6

--- a/solution.py
+++ b/solution.py
@@ -414,6 +414,39 @@
     return received
 
 
+def choose_tail(own_owners, common):
+    count, beam = lax.axis_size("beam"), lax.axis_index("beam")
+    targets = jnp.arange(count, dtype=jnp.int32)
+    sectors = jnp.sum((own_owners[:, None] == targets[None, :]).astype(jnp.int32), axis=0)
+    is_far = ((targets ^ beam) & (count // 2)) != 0
+    full = jnp.where((sectors > common) & is_far, 1, 0).astype(jnp.int32)
+    full = lax.pmax(full, ("aperture", "beam"))
+    return jnp.where(jnp.sum(full) > 1, count, jnp.argmax(full).astype(jnp.int32))
+
+
+def spread_tail(spans, branch, group):
+    count, apertures = lax.axis_size("beam"), lax.axis_size("aperture")
+
+    def only(target, wires_out):
+        received = []
+        for (distance, _, _), wire in zip(spans, wires_out):
+            pair = (target, target ^ distance)
+            route = []
+            for aper in range(apertures):
+                for place in range(count):
+                    if place in pair:
+                        to = aper * count + (place ^ distance)
+                    else:
+                        to = min(aper ^ 1, apertures - 1) * count + place
+                    route.append((aper * count + place, to))
+            received.append(lax.ppermute(wire, ("aperture", "beam"), route))
+        return received
+
+    branches = [functools.partial(only, target) for target in range(count)]
+    branches.append(functools.partial(spread, spans))
+    return lax.switch(branch, branches, group)
+
+
 def stacked_weights(weights):
     return weights[0].reshape(weights.shape[1], -1, weights.shape[4])
 
@@ -436,26 +469,24 @@
 
     sector_count = owners.shape[1]
     capacity = max(2, 2 * sector_count // beam_count)
-    shorter, longer = max(1, capacity // 4), max(1, capacity // 2)
+    common = (5 * capacity + 7) // 8
     far = range(beam_count // 2, beam_count)
-    odd = [distance for distance in far if distance % 2]
-    others = [distance for distance in far if distance % 2 == 0]
-    early = len(odd) * shorter + len(others) * longer
-    early_spans = [(distance, 0, shorter) for distance in odd]
-    early_spans += [(distance, 0, longer) for distance in others]
-    late_spans = [(distance, shorter, capacity) for distance in odd]
+    early_spans = [(distance, 0, common) for distance in far if distance % 2 == 0]
+    late_spans = [(distance, 0, common) for distance in far if distance % 2]
     for distance in range(1, beam_count // 2):
         late_spans += [(distance, 0, capacity // 2), (distance, capacity // 2, capacity)]
     late_spans.append((0, 0, capacity))
-    last_spans = [(distance, longer, capacity) for distance in others]
+    tail_spans = [(distance, common, capacity) for distance in far if common < capacity]
+    early = common * len(early_spans)
 
     sent = resample(subimages[0], range_kernel[0], margin)
     halos = trade_edges(*sent)
     own_owners = owners[0, :, 0]
     other_owners = partner(owners, "aperture", 1)[0, :, 0]
-    planned = plan(longer - shorter, me, own_owners, other_owners, beam_count)
+    planned = plan(common, me, own_owners, other_owners, beam_count)
     begin0 = table_row(starts0, aper_index) - (beam_index * local_blocks - MARGIN_BLOCKS)
-    halos, planned = lax.optimization_barrier((halos, planned))
+    branch = choose_tail(own_owners, common) if tail_spans else me
+    halos, planned, branch = lax.optimization_barrier((halos, planned, branch))
     *planned, target, rank = planned
     width = range_kernel.shape[3] // 2
     weights = stacked_weights(weights0)
@@ -477,14 +508,12 @@
     late = partner(late, "aperture", 1)
     summed, *group = wires(early_spans, me, target, rank, keep, other)
     received = spread(early_spans, group)
-    from_odd, from_others = received[: len(odd)], received[len(odd) :]
-    ready, from_odd = lax.optimization_barrier((late, from_odd))
-    group = wires(late_spans, me, target, rank, keep, ready, summed)
-    received = from_odd + spread(late_spans, group)
-    ready, from_others = lax.optimization_barrier((late, from_others))
-    group = wires(last_spans, me, target, rank, keep, ready, summed)
-    received += from_others + spread(last_spans, group)
-    spans = early_spans[: len(odd)] + late_spans + early_spans[len(odd) :] + last_spans
+    ready, received = lax.optimization_barrier((late, received))
+    group = wires(late_spans + tail_spans, me, target, rank, keep, ready, summed)
+    received += spread(late_spans, group[: len(late_spans)])
+    if tail_spans:
+        received += spread_tail(tail_spans, branch, group[len(late_spans) :])
+    spans = early_spans + late_spans + tail_spans
     return collect(spans, capacity, beam_count, me, received)[None]
 
 

time: 62.3 us -> 107 us (1.72); the launches traced: 62.2 us -> 105 us
  blocking collectives: 0 us -> 40.9 us
  Pallas kernels: 12.7 us -> 18.1 us
  starting transfers between devices: 20.3 us -> 15.4 us
  waiting for transfers between devices: 25.7 us -> 23.1 us
  other arithmetic: 1.1 us -> 3.63 us
  between operations: 0.14 us -> 1.45 us
    pmax x0 -> x1, blocking collectives: none -> 40.9 us  [choose_tail(): full = lax.pmax(full, ('aperture', 'beam'))]
    ppermute x0 -> x2, waiting for transfers between devices: none -> 6.4 us  [only(): received.append(lax.ppermute(wire, ('aperture', 'beam'), route))]
    pallas_call x1, Pallas kernels: 1.02 us -> 7.12 us  [collect(): pl.pallas_call(functools.partial(collect_kernel, spans, capacity), out_sh...]
    ppermute x6 -> x4, starting transfers between devices: 9.7 us -> 4.74 us  [spread(): received.append(lax.ppermute(wire, 'beam', route) if distance else wire)]
    ppermute x6 -> x4, waiting for transfers between devices: 14.1 us -> 10.1 us  [spread(): received.append(lax.ppermute(wire, 'beam', route) if distance else wire)]
    ppermute x4, starting transfers between devices: 6.01 us -> 3.36 us  [trade_edges(): received.append(lax.ppermute(block, ('aperture', 'beam'), route))]
    ppermute x4, waiting for transfers between devices: 4.95 us -> 2.41 us  [partner(): return lax.ppermute(block, axis, route)]
    ppermute x4, waiting for transfers between devices: 6.63 us -> 4.21 us  [trade_edges(): received.append(lax.ppermute(block, ('aperture', 'beam'), route))]
  transfers between devices with their start and end apart: 14 -> 14, of which waited for: 8 -> 7; matrix products, arithmetic and copies ran while one was open for 5% -> 4% of each run, Pallas kernels for 11% -> 5%
where the time goes in v13:
time: 107 us; the launch traced here: 105 us
  blocking collectives  40.9 us (38%)
  waiting for transfers between devices  23.1 us (22%)
  Pallas kernels  18.1 us (17%)
  starting transfers between devices  15.4 us (14%)
  other arithmetic  3.63 us (3%)
  local copies, waits for them, and re-layouts  2.23 us (2%)
  between operations  1.45 us (1%)
    pmax x1, blocking collectives, choose_tail(): full = lax.pmax(full, ('aperture', 'beam'))  40.9 us
    ppermute x4, waiting for transfers between devices, spread(): received.append(lax.ppermute(wire, 'beam', route) if distance else wire)  10.1 us
    pallas_call x1, Pallas kernels, collect(): pl.pallas_call(functools.partial(collect_kernel, spans, capacity), out_sh...  7.12 us
    ppermute x2, waiting for transfers between devices, only(): received.append(lax.ppermute(wire, ('aperture', 'beam'), route))  6.4 us
    ppermute x4, starting transfers between devices, partner(): return lax.ppermute(block, axis, route)  5.72 us
    ppermute x4, starting transfers between devices, spread(): received.append(lax.ppermute(wire, 'beam', route) if distance else wire)  4.74 us
    ppermute x4, waiting for transfers between devices, trade_edges(): received.append(lax.ppermute(block, ('aperture', 'beam'), route))  4.21 us
    ppermute x4, starting transfers between devices, trade_edges(): received.append(lax.ppermute(block, ('aperture', 'beam'), route))  3.36 us
  transfers between devices with their start and end apart: 14, of which 7 were waited for; matrix products, arithmetic and copies ran while one was open for 4% of the time, Pallas kernels for 5%

profile of v13, /device:TPU:0, one launch (start us, length us, event | category | flops | bytes accessed | tf_op | source)
XLA Modules:
  0.0 104.8 jit_solution(2962077219325866368)
XLA Ops:
  0.0 0.0 copy-start
  0.0 0.0 copy-start.1
  0.0 0.0 copy-start.2
  0.0 2.3 %resample.1 = (bf16[2,192,512]{2,1,0:T(8,128)(2,1)S(1)}, bf16[2,192,512]{2,1,0:T(8,128)(2,1)S(1)}) custom-call(bf16[2,256,512]{2,1,0:T(8,128)(2,1)} %bitcast.21, bf16[2,512,512]{2,1,0:T(8,128)(2,1)} %bitcast.20), custom_call_target="tpu_custom_call" | custom-call | flops 536870912 | bytes 2097152 | tf_op jit(solution)/shard_map/resample/pallas_call | solution.py:101
  2.3 3.1 %collective-permute-start.10 = (bf16[2,192,512]{2,1,0:T(8,128)(2,1)S(1)}, bf16[2,192,512]{2,1,0:T(8,128)(2,1)S(1)}, u32[]{:S(2)}, u32[]{:S(2)}) collective-permute-start(bf16[2,192,512]{2,1,0:T(8,128)(2,1)S(1)} %get-tuple-element.67.sent_first_ref), channel_id=1, source_target_pairs={{0,1},{1,0},{2,3},{3,2},{4,5},{5,4},{6,7},{7,6},{8,9},{9,8},{10,11... | collective-permute-start | bytes 1179656 | tf_op jit(solution)/shard_map/ppermute | solution.py:43
  5.4 0.0 collective-permute-start.11
  5.4 0.0 copy-done
  5.4 0.1 convert_reduce_fusion
  5.5 1.6 %collective-permute-start.12 = (s32[1,16,1]{1,2,0:T(1,128)S(1)}, s32[1,16,1]{1,2,0:T(1,128)S(1)}, u32[]{:S(2)}, u32[]{:S(2)}) collective-permute-start(s32[1,16,1]{1,2,0:T(1,128)S(1)} %copy-done), channel_id=1, source_target_pairs={{0,8},{8,0},{4,12},{12,4},{16,24},{24,16},{20,28},{28,20},{1,9},{9... | collective-permute-start | bytes 200 | tf_op jit(solution)/shard_map/ppermute | solution.py:54
  7.1 40.9 %pmax.7 = s32[4]{0:T(128)S(1)} all-reduce(s32[4]{0:T(128)S(1)} %and_select_fusion), channel_id=1, replica_groups=mesh['aperture'=8,'beam'=4] {'aperture','beam'}, use_global_device_ids=true, to_apply=%region_1.2 | all-reduce | flops 4 | bytes 32 | tf_op jit(solution)/shard_map/pmax | solution.py:423
  48.0 0.7 reduce_sum.19
  49.3 0.0 copy-done.1
  49.3 0.4 copy.10
  49.7 0.0 copy-done.2
  49.7 0.2 subtract_reduce_fusion.starts_ref
  49.9 0.1 pad_add_fusion.side_ref
  50.0 0.7 iota_reduce_fusion
  51.3 0.0 collective-permute-done.12
  51.3 1.6 %plan.1 = (s32[16]{0:T(128)S(1)}, s32[16]{0:T(128)S(1)}, s32[16]{0:T(128)S(1)}, s32[16]{0:T(128)S(1)}, s32[16]{0:T(128)S(1)}) custom-call(s32[1]{0:T(128)} %bitcast.me_ref, s32[16]{0:T(128)S(1)} %bitcast.18, s32[16]{0:T(128)S(1)} %bitcast.19), custom_call_target="tpu_custom_call" | custom-call | tf_op jit(solution)/shard_map/plan/pallas_call | solution.py:304
  52.9 0.0 collective-permute-done.10.first_ref
  52.9 0.0 collective-permute-done.11.second_ref
  52.9 1.3 %first_level.3 = bf16[2,512,256]{2,1,0:T(8,128)(2,1)S(1)} custom-call(s32[4]{0:T(128)S(1)} %subtract_reduce_fusion.starts_ref, s32[3]{0:T(128)S(1)} %pad_add_fusion.side_ref, bf16[2,192,512]{2,1,0:T(8,128)(2,1)S(1)} %get-tuple-element.67.sent_first_ref, bf16[2,192,512]{2,1,0:T(8,128)(2,1)S(1)} %get-tuple-element.68.sent_second_ref, ...), custom_call_target="tpu_custom_call" | custom-call | flops 335544320 | bytes 2097152 | tf_op jit(solution)/shard_map/first_level/pallas_call | solution.py:171
  54.3 0.1 collective-permute-start.13
  54.4 1.3 %first_level.2 = bf16[2,512,256]{2,1,0:T(8,128)(2,1)S(1)} custom-call(s32[4]{0:T(128)S(1)} %subtract_reduce_fusion.starts_ref, s32[3]{0:T(128)S(1)} %pad_add_fusion.side_ref, bf16[2,192,512]{2,1,0:T(8,128)(2,1)S(1)} %get-tuple-element.67.sent_first_ref, bf16[2,192,512]{2,1,0:T(8,128)(2,1)S(1)} %get-tuple-element.68.sent_second_ref, ...), custom_call_target="tpu_custom_call" | custom-call | flops 335544320 | bytes 2097152 | tf_op jit(solution)/shard_map/first_level/pallas_call | solution.py:171
  55.7 0.7 collective-permute-done.13
  56.4 1.2 %add_convert_fusion.own_ref = bf16[2,512,256]{2,1,0:T(8,128)(2,1)S(1)} fusion(bf16[2,512,256]{2,1,0:T(8,128)(2,1)} %collective-permute-done.13, bf16[2,512,256]{2,1,0:T(8,128)(2,1)S(1)} %first_level.2), kind=kLoop, calls=%fused_computation | loop fusion | flops 1048576 | bytes 1572864 | tf_op jit(solution)/shard_map/convert_element_type | solution.py:496
  57.6 0.1 collective-permute-start.14
  57.7 0.2 collective-permute-start.15
  57.9 1.8 %copy.11 = bf16[1,8,2,128,320]{4,3,2,1,0:T(8,128)(2,1)S(1)} copy(bf16[1,8,2,128,320]{3,4,2,1,0:T(8,128)(2,1)} %param.16) | data formatting | bytes 2621440 | tf_op args[4]
  59.7 0.7 fusion.1.starts_ref
  60.4 4.2 %collective-permute-done.14.first_ref = bf16[2,192,256]{2,1,0:T(8,128)(2,1)S(1)} collective-permute-done((bf16[2,192,256]{2,1,0:T(8,128)(2,1)S(1)}, bf16[2,192,256]{2,1,0:T(8,128)(2,1)S(1)}, u32[]{:S(2)}, u32[]{:S(2)}) %collective-permute-start.14) | collective-permute-done | bytes 196640 | tf_op jit(solution)/shard_map/ppermute | solution.py:43
  64.6 0.0 collective-permute-done.15.second_ref
  64.6 1.1 %second_level_early.1 = bf16[5,2,64,128]{3,2,1,0:T(8,128)(2,1)S(1)} custom-call(s32[8]{0:T(128)S(1)} %fusion.1.starts_ref, s32[3]{0:T(128)S(1)} %pad_add_fusion.side_ref, s32[16]{0:T(128)S(1)} %get-tuple-element.75.sector_ref, bf16[2,512,256]{2,1,0:T(8,128)(2,1)S(1)} %add_convert_fusion.own_ref, bf16[2,192,256]{2,1,0:T(8,128)(2,1)S(1)} %collective-permute-done.14.first_ref, ...), custom_call_target="tpu_custom_call" | custom-call | flops 104857600 | bytes 1048576 | tf_op jit(solution)/shard_map/second_level_early/pallas_call | solution.py:237
  65.7 2.4 %collective-permute-start.16 = (bf16[5,2,64,128]{3,2,1,0:T(8,128)(2,1)S(1)}, bf16[5,2,64,128]{3,2,1,0:T(8,128)(2,1)S(1)}, u32[]{:S(2)}, u32[]{:S(2)}) collective-permute-start(bf16[5,2,64,128]{3,2,1,0:T(8,128)(2,1)S(1)} %second_level_early.1), channel_id=1, source_target_pairs={{0,8},{8,0},{4,12},{12,4},{16,24},{24,16},{20,28},{28,20},{1,9},{9... | collective-permute-start | bytes 491528 | tf_op jit(solution)/shard_map/ppermute | solution.py:54
  68.0 1.9 %second_level.1 = (bf16[16,2,64,128]{3,2,1,0:T(8,128)(2,1)S(1)}, bf16[11,2,64,128]{3,2,1,0:T(8,128)(2,1)S(1)}) custom-call(s32[8]{0:T(128)S(1)} %fusion.1.starts_ref, s32[3]{0:T(128)S(1)} %pad_add_fusion.side_ref, s32[16]{0:T(128)S(1)} %get-tuple-element.78.own_at_ref, s32[16]{0:T(128)S(1)} %get-tuple-element.79.other_at_ref, ...), custom_call_target="tpu_custom_call" | custom-call | flops 671088640 | bytes 4194304 | tf_op jit(solution)/shard_map/second_level/pallas_call | solution.py:248
  70.0 1.7 %collective-permute-done.16.refs_0_ = bf16[5,2,64,128]{3,2,1,0:T(8,128)(2,1)S(1)} collective-permute-done((bf16[5,2,64,128]{3,2,1,0:T(8,128)(2,1)S(1)}, bf16[5,2,64,128]{3,2,1,0:T(8,128)(2,1)S(1)}, u32[]{:S(2)}, u32[]{:S(2)}) %collective-permute-start.16) | collective-permute-done | bytes 163872 | tf_op jit(solution)/shard_map/ppermute | solution.py:54
  71.7 1.7 %collective-permute-start.17 = (bf16[11,2,64,128]{3,2,1,0:T(8,128)(2,1)S(1)}, bf16[11,2,64,128]{3,2,1,0:T(8,128)(2,1)S(1)}, u32[]{:S(2)}, u32[]{:S(2)}) collective-permute-start(bf16[11,2,64,128]{3,2,1,0:T(8,128)(2,1)S(1)} %get-tuple-element.81), channel_id=1, source_target_pairs={{0,8},{8,0},{4,12},{12,4},{16,24},{24,16},{20,28},{28,20},{1,9},{9... | collective-permute-start | bytes 1081352 | tf_op jit(solution)/shard_map/ppermute | solution.py:54
  73.4 0.6 early_wires.1
  74.0 1.8 %collective-permute-start.18 = (bf16[5,2,64,128]{3,2,1,0:T(8,128)(2,1)S(1)}, bf16[5,2,64,128]{3,2,1,0:T(8,128)(2,1)S(1)}, u32[]{:S(2)}, u32[]{:S(2)}) collective-permute-start(bf16[5,2,64,128]{3,2,1,0:T(8,128)(2,1)S(1)} %get-tuple-element.86), channel_id=1, source_target_pairs={{0,2},{1,3},{2,0},{3,1},{4,6},{5,7},{6,4},{7,5},{8,10},{9,11},{10,... | collective-permute-start | bytes 491528 | tf_op jit(solution)/shard_map/ppermute | solution.py:413
  75.8 7.9 %collective-permute-done.18.refs_0_ = bf16[5,2,64,128]{3,2,1,0:T(8,128)(2,1)S(1)} collective-permute-done((bf16[5,2,64,128]{3,2,1,0:T(8,128)(2,1)S(1)}, bf16[5,2,64,128]{3,2,1,0:T(8,128)(2,1)S(1)}, u32[]{:S(2)}, u32[]{:S(2)}) %collective-permute-start.18) | collective-permute-done | bytes 163872 | tf_op jit(solution)/shard_map/ppermute | solution.py:413
  83.8 0.0 collective-permute-done.17.refs_0_
  83.8 0.9 late_wires.1
  84.6 0.9 collective-permute-start.19
  85.6 0.0 collective-permute-start.20
  85.6 2.0 %collective-permute-start.21 = (bf16[4,2,64,128]{3,2,1,0:T(8,128)(2,1)S(1)}, bf16[4,2,64,128]{3,2,1,0:T(8,128)(2,1)S(1)}, u32[]{:S(2)}, u32[]{:S(2)}) collective-permute-start(bf16[4,2,64,128]{3,2,1,0:T(8,128)(2,1)S(1)} %get-tuple-element.92), channel_id=1, source_target_pairs={{0,1},{1,0},{2,3},{3,2},{4,5},{5,4},{6,7},{7,6},{8,9},{9,8},{10,11... | collective-permute-start | bytes 393224 | tf_op jit(solution)/shard_map/ppermute | solution.py:413
  87.6 7.9 %conditional.1 = (bf16[3,2,64,128]{3,2,1,0:T(8,128)(2,1)}, bf16[3,2,64,128]{3,2,1,0:T(8,128)(2,1)}) conditional(s32[]{:T(128)} %clamp.3, (bf16[3,2,64,128]{3,2,1,0:T(8,128)(2,1)S(1)}, bf16[3,2,64,128]{3,2,1,0:T(8,128)(2,1)S(1)}) %tuple.33, (bf16[3,2,64,128]{3,2,1,0:T(8,128)(2,1)S(1)}, ...), branch_computations={%region_4.5_spmd, %region_5.6_spmd, %region_6.7_spmd, %region_7.8_... | conditional | bytes 786528 | solution.py:447
  87.6 1.5 %collective-permute-start.4 = (bf16[3,2,64,128]{3,2,1,0:T(8,128)(2,1)S(1)}, bf16[3,2,64,128]{3,2,1,0:T(8,128)(2,1)}, u32[]{:S(2)}, u32[]{:S(2)}) collective-permute-start(bf16[3,2,64,128]{3,2,1,0:T(8,128)(2,1)S(1)} %get-tuple-element.29), channel_id=1, source_target_pairs={{0,2},{1,5},{2,0},{3,7},{4,6},{5,1},{6,4},{7,3},{8,10},{9,13},{10,... | collective-permute-start | bytes 294920 | tf_op jit(solution)/shard_map/cond/branch_2_fun/ppermute | solution.py:442
  89.1 0.0 collective-permute-start.5
  89.1 6.4 %collective-permute-done.4 = bf16[3,2,64,128]{3,2,1,0:T(8,128)(2,1)} collective-permute-done((bf16[3,2,64,128]{3,2,1,0:T(8,128)(2,1)S(1)}, bf16[3,2,64,128]{3,2,1,0:T(8,128)(2,1)}, u32[]{:S(2)}, u32[]{:S(2)}) %collective-permute-start.4) | collective-permute-done | bytes 98336 | tf_op jit(solution)/shard_map/cond/branch_2_fun/ppermute | solution.py:442
  95.5 0.0 collective-permute-done.5
  95.5 0.2 collective-permute-done.20.refs_2_
  95.7 2.0 %collective-permute-done.21.refs_3_ = bf16[4,2,64,128]{3,2,1,0:T(8,128)(2,1)S(1)} collective-permute-done((bf16[4,2,64,128]{3,2,1,0:T(8,128)(2,1)S(1)}, bf16[4,2,64,128]{3,2,1,0:T(8,128)(2,1)S(1)}, u32[]{:S(2)}, u32[]{:S(2)}) %collective-permute-start.21) | collective-permute-done | bytes 131104 | tf_op jit(solution)/shard_map/ppermute | solution.py:413
  97.7 0.0 collective-permute-done.19.refs_1_
  97.7 7.1 %collect.1 = bf16[32,2,64,128]{3,2,1,0:T(8,128)(2,1)} custom-call(s32[1]{0:T(128)} %bitcast.me_ref, bf16[5,2,64,128]{3,2,1,0:T(8,128)(2,1)S(1)} %collective-permute-done.18.refs_0_, bf16[5,2,64,128]{3,2,1,0:T(8,128)(2,1)S(1)} %collective-permute-done.19.refs_1_, bf16[4,2,64,128]{3,2,1,0:T(8,128)(2,1)S(1)} %collective-permute-done.20.refs_2_, ...), custom_call_target="tpu_custom_call" | custom-call | bytes 2097152 | tf_op jit(solution)/shard_map/collect/pallas_call | solution.py:396
  (2 shorter events, 0.0 us)
Async XLA Ops:
  0.0 5.4 %copy-start = (s32[1,16,1]{1,2,0:T(1,128)S(1)}, s32[1,16,1]{1,2,0:T(1,128)}, u32[]{:S(2)}) copy-start(s32[1,16,1]{1,2,0:T(1,128)} %param.18) | copy-start | bytes 196
  0.0 49.3 %copy-start.1 = (bf16[1,4,2,128,320]{3,4,2,1,0:T(8,128)(2,1)S(1)}, bf16[1,4,2,128,320]{3,4,2,1,0:T(8,128)(2,1)}, u32[]{:S(2)}) copy-start(bf16[1,4,2,128,320]{3,4,2,1,0:T(8,128)(2,1)} %param.14) | copy-start | bytes 1966084
  0.0 49.7 %copy-start.2 = (s32[8,4]{0,1:T(4,128)S(1)}, s32[8,4]{0,1:T(4,128)}, u32[]{:S(2)}) copy-start(s32[8,4]{0,1:T(4,128)} %param.15) | copy-start | bytes 388
  2.3 50.6 %collective-permute-start.10 = (bf16[2,192,512]{2,1,0:T(8,128)(2,1)S(1)}, bf16[2,192,512]{2,1,0:T(8,128)(2,1)S(1)}, u32[]{:S(2)}, u32[]{:S(2)}) collective-permute-start(bf16[2,192,512]{2,1,0:T(8,128)(2,1)S(1)} %get-tuple-element.67.sent_first_ref), channel_id=1, source_target_pairs={{0,1},{1,0},{2,3},{3,2},{4,5},{5,4},{6,7},{7,6},{8,9},{9,8},{10,11... | collective-permute-start | bytes 1179656 | tf_op jit(solution)/shard_map/ppermute | solution.py:43
  5.4 47.5 %collective-permute-start.11 = (bf16[2,192,512]{2,1,0:T(8,128)(2,1)S(1)}, bf16[2,192,512]{2,1,0:T(8,128)(2,1)S(1)}, u32[]{:S(2)}, u32[]{:S(2)}) collective-permute-start(bf16[2,192,512]{2,1,0:T(8,128)(2,1)S(1)} %get-tuple-element.68.sent_second_ref), channel_id=1, source_target_pairs={{0,4},{1,2},{2,1},{3,7},{4,0},{5,6},{6,5},{7,3},{8,12},{9,10},{10,... | collective-permute-start | bytes 1179656 | tf_op jit(solution)/shard_map/ppermute | solution.py:43
  5.5 45.7 %collective-permute-start.12 = (s32[1,16,1]{1,2,0:T(1,128)S(1)}, s32[1,16,1]{1,2,0:T(1,128)S(1)}, u32[]{:S(2)}, u32[]{:S(2)}) collective-permute-start(s32[1,16,1]{1,2,0:T(1,128)S(1)} %copy-done), channel_id=1, source_target_pairs={{0,8},{8,0},{4,12},{12,4},{16,24},{24,16},{20,28},{28,20},{1,9},{9... | collective-permute-start | bytes 200 | tf_op jit(solution)/shard_map/ppermute | solution.py:54
  54.3 2.1 %collective-permute-start.13 = (bf16[2,512,256]{2,1,0:T(8,128)(2,1)S(1)}, bf16[2,512,256]{2,1,0:T(8,128)(2,1)}, u32[]{:S(2)}, u32[]{:S(2)}) collective-permute-start(bf16[2,512,256]{2,1,0:T(8,128)(2,1)S(1)} %first_level.3), channel_id=1, source_target_pairs={{0,4},{4,0},{8,12},{12,8},{16,20},{20,16},{24,28},{28,24},{1,5},{5... | collective-permute-start | bytes 1572872 | tf_op jit(solution)/shard_map/ppermute | solution.py:54
  57.6 7.0 %collective-permute-start.14 = (bf16[2,192,256]{2,1,0:T(8,128)(2,1)S(1)}, bf16[2,192,256]{2,1,0:T(8,128)(2,1)S(1)}, u32[]{:S(2)}, u32[]{:S(2)}) collective-permute-start(bf16[2,192,256]{2,1,0:T(8,128)(2,1)S(1)} %get-tuple-element.100), channel_id=1, source_target_pairs={{0,1},{1,0},{2,3},{3,2},{4,5},{5,4},{6,7},{7,6},{8,9},{9,8},{10,11... | collective-permute-start | bytes 589832 | tf_op jit(solution)/shard_map/ppermute | solution.py:43
  57.7 6.9 %collective-permute-start.15 = (bf16[2,192,256]{2,1,0:T(8,128)(2,1)S(1)}, bf16[2,192,256]{2,1,0:T(8,128)(2,1)S(1)}, u32[]{:S(2)}, u32[]{:S(2)}) collective-permute-start(bf16[2,192,256]{2,1,0:T(8,128)(2,1)S(1)} %get-tuple-element.99), channel_id=1, source_target_pairs={{0,4},{1,2},{2,1},{3,7},{4,0},{5,6},{6,5},{7,3},{8,12},{9,10},{10,... | collective-permute-start | bytes 589832 | tf_op jit(solution)/shard_map/ppermute | solution.py:43
  65.7 6.0 %collective-permute-start.16 = (bf16[5,2,64,128]{3,2,1,0:T(8,128)(2,1)S(1)}, bf16[5,2,64,128]{3,2,1,0:T(8,128)(2,1)S(1)}, u32[]{:S(2)}, u32[]{:S(2)}) collective-permute-start(bf16[5,2,64,128]{3,2,1,0:T(8,128)(2,1)S(1)} %second_level_early.1), channel_id=1, source_target_pairs={{0,8},{8,0},{4,12},{12,4},{16,24},{24,16},{20,28},{28,20},{1,9},{9... | collective-permute-start | bytes 491528 | tf_op jit(solution)/shard_map/ppermute | solution.py:54
  71.7 12.1 %collective-permute-start.17 = (bf16[11,2,64,128]{3,2,1,0:T(8,128)(2,1)S(1)}, bf16[11,2,64,128]{3,2,1,0:T(8,128)(2,1)S(1)}, u32[]{:S(2)}, u32[]{:S(2)}) collective-permute-start(bf16[11,2,64,128]{3,2,1,0:T(8,128)(2,1)S(1)} %get-tuple-element.81), channel_id=1, source_target_pairs={{0,8},{8,0},{4,12},{12,4},{16,24},{24,16},{20,28},{28,20},{1,9},{9... | collective-permute-start | bytes 1081352 | tf_op jit(solution)/shard_map/ppermute | solution.py:54
  74.0 9.7 %collective-permute-start.18 = (bf16[5,2,64,128]{3,2,1,0:T(8,128)(2,1)S(1)}, bf16[5,2,64,128]{3,2,1,0:T(8,128)(2,1)S(1)}, u32[]{:S(2)}, u32[]{:S(2)}) collective-permute-start(bf16[5,2,64,128]{3,2,1,0:T(8,128)(2,1)S(1)} %get-tuple-element.86), channel_id=1, source_target_pairs={{0,2},{1,3},{2,0},{3,1},{4,6},{5,7},{6,4},{7,5},{8,10},{9,11},{10,... | collective-permute-start | bytes 491528 | tf_op jit(solution)/shard_map/ppermute | solution.py:413
  84.6 13.1 %collective-permute-start.19 = (bf16[5,2,64,128]{3,2,1,0:T(8,128)(2,1)S(1)}, bf16[5,2,64,128]{3,2,1,0:T(8,128)(2,1)S(1)}, u32[]{:S(2)}, u32[]{:S(2)}) collective-permute-start(bf16[5,2,64,128]{3,2,1,0:T(8,128)(2,1)S(1)} %get-tuple-element.90), channel_id=1, source_target_pairs={{0,3},{1,2},{2,1},{3,0},{4,7},{5,6},{6,5},{7,4},{8,11},{9,10},{10,... | collective-permute-start | bytes 491528 | tf_op jit(solution)/shard_map/ppermute | solution.py:413
  85.6 10.2 %collective-permute-start.20 = (bf16[4,2,64,128]{3,2,1,0:T(8,128)(2,1)S(1)}, bf16[4,2,64,128]{3,2,1,0:T(8,128)(2,1)S(1)}, u32[]{:S(2)}, u32[]{:S(2)}) collective-permute-start(bf16[4,2,64,128]{3,2,1,0:T(8,128)(2,1)S(1)} %get-tuple-element.91), channel_id=1, source_target_pairs={{0,1},{1,0},{2,3},{3,2},{4,5},{5,4},{6,7},{7,6},{8,9},{9,8},{10,11... | collective-permute-start | bytes 393224 | tf_op jit(solution)/shard_map/ppermute | solution.py:413
  85.6 12.1 %collective-permute-start.21 = (bf16[4,2,64,128]{3,2,1,0:T(8,128)(2,1)S(1)}, bf16[4,2,64,128]{3,2,1,0:T(8,128)(2,1)S(1)}, u32[]{:S(2)}, u32[]{:S(2)}) collective-permute-start(bf16[4,2,64,128]{3,2,1,0:T(8,128)(2,1)S(1)} %get-tuple-element.92), channel_id=1, source_target_pairs={{0,1},{1,0},{2,3},{3,2},{4,5},{5,4},{6,7},{7,6},{8,9},{9,8},{10,11... | collective-permute-start | bytes 393224 | tf_op jit(solution)/shard_map/ppermute | solution.py:413
  87.6 7.9 %collective-permute-start.4 = (bf16[3,2,64,128]{3,2,1,0:T(8,128)(2,1)S(1)}, bf16[3,2,64,128]{3,2,1,0:T(8,128)(2,1)}, u32[]{:S(2)}, u32[]{:S(2)}) collective-permute-start(bf16[3,2,64,128]{3,2,1,0:T(8,128)(2,1)S(1)} %get-tuple-element.29), channel_id=1, source_target_pairs={{0,2},{1,5},{2,0},{3,7},{4,6},{5,1},{6,4},{7,3},{8,10},{9,13},{10,... | collective-permute-start | bytes 294920 | tf_op jit(solution)/shard_map/cond/branch_2_fun/ppermute | solution.py:442
  89.1 6.4 %collective-permute-start.5 = (bf16[3,2,64,128]{3,2,1,0:T(8,128)(2,1)S(1)}, bf16[3,2,64,128]{3,2,1,0:T(8,128)(2,1)}, u32[]{:S(2)}, u32[]{:S(2)}) collective-permute-start(bf16[3,2,64,128]{3,2,1,0:T(8,128)(2,1)S(1)} %get-tuple-element.30), channel_id=1, source_target_pairs={{0,4},{1,2},{2,1},{3,7},{4,0},{5,6},{6,5},{7,3},{8,12},{9,10},{10,... | collective-permute-start | bytes 294920 | tf_op jit(solution)/shard_map/cond/branch_2_fun/ppermute | solution.py:442

commit v14 on v11

--- a/solution.py
+++ b/solution.py
@@ -115,31 +115,37 @@
     )(child, kernel)
 
 
-def complex_window(weights, real, imag):
-    beams = weights.shape[0] // 2
-    with_real = dot(weights, real)
-    with_imag = dot(weights, imag)
+def complex_window(weights, window):
+    beams, width = weights.shape[0] // 2, window.shape[1] // 2
+    product = dot(weights, window)
     return (
-        (with_real[:beams] - with_imag[beams:]).astype(jnp.bfloat16),
-        (with_imag[:beams] + with_real[beams:]).astype(jnp.bfloat16),
+        (product[:beams, :width] - product[beams:, width:]).astype(jnp.bfloat16),
+        (product[:beams, width:] + product[beams:, :width]).astype(jnp.bfloat16),
     )
 
 
-def place_halos(padded, side_ref, rows, first, second):
+def place_rows(padded, start, source, columns):
+    width = padded.shape[1] // 2
+    for part in range(2):
+        target = slice(part * width, (part + 1) * width)
+        padded[pl.ds(start, source.shape[1]), target] = source[part, :, columns]
+
+
+def place_halos(padded, side_ref, rows, first_ref, second_ref, columns):
     even, lowest, highest = side_ref[0], side_ref[1], side_ref[2]
-    margin = first.shape[1]
+    margin = first_ref.shape[1]
     far = margin + rows
-    padded[:, pl.ds(pl.multiple_of(even * far, BLK), margin), :] = first
-    padded[:, pl.ds(pl.multiple_of((1 - even) * far, BLK), margin), :] = second
-    zeros = jnp.zeros_like(first)
+    place_rows(padded, pl.multiple_of(even * far, BLK), first_ref, columns)
+    place_rows(padded, pl.multiple_of((1 - even) * far, BLK), second_ref, columns)
+    zeros = jnp.zeros((margin, padded.shape[1]), padded.dtype)
 
     @pl.when(lowest == 1)
     def _():
-        padded[:, :margin, :] = zeros
+        padded[:margin, :] = zeros
 
     @pl.when(highest == 1)
     def _():
-        padded[:, far:, :] = zeros
+        padded[far:, :] = zeros
 
 
 def first_level_kernel(
@@ -153,12 +159,12 @@
     even = side_ref[0]
     tail = pl.multiple_of(margin + even * (rows - margin), BLK)
     head = pl.multiple_of(margin + (1 - even) * (rows - margin), BLK)
-    padded[:, pl.ds(tail, margin), :] = sent_first_ref[:, :, columns]
-    padded[:, pl.ds(head, margin), :] = sent_second_ref[:, :, columns]
-    place_halos(padded, side_ref, rows, first_ref[:, :, columns], second_ref[:, :, columns])
+    place_rows(padded, tail, sent_first_ref, columns)
+    place_rows(padded, head, sent_second_ref, columns)
+    place_halos(padded, side_ref, rows, first_ref, second_ref, columns)
     for sector in range(sectors):
         place = pl.ds(pl.multiple_of(starts_ref[sector] * BLK, BLK), window)
-        parts = complex_window(weights_ref[sector], padded[0, place, :], padded[1, place, :])
+        parts = complex_window(weights_ref[sector], padded[place, :])
         for part in range(2):
             out_ref[part, sector * beams : (sector + 1) * beams, :] = parts[part]
 
@@ -173,7 +179,7 @@
         out_shape=jax.ShapeDtypeStruct((2, sectors * stacked // 2, width), jnp.bfloat16),
         in_specs=[SMEM, SMEM] + [VMEM] * 5,
         out_specs=VMEM,
-        scratch_shapes=[pltpu.VMEM((2, rows + 2 * margin, width), jnp.bfloat16)],
+        scratch_shapes=[pltpu.VMEM((rows + 2 * margin, 2 * width), jnp.bfloat16)],
         compiler_params=params(),
         cost_estimate=cost(sectors * 2 * stacked * window * width, 2**21),
         name="first_level",
@@ -187,8 +193,8 @@
     per = stacked // 2 // OS
     margin, rows = first_ref.shape[1], own_ref.shape[1]
     columns = slice(send_ref.shape[3], 2 * send_ref.shape[3])
-    padded[:, margin : margin + rows, :] = own_ref[:, :, columns]
-    place_halos(padded, side_ref, rows, first_ref[:, :, columns], second_ref[:, :, columns])
+    place_rows(padded, margin, own_ref, columns)
+    place_halos(padded, side_ref, rows, first_ref, second_ref, columns)
     for place in range(send_ref.shape[0]):
         sector = sector_ref[place] // per
         piece = pl.multiple_of(sector_ref[place] % per * OS, OS)
@@ -199,7 +205,7 @@
                 weights_ref[sector, pl.ds(pl.multiple_of(piece + stacked // 2, OS), OS), :],
             ]
         )
-        parts = complex_window(weights, padded[0, window_rows, :], padded[1, window_rows, :])
+        parts = complex_window(weights, padded[window_rows, :])
         for part in range(2):
             send_ref[place, part] = parts[part]
 
@@ -212,12 +218,13 @@
     beams = stacked // 2
     width = keep_ref.shape[3]
     margin, rows = first_ref.shape[1], own_ref.shape[1]
-    padded[:, margin : margin + rows, :] = own_ref[...]
-    place_halos(padded, side_ref, rows, first_ref[...], second_ref[...])
+    columns = slice(0, 2 * width)
+    place_rows(padded, margin, own_ref, columns)
+    place_halos(padded, side_ref, rows, first_ref, second_ref, columns)
     per = beams // OS
     for sector in range(sectors):
         place = pl.ds(pl.multiple_of(starts_ref[sector] * BLK, BLK), window)
-        parts = complex_window(weights_ref[sector], padded[0, place, :], padded[1, place, :])
+        parts = complex_window(weights_ref[sector], padded[place, :])
         for piece in range(per):
             own_at = own_at_ref[sector * per + piece]
             other_at = other_at_ref[sector * per + piece]
@@ -239,7 +246,7 @@
         out_shape=jax.ShapeDtypeStruct((early,) + block, jnp.bfloat16),
         in_specs=[SMEM] * 3 + [VMEM] * 4,
         out_specs=VMEM,
-        scratch_shapes=[pltpu.VMEM((2, rows + 2 * margin, rng // 2), jnp.bfloat16)],
+        scratch_shapes=[pltpu.VMEM((rows + 2 * margin, rng), jnp.bfloat16)],
         compiler_params=params(),
         cost_estimate=cost(early * 2 * 2 * OS * window * rng // 2, 2**20),
         name="second_level_early",
@@ -251,7 +258,7 @@
         in_specs=[SMEM] * 4 + [VMEM] * 4,
         out_specs=[VMEM] * 2,
         scratch_shapes=[
-            pltpu.VMEM((2, rows + 2 * margin, rng), jnp.bfloat16),
+            pltpu.VMEM((rows + 2 * margin, 2 * rng), jnp.bfloat16),
             pltpu.VMEM((count,) + block, jnp.bfloat16),
         ],
         compiler_params=params(),

time: 61.9 us -> 61.9 us (level)
  no operation moved by 1% of the time
where the time goes in v14:
time: 61.9 us; the launch traced here: 61.7 us
  waiting for transfers between devices  25.5 us (41%)
  starting transfers between devices  20 us (32%)
  Pallas kernels  12.6 us (20%)
  local copies, waits for them, and re-layouts  2.24 us (4%)
  other arithmetic  1.1 us (2%)
    ppermute x6, waiting for transfers between devices, spread(): received.append(lax.ppermute(wire, 'beam', route) if distance else wire)  13.9 us
    ppermute x6, starting transfers between devices, spread(): received.append(lax.ppermute(wire, 'beam', route) if distance else wire)  9.42 us
    ppermute x4, waiting for transfers between devices, trade_edges(): received.append(lax.ppermute(block, ('aperture', 'beam'), route))  6.63 us
    ppermute x4, starting transfers between devices, trade_edges(): received.append(lax.ppermute(block, ('aperture', 'beam'), route))  6.01 us
    ppermute x4, waiting for transfers between devices, partner(): return lax.ppermute(block, axis, route)  5.03 us
    ppermute x4, starting transfers between devices, partner(): return lax.ppermute(block, axis, route)  4.6 us
    pallas_call x2, Pallas kernels, first_level(): pl.pallas_call(functools.partial(first_level_kernel, column, rows), out_s...  2.68 us
    pallas_call x1, Pallas kernels, resample(): pl.pallas_call(resample_kernel, out_shape=(shape, shape), in_specs=[ANY,...  2.31 us
  transfers between devices with their start and end apart: 14, of which 10 were waited for; matrix products, arithmetic and copies ran while one was open for 5% of the time, Pallas kernels for 11%

profile of v14, /device:TPU:0, one launch (start us, length us, event | category | flops | bytes accessed | tf_op | source)
XLA Modules:
  0.0 61.7 jit_solution(12373179453869137780)
XLA Ops:
  0.0 0.0 copy-start
  0.0 0.0 copy-start.2
  0.0 0.0 copy-start.1
  0.0 2.3 %resample.1 = (bf16[2,192,512]{2,1,0:T(8,128)(2,1)S(1)}, bf16[2,192,512]{2,1,0:T(8,128)(2,1)S(1)}) custom-call(bf16[2,256,512]{2,1,0:T(8,128)(2,1)} %bitcast.20, bf16[2,512,512]{2,1,0:T(8,128)(2,1)} %bitcast.19), custom_call_target="tpu_custom_call" | custom-call | flops 536870912 | bytes 2097152 | tf_op jit(solution)/shard_map/resample/pallas_call | solution.py:101
  2.3 3.1 %collective-permute-start = (bf16[2,192,512]{2,1,0:T(8,128)(2,1)S(1)}, bf16[2,192,512]{2,1,0:T(8,128)(2,1)S(1)}, u32[]{:S(2)}, u32[]{:S(2)}) collective-permute-start(bf16[2,192,512]{2,1,0:T(8,128)(2,1)S(1)} %get-tuple-element.34.sent_first_ref), channel_id=1, source_target_pairs={{0,1},{1,0},{2,3},{3,2},{4,5},{5,4},{6,7},{7,6},{8,9},{9,8},{10,11... | collective-permute-start | bytes 1179656 | tf_op jit(solution)/shard_map/ppermute | solution.py:43
  5.4 0.0 collective-permute-start.1
  5.4 0.0 copy-done
  5.4 1.5 %collective-permute-start.2 = (s32[1,16,1]{1,2,0:T(1,128)S(1)}, s32[1,16,1]{1,2,0:T(1,128)S(1)}, u32[]{:S(2)}, u32[]{:S(2)}) collective-permute-start(s32[1,16,1]{1,2,0:T(1,128)S(1)} %copy-done), channel_id=1, source_target_pairs={{0,8},{8,0},{4,12},{12,4},{16,24},{24,16},{20,28},{28,20},{1,9},{9... | collective-permute-start | bytes 200 | tf_op jit(solution)/shard_map/ppermute | solution.py:54
  6.9 0.0 copy-done.2
  6.9 0.2 subtract_reduce_fusion.starts_ref
  7.1 0.1 pad_add_fusion.side_ref
  7.2 0.0 copy-done.1
  7.2 0.4 copy.8
  7.6 1.4 %collective-permute-done.2 = s32[1,16,1]{1,2,0:T(1,128)S(1)} collective-permute-done((s32[1,16,1]{1,2,0:T(1,128)S(1)}, s32[1,16,1]{1,2,0:T(1,128)S(1)}, u32[]{:S(2)}, u32[]{:S(2)}) %collective-permute-start.2) | collective-permute-done | bytes 96 | tf_op jit(solution)/shard_map/ppermute | solution.py:54
  9.0 1.6 %plan.1 = (s32[16]{0:T(128)S(1)}, s32[16]{0:T(128)S(1)}, s32[16]{0:T(128)S(1)}, s32[16]{0:T(128)S(1)}, s32[16]{0:T(128)S(1)}) custom-call(s32[1]{0:T(128)} %bitcast.me_ref, s32[16]{0:T(128)S(1)} %bitcast.17, s32[16]{0:T(128)S(1)} %bitcast.18), custom_call_target="tpu_custom_call" | custom-call | tf_op jit(solution)/shard_map/plan/pallas_call | solution.py:311
  10.6 4.0 %collective-permute-done.first_ref = bf16[2,192,512]{2,1,0:T(8,128)(2,1)S(1)} collective-permute-done((bf16[2,192,512]{2,1,0:T(8,128)(2,1)S(1)}, bf16[2,192,512]{2,1,0:T(8,128)(2,1)S(1)}, u32[]{:S(2)}, u32[]{:S(2)}) %collective-permute-start) | collective-permute-done | bytes 393248 | tf_op jit(solution)/shard_map/ppermute | solution.py:43
  14.5 0.0 collective-permute-done.1.second_ref
  14.5 1.3 %first_level.3 = bf16[2,512,256]{2,1,0:T(8,128)(2,1)S(1)} custom-call(s32[4]{0:T(128)S(1)} %subtract_reduce_fusion.starts_ref, s32[3]{0:T(128)S(1)} %pad_add_fusion.side_ref, bf16[2,192,512]{2,1,0:T(8,128)(2,1)S(1)} %get-tuple-element.34.sent_first_ref, bf16[2,192,512]{2,1,0:T(8,128)(2,1)S(1)} %get-tuple-element.35.sent_second_ref, ...), custom_call_target="tpu_custom_call" | custom-call | flops 335544320 | bytes 2097152 | tf_op jit(solution)/shard_map/first_level/pallas_call | solution.py:177
  15.9 0.1 collective-permute-start.3
  16.0 1.3 %first_level.2 = bf16[2,512,256]{2,1,0:T(8,128)(2,1)S(1)} custom-call(s32[4]{0:T(128)S(1)} %subtract_reduce_fusion.starts_ref, s32[3]{0:T(128)S(1)} %pad_add_fusion.side_ref, bf16[2,192,512]{2,1,0:T(8,128)(2,1)S(1)} %get-tuple-element.34.sent_first_ref, bf16[2,192,512]{2,1,0:T(8,128)(2,1)S(1)} %get-tuple-element.35.sent_second_ref, ...), custom_call_target="tpu_custom_call" | custom-call | flops 335544320 | bytes 2097152 | tf_op jit(solution)/shard_map/first_level/pallas_call | solution.py:177
  17.3 0.5 collective-permute-done.3
  17.9 0.1 add_convert_fusion.own_ref
  18.0 2.9 %collective-permute-start.4 = (bf16[2,192,256]{2,1,0:T(8,128)(2,1)S(1)}, bf16[2,192,256]{2,1,0:T(8,128)(2,1)S(1)}, u32[]{:S(2)}, u32[]{:S(2)}) collective-permute-start(bf16[2,192,256]{2,1,0:T(8,128)(2,1)S(1)} %get-tuple-element.64), channel_id=1, source_target_pairs={{0,1},{1,0},{2,3},{3,2},{4,5},{5,4},{6,7},{7,6},{8,9},{9,8},{10,11... | collective-permute-start | bytes 589832 | tf_op jit(solution)/shard_map/ppermute | solution.py:43
  21.0 0.0 collective-permute-start.5
  21.0 1.8 %copy.9 = bf16[1,8,2,128,320]{4,3,2,1,0:T(8,128)(2,1)S(1)} copy(bf16[1,8,2,128,320]{3,4,2,1,0:T(8,128)(2,1)} %param.11) | data formatting | bytes 2621440 | tf_op args[4]
  22.8 0.7 %fusion.1.starts_ref = s32[8]{0:T(128)S(1)} fusion(s32[8,8]{1,0:T(8,128)} %param.12, s32[]{:T(128)S(6)} %select_n.19, s32[]{:T(128)S(6)} %sub.25), kind=kLoop, calls=%fused_computation.6 | loop fusion | flops 8 | bytes 72 | tf_op jit(solution)/shard_map/sub | solution.py:479
  23.5 2.7 %collective-permute-done.4.first_ref = bf16[2,192,256]{2,1,0:T(8,128)(2,1)S(1)} collective-permute-done((bf16[2,192,256]{2,1,0:T(8,128)(2,1)S(1)}, bf16[2,192,256]{2,1,0:T(8,128)(2,1)S(1)}, u32[]{:S(2)}, u32[]{:S(2)}) %collective-permute-start.4) | collective-permute-done | bytes 196640 | tf_op jit(solution)/shard_map/ppermute | solution.py:43
  26.2 0.0 collective-permute-done.5.second_ref
  26.2 1.0 %second_level_early.1 = bf16[6,2,64,128]{3,2,1,0:T(8,128)(2,1)S(1)} custom-call(s32[8]{0:T(128)S(1)} %fusion.1.starts_ref, s32[3]{0:T(128)S(1)} %pad_add_fusion.side_ref, s32[16]{0:T(128)S(1)} %get-tuple-element.41.sector_ref, bf16[2,512,256]{2,1,0:T(8,128)(2,1)S(1)} %add_convert_fusion.own_ref, bf16[2,192,256]{2,1,0:T(8,128)(2,1)S(1)} %collective-permute-done.4.first_ref, ...), custom_call_target="tpu_custom_call" | custom-call | flops 125829120 | bytes 1048576 | tf_op jit(solution)/shard_map/second_level_early/pallas_call | solution.py:244
  27.2 1.6 %collective-permute-start.6 = (bf16[6,2,64,128]{3,2,1,0:T(8,128)(2,1)S(1)}, bf16[6,2,64,128]{3,2,1,0:T(8,128)(2,1)S(1)}, u32[]{:S(2)}, u32[]{:S(2)}) collective-permute-start(bf16[6,2,64,128]{3,2,1,0:T(8,128)(2,1)S(1)} %second_level_early.1), channel_id=1, source_target_pairs={{0,8},{8,0},{4,12},{12,4},{16,24},{24,16},{20,28},{28,20},{1,9},{9... | collective-permute-start | bytes 589832 | tf_op jit(solution)/shard_map/ppermute | solution.py:54
  28.8 1.9 %second_level.1 = (bf16[16,2,64,128]{3,2,1,0:T(8,128)(2,1)S(1)}, bf16[10,2,64,128]{3,2,1,0:T(8,128)(2,1)S(1)}) custom-call(s32[8]{0:T(128)S(1)} %fusion.1.starts_ref, s32[3]{0:T(128)S(1)} %pad_add_fusion.side_ref, s32[16]{0:T(128)S(1)} %get-tuple-element.44.own_at_ref, s32[16]{0:T(128)S(1)} %get-tuple-element.45.other_at_ref, ...), custom_call_target="tpu_custom_call" | custom-call | flops 671088640 | bytes 4194304 | tf_op jit(solution)/shard_map/second_level/pallas_call | solution.py:255
  30.7 3.0 %collective-permute-done.6.refs_0_ = bf16[6,2,64,128]{3,2,1,0:T(8,128)(2,1)S(1)} collective-permute-done((bf16[6,2,64,128]{3,2,1,0:T(8,128)(2,1)S(1)}, bf16[6,2,64,128]{3,2,1,0:T(8,128)(2,1)S(1)}, u32[]{:S(2)}, u32[]{:S(2)}) %collective-permute-start.6) | collective-permute-done | bytes 196640 | tf_op jit(solution)/shard_map/ppermute | solution.py:54
  33.7 1.5 %collective-permute-start.7 = (bf16[10,2,64,128]{3,2,1,0:T(8,128)(2,1)S(1)}, bf16[10,2,64,128]{3,2,1,0:T(8,128)(2,1)S(1)}, u32[]{:S(2)}, u32[]{:S(2)}) collective-permute-start(bf16[10,2,64,128]{3,2,1,0:T(8,128)(2,1)S(1)} %get-tuple-element.47), channel_id=1, source_target_pairs={{0,8},{8,0},{4,12},{12,4},{16,24},{24,16},{20,28},{28,20},{1,9},{9... | collective-permute-start | bytes 983048 | tf_op jit(solution)/shard_map/ppermute | solution.py:54
  35.2 0.6 early_wires.1
  35.8 2.4 %collective-permute-start.8 = (bf16[2,2,64,128]{3,2,1,0:T(8,128)(2,1)S(1)}, bf16[2,2,64,128]{3,2,1,0:T(8,128)(2,1)S(1)}, u32[]{:S(2)}, u32[]{:S(2)}) collective-permute-start(bf16[2,2,64,128]{3,2,1,0:T(8,128)(2,1)S(1)} %get-tuple-element.52), channel_id=1, source_target_pairs={{0,3},{1,2},{2,1},{3,0},{4,7},{5,6},{6,5},{7,4},{8,11},{9,10},{10,... | collective-permute-start | bytes 196616 | tf_op jit(solution)/shard_map/ppermute | solution.py:420
  38.2 0.6 %collective-permute-start.12 = (bf16[4,2,64,128]{3,2,1,0:T(8,128)(2,1)S(1)}, bf16[4,2,64,128]{3,2,1,0:T(8,128)(2,1)S(1)}, u32[]{:S(2)}, u32[]{:S(2)}) collective-permute-start(bf16[4,2,64,128]{3,2,1,0:T(8,128)(2,1)S(1)} %get-tuple-element.60), channel_id=1, source_target_pairs={{0,2},{1,3},{2,0},{3,1},{4,6},{5,7},{6,4},{7,5},{8,10},{9,11},{10,... | collective-permute-start | bytes 393224 | tf_op jit(solution)/shard_map/ppermute | solution.py:420
  38.8 3.1 %collective-permute-done.8.refs_0_ = bf16[2,2,64,128]{3,2,1,0:T(8,128)(2,1)S(1)} collective-permute-done((bf16[2,2,64,128]{3,2,1,0:T(8,128)(2,1)S(1)}, bf16[2,2,64,128]{3,2,1,0:T(8,128)(2,1)S(1)}, u32[]{:S(2)}, u32[]{:S(2)}) %collective-permute-start.8) | collective-permute-done | bytes 65568 | tf_op jit(solution)/shard_map/ppermute | solution.py:420
  41.9 0.1 collective-permute-done.7.refs_0_
  42.0 0.8 %late_wires.2 = (bf16[6,2,64,128]{3,2,1,0:T(8,128)(2,1)S(1)}, bf16[5,2,64,128]{3,2,1,0:T(8,128)(2,1)S(1)}, bf16[3,2,64,128]{3,2,1,0:T(8,128)(2,1)S(1)}, bf16[8,2,64,128]{3,2,1,0:T(8,128)(2,1)S(1)}) custom-call(s32[1]{0:T(128)} %bitcast.me_ref, s32[16]{0:T(128)S(1)} %get-tuple-element.48.target_ref, s32[16]{0:T(128)S(1)} %get-tuple-element.49.rank_ref, ...), custom_call_target="tpu_custom_call" | custom-call | bytes 2097152 | tf_op jit(solution)/shard_map/late_wires/pallas_call | solution.py:372
  42.8 2.4 %collective-permute-start.9 = (bf16[6,2,64,128]{3,2,1,0:T(8,128)(2,1)S(1)}, bf16[6,2,64,128]{3,2,1,0:T(8,128)(2,1)S(1)}, u32[]{:S(2)}, u32[]{:S(2)}) collective-permute-start(bf16[6,2,64,128]{3,2,1,0:T(8,128)(2,1)S(1)} %get-tuple-element.56), channel_id=1, source_target_pairs={{0,3},{1,2},{2,1},{3,0},{4,7},{5,6},{6,5},{7,4},{8,11},{9,10},{10,... | collective-permute-start | bytes 589832 | tf_op jit(solution)/shard_map/ppermute | solution.py:420
  45.2 1.7 %collective-permute-start.10 = (bf16[5,2,64,128]{3,2,1,0:T(8,128)(2,1)S(1)}, bf16[5,2,64,128]{3,2,1,0:T(8,128)(2,1)S(1)}, u32[]{:S(2)}, u32[]{:S(2)}) collective-permute-start(bf16[5,2,64,128]{3,2,1,0:T(8,128)(2,1)S(1)} %get-tuple-element.57), channel_id=1, source_target_pairs={{0,1},{1,0},{2,3},{3,2},{4,5},{5,4},{6,7},{7,6},{8,9},{9,8},{10,11... | collective-permute-start | bytes 491528 | tf_op jit(solution)/shard_map/ppermute | solution.py:420
  47.0 5.1 %collective-permute-done.12.refs_5_ = bf16[4,2,64,128]{3,2,1,0:T(8,128)(2,1)S(1)} collective-permute-done((bf16[4,2,64,128]{3,2,1,0:T(8,128)(2,1)S(1)}, bf16[4,2,64,128]{3,2,1,0:T(8,128)(2,1)S(1)}, u32[]{:S(2)}, u32[]{:S(2)}) %collective-permute-start.12) | collective-permute-done | bytes 131104 | tf_op jit(solution)/shard_map/ppermute | solution.py:420
  52.1 0.6 %late_wires.3 = bf16[4,2,64,128]{3,2,1,0:T(8,128)(2,1)S(1)} custom-call(s32[1]{0:T(128)} %bitcast.me_ref, s32[16]{0:T(128)S(1)} %get-tuple-element.48.target_ref, s32[16]{0:T(128)S(1)} %get-tuple-element.49.rank_ref, bf16[16,2,64,128]{3,2,1,0:T(8,128)(2,1)S(1)} %get-tuple-element.50.keep_ref, bf16[10,2,64,128]{3,2,1,0:T(8,128)(2,1)S(1)} %collective-permute-done.7.refs_0_, ...), custom_call_target="tpu_custom_call" | custom-call | bytes 2097152 | tf_op jit(solution)/shard_map/late_wires/pallas_call | solution.py:372
  52.7 0.1 collective-permute-start.13
  52.8 2.2 %collective-permute-start.11 = (bf16[3,2,64,128]{3,2,1,0:T(8,128)(2,1)S(1)}, bf16[3,2,64,128]{3,2,1,0:T(8,128)(2,1)S(1)}, u32[]{:S(2)}, u32[]{:S(2)}) collective-permute-start(bf16[3,2,64,128]{3,2,1,0:T(8,128)(2,1)S(1)} %get-tuple-element.58), channel_id=1, source_target_pairs={{0,1},{1,0},{2,3},{3,2},{4,5},{5,4},{6,7},{7,6},{8,9},{9,8},{10,11... | collective-permute-start | bytes 294920 | tf_op jit(solution)/shard_map/ppermute | solution.py:420
  55.0 2.7 %collective-permute-done.11.refs_3_ = bf16[3,2,64,128]{3,2,1,0:T(8,128)(2,1)S(1)} collective-permute-done((bf16[3,2,64,128]{3,2,1,0:T(8,128)(2,1)S(1)}, bf16[3,2,64,128]{3,2,1,0:T(8,128)(2,1)S(1)}, u32[]{:S(2)}, u32[]{:S(2)}) %collective-permute-start.11) | collective-permute-done | bytes 98336 | tf_op jit(solution)/shard_map/ppermute | solution.py:420
  57.7 2.9 %collective-permute-done.13.refs_6_ = bf16[4,2,64,128]{3,2,1,0:T(8,128)(2,1)S(1)} collective-permute-done((bf16[4,2,64,128]{3,2,1,0:T(8,128)(2,1)S(1)}, bf16[4,2,64,128]{3,2,1,0:T(8,128)(2,1)S(1)}, u32[]{:S(2)}, u32[]{:S(2)}) %collective-permute-start.13) | collective-permute-done | bytes 131104 | tf_op jit(solution)/shard_map/ppermute | solution.py:420
  60.6 0.0 collective-permute-done.10.refs_2_
  60.6 0.0 collective-permute-done.9.refs_1_
  60.7 1.0 %collect.1 = bf16[32,2,64,128]{3,2,1,0:T(8,128)(2,1)} custom-call(s32[1]{0:T(128)} %bitcast.me_ref, bf16[2,2,64,128]{3,2,1,0:T(8,128)(2,1)S(1)} %collective-permute-done.8.refs_0_, bf16[6,2,64,128]{3,2,1,0:T(8,128)(2,1)S(1)} %collective-permute-done.9.refs_1_, bf16[5,2,64,128]{3,2,1,0:T(8,128)(2,1)S(1)} %collective-permute-done.10.refs_2_, ...), custom_call_target="tpu_custom_call" | custom-call | bytes 2097152 | tf_op jit(solution)/shard_map/collect/pallas_call | solution.py:403
  (1 shorter events, 0.0 us)
Async XLA Ops:
  0.0 5.4 %copy-start = (s32[1,16,1]{1,2,0:T(1,128)S(1)}, s32[1,16,1]{1,2,0:T(1,128)}, u32[]{:S(2)}) copy-start(s32[1,16,1]{1,2,0:T(1,128)} %param.13) | copy-start | bytes 196
  0.0 6.9 %copy-start.2 = (s32[8,4]{0,1:T(4,128)S(1)}, s32[8,4]{0,1:T(4,128)}, u32[]{:S(2)}) copy-start(s32[8,4]{0,1:T(4,128)} %param.10) | copy-start | bytes 388
  0.0 7.2 %copy-start.1 = (bf16[1,4,2,128,320]{3,4,2,1,0:T(8,128)(2,1)S(1)}, bf16[1,4,2,128,320]{3,4,2,1,0:T(8,128)(2,1)}, u32[]{:S(2)}) copy-start(bf16[1,4,2,128,320]{3,4,2,1,0:T(8,128)(2,1)} %param.9) | copy-start | bytes 1966084
  2.3 12.2 %collective-permute-start = (bf16[2,192,512]{2,1,0:T(8,128)(2,1)S(1)}, bf16[2,192,512]{2,1,0:T(8,128)(2,1)S(1)}, u32[]{:S(2)}, u32[]{:S(2)}) collective-permute-start(bf16[2,192,512]{2,1,0:T(8,128)(2,1)S(1)} %get-tuple-element.34.sent_first_ref), channel_id=1, source_target_pairs={{0,1},{1,0},{2,3},{3,2},{4,5},{5,4},{6,7},{7,6},{8,9},{9,8},{10,11... | collective-permute-start | bytes 1179656 | tf_op jit(solution)/shard_map/ppermute | solution.py:43
  5.4 9.1 %collective-permute-start.1 = (bf16[2,192,512]{2,1,0:T(8,128)(2,1)S(1)}, bf16[2,192,512]{2,1,0:T(8,128)(2,1)S(1)}, u32[]{:S(2)}, u32[]{:S(2)}) collective-permute-start(bf16[2,192,512]{2,1,0:T(8,128)(2,1)S(1)} %get-tuple-element.35.sent_second_ref), channel_id=1, source_target_pairs={{0,4},{1,2},{2,1},{3,7},{4,0},{5,6},{6,5},{7,3},{8,12},{9,10},{10,... | collective-permute-start | bytes 1179656 | tf_op jit(solution)/shard_map/ppermute | solution.py:43
  5.4 3.5 %collective-permute-start.2 = (s32[1,16,1]{1,2,0:T(1,128)S(1)}, s32[1,16,1]{1,2,0:T(1,128)S(1)}, u32[]{:S(2)}, u32[]{:S(2)}) collective-permute-start(s32[1,16,1]{1,2,0:T(1,128)S(1)} %copy-done), channel_id=1, source_target_pairs={{0,8},{8,0},{4,12},{12,4},{16,24},{24,16},{20,28},{28,20},{1,9},{9... | collective-permute-start | bytes 200 | tf_op jit(solution)/shard_map/ppermute | solution.py:54
  15.9 2.0 %collective-permute-start.3 = (bf16[2,512,256]{2,1,0:T(8,128)(2,1)S(1)}, bf16[2,512,256]{2,1,0:T(8,128)(2,1)S(1)}, u32[]{:S(2)}, u32[]{:S(2)}) collective-permute-start(bf16[2,512,256]{2,1,0:T(8,128)(2,1)S(1)} %first_level.3), channel_id=1, source_target_pairs={{0,4},{4,0},{8,12},{12,8},{16,20},{20,16},{24,28},{28,24},{1,5},{5... | collective-permute-start | bytes 1572872 | tf_op jit(solution)/shard_map/ppermute | solution.py:54
  18.0 8.1 %collective-permute-start.4 = (bf16[2,192,256]{2,1,0:T(8,128)(2,1)S(1)}, bf16[2,192,256]{2,1,0:T(8,128)(2,1)S(1)}, u32[]{:S(2)}, u32[]{:S(2)}) collective-permute-start(bf16[2,192,256]{2,1,0:T(8,128)(2,1)S(1)} %get-tuple-element.64), channel_id=1, source_target_pairs={{0,1},{1,0},{2,3},{3,2},{4,5},{5,4},{6,7},{7,6},{8,9},{9,8},{10,11... | collective-permute-start | bytes 589832 | tf_op jit(solution)/shard_map/ppermute | solution.py:43
  21.0 5.2 %collective-permute-start.5 = (bf16[2,192,256]{2,1,0:T(8,128)(2,1)S(1)}, bf16[2,192,256]{2,1,0:T(8,128)(2,1)S(1)}, u32[]{:S(2)}, u32[]{:S(2)}) collective-permute-start(bf16[2,192,256]{2,1,0:T(8,128)(2,1)S(1)} %get-tuple-element.63), channel_id=1, source_target_pairs={{0,4},{1,2},{2,1},{3,7},{4,0},{5,6},{6,5},{7,3},{8,12},{9,10},{10,... | collective-permute-start | bytes 589832 | tf_op jit(solution)/shard_map/ppermute | solution.py:43
  27.2 6.5 %collective-permute-start.6 = (bf16[6,2,64,128]{3,2,1,0:T(8,128)(2,1)S(1)}, bf16[6,2,64,128]{3,2,1,0:T(8,128)(2,1)S(1)}, u32[]{:S(2)}, u32[]{:S(2)}) collective-permute-start(bf16[6,2,64,128]{3,2,1,0:T(8,128)(2,1)S(1)} %second_level_early.1), channel_id=1, source_target_pairs={{0,8},{8,0},{4,12},{12,4},{16,24},{24,16},{20,28},{28,20},{1,9},{9... | collective-permute-start | bytes 589832 | tf_op jit(solution)/shard_map/ppermute | solution.py:54
  33.7 8.3 %collective-permute-start.7 = (bf16[10,2,64,128]{3,2,1,0:T(8,128)(2,1)S(1)}, bf16[10,2,64,128]{3,2,1,0:T(8,128)(2,1)S(1)}, u32[]{:S(2)}, u32[]{:S(2)}) collective-permute-start(bf16[10,2,64,128]{3,2,1,0:T(8,128)(2,1)S(1)} %get-tuple-element.47), channel_id=1, source_target_pairs={{0,8},{8,0},{4,12},{12,4},{16,24},{24,16},{20,28},{28,20},{1,9},{9... | collective-permute-start | bytes 983048 | tf_op jit(solution)/shard_map/ppermute | solution.py:54
  35.8 6.1 %collective-permute-start.8 = (bf16[2,2,64,128]{3,2,1,0:T(8,128)(2,1)S(1)}, bf16[2,2,64,128]{3,2,1,0:T(8,128)(2,1)S(1)}, u32[]{:S(2)}, u32[]{:S(2)}) collective-permute-start(bf16[2,2,64,128]{3,2,1,0:T(8,128)(2,1)S(1)} %get-tuple-element.52), channel_id=1, source_target_pairs={{0,3},{1,2},{2,1},{3,0},{4,7},{5,6},{6,5},{7,4},{8,11},{9,10},{10,... | collective-permute-start | bytes 196616 | tf_op jit(solution)/shard_map/ppermute | solution.py:420
  38.2 13.9 %collective-permute-start.12 = (bf16[4,2,64,128]{3,2,1,0:T(8,128)(2,1)S(1)}, bf16[4,2,64,128]{3,2,1,0:T(8,128)(2,1)S(1)}, u32[]{:S(2)}, u32[]{:S(2)}) collective-permute-start(bf16[4,2,64,128]{3,2,1,0:T(8,128)(2,1)S(1)} %get-tuple-element.60), channel_id=1, source_target_pairs={{0,2},{1,3},{2,0},{3,1},{4,6},{5,7},{6,4},{7,5},{8,10},{9,11},{10,... | collective-permute-start | bytes 393224 | tf_op jit(solution)/shard_map/ppermute | solution.py:420
  42.8 17.8 %collective-permute-start.9 = (bf16[6,2,64,128]{3,2,1,0:T(8,128)(2,1)S(1)}, bf16[6,2,64,128]{3,2,1,0:T(8,128)(2,1)S(1)}, u32[]{:S(2)}, u32[]{:S(2)}) collective-permute-start(bf16[6,2,64,128]{3,2,1,0:T(8,128)(2,1)S(1)} %get-tuple-element.56), channel_id=1, source_target_pairs={{0,3},{1,2},{2,1},{3,0},{4,7},{5,6},{6,5},{7,4},{8,11},{9,10},{10,... | collective-permute-start | bytes 589832 | tf_op jit(solution)/shard_map/ppermute | solution.py:420
  45.2 15.4 %collective-permute-start.10 = (bf16[5,2,64,128]{3,2,1,0:T(8,128)(2,1)S(1)}, bf16[5,2,64,128]{3,2,1,0:T(8,128)(2,1)S(1)}, u32[]{:S(2)}, u32[]{:S(2)}) collective-permute-start(bf16[5,2,64,128]{3,2,1,0:T(8,128)(2,1)S(1)} %get-tuple-element.57), channel_id=1, source_target_pairs={{0,1},{1,0},{2,3},{3,2},{4,5},{5,4},{6,7},{7,6},{8,9},{9,8},{10,11... | collective-permute-start | bytes 491528 | tf_op jit(solution)/shard_map/ppermute | solution.py:420
  52.7 7.9 %collective-permute-start.13 = (bf16[4,2,64,128]{3,2,1,0:T(8,128)(2,1)S(1)}, bf16[4,2,64,128]{3,2,1,0:T(8,128)(2,1)S(1)}, u32[]{:S(2)}, u32[]{:S(2)}) collective-permute-start(bf16[4,2,64,128]{3,2,1,0:T(8,128)(2,1)S(1)} %late_wires.3), channel_id=1, source_target_pairs={{0,2},{1,3},{2,0},{3,1},{4,6},{5,7},{6,4},{7,5},{8,10},{9,11},{10,... | collective-permute-start | bytes 393224 | tf_op jit(solution)/shard_map/ppermute | solution.py:420
  52.8 4.9 %collective-permute-start.11 = (bf16[3,2,64,128]{3,2,1,0:T(8,128)(2,1)S(1)}, bf16[3,2,64,128]{3,2,1,0:T(8,128)(2,1)S(1)}, u32[]{:S(2)}, u32[]{:S(2)}) collective-permute-start(bf16[3,2,64,128]{3,2,1,0:T(8,128)(2,1)S(1)} %get-tuple-element.58), channel_id=1, source_target_pairs={{0,1},{1,0},{2,3},{3,2},{4,5},{5,4},{6,7},{7,6},{8,9},{9,8},{10,11... | collective-permute-start | bytes 294920 | tf_op jit(solution)/shard_map/ppermute | solution.py:420

commit v15 on v14

--- a/solution.py
+++ b/solution.py
@@ -27,14 +27,14 @@
     return pl.CostEstimate(flops=2 * macs, bytes_accessed=moved, transcendentals=0)
 
 
-def trade_edges(first, second):
+def trade_edges(first, second, inner):
     count, apertures = lax.axis_size("beam"), lax.axis_size("aperture")
     received = []
     for order, block in enumerate((first, second)):
         route = []
         for aper in range(apertures):
             for place in range(count):
-                other = place + 1 if (place - order) % 2 == 0 else place - 1
+                other = place + 1 if (place - order - inner) % 2 == 0 else place - 1
                 if 0 <= other < count:
                     to = aper * count + other
                 else:
@@ -61,7 +61,7 @@
 def resample_kernel(child_hbm, kernel_hbm, first_ref, second_ref, child, kernel, own, sems):
     aper, beam = lax.axis_index("aperture"), lax.axis_index("beam")
     half, quarter = aper & 1, (aper >> 1) & 1
-    even = 1 - (beam & 1)
+    even = beam & 1
     rows, rng = child.shape[1:]
     piece = rng // 4
     child_copy = pltpu.make_async_copy(child_hbm, child, sems.at[4])
@@ -438,7 +438,8 @@
     local_blocks = rows // BLK
     even = (beam_index + 1) % 2
     ends = (beam_index == 0, beam_index == beam_count - 1)
-    side = jnp.stack([even] + [end.astype(jnp.int32) for end in ends])
+    ends = [end.astype(jnp.int32) for end in ends]
+    inner_side, side = jnp.stack([1 - even] + ends), jnp.stack([even] + ends)
     me = beam_index.reshape(1)
 
     sector_count = owners.shape[1]
@@ -458,7 +459,7 @@
     last_spans = [(distance, longer, capacity) for distance in others]
 
     sent = resample(subimages[0], range_kernel[0], margin)
-    halos = trade_edges(*sent)
+    halos = trade_edges(*sent, 1)
     own_owners = owners[0, :, 0]
     other_owners = partner(owners, "aperture", 1)[0, :, 0]
     planned = plan(longer - shorter, me, own_owners, other_owners, beam_count)
@@ -467,15 +468,15 @@
     *planned, target, rank = planned
     width = range_kernel.shape[3] // 2
     weights = stacked_weights(weights0)
-    send = first_level(width, rows, begin0, side, sent, halos, weights)
+    send = first_level(width, rows, begin0, inner_side, sent, halos, weights)
     other = partner(send, "aperture", 0)
-    keep = first_level(0, rows, begin0, side, sent, halos, weights)
+    keep = first_level(0, rows, begin0, inner_side, sent, halos, weights)
     level_one = (keep.astype(jnp.float32) + other.astype(jnp.float32)).astype(jnp.bfloat16)
 
     beams = level_one.shape[1]
     first = lax.dynamic_slice_in_dim(level_one, even * (beams - margin), margin, 1)
     second = lax.dynamic_slice_in_dim(level_one, (1 - even) * (beams - margin), margin, 1)
-    halos = trade_edges(first, second)
+    halos = trade_edges(first, second, 0)
     begin1 = table_row(starts1, aper_index) - (beam_index * 2 * local_blocks - MARGIN_BLOCKS)
     keep, send, late = second_level(
         begin1, side, planned, level_one, halos, stacked_weights(weights1), early

time: 61.9 us -> 67.5 us (1.090)
  starting transfers between devices: 20 us -> 22.5 us
  local copies, waits for them, and re-layouts: 2.24 us -> 4.35 us
  other arithmetic: 1.1 us -> 2.2 us
  waiting for transfers between devices: 25.5 us -> 24.6 us
  Pallas kernels: 12.6 us -> 13.4 us
    unnamed x8 -> x24, local copies, waits for them, and re-layouts: 2.2 us -> 4.31 us
    ppermute x6, starting transfers between devices: 9.42 us -> 11.3 us  [spread(): received.append(lax.ppermute(wire, 'beam', route) if distance else wire)]
    convert_element_type x1, other arithmetic: 0.14 us -> 1.17 us  [local(): (keep.astype(jnp.float32) + other.astype(jnp.float32)).astype(jnp.bfloat16)]
    ppermute x6, waiting for transfers between devices: 13.9 us -> 12.9 us  [spread(): received.append(lax.ppermute(wire, 'beam', route) if distance else wire)]
    pallas_call x2, Pallas kernels: 2.68 us -> 3.45 us  [first_level(): pl.pallas_call(functools.partial(first_level_kernel, column, rows), out_s...]
  transfers between devices with their start and end apart: 14 -> 14, of which waited for: 10 -> 8; matrix products, arithmetic and copies ran while one was open for 5% -> 5% of each run, Pallas kernels for 11% -> 10%
where the time goes in v15:
time: 67.5 us; the launch traced here: 67.3 us
  waiting for transfers between devices  24.6 us (36%)
  starting transfers between devices  22.5 us (33%)
  Pallas kernels  13.4 us (20%)
  local copies, waits for them, and re-layouts  4.35 us (6%)
  other arithmetic  2.2 us (3%)
    ppermute x6, waiting for transfers between devices, spread(): received.append(lax.ppermute(wire, 'beam', route) if distance else wire)  12.9 us
    ppermute x6, starting transfers between devices, spread(): received.append(lax.ppermute(wire, 'beam', route) if distance else wire)  11.3 us
    ppermute x4, waiting for transfers between devices, trade_edges(): received.append(lax.ppermute(block, ('aperture', 'beam'), route))  7.18 us
    ppermute x4, starting transfers between devices, trade_edges(): received.append(lax.ppermute(block, ('aperture', 'beam'), route))  6.67 us
    ppermute x4, starting transfers between devices, partner(): return lax.ppermute(block, axis, route)  4.54 us
    ppermute x4, waiting for transfers between devices, partner(): return lax.ppermute(block, axis, route)  4.5 us
    unnamed x24, local copies, waits for them, and re-layouts  4.31 us
    pallas_call x2, Pallas kernels, first_level(): pl.pallas_call(functools.partial(first_level_kernel, column, rows), out_s...  3.45 us
  transfers between devices with their start and end apart: 14, of which 8 were waited for; matrix products, arithmetic and copies ran while one was open for 5% of the time, Pallas kernels for 10%

profile of v15, /device:TPU:0, one launch (start us, length us, event | category | flops | bytes accessed | tf_op | source)
XLA Modules:
  0.0 67.3 jit_solution(3410615088102549992)
XLA Ops:
  0.0 0.0 copy-start.8
  0.0 0.0 copy-start.10
  0.0 0.0 copy-start.9
  0.0 2.3 %resample.1 = (bf16[2,192,512]{2,1,0:T(8,128)(2,1)S(1)}, bf16[2,192,512]{2,1,0:T(8,128)(2,1)S(1)}) custom-call(bf16[2,256,512]{2,1,0:T(8,128)(2,1)} %bitcast.21, bf16[2,512,512]{2,1,0:T(8,128)(2,1)} %bitcast.20), custom_call_target="tpu_custom_call" | custom-call | flops 536870912 | bytes 2097152 | tf_op jit(solution)/shard_map/resample/pallas_call | solution.py:101
  2.3 0.5 collective-permute-start
  2.8 4.1 %collective-permute-start.1 = (bf16[2,192,512]{2,1,0:T(8,128)(2,1)S(1)}, bf16[2,192,512]{2,1,0:T(8,128)(2,1)S(1)}, u32[]{:S(2)}, u32[]{:S(2)}) collective-permute-start(bf16[2,192,512]{2,1,0:T(8,128)(2,1)S(1)} %get-tuple-element.35.sent_second_ref), channel_id=1, source_target_pairs={{0,1},{1,0},{2,3},{3,2},{4,5},{5,4},{6,7},{7,6},{8,9},{9,8},{10,11... | collective-permute-start | bytes 1179656 | tf_op jit(solution)/shard_map/ppermute | solution.py:43
  7.0 0.0 copy-done.8
  7.0 1.5 %collective-permute-start.2 = (s32[1,16,1]{1,2,0:T(1,128)S(1)}, s32[1,16,1]{1,2,0:T(1,128)S(1)}, u32[]{:S(2)}, u32[]{:S(2)}) collective-permute-start(s32[1,16,1]{1,2,0:T(1,128)S(1)} %copy-done.8), channel_id=1, source_target_pairs={{0,8},{8,0},{4,12},{12,4},{16,24},{24,16},{20,28},{28,20},{1,9},{9... | collective-permute-start | bytes 200 | tf_op jit(solution)/shard_map/ppermute | solution.py:54
  8.5 0.0 copy-done.10
  8.5 0.2 subtract_reduce_fusion.starts_ref
  8.7 0.1 add_add_fusion.1.side_ref
  8.7 0.0 copy-done.9
  8.8 0.4 copy.8
  9.1 1.4 %collective-permute-done.2 = s32[1,16,1]{1,2,0:T(1,128)S(1)} collective-permute-done((s32[1,16,1]{1,2,0:T(1,128)S(1)}, s32[1,16,1]{1,2,0:T(1,128)S(1)}, u32[]{:S(2)}, u32[]{:S(2)}) %collective-permute-start.2) | collective-permute-done | bytes 96 | tf_op jit(solution)/shard_map/ppermute | solution.py:54
  10.5 1.6 %plan.1 = (s32[16]{0:T(128)S(1)}, s32[16]{0:T(128)S(1)}, s32[16]{0:T(128)S(1)}, s32[16]{0:T(128)S(1)}, s32[16]{0:T(128)S(1)}) custom-call(s32[1]{0:T(128)} %bitcast.me_ref, s32[16]{0:T(128)S(1)} %bitcast.18, s32[16]{0:T(128)S(1)} %bitcast.19), custom_call_target="tpu_custom_call" | custom-call | tf_op jit(solution)/shard_map/plan/pallas_call | solution.py:311
  12.1 0.0 copy-start.2
  12.2 0.6 copy-done.2
  12.7 0.5 copy-done.4
  13.2 0.0 collective-permute-done.first_ref
  13.3 2.6 %collective-permute-done.1.second_ref = bf16[2,192,512]{2,1,0:T(8,128)(2,1)S(1)} collective-permute-done((bf16[2,192,512]{2,1,0:T(8,128)(2,1)S(1)}, bf16[2,192,512]{2,1,0:T(8,128)(2,1)S(1)}, u32[]{:S(2)}, u32[]{:S(2)}) %collective-permute-start.1) | collective-permute-done | bytes 393248 | tf_op jit(solution)/shard_map/ppermute | solution.py:43
  15.8 2.1 %first_level.3 = bf16[2,512,256]{2,1,0:T(8,128)(2,1)} custom-call(s32[4]{0:T(128)S(1)} %subtract_reduce_fusion.starts_ref, s32[3]{0:T(128)S(1)} %add_add_fusion.1.side_ref, bf16[2,192,512]{2,1,0:T(8,128)(2,1)S(1)} %get-tuple-element.34.sent_first_ref, bf16[2,192,512]{2,1,0:T(8,128)(2,1)S(1)} %get-tuple-element.35.sent_second_ref, ...), custom_call_target="tpu_custom_call" | custom-call | flops 335544320 | bytes 2097152 | tf_op jit(solution)/shard_map/first_level/pallas_call | solution.py:177
  17.9 0.0 collective-permute-start.3
  18.0 0.0 copy-done.6
  18.0 0.0 copy-done
  18.0 1.8 %copy.9 = bf16[1,8,2,128,320]{4,3,2,1,0:T(8,128)(2,1)S(1)} copy(bf16[1,8,2,128,320]{3,4,2,1,0:T(8,128)(2,1)} %param.11) | data formatting | bytes 2621440 | tf_op args[4]
  19.8 0.0 copy-start.1
  19.8 1.0 %copy-done.1 = bf16[2,192,512]{2,1,0:T(8,128)(2,1)S(1)} copy-done((bf16[2,192,512]{2,1,0:T(8,128)(2,1)S(1)}, bf16[2,192,512]{2,1,0:T(8,128)(2,1)}, u32[]{:S(2)}) %copy-start.1) | copy-done | bytes 393240
  20.8 1.3 %first_level.2 = bf16[2,512,256]{2,1,0:T(8,128)(2,1)S(1)} custom-call(s32[4]{0:T(128)S(1)} %subtract_reduce_fusion.starts_ref, s32[3]{0:T(128)S(1)} %add_add_fusion.1.side_ref, bf16[2,192,512]{2,1,0:T(8,128)(2,1)S(1)} %get-tuple-element.34.sent_first_ref, bf16[2,192,512]{2,1,0:T(8,128)(2,1)S(1)} %get-tuple-element.35.sent_second_ref, ...), custom_call_target="tpu_custom_call" | custom-call | flops 335544320 | bytes 2097152 | tf_op jit(solution)/shard_map/first_level/pallas_call | solution.py:177
  22.1 0.0 copy-start.7
  22.1 0.0 collective-permute-done.3
  22.2 1.2 %add_convert_fusion.own_ref = bf16[2,512,256]{2,1,0:T(8,128)(2,1)S(1)} fusion(bf16[2,512,256]{2,1,0:T(8,128)(2,1)} %collective-permute-done.3, bf16[2,512,256]{2,1,0:T(8,128)(2,1)S(1)} %first_level.2), kind=kLoop, calls=%fused_computation | loop fusion | flops 1048576 | bytes 1572864 | tf_op jit(solution)/shard_map/convert_element_type | solution.py:474
  23.3 0.0 copy-start.3
  23.3 0.0 copy-start.5
  23.4 1.8 %collective-permute-start.4 = (bf16[2,192,256]{2,1,0:T(8,128)(2,1)S(1)}, bf16[2,192,256]{2,1,0:T(8,128)(2,1)S(1)}, u32[]{:S(2)}, u32[]{:S(2)}) collective-permute-start(bf16[2,192,256]{2,1,0:T(8,128)(2,1)S(1)} %get-tuple-element.64), channel_id=1, source_target_pairs={{0,1},{1,0},{2,3},{3,2},{4,5},{5,4},{6,7},{7,6},{8,9},{9,8},{10,11... | collective-permute-start | bytes 589832 | tf_op jit(solution)/shard_map/ppermute | solution.py:43
  25.2 0.2 collective-permute-start.5
  25.4 0.1 add_add_fusion.side_ref
  25.5 0.7 %fusion.1.starts_ref = s32[8]{0:T(128)S(1)} fusion(s32[8,8]{1,0:T(8,128)} %param.12, s32[]{:T(128)S(6)} %select_n.19, s32[]{:T(128)S(6)} %sub.26), kind=kLoop, calls=%fused_computation.6 | loop fusion | flops 8 | bytes 72 | tf_op jit(solution)/shard_map/sub | solution.py:480
  26.2 4.6 %collective-permute-done.4.first_ref = bf16[2,192,256]{2,1,0:T(8,128)(2,1)S(1)} collective-permute-done((bf16[2,192,256]{2,1,0:T(8,128)(2,1)S(1)}, bf16[2,192,256]{2,1,0:T(8,128)(2,1)S(1)}, u32[]{:S(2)}, u32[]{:S(2)}) %collective-permute-start.4) | collective-permute-done | bytes 196640 | tf_op jit(solution)/shard_map/ppermute | solution.py:43
  30.8 0.0 collective-permute-done.5.second_ref
  30.8 0.0 copy-done.7
  30.8 1.0 %second_level_early.1 = bf16[6,2,64,128]{3,2,1,0:T(8,128)(2,1)S(1)} custom-call(s32[8]{0:T(128)S(1)} %fusion.1.starts_ref, s32[3]{0:T(128)S(1)} %add_add_fusion.side_ref, s32[16]{0:T(128)S(1)} %copy-done.7, bf16[2,512,256]{2,1,0:T(8,128)(2,1)S(1)} %add_convert_fusion.own_ref, bf16[2,192,256]{2,1,0:T(8,128)(2,1)S(1)} %collective-permute-done.4.first_ref, ...), custom_call_target="tpu_custom_call" | custom-call | flops 125829120 | bytes 1048576 | tf_op jit(solution)/shard_map/second_level_early/pallas_call | solution.py:244
  31.8 1.6 %collective-permute-start.6 = (bf16[6,2,64,128]{3,2,1,0:T(8,128)(2,1)S(1)}, bf16[6,2,64,128]{3,2,1,0:T(8,128)(2,1)S(1)}, u32[]{:S(2)}, u32[]{:S(2)}) collective-permute-start(bf16[6,2,64,128]{3,2,1,0:T(8,128)(2,1)S(1)} %second_level_early.1), channel_id=1, source_target_pairs={{0,8},{8,0},{4,12},{12,4},{16,24},{24,16},{20,28},{28,20},{1,9},{9... | collective-permute-start | bytes 589832 | tf_op jit(solution)/shard_map/ppermute | solution.py:54
  33.4 0.0 copy-done.3
  33.4 0.0 copy-done.5
  33.4 1.9 %second_level.1 = (bf16[16,2,64,128]{3,2,1,0:T(8,128)(2,1)S(1)}, bf16[10,2,64,128]{3,2,1,0:T(8,128)(2,1)S(1)}) custom-call(s32[8]{0:T(128)S(1)} %fusion.1.starts_ref, s32[3]{0:T(128)S(1)} %add_add_fusion.side_ref, s32[16]{0:T(128)S(1)} %copy-done.3, s32[16]{0:T(128)S(1)} %copy-done.5, bf16[2,512,256]{2,1,0:T(8,128)(2,1)S(1)} %add_convert_fusion.own_ref, ...), custom_call_target="tpu_custom_call" | custom-call | flops 671088640 | bytes 4194304 | tf_op jit(solution)/shard_map/second_level/pallas_call | solution.py:255
  35.3 3.1 %collective-permute-done.6.refs_0_ = bf16[6,2,64,128]{3,2,1,0:T(8,128)(2,1)S(1)} collective-permute-done((bf16[6,2,64,128]{3,2,1,0:T(8,128)(2,1)S(1)}, bf16[6,2,64,128]{3,2,1,0:T(8,128)(2,1)S(1)}, u32[]{:S(2)}, u32[]{:S(2)}) %collective-permute-start.6) | collective-permute-done | bytes 196640 | tf_op jit(solution)/shard_map/ppermute | solution.py:54
  38.4 1.5 %collective-permute-start.7 = (bf16[10,2,64,128]{3,2,1,0:T(8,128)(2,1)S(1)}, bf16[10,2,64,128]{3,2,1,0:T(8,128)(2,1)S(1)}, u32[]{:S(2)}, u32[]{:S(2)}) collective-permute-start(bf16[10,2,64,128]{3,2,1,0:T(8,128)(2,1)S(1)} %get-tuple-element.47), channel_id=1, source_target_pairs={{0,8},{8,0},{4,12},{12,4},{16,24},{24,16},{20,28},{28,20},{1,9},{9... | collective-permute-start | bytes 983048 | tf_op jit(solution)/shard_map/ppermute | solution.py:54
  39.9 0.6 early_wires.1
  40.5 3.2 %collective-permute-start.8 = (bf16[2,2,64,128]{3,2,1,0:T(8,128)(2,1)S(1)}, bf16[2,2,64,128]{3,2,1,0:T(8,128)(2,1)S(1)}, u32[]{:S(2)}, u32[]{:S(2)}) collective-permute-start(bf16[2,2,64,128]{3,2,1,0:T(8,128)(2,1)S(1)} %get-tuple-element.52), channel_id=1, source_target_pairs={{0,3},{1,2},{2,1},{3,0},{4,7},{5,6},{6,5},{7,4},{8,11},{9,10},{10,... | collective-permute-start | bytes 196616 | tf_op jit(solution)/shard_map/ppermute | solution.py:420
  43.7 0.6 collective-permute-start.12
  44.3 3.0 %collective-permute-done.8.refs_0_ = bf16[2,2,64,128]{3,2,1,0:T(8,128)(2,1)S(1)} collective-permute-done((bf16[2,2,64,128]{3,2,1,0:T(8,128)(2,1)S(1)}, bf16[2,2,64,128]{3,2,1,0:T(8,128)(2,1)S(1)}, u32[]{:S(2)}, u32[]{:S(2)}) %collective-permute-start.8) | collective-permute-done | bytes 65568 | tf_op jit(solution)/shard_map/ppermute | solution.py:420
  47.3 0.0 collective-permute-done.7.refs_0_
  47.3 0.8 %late_wires.2 = (bf16[6,2,64,128]{3,2,1,0:T(8,128)(2,1)S(1)}, bf16[5,2,64,128]{3,2,1,0:T(8,128)(2,1)S(1)}, bf16[3,2,64,128]{3,2,1,0:T(8,128)(2,1)S(1)}, bf16[8,2,64,128]{3,2,1,0:T(8,128)(2,1)S(1)}) custom-call(s32[1]{0:T(128)} %bitcast.me_ref, s32[16]{0:T(128)S(1)} %get-tuple-element.48.target_ref, s32[16]{0:T(128)S(1)} %get-tuple-element.49.rank_ref, ...), custom_call_target="tpu_custom_call" | custom-call | bytes 2097152 | tf_op jit(solution)/shard_map/late_wires/pallas_call | solution.py:372
  48.1 2.7 %collective-permute-start.9 = (bf16[6,2,64,128]{3,2,1,0:T(8,128)(2,1)S(1)}, bf16[6,2,64,128]{3,2,1,0:T(8,128)(2,1)S(1)}, u32[]{:S(2)}, u32[]{:S(2)}) collective-permute-start(bf16[6,2,64,128]{3,2,1,0:T(8,128)(2,1)S(1)} %get-tuple-element.56), channel_id=1, source_target_pairs={{0,3},{1,2},{2,1},{3,0},{4,7},{5,6},{6,5},{7,4},{8,11},{9,10},{10,... | collective-permute-start | bytes 589832 | tf_op jit(solution)/shard_map/ppermute | solution.py:420
  50.8 2.8 %collective-permute-start.10 = (bf16[5,2,64,128]{3,2,1,0:T(8,128)(2,1)S(1)}, bf16[5,2,64,128]{3,2,1,0:T(8,128)(2,1)S(1)}, u32[]{:S(2)}, u32[]{:S(2)}) collective-permute-start(bf16[5,2,64,128]{3,2,1,0:T(8,128)(2,1)S(1)} %get-tuple-element.57), channel_id=1, source_target_pairs={{0,1},{1,0},{2,3},{3,2},{4,5},{5,4},{6,7},{7,6},{8,9},{9,8},{10,11... | collective-permute-start | bytes 491528 | tf_op jit(solution)/shard_map/ppermute | solution.py:420
  53.7 4.8 %collective-permute-done.12.refs_5_ = bf16[4,2,64,128]{3,2,1,0:T(8,128)(2,1)S(1)} collective-permute-done((bf16[4,2,64,128]{3,2,1,0:T(8,128)(2,1)S(1)}, bf16[4,2,64,128]{3,2,1,0:T(8,128)(2,1)S(1)}, u32[]{:S(2)}, u32[]{:S(2)}) %collective-permute-start.12) | collective-permute-done | bytes 131104 | tf_op jit(solution)/shard_map/ppermute | solution.py:420
  58.5 0.6 late_wires.3
  59.1 0.1 collective-permute-start.13
  59.2 1.9 %collective-permute-start.11 = (bf16[3,2,64,128]{3,2,1,0:T(8,128)(2,1)S(1)}, bf16[3,2,64,128]{3,2,1,0:T(8,128)(2,1)S(1)}, u32[]{:S(2)}, u32[]{:S(2)}) collective-permute-start(bf16[3,2,64,128]{3,2,1,0:T(8,128)(2,1)S(1)} %get-tuple-element.58), channel_id=1, source_target_pairs={{0,1},{1,0},{2,3},{3,2},{4,5},{5,4},{6,7},{7,6},{8,9},{9,8},{10,11... | collective-permute-start | bytes 294920 | tf_op jit(solution)/shard_map/ppermute | solution.py:420
  61.1 3.0 %collective-permute-done.11.refs_3_ = bf16[3,2,64,128]{3,2,1,0:T(8,128)(2,1)S(1)} collective-permute-done((bf16[3,2,64,128]{3,2,1,0:T(8,128)(2,1)S(1)}, bf16[3,2,64,128]{3,2,1,0:T(8,128)(2,1)S(1)}, u32[]{:S(2)}, u32[]{:S(2)}) %collective-permute-start.11) | collective-permute-done | bytes 98336 | tf_op jit(solution)/shard_map/ppermute | solution.py:420
  64.2 2.1 %collective-permute-done.13.refs_6_ = bf16[4,2,64,128]{3,2,1,0:T(8,128)(2,1)S(1)} collective-permute-done((bf16[4,2,64,128]{3,2,1,0:T(8,128)(2,1)S(1)}, bf16[4,2,64,128]{3,2,1,0:T(8,128)(2,1)S(1)}, u32[]{:S(2)}, u32[]{:S(2)}) %collective-permute-start.13) | collective-permute-done | bytes 131104 | tf_op jit(solution)/shard_map/ppermute | solution.py:420
  66.2 0.0 collective-permute-done.10.refs_2_
  66.2 0.0 collective-permute-done.9.refs_1_
  66.2 1.0 %collect.1 = bf16[32,2,64,128]{3,2,1,0:T(8,128)(2,1)} custom-call(s32[1]{0:T(128)} %bitcast.me_ref, bf16[2,2,64,128]{3,2,1,0:T(8,128)(2,1)S(1)} %collective-permute-done.8.refs_0_, bf16[6,2,64,128]{3,2,1,0:T(8,128)(2,1)S(1)} %collective-permute-done.9.refs_1_, bf16[5,2,64,128]{3,2,1,0:T(8,128)(2,1)S(1)} %collective-permute-done.10.refs_2_, ...), custom_call_target="tpu_custom_call" | custom-call | bytes 2097152 | tf_op jit(solution)/shard_map/collect/pallas_call | solution.py:403
  (4 shorter events, 0.0 us)
Async XLA Ops:
  0.0 7.0 %copy-start.8 = (s32[1,16,1]{1,2,0:T(1,128)S(1)}, s32[1,16,1]{1,2,0:T(1,128)}, u32[]{:S(2)}) copy-start(s32[1,16,1]{1,2,0:T(1,128)} %param.13) | copy-start | bytes 196
  0.0 8.5 %copy-start.10 = (s32[8,4]{0,1:T(4,128)S(1)}, s32[8,4]{0,1:T(4,128)}, u32[]{:S(2)}) copy-start(s32[8,4]{0,1:T(4,128)} %param.10) | copy-start | bytes 388
  0.0 8.7 %copy-start.9 = (bf16[1,4,2,128,320]{3,4,2,1,0:T(8,128)(2,1)S(1)}, bf16[1,4,2,128,320]{3,4,2,1,0:T(8,128)(2,1)}, u32[]{:S(2)}) copy-start(bf16[1,4,2,128,320]{3,4,2,1,0:T(8,128)(2,1)} %param.9) | copy-start | bytes 1966084
  2.3 10.9 %collective-permute-start = (bf16[2,192,512]{2,1,0:T(8,128)(2,1)S(1)}, bf16[2,192,512]{2,1,0:T(8,128)(2,1)S(1)}, u32[]{:S(2)}, u32[]{:S(2)}) collective-permute-start(bf16[2,192,512]{2,1,0:T(8,128)(2,1)S(1)} %get-tuple-element.34.sent_first_ref), channel_id=1, source_target_pairs={{0,4},{1,2},{2,1},{3,7},{4,0},{5,6},{6,5},{7,3},{8,12},{9,10},{10,... | collective-permute-start | bytes 1179656 | tf_op jit(solution)/shard_map/ppermute | solution.py:43
  2.8 13.0 %collective-permute-start.1 = (bf16[2,192,512]{2,1,0:T(8,128)(2,1)S(1)}, bf16[2,192,512]{2,1,0:T(8,128)(2,1)S(1)}, u32[]{:S(2)}, u32[]{:S(2)}) collective-permute-start(bf16[2,192,512]{2,1,0:T(8,128)(2,1)S(1)} %get-tuple-element.35.sent_second_ref), channel_id=1, source_target_pairs={{0,1},{1,0},{2,3},{3,2},{4,5},{5,4},{6,7},{7,6},{8,9},{9,8},{10,11... | collective-permute-start | bytes 1179656 | tf_op jit(solution)/shard_map/ppermute | solution.py:43
  7.0 3.5 %collective-permute-start.2 = (s32[1,16,1]{1,2,0:T(1,128)S(1)}, s32[1,16,1]{1,2,0:T(1,128)S(1)}, u32[]{:S(2)}, u32[]{:S(2)}) collective-permute-start(s32[1,16,1]{1,2,0:T(1,128)S(1)} %copy-done.8), channel_id=1, source_target_pairs={{0,8},{8,0},{4,12},{12,4},{16,24},{24,16},{20,28},{28,20},{1,9},{9... | collective-permute-start | bytes 200 | tf_op jit(solution)/shard_map/ppermute | solution.py:54
  12.1 0.6 copy-start.2
  12.7 0.5 copy-start.4
  13.2 4.7 %copy-start.6 = (s32[16]{0:T(128)}, s32[16]{0:T(128)S(1)}, u32[]{:S(2)}) copy-start(s32[16]{0:T(128)S(1)} %get-tuple-element.41.sector_ref) | copy-start | bytes 196
  15.8 2.1 %copy-start = (bf16[2,192,512]{2,1,0:T(8,128)(2,1)}, bf16[2,192,512]{2,1,0:T(8,128)(2,1)S(1)}, u32[]{:S(2)}) copy-start(bf16[2,192,512]{2,1,0:T(8,128)(2,1)S(1)} %collective-permute-done.1.second_ref) | copy-start | bytes 1179652
  17.9 4.2 %collective-permute-start.3 = (bf16[2,512,256]{2,1,0:T(8,128)(2,1)}, bf16[2,512,256]{2,1,0:T(8,128)(2,1)}, u32[]{:S(2)}, u32[]{:S(2)}) collective-permute-start(bf16[2,512,256]{2,1,0:T(8,128)(2,1)} %first_level.3), channel_id=1, source_target_pairs={{0,4},{4,0},{8,12},{12,8},{16,20},{20,16},{24,28},{28,24},{1,5},{5... | collective-permute-start | bytes 1572872 | tf_op jit(solution)/shard_map/ppermute | solution.py:54
  19.8 1.0 %copy-start.1 = (bf16[2,192,512]{2,1,0:T(8,128)(2,1)S(1)}, bf16[2,192,512]{2,1,0:T(8,128)(2,1)}, u32[]{:S(2)}) copy-start(bf16[2,192,512]{2,1,0:T(8,128)(2,1)} %copy-done) | copy-start | bytes 1179652
  22.1 8.6 %copy-start.7 = (s32[16]{0:T(128)S(1)}, s32[16]{0:T(128)}, u32[]{:S(2)}) copy-start(s32[16]{0:T(128)} %copy-done.6) | copy-start | bytes 196
  23.3 10.0 %copy-start.3 = (s32[16]{0:T(128)S(1)}, s32[16]{0:T(128)}, u32[]{:S(2)}) copy-start(s32[16]{0:T(128)} %copy-done.2) | copy-start | bytes 196
  23.3 10.0 %copy-start.5 = (s32[16]{0:T(128)S(1)}, s32[16]{0:T(128)}, u32[]{:S(2)}) copy-start(s32[16]{0:T(128)} %copy-done.4) | copy-start | bytes 196
  23.4 7.4 %collective-permute-start.4 = (bf16[2,192,256]{2,1,0:T(8,128)(2,1)S(1)}, bf16[2,192,256]{2,1,0:T(8,128)(2,1)S(1)}, u32[]{:S(2)}, u32[]{:S(2)}) collective-permute-start(bf16[2,192,256]{2,1,0:T(8,128)(2,1)S(1)} %get-tuple-element.64), channel_id=1, source_target_pairs={{0,1},{1,0},{2,3},{3,2},{4,5},{5,4},{6,7},{7,6},{8,9},{9,8},{10,11... | collective-permute-start | bytes 589832 | tf_op jit(solution)/shard_map/ppermute | solution.py:43
  25.2 5.6 %collective-permute-start.5 = (bf16[2,192,256]{2,1,0:T(8,128)(2,1)S(1)}, bf16[2,192,256]{2,1,0:T(8,128)(2,1)S(1)}, u32[]{:S(2)}, u32[]{:S(2)}) collective-permute-start(bf16[2,192,256]{2,1,0:T(8,128)(2,1)S(1)} %get-tuple-element.63), channel_id=1, source_target_pairs={{0,4},{1,2},{2,1},{3,7},{4,0},{5,6},{6,5},{7,3},{8,12},{9,10},{10,... | collective-permute-start | bytes 589832 | tf_op jit(solution)/shard_map/ppermute | solution.py:43
  31.8 6.6 %collective-permute-start.6 = (bf16[6,2,64,128]{3,2,1,0:T(8,128)(2,1)S(1)}, bf16[6,2,64,128]{3,2,1,0:T(8,128)(2,1)S(1)}, u32[]{:S(2)}, u32[]{:S(2)}) collective-permute-start(bf16[6,2,64,128]{3,2,1,0:T(8,128)(2,1)S(1)} %second_level_early.1), channel_id=1, source_target_pairs={{0,8},{8,0},{4,12},{12,4},{16,24},{24,16},{20,28},{28,20},{1,9},{9... | collective-permute-start | bytes 589832 | tf_op jit(solution)/shard_map/ppermute | solution.py:54
  38.4 8.9 %collective-permute-start.7 = (bf16[10,2,64,128]{3,2,1,0:T(8,128)(2,1)S(1)}, bf16[10,2,64,128]{3,2,1,0:T(8,128)(2,1)S(1)}, u32[]{:S(2)}, u32[]{:S(2)}) collective-permute-start(bf16[10,2,64,128]{3,2,1,0:T(8,128)(2,1)S(1)} %get-tuple-element.47), channel_id=1, source_target_pairs={{0,8},{8,0},{4,12},{12,4},{16,24},{24,16},{20,28},{28,20},{1,9},{9... | collective-permute-start | bytes 983048 | tf_op jit(solution)/shard_map/ppermute | solution.py:54
  40.5 6.8 %collective-permute-start.8 = (bf16[2,2,64,128]{3,2,1,0:T(8,128)(2,1)S(1)}, bf16[2,2,64,128]{3,2,1,0:T(8,128)(2,1)S(1)}, u32[]{:S(2)}, u32[]{:S(2)}) collective-permute-start(bf16[2,2,64,128]{3,2,1,0:T(8,128)(2,1)S(1)} %get-tuple-element.52), channel_id=1, source_target_pairs={{0,3},{1,2},{2,1},{3,0},{4,7},{5,6},{6,5},{7,4},{8,11},{9,10},{10,... | collective-permute-start | bytes 196616 | tf_op jit(solution)/shard_map/ppermute | solution.py:420
  43.7 14.8 %collective-permute-start.12 = (bf16[4,2,64,128]{3,2,1,0:T(8,128)(2,1)S(1)}, bf16[4,2,64,128]{3,2,1,0:T(8,128)(2,1)S(1)}, u32[]{:S(2)}, u32[]{:S(2)}) collective-permute-start(bf16[4,2,64,128]{3,2,1,0:T(8,128)(2,1)S(1)} %get-tuple-element.60), channel_id=1, source_target_pairs={{0,2},{1,3},{2,0},{3,1},{4,6},{5,7},{6,4},{7,5},{8,10},{9,11},{10,... | collective-permute-start | bytes 393224 | tf_op jit(solution)/shard_map/ppermute | solution.py:420
  48.1 18.1 %collective-permute-start.9 = (bf16[6,2,64,128]{3,2,1,0:T(8,128)(2,1)S(1)}, bf16[6,2,64,128]{3,2,1,0:T(8,128)(2,1)S(1)}, u32[]{:S(2)}, u32[]{:S(2)}) collective-permute-start(bf16[6,2,64,128]{3,2,1,0:T(8,128)(2,1)S(1)} %get-tuple-element.56), channel_id=1, source_target_pairs={{0,3},{1,2},{2,1},{3,0},{4,7},{5,6},{6,5},{7,4},{8,11},{9,10},{10,... | collective-permute-start | bytes 589832 | tf_op jit(solution)/shard_map/ppermute | solution.py:420
  50.8 15.4 %collective-permute-start.10 = (bf16[5,2,64,128]{3,2,1,0:T(8,128)(2,1)S(1)}, bf16[5,2,64,128]{3,2,1,0:T(8,128)(2,1)S(1)}, u32[]{:S(2)}, u32[]{:S(2)}) collective-permute-start(bf16[5,2,64,128]{3,2,1,0:T(8,128)(2,1)S(1)} %get-tuple-element.57), channel_id=1, source_target_pairs={{0,1},{1,0},{2,3},{3,2},{4,5},{5,4},{6,7},{7,6},{8,9},{9,8},{10,11... | collective-permute-start | bytes 491528 | tf_op jit(solution)/shard_map/ppermute | solution.py:420
  59.1 7.1 %collective-permute-start.13 = (bf16[4,2,64,128]{3,2,1,0:T(8,128)(2,1)S(1)}, bf16[4,2,64,128]{3,2,1,0:T(8,128)(2,1)S(1)}, u32[]{:S(2)}, u32[]{:S(2)}) collective-permute-start(bf16[4,2,64,128]{3,2,1,0:T(8,128)(2,1)S(1)} %late_wires.3), channel_id=1, source_target_pairs={{0,2},{1,3},{2,0},{3,1},{4,6},{5,7},{6,4},{7,5},{8,10},{9,11},{10,... | collective-permute-start | bytes 393224 | tf_op jit(solution)/shard_map/ppermute | solution.py:420
  59.2 4.9 %collective-permute-start.11 = (bf16[3,2,64,128]{3,2,1,0:T(8,128)(2,1)S(1)}, bf16[3,2,64,128]{3,2,1,0:T(8,128)(2,1)S(1)}, u32[]{:S(2)}, u32[]{:S(2)}) collective-permute-start(bf16[3,2,64,128]{3,2,1,0:T(8,128)(2,1)S(1)} %get-tuple-element.58), channel_id=1, source_target_pairs={{0,1},{1,0},{2,3},{3,2},{4,5},{5,4},{6,7},{7,6},{8,9},{9,8},{10,11... | collective-permute-start | bytes 294920 | tf_op jit(solution)/shard_map/ppermute | solution.py:420

commit v16 on v15

--- a/solution.py
+++ b/solution.py
@@ -473,6 +473,7 @@
     keep = first_level(0, rows, begin0, inner_side, sent, halos, weights)
     level_one = (keep.astype(jnp.float32) + other.astype(jnp.float32)).astype(jnp.bfloat16)
 
+    level_one, weights1 = lax.optimization_barrier((level_one, weights1))
     beams = level_one.shape[1]
     first = lax.dynamic_slice_in_dim(level_one, even * (beams - margin), margin, 1)
     second = lax.dynamic_slice_in_dim(level_one, (1 - even) * (beams - margin), margin, 1)

time: 67.5 us -> 62.2 us (0.921)
  local copies, waits for them, and re-layouts: 4.35 us -> 2.27 us
  waiting for transfers between devices: 24.6 us -> 23.2 us
  other arithmetic: 2.2 us -> 1.17 us
  Pallas kernels: 13.4 us -> 12.7 us
    unnamed x24 -> x7, local copies, waits for them, and re-layouts: 4.31 us -> 0.38 us
    optimization_barrier x0 -> x1, local copies, waits for them, and re-layouts: none -> 1.85 us  [local(): level_one, weights1 = lax.optimization_barrier((level_one, weights1))]
    convert_element_type x1, other arithmetic: 1.17 us -> 0.14 us  [local(): (keep.astype(jnp.float32) + other.astype(jnp.float32)).astype(jnp.bfloat16)]
    ppermute x4, waiting for transfers between devices: 7.18 us -> 6.26 us  [trade_edges(): received.append(lax.ppermute(block, ('aperture', 'beam'), route))]
    pallas_call x2, Pallas kernels: 3.45 us -> 2.68 us  [first_level(): pl.pallas_call(functools.partial(first_level_kernel, column, rows), out_s...]
  transfers between devices with their start and end apart: 14 -> 14, of which waited for: 8 -> 9; matrix products, arithmetic and copies ran while one was open for 5% -> 5% of each run, Pallas kernels for 10% -> 11%
where the time goes in v16:
time: 62.2 us; the launch traced here: 62 us
  waiting for transfers between devices  23.2 us (37%)
  starting transfers between devices  22.5 us (36%)
  Pallas kernels  12.7 us (20%)
  local copies, waits for them, and re-layouts  2.27 us (4%)
  other arithmetic  1.17 us (2%)
    ppermute x6, waiting for transfers between devices, spread(): received.append(lax.ppermute(wire, 'beam', route) if distance else wire)  12.4 us
    ppermute x6, starting transfers between devices, spread(): received.append(lax.ppermute(wire, 'beam', route) if distance else wire)  11.4 us
    ppermute x4, starting transfers between devices, trade_edges(): received.append(lax.ppermute(block, ('aperture', 'beam'), route))  6.47 us
    ppermute x4, waiting for transfers between devices, trade_edges(): received.append(lax.ppermute(block, ('aperture', 'beam'), route))  6.26 us
    ppermute x4, starting transfers between devices, partner(): return lax.ppermute(block, axis, route)  4.61 us
    ppermute x4, waiting for transfers between devices, partner(): return lax.ppermute(block, axis, route)  4.55 us
    pallas_call x2, Pallas kernels, first_level(): pl.pallas_call(functools.partial(first_level_kernel, column, rows), out_s...  2.68 us
    pallas_call x1, Pallas kernels, resample(): pl.pallas_call(resample_kernel, out_shape=(shape, shape), in_specs=[ANY,...  2.31 us
  transfers between devices with their start and end apart: 14, of which 9 were waited for; matrix products, arithmetic and copies ran while one was open for 5% of the time, Pallas kernels for 11%

profile of v16, /device:TPU:0, one launch (start us, length us, event | category | flops | bytes accessed | tf_op | source)
XLA Modules:
  0.0 62.0 jit_solution(5952585171168667070)
XLA Ops:
  0.0 0.0 copy-start
  0.0 0.0 copy-start.2
  0.0 0.0 copy-start.1
  0.0 2.3 %resample.1 = (bf16[2,192,512]{2,1,0:T(8,128)(2,1)S(1)}, bf16[2,192,512]{2,1,0:T(8,128)(2,1)S(1)}) custom-call(bf16[2,256,512]{2,1,0:T(8,128)(2,1)} %bitcast.21, bf16[2,512,512]{2,1,0:T(8,128)(2,1)} %bitcast.20), custom_call_target="tpu_custom_call" | custom-call | flops 536870912 | bytes 2097152 | tf_op jit(solution)/shard_map/resample/pallas_call | solution.py:101
  2.3 0.5 collective-permute-start
  2.8 4.1 %collective-permute-start.1 = (bf16[2,192,512]{2,1,0:T(8,128)(2,1)S(1)}, bf16[2,192,512]{2,1,0:T(8,128)(2,1)S(1)}, u32[]{:S(2)}, u32[]{:S(2)}) collective-permute-start(bf16[2,192,512]{2,1,0:T(8,128)(2,1)S(1)} %get-tuple-element.37.sent_second_ref), channel_id=1, source_target_pairs={{0,1},{1,0},{2,3},{3,2},{4,5},{5,4},{6,7},{7,6},{8,9},{9,8},{10,11... | collective-permute-start | bytes 1179656 | tf_op jit(solution)/shard_map/ppermute | solution.py:43
  7.0 0.0 copy-done
  7.0 1.5 %collective-permute-start.2 = (s32[1,16,1]{1,2,0:T(1,128)S(1)}, s32[1,16,1]{1,2,0:T(1,128)S(1)}, u32[]{:S(2)}, u32[]{:S(2)}) collective-permute-start(s32[1,16,1]{1,2,0:T(1,128)S(1)} %copy-done), channel_id=1, source_target_pairs={{0,8},{8,0},{4,12},{12,4},{16,24},{24,16},{20,28},{28,20},{1,9},{9... | collective-permute-start | bytes 200 | tf_op jit(solution)/shard_map/ppermute | solution.py:54
  8.5 0.0 copy-done.2
  8.5 0.2 subtract_reduce_fusion.starts_ref
  8.7 0.1 add_add_fusion.1.side_ref
  8.7 0.0 copy-done.1
  8.8 0.4 copy.8
  9.1 1.4 %collective-permute-done.2 = s32[1,16,1]{1,2,0:T(1,128)S(1)} collective-permute-done((s32[1,16,1]{1,2,0:T(1,128)S(1)}, s32[1,16,1]{1,2,0:T(1,128)S(1)}, u32[]{:S(2)}, u32[]{:S(2)}) %collective-permute-start.2) | collective-permute-done | bytes 96 | tf_op jit(solution)/shard_map/ppermute | solution.py:54
  10.5 1.6 %plan.1 = (s32[16]{0:T(128)S(1)}, s32[16]{0:T(128)S(1)}, s32[16]{0:T(128)S(1)}, s32[16]{0:T(128)S(1)}, s32[16]{0:T(128)S(1)}) custom-call(s32[1]{0:T(128)} %bitcast.me_ref, s32[16]{0:T(128)S(1)} %bitcast.18, s32[16]{0:T(128)S(1)} %bitcast.19), custom_call_target="tpu_custom_call" | custom-call | tf_op jit(solution)/shard_map/plan/pallas_call | solution.py:311
  12.1 0.0 collective-permute-done.first_ref
  12.2 3.7 %collective-permute-done.1.second_ref = bf16[2,192,512]{2,1,0:T(8,128)(2,1)S(1)} collective-permute-done((bf16[2,192,512]{2,1,0:T(8,128)(2,1)S(1)}, bf16[2,192,512]{2,1,0:T(8,128)(2,1)S(1)}, u32[]{:S(2)}, u32[]{:S(2)}) %collective-permute-start.1) | collective-permute-done | bytes 393248 | tf_op jit(solution)/shard_map/ppermute | solution.py:43
  15.8 1.3 %first_level.3 = bf16[2,512,256]{2,1,0:T(8,128)(2,1)S(1)} custom-call(s32[4]{0:T(128)S(1)} %subtract_reduce_fusion.starts_ref, s32[3]{0:T(128)S(1)} %add_add_fusion.1.side_ref, bf16[2,192,512]{2,1,0:T(8,128)(2,1)S(1)} %get-tuple-element.36.sent_first_ref, bf16[2,192,512]{2,1,0:T(8,128)(2,1)S(1)} %get-tuple-element.37.sent_second_ref, ...), custom_call_target="tpu_custom_call" | custom-call | flops 335544320 | bytes 2097152 | tf_op jit(solution)/shard_map/first_level/pallas_call | solution.py:177
  17.2 0.1 collective-permute-start.3
  17.3 1.3 %first_level.2 = bf16[2,512,256]{2,1,0:T(8,128)(2,1)S(1)} custom-call(s32[4]{0:T(128)S(1)} %subtract_reduce_fusion.starts_ref, s32[3]{0:T(128)S(1)} %add_add_fusion.1.side_ref, bf16[2,192,512]{2,1,0:T(8,128)(2,1)S(1)} %get-tuple-element.36.sent_first_ref, bf16[2,192,512]{2,1,0:T(8,128)(2,1)S(1)} %get-tuple-element.37.sent_second_ref, ...), custom_call_target="tpu_custom_call" | custom-call | flops 335544320 | bytes 2097152 | tf_op jit(solution)/shard_map/first_level/pallas_call | solution.py:177
  18.6 0.5 collective-permute-done.3
  19.1 0.1 add_convert_fusion.own_ref
  19.3 1.8 %collective-permute-start.4 = (bf16[2,192,256]{2,1,0:T(8,128)(2,1)S(1)}, bf16[2,192,256]{2,1,0:T(8,128)(2,1)S(1)}, u32[]{:S(2)}, u32[]{:S(2)}) collective-permute-start(bf16[2,192,256]{2,1,0:T(8,128)(2,1)S(1)} %get-tuple-element.68), channel_id=1, source_target_pairs={{0,1},{1,0},{2,3},{3,2},{4,5},{5,4},{6,7},{7,6},{8,9},{9,8},{10,11... | collective-permute-start | bytes 589832 | tf_op jit(solution)/shard_map/ppermute | solution.py:43
  21.1 0.0 collective-permute-start.5
  21.1 0.1 add_add_fusion.side_ref
  21.2 0.7 %fusion.1.starts_ref = s32[8]{0:T(128)S(1)} fusion(s32[8,8]{1,0:T(8,128)} %param.12, s32[]{:T(128)S(6)} %select_n.19, s32[]{:T(128)S(6)} %sub.26), kind=kLoop, calls=%fused_computation.6 | loop fusion | flops 8 | bytes 72 | tf_op jit(solution)/shard_map/sub | solution.py:481
  21.9 1.9 %copy.9 = bf16[1,8,2,128,320]{4,3,2,1,0:T(8,128)(2,1)S(1)} copy(bf16[1,8,2,128,320]{3,4,2,1,0:T(8,128)(2,1)} %param.11) | data formatting | bytes 2621440 | tf_op jit(solution)/shard_map/optimization_barrier | solution.py:476
  23.8 2.6 %collective-permute-done.4.first_ref = bf16[2,192,256]{2,1,0:T(8,128)(2,1)S(1)} collective-permute-done((bf16[2,192,256]{2,1,0:T(8,128)(2,1)S(1)}, bf16[2,192,256]{2,1,0:T(8,128)(2,1)S(1)}, u32[]{:S(2)}, u32[]{:S(2)}) %collective-permute-start.4) | collective-permute-done | bytes 196640 | tf_op jit(solution)/shard_map/ppermute | solution.py:43
  26.3 0.0 collective-permute-done.5.second_ref
  26.3 1.0 %second_level_early.1 = bf16[6,2,64,128]{3,2,1,0:T(8,128)(2,1)S(1)} custom-call(s32[8]{0:T(128)S(1)} %fusion.1.starts_ref, s32[3]{0:T(128)S(1)} %add_add_fusion.side_ref, s32[16]{0:T(128)S(1)} %get-tuple-element.43.sector_ref, bf16[2,512,256]{2,1,0:T(8,128)(2,1)S(1)} %add_convert_fusion.own_ref, bf16[2,192,256]{2,1,0:T(8,128)(2,1)S(1)} %collective-permute-done.4.first_ref, ...), custom_call_target="tpu_custom_call" | custom-call | flops 125829120 | bytes 1048576 | tf_op jit(solution)/shard_map/second_level_early/pallas_call | solution.py:244
  27.4 1.6 %collective-permute-start.6 = (bf16[6,2,64,128]{3,2,1,0:T(8,128)(2,1)S(1)}, bf16[6,2,64,128]{3,2,1,0:T(8,128)(2,1)S(1)}, u32[]{:S(2)}, u32[]{:S(2)}) collective-permute-start(bf16[6,2,64,128]{3,2,1,0:T(8,128)(2,1)S(1)} %second_level_early.1), channel_id=1, source_target_pairs={{0,8},{8,0},{4,12},{12,4},{16,24},{24,16},{20,28},{28,20},{1,9},{9... | collective-permute-start | bytes 589832 | tf_op jit(solution)/shard_map/ppermute | solution.py:54
  28.9 2.0 %second_level.1 = (bf16[16,2,64,128]{3,2,1,0:T(8,128)(2,1)S(1)}, bf16[10,2,64,128]{3,2,1,0:T(8,128)(2,1)S(1)}) custom-call(s32[8]{0:T(128)S(1)} %fusion.1.starts_ref, s32[3]{0:T(128)S(1)} %add_add_fusion.side_ref, s32[16]{0:T(128)S(1)} %get-tuple-element.48.own_at_ref, s32[16]{0:T(128)S(1)} %get-tuple-element.49.other_at_ref, ...), custom_call_target="tpu_custom_call" | custom-call | flops 671088640 | bytes 4194304 | tf_op jit(solution)/shard_map/second_level/pallas_call | solution.py:255
  30.9 2.6 %collective-permute-done.6.refs_0_ = bf16[6,2,64,128]{3,2,1,0:T(8,128)(2,1)S(1)} collective-permute-done((bf16[6,2,64,128]{3,2,1,0:T(8,128)(2,1)S(1)}, bf16[6,2,64,128]{3,2,1,0:T(8,128)(2,1)S(1)}, u32[]{:S(2)}, u32[]{:S(2)}) %collective-permute-start.6) | collective-permute-done | bytes 196640 | tf_op jit(solution)/shard_map/ppermute | solution.py:54
  33.6 1.5 %collective-permute-start.7 = (bf16[10,2,64,128]{3,2,1,0:T(8,128)(2,1)S(1)}, bf16[10,2,64,128]{3,2,1,0:T(8,128)(2,1)S(1)}, u32[]{:S(2)}, u32[]{:S(2)}) collective-permute-start(bf16[10,2,64,128]{3,2,1,0:T(8,128)(2,1)S(1)} %get-tuple-element.51), channel_id=1, source_target_pairs={{0,8},{8,0},{4,12},{12,4},{16,24},{24,16},{20,28},{28,20},{1,9},{9... | collective-permute-start | bytes 983048 | tf_op jit(solution)/shard_map/ppermute | solution.py:54
  35.1 0.6 early_wires.1
  35.7 3.2 %collective-permute-start.8 = (bf16[2,2,64,128]{3,2,1,0:T(8,128)(2,1)S(1)}, bf16[2,2,64,128]{3,2,1,0:T(8,128)(2,1)S(1)}, u32[]{:S(2)}, u32[]{:S(2)}) collective-permute-start(bf16[2,2,64,128]{3,2,1,0:T(8,128)(2,1)S(1)} %get-tuple-element.56), channel_id=1, source_target_pairs={{0,3},{1,2},{2,1},{3,0},{4,7},{5,6},{6,5},{7,4},{8,11},{9,10},{10,... | collective-permute-start | bytes 196616 | tf_op jit(solution)/shard_map/ppermute | solution.py:420
  38.9 0.6 collective-permute-start.12
  39.5 2.6 %collective-permute-done.8.refs_0_ = bf16[2,2,64,128]{3,2,1,0:T(8,128)(2,1)S(1)} collective-permute-done((bf16[2,2,64,128]{3,2,1,0:T(8,128)(2,1)S(1)}, bf16[2,2,64,128]{3,2,1,0:T(8,128)(2,1)S(1)}, u32[]{:S(2)}, u32[]{:S(2)}) %collective-permute-start.8) | collective-permute-done | bytes 65568 | tf_op jit(solution)/shard_map/ppermute | solution.py:420
  42.1 0.0 collective-permute-done.7.refs_0_
  42.1 0.8 %late_wires.2 = (bf16[6,2,64,128]{3,2,1,0:T(8,128)(2,1)S(1)}, bf16[5,2,64,128]{3,2,1,0:T(8,128)(2,1)S(1)}, bf16[3,2,64,128]{3,2,1,0:T(8,128)(2,1)S(1)}, bf16[8,2,64,128]{3,2,1,0:T(8,128)(2,1)S(1)}) custom-call(s32[1]{0:T(128)} %bitcast.me_ref, s32[16]{0:T(128)S(1)} %get-tuple-element.52.target_ref, s32[16]{0:T(128)S(1)} %get-tuple-element.53.rank_ref, ...), custom_call_target="tpu_custom_call" | custom-call | bytes 2097152 | tf_op jit(solution)/shard_map/late_wires/pallas_call | solution.py:372
  42.9 3.1 %collective-permute-start.9 = (bf16[6,2,64,128]{3,2,1,0:T(8,128)(2,1)S(1)}, bf16[6,2,64,128]{3,2,1,0:T(8,128)(2,1)S(1)}, u32[]{:S(2)}, u32[]{:S(2)}) collective-permute-start(bf16[6,2,64,128]{3,2,1,0:T(8,128)(2,1)S(1)} %get-tuple-element.60), channel_id=1, source_target_pairs={{0,3},{1,2},{2,1},{3,0},{4,7},{5,6},{6,5},{7,4},{8,11},{9,10},{10,... | collective-permute-start | bytes 589832 | tf_op jit(solution)/shard_map/ppermute | solution.py:420
  45.9 2.5 %collective-permute-start.10 = (bf16[5,2,64,128]{3,2,1,0:T(8,128)(2,1)S(1)}, bf16[5,2,64,128]{3,2,1,0:T(8,128)(2,1)S(1)}, u32[]{:S(2)}, u32[]{:S(2)}) collective-permute-start(bf16[5,2,64,128]{3,2,1,0:T(8,128)(2,1)S(1)} %get-tuple-element.61), channel_id=1, source_target_pairs={{0,1},{1,0},{2,3},{3,2},{4,5},{5,4},{6,7},{7,6},{8,9},{9,8},{10,11... | collective-permute-start | bytes 491528 | tf_op jit(solution)/shard_map/ppermute | solution.py:420
  48.5 4.8 %collective-permute-done.12.refs_5_ = bf16[4,2,64,128]{3,2,1,0:T(8,128)(2,1)S(1)} collective-permute-done((bf16[4,2,64,128]{3,2,1,0:T(8,128)(2,1)S(1)}, bf16[4,2,64,128]{3,2,1,0:T(8,128)(2,1)S(1)}, u32[]{:S(2)}, u32[]{:S(2)}) %collective-permute-start.12) | collective-permute-done | bytes 131104 | tf_op jit(solution)/shard_map/ppermute | solution.py:420
  53.3 0.6 %late_wires.3 = bf16[4,2,64,128]{3,2,1,0:T(8,128)(2,1)S(1)} custom-call(s32[1]{0:T(128)} %bitcast.me_ref, s32[16]{0:T(128)S(1)} %get-tuple-element.52.target_ref, s32[16]{0:T(128)S(1)} %get-tuple-element.53.rank_ref, bf16[16,2,64,128]{3,2,1,0:T(8,128)(2,1)S(1)} %get-tuple-element.54.keep_ref, bf16[10,2,64,128]{3,2,1,0:T(8,128)(2,1)S(1)} %collective-permute-done.7.refs_0_, ...), custom_call_target="tpu_custom_call" | custom-call | bytes 2097152 | tf_op jit(solution)/shard_map/late_wires/pallas_call | solution.py:372
  54.0 0.1 collective-permute-start.13
  54.0 2.0 %collective-permute-start.11 = (bf16[3,2,64,128]{3,2,1,0:T(8,128)(2,1)S(1)}, bf16[3,2,64,128]{3,2,1,0:T(8,128)(2,1)S(1)}, u32[]{:S(2)}, u32[]{:S(2)}) collective-permute-start(bf16[3,2,64,128]{3,2,1,0:T(8,128)(2,1)S(1)} %get-tuple-element.62), channel_id=1, source_target_pairs={{0,1},{1,0},{2,3},{3,2},{4,5},{5,4},{6,7},{7,6},{8,9},{9,8},{10,11... | collective-permute-start | bytes 294920 | tf_op jit(solution)/shard_map/ppermute | solution.py:420
  56.0 2.9 %collective-permute-done.11.refs_3_ = bf16[3,2,64,128]{3,2,1,0:T(8,128)(2,1)S(1)} collective-permute-done((bf16[3,2,64,128]{3,2,1,0:T(8,128)(2,1)S(1)}, bf16[3,2,64,128]{3,2,1,0:T(8,128)(2,1)S(1)}, u32[]{:S(2)}, u32[]{:S(2)}) %collective-permute-start.11) | collective-permute-done | bytes 98336 | tf_op jit(solution)/shard_map/ppermute | solution.py:420
  58.9 2.0 %collective-permute-done.13.refs_6_ = bf16[4,2,64,128]{3,2,1,0:T(8,128)(2,1)S(1)} collective-permute-done((bf16[4,2,64,128]{3,2,1,0:T(8,128)(2,1)S(1)}, bf16[4,2,64,128]{3,2,1,0:T(8,128)(2,1)S(1)}, u32[]{:S(2)}, u32[]{:S(2)}) %collective-permute-start.13) | collective-permute-done | bytes 131104 | tf_op jit(solution)/shard_map/ppermute | solution.py:420
  61.0 0.0 collective-permute-done.10.refs_2_
  61.0 0.0 collective-permute-done.9.refs_1_
  61.0 1.0 %collect.1 = bf16[32,2,64,128]{3,2,1,0:T(8,128)(2,1)} custom-call(s32[1]{0:T(128)} %bitcast.me_ref, bf16[2,2,64,128]{3,2,1,0:T(8,128)(2,1)S(1)} %collective-permute-done.8.refs_0_, bf16[6,2,64,128]{3,2,1,0:T(8,128)(2,1)S(1)} %collective-permute-done.9.refs_1_, bf16[5,2,64,128]{3,2,1,0:T(8,128)(2,1)S(1)} %collective-permute-done.10.refs_2_, ...), custom_call_target="tpu_custom_call" | custom-call | bytes 2097152 | tf_op jit(solution)/shard_map/collect/pallas_call | solution.py:403
  (1 shorter events, 0.0 us)
Async XLA Ops:
  0.0 7.0 %copy-start = (s32[1,16,1]{1,2,0:T(1,128)S(1)}, s32[1,16,1]{1,2,0:T(1,128)}, u32[]{:S(2)}) copy-start(s32[1,16,1]{1,2,0:T(1,128)} %param.13) | copy-start | bytes 196
  0.0 8.5 %copy-start.2 = (s32[8,4]{0,1:T(4,128)S(1)}, s32[8,4]{0,1:T(4,128)}, u32[]{:S(2)}) copy-start(s32[8,4]{0,1:T(4,128)} %param.10) | copy-start | bytes 388
  0.0 8.7 %copy-start.1 = (bf16[1,4,2,128,320]{3,4,2,1,0:T(8,128)(2,1)S(1)}, bf16[1,4,2,128,320]{3,4,2,1,0:T(8,128)(2,1)}, u32[]{:S(2)}) copy-start(bf16[1,4,2,128,320]{3,4,2,1,0:T(8,128)(2,1)} %param.9) | copy-start | bytes 1966084
  2.3 9.8 %collective-permute-start = (bf16[2,192,512]{2,1,0:T(8,128)(2,1)S(1)}, bf16[2,192,512]{2,1,0:T(8,128)(2,1)S(1)}, u32[]{:S(2)}, u32[]{:S(2)}) collective-permute-start(bf16[2,192,512]{2,1,0:T(8,128)(2,1)S(1)} %get-tuple-element.36.sent_first_ref), channel_id=1, source_target_pairs={{0,4},{1,2},{2,1},{3,7},{4,0},{5,6},{6,5},{7,3},{8,12},{9,10},{10,... | collective-permute-start | bytes 1179656 | tf_op jit(solution)/shard_map/ppermute | solution.py:43
  2.8 13.0 %collective-permute-start.1 = (bf16[2,192,512]{2,1,0:T(8,128)(2,1)S(1)}, bf16[2,192,512]{2,1,0:T(8,128)(2,1)S(1)}, u32[]{:S(2)}, u32[]{:S(2)}) collective-permute-start(bf16[2,192,512]{2,1,0:T(8,128)(2,1)S(1)} %get-tuple-element.37.sent_second_ref), channel_id=1, source_target_pairs={{0,1},{1,0},{2,3},{3,2},{4,5},{5,4},{6,7},{7,6},{8,9},{9,8},{10,11... | collective-permute-start | bytes 1179656 | tf_op jit(solution)/shard_map/ppermute | solution.py:43
  7.0 3.5 %collective-permute-start.2 = (s32[1,16,1]{1,2,0:T(1,128)S(1)}, s32[1,16,1]{1,2,0:T(1,128)S(1)}, u32[]{:S(2)}, u32[]{:S(2)}) collective-permute-start(s32[1,16,1]{1,2,0:T(1,128)S(1)} %copy-done), channel_id=1, source_target_pairs={{0,8},{8,0},{4,12},{12,4},{16,24},{24,16},{20,28},{28,20},{1,9},{9... | collective-permute-start | bytes 200 | tf_op jit(solution)/shard_map/ppermute | solution.py:54
  17.2 2.0 %collective-permute-start.3 = (bf16[2,512,256]{2,1,0:T(8,128)(2,1)S(1)}, bf16[2,512,256]{2,1,0:T(8,128)(2,1)S(1)}, u32[]{:S(2)}, u32[]{:S(2)}) collective-permute-start(bf16[2,512,256]{2,1,0:T(8,128)(2,1)S(1)} %first_level.3), channel_id=1, source_target_pairs={{0,4},{4,0},{8,12},{12,8},{16,20},{20,16},{24,28},{28,24},{1,5},{5... | collective-permute-start | bytes 1572872 | tf_op jit(solution)/shard_map/ppermute | solution.py:54
  19.3 7.0 %collective-permute-start.4 = (bf16[2,192,256]{2,1,0:T(8,128)(2,1)S(1)}, bf16[2,192,256]{2,1,0:T(8,128)(2,1)S(1)}, u32[]{:S(2)}, u32[]{:S(2)}) collective-permute-start(bf16[2,192,256]{2,1,0:T(8,128)(2,1)S(1)} %get-tuple-element.68), channel_id=1, source_target_pairs={{0,1},{1,0},{2,3},{3,2},{4,5},{5,4},{6,7},{7,6},{8,9},{9,8},{10,11... | collective-permute-start | bytes 589832 | tf_op jit(solution)/shard_map/ppermute | solution.py:43
  21.1 5.2 %collective-permute-start.5 = (bf16[2,192,256]{2,1,0:T(8,128)(2,1)S(1)}, bf16[2,192,256]{2,1,0:T(8,128)(2,1)S(1)}, u32[]{:S(2)}, u32[]{:S(2)}) collective-permute-start(bf16[2,192,256]{2,1,0:T(8,128)(2,1)S(1)} %get-tuple-element.67), channel_id=1, source_target_pairs={{0,4},{1,2},{2,1},{3,7},{4,0},{5,6},{6,5},{7,3},{8,12},{9,10},{10,... | collective-permute-start | bytes 589832 | tf_op jit(solution)/shard_map/ppermute | solution.py:43
  27.4 6.2 %collective-permute-start.6 = (bf16[6,2,64,128]{3,2,1,0:T(8,128)(2,1)S(1)}, bf16[6,2,64,128]{3,2,1,0:T(8,128)(2,1)S(1)}, u32[]{:S(2)}, u32[]{:S(2)}) collective-permute-start(bf16[6,2,64,128]{3,2,1,0:T(8,128)(2,1)S(1)} %second_level_early.1), channel_id=1, source_target_pairs={{0,8},{8,0},{4,12},{12,4},{16,24},{24,16},{20,28},{28,20},{1,9},{9... | collective-permute-start | bytes 589832 | tf_op jit(solution)/shard_map/ppermute | solution.py:54
  33.6 8.5 %collective-permute-start.7 = (bf16[10,2,64,128]{3,2,1,0:T(8,128)(2,1)S(1)}, bf16[10,2,64,128]{3,2,1,0:T(8,128)(2,1)S(1)}, u32[]{:S(2)}, u32[]{:S(2)}) collective-permute-start(bf16[10,2,64,128]{3,2,1,0:T(8,128)(2,1)S(1)} %get-tuple-element.51), channel_id=1, source_target_pairs={{0,8},{8,0},{4,12},{12,4},{16,24},{24,16},{20,28},{28,20},{1,9},{9... | collective-permute-start | bytes 983048 | tf_op jit(solution)/shard_map/ppermute | solution.py:54
  35.7 6.4 %collective-permute-start.8 = (bf16[2,2,64,128]{3,2,1,0:T(8,128)(2,1)S(1)}, bf16[2,2,64,128]{3,2,1,0:T(8,128)(2,1)S(1)}, u32[]{:S(2)}, u32[]{:S(2)}) collective-permute-start(bf16[2,2,64,128]{3,2,1,0:T(8,128)(2,1)S(1)} %get-tuple-element.56), channel_id=1, source_target_pairs={{0,3},{1,2},{2,1},{3,0},{4,7},{5,6},{6,5},{7,4},{8,11},{9,10},{10,... | collective-permute-start | bytes 196616 | tf_op jit(solution)/shard_map/ppermute | solution.py:420
  38.9 14.4 %collective-permute-start.12 = (bf16[4,2,64,128]{3,2,1,0:T(8,128)(2,1)S(1)}, bf16[4,2,64,128]{3,2,1,0:T(8,128)(2,1)S(1)}, u32[]{:S(2)}, u32[]{:S(2)}) collective-permute-start(bf16[4,2,64,128]{3,2,1,0:T(8,128)(2,1)S(1)} %get-tuple-element.64), channel_id=1, source_target_pairs={{0,2},{1,3},{2,0},{3,1},{4,6},{5,7},{6,4},{7,5},{8,10},{9,11},{10,... | collective-permute-start | bytes 393224 | tf_op jit(solution)/shard_map/ppermute | solution.py:420
  42.9 18.1 %collective-permute-start.9 = (bf16[6,2,64,128]{3,2,1,0:T(8,128)(2,1)S(1)}, bf16[6,2,64,128]{3,2,1,0:T(8,128)(2,1)S(1)}, u32[]{:S(2)}, u32[]{:S(2)}) collective-permute-start(bf16[6,2,64,128]{3,2,1,0:T(8,128)(2,1)S(1)} %get-tuple-element.60), channel_id=1, source_target_pairs={{0,3},{1,2},{2,1},{3,0},{4,7},{5,6},{6,5},{7,4},{8,11},{9,10},{10,... | collective-permute-start | bytes 589832 | tf_op jit(solution)/shard_map/ppermute | solution.py:420
  45.9 15.0 %collective-permute-start.10 = (bf16[5,2,64,128]{3,2,1,0:T(8,128)(2,1)S(1)}, bf16[5,2,64,128]{3,2,1,0:T(8,128)(2,1)S(1)}, u32[]{:S(2)}, u32[]{:S(2)}) collective-permute-start(bf16[5,2,64,128]{3,2,1,0:T(8,128)(2,1)S(1)} %get-tuple-element.61), channel_id=1, source_target_pairs={{0,1},{1,0},{2,3},{3,2},{4,5},{5,4},{6,7},{7,6},{8,9},{9,8},{10,11... | collective-permute-start | bytes 491528 | tf_op jit(solution)/shard_map/ppermute | solution.py:420
  54.0 7.0 %collective-permute-start.13 = (bf16[4,2,64,128]{3,2,1,0:T(8,128)(2,1)S(1)}, bf16[4,2,64,128]{3,2,1,0:T(8,128)(2,1)S(1)}, u32[]{:S(2)}, u32[]{:S(2)}) collective-permute-start(bf16[4,2,64,128]{3,2,1,0:T(8,128)(2,1)S(1)} %late_wires.3), channel_id=1, source_target_pairs={{0,2},{1,3},{2,0},{3,1},{4,6},{5,7},{6,4},{7,5},{8,10},{9,11},{10,... | collective-permute-start | bytes 393224 | tf_op jit(solution)/shard_map/ppermute | solution.py:420
  54.0 4.9 %collective-permute-start.11 = (bf16[3,2,64,128]{3,2,1,0:T(8,128)(2,1)S(1)}, bf16[3,2,64,128]{3,2,1,0:T(8,128)(2,1)S(1)}, u32[]{:S(2)}, u32[]{:S(2)}) collective-permute-start(bf16[3,2,64,128]{3,2,1,0:T(8,128)(2,1)S(1)} %get-tuple-element.62), channel_id=1, source_target_pairs={{0,1},{1,0},{2,3},{3,2},{4,5},{5,4},{6,7},{7,6},{8,9},{9,8},{10,11... | collective-permute-start | bytes 294920 | tf_op jit(solution)/shard_map/ppermute | solution.py:420

commit v17 on v14

--- a/solution.py
+++ b/solution.py
@@ -34,7 +34,7 @@
         route = []
         for aper in range(apertures):
             for place in range(count):
-                other = place + 1 if (place - order) % 2 == 0 else place - 1
+                other = place + 1 if (place - order) % 2 == 1 else place - 1
                 if 0 <= other < count:
                     to = aper * count + other
                 else:
@@ -61,7 +61,7 @@
 def resample_kernel(child_hbm, kernel_hbm, first_ref, second_ref, child, kernel, own, sems):
     aper, beam = lax.axis_index("aperture"), lax.axis_index("beam")
     half, quarter = aper & 1, (aper >> 1) & 1
-    even = 1 - (beam & 1)
+    odd = beam & 1
     rows, rng = child.shape[1:]
     piece = rng // 4
     child_copy = pltpu.make_async_copy(child_hbm, child, sems.at[4])
@@ -81,8 +81,8 @@
     child_copy.wait()
     real, imag = child[0], child[1]
     margin = first_ref.shape[1]
-    tail = pl.ds(pl.multiple_of(even * (rows - margin), BLK), margin)
-    head = pl.ds(pl.multiple_of((1 - even) * (rows - margin), BLK), margin)
+    tail = pl.ds(pl.multiple_of(odd * (rows - margin), BLK), margin)
+    head = pl.ds(pl.multiple_of((1 - odd) * (rows - margin), BLK), margin)
     for side in range(2):
         columns = slice(side * 2 * piece, (side + 1) * 2 * piece)
         copies[2 * side].wait()
@@ -132,11 +132,11 @@
 
 
 def place_halos(padded, side_ref, rows, first_ref, second_ref, columns):
-    even, lowest, highest = side_ref[0], side_ref[1], side_ref[2]
+    odd, lowest, highest = side_ref[0], side_ref[1], side_ref[2]
     margin = first_ref.shape[1]
     far = margin + rows
-    place_rows(padded, pl.multiple_of(even * far, BLK), first_ref, columns)
-    place_rows(padded, pl.multiple_of((1 - even) * far, BLK), second_ref, columns)
+    place_rows(padded, pl.multiple_of(odd * far, BLK), first_ref, columns)
+    place_rows(padded, pl.multiple_of((1 - odd) * far, BLK), second_ref, columns)
     zeros = jnp.zeros((margin, padded.shape[1]), padded.dtype)
 
     @pl.when(lowest == 1)
@@ -156,9 +156,9 @@
     beams = stacked // 2
     margin = first_ref.shape[1]
     columns = slice(column, column + out_ref.shape[2])
-    even = side_ref[0]
-    tail = pl.multiple_of(margin + even * (rows - margin), BLK)
-    head = pl.multiple_of(margin + (1 - even) * (rows - margin), BLK)
+    odd = side_ref[0]
+    tail = pl.multiple_of(margin + odd * (rows - margin), BLK)
+    head = pl.multiple_of(margin + (1 - odd) * (rows - margin), BLK)
     place_rows(padded, tail, sent_first_ref, columns)
     place_rows(padded, head, sent_second_ref, columns)
     place_halos(padded, side_ref, rows, first_ref, second_ref, columns)
@@ -436,9 +436,10 @@
     margin = MARGIN_BLOCKS * BLK
     rows = subimages.shape[2]
     local_blocks = rows // BLK
-    even = (beam_index + 1) % 2
+    upper = beam_index % 2
     ends = (beam_index == 0, beam_index == beam_count - 1)
-    side = jnp.stack([even] + [end.astype(jnp.int32) for end in ends])
+    ends = [end.astype(jnp.int32) for end in ends]
+    side = jnp.stack([upper] + ends)
     me = beam_index.reshape(1)
 
     sector_count = owners.shape[1]
@@ -472,9 +473,10 @@
     keep = first_level(0, rows, begin0, side, sent, halos, weights)
     level_one = (keep.astype(jnp.float32) + other.astype(jnp.float32)).astype(jnp.bfloat16)
 
+    level_one, weights1 = lax.optimization_barrier((level_one, weights1))
     beams = level_one.shape[1]
-    first = lax.dynamic_slice_in_dim(level_one, even * (beams - margin), margin, 1)
-    second = lax.dynamic_slice_in_dim(level_one, (1 - even) * (beams - margin), margin, 1)
+    first = lax.dynamic_slice_in_dim(level_one, upper * (beams - margin), margin, 1)
+    second = lax.dynamic_slice_in_dim(level_one, (1 - upper) * (beams - margin), margin, 1)
     halos = trade_edges(first, second)
     begin1 = table_row(starts1, aper_index) - (beam_index * 2 * local_blocks - MARGIN_BLOCKS)
     keep, send, late = second_level(

time: 61.9 us -> 62 us (level)
  starting transfers between devices: 20 us -> 25 us
  waiting for transfers between devices: 25.5 us -> 20.7 us
    ppermute x6, waiting for transfers between devices: 13.9 us -> 10 us  [spread(): received.append(lax.ppermute(wire, 'beam', route) if distance else wire)]
    ppermute x6, starting transfers between devices: 9.42 us -> 13.1 us  [spread(): received.append(lax.ppermute(wire, 'beam', route) if distance else wire)]
    unnamed x8 -> x7, local copies, waits for them, and re-layouts: 2.2 us -> 0.38 us
    optimization_barrier x0 -> x1, local copies, waits for them, and re-layouts: none -> 1.82 us  [local(): level_one, weights1 = lax.optimization_barrier((level_one, weights1))]
    ppermute x4, starting transfers between devices: 6.01 us -> 7.26 us  [trade_edges(): received.append(lax.ppermute(block, ('aperture', 'beam'), route))]
  transfers between devices with their start and end apart: 14 -> 14, of which waited for: 10 -> 8; matrix products, arithmetic and copies ran while one was open for 5% -> 5% of each run, Pallas kernels for 11% -> 11%
where the time goes in v17:
time: 62 us; the launch traced here: 61.8 us
  starting transfers between devices  25 us (40%)
  waiting for transfers between devices  20.7 us (33%)
  Pallas kernels  12.6 us (20%)
  local copies, waits for them, and re-layouts  2.24 us (4%)
  other arithmetic  1.09 us (2%)
    ppermute x6, starting transfers between devices, spread(): received.append(lax.ppermute(wire, 'beam', route) if distance else wire)  13.1 us
    ppermute x6, waiting for transfers between devices, spread(): received.append(lax.ppermute(wire, 'beam', route) if distance else wire)  10 us
    ppermute x4, starting transfers between devices, trade_edges(): received.append(lax.ppermute(block, ('aperture', 'beam'), route))  7.26 us
    ppermute x4, waiting for transfers between devices, trade_edges(): received.append(lax.ppermute(block, ('aperture', 'beam'), route))  6.06 us
    ppermute x4, waiting for transfers between devices, partner(): return lax.ppermute(block, axis, route)  4.64 us
    ppermute x4, starting transfers between devices, partner(): return lax.ppermute(block, axis, route)  4.6 us
    pallas_call x2, Pallas kernels, first_level(): pl.pallas_call(functools.partial(first_level_kernel, column, rows), out_s...  2.68 us
    pallas_call x1, Pallas kernels, resample(): pl.pallas_call(resample_kernel, out_shape=(shape, shape), in_specs=[ANY,...  2.31 us
  transfers between devices with their start and end apart: 14, of which 8 were waited for; matrix products, arithmetic and copies ran while one was open for 5% of the time, Pallas kernels for 11%

profile of v17, /device:TPU:0, one launch (start us, length us, event | category | flops | bytes accessed | tf_op | source)
XLA Modules:
  0.0 61.8 jit_solution(7942795976977338009)
XLA Ops:
  0.0 0.0 copy-start
  0.0 0.0 copy-start.2
  0.0 0.0 copy-start.1
  0.0 2.3 %resample.1 = (bf16[2,192,512]{2,1,0:T(8,128)(2,1)S(1)}, bf16[2,192,512]{2,1,0:T(8,128)(2,1)S(1)}) custom-call(bf16[2,256,512]{2,1,0:T(8,128)(2,1)} %bitcast.20, bf16[2,512,512]{2,1,0:T(8,128)(2,1)} %bitcast.19), custom_call_target="tpu_custom_call" | custom-call | flops 536870912 | bytes 2097152 | tf_op jit(solution)/shard_map/resample/pallas_call | solution.py:101
  2.3 0.5 collective-permute-start
  2.8 4.1 %collective-permute-start.1 = (bf16[2,192,512]{2,1,0:T(8,128)(2,1)S(1)}, bf16[2,192,512]{2,1,0:T(8,128)(2,1)S(1)}, u32[]{:S(2)}, u32[]{:S(2)}) collective-permute-start(bf16[2,192,512]{2,1,0:T(8,128)(2,1)S(1)} %get-tuple-element.37.sent_second_ref), channel_id=1, source_target_pairs={{0,1},{1,0},{2,3},{3,2},{4,5},{5,4},{6,7},{7,6},{8,9},{9,8},{10,11... | collective-permute-start | bytes 1179656 | tf_op jit(solution)/shard_map/ppermute | solution.py:43
  7.0 0.0 copy-done
  7.0 1.5 %collective-permute-start.2 = (s32[1,16,1]{1,2,0:T(1,128)S(1)}, s32[1,16,1]{1,2,0:T(1,128)S(1)}, u32[]{:S(2)}, u32[]{:S(2)}) collective-permute-start(s32[1,16,1]{1,2,0:T(1,128)S(1)} %copy-done), channel_id=1, source_target_pairs={{0,8},{8,0},{4,12},{12,4},{16,24},{24,16},{20,28},{28,20},{1,9},{9... | collective-permute-start | bytes 200 | tf_op jit(solution)/shard_map/ppermute | solution.py:54
  8.5 0.0 copy-done.2
  8.5 0.2 subtract_reduce_fusion.starts_ref
  8.7 0.1 pad_add_fusion.side_ref
  8.7 0.0 copy-done.1
  8.8 0.4 copy.8
  9.1 1.4 %collective-permute-done.2 = s32[1,16,1]{1,2,0:T(1,128)S(1)} collective-permute-done((s32[1,16,1]{1,2,0:T(1,128)S(1)}, s32[1,16,1]{1,2,0:T(1,128)S(1)}, u32[]{:S(2)}, u32[]{:S(2)}) %collective-permute-start.2) | collective-permute-done | bytes 96 | tf_op jit(solution)/shard_map/ppermute | solution.py:54
  10.5 1.6 %plan.1 = (s32[16]{0:T(128)S(1)}, s32[16]{0:T(128)S(1)}, s32[16]{0:T(128)S(1)}, s32[16]{0:T(128)S(1)}, s32[16]{0:T(128)S(1)}) custom-call(s32[1]{0:T(128)} %bitcast.me_ref, s32[16]{0:T(128)S(1)} %bitcast.17, s32[16]{0:T(128)S(1)} %bitcast.18), custom_call_target="tpu_custom_call" | custom-call | tf_op jit(solution)/shard_map/plan/pallas_call | solution.py:311
  12.1 0.0 collective-permute-done.first_ref
  12.2 3.7 %collective-permute-done.1.second_ref = bf16[2,192,512]{2,1,0:T(8,128)(2,1)S(1)} collective-permute-done((bf16[2,192,512]{2,1,0:T(8,128)(2,1)S(1)}, bf16[2,192,512]{2,1,0:T(8,128)(2,1)S(1)}, u32[]{:S(2)}, u32[]{:S(2)}) %collective-permute-start.1) | collective-permute-done | bytes 393248 | tf_op jit(solution)/shard_map/ppermute | solution.py:43
  15.8 1.3 %first_level.3 = bf16[2,512,256]{2,1,0:T(8,128)(2,1)S(1)} custom-call(s32[4]{0:T(128)S(1)} %subtract_reduce_fusion.starts_ref, s32[3]{0:T(128)S(1)} %pad_add_fusion.side_ref, bf16[2,192,512]{2,1,0:T(8,128)(2,1)S(1)} %get-tuple-element.36.sent_first_ref, bf16[2,192,512]{2,1,0:T(8,128)(2,1)S(1)} %get-tuple-element.37.sent_second_ref, ...), custom_call_target="tpu_custom_call" | custom-call | flops 335544320 | bytes 2097152 | tf_op jit(solution)/shard_map/first_level/pallas_call | solution.py:177
  17.2 0.1 collective-permute-start.3
  17.3 1.3 %first_level.2 = bf16[2,512,256]{2,1,0:T(8,128)(2,1)S(1)} custom-call(s32[4]{0:T(128)S(1)} %subtract_reduce_fusion.starts_ref, s32[3]{0:T(128)S(1)} %pad_add_fusion.side_ref, bf16[2,192,512]{2,1,0:T(8,128)(2,1)S(1)} %get-tuple-element.36.sent_first_ref, bf16[2,192,512]{2,1,0:T(8,128)(2,1)S(1)} %get-tuple-element.37.sent_second_ref, ...), custom_call_target="tpu_custom_call" | custom-call | flops 335544320 | bytes 2097152 | tf_op jit(solution)/shard_map/first_level/pallas_call | solution.py:177
  18.6 0.5 collective-permute-done.3
  19.1 0.1 add_convert_fusion.own_ref
  19.3 0.2 collective-permute-start.4
  19.5 2.4 %collective-permute-start.5 = (bf16[2,192,256]{2,1,0:T(8,128)(2,1)S(1)}, bf16[2,192,256]{2,1,0:T(8,128)(2,1)S(1)}, u32[]{:S(2)}, u32[]{:S(2)}) collective-permute-start(bf16[2,192,256]{2,1,0:T(8,128)(2,1)S(1)} %get-tuple-element.67), channel_id=1, source_target_pairs={{0,1},{1,0},{2,3},{3,2},{4,5},{5,4},{6,7},{7,6},{8,9},{9,8},{10,11... | collective-permute-start | bytes 589832 | tf_op jit(solution)/shard_map/ppermute | solution.py:43
  21.9 0.7 %fusion.1.starts_ref = s32[8]{0:T(128)S(1)} fusion(s32[8,8]{1,0:T(8,128)} %param.12, s32[]{:T(128)S(6)} %select_n.19, s32[]{:T(128)S(6)} %sub.25), kind=kLoop, calls=%fused_computation.6 | loop fusion | flops 8 | bytes 72 | tf_op jit(solution)/shard_map/sub | solution.py:481
  22.6 1.8 %copy.9 = bf16[1,8,2,128,320]{4,3,2,1,0:T(8,128)(2,1)S(1)} copy(bf16[1,8,2,128,320]{3,4,2,1,0:T(8,128)(2,1)} %param.11) | data formatting | bytes 2621440 | tf_op jit(solution)/shard_map/optimization_barrier | solution.py:476
  24.4 0.0 collective-permute-done.4.first_ref
  24.5 2.4 %collective-permute-done.5.second_ref = bf16[2,192,256]{2,1,0:T(8,128)(2,1)S(1)} collective-permute-done((bf16[2,192,256]{2,1,0:T(8,128)(2,1)S(1)}, bf16[2,192,256]{2,1,0:T(8,128)(2,1)S(1)}, u32[]{:S(2)}, u32[]{:S(2)}) %collective-permute-start.5) | collective-permute-done | bytes 196640 | tf_op jit(solution)/shard_map/ppermute | solution.py:43
  26.8 1.0 %second_level_early.1 = bf16[6,2,64,128]{3,2,1,0:T(8,128)(2,1)S(1)} custom-call(s32[8]{0:T(128)S(1)} %fusion.1.starts_ref, s32[3]{0:T(128)S(1)} %pad_add_fusion.side_ref, s32[16]{0:T(128)S(1)} %get-tuple-element.43.sector_ref, bf16[2,512,256]{2,1,0:T(8,128)(2,1)S(1)} %add_convert_fusion.own_ref, bf16[2,192,256]{2,1,0:T(8,128)(2,1)S(1)} %collective-permute-done.4.first_ref, ...), custom_call_target="tpu_custom_call" | custom-call | flops 125829120 | bytes 1048576 | tf_op jit(solution)/shard_map/second_level_early/pallas_call | solution.py:244
  27.9 1.6 %collective-permute-start.6 = (bf16[6,2,64,128]{3,2,1,0:T(8,128)(2,1)S(1)}, bf16[6,2,64,128]{3,2,1,0:T(8,128)(2,1)S(1)}, u32[]{:S(2)}, u32[]{:S(2)}) collective-permute-start(bf16[6,2,64,128]{3,2,1,0:T(8,128)(2,1)S(1)} %second_level_early.1), channel_id=1, source_target_pairs={{0,8},{8,0},{4,12},{12,4},{16,24},{24,16},{20,28},{28,20},{1,9},{9... | collective-permute-start | bytes 589832 | tf_op jit(solution)/shard_map/ppermute | solution.py:54
  29.4 1.9 %second_level.1 = (bf16[16,2,64,128]{3,2,1,0:T(8,128)(2,1)S(1)}, bf16[10,2,64,128]{3,2,1,0:T(8,128)(2,1)S(1)}) custom-call(s32[8]{0:T(128)S(1)} %fusion.1.starts_ref, s32[3]{0:T(128)S(1)} %pad_add_fusion.side_ref, s32[16]{0:T(128)S(1)} %get-tuple-element.48.own_at_ref, s32[16]{0:T(128)S(1)} %get-tuple-element.49.other_at_ref, ...), custom_call_target="tpu_custom_call" | custom-call | flops 671088640 | bytes 4194304 | tf_op jit(solution)/shard_map/second_level/pallas_call | solution.py:255
  31.4 2.7 %collective-permute-done.6.refs_0_ = bf16[6,2,64,128]{3,2,1,0:T(8,128)(2,1)S(1)} collective-permute-done((bf16[6,2,64,128]{3,2,1,0:T(8,128)(2,1)S(1)}, bf16[6,2,64,128]{3,2,1,0:T(8,128)(2,1)S(1)}, u32[]{:S(2)}, u32[]{:S(2)}) %collective-permute-start.6) | collective-permute-done | bytes 196640 | tf_op jit(solution)/shard_map/ppermute | solution.py:54
  34.1 1.5 %collective-permute-start.7 = (bf16[10,2,64,128]{3,2,1,0:T(8,128)(2,1)S(1)}, bf16[10,2,64,128]{3,2,1,0:T(8,128)(2,1)S(1)}, u32[]{:S(2)}, u32[]{:S(2)}) collective-permute-start(bf16[10,2,64,128]{3,2,1,0:T(8,128)(2,1)S(1)} %get-tuple-element.51), channel_id=1, source_target_pairs={{0,8},{8,0},{4,12},{12,4},{16,24},{24,16},{20,28},{28,20},{1,9},{9... | collective-permute-start | bytes 983048 | tf_op jit(solution)/shard_map/ppermute | solution.py:54
  35.5 0.6 early_wires.1
  36.2 3.3 %collective-permute-start.8 = (bf16[2,2,64,128]{3,2,1,0:T(8,128)(2,1)S(1)}, bf16[2,2,64,128]{3,2,1,0:T(8,128)(2,1)S(1)}, u32[]{:S(2)}, u32[]{:S(2)}) collective-permute-start(bf16[2,2,64,128]{3,2,1,0:T(8,128)(2,1)S(1)} %get-tuple-element.56), channel_id=1, source_target_pairs={{0,3},{1,2},{2,1},{3,0},{4,7},{5,6},{6,5},{7,4},{8,11},{9,10},{10,... | collective-permute-start | bytes 196616 | tf_op jit(solution)/shard_map/ppermute | solution.py:420
  39.5 0.0 collective-permute-start.12
  39.5 2.9 %collective-permute-done.8.refs_0_ = bf16[2,2,64,128]{3,2,1,0:T(8,128)(2,1)S(1)} collective-permute-done((bf16[2,2,64,128]{3,2,1,0:T(8,128)(2,1)S(1)}, bf16[2,2,64,128]{3,2,1,0:T(8,128)(2,1)S(1)}, u32[]{:S(2)}, u32[]{:S(2)}) %collective-permute-start.8) | collective-permute-done | bytes 65568 | tf_op jit(solution)/shard_map/ppermute | solution.py:420
  42.4 0.0 collective-permute-done.7.refs_0_
  42.4 0.8 %late_wires.2 = (bf16[6,2,64,128]{3,2,1,0:T(8,128)(2,1)S(1)}, bf16[5,2,64,128]{3,2,1,0:T(8,128)(2,1)S(1)}, bf16[3,2,64,128]{3,2,1,0:T(8,128)(2,1)S(1)}, bf16[8,2,64,128]{3,2,1,0:T(8,128)(2,1)S(1)}) custom-call(s32[1]{0:T(128)} %bitcast.me_ref, s32[16]{0:T(128)S(1)} %get-tuple-element.52.target_ref, s32[16]{0:T(128)S(1)} %get-tuple-element.53.rank_ref, ...), custom_call_target="tpu_custom_call" | custom-call | bytes 2097152 | tf_op jit(solution)/shard_map/late_wires/pallas_call | solution.py:372
  43.2 3.3 %collective-permute-start.9 = (bf16[6,2,64,128]{3,2,1,0:T(8,128)(2,1)S(1)}, bf16[6,2,64,128]{3,2,1,0:T(8,128)(2,1)S(1)}, u32[]{:S(2)}, u32[]{:S(2)}) collective-permute-start(bf16[6,2,64,128]{3,2,1,0:T(8,128)(2,1)S(1)} %get-tuple-element.60), channel_id=1, source_target_pairs={{0,3},{1,2},{2,1},{3,0},{4,7},{5,6},{6,5},{7,4},{8,11},{9,10},{10,... | collective-permute-start | bytes 589832 | tf_op jit(solution)/shard_map/ppermute | solution.py:420
  46.5 2.1 %collective-permute-start.10 = (bf16[5,2,64,128]{3,2,1,0:T(8,128)(2,1)S(1)}, bf16[5,2,64,128]{3,2,1,0:T(8,128)(2,1)S(1)}, u32[]{:S(2)}, u32[]{:S(2)}) collective-permute-start(bf16[5,2,64,128]{3,2,1,0:T(8,128)(2,1)S(1)} %get-tuple-element.61), channel_id=1, source_target_pairs={{0,1},{1,0},{2,3},{3,2},{4,5},{5,4},{6,7},{7,6},{8,9},{9,8},{10,11... | collective-permute-start | bytes 491528 | tf_op jit(solution)/shard_map/ppermute | solution.py:420
  48.6 4.1 %collective-permute-done.12.refs_5_ = bf16[4,2,64,128]{3,2,1,0:T(8,128)(2,1)S(1)} collective-permute-done((bf16[4,2,64,128]{3,2,1,0:T(8,128)(2,1)S(1)}, bf16[4,2,64,128]{3,2,1,0:T(8,128)(2,1)S(1)}, u32[]{:S(2)}, u32[]{:S(2)}) %collective-permute-start.12) | collective-permute-done | bytes 131104 | tf_op jit(solution)/shard_map/ppermute | solution.py:420
  52.7 0.6 %late_wires.3 = bf16[4,2,64,128]{3,2,1,0:T(8,128)(2,1)S(1)} custom-call(s32[1]{0:T(128)} %bitcast.me_ref, s32[16]{0:T(128)S(1)} %get-tuple-element.52.target_ref, s32[16]{0:T(128)S(1)} %get-tuple-element.53.rank_ref, bf16[16,2,64,128]{3,2,1,0:T(8,128)(2,1)S(1)} %get-tuple-element.54.keep_ref, bf16[10,2,64,128]{3,2,1,0:T(8,128)(2,1)S(1)} %collective-permute-done.7.refs_0_, ...), custom_call_target="tpu_custom_call" | custom-call | bytes 2097152 | tf_op jit(solution)/shard_map/late_wires/pallas_call | solution.py:372
  53.3 0.1 collective-permute-start.13
  53.4 4.3 %collective-permute-start.11 = (bf16[3,2,64,128]{3,2,1,0:T(8,128)(2,1)S(1)}, bf16[3,2,64,128]{3,2,1,0:T(8,128)(2,1)S(1)}, u32[]{:S(2)}, u32[]{:S(2)}) collective-permute-start(bf16[3,2,64,128]{3,2,1,0:T(8,128)(2,1)S(1)} %get-tuple-element.62), channel_id=1, source_target_pairs={{0,1},{1,0},{2,3},{3,2},{4,5},{5,4},{6,7},{7,6},{8,9},{9,8},{10,11... | collective-permute-start | bytes 294920 | tf_op jit(solution)/shard_map/ppermute | solution.py:420
  57.7 3.0 %collective-permute-done.11.refs_3_ = bf16[3,2,64,128]{3,2,1,0:T(8,128)(2,1)S(1)} collective-permute-done((bf16[3,2,64,128]{3,2,1,0:T(8,128)(2,1)S(1)}, bf16[3,2,64,128]{3,2,1,0:T(8,128)(2,1)S(1)}, u32[]{:S(2)}, u32[]{:S(2)}) %collective-permute-start.11) | collective-permute-done | bytes 98336 | tf_op jit(solution)/shard_map/ppermute | solution.py:420
  60.8 0.0 collective-permute-done.13.refs_6_
  60.8 0.0 collective-permute-done.10.refs_2_
  60.8 0.0 collective-permute-done.9.refs_1_
  60.8 1.0 %collect.1 = bf16[32,2,64,128]{3,2,1,0:T(8,128)(2,1)} custom-call(s32[1]{0:T(128)} %bitcast.me_ref, bf16[2,2,64,128]{3,2,1,0:T(8,128)(2,1)S(1)} %collective-permute-done.8.refs_0_, bf16[6,2,64,128]{3,2,1,0:T(8,128)(2,1)S(1)} %collective-permute-done.9.refs_1_, bf16[5,2,64,128]{3,2,1,0:T(8,128)(2,1)S(1)} %collective-permute-done.10.refs_2_, ...), custom_call_target="tpu_custom_call" | custom-call | bytes 2097152 | tf_op jit(solution)/shard_map/collect/pallas_call | solution.py:403
  (1 shorter events, 0.0 us)
Async XLA Ops:
  0.0 7.0 %copy-start = (s32[1,16,1]{1,2,0:T(1,128)S(1)}, s32[1,16,1]{1,2,0:T(1,128)}, u32[]{:S(2)}) copy-start(s32[1,16,1]{1,2,0:T(1,128)} %param.13) | copy-start | bytes 196
  0.0 8.5 %copy-start.2 = (s32[8,4]{0,1:T(4,128)S(1)}, s32[8,4]{0,1:T(4,128)}, u32[]{:S(2)}) copy-start(s32[8,4]{0,1:T(4,128)} %param.10) | copy-start | bytes 388
  0.0 8.7 %copy-start.1 = (bf16[1,4,2,128,320]{3,4,2,1,0:T(8,128)(2,1)S(1)}, bf16[1,4,2,128,320]{3,4,2,1,0:T(8,128)(2,1)}, u32[]{:S(2)}) copy-start(bf16[1,4,2,128,320]{3,4,2,1,0:T(8,128)(2,1)} %param.9) | copy-start | bytes 1966084
  2.3 9.8 %collective-permute-start = (bf16[2,192,512]{2,1,0:T(8,128)(2,1)S(1)}, bf16[2,192,512]{2,1,0:T(8,128)(2,1)S(1)}, u32[]{:S(2)}, u32[]{:S(2)}) collective-permute-start(bf16[2,192,512]{2,1,0:T(8,128)(2,1)S(1)} %get-tuple-element.36.sent_first_ref), channel_id=1, source_target_pairs={{0,4},{1,2},{2,1},{3,7},{4,0},{5,6},{6,5},{7,3},{8,12},{9,10},{10,... | collective-permute-start | bytes 1179656 | tf_op jit(solution)/shard_map/ppermute | solution.py:43
  2.8 13.0 %collective-permute-start.1 = (bf16[2,192,512]{2,1,0:T(8,128)(2,1)S(1)}, bf16[2,192,512]{2,1,0:T(8,128)(2,1)S(1)}, u32[]{:S(2)}, u32[]{:S(2)}) collective-permute-start(bf16[2,192,512]{2,1,0:T(8,128)(2,1)S(1)} %get-tuple-element.37.sent_second_ref), channel_id=1, source_target_pairs={{0,1},{1,0},{2,3},{3,2},{4,5},{5,4},{6,7},{7,6},{8,9},{9,8},{10,11... | collective-permute-start | bytes 1179656 | tf_op jit(solution)/shard_map/ppermute | solution.py:43
  7.0 3.5 %collective-permute-start.2 = (s32[1,16,1]{1,2,0:T(1,128)S(1)}, s32[1,16,1]{1,2,0:T(1,128)S(1)}, u32[]{:S(2)}, u32[]{:S(2)}) collective-permute-start(s32[1,16,1]{1,2,0:T(1,128)S(1)} %copy-done), channel_id=1, source_target_pairs={{0,8},{8,0},{4,12},{12,4},{16,24},{24,16},{20,28},{28,20},{1,9},{9... | collective-permute-start | bytes 200 | tf_op jit(solution)/shard_map/ppermute | solution.py:54
  17.2 2.0 %collective-permute-start.3 = (bf16[2,512,256]{2,1,0:T(8,128)(2,1)S(1)}, bf16[2,512,256]{2,1,0:T(8,128)(2,1)S(1)}, u32[]{:S(2)}, u32[]{:S(2)}) collective-permute-start(bf16[2,512,256]{2,1,0:T(8,128)(2,1)S(1)} %first_level.3), channel_id=1, source_target_pairs={{0,4},{4,0},{8,12},{12,8},{16,20},{20,16},{24,28},{28,24},{1,5},{5... | collective-permute-start | bytes 1572872 | tf_op jit(solution)/shard_map/ppermute | solution.py:54
  19.3 5.1 %collective-permute-start.4 = (bf16[2,192,256]{2,1,0:T(8,128)(2,1)S(1)}, bf16[2,192,256]{2,1,0:T(8,128)(2,1)S(1)}, u32[]{:S(2)}, u32[]{:S(2)}) collective-permute-start(bf16[2,192,256]{2,1,0:T(8,128)(2,1)S(1)} %get-tuple-element.68), channel_id=1, source_target_pairs={{0,4},{1,2},{2,1},{3,7},{4,0},{5,6},{6,5},{7,3},{8,12},{9,10},{10,... | collective-permute-start | bytes 589832 | tf_op jit(solution)/shard_map/ppermute | solution.py:43
  19.5 7.3 %collective-permute-start.5 = (bf16[2,192,256]{2,1,0:T(8,128)(2,1)S(1)}, bf16[2,192,256]{2,1,0:T(8,128)(2,1)S(1)}, u32[]{:S(2)}, u32[]{:S(2)}) collective-permute-start(bf16[2,192,256]{2,1,0:T(8,128)(2,1)S(1)} %get-tuple-element.67), channel_id=1, source_target_pairs={{0,1},{1,0},{2,3},{3,2},{4,5},{5,4},{6,7},{7,6},{8,9},{9,8},{10,11... | collective-permute-start | bytes 589832 | tf_op jit(solution)/shard_map/ppermute | solution.py:43
  27.9 6.2 %collective-permute-start.6 = (bf16[6,2,64,128]{3,2,1,0:T(8,128)(2,1)S(1)}, bf16[6,2,64,128]{3,2,1,0:T(8,128)(2,1)S(1)}, u32[]{:S(2)}, u32[]{:S(2)}) collective-permute-start(bf16[6,2,64,128]{3,2,1,0:T(8,128)(2,1)S(1)} %second_level_early.1), channel_id=1, source_target_pairs={{0,8},{8,0},{4,12},{12,4},{16,24},{24,16},{20,28},{28,20},{1,9},{9... | collective-permute-start | bytes 589832 | tf_op jit(solution)/shard_map/ppermute | solution.py:54
  34.1 8.3 %collective-permute-start.7 = (bf16[10,2,64,128]{3,2,1,0:T(8,128)(2,1)S(1)}, bf16[10,2,64,128]{3,2,1,0:T(8,128)(2,1)S(1)}, u32[]{:S(2)}, u32[]{:S(2)}) collective-permute-start(bf16[10,2,64,128]{3,2,1,0:T(8,128)(2,1)S(1)} %get-tuple-element.51), channel_id=1, source_target_pairs={{0,8},{8,0},{4,12},{12,4},{16,24},{24,16},{20,28},{28,20},{1,9},{9... | collective-permute-start | bytes 983048 | tf_op jit(solution)/shard_map/ppermute | solution.py:54
  36.2 6.2 %collective-permute-start.8 = (bf16[2,2,64,128]{3,2,1,0:T(8,128)(2,1)S(1)}, bf16[2,2,64,128]{3,2,1,0:T(8,128)(2,1)S(1)}, u32[]{:S(2)}, u32[]{:S(2)}) collective-permute-start(bf16[2,2,64,128]{3,2,1,0:T(8,128)(2,1)S(1)} %get-tuple-element.56), channel_id=1, source_target_pairs={{0,3},{1,2},{2,1},{3,0},{4,7},{5,6},{6,5},{7,4},{8,11},{9,10},{10,... | collective-permute-start | bytes 196616 | tf_op jit(solution)/shard_map/ppermute | solution.py:420
  39.5 13.2 %collective-permute-start.12 = (bf16[4,2,64,128]{3,2,1,0:T(8,128)(2,1)S(1)}, bf16[4,2,64,128]{3,2,1,0:T(8,128)(2,1)S(1)}, u32[]{:S(2)}, u32[]{:S(2)}) collective-permute-start(bf16[4,2,64,128]{3,2,1,0:T(8,128)(2,1)S(1)} %get-tuple-element.64), channel_id=1, source_target_pairs={{0,2},{1,3},{2,0},{3,1},{4,6},{5,7},{6,4},{7,5},{8,10},{9,11},{10,... | collective-permute-start | bytes 393224 | tf_op jit(solution)/shard_map/ppermute | solution.py:420
  43.2 17.6 %collective-permute-start.9 = (bf16[6,2,64,128]{3,2,1,0:T(8,128)(2,1)S(1)}, bf16[6,2,64,128]{3,2,1,0:T(8,128)(2,1)S(1)}, u32[]{:S(2)}, u32[]{:S(2)}) collective-permute-start(bf16[6,2,64,128]{3,2,1,0:T(8,128)(2,1)S(1)} %get-tuple-element.60), channel_id=1, source_target_pairs={{0,3},{1,2},{2,1},{3,0},{4,7},{5,6},{6,5},{7,4},{8,11},{9,10},{10,... | collective-permute-start | bytes 589832 | tf_op jit(solution)/shard_map/ppermute | solution.py:420
  46.5 14.3 %collective-permute-start.10 = (bf16[5,2,64,128]{3,2,1,0:T(8,128)(2,1)S(1)}, bf16[5,2,64,128]{3,2,1,0:T(8,128)(2,1)S(1)}, u32[]{:S(2)}, u32[]{:S(2)}) collective-permute-start(bf16[5,2,64,128]{3,2,1,0:T(8,128)(2,1)S(1)} %get-tuple-element.61), channel_id=1, source_target_pairs={{0,1},{1,0},{2,3},{3,2},{4,5},{5,4},{6,7},{7,6},{8,9},{9,8},{10,11... | collective-permute-start | bytes 491528 | tf_op jit(solution)/shard_map/ppermute | solution.py:420
  53.3 7.4 %collective-permute-start.13 = (bf16[4,2,64,128]{3,2,1,0:T(8,128)(2,1)S(1)}, bf16[4,2,64,128]{3,2,1,0:T(8,128)(2,1)S(1)}, u32[]{:S(2)}, u32[]{:S(2)}) collective-permute-start(bf16[4,2,64,128]{3,2,1,0:T(8,128)(2,1)S(1)} %late_wires.3), channel_id=1, source_target_pairs={{0,2},{1,3},{2,0},{3,1},{4,6},{5,7},{6,4},{7,5},{8,10},{9,11},{10,... | collective-permute-start | bytes 393224 | tf_op jit(solution)/shard_map/ppermute | solution.py:420
  53.4 7.4 %collective-permute-start.11 = (bf16[3,2,64,128]{3,2,1,0:T(8,128)(2,1)S(1)}, bf16[3,2,64,128]{3,2,1,0:T(8,128)(2,1)S(1)}, u32[]{:S(2)}, u32[]{:S(2)}) collective-permute-start(bf16[3,2,64,128]{3,2,1,0:T(8,128)(2,1)S(1)} %get-tuple-element.62), channel_id=1, source_target_pairs={{0,1},{1,0},{2,3},{3,2},{4,5},{5,4},{6,7},{7,6},{8,9},{9,8},{10,11... | collective-permute-start | bytes 294920 | tf_op jit(solution)/shard_map/ppermute | solution.py:420

commit v18 on v14

--- a/solution.py
+++ b/solution.py
@@ -451,11 +451,12 @@
     early_spans = [(distance, 0, shorter) for distance in odd]
     early_spans += [(distance, 0, longer) for distance in others]
     late_spans = [(distance, shorter, capacity) for distance in odd]
+    last_spans = [(distance, longer, capacity) for distance in others]
+    third = (3 * capacity + 7) // 8
     for distance in range(1, beam_count // 2):
-        cut = (5 * capacity + 4) // 8
-        late_spans += [(distance, 0, cut), (distance, cut, capacity)]
-    late_spans.append((0, 0, capacity))
-    last_spans = [(distance, longer, capacity) for distance in others]
+        cuts = sorted({0, min(third, capacity), min(2 * third, capacity), capacity})
+        last_spans += [(distance, low, high) for low, high in zip(cuts, cuts[1:])]
+    last_spans.append((0, 0, capacity))
 
     sent = resample(subimages[0], range_kernel[0], margin)
     halos = trade_edges(*sent)

time: 61.9 us -> 62.3 us (level)
  starting transfers between devices: 20 us -> 22.2 us
  waiting for transfers between devices: 25.5 us -> 23.8 us
    ppermute x6 -> x7, starting transfers between devices: 9.42 us -> 11.5 us  [spread(): received.append(lax.ppermute(wire, 'beam', route) if distance else wire)]
    ppermute x6 -> x7, waiting for transfers between devices: 13.9 us -> 12.3 us  [spread(): received.append(lax.ppermute(wire, 'beam', route) if distance else wire)]
  transfers between devices with their start and end apart: 14 -> 15, of which waited for: 10 -> 7; matrix products, arithmetic and copies ran while one was open for 5% -> 5% of each run, Pallas kernels for 11% -> 11%
where the time goes in v18:
time: 62.3 us; the launch traced here: 62.1 us
  waiting for transfers between devices  23.8 us (38%)
  starting transfers between devices  22.2 us (36%)
  Pallas kernels  12.7 us (20%)
  local copies, waits for them, and re-layouts  2.24 us (4%)
  other arithmetic  1.1 us (2%)
    ppermute x7, waiting for transfers between devices, spread(): received.append(lax.ppermute(wire, 'beam', route) if distance else wire)  12.3 us
    ppermute x7, starting transfers between devices, spread(): received.append(lax.ppermute(wire, 'beam', route) if distance else wire)  11.5 us
    ppermute x4, waiting for transfers between devices, trade_edges(): received.append(lax.ppermute(block, ('aperture', 'beam'), route))  6.63 us
    ppermute x4, starting transfers between devices, trade_edges(): received.append(lax.ppermute(block, ('aperture', 'beam'), route))  6.01 us
    ppermute x4, waiting for transfers between devices, partner(): return lax.ppermute(block, axis, route)  4.94 us
    ppermute x4, starting transfers between devices, partner(): return lax.ppermute(block, axis, route)  4.6 us
    pallas_call x2, Pallas kernels, first_level(): pl.pallas_call(functools.partial(first_level_kernel, column, rows), out_s...  2.68 us
    pallas_call x1, Pallas kernels, resample(): pl.pallas_call(resample_kernel, out_shape=(shape, shape), in_specs=[ANY,...  2.31 us
  transfers between devices with their start and end apart: 15, of which 7 were waited for; matrix products, arithmetic and copies ran while one was open for 5% of the time, Pallas kernels for 11%

profile of v18, /device:TPU:0, one launch (start us, length us, event | category | flops | bytes accessed | tf_op | source)
XLA Modules:
  0.0 62.1 jit_solution(14184868337430286217)
XLA Ops:
  0.0 0.0 copy-start
  0.0 0.0 copy-start.2
  0.0 0.0 copy-start.1
  0.0 2.3 %resample.1 = (bf16[2,192,512]{2,1,0:T(8,128)(2,1)S(1)}, bf16[2,192,512]{2,1,0:T(8,128)(2,1)S(1)}) custom-call(bf16[2,256,512]{2,1,0:T(8,128)(2,1)} %bitcast.20, bf16[2,512,512]{2,1,0:T(8,128)(2,1)} %bitcast.19), custom_call_target="tpu_custom_call" | custom-call | flops 536870912 | bytes 2097152 | tf_op jit(solution)/shard_map/resample/pallas_call | solution.py:101
  2.3 3.1 %collective-permute-start = (bf16[2,192,512]{2,1,0:T(8,128)(2,1)S(1)}, bf16[2,192,512]{2,1,0:T(8,128)(2,1)S(1)}, u32[]{:S(2)}, u32[]{:S(2)}) collective-permute-start(bf16[2,192,512]{2,1,0:T(8,128)(2,1)S(1)} %get-tuple-element.35.sent_first_ref), channel_id=1, source_target_pairs={{0,1},{1,0},{2,3},{3,2},{4,5},{5,4},{6,7},{7,6},{8,9},{9,8},{10,11... | collective-permute-start | bytes 1179656 | tf_op jit(solution)/shard_map/ppermute | solution.py:43
  5.4 0.0 collective-permute-start.1
  5.4 0.0 copy-done
  5.4 1.5 %collective-permute-start.2 = (s32[1,16,1]{1,2,0:T(1,128)S(1)}, s32[1,16,1]{1,2,0:T(1,128)S(1)}, u32[]{:S(2)}, u32[]{:S(2)}) collective-permute-start(s32[1,16,1]{1,2,0:T(1,128)S(1)} %copy-done), channel_id=1, source_target_pairs={{0,8},{8,0},{4,12},{12,4},{16,24},{24,16},{20,28},{28,20},{1,9},{9... | collective-permute-start | bytes 200 | tf_op jit(solution)/shard_map/ppermute | solution.py:54
  6.9 0.0 copy-done.2
  6.9 0.2 subtract_reduce_fusion.starts_ref
  7.1 0.1 pad_add_fusion.side_ref
  7.2 0.0 copy-done.1
  7.2 0.4 copy.8
  7.6 1.4 %collective-permute-done.2 = s32[1,16,1]{1,2,0:T(1,128)S(1)} collective-permute-done((s32[1,16,1]{1,2,0:T(1,128)S(1)}, s32[1,16,1]{1,2,0:T(1,128)S(1)}, u32[]{:S(2)}, u32[]{:S(2)}) %collective-permute-start.2) | collective-permute-done | bytes 96 | tf_op jit(solution)/shard_map/ppermute | solution.py:54
  9.0 1.6 %plan.1 = (s32[16]{0:T(128)S(1)}, s32[16]{0:T(128)S(1)}, s32[16]{0:T(128)S(1)}, s32[16]{0:T(128)S(1)}, s32[16]{0:T(128)S(1)}) custom-call(s32[1]{0:T(128)} %bitcast.me_ref, s32[16]{0:T(128)S(1)} %bitcast.17, s32[16]{0:T(128)S(1)} %bitcast.18), custom_call_target="tpu_custom_call" | custom-call | tf_op jit(solution)/shard_map/plan/pallas_call | solution.py:311
  10.6 4.0 %collective-permute-done.first_ref = bf16[2,192,512]{2,1,0:T(8,128)(2,1)S(1)} collective-permute-done((bf16[2,192,512]{2,1,0:T(8,128)(2,1)S(1)}, bf16[2,192,512]{2,1,0:T(8,128)(2,1)S(1)}, u32[]{:S(2)}, u32[]{:S(2)}) %collective-permute-start) | collective-permute-done | bytes 393248 | tf_op jit(solution)/shard_map/ppermute | solution.py:43
  14.5 0.0 collective-permute-done.1.second_ref
  14.5 1.3 %first_level.3 = bf16[2,512,256]{2,1,0:T(8,128)(2,1)S(1)} custom-call(s32[4]{0:T(128)S(1)} %subtract_reduce_fusion.starts_ref, s32[3]{0:T(128)S(1)} %pad_add_fusion.side_ref, bf16[2,192,512]{2,1,0:T(8,128)(2,1)S(1)} %get-tuple-element.35.sent_first_ref, bf16[2,192,512]{2,1,0:T(8,128)(2,1)S(1)} %get-tuple-element.36.sent_second_ref, ...), custom_call_target="tpu_custom_call" | custom-call | flops 335544320 | bytes 2097152 | tf_op jit(solution)/shard_map/first_level/pallas_call | solution.py:177
  15.9 0.1 collective-permute-start.3
  16.0 1.3 %first_level.2 = bf16[2,512,256]{2,1,0:T(8,128)(2,1)S(1)} custom-call(s32[4]{0:T(128)S(1)} %subtract_reduce_fusion.starts_ref, s32[3]{0:T(128)S(1)} %pad_add_fusion.side_ref, bf16[2,192,512]{2,1,0:T(8,128)(2,1)S(1)} %get-tuple-element.35.sent_first_ref, bf16[2,192,512]{2,1,0:T(8,128)(2,1)S(1)} %get-tuple-element.36.sent_second_ref, ...), custom_call_target="tpu_custom_call" | custom-call | flops 335544320 | bytes 2097152 | tf_op jit(solution)/shard_map/first_level/pallas_call | solution.py:177
  17.3 0.5 collective-permute-done.3
  17.9 0.1 add_convert_fusion.own_ref
  18.0 2.9 %collective-permute-start.4 = (bf16[2,192,256]{2,1,0:T(8,128)(2,1)S(1)}, bf16[2,192,256]{2,1,0:T(8,128)(2,1)S(1)}, u32[]{:S(2)}, u32[]{:S(2)}) collective-permute-start(bf16[2,192,256]{2,1,0:T(8,128)(2,1)S(1)} %get-tuple-element.66), channel_id=1, source_target_pairs={{0,1},{1,0},{2,3},{3,2},{4,5},{5,4},{6,7},{7,6},{8,9},{9,8},{10,11... | collective-permute-start | bytes 589832 | tf_op jit(solution)/shard_map/ppermute | solution.py:43
  21.0 0.0 collective-permute-start.5
  21.0 1.8 %copy.9 = bf16[1,8,2,128,320]{4,3,2,1,0:T(8,128)(2,1)S(1)} copy(bf16[1,8,2,128,320]{3,4,2,1,0:T(8,128)(2,1)} %param.11) | data formatting | bytes 2621440 | tf_op args[4]
  22.8 0.7 %fusion.1.starts_ref = s32[8]{0:T(128)S(1)} fusion(s32[8,8]{1,0:T(8,128)} %param.12, s32[]{:T(128)S(6)} %select_n.19, s32[]{:T(128)S(6)} %sub.25), kind=kLoop, calls=%fused_computation.6 | loop fusion | flops 8 | bytes 72 | tf_op jit(solution)/shard_map/sub | solution.py:480
  23.5 2.7 %collective-permute-done.4.first_ref = bf16[2,192,256]{2,1,0:T(8,128)(2,1)S(1)} collective-permute-done((bf16[2,192,256]{2,1,0:T(8,128)(2,1)S(1)}, bf16[2,192,256]{2,1,0:T(8,128)(2,1)S(1)}, u32[]{:S(2)}, u32[]{:S(2)}) %collective-permute-start.4) | collective-permute-done | bytes 196640 | tf_op jit(solution)/shard_map/ppermute | solution.py:43
  26.2 0.0 collective-permute-done.5.second_ref
  26.2 1.0 %second_level_early.1 = bf16[6,2,64,128]{3,2,1,0:T(8,128)(2,1)S(1)} custom-call(s32[8]{0:T(128)S(1)} %fusion.1.starts_ref, s32[3]{0:T(128)S(1)} %pad_add_fusion.side_ref, s32[16]{0:T(128)S(1)} %get-tuple-element.42.sector_ref, bf16[2,512,256]{2,1,0:T(8,128)(2,1)S(1)} %add_convert_fusion.own_ref, bf16[2,192,256]{2,1,0:T(8,128)(2,1)S(1)} %collective-permute-done.4.first_ref, ...), custom_call_target="tpu_custom_call" | custom-call | flops 125829120 | bytes 1048576 | tf_op jit(solution)/shard_map/second_level_early/pallas_call | solution.py:244
  27.2 1.6 %collective-permute-start.6 = (bf16[6,2,64,128]{3,2,1,0:T(8,128)(2,1)S(1)}, bf16[6,2,64,128]{3,2,1,0:T(8,128)(2,1)S(1)}, u32[]{:S(2)}, u32[]{:S(2)}) collective-permute-start(bf16[6,2,64,128]{3,2,1,0:T(8,128)(2,1)S(1)} %second_level_early.1), channel_id=1, source_target_pairs={{0,8},{8,0},{4,12},{12,4},{16,24},{24,16},{20,28},{28,20},{1,9},{9... | collective-permute-start | bytes 589832 | tf_op jit(solution)/shard_map/ppermute | solution.py:54
  28.8 1.9 %second_level.1 = (bf16[16,2,64,128]{3,2,1,0:T(8,128)(2,1)S(1)}, bf16[10,2,64,128]{3,2,1,0:T(8,128)(2,1)S(1)}) custom-call(s32[8]{0:T(128)S(1)} %fusion.1.starts_ref, s32[3]{0:T(128)S(1)} %pad_add_fusion.side_ref, s32[16]{0:T(128)S(1)} %get-tuple-element.45.own_at_ref, s32[16]{0:T(128)S(1)} %get-tuple-element.46.other_at_ref, ...), custom_call_target="tpu_custom_call" | custom-call | flops 671088640 | bytes 4194304 | tf_op jit(solution)/shard_map/second_level/pallas_call | solution.py:255
  30.7 3.0 %collective-permute-done.6.refs_0_ = bf16[6,2,64,128]{3,2,1,0:T(8,128)(2,1)S(1)} collective-permute-done((bf16[6,2,64,128]{3,2,1,0:T(8,128)(2,1)S(1)}, bf16[6,2,64,128]{3,2,1,0:T(8,128)(2,1)S(1)}, u32[]{:S(2)}, u32[]{:S(2)}) %collective-permute-start.6) | collective-permute-done | bytes 196640 | tf_op jit(solution)/shard_map/ppermute | solution.py:54
  33.7 1.5 %collective-permute-start.7 = (bf16[10,2,64,128]{3,2,1,0:T(8,128)(2,1)S(1)}, bf16[10,2,64,128]{3,2,1,0:T(8,128)(2,1)S(1)}, u32[]{:S(2)}, u32[]{:S(2)}) collective-permute-start(bf16[10,2,64,128]{3,2,1,0:T(8,128)(2,1)S(1)} %get-tuple-element.48), channel_id=1, source_target_pairs={{0,8},{8,0},{4,12},{12,4},{16,24},{24,16},{20,28},{28,20},{1,9},{9... | collective-permute-start | bytes 983048 | tf_op jit(solution)/shard_map/ppermute | solution.py:54
  35.2 0.6 early_wires.1
  35.8 2.7 %collective-permute-start.10 = (bf16[4,2,64,128]{3,2,1,0:T(8,128)(2,1)S(1)}, bf16[4,2,64,128]{3,2,1,0:T(8,128)(2,1)S(1)}, u32[]{:S(2)}, u32[]{:S(2)}) collective-permute-start(bf16[4,2,64,128]{3,2,1,0:T(8,128)(2,1)S(1)} %get-tuple-element.57), channel_id=1, source_target_pairs={{0,2},{1,3},{2,0},{3,1},{4,6},{5,7},{6,4},{7,5},{8,10},{9,11},{10,... | collective-permute-start | bytes 393224 | tf_op jit(solution)/shard_map/ppermute | solution.py:420
  38.5 1.3 %collective-permute-start.8 = (bf16[2,2,64,128]{3,2,1,0:T(8,128)(2,1)S(1)}, bf16[2,2,64,128]{3,2,1,0:T(8,128)(2,1)S(1)}, u32[]{:S(2)}, u32[]{:S(2)}) collective-permute-start(bf16[2,2,64,128]{3,2,1,0:T(8,128)(2,1)S(1)} %get-tuple-element.53), channel_id=1, source_target_pairs={{0,3},{1,2},{2,1},{3,0},{4,7},{5,6},{6,5},{7,4},{8,11},{9,10},{10,... | collective-permute-start | bytes 196616 | tf_op jit(solution)/shard_map/ppermute | solution.py:420
  39.7 4.9 %collective-permute-done.8.refs_0_ = bf16[2,2,64,128]{3,2,1,0:T(8,128)(2,1)S(1)} collective-permute-done((bf16[2,2,64,128]{3,2,1,0:T(8,128)(2,1)S(1)}, bf16[2,2,64,128]{3,2,1,0:T(8,128)(2,1)S(1)}, u32[]{:S(2)}, u32[]{:S(2)}) %collective-permute-start.8) | collective-permute-done | bytes 65568 | tf_op jit(solution)/shard_map/ppermute | solution.py:420
  44.6 0.0 collective-permute-done.7.refs_0_
  44.6 0.7 %late_wires.2 = bf16[6,2,64,128]{3,2,1,0:T(8,128)(2,1)S(1)} custom-call(s32[1]{0:T(128)} %bitcast.me_ref, s32[16]{0:T(128)S(1)} %get-tuple-element.49.target_ref, s32[16]{0:T(128)S(1)} %get-tuple-element.50.rank_ref, bf16[16,2,64,128]{3,2,1,0:T(8,128)(2,1)S(1)} %get-tuple-element.51.keep_ref, bf16[10,2,64,128]{3,2,1,0:T(8,128)(2,1)S(1)} %collective-permute-done.7.refs_0_, ...), custom_call_target="tpu_custom_call" | custom-call | bytes 2097152 | tf_op jit(solution)/shard_map/late_wires/pallas_call | solution.py:372
  45.3 1.5 %collective-permute-start.9 = (bf16[6,2,64,128]{3,2,1,0:T(8,128)(2,1)S(1)}, bf16[6,2,64,128]{3,2,1,0:T(8,128)(2,1)S(1)}, u32[]{:S(2)}, u32[]{:S(2)}) collective-permute-start(bf16[6,2,64,128]{3,2,1,0:T(8,128)(2,1)S(1)} %late_wires.2), channel_id=1, source_target_pairs={{0,3},{1,2},{2,1},{3,0},{4,7},{5,6},{6,5},{7,4},{8,11},{9,10},{10,... | collective-permute-start | bytes 589832 | tf_op jit(solution)/shard_map/ppermute | solution.py:420
  46.8 0.0 collective-permute-done.10.refs_2_
  46.8 0.8 %late_wires.3 = (bf16[4,2,64,128]{3,2,1,0:T(8,128)(2,1)S(1)}, bf16[3,2,64,128]{3,2,1,0:T(8,128)(2,1)S(1)}, bf16[3,2,64,128]{3,2,1,0:T(8,128)(2,1)S(1)}, bf16[2,2...) custom-call(s32[1]{0:T(128)} %bitcast.me_ref, s32[16]{0:T(128)S(1)} %get-tuple-element.49.target_ref, ...), custom_call_target="tpu_custom_call" | custom-call | bytes 2097152 | tf_op jit(solution)/shard_map/late_wires/pallas_call | solution.py:372
  47.6 3.5 %collective-permute-start.11 = (bf16[4,2,64,128]{3,2,1,0:T(8,128)(2,1)S(1)}, bf16[4,2,64,128]{3,2,1,0:T(8,128)(2,1)S(1)}, u32[]{:S(2)}, u32[]{:S(2)}) collective-permute-start(bf16[4,2,64,128]{3,2,1,0:T(8,128)(2,1)S(1)} %get-tuple-element.60), channel_id=1, source_target_pairs={{0,2},{1,3},{2,0},{3,1},{4,6},{5,7},{6,4},{7,5},{8,10},{9,11},{10,... | collective-permute-start | bytes 393224 | tf_op jit(solution)/shard_map/ppermute | solution.py:420
  51.1 0.6 collective-permute-start.12
  51.7 1.4 %collective-permute-start.13 = (bf16[3,2,64,128]{3,2,1,0:T(8,128)(2,1)S(1)}, bf16[3,2,64,128]{3,2,1,0:T(8,128)(2,1)S(1)}, u32[]{:S(2)}, u32[]{:S(2)}) collective-permute-start(bf16[3,2,64,128]{3,2,1,0:T(8,128)(2,1)S(1)} %get-tuple-element.62), channel_id=1, source_target_pairs={{0,1},{1,0},{2,3},{3,2},{4,5},{5,4},{6,7},{7,6},{8,9},{9,8},{10,11... | collective-permute-start | bytes 294920 | tf_op jit(solution)/shard_map/ppermute | solution.py:420
  53.1 0.6 collective-permute-start.14
  53.7 7.3 %collective-permute-done.14.refs_6_ = bf16[2,2,64,128]{3,2,1,0:T(8,128)(2,1)S(1)} collective-permute-done((bf16[2,2,64,128]{3,2,1,0:T(8,128)(2,1)S(1)}, bf16[2,2,64,128]{3,2,1,0:T(8,128)(2,1)S(1)}, u32[]{:S(2)}, u32[]{:S(2)}) %collective-permute-start.14) | collective-permute-done | bytes 65568 | tf_op jit(solution)/shard_map/ppermute | solution.py:420
  61.1 0.0 collective-permute-done.12.refs_4_
  61.1 0.0 collective-permute-done.13.refs_5_
  61.1 0.0 collective-permute-done.11.refs_3_
  61.1 0.0 collective-permute-done.9.refs_1_
  61.1 1.0 %collect.1 = bf16[32,2,64,128]{3,2,1,0:T(8,128)(2,1)} custom-call(s32[1]{0:T(128)} %bitcast.me_ref, bf16[2,2,64,128]{3,2,1,0:T(8,128)(2,1)S(1)} %collective-permute-done.8.refs_0_, bf16[6,2,64,128]{3,2,1,0:T(8,128)(2,1)S(1)} %collective-permute-done.9.refs_1_, bf16[4,2,64,128]{3,2,1,0:T(8,128)(2,1)S(1)} %collective-permute-done.10.refs_2_, ...), custom_call_target="tpu_custom_call" | custom-call | bytes 2097152 | tf_op jit(solution)/shard_map/collect/pallas_call | solution.py:403
  (1 shorter events, 0.0 us)
Async XLA Ops:
  0.0 5.4 %copy-start = (s32[1,16,1]{1,2,0:T(1,128)S(1)}, s32[1,16,1]{1,2,0:T(1,128)}, u32[]{:S(2)}) copy-start(s32[1,16,1]{1,2,0:T(1,128)} %param.13) | copy-start | bytes 196
  0.0 6.9 %copy-start.2 = (s32[8,4]{0,1:T(4,128)S(1)}, s32[8,4]{0,1:T(4,128)}, u32[]{:S(2)}) copy-start(s32[8,4]{0,1:T(4,128)} %param.10) | copy-start | bytes 388
  0.0 7.2 %copy-start.1 = (bf16[1,4,2,128,320]{3,4,2,1,0:T(8,128)(2,1)S(1)}, bf16[1,4,2,128,320]{3,4,2,1,0:T(8,128)(2,1)}, u32[]{:S(2)}) copy-start(bf16[1,4,2,128,320]{3,4,2,1,0:T(8,128)(2,1)} %param.9) | copy-start | bytes 1966084
  2.3 12.2 %collective-permute-start = (bf16[2,192,512]{2,1,0:T(8,128)(2,1)S(1)}, bf16[2,192,512]{2,1,0:T(8,128)(2,1)S(1)}, u32[]{:S(2)}, u32[]{:S(2)}) collective-permute-start(bf16[2,192,512]{2,1,0:T(8,128)(2,1)S(1)} %get-tuple-element.35.sent_first_ref), channel_id=1, source_target_pairs={{0,1},{1,0},{2,3},{3,2},{4,5},{5,4},{6,7},{7,6},{8,9},{9,8},{10,11... | collective-permute-start | bytes 1179656 | tf_op jit(solution)/shard_map/ppermute | solution.py:43
  5.4 9.1 %collective-permute-start.1 = (bf16[2,192,512]{2,1,0:T(8,128)(2,1)S(1)}, bf16[2,192,512]{2,1,0:T(8,128)(2,1)S(1)}, u32[]{:S(2)}, u32[]{:S(2)}) collective-permute-start(bf16[2,192,512]{2,1,0:T(8,128)(2,1)S(1)} %get-tuple-element.36.sent_second_ref), channel_id=1, source_target_pairs={{0,4},{1,2},{2,1},{3,7},{4,0},{5,6},{6,5},{7,3},{8,12},{9,10},{10,... | collective-permute-start | bytes 1179656 | tf_op jit(solution)/shard_map/ppermute | solution.py:43
  5.4 3.5 %collective-permute-start.2 = (s32[1,16,1]{1,2,0:T(1,128)S(1)}, s32[1,16,1]{1,2,0:T(1,128)S(1)}, u32[]{:S(2)}, u32[]{:S(2)}) collective-permute-start(s32[1,16,1]{1,2,0:T(1,128)S(1)} %copy-done), channel_id=1, source_target_pairs={{0,8},{8,0},{4,12},{12,4},{16,24},{24,16},{20,28},{28,20},{1,9},{9... | collective-permute-start | bytes 200 | tf_op jit(solution)/shard_map/ppermute | solution.py:54
  15.9 2.0 %collective-permute-start.3 = (bf16[2,512,256]{2,1,0:T(8,128)(2,1)S(1)}, bf16[2,512,256]{2,1,0:T(8,128)(2,1)S(1)}, u32[]{:S(2)}, u32[]{:S(2)}) collective-permute-start(bf16[2,512,256]{2,1,0:T(8,128)(2,1)S(1)} %first_level.3), channel_id=1, source_target_pairs={{0,4},{4,0},{8,12},{12,8},{16,20},{20,16},{24,28},{28,24},{1,5},{5... | collective-permute-start | bytes 1572872 | tf_op jit(solution)/shard_map/ppermute | solution.py:54
  18.0 8.1 %collective-permute-start.4 = (bf16[2,192,256]{2,1,0:T(8,128)(2,1)S(1)}, bf16[2,192,256]{2,1,0:T(8,128)(2,1)S(1)}, u32[]{:S(2)}, u32[]{:S(2)}) collective-permute-start(bf16[2,192,256]{2,1,0:T(8,128)(2,1)S(1)} %get-tuple-element.66), channel_id=1, source_target_pairs={{0,1},{1,0},{2,3},{3,2},{4,5},{5,4},{6,7},{7,6},{8,9},{9,8},{10,11... | collective-permute-start | bytes 589832 | tf_op jit(solution)/shard_map/ppermute | solution.py:43
  21.0 5.2 %collective-permute-start.5 = (bf16[2,192,256]{2,1,0:T(8,128)(2,1)S(1)}, bf16[2,192,256]{2,1,0:T(8,128)(2,1)S(1)}, u32[]{:S(2)}, u32[]{:S(2)}) collective-permute-start(bf16[2,192,256]{2,1,0:T(8,128)(2,1)S(1)} %get-tuple-element.65), channel_id=1, source_target_pairs={{0,4},{1,2},{2,1},{3,7},{4,0},{5,6},{6,5},{7,3},{8,12},{9,10},{10,... | collective-permute-start | bytes 589832 | tf_op jit(solution)/shard_map/ppermute | solution.py:43
  27.2 6.5 %collective-permute-start.6 = (bf16[6,2,64,128]{3,2,1,0:T(8,128)(2,1)S(1)}, bf16[6,2,64,128]{3,2,1,0:T(8,128)(2,1)S(1)}, u32[]{:S(2)}, u32[]{:S(2)}) collective-permute-start(bf16[6,2,64,128]{3,2,1,0:T(8,128)(2,1)S(1)} %second_level_early.1), channel_id=1, source_target_pairs={{0,8},{8,0},{4,12},{12,4},{16,24},{24,16},{20,28},{28,20},{1,9},{9... | collective-permute-start | bytes 589832 | tf_op jit(solution)/shard_map/ppermute | solution.py:54
  33.7 10.9 %collective-permute-start.7 = (bf16[10,2,64,128]{3,2,1,0:T(8,128)(2,1)S(1)}, bf16[10,2,64,128]{3,2,1,0:T(8,128)(2,1)S(1)}, u32[]{:S(2)}, u32[]{:S(2)}) collective-permute-start(bf16[10,2,64,128]{3,2,1,0:T(8,128)(2,1)S(1)} %get-tuple-element.48), channel_id=1, source_target_pairs={{0,8},{8,0},{4,12},{12,4},{16,24},{24,16},{20,28},{28,20},{1,9},{9... | collective-permute-start | bytes 983048 | tf_op jit(solution)/shard_map/ppermute | solution.py:54
  35.8 11.0 %collective-permute-start.10 = (bf16[4,2,64,128]{3,2,1,0:T(8,128)(2,1)S(1)}, bf16[4,2,64,128]{3,2,1,0:T(8,128)(2,1)S(1)}, u32[]{:S(2)}, u32[]{:S(2)}) collective-permute-start(bf16[4,2,64,128]{3,2,1,0:T(8,128)(2,1)S(1)} %get-tuple-element.57), channel_id=1, source_target_pairs={{0,2},{1,3},{2,0},{3,1},{4,6},{5,7},{6,4},{7,5},{8,10},{9,11},{10,... | collective-permute-start | bytes 393224 | tf_op jit(solution)/shard_map/ppermute | solution.py:420
  38.5 6.2 %collective-permute-start.8 = (bf16[2,2,64,128]{3,2,1,0:T(8,128)(2,1)S(1)}, bf16[2,2,64,128]{3,2,1,0:T(8,128)(2,1)S(1)}, u32[]{:S(2)}, u32[]{:S(2)}) collective-permute-start(bf16[2,2,64,128]{3,2,1,0:T(8,128)(2,1)S(1)} %get-tuple-element.53), channel_id=1, source_target_pairs={{0,3},{1,2},{2,1},{3,0},{4,7},{5,6},{6,5},{7,4},{8,11},{9,10},{10,... | collective-permute-start | bytes 196616 | tf_op jit(solution)/shard_map/ppermute | solution.py:420
  45.3 15.8 %collective-permute-start.9 = (bf16[6,2,64,128]{3,2,1,0:T(8,128)(2,1)S(1)}, bf16[6,2,64,128]{3,2,1,0:T(8,128)(2,1)S(1)}, u32[]{:S(2)}, u32[]{:S(2)}) collective-permute-start(bf16[6,2,64,128]{3,2,1,0:T(8,128)(2,1)S(1)} %late_wires.2), channel_id=1, source_target_pairs={{0,3},{1,2},{2,1},{3,0},{4,7},{5,6},{6,5},{7,4},{8,11},{9,10},{10,... | collective-permute-start | bytes 589832 | tf_op jit(solution)/shard_map/ppermute | solution.py:420
  47.6 13.5 %collective-permute-start.11 = (bf16[4,2,64,128]{3,2,1,0:T(8,128)(2,1)S(1)}, bf16[4,2,64,128]{3,2,1,0:T(8,128)(2,1)S(1)}, u32[]{:S(2)}, u32[]{:S(2)}) collective-permute-start(bf16[4,2,64,128]{3,2,1,0:T(8,128)(2,1)S(1)} %get-tuple-element.60), channel_id=1, source_target_pairs={{0,2},{1,3},{2,0},{3,1},{4,6},{5,7},{6,4},{7,5},{8,10},{9,11},{10,... | collective-permute-start | bytes 393224 | tf_op jit(solution)/shard_map/ppermute | solution.py:420
  51.1 10.0 %collective-permute-start.12 = (bf16[3,2,64,128]{3,2,1,0:T(8,128)(2,1)S(1)}, bf16[3,2,64,128]{3,2,1,0:T(8,128)(2,1)S(1)}, u32[]{:S(2)}, u32[]{:S(2)}) collective-permute-start(bf16[3,2,64,128]{3,2,1,0:T(8,128)(2,1)S(1)} %get-tuple-element.61), channel_id=1, source_target_pairs={{0,1},{1,0},{2,3},{3,2},{4,5},{5,4},{6,7},{7,6},{8,9},{9,8},{10,11... | collective-permute-start | bytes 294920 | tf_op jit(solution)/shard_map/ppermute | solution.py:420
  51.7 9.4 %collective-permute-start.13 = (bf16[3,2,64,128]{3,2,1,0:T(8,128)(2,1)S(1)}, bf16[3,2,64,128]{3,2,1,0:T(8,128)(2,1)S(1)}, u32[]{:S(2)}, u32[]{:S(2)}) collective-permute-start(bf16[3,2,64,128]{3,2,1,0:T(8,128)(2,1)S(1)} %get-tuple-element.62), channel_id=1, source_target_pairs={{0,1},{1,0},{2,3},{3,2},{4,5},{5,4},{6,7},{7,6},{8,9},{9,8},{10,11... | collective-permute-start | bytes 294920 | tf_op jit(solution)/shard_map/ppermute | solution.py:420
  53.1 8.0 %collective-permute-start.14 = (bf16[2,2,64,128]{3,2,1,0:T(8,128)(2,1)S(1)}, bf16[2,2,64,128]{3,2,1,0:T(8,128)(2,1)S(1)}, u32[]{:S(2)}, u32[]{:S(2)}) collective-permute-start(bf16[2,2,64,128]{3,2,1,0:T(8,128)(2,1)S(1)} %get-tuple-element.63), channel_id=1, source_target_pairs={{0,1},{1,0},{2,3},{3,2},{4,5},{5,4},{6,7},{7,6},{8,9},{9,8},{10,11... | collective-permute-start | bytes 196616 | tf_op jit(solution)/shard_map/ppermute | solution.py:420

commit v19 on v14

--- a/solution.py
+++ b/solution.py
@@ -452,8 +452,8 @@
     early_spans += [(distance, 0, longer) for distance in others]
     late_spans = [(distance, shorter, capacity) for distance in odd]
     for distance in range(1, beam_count // 2):
-        cut = (5 * capacity + 4) // 8
-        late_spans += [(distance, 0, cut), (distance, cut, capacity)]
+        cuts = sorted({cut * capacity // 8 for cut in (0, 3, 6, 8)})
+        late_spans += [(distance, low, high) for low, high in zip(cuts, cuts[1:])]
     late_spans.append((0, 0, capacity))
     last_spans = [(distance, longer, capacity) for distance in others]
 

time: 61.9 us -> 63.6 us (1.027)
  waiting for transfers between devices: 25.5 us -> 26.9 us
    ppermute x6 -> x7, waiting for transfers between devices: 13.9 us -> 15.2 us  [spread(): received.append(lax.ppermute(wire, 'beam', route) if distance else wire)]
    ppermute x6 -> x7, starting transfers between devices: 9.42 us -> 9.79 us  [spread(): received.append(lax.ppermute(wire, 'beam', route) if distance else wire)]
  transfers between devices with their start and end apart: 14 -> 15, of which waited for: 10 -> 9; matrix products, arithmetic and copies ran while one was open for 5% -> 5% of each run, Pallas kernels for 11% -> 11%
where the time goes in v19:
time: 63.6 us; the launch traced here: 63.4 us
  waiting for transfers between devices  26.9 us (42%)
  starting transfers between devices  20.4 us (32%)
  Pallas kernels  12.6 us (20%)
  local copies, waits for them, and re-layouts  2.24 us (4%)
  other arithmetic  1.1 us (2%)
    ppermute x7, waiting for transfers between devices, spread(): received.append(lax.ppermute(wire, 'beam', route) if distance else wire)  15.2 us
    ppermute x7, starting transfers between devices, spread(): received.append(lax.ppermute(wire, 'beam', route) if distance else wire)  9.79 us
    ppermute x4, waiting for transfers between devices, trade_edges(): received.append(lax.ppermute(block, ('aperture', 'beam'), route))  6.63 us
    ppermute x4, starting transfers between devices, trade_edges(): received.append(lax.ppermute(block, ('aperture', 'beam'), route))  6.01 us
    ppermute x4, waiting for transfers between devices, partner(): return lax.ppermute(block, axis, route)  5.03 us
    ppermute x4, starting transfers between devices, partner(): return lax.ppermute(block, axis, route)  4.6 us
    pallas_call x2, Pallas kernels, first_level(): pl.pallas_call(functools.partial(first_level_kernel, column, rows), out_s...  2.68 us
    pallas_call x1, Pallas kernels, resample(): pl.pallas_call(resample_kernel, out_shape=(shape, shape), in_specs=[ANY,...  2.31 us
  transfers between devices with their start and end apart: 15, of which 9 were waited for; matrix products, arithmetic and copies ran while one was open for 5% of the time, Pallas kernels for 11%

profile of v19, /device:TPU:0, one launch (start us, length us, event | category | flops | bytes accessed | tf_op | source)
XLA Modules:
  0.0 63.4 jit_solution(12848521577661833268)
XLA Ops:
  0.0 0.0 copy-start
  0.0 0.0 copy-start.2
  0.0 0.0 copy-start.1
  0.0 2.3 %resample.1 = (bf16[2,192,512]{2,1,0:T(8,128)(2,1)S(1)}, bf16[2,192,512]{2,1,0:T(8,128)(2,1)S(1)}) custom-call(bf16[2,256,512]{2,1,0:T(8,128)(2,1)} %bitcast.20, bf16[2,512,512]{2,1,0:T(8,128)(2,1)} %bitcast.19), custom_call_target="tpu_custom_call" | custom-call | flops 536870912 | bytes 2097152 | tf_op jit(solution)/shard_map/resample/pallas_call | solution.py:101
  2.3 3.1 %collective-permute-start = (bf16[2,192,512]{2,1,0:T(8,128)(2,1)S(1)}, bf16[2,192,512]{2,1,0:T(8,128)(2,1)S(1)}, u32[]{:S(2)}, u32[]{:S(2)}) collective-permute-start(bf16[2,192,512]{2,1,0:T(8,128)(2,1)S(1)} %get-tuple-element.35.sent_first_ref), channel_id=1, source_target_pairs={{0,1},{1,0},{2,3},{3,2},{4,5},{5,4},{6,7},{7,6},{8,9},{9,8},{10,11... | collective-permute-start | bytes 1179656 | tf_op jit(solution)/shard_map/ppermute | solution.py:43
  5.4 0.0 collective-permute-start.1
  5.4 0.0 copy-done
  5.4 1.5 %collective-permute-start.2 = (s32[1,16,1]{1,2,0:T(1,128)S(1)}, s32[1,16,1]{1,2,0:T(1,128)S(1)}, u32[]{:S(2)}, u32[]{:S(2)}) collective-permute-start(s32[1,16,1]{1,2,0:T(1,128)S(1)} %copy-done), channel_id=1, source_target_pairs={{0,8},{8,0},{4,12},{12,4},{16,24},{24,16},{20,28},{28,20},{1,9},{9... | collective-permute-start | bytes 200 | tf_op jit(solution)/shard_map/ppermute | solution.py:54
  6.9 0.0 copy-done.2
  6.9 0.2 subtract_reduce_fusion.starts_ref
  7.1 0.1 pad_add_fusion.side_ref
  7.2 0.0 copy-done.1
  7.2 0.4 copy.8
  7.6 1.4 %collective-permute-done.2 = s32[1,16,1]{1,2,0:T(1,128)S(1)} collective-permute-done((s32[1,16,1]{1,2,0:T(1,128)S(1)}, s32[1,16,1]{1,2,0:T(1,128)S(1)}, u32[]{:S(2)}, u32[]{:S(2)}) %collective-permute-start.2) | collective-permute-done | bytes 96 | tf_op jit(solution)/shard_map/ppermute | solution.py:54
  9.0 1.6 %plan.1 = (s32[16]{0:T(128)S(1)}, s32[16]{0:T(128)S(1)}, s32[16]{0:T(128)S(1)}, s32[16]{0:T(128)S(1)}, s32[16]{0:T(128)S(1)}) custom-call(s32[1]{0:T(128)} %bitcast.me_ref, s32[16]{0:T(128)S(1)} %bitcast.17, s32[16]{0:T(128)S(1)} %bitcast.18), custom_call_target="tpu_custom_call" | custom-call | tf_op jit(solution)/shard_map/plan/pallas_call | solution.py:311
  10.6 4.0 %collective-permute-done.first_ref = bf16[2,192,512]{2,1,0:T(8,128)(2,1)S(1)} collective-permute-done((bf16[2,192,512]{2,1,0:T(8,128)(2,1)S(1)}, bf16[2,192,512]{2,1,0:T(8,128)(2,1)S(1)}, u32[]{:S(2)}, u32[]{:S(2)}) %collective-permute-start) | collective-permute-done | bytes 393248 | tf_op jit(solution)/shard_map/ppermute | solution.py:43
  14.5 0.0 collective-permute-done.1.second_ref
  14.5 1.3 %first_level.3 = bf16[2,512,256]{2,1,0:T(8,128)(2,1)S(1)} custom-call(s32[4]{0:T(128)S(1)} %subtract_reduce_fusion.starts_ref, s32[3]{0:T(128)S(1)} %pad_add_fusion.side_ref, bf16[2,192,512]{2,1,0:T(8,128)(2,1)S(1)} %get-tuple-element.35.sent_first_ref, bf16[2,192,512]{2,1,0:T(8,128)(2,1)S(1)} %get-tuple-element.36.sent_second_ref, ...), custom_call_target="tpu_custom_call" | custom-call | flops 335544320 | bytes 2097152 | tf_op jit(solution)/shard_map/first_level/pallas_call | solution.py:177
  15.9 0.1 collective-permute-start.3
  16.0 1.3 %first_level.2 = bf16[2,512,256]{2,1,0:T(8,128)(2,1)S(1)} custom-call(s32[4]{0:T(128)S(1)} %subtract_reduce_fusion.starts_ref, s32[3]{0:T(128)S(1)} %pad_add_fusion.side_ref, bf16[2,192,512]{2,1,0:T(8,128)(2,1)S(1)} %get-tuple-element.35.sent_first_ref, bf16[2,192,512]{2,1,0:T(8,128)(2,1)S(1)} %get-tuple-element.36.sent_second_ref, ...), custom_call_target="tpu_custom_call" | custom-call | flops 335544320 | bytes 2097152 | tf_op jit(solution)/shard_map/first_level/pallas_call | solution.py:177
  17.3 0.5 collective-permute-done.3
  17.9 0.1 add_convert_fusion.own_ref
  18.0 2.9 %collective-permute-start.4 = (bf16[2,192,256]{2,1,0:T(8,128)(2,1)S(1)}, bf16[2,192,256]{2,1,0:T(8,128)(2,1)S(1)}, u32[]{:S(2)}, u32[]{:S(2)}) collective-permute-start(bf16[2,192,256]{2,1,0:T(8,128)(2,1)S(1)} %get-tuple-element.66), channel_id=1, source_target_pairs={{0,1},{1,0},{2,3},{3,2},{4,5},{5,4},{6,7},{7,6},{8,9},{9,8},{10,11... | collective-permute-start | bytes 589832 | tf_op jit(solution)/shard_map/ppermute | solution.py:43
  21.0 0.0 collective-permute-start.5
  21.0 1.8 %copy.9 = bf16[1,8,2,128,320]{4,3,2,1,0:T(8,128)(2,1)S(1)} copy(bf16[1,8,2,128,320]{3,4,2,1,0:T(8,128)(2,1)} %param.11) | data formatting | bytes 2621440 | tf_op args[4]
  22.8 0.7 %fusion.1.starts_ref = s32[8]{0:T(128)S(1)} fusion(s32[8,8]{1,0:T(8,128)} %param.12, s32[]{:T(128)S(6)} %select_n.19, s32[]{:T(128)S(6)} %sub.25), kind=kLoop, calls=%fused_computation.6 | loop fusion | flops 8 | bytes 72 | tf_op jit(solution)/shard_map/sub | solution.py:479
  23.5 2.7 %collective-permute-done.4.first_ref = bf16[2,192,256]{2,1,0:T(8,128)(2,1)S(1)} collective-permute-done((bf16[2,192,256]{2,1,0:T(8,128)(2,1)S(1)}, bf16[2,192,256]{2,1,0:T(8,128)(2,1)S(1)}, u32[]{:S(2)}, u32[]{:S(2)}) %collective-permute-start.4) | collective-permute-done | bytes 196640 | tf_op jit(solution)/shard_map/ppermute | solution.py:43
  26.2 0.0 collective-permute-done.5.second_ref
  26.2 1.0 %second_level_early.1 = bf16[6,2,64,128]{3,2,1,0:T(8,128)(2,1)S(1)} custom-call(s32[8]{0:T(128)S(1)} %fusion.1.starts_ref, s32[3]{0:T(128)S(1)} %pad_add_fusion.side_ref, s32[16]{0:T(128)S(1)} %get-tuple-element.42.sector_ref, bf16[2,512,256]{2,1,0:T(8,128)(2,1)S(1)} %add_convert_fusion.own_ref, bf16[2,192,256]{2,1,0:T(8,128)(2,1)S(1)} %collective-permute-done.4.first_ref, ...), custom_call_target="tpu_custom_call" | custom-call | flops 125829120 | bytes 1048576 | tf_op jit(solution)/shard_map/second_level_early/pallas_call | solution.py:244
  27.2 1.6 %collective-permute-start.6 = (bf16[6,2,64,128]{3,2,1,0:T(8,128)(2,1)S(1)}, bf16[6,2,64,128]{3,2,1,0:T(8,128)(2,1)S(1)}, u32[]{:S(2)}, u32[]{:S(2)}) collective-permute-start(bf16[6,2,64,128]{3,2,1,0:T(8,128)(2,1)S(1)} %second_level_early.1), channel_id=1, source_target_pairs={{0,8},{8,0},{4,12},{12,4},{16,24},{24,16},{20,28},{28,20},{1,9},{9... | collective-permute-start | bytes 589832 | tf_op jit(solution)/shard_map/ppermute | solution.py:54
  28.8 1.9 %second_level.1 = (bf16[16,2,64,128]{3,2,1,0:T(8,128)(2,1)S(1)}, bf16[10,2,64,128]{3,2,1,0:T(8,128)(2,1)S(1)}) custom-call(s32[8]{0:T(128)S(1)} %fusion.1.starts_ref, s32[3]{0:T(128)S(1)} %pad_add_fusion.side_ref, s32[16]{0:T(128)S(1)} %get-tuple-element.45.own_at_ref, s32[16]{0:T(128)S(1)} %get-tuple-element.46.other_at_ref, ...), custom_call_target="tpu_custom_call" | custom-call | flops 671088640 | bytes 4194304 | tf_op jit(solution)/shard_map/second_level/pallas_call | solution.py:255
  30.7 3.0 %collective-permute-done.6.refs_0_ = bf16[6,2,64,128]{3,2,1,0:T(8,128)(2,1)S(1)} collective-permute-done((bf16[6,2,64,128]{3,2,1,0:T(8,128)(2,1)S(1)}, bf16[6,2,64,128]{3,2,1,0:T(8,128)(2,1)S(1)}, u32[]{:S(2)}, u32[]{:S(2)}) %collective-permute-start.6) | collective-permute-done | bytes 196640 | tf_op jit(solution)/shard_map/ppermute | solution.py:54
  33.7 1.5 %collective-permute-start.7 = (bf16[10,2,64,128]{3,2,1,0:T(8,128)(2,1)S(1)}, bf16[10,2,64,128]{3,2,1,0:T(8,128)(2,1)S(1)}, u32[]{:S(2)}, u32[]{:S(2)}) collective-permute-start(bf16[10,2,64,128]{3,2,1,0:T(8,128)(2,1)S(1)} %get-tuple-element.48), channel_id=1, source_target_pairs={{0,8},{8,0},{4,12},{12,4},{16,24},{24,16},{20,28},{28,20},{1,9},{9... | collective-permute-start | bytes 983048 | tf_op jit(solution)/shard_map/ppermute | solution.py:54
  35.2 0.6 early_wires.1
  35.8 2.4 %collective-permute-start.8 = (bf16[2,2,64,128]{3,2,1,0:T(8,128)(2,1)S(1)}, bf16[2,2,64,128]{3,2,1,0:T(8,128)(2,1)S(1)}, u32[]{:S(2)}, u32[]{:S(2)}) collective-permute-start(bf16[2,2,64,128]{3,2,1,0:T(8,128)(2,1)S(1)} %get-tuple-element.53), channel_id=1, source_target_pairs={{0,3},{1,2},{2,1},{3,0},{4,7},{5,6},{6,5},{7,4},{8,11},{9,10},{10,... | collective-permute-start | bytes 196616 | tf_op jit(solution)/shard_map/ppermute | solution.py:420
  38.2 0.6 collective-permute-start.13
  38.8 3.1 %collective-permute-done.8.refs_0_ = bf16[2,2,64,128]{3,2,1,0:T(8,128)(2,1)S(1)} collective-permute-done((bf16[2,2,64,128]{3,2,1,0:T(8,128)(2,1)S(1)}, bf16[2,2,64,128]{3,2,1,0:T(8,128)(2,1)S(1)}, u32[]{:S(2)}, u32[]{:S(2)}) %collective-permute-start.8) | collective-permute-done | bytes 65568 | tf_op jit(solution)/shard_map/ppermute | solution.py:420
  41.9 0.1 collective-permute-done.7.refs_0_
  42.0 0.8 %late_wires.2 = (bf16[6,2,64,128]{3,2,1,0:T(8,128)(2,1)S(1)}, bf16[3,2,64,128]{3,2,1,0:T(8,128)(2,1)S(1)}, bf16[3,2,64,128]{3,2,1,0:T(8,128)(2,1)S(1)}, bf16[2,2...) custom-call(s32[1]{0:T(128)} %bitcast.me_ref, s32[16]{0:T(128)S(1)} %get-tuple-element.49.target_ref, ...), custom_call_target="tpu_custom_call" | custom-call | bytes 2097152 | tf_op jit(solution)/shard_map/late_wires/pallas_call | solution.py:372
  42.8 2.4 %collective-permute-start.9 = (bf16[6,2,64,128]{3,2,1,0:T(8,128)(2,1)S(1)}, bf16[6,2,64,128]{3,2,1,0:T(8,128)(2,1)S(1)}, u32[]{:S(2)}, u32[]{:S(2)}) collective-permute-start(bf16[6,2,64,128]{3,2,1,0:T(8,128)(2,1)S(1)} %get-tuple-element.57), channel_id=1, source_target_pairs={{0,3},{1,2},{2,1},{3,0},{4,7},{5,6},{6,5},{7,4},{8,11},{9,10},{10,... | collective-permute-start | bytes 589832 | tf_op jit(solution)/shard_map/ppermute | solution.py:420
  45.3 7.9 %collective-permute-done.13.refs_6_ = bf16[4,2,64,128]{3,2,1,0:T(8,128)(2,1)S(1)} collective-permute-done((bf16[4,2,64,128]{3,2,1,0:T(8,128)(2,1)S(1)}, bf16[4,2,64,128]{3,2,1,0:T(8,128)(2,1)S(1)}, u32[]{:S(2)}, u32[]{:S(2)}) %collective-permute-start.13) | collective-permute-done | bytes 131104 | tf_op jit(solution)/shard_map/ppermute | solution.py:420
  53.2 0.6 %late_wires.3 = bf16[4,2,64,128]{3,2,1,0:T(8,128)(2,1)S(1)} custom-call(s32[1]{0:T(128)} %bitcast.me_ref, s32[16]{0:T(128)S(1)} %get-tuple-element.49.target_ref, s32[16]{0:T(128)S(1)} %get-tuple-element.50.rank_ref, bf16[16,2,64,128]{3,2,1,0:T(8,128)(2,1)S(1)} %get-tuple-element.51.keep_ref, bf16[10,2,64,128]{3,2,1,0:T(8,128)(2,1)S(1)} %collective-permute-done.7.refs_0_, ...), custom_call_target="tpu_custom_call" | custom-call | bytes 2097152 | tf_op jit(solution)/shard_map/late_wires/pallas_call | solution.py:372
  53.8 0.1 collective-permute-start.14
  53.9 2.3 %collective-permute-start.10 = (bf16[3,2,64,128]{3,2,1,0:T(8,128)(2,1)S(1)}, bf16[3,2,64,128]{3,2,1,0:T(8,128)(2,1)S(1)}, u32[]{:S(2)}, u32[]{:S(2)}) collective-permute-start(bf16[3,2,64,128]{3,2,1,0:T(8,128)(2,1)S(1)} %get-tuple-element.58), channel_id=1, source_target_pairs={{0,1},{1,0},{2,3},{3,2},{4,5},{5,4},{6,7},{7,6},{8,9},{9,8},{10,11... | collective-permute-start | bytes 294920 | tf_op jit(solution)/shard_map/ppermute | solution.py:420
  56.2 0.0 collective-permute-start.11
  56.2 2.0 %collective-permute-start.12 = (bf16[2,2,64,128]{3,2,1,0:T(8,128)(2,1)S(1)}, bf16[2,2,64,128]{3,2,1,0:T(8,128)(2,1)S(1)}, u32[]{:S(2)}, u32[]{:S(2)}) collective-permute-start(bf16[2,2,64,128]{3,2,1,0:T(8,128)(2,1)S(1)} %get-tuple-element.60), channel_id=1, source_target_pairs={{0,1},{1,0},{2,3},{3,2},{4,5},{5,4},{6,7},{7,6},{8,9},{9,8},{10,11... | collective-permute-start | bytes 196616 | tf_op jit(solution)/shard_map/ppermute | solution.py:420
  58.2 4.2 %collective-permute-done.12.refs_4_ = bf16[2,2,64,128]{3,2,1,0:T(8,128)(2,1)S(1)} collective-permute-done((bf16[2,2,64,128]{3,2,1,0:T(8,128)(2,1)S(1)}, bf16[2,2,64,128]{3,2,1,0:T(8,128)(2,1)S(1)}, u32[]{:S(2)}, u32[]{:S(2)}) %collective-permute-start.12) | collective-permute-done | bytes 65568 | tf_op jit(solution)/shard_map/ppermute | solution.py:420
  62.4 0.0 collective-permute-done.10.refs_2_
  62.4 0.0 collective-permute-done.11.refs_3_
  62.4 0.0 collective-permute-done.14.refs_7_
  62.4 0.0 collective-permute-done.9.refs_1_
  62.4 1.0 %collect.1 = bf16[32,2,64,128]{3,2,1,0:T(8,128)(2,1)} custom-call(s32[1]{0:T(128)} %bitcast.me_ref, bf16[2,2,64,128]{3,2,1,0:T(8,128)(2,1)S(1)} %collective-permute-done.8.refs_0_, bf16[6,2,64,128]{3,2,1,0:T(8,128)(2,1)S(1)} %collective-permute-done.9.refs_1_, bf16[3,2,64,128]{3,2,1,0:T(8,128)(2,1)S(1)} %collective-permute-done.10.refs_2_, ...), custom_call_target="tpu_custom_call" | custom-call | bytes 2097152 | tf_op jit(solution)/shard_map/collect/pallas_call | solution.py:403
  (1 shorter events, 0.0 us)
Async XLA Ops:
  0.0 5.4 %copy-start = (s32[1,16,1]{1,2,0:T(1,128)S(1)}, s32[1,16,1]{1,2,0:T(1,128)}, u32[]{:S(2)}) copy-start(s32[1,16,1]{1,2,0:T(1,128)} %param.13) | copy-start | bytes 196
  0.0 6.9 %copy-start.2 = (s32[8,4]{0,1:T(4,128)S(1)}, s32[8,4]{0,1:T(4,128)}, u32[]{:S(2)}) copy-start(s32[8,4]{0,1:T(4,128)} %param.10) | copy-start | bytes 388
  0.0 7.2 %copy-start.1 = (bf16[1,4,2,128,320]{3,4,2,1,0:T(8,128)(2,1)S(1)}, bf16[1,4,2,128,320]{3,4,2,1,0:T(8,128)(2,1)}, u32[]{:S(2)}) copy-start(bf16[1,4,2,128,320]{3,4,2,1,0:T(8,128)(2,1)} %param.9) | copy-start | bytes 1966084
  2.3 12.2 %collective-permute-start = (bf16[2,192,512]{2,1,0:T(8,128)(2,1)S(1)}, bf16[2,192,512]{2,1,0:T(8,128)(2,1)S(1)}, u32[]{:S(2)}, u32[]{:S(2)}) collective-permute-start(bf16[2,192,512]{2,1,0:T(8,128)(2,1)S(1)} %get-tuple-element.35.sent_first_ref), channel_id=1, source_target_pairs={{0,1},{1,0},{2,3},{3,2},{4,5},{5,4},{6,7},{7,6},{8,9},{9,8},{10,11... | collective-permute-start | bytes 1179656 | tf_op jit(solution)/shard_map/ppermute | solution.py:43
  5.4 9.1 %collective-permute-start.1 = (bf16[2,192,512]{2,1,0:T(8,128)(2,1)S(1)}, bf16[2,192,512]{2,1,0:T(8,128)(2,1)S(1)}, u32[]{:S(2)}, u32[]{:S(2)}) collective-permute-start(bf16[2,192,512]{2,1,0:T(8,128)(2,1)S(1)} %get-tuple-element.36.sent_second_ref), channel_id=1, source_target_pairs={{0,4},{1,2},{2,1},{3,7},{4,0},{5,6},{6,5},{7,3},{8,12},{9,10},{10,... | collective-permute-start | bytes 1179656 | tf_op jit(solution)/shard_map/ppermute | solution.py:43
  5.4 3.5 %collective-permute-start.2 = (s32[1,16,1]{1,2,0:T(1,128)S(1)}, s32[1,16,1]{1,2,0:T(1,128)S(1)}, u32[]{:S(2)}, u32[]{:S(2)}) collective-permute-start(s32[1,16,1]{1,2,0:T(1,128)S(1)} %copy-done), channel_id=1, source_target_pairs={{0,8},{8,0},{4,12},{12,4},{16,24},{24,16},{20,28},{28,20},{1,9},{9... | collective-permute-start | bytes 200 | tf_op jit(solution)/shard_map/ppermute | solution.py:54
  15.9 2.0 %collective-permute-start.3 = (bf16[2,512,256]{2,1,0:T(8,128)(2,1)S(1)}, bf16[2,512,256]{2,1,0:T(8,128)(2,1)S(1)}, u32[]{:S(2)}, u32[]{:S(2)}) collective-permute-start(bf16[2,512,256]{2,1,0:T(8,128)(2,1)S(1)} %first_level.3), channel_id=1, source_target_pairs={{0,4},{4,0},{8,12},{12,8},{16,20},{20,16},{24,28},{28,24},{1,5},{5... | collective-permute-start | bytes 1572872 | tf_op jit(solution)/shard_map/ppermute | solution.py:54
  18.0 8.1 %collective-permute-start.4 = (bf16[2,192,256]{2,1,0:T(8,128)(2,1)S(1)}, bf16[2,192,256]{2,1,0:T(8,128)(2,1)S(1)}, u32[]{:S(2)}, u32[]{:S(2)}) collective-permute-start(bf16[2,192,256]{2,1,0:T(8,128)(2,1)S(1)} %get-tuple-element.66), channel_id=1, source_target_pairs={{0,1},{1,0},{2,3},{3,2},{4,5},{5,4},{6,7},{7,6},{8,9},{9,8},{10,11... | collective-permute-start | bytes 589832 | tf_op jit(solution)/shard_map/ppermute | solution.py:43
  21.0 5.2 %collective-permute-start.5 = (bf16[2,192,256]{2,1,0:T(8,128)(2,1)S(1)}, bf16[2,192,256]{2,1,0:T(8,128)(2,1)S(1)}, u32[]{:S(2)}, u32[]{:S(2)}) collective-permute-start(bf16[2,192,256]{2,1,0:T(8,128)(2,1)S(1)} %get-tuple-element.65), channel_id=1, source_target_pairs={{0,4},{1,2},{2,1},{3,7},{4,0},{5,6},{6,5},{7,3},{8,12},{9,10},{10,... | collective-permute-start | bytes 589832 | tf_op jit(solution)/shard_map/ppermute | solution.py:43
  27.2 6.5 %collective-permute-start.6 = (bf16[6,2,64,128]{3,2,1,0:T(8,128)(2,1)S(1)}, bf16[6,2,64,128]{3,2,1,0:T(8,128)(2,1)S(1)}, u32[]{:S(2)}, u32[]{:S(2)}) collective-permute-start(bf16[6,2,64,128]{3,2,1,0:T(8,128)(2,1)S(1)} %second_level_early.1), channel_id=1, source_target_pairs={{0,8},{8,0},{4,12},{12,4},{16,24},{24,16},{20,28},{28,20},{1,9},{9... | collective-permute-start | bytes 589832 | tf_op jit(solution)/shard_map/ppermute | solution.py:54
  33.7 8.3 %collective-permute-start.7 = (bf16[10,2,64,128]{3,2,1,0:T(8,128)(2,1)S(1)}, bf16[10,2,64,128]{3,2,1,0:T(8,128)(2,1)S(1)}, u32[]{:S(2)}, u32[]{:S(2)}) collective-permute-start(bf16[10,2,64,128]{3,2,1,0:T(8,128)(2,1)S(1)} %get-tuple-element.48), channel_id=1, source_target_pairs={{0,8},{8,0},{4,12},{12,4},{16,24},{24,16},{20,28},{28,20},{1,9},{9... | collective-permute-start | bytes 983048 | tf_op jit(solution)/shard_map/ppermute | solution.py:54
  35.8 6.1 %collective-permute-start.8 = (bf16[2,2,64,128]{3,2,1,0:T(8,128)(2,1)S(1)}, bf16[2,2,64,128]{3,2,1,0:T(8,128)(2,1)S(1)}, u32[]{:S(2)}, u32[]{:S(2)}) collective-permute-start(bf16[2,2,64,128]{3,2,1,0:T(8,128)(2,1)S(1)} %get-tuple-element.53), channel_id=1, source_target_pairs={{0,3},{1,2},{2,1},{3,0},{4,7},{5,6},{6,5},{7,4},{8,11},{9,10},{10,... | collective-permute-start | bytes 196616 | tf_op jit(solution)/shard_map/ppermute | solution.py:420
  38.2 14.9 %collective-permute-start.13 = (bf16[4,2,64,128]{3,2,1,0:T(8,128)(2,1)S(1)}, bf16[4,2,64,128]{3,2,1,0:T(8,128)(2,1)S(1)}, u32[]{:S(2)}, u32[]{:S(2)}) collective-permute-start(bf16[4,2,64,128]{3,2,1,0:T(8,128)(2,1)S(1)} %get-tuple-element.62), channel_id=1, source_target_pairs={{0,2},{1,3},{2,0},{3,1},{4,6},{5,7},{6,4},{7,5},{8,10},{9,11},{10,... | collective-permute-start | bytes 393224 | tf_op jit(solution)/shard_map/ppermute | solution.py:420
  42.8 19.6 %collective-permute-start.9 = (bf16[6,2,64,128]{3,2,1,0:T(8,128)(2,1)S(1)}, bf16[6,2,64,128]{3,2,1,0:T(8,128)(2,1)S(1)}, u32[]{:S(2)}, u32[]{:S(2)}) collective-permute-start(bf16[6,2,64,128]{3,2,1,0:T(8,128)(2,1)S(1)} %get-tuple-element.57), channel_id=1, source_target_pairs={{0,3},{1,2},{2,1},{3,0},{4,7},{5,6},{6,5},{7,4},{8,11},{9,10},{10,... | collective-permute-start | bytes 589832 | tf_op jit(solution)/shard_map/ppermute | solution.py:420
  53.8 8.6 %collective-permute-start.14 = (bf16[4,2,64,128]{3,2,1,0:T(8,128)(2,1)S(1)}, bf16[4,2,64,128]{3,2,1,0:T(8,128)(2,1)S(1)}, u32[]{:S(2)}, u32[]{:S(2)}) collective-permute-start(bf16[4,2,64,128]{3,2,1,0:T(8,128)(2,1)S(1)} %late_wires.3), channel_id=1, source_target_pairs={{0,2},{1,3},{2,0},{3,1},{4,6},{5,7},{6,4},{7,5},{8,10},{9,11},{10,... | collective-permute-start | bytes 393224 | tf_op jit(solution)/shard_map/ppermute | solution.py:420
  53.9 8.5 %collective-permute-start.10 = (bf16[3,2,64,128]{3,2,1,0:T(8,128)(2,1)S(1)}, bf16[3,2,64,128]{3,2,1,0:T(8,128)(2,1)S(1)}, u32[]{:S(2)}, u32[]{:S(2)}) collective-permute-start(bf16[3,2,64,128]{3,2,1,0:T(8,128)(2,1)S(1)} %get-tuple-element.58), channel_id=1, source_target_pairs={{0,1},{1,0},{2,3},{3,2},{4,5},{5,4},{6,7},{7,6},{8,9},{9,8},{10,11... | collective-permute-start | bytes 294920 | tf_op jit(solution)/shard_map/ppermute | solution.py:420
  56.2 6.2 %collective-permute-start.11 = (bf16[3,2,64,128]{3,2,1,0:T(8,128)(2,1)S(1)}, bf16[3,2,64,128]{3,2,1,0:T(8,128)(2,1)S(1)}, u32[]{:S(2)}, u32[]{:S(2)}) collective-permute-start(bf16[3,2,64,128]{3,2,1,0:T(8,128)(2,1)S(1)} %get-tuple-element.59), channel_id=1, source_target_pairs={{0,1},{1,0},{2,3},{3,2},{4,5},{5,4},{6,7},{7,6},{8,9},{9,8},{10,11... | collective-permute-start | bytes 294920 | tf_op jit(solution)/shard_map/ppermute | solution.py:420
  56.2 6.2 %collective-permute-start.12 = (bf16[2,2,64,128]{3,2,1,0:T(8,128)(2,1)S(1)}, bf16[2,2,64,128]{3,2,1,0:T(8,128)(2,1)S(1)}, u32[]{:S(2)}, u32[]{:S(2)}) collective-permute-start(bf16[2,2,64,128]{3,2,1,0:T(8,128)(2,1)S(1)} %get-tuple-element.60), channel_id=1, source_target_pairs={{0,1},{1,0},{2,3},{3,2},{4,5},{5,4},{6,7},{7,6},{8,9},{9,8},{10,11... | collective-permute-start | bytes 196616 | tf_op jit(solution)/shard_map/ppermute | solution.py:420

commit v20 on v14

--- a/solution.py
+++ b/solution.py
@@ -153,6 +153,7 @@
     weights_ref, out_ref, padded,
 ):
     sectors, stacked, window = weights_ref.shape
+    window //= 2
     beams = stacked // 2
     margin = first_ref.shape[1]
     columns = slice(column, column + out_ref.shape[2])
@@ -164,9 +165,13 @@
     place_halos(padded, side_ref, rows, first_ref, second_ref, columns)
     for sector in range(sectors):
         place = pl.ds(pl.multiple_of(starts_ref[sector] * BLK, BLK), window)
-        parts = complex_window(weights_ref[sector], padded[place, :])
+        width = out_ref.shape[2]
+        both = jnp.concatenate([padded[place, :width], padded[place, width:]])
+        parts = dot(weights_ref[sector], both).astype(jnp.bfloat16)
         for part in range(2):
-            out_ref[part, sector * beams : (sector + 1) * beams, :] = parts[part]
+            out_ref[part, sector * beams : (sector + 1) * beams, :] = parts[
+                part * beams : (part + 1) * beams
+            ]
 
 
 def first_level(column, rows, starts, side, sent, halos, weights):
@@ -181,7 +186,7 @@
         out_specs=VMEM,
         scratch_shapes=[pltpu.VMEM((rows + 2 * margin, 2 * width), jnp.bfloat16)],
         compiler_params=params(),
-        cost_estimate=cost(sectors * 2 * stacked * window * width, 2**21),
+        cost_estimate=cost(sectors * stacked * window * width, 2**21),
         name="first_level",
     )(starts, side, *sent, *halos, weights)
 
@@ -421,6 +426,13 @@
     return received
 
 
+def real_form(weights):
+    real, imag = weights[0, :, 0], weights[0, :, 1]
+    upper = jnp.concatenate([real, -imag], axis=-1)
+    lower = jnp.concatenate([imag, real], axis=-1)
+    return jnp.concatenate([upper, lower], axis=1)
+
+
 def stacked_weights(weights):
     return weights[0].reshape(weights.shape[1], -1, weights.shape[4])
 
@@ -458,6 +470,8 @@
     last_spans = [(distance, longer, capacity) for distance in others]
 
     sent = resample(subimages[0], range_kernel[0], margin)
+    sent, weights0 = lax.optimization_barrier((sent, weights0))
+    weights, owners = lax.optimization_barrier((real_form(weights0), owners))
     halos = trade_edges(*sent)
     own_owners = owners[0, :, 0]
     other_owners = partner(owners, "aperture", 1)[0, :, 0]
@@ -466,7 +480,6 @@
     halos, planned = lax.optimization_barrier((halos, planned))
     *planned, target, rank = planned
     width = range_kernel.shape[3] // 2
-    weights = stacked_weights(weights0)
     send = first_level(width, rows, begin0, side, sent, halos, weights)
     other = partner(send, "aperture", 0)
     keep = first_level(0, rows, begin0, side, sent, halos, weights)

time: 61.9 us -> 62.9 us (1.016)
  other arithmetic: 1.1 us -> 2.6 us
    ppermute x4, waiting for transfers between devices: 6.63 us -> 5.52 us  [trade_edges(): received.append(lax.ppermute(block, ('aperture', 'beam'), route))]
    convert_element_type x1, other arithmetic: 0.14 us -> 1.17 us  [local(): (keep.astype(jnp.float32) + other.astype(jnp.float32)).astype(jnp.bfloat16)]
    ppermute x4, waiting for transfers between devices: 5.03 us -> 5.68 us  [partner(): return lax.ppermute(block, axis, route)]
    unnamed x8 -> x7, local copies, waits for them, and re-layouts: 2.2 us -> 1.98 us
  transfers between devices with their start and end apart: 14 -> 14, of which waited for: 10 -> 10; matrix products, arithmetic and copies ran while one was open for 5% -> 6% of each run, Pallas kernels for 11% -> 11%
where the time goes in v20:
time: 62.9 us; the launch traced here: 62.7 us
  waiting for transfers between devices  25 us (40%)
  starting transfers between devices  20.1 us (32%)
  Pallas kernels  12.3 us (20%)
  other arithmetic  2.6 us (4%)
  local copies, waits for them, and re-layouts  2.46 us (4%)
    ppermute x6, waiting for transfers between devices, spread(): received.append(lax.ppermute(wire, 'beam', route) if distance else wire)  13.8 us
    ppermute x6, starting transfers between devices, spread(): received.append(lax.ppermute(wire, 'beam', route) if distance else wire)  9.44 us
    ppermute x4, starting transfers between devices, trade_edges(): received.append(lax.ppermute(block, ('aperture', 'beam'), route))  6.01 us
    ppermute x4, waiting for transfers between devices, partner(): return lax.ppermute(block, axis, route)  5.68 us
    ppermute x4, waiting for transfers between devices, trade_edges(): received.append(lax.ppermute(block, ('aperture', 'beam'), route))  5.52 us
    ppermute x4, starting transfers between devices, partner(): return lax.ppermute(block, axis, route)  4.61 us
    pallas_call x2, Pallas kernels, first_level(): pl.pallas_call(functools.partial(first_level_kernel, column, rows), out_s...  2.39 us
    pallas_call x1, Pallas kernels, resample(): pl.pallas_call(resample_kernel, out_shape=(shape, shape), in_specs=[ANY,...  2.31 us
  transfers between devices with their start and end apart: 14, of which 10 were waited for; matrix products, arithmetic and copies ran while one was open for 6% of the time, Pallas kernels for 11%

profile of v20, /device:TPU:0, one launch (start us, length us, event | category | flops | bytes accessed | tf_op | source)
XLA Modules:
  0.0 62.7 jit_solution(5266995368204162063)
XLA Ops:
  0.0 0.0 copy-start.1
  0.0 2.3 %resample.1 = (bf16[2,192,512]{2,1,0:T(8,128)(2,1)S(1)}, bf16[2,192,512]{2,1,0:T(8,128)(2,1)S(1)}) custom-call(bf16[2,256,512]{2,1,0:T(8,128)(2,1)} %bitcast.23, bf16[2,512,512]{2,1,0:T(8,128)(2,1)} %bitcast.22), custom_call_target="tpu_custom_call" | custom-call | flops 536870912 | bytes 2097152 | tf_op jit(solution)/shard_map/resample/pallas_call | solution.py:101
  2.3 3.1 %collective-permute-start = (bf16[2,192,512]{2,1,0:T(8,128)(2,1)S(1)}, bf16[2,192,512]{2,1,0:T(8,128)(2,1)S(1)}, u32[]{:S(2)}, u32[]{:S(2)}) collective-permute-start(bf16[2,192,512]{2,1,0:T(8,128)(2,1)S(1)} %get-tuple-element.41.sent_first_ref), channel_id=1, source_target_pairs={{0,1},{1,0},{2,3},{3,2},{4,5},{5,4},{6,7},{7,6},{8,9},{9,8},{10,11... | collective-permute-start | bytes 1179656 | tf_op jit(solution)/shard_map/ppermute | solution.py:43
  5.4 0.0 collective-permute-start.1
  5.4 0.0 copy-done.1
  5.4 0.4 copy.8
  5.8 0.1 slice_bitcast_fusion
  5.9 0.0 copy-start
  5.9 0.0 copy-start.2
  5.9 0.4 maximum_maximum_fusion.weights_ref
  6.4 0.1 copy-done
  6.5 1.5 %collective-permute-start.2 = (s32[1,16,1]{1,2,0:T(1,128)S(1)}, s32[1,16,1]{1,2,0:T(1,128)S(1)}, u32[]{:S(2)}, u32[]{:S(2)}) collective-permute-start(s32[1,16,1]{1,2,0:T(1,128)S(1)} %copy-done), channel_id=1, source_target_pairs={{0,8},{8,0},{4,12},{12,4},{16,24},{24,16},{20,28},{28,20},{1,9},{9... | collective-permute-start | bytes 200 | tf_op jit(solution)/shard_map/ppermute | solution.py:54
  8.0 0.1 pad_add_fusion.side_ref
  8.1 0.0 copy-done.2
  8.1 0.2 subtract_reduce_fusion.starts_ref
  8.3 1.8 %collective-permute-done.2 = s32[1,16,1]{1,2,0:T(1,128)S(1)} collective-permute-done((s32[1,16,1]{1,2,0:T(1,128)S(1)}, s32[1,16,1]{1,2,0:T(1,128)S(1)}, u32[]{:S(2)}, u32[]{:S(2)}) %collective-permute-start.2) | collective-permute-done | bytes 96 | tf_op jit(solution)/shard_map/ppermute | solution.py:54
  10.1 1.6 %plan.1 = (s32[16]{0:T(128)S(1)}, s32[16]{0:T(128)S(1)}, s32[16]{0:T(128)S(1)}, s32[16]{0:T(128)S(1)}, s32[16]{0:T(128)S(1)}) custom-call(s32[1]{0:T(128)} %bitcast.me_ref, s32[16]{0:T(128)S(1)} %bitcast.20, s32[16]{0:T(128)S(1)} %bitcast.21), custom_call_target="tpu_custom_call" | custom-call | tf_op jit(solution)/shard_map/plan/pallas_call | solution.py:316
  11.7 2.8 %collective-permute-done.first_ref = bf16[2,192,512]{2,1,0:T(8,128)(2,1)S(1)} collective-permute-done((bf16[2,192,512]{2,1,0:T(8,128)(2,1)S(1)}, bf16[2,192,512]{2,1,0:T(8,128)(2,1)S(1)}, u32[]{:S(2)}, u32[]{:S(2)}) %collective-permute-start) | collective-permute-done | bytes 393248 | tf_op jit(solution)/shard_map/ppermute | solution.py:43
  14.5 0.0 collective-permute-done.1.second_ref
  14.5 1.2 %first_level.3 = bf16[2,512,256]{2,1,0:T(8,128)(2,1)S(1)} custom-call(s32[4]{0:T(128)S(1)} %subtract_reduce_fusion.starts_ref, s32[3]{0:T(128)S(1)} %pad_add_fusion.side_ref, bf16[2,192,512]{2,1,0:T(8,128)(2,1)S(1)} %get-tuple-element.41.sent_first_ref, bf16[2,192,512]{2,1,0:T(8,128)(2,1)S(1)} %get-tuple-element.42.sent_second_ref, ...), custom_call_target="tpu_custom_call" | custom-call | flops 335544320 | bytes 2097152 | tf_op jit(solution)/shard_map/first_level/pallas_call | solution.py:182
  15.7 0.1 collective-permute-start.3
  15.8 1.2 %first_level.2 = bf16[2,512,256]{2,1,0:T(8,128)(2,1)S(1)} custom-call(s32[4]{0:T(128)S(1)} %subtract_reduce_fusion.starts_ref, s32[3]{0:T(128)S(1)} %pad_add_fusion.side_ref, bf16[2,192,512]{2,1,0:T(8,128)(2,1)S(1)} %get-tuple-element.41.sent_first_ref, bf16[2,192,512]{2,1,0:T(8,128)(2,1)S(1)} %get-tuple-element.42.sent_second_ref, ...), custom_call_target="tpu_custom_call" | custom-call | flops 335544320 | bytes 2097152 | tf_op jit(solution)/shard_map/first_level/pallas_call | solution.py:182
  17.0 0.8 %collective-permute-done.3 = bf16[2,512,256]{2,1,0:T(8,128)(2,1)} collective-permute-done((bf16[2,512,256]{2,1,0:T(8,128)(2,1)S(1)}, bf16[2,512,256]{2,1,0:T(8,128)(2,1)}, u32[]{:S(2)}, u32[]{:S(2)}) %collective-permute-start.3) | collective-permute-done | bytes 524320 | tf_op jit(solution)/shard_map/ppermute | solution.py:54
  17.8 1.2 %add_convert_fusion.own_ref = bf16[2,512,256]{2,1,0:T(8,128)(2,1)S(1)} fusion(bf16[2,512,256]{2,1,0:T(8,128)(2,1)} %collective-permute-done.3, bf16[2,512,256]{2,1,0:T(8,128)(2,1)S(1)} %first_level.2), kind=kLoop, calls=%fused_computation.1 | loop fusion | flops 1048576 | bytes 1572864 | tf_op jit(solution)/shard_map/convert_element_type | solution.py:486
  19.1 2.9 %collective-permute-start.4 = (bf16[2,192,256]{2,1,0:T(8,128)(2,1)S(1)}, bf16[2,192,256]{2,1,0:T(8,128)(2,1)S(1)}, u32[]{:S(2)}, u32[]{:S(2)}) collective-permute-start(bf16[2,192,256]{2,1,0:T(8,128)(2,1)S(1)} %get-tuple-element.76), channel_id=1, source_target_pairs={{0,1},{1,0},{2,3},{3,2},{4,5},{5,4},{6,7},{7,6},{8,9},{9,8},{10,11... | collective-permute-start | bytes 589832 | tf_op jit(solution)/shard_map/ppermute | solution.py:43
  22.0 0.0 collective-permute-start.5
  22.0 1.8 %copy.10 = bf16[1,8,2,128,320]{4,3,2,1,0:T(8,128)(2,1)S(1)} copy(bf16[1,8,2,128,320]{3,4,2,1,0:T(8,128)(2,1)} %param.11) | data formatting | bytes 2621440 | tf_op args[4]
  23.8 0.7 %fusion.1.starts_ref = s32[8]{0:T(128)S(1)} fusion(s32[8,8]{1,0:T(8,128)} %param.12, s32[]{:T(128)S(6)} %select_n.19, s32[]{:T(128)S(6)} %sub.25), kind=kLoop, calls=%fused_computation.9 | loop fusion | flops 8 | bytes 72 | tf_op jit(solution)/shard_map/sub | solution.py:492
  24.5 2.7 %collective-permute-done.4.first_ref = bf16[2,192,256]{2,1,0:T(8,128)(2,1)S(1)} collective-permute-done((bf16[2,192,256]{2,1,0:T(8,128)(2,1)S(1)}, bf16[2,192,256]{2,1,0:T(8,128)(2,1)S(1)}, u32[]{:S(2)}, u32[]{:S(2)}) %collective-permute-start.4) | collective-permute-done | bytes 196640 | tf_op jit(solution)/shard_map/ppermute | solution.py:43
  27.2 0.0 collective-permute-done.5.second_ref
  27.2 1.0 %second_level_early.1 = bf16[6,2,64,128]{3,2,1,0:T(8,128)(2,1)S(1)} custom-call(s32[8]{0:T(128)S(1)} %fusion.1.starts_ref, s32[3]{0:T(128)S(1)} %pad_add_fusion.side_ref, s32[16]{0:T(128)S(1)} %get-tuple-element.50.sector_ref, bf16[2,512,256]{2,1,0:T(8,128)(2,1)S(1)} %add_convert_fusion.own_ref, bf16[2,192,256]{2,1,0:T(8,128)(2,1)S(1)} %collective-permute-done.4.first_ref, ...), custom_call_target="tpu_custom_call" | custom-call | flops 125829120 | bytes 1048576 | tf_op jit(solution)/shard_map/second_level_early/pallas_call | solution.py:249
  28.2 1.6 %collective-permute-start.6 = (bf16[6,2,64,128]{3,2,1,0:T(8,128)(2,1)S(1)}, bf16[6,2,64,128]{3,2,1,0:T(8,128)(2,1)S(1)}, u32[]{:S(2)}, u32[]{:S(2)}) collective-permute-start(bf16[6,2,64,128]{3,2,1,0:T(8,128)(2,1)S(1)} %second_level_early.1), channel_id=1, source_target_pairs={{0,8},{8,0},{4,12},{12,4},{16,24},{24,16},{20,28},{28,20},{1,9},{9... | collective-permute-start | bytes 589832 | tf_op jit(solution)/shard_map/ppermute | solution.py:54
  29.8 1.9 %second_level.1 = (bf16[16,2,64,128]{3,2,1,0:T(8,128)(2,1)S(1)}, bf16[10,2,64,128]{3,2,1,0:T(8,128)(2,1)S(1)}) custom-call(s32[8]{0:T(128)S(1)} %fusion.1.starts_ref, s32[3]{0:T(128)S(1)} %pad_add_fusion.side_ref, s32[16]{0:T(128)S(1)} %get-tuple-element.54.own_at_ref, s32[16]{0:T(128)S(1)} %get-tuple-element.55.other_at_ref, ...), custom_call_target="tpu_custom_call" | custom-call | flops 671088640 | bytes 4194304 | tf_op jit(solution)/shard_map/second_level/pallas_call | solution.py:260
  31.7 3.0 %collective-permute-done.6.refs_0_ = bf16[6,2,64,128]{3,2,1,0:T(8,128)(2,1)S(1)} collective-permute-done((bf16[6,2,64,128]{3,2,1,0:T(8,128)(2,1)S(1)}, bf16[6,2,64,128]{3,2,1,0:T(8,128)(2,1)S(1)}, u32[]{:S(2)}, u32[]{:S(2)}) %collective-permute-start.6) | collective-permute-done | bytes 196640 | tf_op jit(solution)/shard_map/ppermute | solution.py:54
  34.7 1.5 %collective-permute-start.7 = (bf16[10,2,64,128]{3,2,1,0:T(8,128)(2,1)S(1)}, bf16[10,2,64,128]{3,2,1,0:T(8,128)(2,1)S(1)}, u32[]{:S(2)}, u32[]{:S(2)}) collective-permute-start(bf16[10,2,64,128]{3,2,1,0:T(8,128)(2,1)S(1)} %get-tuple-element.57), channel_id=1, source_target_pairs={{0,8},{8,0},{4,12},{12,4},{16,24},{24,16},{20,28},{28,20},{1,9},{9... | collective-permute-start | bytes 983048 | tf_op jit(solution)/shard_map/ppermute | solution.py:54
  36.2 0.6 early_wires.1
  36.8 2.4 %collective-permute-start.8 = (bf16[2,2,64,128]{3,2,1,0:T(8,128)(2,1)S(1)}, bf16[2,2,64,128]{3,2,1,0:T(8,128)(2,1)S(1)}, u32[]{:S(2)}, u32[]{:S(2)}) collective-permute-start(bf16[2,2,64,128]{3,2,1,0:T(8,128)(2,1)S(1)} %get-tuple-element.62), channel_id=1, source_target_pairs={{0,3},{1,2},{2,1},{3,0},{4,7},{5,6},{6,5},{7,4},{8,11},{9,10},{10,... | collective-permute-start | bytes 196616 | tf_op jit(solution)/shard_map/ppermute | solution.py:425
  39.2 0.6 %collective-permute-start.12 = (bf16[4,2,64,128]{3,2,1,0:T(8,128)(2,1)S(1)}, bf16[4,2,64,128]{3,2,1,0:T(8,128)(2,1)S(1)}, u32[]{:S(2)}, u32[]{:S(2)}) collective-permute-start(bf16[4,2,64,128]{3,2,1,0:T(8,128)(2,1)S(1)} %get-tuple-element.70), channel_id=1, source_target_pairs={{0,2},{1,3},{2,0},{3,1},{4,6},{5,7},{6,4},{7,5},{8,10},{9,11},{10,... | collective-permute-start | bytes 393224 | tf_op jit(solution)/shard_map/ppermute | solution.py:425
  39.9 3.1 %collective-permute-done.8.refs_0_ = bf16[2,2,64,128]{3,2,1,0:T(8,128)(2,1)S(1)} collective-permute-done((bf16[2,2,64,128]{3,2,1,0:T(8,128)(2,1)S(1)}, bf16[2,2,64,128]{3,2,1,0:T(8,128)(2,1)S(1)}, u32[]{:S(2)}, u32[]{:S(2)}) %collective-permute-start.8) | collective-permute-done | bytes 65568 | tf_op jit(solution)/shard_map/ppermute | solution.py:425
  43.0 0.1 collective-permute-done.7.refs_0_
  43.0 0.8 %late_wires.2 = (bf16[6,2,64,128]{3,2,1,0:T(8,128)(2,1)S(1)}, bf16[5,2,64,128]{3,2,1,0:T(8,128)(2,1)S(1)}, bf16[3,2,64,128]{3,2,1,0:T(8,128)(2,1)S(1)}, bf16[8,2,64,128]{3,2,1,0:T(8,128)(2,1)S(1)}) custom-call(s32[1]{0:T(128)} %bitcast.me_ref, s32[16]{0:T(128)S(1)} %get-tuple-element.58.target_ref, s32[16]{0:T(128)S(1)} %get-tuple-element.59.rank_ref, ...), custom_call_target="tpu_custom_call" | custom-call | bytes 2097152 | tf_op jit(solution)/shard_map/late_wires/pallas_call | solution.py:377
  43.8 2.4 %collective-permute-start.9 = (bf16[6,2,64,128]{3,2,1,0:T(8,128)(2,1)S(1)}, bf16[6,2,64,128]{3,2,1,0:T(8,128)(2,1)S(1)}, u32[]{:S(2)}, u32[]{:S(2)}) collective-permute-start(bf16[6,2,64,128]{3,2,1,0:T(8,128)(2,1)S(1)} %get-tuple-element.66), channel_id=1, source_target_pairs={{0,3},{1,2},{2,1},{3,0},{4,7},{5,6},{6,5},{7,4},{8,11},{9,10},{10,... | collective-permute-start | bytes 589832 | tf_op jit(solution)/shard_map/ppermute | solution.py:425
  46.2 1.7 %collective-permute-start.10 = (bf16[5,2,64,128]{3,2,1,0:T(8,128)(2,1)S(1)}, bf16[5,2,64,128]{3,2,1,0:T(8,128)(2,1)S(1)}, u32[]{:S(2)}, u32[]{:S(2)}) collective-permute-start(bf16[5,2,64,128]{3,2,1,0:T(8,128)(2,1)S(1)} %get-tuple-element.67), channel_id=1, source_target_pairs={{0,1},{1,0},{2,3},{3,2},{4,5},{5,4},{6,7},{7,6},{8,9},{9,8},{10,11... | collective-permute-start | bytes 491528 | tf_op jit(solution)/shard_map/ppermute | solution.py:425
  48.0 5.1 %collective-permute-done.12.refs_5_ = bf16[4,2,64,128]{3,2,1,0:T(8,128)(2,1)S(1)} collective-permute-done((bf16[4,2,64,128]{3,2,1,0:T(8,128)(2,1)S(1)}, bf16[4,2,64,128]{3,2,1,0:T(8,128)(2,1)S(1)}, u32[]{:S(2)}, u32[]{:S(2)}) %collective-permute-start.12) | collective-permute-done | bytes 131104 | tf_op jit(solution)/shard_map/ppermute | solution.py:425
  53.1 0.6 %late_wires.3 = bf16[4,2,64,128]{3,2,1,0:T(8,128)(2,1)S(1)} custom-call(s32[1]{0:T(128)} %bitcast.me_ref, s32[16]{0:T(128)S(1)} %get-tuple-element.58.target_ref, s32[16]{0:T(128)S(1)} %get-tuple-element.59.rank_ref, bf16[16,2,64,128]{3,2,1,0:T(8,128)(2,1)S(1)} %get-tuple-element.60.keep_ref, bf16[10,2,64,128]{3,2,1,0:T(8,128)(2,1)S(1)} %collective-permute-done.7.refs_0_, ...), custom_call_target="tpu_custom_call" | custom-call | bytes 2097152 | tf_op jit(solution)/shard_map/late_wires/pallas_call | solution.py:377
  53.7 0.1 collective-permute-start.13
  53.8 2.2 %collective-permute-start.11 = (bf16[3,2,64,128]{3,2,1,0:T(8,128)(2,1)S(1)}, bf16[3,2,64,128]{3,2,1,0:T(8,128)(2,1)S(1)}, u32[]{:S(2)}, u32[]{:S(2)}) collective-permute-start(bf16[3,2,64,128]{3,2,1,0:T(8,128)(2,1)S(1)} %get-tuple-element.68), channel_id=1, source_target_pairs={{0,1},{1,0},{2,3},{3,2},{4,5},{5,4},{6,7},{7,6},{8,9},{9,8},{10,11... | collective-permute-start | bytes 294920 | tf_op jit(solution)/shard_map/ppermute | solution.py:425
  56.0 2.7 %collective-permute-done.11.refs_3_ = bf16[3,2,64,128]{3,2,1,0:T(8,128)(2,1)S(1)} collective-permute-done((bf16[3,2,64,128]{3,2,1,0:T(8,128)(2,1)S(1)}, bf16[3,2,64,128]{3,2,1,0:T(8,128)(2,1)S(1)}, u32[]{:S(2)}, u32[]{:S(2)}) %collective-permute-start.11) | collective-permute-done | bytes 98336 | tf_op jit(solution)/shard_map/ppermute | solution.py:425
  58.7 2.9 %collective-permute-done.13.refs_6_ = bf16[4,2,64,128]{3,2,1,0:T(8,128)(2,1)S(1)} collective-permute-done((bf16[4,2,64,128]{3,2,1,0:T(8,128)(2,1)S(1)}, bf16[4,2,64,128]{3,2,1,0:T(8,128)(2,1)S(1)}, u32[]{:S(2)}, u32[]{:S(2)}) %collective-permute-start.13) | collective-permute-done | bytes 131104 | tf_op jit(solution)/shard_map/ppermute | solution.py:425
  61.7 0.0 collective-permute-done.10.refs_2_
  61.7 0.0 collective-permute-done.9.refs_1_
  61.7 1.0 %collect.1 = bf16[32,2,64,128]{3,2,1,0:T(8,128)(2,1)} custom-call(s32[1]{0:T(128)} %bitcast.me_ref, bf16[2,2,64,128]{3,2,1,0:T(8,128)(2,1)S(1)} %collective-permute-done.8.refs_0_, bf16[6,2,64,128]{3,2,1,0:T(8,128)(2,1)S(1)} %collective-permute-done.9.refs_1_, bf16[5,2,64,128]{3,2,1,0:T(8,128)(2,1)S(1)} %collective-permute-done.10.refs_2_, ...), custom_call_target="tpu_custom_call" | custom-call | bytes 2097152 | tf_op jit(solution)/shard_map/collect/pallas_call | solution.py:408
  (2 shorter events, 0.1 us)
Async XLA Ops:
  0.0 5.4 %copy-start.1 = (bf16[1,4,2,128,320]{3,4,2,1,0:T(8,128)(2,1)S(1)}, bf16[1,4,2,128,320]{3,4,2,1,0:T(8,128)(2,1)}, u32[]{:S(2)}) copy-start(bf16[1,4,2,128,320]{3,4,2,1,0:T(8,128)(2,1)} %param.9) | copy-start | bytes 1966084
  2.3 12.2 %collective-permute-start = (bf16[2,192,512]{2,1,0:T(8,128)(2,1)S(1)}, bf16[2,192,512]{2,1,0:T(8,128)(2,1)S(1)}, u32[]{:S(2)}, u32[]{:S(2)}) collective-permute-start(bf16[2,192,512]{2,1,0:T(8,128)(2,1)S(1)} %get-tuple-element.41.sent_first_ref), channel_id=1, source_target_pairs={{0,1},{1,0},{2,3},{3,2},{4,5},{5,4},{6,7},{7,6},{8,9},{9,8},{10,11... | collective-permute-start | bytes 1179656 | tf_op jit(solution)/shard_map/ppermute | solution.py:43
  5.4 9.1 %collective-permute-start.1 = (bf16[2,192,512]{2,1,0:T(8,128)(2,1)S(1)}, bf16[2,192,512]{2,1,0:T(8,128)(2,1)S(1)}, u32[]{:S(2)}, u32[]{:S(2)}) collective-permute-start(bf16[2,192,512]{2,1,0:T(8,128)(2,1)S(1)} %get-tuple-element.42.sent_second_ref), channel_id=1, source_target_pairs={{0,4},{1,2},{2,1},{3,7},{4,0},{5,6},{6,5},{7,3},{8,12},{9,10},{10,... | collective-permute-start | bytes 1179656 | tf_op jit(solution)/shard_map/ppermute | solution.py:43
  5.9 0.7 %copy-start = (s32[1,16,1]{1,2,0:T(1,128)S(1)}, s32[1,16,1]{1,2,0:T(1,128)}, u32[]{:S(2)}) copy-start(s32[1,16,1]{1,2,0:T(1,128)} %param.13) | copy-start | bytes 196
  5.9 2.2 %copy-start.2 = (s32[8,4]{0,1:T(4,128)S(1)}, s32[8,4]{0,1:T(4,128)}, u32[]{:S(2)}) copy-start(s32[8,4]{0,1:T(4,128)} %param.10) | copy-start | bytes 388
  6.5 3.5 %collective-permute-start.2 = (s32[1,16,1]{1,2,0:T(1,128)S(1)}, s32[1,16,1]{1,2,0:T(1,128)S(1)}, u32[]{:S(2)}, u32[]{:S(2)}) collective-permute-start(s32[1,16,1]{1,2,0:T(1,128)S(1)} %copy-done), channel_id=1, source_target_pairs={{0,8},{8,0},{4,12},{12,4},{16,24},{24,16},{20,28},{28,20},{1,9},{9... | collective-permute-start | bytes 200 | tf_op jit(solution)/shard_map/ppermute | solution.py:54
  15.7 2.1 %collective-permute-start.3 = (bf16[2,512,256]{2,1,0:T(8,128)(2,1)S(1)}, bf16[2,512,256]{2,1,0:T(8,128)(2,1)}, u32[]{:S(2)}, u32[]{:S(2)}) collective-permute-start(bf16[2,512,256]{2,1,0:T(8,128)(2,1)S(1)} %first_level.3), channel_id=1, source_target_pairs={{0,4},{4,0},{8,12},{12,8},{16,20},{20,16},{24,28},{28,24},{1,5},{5... | collective-permute-start | bytes 1572872 | tf_op jit(solution)/shard_map/ppermute | solution.py:54
  19.1 8.1 %collective-permute-start.4 = (bf16[2,192,256]{2,1,0:T(8,128)(2,1)S(1)}, bf16[2,192,256]{2,1,0:T(8,128)(2,1)S(1)}, u32[]{:S(2)}, u32[]{:S(2)}) collective-permute-start(bf16[2,192,256]{2,1,0:T(8,128)(2,1)S(1)} %get-tuple-element.76), channel_id=1, source_target_pairs={{0,1},{1,0},{2,3},{3,2},{4,5},{5,4},{6,7},{7,6},{8,9},{9,8},{10,11... | collective-permute-start | bytes 589832 | tf_op jit(solution)/shard_map/ppermute | solution.py:43
  22.0 5.2 %collective-permute-start.5 = (bf16[2,192,256]{2,1,0:T(8,128)(2,1)S(1)}, bf16[2,192,256]{2,1,0:T(8,128)(2,1)S(1)}, u32[]{:S(2)}, u32[]{:S(2)}) collective-permute-start(bf16[2,192,256]{2,1,0:T(8,128)(2,1)S(1)} %get-tuple-element.75), channel_id=1, source_target_pairs={{0,4},{1,2},{2,1},{3,7},{4,0},{5,6},{6,5},{7,3},{8,12},{9,10},{10,... | collective-permute-start | bytes 589832 | tf_op jit(solution)/shard_map/ppermute | solution.py:43
  28.2 6.5 %collective-permute-start.6 = (bf16[6,2,64,128]{3,2,1,0:T(8,128)(2,1)S(1)}, bf16[6,2,64,128]{3,2,1,0:T(8,128)(2,1)S(1)}, u32[]{:S(2)}, u32[]{:S(2)}) collective-permute-start(bf16[6,2,64,128]{3,2,1,0:T(8,128)(2,1)S(1)} %second_level_early.1), channel_id=1, source_target_pairs={{0,8},{8,0},{4,12},{12,4},{16,24},{24,16},{20,28},{28,20},{1,9},{9... | collective-permute-start | bytes 589832 | tf_op jit(solution)/shard_map/ppermute | solution.py:54
  34.7 8.3 %collective-permute-start.7 = (bf16[10,2,64,128]{3,2,1,0:T(8,128)(2,1)S(1)}, bf16[10,2,64,128]{3,2,1,0:T(8,128)(2,1)S(1)}, u32[]{:S(2)}, u32[]{:S(2)}) collective-permute-start(bf16[10,2,64,128]{3,2,1,0:T(8,128)(2,1)S(1)} %get-tuple-element.57), channel_id=1, source_target_pairs={{0,8},{8,0},{4,12},{12,4},{16,24},{24,16},{20,28},{28,20},{1,9},{9... | collective-permute-start | bytes 983048 | tf_op jit(solution)/shard_map/ppermute | solution.py:54
  36.8 6.1 %collective-permute-start.8 = (bf16[2,2,64,128]{3,2,1,0:T(8,128)(2,1)S(1)}, bf16[2,2,64,128]{3,2,1,0:T(8,128)(2,1)S(1)}, u32[]{:S(2)}, u32[]{:S(2)}) collective-permute-start(bf16[2,2,64,128]{3,2,1,0:T(8,128)(2,1)S(1)} %get-tuple-element.62), channel_id=1, source_target_pairs={{0,3},{1,2},{2,1},{3,0},{4,7},{5,6},{6,5},{7,4},{8,11},{9,10},{10,... | collective-permute-start | bytes 196616 | tf_op jit(solution)/shard_map/ppermute | solution.py:425
  39.2 13.9 %collective-permute-start.12 = (bf16[4,2,64,128]{3,2,1,0:T(8,128)(2,1)S(1)}, bf16[4,2,64,128]{3,2,1,0:T(8,128)(2,1)S(1)}, u32[]{:S(2)}, u32[]{:S(2)}) collective-permute-start(bf16[4,2,64,128]{3,2,1,0:T(8,128)(2,1)S(1)} %get-tuple-element.70), channel_id=1, source_target_pairs={{0,2},{1,3},{2,0},{3,1},{4,6},{5,7},{6,4},{7,5},{8,10},{9,11},{10,... | collective-permute-start | bytes 393224 | tf_op jit(solution)/shard_map/ppermute | solution.py:425
  43.8 17.8 %collective-permute-start.9 = (bf16[6,2,64,128]{3,2,1,0:T(8,128)(2,1)S(1)}, bf16[6,2,64,128]{3,2,1,0:T(8,128)(2,1)S(1)}, u32[]{:S(2)}, u32[]{:S(2)}) collective-permute-start(bf16[6,2,64,128]{3,2,1,0:T(8,128)(2,1)S(1)} %get-tuple-element.66), channel_id=1, source_target_pairs={{0,3},{1,2},{2,1},{3,0},{4,7},{5,6},{6,5},{7,4},{8,11},{9,10},{10,... | collective-permute-start | bytes 589832 | tf_op jit(solution)/shard_map/ppermute | solution.py:425
  46.2 15.4 %collective-permute-start.10 = (bf16[5,2,64,128]{3,2,1,0:T(8,128)(2,1)S(1)}, bf16[5,2,64,128]{3,2,1,0:T(8,128)(2,1)S(1)}, u32[]{:S(2)}, u32[]{:S(2)}) collective-permute-start(bf16[5,2,64,128]{3,2,1,0:T(8,128)(2,1)S(1)} %get-tuple-element.67), channel_id=1, source_target_pairs={{0,1},{1,0},{2,3},{3,2},{4,5},{5,4},{6,7},{7,6},{8,9},{9,8},{10,11... | collective-permute-start | bytes 491528 | tf_op jit(solution)/shard_map/ppermute | solution.py:425
  53.7 7.9 %collective-permute-start.13 = (bf16[4,2,64,128]{3,2,1,0:T(8,128)(2,1)S(1)}, bf16[4,2,64,128]{3,2,1,0:T(8,128)(2,1)S(1)}, u32[]{:S(2)}, u32[]{:S(2)}) collective-permute-start(bf16[4,2,64,128]{3,2,1,0:T(8,128)(2,1)S(1)} %late_wires.3), channel_id=1, source_target_pairs={{0,2},{1,3},{2,0},{3,1},{4,6},{5,7},{6,4},{7,5},{8,10},{9,11},{10,... | collective-permute-start | bytes 393224 | tf_op jit(solution)/shard_map/ppermute | solution.py:425
  53.8 4.9 %collective-permute-start.11 = (bf16[3,2,64,128]{3,2,1,0:T(8,128)(2,1)S(1)}, bf16[3,2,64,128]{3,2,1,0:T(8,128)(2,1)S(1)}, u32[]{:S(2)}, u32[]{:S(2)}) collective-permute-start(bf16[3,2,64,128]{3,2,1,0:T(8,128)(2,1)S(1)} %get-tuple-element.68), channel_id=1, source_target_pairs={{0,1},{1,0},{2,3},{3,2},{4,5},{5,4},{6,7},{7,6},{8,9},{9,8},{10,11... | collective-permute-start | bytes 294920 | tf_op jit(solution)/shard_map/ppermute | solution.py:425

commit v21 on v20

--- a/solution.py
+++ b/solution.py
@@ -12,7 +12,7 @@
 REACH = 2
 OS = 64
 MARGIN_BLOCKS = (NW - 2) // 2 + REACH
-VMEM_LIMIT = 8 * 1024 * 1024
+VMEM_LIMIT = 4 * 1024 * 1024
 MOST_VMEM = 53 * 1024 * 1024
 ANY = pl.BlockSpec(memory_space=pl.ANY)
 VMEM = pl.BlockSpec(memory_space=pltpu.VMEM)

time: 62.9 us -> 62.9 us (level)
  no operation moved by 1% of the time
where the time goes in v21:
time: 62.9 us; the launch traced here: 62.7 us
  waiting for transfers between devices  25 us (40%)
  starting transfers between devices  20.1 us (32%)
  Pallas kernels  12.3 us (20%)
  other arithmetic  2.6 us (4%)
  local copies, waits for them, and re-layouts  2.46 us (4%)
    ppermute x6, waiting for transfers between devices, spread(): received.append(lax.ppermute(wire, 'beam', route) if distance else wire)  13.8 us
    ppermute x6, starting transfers between devices, spread(): received.append(lax.ppermute(wire, 'beam', route) if distance else wire)  9.44 us
    ppermute x4, starting transfers between devices, trade_edges(): received.append(lax.ppermute(block, ('aperture', 'beam'), route))  6.01 us
    ppermute x4, waiting for transfers between devices, partner(): return lax.ppermute(block, axis, route)  5.68 us
    ppermute x4, waiting for transfers between devices, trade_edges(): received.append(lax.ppermute(block, ('aperture', 'beam'), route))  5.52 us
    ppermute x4, starting transfers between devices, partner(): return lax.ppermute(block, axis, route)  4.61 us
    pallas_call x2, Pallas kernels, first_level(): pl.pallas_call(functools.partial(first_level_kernel, column, rows), out_s...  2.39 us
    pallas_call x1, Pallas kernels, resample(): pl.pallas_call(resample_kernel, out_shape=(shape, shape), in_specs=[ANY,...  2.31 us
  transfers between devices with their start and end apart: 14, of which 10 were waited for; matrix products, arithmetic and copies ran while one was open for 6% of the time, Pallas kernels for 11%

profile of v21, /device:TPU:0, one launch (start us, length us, event | category | flops | bytes accessed | tf_op | source)
XLA Modules:
  0.0 62.7 jit_solution(5156130346625237810)
XLA Ops:
  0.0 0.0 copy-start.1
  0.0 2.3 %resample.1 = (bf16[2,192,512]{2,1,0:T(8,128)(2,1)S(1)}, bf16[2,192,512]{2,1,0:T(8,128)(2,1)S(1)}) custom-call(bf16[2,256,512]{2,1,0:T(8,128)(2,1)} %bitcast.23, bf16[2,512,512]{2,1,0:T(8,128)(2,1)} %bitcast.22), custom_call_target="tpu_custom_call" | custom-call | flops 536870912 | bytes 2097152 | tf_op jit(solution)/shard_map/resample/pallas_call | solution.py:101
  2.3 3.1 %collective-permute-start = (bf16[2,192,512]{2,1,0:T(8,128)(2,1)S(1)}, bf16[2,192,512]{2,1,0:T(8,128)(2,1)S(1)}, u32[]{:S(2)}, u32[]{:S(2)}) collective-permute-start(bf16[2,192,512]{2,1,0:T(8,128)(2,1)S(1)} %get-tuple-element.41.sent_first_ref), channel_id=1, source_target_pairs={{0,1},{1,0},{2,3},{3,2},{4,5},{5,4},{6,7},{7,6},{8,9},{9,8},{10,11... | collective-permute-start | bytes 1179656 | tf_op jit(solution)/shard_map/ppermute | solution.py:43
  5.4 0.0 collective-permute-start.1
  5.4 0.0 copy-done.1
  5.4 0.4 copy.8
  5.8 0.1 slice_bitcast_fusion
  5.9 0.0 copy-start
  5.9 0.0 copy-start.2
  5.9 0.4 maximum_maximum_fusion.weights_ref
  6.4 0.1 copy-done
  6.5 1.5 %collective-permute-start.2 = (s32[1,16,1]{1,2,0:T(1,128)S(1)}, s32[1,16,1]{1,2,0:T(1,128)S(1)}, u32[]{:S(2)}, u32[]{:S(2)}) collective-permute-start(s32[1,16,1]{1,2,0:T(1,128)S(1)} %copy-done), channel_id=1, source_target_pairs={{0,8},{8,0},{4,12},{12,4},{16,24},{24,16},{20,28},{28,20},{1,9},{9... | collective-permute-start | bytes 200 | tf_op jit(solution)/shard_map/ppermute | solution.py:54
  8.0 0.1 pad_add_fusion.side_ref
  8.1 0.0 copy-done.2
  8.1 0.2 subtract_reduce_fusion.starts_ref
  8.3 1.8 %collective-permute-done.2 = s32[1,16,1]{1,2,0:T(1,128)S(1)} collective-permute-done((s32[1,16,1]{1,2,0:T(1,128)S(1)}, s32[1,16,1]{1,2,0:T(1,128)S(1)}, u32[]{:S(2)}, u32[]{:S(2)}) %collective-permute-start.2) | collective-permute-done | bytes 96 | tf_op jit(solution)/shard_map/ppermute | solution.py:54
  10.1 1.6 %plan.1 = (s32[16]{0:T(128)S(1)}, s32[16]{0:T(128)S(1)}, s32[16]{0:T(128)S(1)}, s32[16]{0:T(128)S(1)}, s32[16]{0:T(128)S(1)}) custom-call(s32[1]{0:T(128)} %bitcast.me_ref, s32[16]{0:T(128)S(1)} %bitcast.20, s32[16]{0:T(128)S(1)} %bitcast.21), custom_call_target="tpu_custom_call" | custom-call | tf_op jit(solution)/shard_map/plan/pallas_call | solution.py:316
  11.7 2.8 %collective-permute-done.first_ref = bf16[2,192,512]{2,1,0:T(8,128)(2,1)S(1)} collective-permute-done((bf16[2,192,512]{2,1,0:T(8,128)(2,1)S(1)}, bf16[2,192,512]{2,1,0:T(8,128)(2,1)S(1)}, u32[]{:S(2)}, u32[]{:S(2)}) %collective-permute-start) | collective-permute-done | bytes 393248 | tf_op jit(solution)/shard_map/ppermute | solution.py:43
  14.5 0.0 collective-permute-done.1.second_ref
  14.5 1.2 %first_level.3 = bf16[2,512,256]{2,1,0:T(8,128)(2,1)S(1)} custom-call(s32[4]{0:T(128)S(1)} %subtract_reduce_fusion.starts_ref, s32[3]{0:T(128)S(1)} %pad_add_fusion.side_ref, bf16[2,192,512]{2,1,0:T(8,128)(2,1)S(1)} %get-tuple-element.41.sent_first_ref, bf16[2,192,512]{2,1,0:T(8,128)(2,1)S(1)} %get-tuple-element.42.sent_second_ref, ...), custom_call_target="tpu_custom_call" | custom-call | flops 335544320 | bytes 2097152 | tf_op jit(solution)/shard_map/first_level/pallas_call | solution.py:182
  15.7 0.1 collective-permute-start.3
  15.8 1.2 %first_level.2 = bf16[2,512,256]{2,1,0:T(8,128)(2,1)S(1)} custom-call(s32[4]{0:T(128)S(1)} %subtract_reduce_fusion.starts_ref, s32[3]{0:T(128)S(1)} %pad_add_fusion.side_ref, bf16[2,192,512]{2,1,0:T(8,128)(2,1)S(1)} %get-tuple-element.41.sent_first_ref, bf16[2,192,512]{2,1,0:T(8,128)(2,1)S(1)} %get-tuple-element.42.sent_second_ref, ...), custom_call_target="tpu_custom_call" | custom-call | flops 335544320 | bytes 2097152 | tf_op jit(solution)/shard_map/first_level/pallas_call | solution.py:182
  17.0 0.8 %collective-permute-done.3 = bf16[2,512,256]{2,1,0:T(8,128)(2,1)} collective-permute-done((bf16[2,512,256]{2,1,0:T(8,128)(2,1)S(1)}, bf16[2,512,256]{2,1,0:T(8,128)(2,1)}, u32[]{:S(2)}, u32[]{:S(2)}) %collective-permute-start.3) | collective-permute-done | bytes 524320 | tf_op jit(solution)/shard_map/ppermute | solution.py:54
  17.8 1.2 %add_convert_fusion.own_ref = bf16[2,512,256]{2,1,0:T(8,128)(2,1)S(1)} fusion(bf16[2,512,256]{2,1,0:T(8,128)(2,1)} %collective-permute-done.3, bf16[2,512,256]{2,1,0:T(8,128)(2,1)S(1)} %first_level.2), kind=kLoop, calls=%fused_computation.1 | loop fusion | flops 1048576 | bytes 1572864 | tf_op jit(solution)/shard_map/convert_element_type | solution.py:486
  19.1 2.9 %collective-permute-start.4 = (bf16[2,192,256]{2,1,0:T(8,128)(2,1)S(1)}, bf16[2,192,256]{2,1,0:T(8,128)(2,1)S(1)}, u32[]{:S(2)}, u32[]{:S(2)}) collective-permute-start(bf16[2,192,256]{2,1,0:T(8,128)(2,1)S(1)} %get-tuple-element.76), channel_id=1, source_target_pairs={{0,1},{1,0},{2,3},{3,2},{4,5},{5,4},{6,7},{7,6},{8,9},{9,8},{10,11... | collective-permute-start | bytes 589832 | tf_op jit(solution)/shard_map/ppermute | solution.py:43
  22.0 0.0 collective-permute-start.5
  22.0 1.8 %copy.10 = bf16[1,8,2,128,320]{4,3,2,1,0:T(8,128)(2,1)S(1)} copy(bf16[1,8,2,128,320]{3,4,2,1,0:T(8,128)(2,1)} %param.11) | data formatting | bytes 2621440 | tf_op args[4]
  23.8 0.7 %fusion.1.starts_ref = s32[8]{0:T(128)S(1)} fusion(s32[8,8]{1,0:T(8,128)} %param.12, s32[]{:T(128)S(6)} %select_n.19, s32[]{:T(128)S(6)} %sub.25), kind=kLoop, calls=%fused_computation.9 | loop fusion | flops 8 | bytes 72 | tf_op jit(solution)/shard_map/sub | solution.py:492
  24.5 2.7 %collective-permute-done.4.first_ref = bf16[2,192,256]{2,1,0:T(8,128)(2,1)S(1)} collective-permute-done((bf16[2,192,256]{2,1,0:T(8,128)(2,1)S(1)}, bf16[2,192,256]{2,1,0:T(8,128)(2,1)S(1)}, u32[]{:S(2)}, u32[]{:S(2)}) %collective-permute-start.4) | collective-permute-done | bytes 196640 | tf_op jit(solution)/shard_map/ppermute | solution.py:43
  27.2 0.0 collective-permute-done.5.second_ref
  27.2 1.0 %second_level_early.1 = bf16[6,2,64,128]{3,2,1,0:T(8,128)(2,1)S(1)} custom-call(s32[8]{0:T(128)S(1)} %fusion.1.starts_ref, s32[3]{0:T(128)S(1)} %pad_add_fusion.side_ref, s32[16]{0:T(128)S(1)} %get-tuple-element.50.sector_ref, bf16[2,512,256]{2,1,0:T(8,128)(2,1)S(1)} %add_convert_fusion.own_ref, bf16[2,192,256]{2,1,0:T(8,128)(2,1)S(1)} %collective-permute-done.4.first_ref, ...), custom_call_target="tpu_custom_call" | custom-call | flops 125829120 | bytes 1048576 | tf_op jit(solution)/shard_map/second_level_early/pallas_call | solution.py:249
  28.2 1.6 %collective-permute-start.6 = (bf16[6,2,64,128]{3,2,1,0:T(8,128)(2,1)S(1)}, bf16[6,2,64,128]{3,2,1,0:T(8,128)(2,1)S(1)}, u32[]{:S(2)}, u32[]{:S(2)}) collective-permute-start(bf16[6,2,64,128]{3,2,1,0:T(8,128)(2,1)S(1)} %second_level_early.1), channel_id=1, source_target_pairs={{0,8},{8,0},{4,12},{12,4},{16,24},{24,16},{20,28},{28,20},{1,9},{9... | collective-permute-start | bytes 589832 | tf_op jit(solution)/shard_map/ppermute | solution.py:54
  29.8 1.9 %second_level.1 = (bf16[16,2,64,128]{3,2,1,0:T(8,128)(2,1)S(1)}, bf16[10,2,64,128]{3,2,1,0:T(8,128)(2,1)S(1)}) custom-call(s32[8]{0:T(128)S(1)} %fusion.1.starts_ref, s32[3]{0:T(128)S(1)} %pad_add_fusion.side_ref, s32[16]{0:T(128)S(1)} %get-tuple-element.54.own_at_ref, s32[16]{0:T(128)S(1)} %get-tuple-element.55.other_at_ref, ...), custom_call_target="tpu_custom_call" | custom-call | flops 671088640 | bytes 4194304 | tf_op jit(solution)/shard_map/second_level/pallas_call | solution.py:260
  31.7 3.0 %collective-permute-done.6.refs_0_ = bf16[6,2,64,128]{3,2,1,0:T(8,128)(2,1)S(1)} collective-permute-done((bf16[6,2,64,128]{3,2,1,0:T(8,128)(2,1)S(1)}, bf16[6,2,64,128]{3,2,1,0:T(8,128)(2,1)S(1)}, u32[]{:S(2)}, u32[]{:S(2)}) %collective-permute-start.6) | collective-permute-done | bytes 196640 | tf_op jit(solution)/shard_map/ppermute | solution.py:54
  34.7 1.5 %collective-permute-start.7 = (bf16[10,2,64,128]{3,2,1,0:T(8,128)(2,1)S(1)}, bf16[10,2,64,128]{3,2,1,0:T(8,128)(2,1)S(1)}, u32[]{:S(2)}, u32[]{:S(2)}) collective-permute-start(bf16[10,2,64,128]{3,2,1,0:T(8,128)(2,1)S(1)} %get-tuple-element.57), channel_id=1, source_target_pairs={{0,8},{8,0},{4,12},{12,4},{16,24},{24,16},{20,28},{28,20},{1,9},{9... | collective-permute-start | bytes 983048 | tf_op jit(solution)/shard_map/ppermute | solution.py:54
  36.2 0.6 early_wires.1
  36.8 2.4 %collective-permute-start.8 = (bf16[2,2,64,128]{3,2,1,0:T(8,128)(2,1)S(1)}, bf16[2,2,64,128]{3,2,1,0:T(8,128)(2,1)S(1)}, u32[]{:S(2)}, u32[]{:S(2)}) collective-permute-start(bf16[2,2,64,128]{3,2,1,0:T(8,128)(2,1)S(1)} %get-tuple-element.62), channel_id=1, source_target_pairs={{0,3},{1,2},{2,1},{3,0},{4,7},{5,6},{6,5},{7,4},{8,11},{9,10},{10,... | collective-permute-start | bytes 196616 | tf_op jit(solution)/shard_map/ppermute | solution.py:425
  39.2 0.6 %collective-permute-start.12 = (bf16[4,2,64,128]{3,2,1,0:T(8,128)(2,1)S(1)}, bf16[4,2,64,128]{3,2,1,0:T(8,128)(2,1)S(1)}, u32[]{:S(2)}, u32[]{:S(2)}) collective-permute-start(bf16[4,2,64,128]{3,2,1,0:T(8,128)(2,1)S(1)} %get-tuple-element.70), channel_id=1, source_target_pairs={{0,2},{1,3},{2,0},{3,1},{4,6},{5,7},{6,4},{7,5},{8,10},{9,11},{10,... | collective-permute-start | bytes 393224 | tf_op jit(solution)/shard_map/ppermute | solution.py:425
  39.9 3.1 %collective-permute-done.8.refs_0_ = bf16[2,2,64,128]{3,2,1,0:T(8,128)(2,1)S(1)} collective-permute-done((bf16[2,2,64,128]{3,2,1,0:T(8,128)(2,1)S(1)}, bf16[2,2,64,128]{3,2,1,0:T(8,128)(2,1)S(1)}, u32[]{:S(2)}, u32[]{:S(2)}) %collective-permute-start.8) | collective-permute-done | bytes 65568 | tf_op jit(solution)/shard_map/ppermute | solution.py:425
  43.0 0.1 collective-permute-done.7.refs_0_
  43.0 0.8 %late_wires.2 = (bf16[6,2,64,128]{3,2,1,0:T(8,128)(2,1)S(1)}, bf16[5,2,64,128]{3,2,1,0:T(8,128)(2,1)S(1)}, bf16[3,2,64,128]{3,2,1,0:T(8,128)(2,1)S(1)}, bf16[8,2,64,128]{3,2,1,0:T(8,128)(2,1)S(1)}) custom-call(s32[1]{0:T(128)} %bitcast.me_ref, s32[16]{0:T(128)S(1)} %get-tuple-element.58.target_ref, s32[16]{0:T(128)S(1)} %get-tuple-element.59.rank_ref, ...), custom_call_target="tpu_custom_call" | custom-call | bytes 2097152 | tf_op jit(solution)/shard_map/late_wires/pallas_call | solution.py:377
  43.8 2.4 %collective-permute-start.9 = (bf16[6,2,64,128]{3,2,1,0:T(8,128)(2,1)S(1)}, bf16[6,2,64,128]{3,2,1,0:T(8,128)(2,1)S(1)}, u32[]{:S(2)}, u32[]{:S(2)}) collective-permute-start(bf16[6,2,64,128]{3,2,1,0:T(8,128)(2,1)S(1)} %get-tuple-element.66), channel_id=1, source_target_pairs={{0,3},{1,2},{2,1},{3,0},{4,7},{5,6},{6,5},{7,4},{8,11},{9,10},{10,... | collective-permute-start | bytes 589832 | tf_op jit(solution)/shard_map/ppermute | solution.py:425
  46.2 1.7 %collective-permute-start.10 = (bf16[5,2,64,128]{3,2,1,0:T(8,128)(2,1)S(1)}, bf16[5,2,64,128]{3,2,1,0:T(8,128)(2,1)S(1)}, u32[]{:S(2)}, u32[]{:S(2)}) collective-permute-start(bf16[5,2,64,128]{3,2,1,0:T(8,128)(2,1)S(1)} %get-tuple-element.67), channel_id=1, source_target_pairs={{0,1},{1,0},{2,3},{3,2},{4,5},{5,4},{6,7},{7,6},{8,9},{9,8},{10,11... | collective-permute-start | bytes 491528 | tf_op jit(solution)/shard_map/ppermute | solution.py:425
  48.0 5.1 %collective-permute-done.12.refs_5_ = bf16[4,2,64,128]{3,2,1,0:T(8,128)(2,1)S(1)} collective-permute-done((bf16[4,2,64,128]{3,2,1,0:T(8,128)(2,1)S(1)}, bf16[4,2,64,128]{3,2,1,0:T(8,128)(2,1)S(1)}, u32[]{:S(2)}, u32[]{:S(2)}) %collective-permute-start.12) | collective-permute-done | bytes 131104 | tf_op jit(solution)/shard_map/ppermute | solution.py:425
  53.1 0.6 %late_wires.3 = bf16[4,2,64,128]{3,2,1,0:T(8,128)(2,1)S(1)} custom-call(s32[1]{0:T(128)} %bitcast.me_ref, s32[16]{0:T(128)S(1)} %get-tuple-element.58.target_ref, s32[16]{0:T(128)S(1)} %get-tuple-element.59.rank_ref, bf16[16,2,64,128]{3,2,1,0:T(8,128)(2,1)S(1)} %get-tuple-element.60.keep_ref, bf16[10,2,64,128]{3,2,1,0:T(8,128)(2,1)S(1)} %collective-permute-done.7.refs_0_, ...), custom_call_target="tpu_custom_call" | custom-call | bytes 2097152 | tf_op jit(solution)/shard_map/late_wires/pallas_call | solution.py:377
  53.7 0.1 collective-permute-start.13
  53.8 2.2 %collective-permute-start.11 = (bf16[3,2,64,128]{3,2,1,0:T(8,128)(2,1)S(1)}, bf16[3,2,64,128]{3,2,1,0:T(8,128)(2,1)S(1)}, u32[]{:S(2)}, u32[]{:S(2)}) collective-permute-start(bf16[3,2,64,128]{3,2,1,0:T(8,128)(2,1)S(1)} %get-tuple-element.68), channel_id=1, source_target_pairs={{0,1},{1,0},{2,3},{3,2},{4,5},{5,4},{6,7},{7,6},{8,9},{9,8},{10,11... | collective-permute-start | bytes 294920 | tf_op jit(solution)/shard_map/ppermute | solution.py:425
  56.0 2.7 %collective-permute-done.11.refs_3_ = bf16[3,2,64,128]{3,2,1,0:T(8,128)(2,1)S(1)} collective-permute-done((bf16[3,2,64,128]{3,2,1,0:T(8,128)(2,1)S(1)}, bf16[3,2,64,128]{3,2,1,0:T(8,128)(2,1)S(1)}, u32[]{:S(2)}, u32[]{:S(2)}) %collective-permute-start.11) | collective-permute-done | bytes 98336 | tf_op jit(solution)/shard_map/ppermute | solution.py:425
  58.7 2.9 %collective-permute-done.13.refs_6_ = bf16[4,2,64,128]{3,2,1,0:T(8,128)(2,1)S(1)} collective-permute-done((bf16[4,2,64,128]{3,2,1,0:T(8,128)(2,1)S(1)}, bf16[4,2,64,128]{3,2,1,0:T(8,128)(2,1)S(1)}, u32[]{:S(2)}, u32[]{:S(2)}) %collective-permute-start.13) | collective-permute-done | bytes 131104 | tf_op jit(solution)/shard_map/ppermute | solution.py:425
  61.7 0.0 collective-permute-done.10.refs_2_
  61.7 0.0 collective-permute-done.9.refs_1_
  61.7 1.0 %collect.1 = bf16[32,2,64,128]{3,2,1,0:T(8,128)(2,1)} custom-call(s32[1]{0:T(128)} %bitcast.me_ref, bf16[2,2,64,128]{3,2,1,0:T(8,128)(2,1)S(1)} %collective-permute-done.8.refs_0_, bf16[6,2,64,128]{3,2,1,0:T(8,128)(2,1)S(1)} %collective-permute-done.9.refs_1_, bf16[5,2,64,128]{3,2,1,0:T(8,128)(2,1)S(1)} %collective-permute-done.10.refs_2_, ...), custom_call_target="tpu_custom_call" | custom-call | bytes 2097152 | tf_op jit(solution)/shard_map/collect/pallas_call | solution.py:408
  (2 shorter events, 0.1 us)
Async XLA Ops:
  0.0 5.4 %copy-start.1 = (bf16[1,4,2,128,320]{3,4,2,1,0:T(8,128)(2,1)S(1)}, bf16[1,4,2,128,320]{3,4,2,1,0:T(8,128)(2,1)}, u32[]{:S(2)}) copy-start(bf16[1,4,2,128,320]{3,4,2,1,0:T(8,128)(2,1)} %param.9) | copy-start | bytes 1966084
  2.3 12.2 %collective-permute-start = (bf16[2,192,512]{2,1,0:T(8,128)(2,1)S(1)}, bf16[2,192,512]{2,1,0:T(8,128)(2,1)S(1)}, u32[]{:S(2)}, u32[]{:S(2)}) collective-permute-start(bf16[2,192,512]{2,1,0:T(8,128)(2,1)S(1)} %get-tuple-element.41.sent_first_ref), channel_id=1, source_target_pairs={{0,1},{1,0},{2,3},{3,2},{4,5},{5,4},{6,7},{7,6},{8,9},{9,8},{10,11... | collective-permute-start | bytes 1179656 | tf_op jit(solution)/shard_map/ppermute | solution.py:43
  5.4 9.1 %collective-permute-start.1 = (bf16[2,192,512]{2,1,0:T(8,128)(2,1)S(1)}, bf16[2,192,512]{2,1,0:T(8,128)(2,1)S(1)}, u32[]{:S(2)}, u32[]{:S(2)}) collective-permute-start(bf16[2,192,512]{2,1,0:T(8,128)(2,1)S(1)} %get-tuple-element.42.sent_second_ref), channel_id=1, source_target_pairs={{0,4},{1,2},{2,1},{3,7},{4,0},{5,6},{6,5},{7,3},{8,12},{9,10},{10,... | collective-permute-start | bytes 1179656 | tf_op jit(solution)/shard_map/ppermute | solution.py:43
  5.9 0.7 %copy-start = (s32[1,16,1]{1,2,0:T(1,128)S(1)}, s32[1,16,1]{1,2,0:T(1,128)}, u32[]{:S(2)}) copy-start(s32[1,16,1]{1,2,0:T(1,128)} %param.13) | copy-start | bytes 196
  5.9 2.2 %copy-start.2 = (s32[8,4]{0,1:T(4,128)S(1)}, s32[8,4]{0,1:T(4,128)}, u32[]{:S(2)}) copy-start(s32[8,4]{0,1:T(4,128)} %param.10) | copy-start | bytes 388
  6.5 3.5 %collective-permute-start.2 = (s32[1,16,1]{1,2,0:T(1,128)S(1)}, s32[1,16,1]{1,2,0:T(1,128)S(1)}, u32[]{:S(2)}, u32[]{:S(2)}) collective-permute-start(s32[1,16,1]{1,2,0:T(1,128)S(1)} %copy-done), channel_id=1, source_target_pairs={{0,8},{8,0},{4,12},{12,4},{16,24},{24,16},{20,28},{28,20},{1,9},{9... | collective-permute-start | bytes 200 | tf_op jit(solution)/shard_map/ppermute | solution.py:54
  15.7 2.1 %collective-permute-start.3 = (bf16[2,512,256]{2,1,0:T(8,128)(2,1)S(1)}, bf16[2,512,256]{2,1,0:T(8,128)(2,1)}, u32[]{:S(2)}, u32[]{:S(2)}) collective-permute-start(bf16[2,512,256]{2,1,0:T(8,128)(2,1)S(1)} %first_level.3), channel_id=1, source_target_pairs={{0,4},{4,0},{8,12},{12,8},{16,20},{20,16},{24,28},{28,24},{1,5},{5... | collective-permute-start | bytes 1572872 | tf_op jit(solution)/shard_map/ppermute | solution.py:54
  19.1 8.1 %collective-permute-start.4 = (bf16[2,192,256]{2,1,0:T(8,128)(2,1)S(1)}, bf16[2,192,256]{2,1,0:T(8,128)(2,1)S(1)}, u32[]{:S(2)}, u32[]{:S(2)}) collective-permute-start(bf16[2,192,256]{2,1,0:T(8,128)(2,1)S(1)} %get-tuple-element.76), channel_id=1, source_target_pairs={{0,1},{1,0},{2,3},{3,2},{4,5},{5,4},{6,7},{7,6},{8,9},{9,8},{10,11... | collective-permute-start | bytes 589832 | tf_op jit(solution)/shard_map/ppermute | solution.py:43
  22.0 5.2 %collective-permute-start.5 = (bf16[2,192,256]{2,1,0:T(8,128)(2,1)S(1)}, bf16[2,192,256]{2,1,0:T(8,128)(2,1)S(1)}, u32[]{:S(2)}, u32[]{:S(2)}) collective-permute-start(bf16[2,192,256]{2,1,0:T(8,128)(2,1)S(1)} %get-tuple-element.75), channel_id=1, source_target_pairs={{0,4},{1,2},{2,1},{3,7},{4,0},{5,6},{6,5},{7,3},{8,12},{9,10},{10,... | collective-permute-start | bytes 589832 | tf_op jit(solution)/shard_map/ppermute | solution.py:43
  28.2 6.5 %collective-permute-start.6 = (bf16[6,2,64,128]{3,2,1,0:T(8,128)(2,1)S(1)}, bf16[6,2,64,128]{3,2,1,0:T(8,128)(2,1)S(1)}, u32[]{:S(2)}, u32[]{:S(2)}) collective-permute-start(bf16[6,2,64,128]{3,2,1,0:T(8,128)(2,1)S(1)} %second_level_early.1), channel_id=1, source_target_pairs={{0,8},{8,0},{4,12},{12,4},{16,24},{24,16},{20,28},{28,20},{1,9},{9... | collective-permute-start | bytes 589832 | tf_op jit(solution)/shard_map/ppermute | solution.py:54
  34.7 8.3 %collective-permute-start.7 = (bf16[10,2,64,128]{3,2,1,0:T(8,128)(2,1)S(1)}, bf16[10,2,64,128]{3,2,1,0:T(8,128)(2,1)S(1)}, u32[]{:S(2)}, u32[]{:S(2)}) collective-permute-start(bf16[10,2,64,128]{3,2,1,0:T(8,128)(2,1)S(1)} %get-tuple-element.57), channel_id=1, source_target_pairs={{0,8},{8,0},{4,12},{12,4},{16,24},{24,16},{20,28},{28,20},{1,9},{9... | collective-permute-start | bytes 983048 | tf_op jit(solution)/shard_map/ppermute | solution.py:54
  36.8 6.1 %collective-permute-start.8 = (bf16[2,2,64,128]{3,2,1,0:T(8,128)(2,1)S(1)}, bf16[2,2,64,128]{3,2,1,0:T(8,128)(2,1)S(1)}, u32[]{:S(2)}, u32[]{:S(2)}) collective-permute-start(bf16[2,2,64,128]{3,2,1,0:T(8,128)(2,1)S(1)} %get-tuple-element.62), channel_id=1, source_target_pairs={{0,3},{1,2},{2,1},{3,0},{4,7},{5,6},{6,5},{7,4},{8,11},{9,10},{10,... | collective-permute-start | bytes 196616 | tf_op jit(solution)/shard_map/ppermute | solution.py:425
  39.2 13.9 %collective-permute-start.12 = (bf16[4,2,64,128]{3,2,1,0:T(8,128)(2,1)S(1)}, bf16[4,2,64,128]{3,2,1,0:T(8,128)(2,1)S(1)}, u32[]{:S(2)}, u32[]{:S(2)}) collective-permute-start(bf16[4,2,64,128]{3,2,1,0:T(8,128)(2,1)S(1)} %get-tuple-element.70), channel_id=1, source_target_pairs={{0,2},{1,3},{2,0},{3,1},{4,6},{5,7},{6,4},{7,5},{8,10},{9,11},{10,... | collective-permute-start | bytes 393224 | tf_op jit(solution)/shard_map/ppermute | solution.py:425
  43.8 17.8 %collective-permute-start.9 = (bf16[6,2,64,128]{3,2,1,0:T(8,128)(2,1)S(1)}, bf16[6,2,64,128]{3,2,1,0:T(8,128)(2,1)S(1)}, u32[]{:S(2)}, u32[]{:S(2)}) collective-permute-start(bf16[6,2,64,128]{3,2,1,0:T(8,128)(2,1)S(1)} %get-tuple-element.66), channel_id=1, source_target_pairs={{0,3},{1,2},{2,1},{3,0},{4,7},{5,6},{6,5},{7,4},{8,11},{9,10},{10,... | collective-permute-start | bytes 589832 | tf_op jit(solution)/shard_map/ppermute | solution.py:425
  46.2 15.4 %collective-permute-start.10 = (bf16[5,2,64,128]{3,2,1,0:T(8,128)(2,1)S(1)}, bf16[5,2,64,128]{3,2,1,0:T(8,128)(2,1)S(1)}, u32[]{:S(2)}, u32[]{:S(2)}) collective-permute-start(bf16[5,2,64,128]{3,2,1,0:T(8,128)(2,1)S(1)} %get-tuple-element.67), channel_id=1, source_target_pairs={{0,1},{1,0},{2,3},{3,2},{4,5},{5,4},{6,7},{7,6},{8,9},{9,8},{10,11... | collective-permute-start | bytes 491528 | tf_op jit(solution)/shard_map/ppermute | solution.py:425
  53.7 7.9 %collective-permute-start.13 = (bf16[4,2,64,128]{3,2,1,0:T(8,128)(2,1)S(1)}, bf16[4,2,64,128]{3,2,1,0:T(8,128)(2,1)S(1)}, u32[]{:S(2)}, u32[]{:S(2)}) collective-permute-start(bf16[4,2,64,128]{3,2,1,0:T(8,128)(2,1)S(1)} %late_wires.3), channel_id=1, source_target_pairs={{0,2},{1,3},{2,0},{3,1},{4,6},{5,7},{6,4},{7,5},{8,10},{9,11},{10,... | collective-permute-start | bytes 393224 | tf_op jit(solution)/shard_map/ppermute | solution.py:425
  53.8 4.9 %collective-permute-start.11 = (bf16[3,2,64,128]{3,2,1,0:T(8,128)(2,1)S(1)}, bf16[3,2,64,128]{3,2,1,0:T(8,128)(2,1)S(1)}, u32[]{:S(2)}, u32[]{:S(2)}) collective-permute-start(bf16[3,2,64,128]{3,2,1,0:T(8,128)(2,1)S(1)} %get-tuple-element.68), channel_id=1, source_target_pairs={{0,1},{1,0},{2,3},{3,2},{4,5},{5,4},{6,7},{7,6},{8,9},{9,8},{10,11... | collective-permute-start | bytes 294920 | tf_op jit(solution)/shard_map/ppermute | solution.py:425

commit v22 on v20

--- a/solution.py
+++ b/solution.py
@@ -153,7 +153,8 @@
     weights_ref, out_ref, padded,
 ):
     sectors, stacked, window = weights_ref.shape
-    window //= 2
+    one_product = column > 0
+    window = window // 2 if one_product else window
     beams = stacked // 2
     margin = first_ref.shape[1]
     columns = slice(column, column + out_ref.shape[2])
@@ -166,12 +167,14 @@
     for sector in range(sectors):
         place = pl.ds(pl.multiple_of(starts_ref[sector] * BLK, BLK), window)
         width = out_ref.shape[2]
-        both = jnp.concatenate([padded[place, :width], padded[place, width:]])
-        parts = dot(weights_ref[sector], both).astype(jnp.bfloat16)
+        if one_product:
+            both = jnp.concatenate([padded[place, :width], padded[place, width:]])
+            product = dot(weights_ref[sector], both).astype(jnp.bfloat16)
+            parts = (product[:beams], product[beams:])
+        else:
+            parts = complex_window(weights_ref[sector], padded[place, :])
         for part in range(2):
-            out_ref[part, sector * beams : (sector + 1) * beams, :] = parts[
-                part * beams : (part + 1) * beams
-            ]
+            out_ref[part, sector * beams : (sector + 1) * beams, :] = parts[part]
 
 
 def first_level(column, rows, starts, side, sent, halos, weights):
@@ -482,7 +485,7 @@
     width = range_kernel.shape[3] // 2
     send = first_level(width, rows, begin0, side, sent, halos, weights)
     other = partner(send, "aperture", 0)
-    keep = first_level(0, rows, begin0, side, sent, halos, weights)
+    keep = first_level(0, rows, begin0, side, sent, halos, stacked_weights(weights0))
     level_one = (keep.astype(jnp.float32) + other.astype(jnp.float32)).astype(jnp.bfloat16)
 
     beams = level_one.shape[1]

time: 62.9 us -> 64.9 us (1.032)
  local copies, waits for them, and re-layouts: 2.46 us -> 3.9 us
    optimization_barrier x1 -> x2, local copies, waits for them, and re-layouts: 0.36 us -> 1.8 us  [local(): sent, weights0 = lax.optimization_barrier((sent, weights0))]
  transfers between devices with their start and end apart: 14 -> 14, of which waited for: 10 -> 8; matrix products, arithmetic and copies ran while one was open for 6% -> 8% of each run, Pallas kernels for 11% -> 11%
where the time goes in v22:
time: 64.9 us; the launch traced here: 64.6 us
  waiting for transfers between devices  25.1 us (39%)
  starting transfers between devices  20.4 us (31%)
  Pallas kernels  12.4 us (19%)
  local copies, waits for them, and re-layouts  3.9 us (6%)
  other arithmetic  2.61 us (4%)
    ppermute x6, waiting for transfers between devices, spread(): received.append(lax.ppermute(wire, 'beam', route) if distance else wire)  14.3 us
    ppermute x6, starting transfers between devices, spread(): received.append(lax.ppermute(wire, 'beam', route) if distance else wire)  9.62 us
    ppermute x4, starting transfers between devices, trade_edges(): received.append(lax.ppermute(block, ('aperture', 'beam'), route))  6.21 us
    ppermute x4, waiting for transfers between devices, trade_edges(): received.append(lax.ppermute(block, ('aperture', 'beam'), route))  5.67 us
    ppermute x4, waiting for transfers between devices, partner(): return lax.ppermute(block, axis, route)  5.08 us
    ppermute x4, starting transfers between devices, partner(): return lax.ppermute(block, axis, route)  4.6 us
    pallas_call x2, Pallas kernels, first_level(): pl.pallas_call(functools.partial(first_level_kernel, column, rows), out_s...  2.52 us
    pallas_call x1, Pallas kernels, resample(): pl.pallas_call(resample_kernel, out_shape=(shape, shape), in_specs=[ANY,...  2.31 us
  transfers between devices with their start and end apart: 14, of which 8 were waited for; matrix products, arithmetic and copies ran while one was open for 8% of the time, Pallas kernels for 11%

profile of v22, /device:TPU:0, one launch (start us, length us, event | category | flops | bytes accessed | tf_op | source)
XLA Modules:
  0.0 64.6 jit_solution(8449325985105941551)
XLA Ops:
  0.0 0.0 copy-start.1
  0.0 2.3 %resample.1 = (bf16[2,192,512]{2,1,0:T(8,128)(2,1)S(1)}, bf16[2,192,512]{2,1,0:T(8,128)(2,1)S(1)}) custom-call(bf16[2,256,512]{2,1,0:T(8,128)(2,1)} %bitcast.25, bf16[2,512,512]{2,1,0:T(8,128)(2,1)} %bitcast.24), custom_call_target="tpu_custom_call" | custom-call | flops 536870912 | bytes 2097152 | tf_op jit(solution)/shard_map/resample/pallas_call | solution.py:101
  2.3 3.1 %collective-permute-start = (bf16[2,192,512]{2,1,0:T(8,128)(2,1)S(1)}, bf16[2,192,512]{2,1,0:T(8,128)(2,1)S(1)}, u32[]{:S(2)}, u32[]{:S(2)}) collective-permute-start(bf16[2,192,512]{2,1,0:T(8,128)(2,1)S(1)} %get-tuple-element.41.sent_first_ref), channel_id=1, source_target_pairs={{0,1},{1,0},{2,3},{3,2},{4,5},{5,4},{6,7},{7,6},{8,9},{9,8},{10,11... | collective-permute-start | bytes 1179656 | tf_op jit(solution)/shard_map/ppermute | solution.py:43
  5.4 0.0 collective-permute-start.1
  5.4 0.0 copy-done.1
  5.4 0.4 copy.8
  5.8 0.1 slice_bitcast_fusion
  5.9 0.0 copy-start
  5.9 0.0 copy-start.2
  5.9 0.4 maximum_maximum_fusion.weights_ref
  6.4 0.1 copy-done
  6.5 1.5 %collective-permute-start.2 = (s32[1,16,1]{1,2,0:T(1,128)S(1)}, s32[1,16,1]{1,2,0:T(1,128)S(1)}, u32[]{:S(2)}, u32[]{:S(2)}) collective-permute-start(s32[1,16,1]{1,2,0:T(1,128)S(1)} %copy-done), channel_id=1, source_target_pairs={{0,8},{8,0},{4,12},{12,4},{16,24},{24,16},{20,28},{28,20},{1,9},{9... | collective-permute-start | bytes 200 | tf_op jit(solution)/shard_map/ppermute | solution.py:54
  8.0 0.1 pad_add_fusion.side_ref
  8.1 0.0 copy-done.2
  8.1 0.2 subtract_reduce_fusion.starts_ref
  8.3 1.8 %collective-permute-done.2 = s32[1,16,1]{1,2,0:T(1,128)S(1)} collective-permute-done((s32[1,16,1]{1,2,0:T(1,128)S(1)}, s32[1,16,1]{1,2,0:T(1,128)S(1)}, u32[]{:S(2)}, u32[]{:S(2)}) %collective-permute-start.2) | collective-permute-done | bytes 96 | tf_op jit(solution)/shard_map/ppermute | solution.py:54
  10.1 1.6 %plan.1 = (s32[16]{0:T(128)S(1)}, s32[16]{0:T(128)S(1)}, s32[16]{0:T(128)S(1)}, s32[16]{0:T(128)S(1)}, s32[16]{0:T(128)S(1)}) custom-call(s32[1]{0:T(128)} %bitcast.me_ref, s32[16]{0:T(128)S(1)} %bitcast.22, s32[16]{0:T(128)S(1)} %bitcast.23), custom_call_target="tpu_custom_call" | custom-call | tf_op jit(solution)/shard_map/plan/pallas_call | solution.py:319
  11.7 2.8 %collective-permute-done.first_ref = bf16[2,192,512]{2,1,0:T(8,128)(2,1)S(1)} collective-permute-done((bf16[2,192,512]{2,1,0:T(8,128)(2,1)S(1)}, bf16[2,192,512]{2,1,0:T(8,128)(2,1)S(1)}, u32[]{:S(2)}, u32[]{:S(2)}) %collective-permute-start) | collective-permute-done | bytes 393248 | tf_op jit(solution)/shard_map/ppermute | solution.py:43
  14.5 0.0 collective-permute-done.1.second_ref
  14.5 1.2 %first_level.3 = bf16[2,512,256]{2,1,0:T(8,128)(2,1)S(1)} custom-call(s32[4]{0:T(128)S(1)} %subtract_reduce_fusion.starts_ref, s32[3]{0:T(128)S(1)} %pad_add_fusion.side_ref, bf16[2,192,512]{2,1,0:T(8,128)(2,1)S(1)} %get-tuple-element.41.sent_first_ref, bf16[2,192,512]{2,1,0:T(8,128)(2,1)S(1)} %get-tuple-element.42.sent_second_ref, ...), custom_call_target="tpu_custom_call" | custom-call | flops 335544320 | bytes 2097152 | tf_op jit(solution)/shard_map/first_level/pallas_call | solution.py:185
  15.7 0.1 collective-permute-start.3
  15.8 1.4 %copy.10 = bf16[1,4,2,128,320]{4,3,2,1,0:T(8,128)(2,1)S(1)} copy(bf16[1,4,2,128,320]{3,4,2,1,0:T(8,128)(2,1)} %param.9) | data formatting | bytes 1310720 | tf_op jit(solution)/shard_map/optimization_barrier | solution.py:476
  17.3 1.3 %first_level.2 = bf16[2,512,256]{2,1,0:T(8,128)(2,1)S(1)} custom-call(s32[4]{0:T(128)S(1)} %subtract_reduce_fusion.starts_ref, s32[3]{0:T(128)S(1)} %pad_add_fusion.side_ref, bf16[2,192,512]{2,1,0:T(8,128)(2,1)S(1)} %get-tuple-element.41.sent_first_ref, bf16[2,192,512]{2,1,0:T(8,128)(2,1)S(1)} %get-tuple-element.42.sent_second_ref, ...), custom_call_target="tpu_custom_call" | custom-call | flops 167772160 | bytes 2097152 | tf_op jit(solution)/shard_map/first_level/pallas_call | solution.py:185
  18.6 0.0 collective-permute-done.3
  18.6 1.2 %add_convert_fusion.own_ref = bf16[2,512,256]{2,1,0:T(8,128)(2,1)S(1)} fusion(bf16[2,512,256]{2,1,0:T(8,128)(2,1)} %collective-permute-done.3, bf16[2,512,256]{2,1,0:T(8,128)(2,1)S(1)} %first_level.2), kind=kLoop, calls=%fused_computation.1 | loop fusion | flops 1048576 | bytes 1572864 | tf_op jit(solution)/shard_map/convert_element_type | solution.py:489
  19.8 2.9 %collective-permute-start.4 = (bf16[2,192,256]{2,1,0:T(8,128)(2,1)S(1)}, bf16[2,192,256]{2,1,0:T(8,128)(2,1)S(1)}, u32[]{:S(2)}, u32[]{:S(2)}) collective-permute-start(bf16[2,192,256]{2,1,0:T(8,128)(2,1)S(1)} %get-tuple-element.76), channel_id=1, source_target_pairs={{0,1},{1,0},{2,3},{3,2},{4,5},{5,4},{6,7},{7,6},{8,9},{9,8},{10,11... | collective-permute-start | bytes 589832 | tf_op jit(solution)/shard_map/ppermute | solution.py:43
  22.7 0.2 collective-permute-start.5
  23.0 1.8 %copy.11 = bf16[1,8,2,128,320]{4,3,2,1,0:T(8,128)(2,1)S(1)} copy(bf16[1,8,2,128,320]{3,4,2,1,0:T(8,128)(2,1)} %param.11) | data formatting | bytes 2621440 | tf_op args[4]
  24.8 0.7 %fusion.1.starts_ref = s32[8]{0:T(128)S(1)} fusion(s32[8,8]{1,0:T(8,128)} %param.12, s32[]{:T(128)S(6)} %select_n.19, s32[]{:T(128)S(6)} %sub.25), kind=kLoop, calls=%fused_computation.9 | loop fusion | flops 8 | bytes 72 | tf_op jit(solution)/shard_map/sub | solution.py:495
  25.5 2.8 %collective-permute-done.4.first_ref = bf16[2,192,256]{2,1,0:T(8,128)(2,1)S(1)} collective-permute-done((bf16[2,192,256]{2,1,0:T(8,128)(2,1)S(1)}, bf16[2,192,256]{2,1,0:T(8,128)(2,1)S(1)}, u32[]{:S(2)}, u32[]{:S(2)}) %collective-permute-start.4) | collective-permute-done | bytes 196640 | tf_op jit(solution)/shard_map/ppermute | solution.py:43
  28.3 0.0 collective-permute-done.5.second_ref
  28.3 1.0 %second_level_early.1 = bf16[6,2,64,128]{3,2,1,0:T(8,128)(2,1)S(1)} custom-call(s32[8]{0:T(128)S(1)} %fusion.1.starts_ref, s32[3]{0:T(128)S(1)} %pad_add_fusion.side_ref, s32[16]{0:T(128)S(1)} %get-tuple-element.50.sector_ref, bf16[2,512,256]{2,1,0:T(8,128)(2,1)S(1)} %add_convert_fusion.own_ref, bf16[2,192,256]{2,1,0:T(8,128)(2,1)S(1)} %collective-permute-done.4.first_ref, ...), custom_call_target="tpu_custom_call" | custom-call | flops 125829120 | bytes 1048576 | tf_op jit(solution)/shard_map/second_level_early/pallas_call | solution.py:252
  29.3 1.6 %collective-permute-start.6 = (bf16[6,2,64,128]{3,2,1,0:T(8,128)(2,1)S(1)}, bf16[6,2,64,128]{3,2,1,0:T(8,128)(2,1)S(1)}, u32[]{:S(2)}, u32[]{:S(2)}) collective-permute-start(bf16[6,2,64,128]{3,2,1,0:T(8,128)(2,1)S(1)} %second_level_early.1), channel_id=1, source_target_pairs={{0,8},{8,0},{4,12},{12,4},{16,24},{24,16},{20,28},{28,20},{1,9},{9... | collective-permute-start | bytes 589832 | tf_op jit(solution)/shard_map/ppermute | solution.py:54
  30.9 1.9 %second_level.1 = (bf16[16,2,64,128]{3,2,1,0:T(8,128)(2,1)S(1)}, bf16[10,2,64,128]{3,2,1,0:T(8,128)(2,1)S(1)}) custom-call(s32[8]{0:T(128)S(1)} %fusion.1.starts_ref, s32[3]{0:T(128)S(1)} %pad_add_fusion.side_ref, s32[16]{0:T(128)S(1)} %get-tuple-element.54.own_at_ref, s32[16]{0:T(128)S(1)} %get-tuple-element.55.other_at_ref, ...), custom_call_target="tpu_custom_call" | custom-call | flops 671088640 | bytes 4194304 | tf_op jit(solution)/shard_map/second_level/pallas_call | solution.py:263
  32.8 3.3 %collective-permute-done.6.refs_0_ = bf16[6,2,64,128]{3,2,1,0:T(8,128)(2,1)S(1)} collective-permute-done((bf16[6,2,64,128]{3,2,1,0:T(8,128)(2,1)S(1)}, bf16[6,2,64,128]{3,2,1,0:T(8,128)(2,1)S(1)}, u32[]{:S(2)}, u32[]{:S(2)}) %collective-permute-start.6) | collective-permute-done | bytes 196640 | tf_op jit(solution)/shard_map/ppermute | solution.py:54
  36.1 1.5 %collective-permute-start.7 = (bf16[10,2,64,128]{3,2,1,0:T(8,128)(2,1)S(1)}, bf16[10,2,64,128]{3,2,1,0:T(8,128)(2,1)S(1)}, u32[]{:S(2)}, u32[]{:S(2)}) collective-permute-start(bf16[10,2,64,128]{3,2,1,0:T(8,128)(2,1)S(1)} %get-tuple-element.57), channel_id=1, source_target_pairs={{0,8},{8,0},{4,12},{12,4},{16,24},{24,16},{20,28},{28,20},{1,9},{9... | collective-permute-start | bytes 983048 | tf_op jit(solution)/shard_map/ppermute | solution.py:54
  37.6 0.6 early_wires.1
  38.2 2.5 %collective-permute-start.8 = (bf16[2,2,64,128]{3,2,1,0:T(8,128)(2,1)S(1)}, bf16[2,2,64,128]{3,2,1,0:T(8,128)(2,1)S(1)}, u32[]{:S(2)}, u32[]{:S(2)}) collective-permute-start(bf16[2,2,64,128]{3,2,1,0:T(8,128)(2,1)S(1)} %get-tuple-element.62), channel_id=1, source_target_pairs={{0,3},{1,2},{2,1},{3,0},{4,7},{5,6},{6,5},{7,4},{8,11},{9,10},{10,... | collective-permute-start | bytes 196616 | tf_op jit(solution)/shard_map/ppermute | solution.py:428
  40.8 0.6 collective-permute-start.12
  41.4 3.5 %collective-permute-done.8.refs_0_ = bf16[2,2,64,128]{3,2,1,0:T(8,128)(2,1)S(1)} collective-permute-done((bf16[2,2,64,128]{3,2,1,0:T(8,128)(2,1)S(1)}, bf16[2,2,64,128]{3,2,1,0:T(8,128)(2,1)S(1)}, u32[]{:S(2)}, u32[]{:S(2)}) %collective-permute-start.8) | collective-permute-done | bytes 65568 | tf_op jit(solution)/shard_map/ppermute | solution.py:428
  44.9 0.0 collective-permute-done.7.refs_0_
  44.9 0.8 %late_wires.2 = (bf16[6,2,64,128]{3,2,1,0:T(8,128)(2,1)S(1)}, bf16[5,2,64,128]{3,2,1,0:T(8,128)(2,1)S(1)}, bf16[3,2,64,128]{3,2,1,0:T(8,128)(2,1)S(1)}, bf16[8,2,64,128]{3,2,1,0:T(8,128)(2,1)S(1)}) custom-call(s32[1]{0:T(128)} %bitcast.me_ref, s32[16]{0:T(128)S(1)} %get-tuple-element.58.target_ref, s32[16]{0:T(128)S(1)} %get-tuple-element.59.rank_ref, ...), custom_call_target="tpu_custom_call" | custom-call | bytes 2097152 | tf_op jit(solution)/shard_map/late_wires/pallas_call | solution.py:380
  45.7 2.2 %collective-permute-start.9 = (bf16[6,2,64,128]{3,2,1,0:T(8,128)(2,1)S(1)}, bf16[6,2,64,128]{3,2,1,0:T(8,128)(2,1)S(1)}, u32[]{:S(2)}, u32[]{:S(2)}) collective-permute-start(bf16[6,2,64,128]{3,2,1,0:T(8,128)(2,1)S(1)} %get-tuple-element.66), channel_id=1, source_target_pairs={{0,3},{1,2},{2,1},{3,0},{4,7},{5,6},{6,5},{7,4},{8,11},{9,10},{10,... | collective-permute-start | bytes 589832 | tf_op jit(solution)/shard_map/ppermute | solution.py:428
  47.9 2.0 %collective-permute-start.10 = (bf16[5,2,64,128]{3,2,1,0:T(8,128)(2,1)S(1)}, bf16[5,2,64,128]{3,2,1,0:T(8,128)(2,1)S(1)}, u32[]{:S(2)}, u32[]{:S(2)}) collective-permute-start(bf16[5,2,64,128]{3,2,1,0:T(8,128)(2,1)S(1)} %get-tuple-element.67), channel_id=1, source_target_pairs={{0,1},{1,0},{2,3},{3,2},{4,5},{5,4},{6,7},{7,6},{8,9},{9,8},{10,11... | collective-permute-start | bytes 491528 | tf_op jit(solution)/shard_map/ppermute | solution.py:428
  49.9 5.1 %collective-permute-done.12.refs_5_ = bf16[4,2,64,128]{3,2,1,0:T(8,128)(2,1)S(1)} collective-permute-done((bf16[4,2,64,128]{3,2,1,0:T(8,128)(2,1)S(1)}, bf16[4,2,64,128]{3,2,1,0:T(8,128)(2,1)S(1)}, u32[]{:S(2)}, u32[]{:S(2)}) %collective-permute-start.12) | collective-permute-done | bytes 131104 | tf_op jit(solution)/shard_map/ppermute | solution.py:428
  55.0 0.6 late_wires.3
  55.7 0.1 collective-permute-start.13
  55.8 2.2 %collective-permute-start.11 = (bf16[3,2,64,128]{3,2,1,0:T(8,128)(2,1)S(1)}, bf16[3,2,64,128]{3,2,1,0:T(8,128)(2,1)S(1)}, u32[]{:S(2)}, u32[]{:S(2)}) collective-permute-start(bf16[3,2,64,128]{3,2,1,0:T(8,128)(2,1)S(1)} %get-tuple-element.68), channel_id=1, source_target_pairs={{0,1},{1,0},{2,3},{3,2},{4,5},{5,4},{6,7},{7,6},{8,9},{9,8},{10,11... | collective-permute-start | bytes 294920 | tf_op jit(solution)/shard_map/ppermute | solution.py:428
  57.9 2.7 %collective-permute-done.11.refs_3_ = bf16[3,2,64,128]{3,2,1,0:T(8,128)(2,1)S(1)} collective-permute-done((bf16[3,2,64,128]{3,2,1,0:T(8,128)(2,1)S(1)}, bf16[3,2,64,128]{3,2,1,0:T(8,128)(2,1)S(1)}, u32[]{:S(2)}, u32[]{:S(2)}) %collective-permute-start.11) | collective-permute-done | bytes 98336 | tf_op jit(solution)/shard_map/ppermute | solution.py:428
  60.6 3.0 %collective-permute-done.13.refs_6_ = bf16[4,2,64,128]{3,2,1,0:T(8,128)(2,1)S(1)} collective-permute-done((bf16[4,2,64,128]{3,2,1,0:T(8,128)(2,1)S(1)}, bf16[4,2,64,128]{3,2,1,0:T(8,128)(2,1)S(1)}, u32[]{:S(2)}, u32[]{:S(2)}) %collective-permute-start.13) | collective-permute-done | bytes 131104 | tf_op jit(solution)/shard_map/ppermute | solution.py:428
  63.6 0.0 collective-permute-done.10.refs_2_
  63.6 0.0 collective-permute-done.9.refs_1_
  63.6 1.0 %collect.1 = bf16[32,2,64,128]{3,2,1,0:T(8,128)(2,1)} custom-call(s32[1]{0:T(128)} %bitcast.me_ref, bf16[2,2,64,128]{3,2,1,0:T(8,128)(2,1)S(1)} %collective-permute-done.8.refs_0_, bf16[6,2,64,128]{3,2,1,0:T(8,128)(2,1)S(1)} %collective-permute-done.9.refs_1_, bf16[5,2,64,128]{3,2,1,0:T(8,128)(2,1)S(1)} %collective-permute-done.10.refs_2_, ...), custom_call_target="tpu_custom_call" | custom-call | bytes 2097152 | tf_op jit(solution)/shard_map/collect/pallas_call | solution.py:411
  (2 shorter events, 0.1 us)
Async XLA Ops:
  0.0 5.4 %copy-start.1 = (bf16[1,4,2,128,320]{3,4,2,1,0:T(8,128)(2,1)S(1)}, bf16[1,4,2,128,320]{3,4,2,1,0:T(8,128)(2,1)}, u32[]{:S(2)}) copy-start(bf16[1,4,2,128,320]{3,4,2,1,0:T(8,128)(2,1)} %param.9) | copy-start | bytes 1966084
  2.3 12.2 %collective-permute-start = (bf16[2,192,512]{2,1,0:T(8,128)(2,1)S(1)}, bf16[2,192,512]{2,1,0:T(8,128)(2,1)S(1)}, u32[]{:S(2)}, u32[]{:S(2)}) collective-permute-start(bf16[2,192,512]{2,1,0:T(8,128)(2,1)S(1)} %get-tuple-element.41.sent_first_ref), channel_id=1, source_target_pairs={{0,1},{1,0},{2,3},{3,2},{4,5},{5,4},{6,7},{7,6},{8,9},{9,8},{10,11... | collective-permute-start | bytes 1179656 | tf_op jit(solution)/shard_map/ppermute | solution.py:43
  5.4 9.1 %collective-permute-start.1 = (bf16[2,192,512]{2,1,0:T(8,128)(2,1)S(1)}, bf16[2,192,512]{2,1,0:T(8,128)(2,1)S(1)}, u32[]{:S(2)}, u32[]{:S(2)}) collective-permute-start(bf16[2,192,512]{2,1,0:T(8,128)(2,1)S(1)} %get-tuple-element.42.sent_second_ref), channel_id=1, source_target_pairs={{0,4},{1,2},{2,1},{3,7},{4,0},{5,6},{6,5},{7,3},{8,12},{9,10},{10,... | collective-permute-start | bytes 1179656 | tf_op jit(solution)/shard_map/ppermute | solution.py:43
  5.9 0.7 %copy-start = (s32[1,16,1]{1,2,0:T(1,128)S(1)}, s32[1,16,1]{1,2,0:T(1,128)}, u32[]{:S(2)}) copy-start(s32[1,16,1]{1,2,0:T(1,128)} %param.13) | copy-start | bytes 196
  5.9 2.2 %copy-start.2 = (s32[8,4]{0,1:T(4,128)S(1)}, s32[8,4]{0,1:T(4,128)}, u32[]{:S(2)}) copy-start(s32[8,4]{0,1:T(4,128)} %param.10) | copy-start | bytes 388
  6.5 3.5 %collective-permute-start.2 = (s32[1,16,1]{1,2,0:T(1,128)S(1)}, s32[1,16,1]{1,2,0:T(1,128)S(1)}, u32[]{:S(2)}, u32[]{:S(2)}) collective-permute-start(s32[1,16,1]{1,2,0:T(1,128)S(1)} %copy-done), channel_id=1, source_target_pairs={{0,8},{8,0},{4,12},{12,4},{16,24},{24,16},{20,28},{28,20},{1,9},{9... | collective-permute-start | bytes 200 | tf_op jit(solution)/shard_map/ppermute | solution.py:54
  15.7 2.9 %collective-permute-start.3 = (bf16[2,512,256]{2,1,0:T(8,128)(2,1)S(1)}, bf16[2,512,256]{2,1,0:T(8,128)(2,1)}, u32[]{:S(2)}, u32[]{:S(2)}) collective-permute-start(bf16[2,512,256]{2,1,0:T(8,128)(2,1)S(1)} %first_level.3), channel_id=1, source_target_pairs={{0,4},{4,0},{8,12},{12,8},{16,20},{20,16},{24,28},{28,24},{1,5},{5... | collective-permute-start | bytes 1572872 | tf_op jit(solution)/shard_map/ppermute | solution.py:54
  19.8 8.5 %collective-permute-start.4 = (bf16[2,192,256]{2,1,0:T(8,128)(2,1)S(1)}, bf16[2,192,256]{2,1,0:T(8,128)(2,1)S(1)}, u32[]{:S(2)}, u32[]{:S(2)}) collective-permute-start(bf16[2,192,256]{2,1,0:T(8,128)(2,1)S(1)} %get-tuple-element.76), channel_id=1, source_target_pairs={{0,1},{1,0},{2,3},{3,2},{4,5},{5,4},{6,7},{7,6},{8,9},{9,8},{10,11... | collective-permute-start | bytes 589832 | tf_op jit(solution)/shard_map/ppermute | solution.py:43
  22.7 5.6 %collective-permute-start.5 = (bf16[2,192,256]{2,1,0:T(8,128)(2,1)S(1)}, bf16[2,192,256]{2,1,0:T(8,128)(2,1)S(1)}, u32[]{:S(2)}, u32[]{:S(2)}) collective-permute-start(bf16[2,192,256]{2,1,0:T(8,128)(2,1)S(1)} %get-tuple-element.75), channel_id=1, source_target_pairs={{0,4},{1,2},{2,1},{3,7},{4,0},{5,6},{6,5},{7,3},{8,12},{9,10},{10,... | collective-permute-start | bytes 589832 | tf_op jit(solution)/shard_map/ppermute | solution.py:43
  29.3 6.8 %collective-permute-start.6 = (bf16[6,2,64,128]{3,2,1,0:T(8,128)(2,1)S(1)}, bf16[6,2,64,128]{3,2,1,0:T(8,128)(2,1)S(1)}, u32[]{:S(2)}, u32[]{:S(2)}) collective-permute-start(bf16[6,2,64,128]{3,2,1,0:T(8,128)(2,1)S(1)} %second_level_early.1), channel_id=1, source_target_pairs={{0,8},{8,0},{4,12},{12,4},{16,24},{24,16},{20,28},{28,20},{1,9},{9... | collective-permute-start | bytes 589832 | tf_op jit(solution)/shard_map/ppermute | solution.py:54
  36.1 8.8 %collective-permute-start.7 = (bf16[10,2,64,128]{3,2,1,0:T(8,128)(2,1)S(1)}, bf16[10,2,64,128]{3,2,1,0:T(8,128)(2,1)S(1)}, u32[]{:S(2)}, u32[]{:S(2)}) collective-permute-start(bf16[10,2,64,128]{3,2,1,0:T(8,128)(2,1)S(1)} %get-tuple-element.57), channel_id=1, source_target_pairs={{0,8},{8,0},{4,12},{12,4},{16,24},{24,16},{20,28},{28,20},{1,9},{9... | collective-permute-start | bytes 983048 | tf_op jit(solution)/shard_map/ppermute | solution.py:54
  38.2 6.7 %collective-permute-start.8 = (bf16[2,2,64,128]{3,2,1,0:T(8,128)(2,1)S(1)}, bf16[2,2,64,128]{3,2,1,0:T(8,128)(2,1)S(1)}, u32[]{:S(2)}, u32[]{:S(2)}) collective-permute-start(bf16[2,2,64,128]{3,2,1,0:T(8,128)(2,1)S(1)} %get-tuple-element.62), channel_id=1, source_target_pairs={{0,3},{1,2},{2,1},{3,0},{4,7},{5,6},{6,5},{7,4},{8,11},{9,10},{10,... | collective-permute-start | bytes 196616 | tf_op jit(solution)/shard_map/ppermute | solution.py:428
  40.8 14.3 %collective-permute-start.12 = (bf16[4,2,64,128]{3,2,1,0:T(8,128)(2,1)S(1)}, bf16[4,2,64,128]{3,2,1,0:T(8,128)(2,1)S(1)}, u32[]{:S(2)}, u32[]{:S(2)}) collective-permute-start(bf16[4,2,64,128]{3,2,1,0:T(8,128)(2,1)S(1)} %get-tuple-element.70), channel_id=1, source_target_pairs={{0,2},{1,3},{2,0},{3,1},{4,6},{5,7},{6,4},{7,5},{8,10},{9,11},{10,... | collective-permute-start | bytes 393224 | tf_op jit(solution)/shard_map/ppermute | solution.py:428
  45.7 17.9 %collective-permute-start.9 = (bf16[6,2,64,128]{3,2,1,0:T(8,128)(2,1)S(1)}, bf16[6,2,64,128]{3,2,1,0:T(8,128)(2,1)S(1)}, u32[]{:S(2)}, u32[]{:S(2)}) collective-permute-start(bf16[6,2,64,128]{3,2,1,0:T(8,128)(2,1)S(1)} %get-tuple-element.66), channel_id=1, source_target_pairs={{0,3},{1,2},{2,1},{3,0},{4,7},{5,6},{6,5},{7,4},{8,11},{9,10},{10,... | collective-permute-start | bytes 589832 | tf_op jit(solution)/shard_map/ppermute | solution.py:428
  47.9 15.7 %collective-permute-start.10 = (bf16[5,2,64,128]{3,2,1,0:T(8,128)(2,1)S(1)}, bf16[5,2,64,128]{3,2,1,0:T(8,128)(2,1)S(1)}, u32[]{:S(2)}, u32[]{:S(2)}) collective-permute-start(bf16[5,2,64,128]{3,2,1,0:T(8,128)(2,1)S(1)} %get-tuple-element.67), channel_id=1, source_target_pairs={{0,1},{1,0},{2,3},{3,2},{4,5},{5,4},{6,7},{7,6},{8,9},{9,8},{10,11... | collective-permute-start | bytes 491528 | tf_op jit(solution)/shard_map/ppermute | solution.py:428
  55.7 7.9 %collective-permute-start.13 = (bf16[4,2,64,128]{3,2,1,0:T(8,128)(2,1)S(1)}, bf16[4,2,64,128]{3,2,1,0:T(8,128)(2,1)S(1)}, u32[]{:S(2)}, u32[]{:S(2)}) collective-permute-start(bf16[4,2,64,128]{3,2,1,0:T(8,128)(2,1)S(1)} %late_wires.3), channel_id=1, source_target_pairs={{0,2},{1,3},{2,0},{3,1},{4,6},{5,7},{6,4},{7,5},{8,10},{9,11},{10,... | collective-permute-start | bytes 393224 | tf_op jit(solution)/shard_map/ppermute | solution.py:428
  55.8 4.9 %collective-permute-start.11 = (bf16[3,2,64,128]{3,2,1,0:T(8,128)(2,1)S(1)}, bf16[3,2,64,128]{3,2,1,0:T(8,128)(2,1)S(1)}, u32[]{:S(2)}, u32[]{:S(2)}) collective-permute-start(bf16[3,2,64,128]{3,2,1,0:T(8,128)(2,1)S(1)} %get-tuple-element.68), channel_id=1, source_target_pairs={{0,1},{1,0},{2,3},{3,2},{4,5},{5,4},{6,7},{7,6},{8,9},{9,8},{10,11... | collective-permute-start | bytes 294920 | tf_op jit(solution)/shard_map/ppermute | solution.py:428
